TPU v7x, 32 devices: a whole 2x2x4 slice. The times are simulated.
32 devices in a mesh: space: 16 (over z, y, x), knot: 2 (over core).
Axes of the slice: x: 2, y: 2, z: 4, core: 2. Of those that a mesh axis runs over, the one named last changes fastest.
Arguments:
- probes: float32 [16, 32768], P(None, ('space', 'knot')), may hold values from -6 to 6
- locations: float32 [2, 32768], P(None, ('space', 'knot')), may hold values from 0 to 1.6, as said below
- knot_locs: float32 [2, 2048], P(None, 'knot'), may hold values from 0 to 1.6, as said below
- knot_precision: float32 [2048, 2048], P('knot'), may hold values from -0.125 to 0.125
- neighbours: int32 [256, 8], P(('space', 'knot')), may hold values from 0 to 255, as said below
- counts: int32 [256], P(('space', 'knot')), may hold values from 1 to 8
Outputs:
- applied: float32 [16, 32768], P(None, ('space', 'knot'))
Inputs may be any that keep to these rules, and one draw needn't show every extreme that they name: `locations`: block b lies in one cell of a grid of 16 x 16 cells of side 0.1: its east coordinates in [0.1 (b // 16), 0.1 (b // 16 + 1)], its north ones in [0.1 (b % 16), 0.1 (b % 16 + 1)]. `knot_locs`: knots lie in [0, 0.1 * 16] east and [0, 0.1 * 16] north. neighbours[b, 0] = b; every other entry of row b is the block of one of the eight cells around b's cell, where a step off the grid is turned back in that direction; the steps of a row are distinct.
All inputs are finite; a program needn't handle non-finite values.
Results may differ from a plain program's by a relative error of at most 0.0003.
Values sent between devices are 32-bit elements; how exact they have to be, the bound alone decides.
No kernel may reach another device: no remote copies, remote signals or barrier semaphores. Data moves between devices by JAX's collectives and lax.ppermute only.
A program may use at most 64 MiB of HBM per device.

v0:
```python
import math

import jax
import jax.numpy as jnp
from jax import lax
from jax.sharding import PartitionSpec as P

COV_RANGE = 0.05
TAPER_LEN = 0.15
KNOT_REACH = 0.15
TAPER_SCALE = 0.1
PROJ_GAIN = 0.5
EXPAND_GAIN = 0.5
LOW_SCALE = 0.5
NUGGET = 0.25
PRECISE = lax.Precision.HIGHEST


def with_halo(block, sides, width):
    for axis, dim in sides:
        count = lax.axis_size(axis)
        forward = [(i, i + 1) for i in range(count - 1)]
        backward = [(target, source) for source, target in forward]
        low = lax.ppermute(
            lax.slice_in_dim(block, block.shape[dim] - width, None, axis=dim), axis, forward
        )
        high = lax.ppermute(lax.slice_in_dim(block, 0, width, axis=dim), axis, backward)
        block = jnp.concatenate([low, block, high], axis=dim)
    return block


def tapered(own_locs, near_locs, near_vals, weights):
    delta_x = own_locs[0][:, None, :, None] - near_locs[0][:, :, None, :]
    delta_y = own_locs[1][:, None, :, None] - near_locs[1][:, :, None, :]
    distance = jnp.sqrt(delta_x * delta_x + delta_y * delta_y)
    scaled = jnp.minimum(distance / TAPER_LEN, 1.0)
    remain = (1.0 - scaled) * (1.0 - scaled)
    kernel = (
        jnp.exp(-distance / COV_RANGE)
        * remain
        * remain
        * (1.0 + 4.0 * scaled)
        * weights[:, :, None, None]
    )
    return jnp.einsum("gkpq,rgkq->rgp", kernel, near_vals, precision=PRECISE)


def knot_kernel(points, knot_pts, knot_range):
    delta_x = points[0][:, None] - knot_pts[0][None, :]
    delta_y = points[1][:, None] - knot_pts[1][None, :]
    return jnp.exp(-jnp.sqrt(delta_x * delta_x + delta_y * delta_y) / knot_range)


def contract_last(left, right):
    return lax.dot_general(left, right, (((1,), (1,)), ((), ())), precision=PRECISE)


def shards(probes, locations, knot_locs, knot_precision, neighbours, counts):
    own_blocks = neighbours.shape[0]
    slot_count = neighbours.shape[1]
    row_count = probes.shape[1]
    block_len = row_count // own_blocks
    probe_count = probes.shape[0]
    knot_total = knot_precision.shape[1]
    device_count = lax.axis_size(("space", "knot"))
    north_cells = lax.axis_size("knot") * own_blocks
    knot_range = KNOT_REACH * math.sqrt(own_blocks * device_count / knot_total)
    proj_scale = PROJ_GAIN * math.sqrt(knot_total / (row_count * device_count))
    stacked = jnp.concatenate([probes, locations], axis=0).reshape(
        probe_count + 2, 1, own_blocks, block_len
    )
    padded = with_halo(stacked, (("space", 1), ("knot", 2)), 1)
    near = padded.reshape(probe_count + 2, 3 * (own_blocks + 2), block_len)
    east_base = lax.axis_index("space") - 1
    north_base = lax.axis_index("knot") * own_blocks - 1
    local_ids = (neighbours // north_cells - east_base) * (own_blocks + 2) + (
        neighbours % north_cells - north_base
    )
    picked = near[:, local_ids]
    slot_ids = jnp.arange(slot_count, dtype=jnp.int32)
    weights = (slot_ids[None, :] < counts[:, None]).astype(jnp.float32)
    taper_part = tapered(
        locations.reshape(2, own_blocks, block_len),
        picked[probe_count:],
        picked[:probe_count],
        weights,
    )
    taper_part = taper_part.reshape(probe_count, row_count)
    gathered_vals, gathered_locs = (
        lax.all_gather(probes, "knot", axis=1, tiled=True),
        lax.all_gather(locations, "knot", axis=1, tiled=True),
    )
    kernel = knot_kernel(gathered_locs, knot_locs, knot_range)
    local_terms = jnp.dot(gathered_vals, kernel, precision=PRECISE)
    projection = lax.psum(local_terms, "space") * proj_scale
    factor = contract_last(lax.all_gather(projection, "knot", axis=1, tiled=True), knot_precision)
    spread = contract_last(factor, kernel)
    low_part = lax.psum_scatter(spread, "knot", scatter_dimension=1, tiled=True)
    low_part = low_part * EXPAND_GAIN
    return TAPER_SCALE * taper_part + LOW_SCALE * low_part + NUGGET * probes


def solution(mesh):
    return jax.shard_map(
        shards,
        mesh=mesh,
        in_specs=(
            P(None, ("space", "knot")),
            P(None, ("space", "knot")),
            P(None, "knot"),
            P("knot", None),
            P(("space", "knot"), None),
            P(("space", "knot")),
        ),
        out_specs=P(None, ("space", "knot")),
        check_vma=False,
    )
```

profile of v0, /device:TPU:0, one launch (start us, length us, event | category | flops | bytes accessed | tf_op | source)
XLA Modules:
  0.0 191.0 jit_solution(4465474876012478968)
XLA Ops:
  6.5 0.0 all-reduce.2.cloned.1.call-start
  6.5 0.9 pad_maximum_fusion.1
  7.5 4.8 %collective-permute-start = (f32[18,1,8,128]{3,0,2,1:T(8,128)S(1)}, f32[18,1,8,128]{3,0,2,1:T(8,128)S(1)}, u32[]{:S(2)}, u32[]{:S(2)}) collective-permute-start(f32[18,1,8,128]{3,0,2,1:T(8,128)S(1)} %copy.7), channel_id=1, source_target_pairs={{0,2},{2,4},{4,6},{6,8},{8,10},{10,12},{12,14},{14,16},{16,18},{18... | collective-permute-start | bytes 221192 | tf_op jit(solution)/shard_map/ppermute | solution.py:24
  12.3 1.3 collective-permute-start.1
  13.6 2.0 %all_gather.9 = f32[2,2048]{1,0:T(2,128)S(1)} all-gather(f32[2,1024]{1,0:T(2,128)} %param.7), channel_id=1, replica_groups=mesh['space'=16,'knot'=2] {'knot'}, dimensions={1}, use_global_device_ids=true | all-gather | bytes 24576 | tf_op jit(solution)/shard_map/all_gather | solution.py:91
  15.6 2.2 %all_gather.10 = f32[16,2048]{1,0:T(8,128)S(1)} all-gather(f32[16,1024]{1,0:T(8,128)} %param.6), channel_id=1, replica_groups=mesh['space'=16,'knot'=2] {'knot'}, dimensions={1}, use_global_device_ids=true | all-gather | bytes 196608 | tf_op jit(solution)/shard_map/all_gather | solution.py:90
  17.9 0.8 fusion.70
  18.7 0.0 copy-start.1
  18.7 0.0 copy-start.2
  18.7 0.0 copy-start.3
  18.7 17.4 %fusion.40 = f32[16,1024]{0,1:T(8,128)} fusion(f32[16,2048]{1,0:T(8,128)S(1)} %all_gather.10, f32[1024]{0:T(1024)S(1)} %bitcast.53, f32[2048]{0:T(1024)S(1)} %bitcast.47, f32[1024]{0:T(1024)S(1)} %bitcast.51, f32[2048]{0:T(1024)S(1)} %bitcast.45), kind=kOutput, calls=%fused_computation.42 | convolution fusion | flops 417333248 | bytes 221184 | tf_op jit(solution)/shard_map/dot_general | solution.py:94
  36.2 0.0 all-reduce.2.cloned.1.call-update
  36.2 0.0 reduce-scatter.2.cloned.1.call-start
  36.2 0.0 copy-done.1
  36.3 0.0 copy-done.2
  36.3 0.1 reshape.46
  36.4 0.0 copy-done.3
  36.4 0.1 fusion.60
  36.5 110.6 %all-reduce.2.cloned.1.call-done = f32[16,1024]{0,1:T(8,128)} async-done(((f32[16,1024]{0,1:T(8,128)}), f32[16,1024]{0,1:T(8,128)}) %all-reduce.2.cloned.1.call-update) | async-done | bytes 65552 | tf_op jit(solution)/shard_map/psum | solution.py:95
  147.0 1.1 broadcast_multiply_fusion
  148.1 2.6 %all_gather.11 = f32[16,2048]{0,1:T(8,128)S(1)} all-gather(f32[16,1024]{0,1:T(8,128)S(1)} %broadcast_multiply_fusion), channel_id=1, replica_groups=mesh['space'=16,'knot'=2] {'knot'}, dimensions={1}, use_global_device_ids=true | all-gather | bytes 196608 | tf_op jit(solution)/shard_map/all_gather | solution.py:96
  150.7 9.3 %fusion.72 = f32[16,1024]{1,0:T(8,128)S(1)} fusion(f32[16,2048]{0,1:T(8,128)S(1)} %all_gather.11, f32[1024,2048]{1,0:T(8,128)} %param.9), kind=kOutput, calls=%fused_computation.85 | convolution fusion | flops 402653184 | bytes 8585216 | tf_op jit(solution)/shard_map/dot_general | solution.py:55
  160.0 0.0 collective-permute-done
  160.1 0.0 collective-permute-done.1
  160.1 2.0 %collective-permute-start.2 = (f32[18,3,1,128]{3,0,2,1:T(8,128)S(1)}, f32[18,3,1,128]{3,0,2,1:T(8,128)S(1)}, u32[]{:S(2)}, u32[]{:S(2)}) collective-permute-start(f32[18,3,1,128]{3,0,2,1:T(8,128)S(1)} %get-tuple-element.7), channel_id=1, source_target_pairs={{0,1},{2,3},{4,5},{6,7},{8,9},{10,11},{12,13},{14,15},{16,17},{18,... | collective-permute-start | bytes 82952 | tf_op jit(solution)/shard_map/ppermute | solution.py:24
  162.2 1.5 collective-permute-start.3
  163.7 11.2 %fusion = f32[16,2048]{1,0:T(8,128)} fusion(f32[16,1024]{1,0:T(8,128)S(1)} %fusion.72, f32[1024]{0:T(1024)S(1)} %bitcast.54, f32[2048]{0:T(1024)S(1)} %bitcast.48, f32[1024]{0:T(1024)S(1)} %bitcast.52, f32[2048]{0:T(1024)S(1)} %bitcast.46), kind=kOutput, calls=%fused_computation.2 | convolution fusion | flops 417333248 | bytes 221184 | tf_op jit(solution)/shard_map/dot_general | solution.py:55
  174.9 0.0 reduce-scatter.2.cloned.1.call-update
  175.0 0.0 collective-permute-done.2
  175.0 0.0 collective-permute-done.3
  175.0 0.6 gather_fusion
  175.7 0.0 copy-start
  175.7 7.0 %fusion.47 = f32[8,2,8,128]{3,2,1,0:T(8,128)S(1)} fusion(f32[8,8]{1,0:T(8,128)S(1)} %fusion.60, f32[8,8,128]{2,1,0:T(8,128)S(1)} %bitcast.44, f32[8,128]{1,0:T(8,128)S(1)} %bitcast.50, f32[8,8,128]{2,1,0:T(8,128)S(1)} %bitcast.43, f32[8,128]{1,0:T(8,128)S(1)} %bitcast.49, f32[18,8,8,128]{3,0,2,1:T(8,128)S(1)} %bitcast.40), kind=kOutput, calls=%fused_computation.45 | convolution fusion | flops 219168768 | bytes 667648 | tf_op jit(solution)/shard_map/gkpq,rgkq->rgp/dot_general | solution.py:45
  182.7 0.0 reduce-scatter.2.cloned.1.call-done
  182.7 0.0 copy-done
  182.7 1.5 fusion.51
  (13 shorter events, 0.2 us)
Async XLA Ops:
  6.5 140.5 %all-reduce.2.cloned.1.call-start = ((), (), s32[]{:S(2)}) async-start(), calls=%async_computation.1 | async-start | bytes 1048576 | tf_op jit(solution)/shard_map/psum | solution.py:95
  7.5 152.6 %collective-permute-start = (f32[18,1,8,128]{3,0,2,1:T(8,128)S(1)}, f32[18,1,8,128]{3,0,2,1:T(8,128)S(1)}, u32[]{:S(2)}, u32[]{:S(2)}) collective-permute-start(f32[18,1,8,128]{3,0,2,1:T(8,128)S(1)} %copy.7), channel_id=1, source_target_pairs={{0,2},{2,4},{4,6},{6,8},{8,10},{10,12},{12,14},{14,16},{16,18},{18... | collective-permute-start | bytes 221192 | tf_op jit(solution)/shard_map/ppermute | solution.py:24
  12.3 147.8 %collective-permute-start.1 = (f32[18,1,8,128]{3,0,2,1:T(8,128)S(1)}, f32[18,1,8,128]{3,0,2,1:T(8,128)S(1)}, u32[]{:S(2)}, u32[]{:S(2)}) collective-permute-start(f32[18,1,8,128]{3,0,2,1:T(8,128)S(1)} %copy.7), channel_id=1, source_target_pairs={{2,0},{4,2},{6,4},{8,6},{10,8},{12,10},{14,12},{16,14},{18,16},{20... | collective-permute-start | bytes 221192 | tf_op jit(solution)/shard_map/ppermute | solution.py:27
  18.7 17.6 %copy-start.1 = (f32[2,1024]{1,0:T(2,128)S(1)}, f32[2,1024]{1,0:T(2,128)}, u32[]{:S(2)}) copy-start(f32[2,1024]{1,0:T(2,128)} %param.7) | copy-start | bytes 24580
  18.7 17.6 %copy-start.2 = (s32[8,8]{1,0:T(8,128)S(1)}, s32[8,8]{1,0:T(8,128)}, u32[]{:S(2)}) copy-start(s32[8,8]{1,0:T(8,128)} %param.10) | copy-start | bytes 772
  18.7 17.7 %copy-start.3 = (s32[8]{0:T(128)S(1)}, s32[8]{0:T(128)}, u32[]{:S(2)}) copy-start(s32[8]{0:T(128)} %param.11) | copy-start | bytes 100
  36.2 146.5 %reduce-scatter.2.cloned.1.call-start = ((), (), s32[]{:S(2)}) async-start(), calls=%async_computation.2 | async-start | bytes 196608 | tf_op jit(solution)/shard_map/reduce_scatter | solution.py:98
  160.1 14.8 %collective-permute-start.2 = (f32[18,3,1,128]{3,0,2,1:T(8,128)S(1)}, f32[18,3,1,128]{3,0,2,1:T(8,128)S(1)}, u32[]{:S(2)}, u32[]{:S(2)}) collective-permute-start(f32[18,3,1,128]{3,0,2,1:T(8,128)S(1)} %get-tuple-element.7), channel_id=1, source_target_pairs={{0,1},{2,3},{4,5},{6,7},{8,9},{10,11},{12,13},{14,15},{16,17},{18,... | collective-permute-start | bytes 82952 | tf_op jit(solution)/shard_map/ppermute | solution.py:24
  162.2 12.8 %collective-permute-start.3 = (f32[18,3,1,128]{3,0,2,1:T(8,128)S(1)}, f32[18,3,1,128]{3,0,2,1:T(8,128)S(1)}, u32[]{:S(2)}, u32[]{:S(2)}) collective-permute-start(f32[18,3,1,128]{3,0,2,1:T(8,128)S(1)} %get-tuple-element.8), channel_id=1, source_target_pairs={{1,0},{3,2},{5,4},{7,6},{9,8},{11,10},{13,12},{15,14},{17,16},{19,... | collective-permute-start | bytes 82952 | tf_op jit(solution)/shard_map/ppermute | solution.py:27
  175.7 7.0 %copy-start = (f32[16,1024]{1,0:T(8,128)S(1)}, f32[16,1024]{1,0:T(8,128)}, u32[]{:S(2)}) copy-start(f32[16,1024]{1,0:T(8,128)} %param.6) | copy-start | bytes 196612
Sparse Core Ops, SparseCore 0:
  36.3 110.6 all-reduce.1
  175.1 7.3 reduce-scatter.1
where the time goes:
time: 192 us; the launch traced here: 191 us
  waiting for transfers between devices  111 us (58%)
  matrix products  45 us (23%)
  between operations  13.6 us (7%)
  starting transfers between devices  9.74 us (5%)
  blocking collectives  6.82 us (4%)
  other arithmetic  3.56 us (2%)
    psum x1, waiting for transfers between devices, shards(): projection = lax.psum(local_terms, 'space') * proj_scale  111 us
    dot_general x2, matrix products, contract_last(): lax.dot_general(left, right, (((1,), (1,)), ((), ())), precision=PRECISE)  20.6 us
    dot_general x1, matrix products, shards(): local_terms = jnp.dot(gathered_vals, kernel, precision=PRECISE)  17.4 us
    dot_general x1, matrix products, tapered(): return jnp.einsum('gkpq,rgkq->rgp', kernel, near_vals, precision=PRECISE)  6.96 us
    ppermute x2, starting transfers between devices, with_halo(): lax.ppermute(lax.slice_in_dim(block, block.shape[dim] - width, None, axis...  6.89 us
  transfers between devices with their start and end apart: 6, of which 1 were waited for; matrix products, arithmetic and copies ran while one was open for 25% of the time, Pallas kernels for 0%

commit v1 on v0

--- a/solution.py
+++ b/solution.py
@@ -55,6 +55,27 @@
     return lax.dot_general(left, right, (((1,), (1,)), ((), ())), precision=PRECISE)
 
 
+def doubling_sum(value, axis):
+    count = lax.axis_size(axis)
+    if count & (count - 1):
+        return lax.psum(value, axis)
+    step = 1
+    while step < count:
+        value = value + lax.ppermute(value, axis, [(i, i ^ step) for i in range(count)])
+        step *= 2
+    return value
+
+
+def own_share_sum(value, axis, width):
+    count = lax.axis_size(axis)
+    me = lax.axis_index(axis)
+    total = lax.dynamic_slice_in_dim(value, me * width, width, axis=1)
+    for step in range(1, count):
+        share = lax.dynamic_slice_in_dim(value, ((me + step) % count) * width, width, axis=1)
+        total = total + lax.ppermute(share, axis, [(i, (i + step) % count) for i in range(count)])
+    return total
+
+
 def shards(probes, locations, knot_locs, knot_precision, neighbours, counts):
     own_blocks = neighbours.shape[0]
     slot_count = neighbours.shape[1]
@@ -92,10 +113,10 @@
     )
     kernel = knot_kernel(gathered_locs, knot_locs, knot_range)
     local_terms = jnp.dot(gathered_vals, kernel, precision=PRECISE)
-    projection = lax.psum(local_terms, "space") * proj_scale
+    projection = doubling_sum(local_terms, "space") * proj_scale
     factor = contract_last(lax.all_gather(projection, "knot", axis=1, tiled=True), knot_precision)
     spread = contract_last(factor, kernel)
-    low_part = lax.psum_scatter(spread, "knot", scatter_dimension=1, tiled=True)
+    low_part = own_share_sum(spread, "knot", row_count)
     low_part = low_part * EXPAND_GAIN
     return TAPER_SCALE * taper_part + LOW_SCALE * low_part + NUGGET * probes
 

time: 192 us -> 72.8 us (0.38)
  waiting for transfers between devices: 111 us -> 6.79 us
  between operations: 13.6 us -> 0.27 us
  starting transfers between devices: 9.74 us -> 20.5 us
  matrix products: 45 us -> 35.1 us
    psum x1 -> x0, waiting for transfers between devices: 111 us -> none  [shards(): projection = lax.psum(local_terms, 'space') * proj_scale]
    ppermute x0 -> x5, starting transfers between devices: none -> 10 us  [the longest x4 9.82 us: doubling_sum(): lax.ppermute(value, axis, [(i, i ^ step) for i in range(count)])]
    dot_general x1, matrix products: 17.4 us -> 8.52 us  [shards(): local_terms = jnp.dot(gathered_vals, kernel, precision=PRECISE)]
    ppermute x0 -> x5, waiting for transfers between devices: none -> 6.78 us  [the longest x4 6.78 us: doubling_sum(): lax.ppermute(value, axis, [(i, i ^ step) for i in range(count)])]
  transfers between devices with their start and end apart: 6 -> 9, of which waited for: 1 -> 3; matrix products, arithmetic and copies ran while one was open for 25% -> 24% of each run, Pallas kernels for 0% -> 0%
where the time goes in v1:
time: 72.8 us; the launch traced here: 72.4 us
  matrix products  35.1 us (48%)
  starting transfers between devices  20.5 us (28%)
  waiting for transfers between devices  6.79 us (9%)
  blocking collectives  6.35 us (9%)
  other arithmetic  1.68 us (2%)
  local copies, waits for them, and re-layouts  1.68 us (2%)
    dot_general x2, matrix products, contract_last(): lax.dot_general(left, right, (((1,), (1,)), ((), ())), precision=PRECISE)  19.6 us
    ppermute x4, starting transfers between devices, doubling_sum(): lax.ppermute(value, axis, [(i, i ^ step) for i in range(count)])  9.82 us
    dot_general x1, matrix products, shards(): local_terms = jnp.dot(gathered_vals, kernel, precision=PRECISE)  8.52 us
    ppermute x2, starting transfers between devices, with_halo(): lax.ppermute(lax.slice_in_dim(block, block.shape[dim] - width, None, axis...  7.88 us
    dot_general x1, matrix products, tapered(): return jnp.einsum('gkpq,rgkq->rgp', kernel, near_vals, precision=PRECISE)  7.04 us
    ppermute x4, waiting for transfers between devices, doubling_sum(): lax.ppermute(value, axis, [(i, i ^ step) for i in range(count)])  6.78 us
    ppermute x2, starting transfers between devices, with_halo(): lax.ppermute(lax.slice_in_dim(block, 0, width, axis=dim), axis, backward)  2.58 us
    all_gather x1, blocking collectives, shards(): lax.all_gather(probes, 'knot', axis=1, tiled=True)  2.25 us
  transfers between devices with their start and end apart: 9, of which 3 were waited for; matrix products, arithmetic and copies ran while one was open for 24% of the time, Pallas kernels for 0%

profile of v1, /device:TPU:0, one launch (start us, length us, event | category | flops | bytes accessed | tf_op | source)
XLA Modules:
  0.0 72.4 jit_solution(2367726112366100520)
XLA Ops:
  0.0 0.9 %pad_maximum_fusion.1 = f32[18,1024]{1,0:T(8,128)S(1)} fusion(f32[2,1024]{1,0:T(2,128)} %param.7, f32[16,1024]{1,0:T(8,128)} %param.6), kind=kLoop, calls=%fused_computation.48 | loop fusion | flops 18432 | bytes 147456 | tf_op jit(solution)/shard_map/concatenate | solution.py:90
  0.9 4.8 %collective-permute-start = (f32[18,1,8,128]{3,0,2,1:T(8,128)S(1)}, f32[18,1,8,128]{3,0,2,1:T(8,128)S(1)}, u32[]{:S(2)}, u32[]{:S(2)}) collective-permute-start(f32[18,1,8,128]{3,0,2,1:T(8,128)S(1)} %copy.7), channel_id=1, source_target_pairs={{0,2},{2,4},{4,6},{6,8},{8,10},{10,12},{12,14},{14,16},{16,18},{18... | collective-permute-start | bytes 221192 | tf_op jit(solution)/shard_map/ppermute | solution.py:24
  5.8 1.3 %collective-permute-start.1 = (f32[18,1,8,128]{3,0,2,1:T(8,128)S(1)}, f32[18,1,8,128]{3,0,2,1:T(8,128)S(1)}, u32[]{:S(2)}, u32[]{:S(2)}) collective-permute-start(f32[18,1,8,128]{3,0,2,1:T(8,128)S(1)} %copy.7), channel_id=1, source_target_pairs={{2,0},{4,2},{6,4},{8,6},{10,8},{12,10},{14,12},{16,14},{18,16},{20... | collective-permute-start | bytes 221192 | tf_op jit(solution)/shard_map/ppermute | solution.py:27
  7.1 2.3 %all_gather.10 = f32[16,2048]{1,0:T(8,128)S(1)} all-gather(f32[16,1024]{1,0:T(8,128)} %param.6), channel_id=1, replica_groups=mesh['space'=16,'knot'=2] {'knot'}, dimensions={1}, use_global_device_ids=true | all-gather | bytes 196608 | tf_op jit(solution)/shard_map/all_gather | solution.py:111
  9.3 2.0 %all_gather.9 = f32[2,2048]{1,0:T(2,128)S(1)} all-gather(f32[2,1024]{1,0:T(2,128)} %param.7), channel_id=1, replica_groups=mesh['space'=16,'knot'=2] {'knot'}, dimensions={1}, use_global_device_ids=true | all-gather | bytes 24576 | tf_op jit(solution)/shard_map/all_gather | solution.py:112
  11.3 0.8 %fusion.70 = (f32[1,1024]{1,0:T(1,128)S(1)}, f32[1,1024]{1,0:T(1,128)S(1)}) fusion(f32[2,1024]{1,0:T(2,128)} %param.8), kind=kLoop, calls=%fused_computation.84 | loop fusion | bytes 16384 | tf_op jit(solution)/shard_map/slice | solution.py:49
  12.2 0.0 copy-start.1
  12.2 0.0 copy-start.2
  12.2 0.0 copy-start.3
  12.2 8.5 %fusion.43 = f32[16,1024]{1,0:T(8,128)S(1)} fusion(f32[16,2048]{1,0:T(8,128)S(1)} %all_gather.10, f32[1024]{0:T(1024)S(1)} %bitcast.51, f32[2048]{0:T(1024)S(1)} %bitcast.47, f32[1024]{0:T(1024)S(1)} %bitcast.49, f32[2048]{0:T(1024)S(1)} %bitcast.45), kind=kOutput, calls=%fused_computation.43 | convolution fusion | flops 417333248 | bytes 221184 | tf_op jit(solution)/shard_map/dot_general | solution.py:115
  20.7 2.7 %collective-permute-start.4 = (f32[16,1024]{1,0:T(8,128)S(1)}, f32[16,1024]{1,0:T(8,128)S(1)}, u32[]{:S(2)}, u32[]{:S(2)}) collective-permute-start(f32[16,1024]{1,0:T(8,128)S(1)} %fusion.43), channel_id=1, source_target_pairs={{0,2},{2,0},{4,6},{6,4},{8,10},{10,8},{12,14},{14,12},{16,18},{18,... | collective-permute-start | bytes 196616 | tf_op jit(solution)/shard_map/ppermute | solution.py:64
  23.4 0.0 copy-done.1
  23.4 0.0 copy-done.2
  23.5 0.0 copy-done.3
  23.5 0.1 fusion.60
  23.6 0.1 reshape.46
  23.6 2.2 %collective-permute-done.4 = f32[16,1024]{1,0:T(8,128)S(1)} collective-permute-done((f32[16,1024]{1,0:T(8,128)S(1)}, f32[16,1024]{1,0:T(8,128)S(1)}, u32[]{:S(2)}, u32[]{:S(2)}) %collective-permute-start.4) | collective-permute-done | bytes 65568 | tf_op jit(solution)/shard_map/ppermute | solution.py:64
  25.9 2.8 %collective-permute-start.5 = (f32[16,1024]{1,0:T(8,128)S(1)}, f32[16,1024]{1,0:T(8,128)S(1)}, u32[]{:S(2)}, u32[]{:S(2)}) collective-permute-start(f32[16,1024]{1,0:T(8,128)S(1)} %add.68), channel_id=1, source_target_pairs={{0,4},{2,6},{4,0},{6,2},{8,12},{10,14},{12,8},{14,10},{16,20},{18,... | collective-permute-start | bytes 196616 | tf_op jit(solution)/shard_map/ppermute | solution.py:64
  28.7 0.0 collective-permute-done
  28.7 0.0 collective-permute-done.1
  28.8 1.3 %collective-permute-start.3 = (f32[18,3,1,128]{3,0,2,1:T(8,128)S(1)}, f32[18,3,1,128]{3,0,2,1:T(8,128)S(1)}, u32[]{:S(2)}, u32[]{:S(2)}) collective-permute-start(f32[18,3,1,128]{3,0,2,1:T(8,128)S(1)} %get-tuple-element.8), channel_id=1, source_target_pairs={{1,0},{3,2},{5,4},{7,6},{9,8},{11,10},{13,12},{15,14},{17,16},{19,... | collective-permute-start | bytes 82952 | tf_op jit(solution)/shard_map/ppermute | solution.py:27
  30.1 3.0 %collective-permute-start.2 = (f32[18,3,1,128]{3,0,2,1:T(8,128)S(1)}, f32[18,3,1,128]{3,0,2,1:T(8,128)S(1)}, u32[]{:S(2)}, u32[]{:S(2)}) collective-permute-start(f32[18,3,1,128]{3,0,2,1:T(8,128)S(1)} %get-tuple-element.7), channel_id=1, source_target_pairs={{0,1},{2,3},{4,5},{6,7},{8,9},{10,11},{12,13},{14,15},{16,17},{18,... | collective-permute-start | bytes 82952 | tf_op jit(solution)/shard_map/ppermute | solution.py:24
  33.1 0.0 collective-permute-done.5
  33.2 1.6 %collective-permute-start.6 = (f32[16,1024]{1,0:T(8,128)S(1)}, f32[16,1024]{1,0:T(8,128)S(1)}, u32[]{:S(2)}, u32[]{:S(2)}) collective-permute-start(f32[16,1024]{1,0:T(8,128)S(1)} %add.69), channel_id=1, source_target_pairs={{0,8},{2,10},{4,12},{6,14},{8,0},{10,2},{12,4},{14,6},{16,24},{18,... | collective-permute-start | bytes 196616 | tf_op jit(solution)/shard_map/ppermute | solution.py:64
  34.8 0.0 collective-permute-done.3
  34.8 0.0 collective-permute-done.2
  34.8 0.6 gather_fusion
  35.5 2.0 %collective-permute-done.6 = f32[16,1024]{1,0:T(8,128)S(1)} collective-permute-done((f32[16,1024]{1,0:T(8,128)S(1)}, f32[16,1024]{1,0:T(8,128)S(1)}, u32[]{:S(2)}, u32[]{:S(2)}) %collective-permute-start.6) | collective-permute-done | bytes 65568 | tf_op jit(solution)/shard_map/ppermute | solution.py:64
  37.5 2.7 %collective-permute-start.7 = (f32[16,1024]{1,0:T(8,128)S(1)}, f32[16,1024]{1,0:T(8,128)S(1)}, u32[]{:S(2)}, u32[]{:S(2)}) collective-permute-start(f32[16,1024]{1,0:T(8,128)S(1)} %add.70), channel_id=1, source_target_pairs={{0,16},{2,18},{4,20},{6,22},{8,24},{10,26},{12,28},{14,30},{16,0},... | collective-permute-start | bytes 196616 | tf_op jit(solution)/shard_map/ppermute | solution.py:64
  40.2 2.5 %collective-permute-done.7 = f32[16,1024]{1,0:T(8,128)S(1)} collective-permute-done((f32[16,1024]{1,0:T(8,128)S(1)}, f32[16,1024]{1,0:T(8,128)S(1)}, u32[]{:S(2)}, u32[]{:S(2)}) %collective-permute-start.7) | collective-permute-done | bytes 65568 | tf_op jit(solution)/shard_map/ppermute | solution.py:64
  42.8 2.1 %all_gather.11 = f32[16,2048]{1,0:T(8,128)S(1)} all-gather(f32[16,1024]{1,0:T(8,128)S(1)} %add_multiply_fusion), channel_id=1, replica_groups=mesh['space'=16,'knot'=2] {'knot'}, dimensions={1}, use_global_device_ids=true | all-gather | bytes 196608 | tf_op jit(solution)/shard_map/all_gather | solution.py:117
  44.8 9.2 %fusion.72 = f32[16,1024]{1,0:T(8,128)S(1)} fusion(f32[16,2048]{1,0:T(8,128)S(1)} %all_gather.11, f32[1024,2048]{1,0:T(8,128)} %param.9), kind=kOutput, calls=%fused_computation.86 | convolution fusion | flops 402653184 | bytes 8585216 | tf_op jit(solution)/shard_map/dot_general | solution.py:55
  54.0 10.4 %fusion = f32[16,2048]{1,0:T(8,128)S(1)} fusion(f32[16,1024]{1,0:T(8,128)S(1)} %fusion.72, f32[1024]{0:T(1024)S(1)} %bitcast.52, f32[2048]{0:T(1024)S(1)} %bitcast.48, f32[1024]{0:T(1024)S(1)} %bitcast.50, f32[2048]{0:T(1024)S(1)} %bitcast.46), kind=kOutput, calls=%fused_computation.2 | convolution fusion | flops 417333248 | bytes 221184 | tf_op jit(solution)/shard_map/dot_general | solution.py:55
  64.5 0.2 collective-permute-start.8
  64.7 0.0 copy-start
  64.7 7.0 %fusion.47 = f32[8,2,8,128]{3,2,1,0:T(8,128)S(1)} fusion(f32[8,8]{1,0:T(8,128)S(1)} %fusion.60, f32[8,8,128]{2,1,0:T(8,128)S(1)} %bitcast.44, f32[8,128]{1,0:T(8,128)S(1)} %bitcast.54, f32[8,8,128]{2,1,0:T(8,128)S(1)} %bitcast.43, f32[8,128]{1,0:T(8,128)S(1)} %bitcast.53, f32[18,8,8,128]{3,0,2,1:T(8,128)S(1)} %bitcast.40), kind=kOutput, calls=%fused_computation.45 | convolution fusion | flops 219168768 | bytes 667648 | tf_op jit(solution)/shard_map/gkpq,rgkq->rgp/dot_general | solution.py:45
  71.7 0.0 collective-permute-done.8
  71.7 0.0 copy-done
  71.7 0.7 fusion.51
  (18 shorter events, 0.2 us)
Async XLA Ops:
  0.9 27.8 %collective-permute-start = (f32[18,1,8,128]{3,0,2,1:T(8,128)S(1)}, f32[18,1,8,128]{3,0,2,1:T(8,128)S(1)}, u32[]{:S(2)}, u32[]{:S(2)}) collective-permute-start(f32[18,1,8,128]{3,0,2,1:T(8,128)S(1)} %copy.7), channel_id=1, source_target_pairs={{0,2},{2,4},{4,6},{6,8},{8,10},{10,12},{12,14},{14,16},{16,18},{18... | collective-permute-start | bytes 221192 | tf_op jit(solution)/shard_map/ppermute | solution.py:24
  5.8 22.9 %collective-permute-start.1 = (f32[18,1,8,128]{3,0,2,1:T(8,128)S(1)}, f32[18,1,8,128]{3,0,2,1:T(8,128)S(1)}, u32[]{:S(2)}, u32[]{:S(2)}) collective-permute-start(f32[18,1,8,128]{3,0,2,1:T(8,128)S(1)} %copy.7), channel_id=1, source_target_pairs={{2,0},{4,2},{6,4},{8,6},{10,8},{12,10},{14,12},{16,14},{18,16},{20... | collective-permute-start | bytes 221192 | tf_op jit(solution)/shard_map/ppermute | solution.py:27
  12.2 11.3 %copy-start.1 = (f32[2,1024]{1,0:T(2,128)S(1)}, f32[2,1024]{1,0:T(2,128)}, u32[]{:S(2)}) copy-start(f32[2,1024]{1,0:T(2,128)} %param.7) | copy-start | bytes 24580
  12.2 11.3 %copy-start.2 = (s32[8,8]{1,0:T(8,128)S(1)}, s32[8,8]{1,0:T(8,128)}, u32[]{:S(2)}) copy-start(s32[8,8]{1,0:T(8,128)} %param.10) | copy-start | bytes 772
  12.2 11.3 %copy-start.3 = (s32[8]{0:T(128)S(1)}, s32[8]{0:T(128)}, u32[]{:S(2)}) copy-start(s32[8]{0:T(128)} %param.11) | copy-start | bytes 100
  20.7 5.2 %collective-permute-start.4 = (f32[16,1024]{1,0:T(8,128)S(1)}, f32[16,1024]{1,0:T(8,128)S(1)}, u32[]{:S(2)}, u32[]{:S(2)}) collective-permute-start(f32[16,1024]{1,0:T(8,128)S(1)} %fusion.43), channel_id=1, source_target_pairs={{0,2},{2,0},{4,6},{6,4},{8,10},{10,8},{12,14},{14,12},{16,18},{18,... | collective-permute-start | bytes 196616 | tf_op jit(solution)/shard_map/ppermute | solution.py:64
  25.9 7.3 %collective-permute-start.5 = (f32[16,1024]{1,0:T(8,128)S(1)}, f32[16,1024]{1,0:T(8,128)S(1)}, u32[]{:S(2)}, u32[]{:S(2)}) collective-permute-start(f32[16,1024]{1,0:T(8,128)S(1)} %add.68), channel_id=1, source_target_pairs={{0,4},{2,6},{4,0},{6,2},{8,12},{10,14},{12,8},{14,10},{16,20},{18,... | collective-permute-start | bytes 196616 | tf_op jit(solution)/shard_map/ppermute | solution.py:64
  28.8 6.0 %collective-permute-start.3 = (f32[18,3,1,128]{3,0,2,1:T(8,128)S(1)}, f32[18,3,1,128]{3,0,2,1:T(8,128)S(1)}, u32[]{:S(2)}, u32[]{:S(2)}) collective-permute-start(f32[18,3,1,128]{3,0,2,1:T(8,128)S(1)} %get-tuple-element.8), channel_id=1, source_target_pairs={{1,0},{3,2},{5,4},{7,6},{9,8},{11,10},{13,12},{15,14},{17,16},{19,... | collective-permute-start | bytes 82952 | tf_op jit(solution)/shard_map/ppermute | solution.py:27
  30.1 4.7 %collective-permute-start.2 = (f32[18,3,1,128]{3,0,2,1:T(8,128)S(1)}, f32[18,3,1,128]{3,0,2,1:T(8,128)S(1)}, u32[]{:S(2)}, u32[]{:S(2)}) collective-permute-start(f32[18,3,1,128]{3,0,2,1:T(8,128)S(1)} %get-tuple-element.7), channel_id=1, source_target_pairs={{0,1},{2,3},{4,5},{6,7},{8,9},{10,11},{12,13},{14,15},{16,17},{18,... | collective-permute-start | bytes 82952 | tf_op jit(solution)/shard_map/ppermute | solution.py:24
  33.2 4.3 %collective-permute-start.6 = (f32[16,1024]{1,0:T(8,128)S(1)}, f32[16,1024]{1,0:T(8,128)S(1)}, u32[]{:S(2)}, u32[]{:S(2)}) collective-permute-start(f32[16,1024]{1,0:T(8,128)S(1)} %add.69), channel_id=1, source_target_pairs={{0,8},{2,10},{4,12},{6,14},{8,0},{10,2},{12,4},{14,6},{16,24},{18,... | collective-permute-start | bytes 196616 | tf_op jit(solution)/shard_map/ppermute | solution.py:64
  37.5 5.2 %collective-permute-start.7 = (f32[16,1024]{1,0:T(8,128)S(1)}, f32[16,1024]{1,0:T(8,128)S(1)}, u32[]{:S(2)}, u32[]{:S(2)}) collective-permute-start(f32[16,1024]{1,0:T(8,128)S(1)} %add.70), channel_id=1, source_target_pairs={{0,16},{2,18},{4,20},{6,22},{8,24},{10,26},{12,28},{14,30},{16,0},... | collective-permute-start | bytes 196616 | tf_op jit(solution)/shard_map/ppermute | solution.py:64
  64.5 7.3 %collective-permute-start.8 = (f32[16,1024]{1,0:T(8,128)S(1)}, f32[16,1024]{1,0:T(8,128)S(1)}, u32[]{:S(2)}, u32[]{:S(2)}) collective-permute-start(f32[16,1024]{1,0:T(8,128)S(1)} %constant_dynamic-slice_fusion), channel_id=1, source_target_pairs={{0,1},{1,0},{2,3},{3,2},{4,5},{5,4},{6,7},{7,6},{8,9},{9,8},{10,11... | collective-permute-start | bytes 196616 | tf_op jit(solution)/shard_map/ppermute | solution.py:75
  64.7 7.0 %copy-start = (f32[16,1024]{1,0:T(8,128)S(1)}, f32[16,1024]{1,0:T(8,128)}, u32[]{:S(2)}) copy-start(f32[16,1024]{1,0:T(8,128)} %param.6) | copy-start | bytes 196612

commit v2 on v1

v2 whole, which is shorter than its diff:
```python
import functools
import math

import jax
import jax.numpy as jnp
from jax import lax
from jax.experimental import pallas as pl
from jax.experimental.pallas import tpu as pltpu
from jax.sharding import PartitionSpec as P

COV_RANGE = 0.05
TAPER_LEN = 0.15
KNOT_REACH = 0.15
TAPER_SCALE = 0.1
PROJ_GAIN = 0.5
EXPAND_GAIN = 0.5
LOW_SCALE = 0.5
NUGGET = 0.25
LOG2E = math.log2(math.e)
STACK_ROWS = 24
TINY = 1e-30
TILE = 256
LIMIT = 16 * 1024 * 1024
VMEM = pl.BlockSpec(memory_space=pltpu.VMEM)
SMEM = pl.BlockSpec(memory_space=pltpu.SMEM)


def halves(x):
    high = x.astype(jnp.bfloat16)
    return high, (x - high.astype(jnp.float32)).astype(jnp.bfloat16)


def stacked_halves(x):
    return jnp.concatenate(halves(x), axis=0)


def folded(x):
    rows = x.shape[0] // 2
    return x[:rows] + x[rows:]


def dot_nt(left, right):
    return lax.dot_general(
        left, right, (((1,), (1,)), ((), ())), preferred_element_type=jnp.float32
    )


def dot_nn(left, right):
    return jnp.dot(left, right, preferred_element_type=jnp.float32)


def distance(ax, ay, bx, by):
    dx = ax - bx
    dy = ay - by
    square = dx * dx + dy * dy
    return square * lax.rsqrt(jnp.maximum(square, TINY))


def as_columns(rows):
    fill = jnp.zeros((8 - rows.shape[0], rows.shape[1]), rows.dtype)
    return jnp.transpose(jnp.concatenate([rows, fill], axis=0))


def project_kernel(probes, scale, stack_ref, knots_ref, out_ref, high_ref, low_ref, columns, weights):
    knots, points = high_ref.shape
    tile = min(TILE, knots)
    wide = min(TILE, points)
    columns[...] = as_columns(knots_ref[...] * scale)
    weights[...] = stacked_halves(stack_ref[:probes, :])

    @pl.loop(0, knots // tile)
    def _(step):
        rows = pl.ds(pl.multiple_of(step * tile, tile), tile)
        kx = columns[rows, 0:1]
        ky = columns[rows, 1:2]
        total = jnp.zeros((2 * probes, tile), jnp.float32)
        for start in range(0, points, wide):
            lanes = slice(start, start + wide)
            px = stack_ref[probes : probes + 1, lanes] * scale
            py = stack_ref[probes + 1 : probes + 2, lanes] * scale
            high, low = halves(jnp.exp2(-distance(kx, ky, px, py)))
            high_ref[rows, lanes] = high
            low_ref[rows, lanes] = low
            part = weights[:, lanes]
            total = total + (dot_nt(part, high) + dot_nt(part, low))
        out_ref[:, rows] = folded(total)


def project(stack, knot_locs, probes, scale):
    points, knots = stack.shape[1], knot_locs.shape[1]
    pairs = points * knots
    return pl.pallas_call(
        functools.partial(project_kernel, probes, scale),
        out_shape=(
            jax.ShapeDtypeStruct((probes, knots), jnp.float32),
            pltpu.VMEM((knots, points), jnp.bfloat16),
            pltpu.VMEM((knots, points), jnp.bfloat16),
        ),
        in_specs=[VMEM, VMEM],
        out_specs=(VMEM, VMEM, VMEM),
        scratch_shapes=[
            pltpu.VMEM((knots, 8), jnp.float32),
            pltpu.VMEM((2 * probes, points), jnp.bfloat16),
        ],
        compiler_params=pltpu.CompilerParams(vmem_limit_bytes=LIMIT),
        cost_estimate=pl.CostEstimate(flops=128 * pairs, bytes_accessed=4 * pairs, transcendentals=2 * pairs),
        name="project",
    )(stack, knot_locs)


def factor_kernel(scale, proj_ref, precision_ref, out_ref, weights):
    rows_all, depth = precision_ref.shape
    tile = min(TILE, rows_all)
    wide = min(TILE, depth)
    weights[...] = stacked_halves(proj_ref[...] * scale)

    @pl.loop(0, rows_all // tile)
    def _(step):
        rows = pl.ds(pl.multiple_of(step * tile, tile), tile)
        total = jnp.zeros((weights.shape[0], tile), jnp.float32)
        for start in range(0, depth, wide):
            lanes = slice(start, start + wide)
            high, low = halves(precision_ref[rows, lanes])
            part = weights[:, lanes]
            total = total + (dot_nt(part, high) + dot_nt(part, low))
        out_ref[:, rows] = folded(total)


def factored(projection, precision, scale):
    probes, depth = projection.shape
    rows = precision.shape[0]
    return pl.pallas_call(
        functools.partial(factor_kernel, scale),
        out_shape=jax.ShapeDtypeStruct((probes, rows), jnp.float32),
        in_specs=[VMEM, VMEM],
        out_specs=VMEM,
        scratch_shapes=[pltpu.VMEM((2 * probes, depth), jnp.bfloat16)],
        compiler_params=pltpu.CompilerParams(vmem_limit_bytes=LIMIT),
        cost_estimate=pl.CostEstimate(flops=128 * rows * depth, bytes_accessed=4 * rows * depth, transcendentals=0),
        name="factor",
    )(projection, precision)


def spread_kernel(scale, factor_ref, high_ref, low_ref, out_ref):
    points = high_ref.shape[1]
    wide = min(TILE, points)
    part = stacked_halves(factor_ref[...] * scale)
    for start in range(0, points, wide):
        lanes = slice(start, start + wide)
        out_ref[:, lanes] = folded(dot_nn(part, high_ref[:, lanes]) + dot_nn(part, low_ref[:, lanes]))


def spread(factor, high, low, scale):
    probes, points = factor.shape[0], high.shape[1]
    high = pltpu.with_memory_space_constraint(high, pltpu.VMEM)
    low = pltpu.with_memory_space_constraint(low, pltpu.VMEM)
    return pl.pallas_call(
        functools.partial(spread_kernel, scale),
        out_shape=jax.ShapeDtypeStruct((probes, points), jnp.float32),
        in_specs=[VMEM, VMEM, VMEM],
        out_specs=VMEM,
        compiler_params=pltpu.CompilerParams(vmem_limit_bytes=LIMIT),
        cost_estimate=pl.CostEstimate(flops=128 * high.size, bytes_accessed=4 * high.size, transcendentals=0),
        name="spread",
    )(factor, high, low)


def taper_kernel(probes, first, ids_ref, counts_ref, own_ref, near_ref, out_ref):
    slots = ids_ref.shape[1]
    block = own_ref.shape[1] // ids_ref.shape[0]
    inverse = 1.0 / TAPER_LEN
    decay = -LOG2E * TAPER_LEN / COV_RANGE
    for index in range(out_ref.shape[1] // block):
        group = first + index
        here = slice(group * block, (group + 1) * block)
        own = as_columns(own_ref[probes : probes + 2, here] * inverse)
        px = own[:, 0:1]
        py = own[:, 1:2]
        total = jnp.zeros((2 * probes, block), jnp.float32)
        for slot in range(slots):
            lanes = pl.ds(pl.multiple_of(ids_ref[group, slot] * block, block), block)
            live = jnp.where(slot < counts_ref[group], 1.0, 0.0)
            qx = near_ref[probes : probes + 1, lanes] * inverse
            qy = near_ref[probes + 1 : probes + 2, lanes] * inverse
            scaled = jnp.minimum(distance(px, py, qx, qy), 1.0)
            remain = (1.0 - scaled) * (1.0 - scaled)
            covariance = jnp.exp2(scaled * decay) * (remain * remain) * (1.0 + 4.0 * scaled)
            high, low = halves(covariance)
            part = stacked_halves(near_ref[:probes, lanes] * live)
            total = total + (dot_nt(part, high) + dot_nt(part, low))
        out_ref[:, index * block : (index + 1) * block] = (
            TAPER_SCALE * folded(total) + NUGGET * own_ref[:probes, here]
        )


def taper(ids, counts, own, near, probes, first, blocks):
    block = own.shape[1] // ids.shape[0]
    pairs = blocks * ids.shape[1] * block * block
    return pl.pallas_call(
        functools.partial(taper_kernel, probes, first),
        out_shape=jax.ShapeDtypeStruct((probes, blocks * block), jnp.float32),
        in_specs=[SMEM, SMEM, VMEM, VMEM],
        out_specs=VMEM,
        compiler_params=pltpu.CompilerParams(vmem_limit_bytes=LIMIT),
        cost_estimate=pl.CostEstimate(flops=512 * pairs, bytes_accessed=4 * pairs, transcendentals=2 * pairs),
        name="taper",
    )(ids, counts, own, near)


def doubling_sum(value, axis):
    count = lax.axis_size(axis)
    if count & (count - 1):
        return lax.psum(value, axis)
    step = 1
    while step < count:
        value = value + lax.ppermute(value, axis, [(i, i ^ step) for i in range(count)])
        step *= 2
    return value


def shifted(value, axis, step):
    count = lax.axis_size(axis)
    if step % count == 0:
        return value
    return lax.ppermute(value, axis, [((i + step) % count, i) for i in range(count)])


def paired(value, axis, first):
    count = lax.axis_size(axis)
    pairs = [(i, i + 1) for i in range(first, count - 1, 2)]
    return lax.ppermute(value, axis, pairs + [(b, a) for a, b in pairs])


def shards(probes, locations, knot_locs, knot_precision, neighbours, counts):
    own_blocks = neighbours.shape[0]
    probe_count, row_count = probes.shape
    block_len = row_count // own_blocks
    knot_total = knot_precision.shape[1]
    device_count = lax.axis_size(("space", "knot"))
    groups = lax.axis_size("knot")
    north_cells = groups * own_blocks
    knot_range = KNOT_REACH * math.sqrt(own_blocks * device_count / knot_total)
    proj_scale = PROJ_GAIN * math.sqrt(knot_total / (row_count * device_count))
    column = lax.axis_index("space")

    fill = jnp.zeros((STACK_ROWS - probe_count - 2, row_count), jnp.float32)
    stack = jnp.concatenate([probes, locations, fill], axis=0)
    chunks = [shifted(stack, "knot", step) for step in range(groups)]

    own_strip = jnp.concatenate(
        [chunks[-1][:, row_count - block_len :], stack, chunks[1 % groups][:, :block_len]], axis=1
    )
    near = jnp.concatenate(
        [own_strip, paired(own_strip, "space", 0), paired(own_strip, "space", 1)], axis=1
    )
    move = neighbours // north_cells - column
    east_strip = 1 + column % 2
    strip = jnp.where(move == 0, 0, jnp.where(move > 0, east_strip, 3 - east_strip))
    north = neighbours % north_cells - lax.axis_index("knot") * own_blocks + 1
    ids = strip * (own_blocks + 2) + north
    pieces = math.gcd(own_blocks, 4)
    per_piece = own_blocks // pieces
    base = jnp.concatenate(
        [taper(ids, counts, stack, near, probe_count, i * per_piece, per_piece) for i in range(pieces)],
        axis=1,
    )

    rate = LOG2E / knot_range
    parts = [project(chunk, knot_locs, probe_count, rate) for chunk in chunks]
    projection = doubling_sum(sum(part[0] for part in parts), "space")
    projection = lax.all_gather(projection, "knot", axis=1, tiled=True)
    factor = factored(projection, knot_precision, proj_scale)
    total = base
    for step in reversed(range(groups)):
        share = spread(factor, parts[step][1], parts[step][2], LOW_SCALE * EXPAND_GAIN)
        total = total + shifted(share, "knot", -step)
    return total


def solution(mesh):
    return jax.shard_map(
        shards,
        mesh=mesh,
        in_specs=(
            P(None, ("space", "knot")),
            P(None, ("space", "knot")),
            P(None, "knot"),
            P("knot", None),
            P(("space", "knot"), None),
            P(("space", "knot")),
        ),
        out_specs=P(None, ("space", "knot")),
        check_vma=False,
    )
```

time: 72.8 us -> 47 us (0.65)
  matrix products: 35.1 us -> 0 us
  Pallas kernels: 0 us -> 18.6 us
  starting transfers between devices: 20.5 us -> 15.8 us
  blocking collectives: 6.35 us -> 1.9 us
  local copies, waits for them, and re-layouts: 1.68 us -> 0.73 us
    dot_general x4 -> x0, matrix products: 35.1 us -> none  [the longest x2 19.6 us: contract_last(): lax.dot_general(left, right, (((1,), (1,)), ((), ())), precision=PRECISE)]
    pallas_call x0 -> x9, Pallas kernels: none -> 18.6 us  [the longest x2 7.18 us: project(): pl.pallas_call(functools.partial(project_kernel, probes, scale), out_shap...]
    ppermute x5 -> x4, starting transfers between devices: 10.7 us -> 5.65 us  [the longest x2 4.96 us: paired(): return lax.ppermute(value, axis, pairs + [(b, a) for a, b in pairs])]
    all_gather x3 -> x1, blocking collectives: 6.35 us -> 1.9 us  [shards(): projection = lax.all_gather(projection, 'knot', axis=1, tiled=True)]
    slice x5 -> x1, local copies, waits for them, and re-layouts: 0.85 us -> 0.01 us  [shards(): chunks[-1][:, row_count - block_len:]]
    add x1 -> x3, other arithmetic: 0.65 us -> 1.39 us  [the longest x1 0.7 us: shards(): ids = strip * (own_blocks + 2) + north]
  transfers between devices with their start and end apart: 9 -> 8, of which waited for: 3 -> 3; matrix products, arithmetic and copies ran while one was open for 24% -> 2% of each run, Pallas kernels for 0% -> 32%
where the time goes in v2:
time: 47 us; the launch traced here: 46.8 us
  Pallas kernels  18.6 us (40%)
  starting transfers between devices  15.8 us (34%)
  waiting for transfers between devices  7.24 us (15%)
  other arithmetic  2.38 us (5%)
  blocking collectives  1.9 us (4%)
  local copies, waits for them, and re-layouts  0.73 us (2%)
    ppermute x4, starting transfers between devices, doubling_sum(): lax.ppermute(value, axis, [(i, i ^ step) for i in range(count)])  10.1 us
    ppermute x4, waiting for transfers between devices, doubling_sum(): lax.ppermute(value, axis, [(i, i ^ step) for i in range(count)])  7.23 us
    pallas_call x2, Pallas kernels, project(): pl.pallas_call(functools.partial(project_kernel, probes, scale), out_shap...  7.18 us
    pallas_call x4, Pallas kernels, taper(): pl.pallas_call(functools.partial(taper_kernel, probes, first), out_shape=...  6.96 us
    ppermute x2, starting transfers between devices, paired(): return lax.ppermute(value, axis, pairs + [(b, a) for a, b in pairs])  4.96 us
    pallas_call x1, Pallas kernels, factored(): pl.pallas_call(functools.partial(factor_kernel, scale), out_shape=jax.Sha...  2.88 us
    all_gather x1, blocking collectives, shards(): projection = lax.all_gather(projection, 'knot', axis=1, tiled=True)  1.9 us
    pallas_call x2, Pallas kernels, spread(): pl.pallas_call(functools.partial(spread_kernel, scale), out_shape=jax.Sha...  1.55 us
  transfers between devices with their start and end apart: 8, of which 3 were waited for; matrix products, arithmetic and copies ran while one was open for 2% of the time, Pallas kernels for 32%

profile of v2, /device:TPU:0, one launch (start us, length us, event | category | flops | bytes accessed | tf_op | source)
XLA Modules:
  0.0 46.8 jit_solution(6884329176459534904)
XLA Ops:
  0.0 0.0 copy-start.3
  0.0 0.0 copy-start.4
  0.0 0.9 %pad_maximum_fusion.1.own_ref.stack_ref = f32[24,1024]{1,0:T(8,128)S(1)} fusion(f32[6,1024]{1,0:T(8,128)S(1)} %broadcast_in_dim.15, f32[2,1024]{1,0:T(2,128)} %param.7, f32[16,1024]{1,0:T(8,128)} %param.6), kind=kLoop, calls=%fused_computation.1 | loop fusion | flops 49152 | bytes 196608 | tf_op jit(solution)/shard_map/concatenate | solution.py:247
  0.9 0.5 %collective-permute-start = (f32[24,1024]{1,0:T(8,128)S(1)}, f32[24,1024]{1,0:T(8,128)S(1)}, u32[]{:S(2)}, u32[]{:S(2)}) collective-permute-start(f32[24,1024]{1,0:T(8,128)S(1)} %pad_maximum_fusion.1.own_ref.stack_ref), channel_id=1, source_target_pairs={{1,0},{0,1},{3,2},{2,3},{5,4},{4,5},{7,6},{6,7},{9,8},{8,9},{11,10... | collective-permute-start | bytes 294920 | tf_op jit(solution)/shard_map/ppermute | solution.py:225
  1.5 0.7 %fusion.4.ids_ref = s32[8,8]{1,0:T(8,128)S(1)} fusion(s32[8,8]{1,0:T(8,128)} %param.10, s32[]{:T(128)S(6)} %mul.11, s32[]{:T(128)S(6)} %sub.24, s32[]{:T(128)S(6)} %add.43, s32[]{:T(128)S(6)} %axis_index.23), kind=kLoop, calls=%fused_computation.17 | loop fusion | flops 1792 | bytes 528 | tf_op jit(solution)/shard_map/add | solution.py:260
  2.2 0.0 copy-start.1
  2.2 0.7 %copy-done.1 = f32[2,1024]{1,0:T(2,128)S(1)} copy-done((f32[2,1024]{1,0:T(2,128)S(1)}, f32[2,1024]{1,0:T(2,128)}, u32[]{:S(2)}) %copy-start.1) | copy-done | bytes 8216
  2.9 0.0 copy-start
  2.9 3.6 %project.2 = (f32[16,1024]{1,0:T(8,128)S(1)}, bf16[1024,1024]{1,0:T(8,128)(2,1)S(1)}, bf16[1024,1024]{1,0:T(8,128)(2,1)S(1)}) custom-call(f32[24,1024]{1,0:T(8,128)S(1)} %pad_maximum_fusion.1.own_ref.stack_ref, f32[2,1024]{1,0:T(2,128)S(1)} %copy-done.1), custom_call_target="tpu_custom_call" | custom-call | flops 134217728 | bytes 4194304 | tf_op jit(solution)/shard_map/project/pallas_call | solution.py:92
  6.4 0.0 collective-permute-done.stack_ref
  6.4 3.6 %project.3 = (f32[16,1024]{1,0:T(8,128)S(1)}, bf16[1024,1024]{1,0:T(8,128)(2,1)S(1)}, bf16[1024,1024]{1,0:T(8,128)(2,1)S(1)}) custom-call(f32[24,1024]{1,0:T(8,128)S(1)} %collective-permute-done.stack_ref, f32[2,1024]{1,0:T(2,128)S(1)} %copy-done.1), custom_call_target="tpu_custom_call" | custom-call | flops 134217728 | bytes 4194304 | tf_op jit(solution)/shard_map/project/pallas_call | solution.py:92
  10.1 2.6 %collective-permute-start.3 = (f32[16,1024]{1,0:T(8,128)S(1)}, f32[16,1024]{1,0:T(8,128)S(1)}, u32[]{:S(2)}, u32[]{:S(2)}) collective-permute-start(f32[16,1024]{1,0:T(8,128)S(1)} %add.47), channel_id=1, source_target_pairs={{0,2},{2,0},{4,6},{6,4},{8,10},{10,8},{12,14},{14,12},{16,18},{18,... | collective-permute-start | bytes 196616 | tf_op jit(solution)/shard_map/ppermute | solution.py:216
  12.7 0.0 copy-done.3
  12.7 0.0 copy-done.4
  12.7 0.7 %collective-permute-start.2 = (f32[24,1280]{1,0:T(8,128)S(1)}, f32[24,1280]{1,0:T(8,128)S(1)}, u32[]{:S(2)}, u32[]{:S(2)}) collective-permute-start(f32[24,1280]{1,0:T(8,128)S(1)} %pad_maximum_fusion), channel_id=1, source_target_pairs={{2,4},{6,8},{10,12},{14,16},{18,20},{22,24},{26,28},{4,2},{8,6},{1... | collective-permute-start | bytes 368648 | tf_op jit(solution)/shard_map/ppermute | solution.py:231
  13.4 4.3 %collective-permute-start.1 = (f32[24,1280]{1,0:T(8,128)S(1)}, f32[24,1280]{1,0:T(8,128)S(1)}, u32[]{:S(2)}, u32[]{:S(2)}) collective-permute-start(f32[24,1280]{1,0:T(8,128)S(1)} %pad_maximum_fusion), channel_id=1, source_target_pairs={{0,2},{4,6},{8,10},{12,14},{16,18},{20,22},{24,26},{28,30},{2,0},{... | collective-permute-start | bytes 368648 | tf_op jit(solution)/shard_map/ppermute | solution.py:231
  17.7 0.0 collective-permute-done.3
  17.7 1.6 %collective-permute-start.4 = (f32[16,1024]{1,0:T(8,128)S(1)}, f32[16,1024]{1,0:T(8,128)S(1)}, u32[]{:S(2)}, u32[]{:S(2)}) collective-permute-start(f32[16,1024]{1,0:T(8,128)S(1)} %add.48), channel_id=1, source_target_pairs={{0,4},{2,6},{4,0},{6,2},{8,12},{10,14},{12,8},{14,10},{16,20},{18,... | collective-permute-start | bytes 196616 | tf_op jit(solution)/shard_map/ppermute | solution.py:216
  19.3 2.7 %collective-permute-done.4 = f32[16,1024]{1,0:T(8,128)S(1)} collective-permute-done((f32[16,1024]{1,0:T(8,128)S(1)}, f32[16,1024]{1,0:T(8,128)S(1)}, u32[]{:S(2)}, u32[]{:S(2)}) %collective-permute-start.4) | collective-permute-done | bytes 65568 | tf_op jit(solution)/shard_map/ppermute | solution.py:216
  22.0 2.9 %collective-permute-start.5 = (f32[16,1024]{1,0:T(8,128)S(1)}, f32[16,1024]{1,0:T(8,128)S(1)}, u32[]{:S(2)}, u32[]{:S(2)}) collective-permute-start(f32[16,1024]{1,0:T(8,128)S(1)} %add.49), channel_id=1, source_target_pairs={{0,8},{2,10},{4,12},{6,14},{8,0},{10,2},{12,4},{14,6},{16,24},{18,... | collective-permute-start | bytes 196616 | tf_op jit(solution)/shard_map/ppermute | solution.py:216
  24.9 2.3 %collective-permute-done.5 = f32[16,1024]{1,0:T(8,128)S(1)} collective-permute-done((f32[16,1024]{1,0:T(8,128)S(1)}, f32[16,1024]{1,0:T(8,128)S(1)}, u32[]{:S(2)}, u32[]{:S(2)}) %collective-permute-start.5) | collective-permute-done | bytes 65568 | tf_op jit(solution)/shard_map/ppermute | solution.py:216
  27.2 3.1 %collective-permute-start.6 = (f32[16,1024]{1,0:T(8,128)S(1)}, f32[16,1024]{1,0:T(8,128)S(1)}, u32[]{:S(2)}, u32[]{:S(2)}) collective-permute-start(f32[16,1024]{1,0:T(8,128)S(1)} %add.50), channel_id=1, source_target_pairs={{0,16},{2,18},{4,20},{6,22},{8,24},{10,26},{12,28},{14,30},{16,0},... | collective-permute-start | bytes 196616 | tf_op jit(solution)/shard_map/ppermute | solution.py:216
  30.3 0.0 collective-permute-done.1
  30.3 2.2 %collective-permute-done.6 = f32[16,1024]{1,0:T(8,128)S(1)} collective-permute-done((f32[16,1024]{1,0:T(8,128)S(1)}, f32[16,1024]{1,0:T(8,128)S(1)}, u32[]{:S(2)}, u32[]{:S(2)}) %collective-permute-start.6) | collective-permute-done | bytes 65568 | tf_op jit(solution)/shard_map/ppermute | solution.py:216
  32.5 1.9 %all_gather.3.proj_ref = f32[16,2048]{1,0:T(8,128)S(1)} all-gather(f32[16,1024]{1,0:T(8,128)S(1)} %add.51), channel_id=1, replica_groups=mesh['space'=16,'knot'=2] {'knot'}, dimensions={1}, use_global_device_ids=true | all-gather | bytes 196608 | tf_op jit(solution)/shard_map/all_gather | solution.py:271
  34.4 0.0 copy-done
  34.4 2.9 %factor.1.factor_ref = f32[16,1024]{1,0:T(8,128)S(1)} custom-call(f32[16,2048]{1,0:T(8,128)S(1)} %all_gather.3.proj_ref, f32[1024,2048]{1,0:T(8,128)S(1)} %copy-done), custom_call_target="tpu_custom_call" | custom-call | flops 268435456 | bytes 8388608 | tf_op jit(solution)/shard_map/factor/pallas_call | solution.py:132
  37.3 0.0 copy-start.2
  37.3 0.8 %spread.2 = f32[16,1024]{1,0:T(8,128)S(1)} custom-call(f32[16,1024]{1,0:T(8,128)S(1)} %factor.1.factor_ref, bf16[1024,1024]{1,0:T(8,128)(2,1)S(1)} %get-tuple-element.13.high_ref, bf16[1024,1024]{1,0:T(8,128)(2,1)S(1)} %get-tuple-element.14.low_ref), custom_call_target="tpu_custom_call" | custom-call | flops 134217728 | bytes 4194304 | tf_op jit(solution)/shard_map/spread/pallas_call | solution.py:157
  38.1 0.2 collective-permute-start.7
  38.3 0.0 collective-permute-done.2
  38.3 0.0 copy-done.2
  38.3 1.7 %taper.7 = f32[16,256]{1,0:T(8,128)S(1)} custom-call(s32[8,8]{1,0:T(8,128)S(1)} %fusion.4.ids_ref, s32[8]{0:T(128)S(1)} %copy-done.2, f32[24,1024]{1,0:T(8,128)S(1)} %pad_maximum_fusion.1.own_ref.stack_ref, f32[24,3840]{1,0:T(8,128)S(1)} %constant_dynamic-update-slice_fusion.near_ref), custom_call_target="tpu_custom_call" | custom-call | flops 134217728 | bytes 1048576 | tf_op jit(solution)/shard_map/taper/pallas_call | solution.py:199
  40.1 1.7 %taper.6 = f32[16,256]{1,0:T(8,128)S(1)} custom-call(s32[8,8]{1,0:T(8,128)S(1)} %fusion.4.ids_ref, s32[8]{0:T(128)S(1)} %copy-done.2, f32[24,1024]{1,0:T(8,128)S(1)} %pad_maximum_fusion.1.own_ref.stack_ref, f32[24,3840]{1,0:T(8,128)S(1)} %constant_dynamic-update-slice_fusion.near_ref), custom_call_target="tpu_custom_call" | custom-call | flops 134217728 | bytes 1048576 | tf_op jit(solution)/shard_map/taper/pallas_call | solution.py:199
  41.8 1.7 %taper.5 = f32[16,256]{1,0:T(8,128)S(1)} custom-call(s32[8,8]{1,0:T(8,128)S(1)} %fusion.4.ids_ref, s32[8]{0:T(128)S(1)} %copy-done.2, f32[24,1024]{1,0:T(8,128)S(1)} %pad_maximum_fusion.1.own_ref.stack_ref, f32[24,3840]{1,0:T(8,128)S(1)} %constant_dynamic-update-slice_fusion.near_ref), custom_call_target="tpu_custom_call" | custom-call | flops 134217728 | bytes 1048576 | tf_op jit(solution)/shard_map/taper/pallas_call | solution.py:199
  43.6 1.7 %taper.4 = f32[16,256]{1,0:T(8,128)S(1)} custom-call(s32[8,8]{1,0:T(8,128)S(1)} %fusion.4.ids_ref, s32[8]{0:T(128)S(1)} %copy-done.2, f32[24,1024]{1,0:T(8,128)S(1)} %pad_maximum_fusion.1.own_ref.stack_ref, f32[24,3840]{1,0:T(8,128)S(1)} %constant_dynamic-update-slice_fusion.near_ref), custom_call_target="tpu_custom_call" | custom-call | flops 134217728 | bytes 1048576 | tf_op jit(solution)/shard_map/taper/pallas_call | solution.py:199
  45.3 0.8 %spread.3 = f32[16,1024]{1,0:T(8,128)S(1)} custom-call(f32[16,1024]{1,0:T(8,128)S(1)} %factor.1.factor_ref, bf16[1024,1024]{1,0:T(8,128)(2,1)S(1)} %get-tuple-element.15.high_ref, bf16[1024,1024]{1,0:T(8,128)(2,1)S(1)} %get-tuple-element.16.low_ref), custom_call_target="tpu_custom_call" | custom-call | flops 134217728 | bytes 4194304 | tf_op jit(solution)/shard_map/spread/pallas_call | solution.py:157
  46.1 0.0 collective-permute-done.7
  46.1 0.7 %fusion = f32[16,1024]{1,0:T(8,128)} fusion(f32[16,1024]{1,0:T(8,128)S(1)} %spread.3, f32[16,1024]{1,0:T(8,128)S(1)} %collective-permute-done.7, f32[16,256]{1,0:T(8,128)S(1)} %taper.7, f32[16,256]{1,0:T(8,128)S(1)} %taper.6, f32[16,256]{1,0:T(8,128)S(1)} %taper.5, f32[16,256]{1,0:T(8,128)S(1)} %taper.4), kind=kLoop, calls=%fused_computation.3 | loop fusion | flops 81920 | bytes 262144 | tf_op jit(solution)/shard_map/add | solution.py:276
  (12 shorter events, 0.1 us)
Async XLA Ops:
  0.0 12.7 %copy-start.3 = (f32[16,1024]{1,0:T(8,128)S(1)}, f32[16,1024]{1,0:T(8,128)}, u32[]{:S(2)}) copy-start(f32[16,1024]{1,0:T(8,128)} %param.6) | copy-start | bytes 196612
  0.0 12.7 %copy-start.4 = (f32[2,1024]{1,0:T(2,128)S(1)}, f32[2,1024]{1,0:T(2,128)}, u32[]{:S(2)}) copy-start(f32[2,1024]{1,0:T(2,128)} %param.7) | copy-start | bytes 24580
  0.9 5.5 %collective-permute-start = (f32[24,1024]{1,0:T(8,128)S(1)}, f32[24,1024]{1,0:T(8,128)S(1)}, u32[]{:S(2)}, u32[]{:S(2)}) collective-permute-start(f32[24,1024]{1,0:T(8,128)S(1)} %pad_maximum_fusion.1.own_ref.stack_ref), channel_id=1, source_target_pairs={{1,0},{0,1},{3,2},{2,3},{5,4},{4,5},{7,6},{6,7},{9,8},{8,9},{11,10... | collective-permute-start | bytes 294920 | tf_op jit(solution)/shard_map/ppermute | solution.py:225
  2.2 0.7 %copy-start.1 = (f32[2,1024]{1,0:T(2,128)S(1)}, f32[2,1024]{1,0:T(2,128)}, u32[]{:S(2)}) copy-start(f32[2,1024]{1,0:T(2,128)} %knots_ref.3) | copy-start | bytes 24580
  2.9 31.6 %copy-start = (f32[1024,2048]{1,0:T(8,128)S(1)}, f32[1024,2048]{1,0:T(8,128)}, u32[]{:S(2)}) copy-start(f32[1024,2048]{1,0:T(8,128)} %precision_ref.1) | copy-start | bytes 25165828
  10.1 7.6 %collective-permute-start.3 = (f32[16,1024]{1,0:T(8,128)S(1)}, f32[16,1024]{1,0:T(8,128)S(1)}, u32[]{:S(2)}, u32[]{:S(2)}) collective-permute-start(f32[16,1024]{1,0:T(8,128)S(1)} %add.47), channel_id=1, source_target_pairs={{0,2},{2,0},{4,6},{6,4},{8,10},{10,8},{12,14},{14,12},{16,18},{18,... | collective-permute-start | bytes 196616 | tf_op jit(solution)/shard_map/ppermute | solution.py:216
  12.7 25.6 %collective-permute-start.2 = (f32[24,1280]{1,0:T(8,128)S(1)}, f32[24,1280]{1,0:T(8,128)S(1)}, u32[]{:S(2)}, u32[]{:S(2)}) collective-permute-start(f32[24,1280]{1,0:T(8,128)S(1)} %pad_maximum_fusion), channel_id=1, source_target_pairs={{2,4},{6,8},{10,12},{14,16},{18,20},{22,24},{26,28},{4,2},{8,6},{1... | collective-permute-start | bytes 368648 | tf_op jit(solution)/shard_map/ppermute | solution.py:231
  13.4 16.9 %collective-permute-start.1 = (f32[24,1280]{1,0:T(8,128)S(1)}, f32[24,1280]{1,0:T(8,128)S(1)}, u32[]{:S(2)}, u32[]{:S(2)}) collective-permute-start(f32[24,1280]{1,0:T(8,128)S(1)} %pad_maximum_fusion), channel_id=1, source_target_pairs={{0,2},{4,6},{8,10},{12,14},{16,18},{20,22},{24,26},{28,30},{2,0},{... | collective-permute-start | bytes 368648 | tf_op jit(solution)/shard_map/ppermute | solution.py:231
  17.7 4.3 %collective-permute-start.4 = (f32[16,1024]{1,0:T(8,128)S(1)}, f32[16,1024]{1,0:T(8,128)S(1)}, u32[]{:S(2)}, u32[]{:S(2)}) collective-permute-start(f32[16,1024]{1,0:T(8,128)S(1)} %add.48), channel_id=1, source_target_pairs={{0,4},{2,6},{4,0},{6,2},{8,12},{10,14},{12,8},{14,10},{16,20},{18,... | collective-permute-start | bytes 196616 | tf_op jit(solution)/shard_map/ppermute | solution.py:216
  22.0 5.2 %collective-permute-start.5 = (f32[16,1024]{1,0:T(8,128)S(1)}, f32[16,1024]{1,0:T(8,128)S(1)}, u32[]{:S(2)}, u32[]{:S(2)}) collective-permute-start(f32[16,1024]{1,0:T(8,128)S(1)} %add.49), channel_id=1, source_target_pairs={{0,8},{2,10},{4,12},{6,14},{8,0},{10,2},{12,4},{14,6},{16,24},{18,... | collective-permute-start | bytes 196616 | tf_op jit(solution)/shard_map/ppermute | solution.py:216
  27.2 5.3 %collective-permute-start.6 = (f32[16,1024]{1,0:T(8,128)S(1)}, f32[16,1024]{1,0:T(8,128)S(1)}, u32[]{:S(2)}, u32[]{:S(2)}) collective-permute-start(f32[16,1024]{1,0:T(8,128)S(1)} %add.50), channel_id=1, source_target_pairs={{0,16},{2,18},{4,20},{6,22},{8,24},{10,26},{12,28},{14,30},{16,0},... | collective-permute-start | bytes 196616 | tf_op jit(solution)/shard_map/ppermute | solution.py:216
  37.3 1.0 %copy-start.2 = (s32[8]{0:T(128)S(1)}, s32[8]{0:T(128)}, u32[]{:S(2)}) copy-start(s32[8]{0:T(128)} %counts_ref.7) | copy-start | bytes 100
  38.1 8.0 %collective-permute-start.7 = (f32[16,1024]{1,0:T(8,128)S(1)}, f32[16,1024]{1,0:T(8,128)S(1)}, u32[]{:S(2)}, u32[]{:S(2)}) collective-permute-start(f32[16,1024]{1,0:T(8,128)S(1)} %spread.2), channel_id=1, source_target_pairs={{1,0},{0,1},{3,2},{2,3},{5,4},{4,5},{7,6},{6,7},{9,8},{8,9},{11,10... | collective-permute-start | bytes 196616 | tf_op jit(solution)/shard_map/ppermute | solution.py:225

commit v3 on v2

--- a/solution.py
+++ b/solution.py
@@ -207,15 +207,16 @@
     )(ids, counts, own, near)
 
 
-def doubling_sum(value, axis):
-    count = lax.axis_size(axis)
-    if count & (count - 1):
-        return lax.psum(value, axis)
-    step = 1
-    while step < count:
-        value = value + lax.ppermute(value, axis, [(i, i ^ step) for i in range(count)])
-        step *= 2
-    return value
+def gathered_sum(value, axis, other):
+    rows, width = value.shape
+    count, groups = lax.axis_size(axis), lax.axis_size(other)
+    shares = value.reshape(count, rows * width // count)
+    shares = lax.all_to_all(shares, axis, 0, 0, tiled=True)
+    share = jnp.sum(shares, axis=0, keepdims=True)
+    copies = jnp.broadcast_to(share, (count * groups, share.shape[1]))
+    whole = lax.all_to_all(copies, (axis, other), 0, 0, tiled=True)
+    whole = jnp.swapaxes(whole.reshape(count, groups, -1), 0, 1).reshape(groups, rows, width)
+    return jnp.swapaxes(whole, 0, 1).reshape(rows, groups * width)
 
 
 def shifted(value, axis, step):
@@ -267,8 +268,7 @@
 
     rate = LOG2E / knot_range
     parts = [project(chunk, knot_locs, probe_count, rate) for chunk in chunks]
-    projection = doubling_sum(sum(part[0] for part in parts), "space")
-    projection = lax.all_gather(projection, "knot", axis=1, tiled=True)
+    projection = gathered_sum(sum(part[0] for part in parts), "space", "knot")
     factor = factored(projection, knot_precision, proj_scale)
     total = base
     for step in reversed(range(groups)):

time: 47 us -> 58.4 us (1.24)
  local copies, waits for them, and re-layouts: 0.73 us -> 9.65 us
  waiting for transfers between devices: 7.24 us -> 10.4 us
  blocking collectives: 1.9 us -> 0 us
  starting transfers between devices: 15.8 us -> 16.6 us
    all_to_all x0 -> x2, starting transfers between devices: none -> 10.4 us  [the longest x1 7.89 us: gathered_sum(): shares = lax.all_to_all(shares, axis, 0, 0, tiled=True)]
    ppermute x4 -> x0, starting transfers between devices: 10.1 us -> none  [doubling_sum(): lax.ppermute(value, axis, [(i, i ^ step) for i in range(count)])]
    all_to_all x0 -> x2, waiting for transfers between devices: none -> 10.1 us  [the longest x1 7.89 us: gathered_sum(): whole = lax.all_to_all(copies, (axis, other), 0, 0, tiled=True)]
    unnamed x12 -> x24, local copies, waits for them, and re-layouts: 0.72 us -> 8.18 us
    ppermute x4 -> x0, waiting for transfers between devices: 7.23 us -> none  [doubling_sum(): lax.ppermute(value, axis, [(i, i ^ step) for i in range(count)])]
    all_gather x1 -> x0, blocking collectives: 1.9 us -> none  [shards(): projection = lax.all_gather(projection, 'knot', axis=1, tiled=True)]
    broadcast_in_dim x0 -> x1, local copies, waits for them, and re-layouts: none -> 0.72 us  [gathered_sum(): copies = jnp.broadcast_to(share, (count * groups, share.shape[1]))]
    all_to_all x0 -> x1, local copies, waits for them, and re-layouts: none -> 0.7 us  [gathered_sum(): shares = lax.all_to_all(shares, axis, 0, 0, tiled=True)]
  transfers between devices with their start and end apart: 8 -> 6, of which waited for: 3 -> 3; matrix products, arithmetic and copies ran while one was open for 2% -> 3% of each run, Pallas kernels for 32% -> 26%
where the time goes in v3:
time: 58.4 us; the launch traced here: 58 us
  Pallas kernels  18.5 us (32%)
  starting transfers between devices  16.6 us (28%)
  waiting for transfers between devices  10.4 us (18%)
  local copies, waits for them, and re-layouts  9.65 us (17%)
  other arithmetic  2.63 us (5%)
    unnamed x24, local copies, waits for them, and re-layouts  8.18 us
    all_to_all x1, waiting for transfers between devices, gathered_sum(): whole = lax.all_to_all(copies, (axis, other), 0, 0, tiled=True)  7.89 us
    all_to_all x1, starting transfers between devices, gathered_sum(): shares = lax.all_to_all(shares, axis, 0, 0, tiled=True)  7.89 us
    pallas_call x2, Pallas kernels, project(): pl.pallas_call(functools.partial(project_kernel, probes, scale), out_shap...  7.17 us
    pallas_call x4, Pallas kernels, taper(): pl.pallas_call(functools.partial(taper_kernel, probes, first), out_shape=...  6.96 us
    ppermute x2, starting transfers between devices, paired(): return lax.ppermute(value, axis, pairs + [(b, a) for a, b in pairs])  5.36 us
    pallas_call x1, Pallas kernels, factored(): pl.pallas_call(functools.partial(factor_kernel, scale), out_shape=jax.Sha...  2.88 us
    all_to_all x1, starting transfers between devices, gathered_sum(): whole = lax.all_to_all(copies, (axis, other), 0, 0, tiled=True)  2.56 us
  transfers between devices with their start and end apart: 6, of which 3 were waited for; matrix products, arithmetic and copies ran while one was open for 3% of the time, Pallas kernels for 26%

profile of v3, /device:TPU:0, one launch (start us, length us, event | category | flops | bytes accessed | tf_op | source)
XLA Modules:
  0.0 58.0 jit_solution(9411911982412844605)
XLA Ops:
  0.0 0.9 %pad_maximum_fusion.1.own_ref.stack_ref = f32[24,1024]{1,0:T(8,128)S(1)} fusion(f32[6,1024]{1,0:T(8,128)S(1)} %broadcast_in_dim.21, f32[2,1024]{1,0:T(2,128)} %param.7, f32[16,1024]{1,0:T(8,128)} %param.6), kind=kLoop, calls=%fused_computation.1 | loop fusion | flops 49152 | bytes 196608 | tf_op jit(solution)/shard_map/concatenate | solution.py:248
  0.9 0.5 collective-permute-start
  1.4 0.7 %fusion.4.ids_ref = s32[8,8]{1,0:T(8,128)S(1)} fusion(s32[8,8]{1,0:T(8,128)} %param.10, s32[]{:T(128)S(6)} %mul.11, s32[]{:T(128)S(6)} %sub.24, s32[]{:T(128)S(6)} %add.31, s32[]{:T(128)S(6)} %axis_index.23), kind=kLoop, calls=%fused_computation.18 | loop fusion | flops 1792 | bytes 528 | tf_op jit(solution)/shard_map/add | solution.py:261
  2.1 0.0 copy-start.7
  2.1 0.7 %copy-done.7 = f32[2,1024]{1,0:T(2,128)S(1)} copy-done((f32[2,1024]{1,0:T(2,128)S(1)}, f32[2,1024]{1,0:T(2,128)}, u32[]{:S(2)}) %copy-start.7) | copy-done | bytes 8216
  2.8 3.6 %project.2 = (f32[16,1024]{1,0:T(8,128)S(1)}, bf16[1024,1024]{1,0:T(8,128)(2,1)S(1)}, bf16[1024,1024]{1,0:T(8,128)(2,1)S(1)}) custom-call(f32[24,1024]{1,0:T(8,128)S(1)} %pad_maximum_fusion.1.own_ref.stack_ref, f32[2,1024]{1,0:T(2,128)S(1)} %copy-done.7), custom_call_target="tpu_custom_call" | custom-call | flops 134217728 | bytes 4194304 | tf_op jit(solution)/shard_map/project/pallas_call | solution.py:92
  6.4 0.0 copy-start.1
  6.4 1.3 %copy-done.1 = bf16[1024,1024]{1,0:T(8,128)(2,1)} copy-done((bf16[1024,1024]{1,0:T(8,128)(2,1)}, bf16[1024,1024]{1,0:T(8,128)(2,1)S(1)}, u32[]{:S(2)}) %copy-start.1) | copy-done | bytes 2097176
  7.7 0.0 copy-start.9
  7.7 0.0 copy-start.10
  7.7 0.0 collective-permute-done.stack_ref
  7.7 3.6 %project.3 = (f32[16,1024]{1,0:T(8,128)S(1)}, bf16[1024,1024]{1,0:T(8,128)(2,1)S(1)}, bf16[1024,1024]{1,0:T(8,128)(2,1)S(1)}) custom-call(f32[24,1024]{1,0:T(8,128)S(1)} %collective-permute-done.stack_ref, f32[2,1024]{1,0:T(2,128)S(1)} %copy-done.7), custom_call_target="tpu_custom_call" | custom-call | flops 134217728 | bytes 4194304 | tf_op jit(solution)/shard_map/project/pallas_call | solution.py:92
  11.3 0.0 copy-start.3
  11.3 1.3 %copy-done.3 = bf16[1024,1024]{1,0:T(8,128)(2,1)} copy-done((bf16[1024,1024]{1,0:T(8,128)(2,1)}, bf16[1024,1024]{1,0:T(8,128)(2,1)S(1)}, u32[]{:S(2)}) %copy-start.3) | copy-done | bytes 2097176
  12.7 0.0 copy-start.5
  12.7 1.4 %copy-done.5 = bf16[1024,1024]{1,0:T(8,128)(2,1)} copy-done((bf16[1024,1024]{1,0:T(8,128)(2,1)}, bf16[1024,1024]{1,0:T(8,128)(2,1)S(1)}, u32[]{:S(2)}) %copy-start.5) | copy-done | bytes 2097176
  14.0 0.7 %copy.7 = f32[16,1,1024]{2,1,0:T(1,128)} copy(f32[16,1,1024]{2,0,1:T(8,128)S(1)} %add_bitcast_fusion) | data formatting | bytes 131072 | tf_op jit(solution)/shard_map/all_to_all | solution.py:214
  14.7 7.9 %all-to-all-start = ((f32[16,1,1024]{2,1,0:T(1,128)}), f32[16,1,1024]{2,1,0:T(1,128)S(1)}, u32[]{:S(2)}, u32[]{:S(2)}) async-start(f32[16,1,1024]{2,1,0:T(1,128)} %copy.7), calls=%async_computation | async-start | bytes 131072 | tf_op jit(solution)/shard_map/all_to_all | solution.py:214
  22.6 0.0 copy-done.9
  22.7 0.0 copy-done.10
  22.7 0.7 %collective-permute-start.2 = (f32[24,1280]{1,0:T(8,128)S(1)}, f32[24,1280]{1,0:T(8,128)S(1)}, u32[]{:S(2)}, u32[]{:S(2)}) collective-permute-start(f32[24,1280]{1,0:T(8,128)S(1)} %pad_maximum_fusion), channel_id=1, source_target_pairs={{2,4},{6,8},{10,12},{14,16},{18,20},{22,24},{26,28},{4,2},{8,6},{1... | collective-permute-start | bytes 368648 | tf_op jit(solution)/shard_map/ppermute | solution.py:232
  23.4 4.7 %collective-permute-start.1 = (f32[24,1280]{1,0:T(8,128)S(1)}, f32[24,1280]{1,0:T(8,128)S(1)}, u32[]{:S(2)}, u32[]{:S(2)}) collective-permute-start(f32[24,1280]{1,0:T(8,128)S(1)} %pad_maximum_fusion), channel_id=1, source_target_pairs={{0,2},{4,6},{8,10},{12,14},{16,18},{20,22},{24,26},{28,30},{2,0},{... | collective-permute-start | bytes 368648 | tf_op jit(solution)/shard_map/ppermute | solution.py:232
  28.1 2.2 %all-to-all-done = f32[16,1,1024]{2,1,0:T(1,128)S(1)} async-done(((f32[16,1,1024]{2,1,0:T(1,128)}), f32[16,1,1024]{2,1,0:T(1,128)S(1)}, u32[]{:S(2)}, u32[]{:S(2)}) %all-to-all-start) | async-done | bytes 65568 | tf_op jit(solution)/shard_map/all_to_all | solution.py:214
  30.3 0.1 reduce_sum.9
  30.3 0.7 %broadcast_in_dim.22 = f32[32,1,1024]{2,1,0:T(1,128)} broadcast(f32[1024]{0:T(1024)S(1)} %reduce_sum.9), dimensions={2} | broadcast | bytes 135168 | tf_op jit(solution)/shard_map/broadcast_in_dim | solution.py:216
  31.0 2.6 %all-to-all-start.1 = ((f32[32,1,1024]{2,1,0:T(1,128)}), f32[32,1,1024]{2,1,0:T(1,128)S(1)}, u32[]{:S(2)}, u32[]{:S(2)}) async-start(f32[32,1,1024]{2,1,0:T(1,128)} %broadcast_in_dim.22), calls=%async_computation.1 | async-start | bytes 262144 | tf_op jit(solution)/shard_map/all_to_all | solution.py:217
  33.6 0.3 collective-permute-done.1
  33.9 7.9 %all-to-all-done.1 = f32[32,1,1024]{2,1,0:T(1,128)S(1)} async-done(((f32[32,1,1024]{2,1,0:T(1,128)}), f32[32,1,1024]{2,1,0:T(1,128)S(1)}, u32[]{:S(2)}, u32[]{:S(2)}) %all-to-all-start.1) | async-done | bytes 131104 | tf_op jit(solution)/shard_map/all_to_all | solution.py:217
  41.8 0.3 reduce.1
  42.2 0.0 copy-start
  42.2 3.4 %copy-done = f32[1024,2048]{1,0:T(8,128)S(1)} copy-done((f32[1024,2048]{1,0:T(8,128)S(1)}, f32[1024,2048]{1,0:T(8,128)}, u32[]{:S(2)}) %copy-start) | copy-done | bytes 8388632
  45.6 0.0 copy-start.4
  45.6 2.9 %factor.1.factor_ref = f32[16,1024]{1,0:T(8,128)S(1)} custom-call(f32[16,2048]{1,0:T(8,128)S(1)} %reshape_reshape.3.proj_ref, f32[1024,2048]{1,0:T(8,128)S(1)} %copy-done), custom_call_target="tpu_custom_call" | custom-call | flops 268435456 | bytes 8388608 | tf_op jit(solution)/shard_map/factor/pallas_call | solution.py:132
  48.5 0.0 copy-done.4
  48.5 0.0 copy-done.6
  48.5 0.0 copy-start.8
  48.5 0.8 %spread.2 = f32[16,1024]{1,0:T(8,128)S(1)} custom-call(f32[16,1024]{1,0:T(8,128)S(1)} %factor.1.factor_ref, bf16[1024,1024]{1,0:T(8,128)(2,1)S(1)} %copy-done.4, bf16[1024,1024]{1,0:T(8,128)(2,1)S(1)} %copy-done.6), custom_call_target="tpu_custom_call" | custom-call | flops 134217728 | bytes 4194304 | tf_op jit(solution)/shard_map/spread/pallas_call | solution.py:157
  49.3 0.2 collective-permute-start.3
  49.5 0.0 collective-permute-done.2
  49.5 0.0 copy-done.8
  49.5 1.7 %taper.7 = f32[16,256]{1,0:T(8,128)S(1)} custom-call(s32[8,8]{1,0:T(8,128)S(1)} %fusion.4.ids_ref, s32[8]{0:T(128)S(1)} %copy-done.8, f32[24,1024]{1,0:T(8,128)S(1)} %pad_maximum_fusion.1.own_ref.stack_ref, f32[24,3840]{1,0:T(8,128)S(1)} %constant_dynamic-update-slice_fusion.near_ref), custom_call_target="tpu_custom_call" | custom-call | flops 134217728 | bytes 1048576 | tf_op jit(solution)/shard_map/taper/pallas_call | solution.py:199
  51.3 1.7 %taper.6 = f32[16,256]{1,0:T(8,128)S(1)} custom-call(s32[8,8]{1,0:T(8,128)S(1)} %fusion.4.ids_ref, s32[8]{0:T(128)S(1)} %copy-done.8, f32[24,1024]{1,0:T(8,128)S(1)} %pad_maximum_fusion.1.own_ref.stack_ref, f32[24,3840]{1,0:T(8,128)S(1)} %constant_dynamic-update-slice_fusion.near_ref), custom_call_target="tpu_custom_call" | custom-call | flops 134217728 | bytes 1048576 | tf_op jit(solution)/shard_map/taper/pallas_call | solution.py:199
  53.0 1.7 %taper.5 = f32[16,256]{1,0:T(8,128)S(1)} custom-call(s32[8,8]{1,0:T(8,128)S(1)} %fusion.4.ids_ref, s32[8]{0:T(128)S(1)} %copy-done.8, f32[24,1024]{1,0:T(8,128)S(1)} %pad_maximum_fusion.1.own_ref.stack_ref, f32[24,3840]{1,0:T(8,128)S(1)} %constant_dynamic-update-slice_fusion.near_ref), custom_call_target="tpu_custom_call" | custom-call | flops 134217728 | bytes 1048576 | tf_op jit(solution)/shard_map/taper/pallas_call | solution.py:199
  54.8 1.7 %taper.4 = f32[16,256]{1,0:T(8,128)S(1)} custom-call(s32[8,8]{1,0:T(8,128)S(1)} %fusion.4.ids_ref, s32[8]{0:T(128)S(1)} %copy-done.8, f32[24,1024]{1,0:T(8,128)S(1)} %pad_maximum_fusion.1.own_ref.stack_ref, f32[24,3840]{1,0:T(8,128)S(1)} %constant_dynamic-update-slice_fusion.near_ref), custom_call_target="tpu_custom_call" | custom-call | flops 134217728 | bytes 1048576 | tf_op jit(solution)/shard_map/taper/pallas_call | solution.py:199
  56.5 0.0 copy-done.2
  56.5 0.8 %spread.3 = f32[16,1024]{1,0:T(8,128)S(1)} custom-call(f32[16,1024]{1,0:T(8,128)S(1)} %factor.1.factor_ref, bf16[1024,1024]{1,0:T(8,128)(2,1)S(1)} %get-tuple-element.15.high_ref, bf16[1024,1024]{1,0:T(8,128)(2,1)S(1)} %copy-done.2), custom_call_target="tpu_custom_call" | custom-call | flops 134217728 | bytes 4194304 | tf_op jit(solution)/shard_map/spread/pallas_call | solution.py:157
  57.3 0.0 collective-permute-done.3
  57.3 0.7 %fusion = f32[16,1024]{1,0:T(8,128)} fusion(f32[16,1024]{1,0:T(8,128)S(1)} %spread.3, f32[16,1024]{1,0:T(8,128)S(1)} %collective-permute-done.3, f32[16,256]{1,0:T(8,128)S(1)} %taper.7, f32[16,256]{1,0:T(8,128)S(1)} %taper.6, f32[16,256]{1,0:T(8,128)S(1)} %taper.5, f32[16,256]{1,0:T(8,128)S(1)} %taper.4), kind=kLoop, calls=%fused_computation.3 | loop fusion | flops 81920 | bytes 262144 | tf_op jit(solution)/shard_map/add | solution.py:276
  (11 shorter events, 0.1 us)
Async XLA Ops:
  0.9 6.9 %collective-permute-start = (f32[24,1024]{1,0:T(8,128)S(1)}, f32[24,1024]{1,0:T(8,128)S(1)}, u32[]{:S(2)}, u32[]{:S(2)}) collective-permute-start(f32[24,1024]{1,0:T(8,128)S(1)} %pad_maximum_fusion.1.own_ref.stack_ref), channel_id=1, source_target_pairs={{1,0},{0,1},{3,2},{2,3},{5,4},{4,5},{7,6},{6,7},{9,8},{8,9},{11,10... | collective-permute-start | bytes 294920 | tf_op jit(solution)/shard_map/ppermute | solution.py:226
  2.1 0.7 %copy-start.7 = (f32[2,1024]{1,0:T(2,128)S(1)}, f32[2,1024]{1,0:T(2,128)}, u32[]{:S(2)}) copy-start(f32[2,1024]{1,0:T(2,128)} %knots_ref.3) | copy-start | bytes 24580
  6.4 1.4 %copy-start.1 = (bf16[1024,1024]{1,0:T(8,128)(2,1)}, bf16[1024,1024]{1,0:T(8,128)(2,1)S(1)}, u32[]{:S(2)}) copy-start(bf16[1024,1024]{1,0:T(8,128)(2,1)S(1)} %get-tuple-element.16.low_ref) | copy-start | bytes 6291460
  7.7 14.9 %copy-start.9 = (f32[16,1024]{1,0:T(8,128)S(1)}, f32[16,1024]{1,0:T(8,128)}, u32[]{:S(2)}) copy-start(f32[16,1024]{1,0:T(8,128)} %param.6) | copy-start | bytes 196612
  7.7 14.9 %copy-start.10 = (f32[2,1024]{1,0:T(2,128)S(1)}, f32[2,1024]{1,0:T(2,128)}, u32[]{:S(2)}) copy-start(f32[2,1024]{1,0:T(2,128)} %param.7) | copy-start | bytes 24580
  11.3 1.4 %copy-start.3 = (bf16[1024,1024]{1,0:T(8,128)(2,1)}, bf16[1024,1024]{1,0:T(8,128)(2,1)S(1)}, u32[]{:S(2)}) copy-start(bf16[1024,1024]{1,0:T(8,128)(2,1)S(1)} %get-tuple-element.13.high_ref) | copy-start | bytes 6291460
  12.7 1.4 %copy-start.5 = (bf16[1024,1024]{1,0:T(8,128)(2,1)}, bf16[1024,1024]{1,0:T(8,128)(2,1)S(1)}, u32[]{:S(2)}) copy-start(bf16[1024,1024]{1,0:T(8,128)(2,1)S(1)} %get-tuple-element.14.low_ref) | copy-start | bytes 6291460
  14.7 15.5 %all-to-all-start = ((f32[16,1,1024]{2,1,0:T(1,128)}), f32[16,1,1024]{2,1,0:T(1,128)S(1)}, u32[]{:S(2)}, u32[]{:S(2)}) async-start(f32[16,1,1024]{2,1,0:T(1,128)} %copy.7), calls=%async_computation | async-start | bytes 131072 | tf_op jit(solution)/shard_map/all_to_all | solution.py:214
  22.7 26.8 %collective-permute-start.2 = (f32[24,1280]{1,0:T(8,128)S(1)}, f32[24,1280]{1,0:T(8,128)S(1)}, u32[]{:S(2)}, u32[]{:S(2)}) collective-permute-start(f32[24,1280]{1,0:T(8,128)S(1)} %pad_maximum_fusion), channel_id=1, source_target_pairs={{2,4},{6,8},{10,12},{14,16},{18,20},{22,24},{26,28},{4,2},{8,6},{1... | collective-permute-start | bytes 368648 | tf_op jit(solution)/shard_map/ppermute | solution.py:232
  23.4 10.6 %collective-permute-start.1 = (f32[24,1280]{1,0:T(8,128)S(1)}, f32[24,1280]{1,0:T(8,128)S(1)}, u32[]{:S(2)}, u32[]{:S(2)}) collective-permute-start(f32[24,1280]{1,0:T(8,128)S(1)} %pad_maximum_fusion), channel_id=1, source_target_pairs={{0,2},{4,6},{8,10},{12,14},{16,18},{20,22},{24,26},{28,30},{2,0},{... | collective-permute-start | bytes 368648 | tf_op jit(solution)/shard_map/ppermute | solution.py:232
  31.0 10.8 %all-to-all-start.1 = ((f32[32,1,1024]{2,1,0:T(1,128)}), f32[32,1,1024]{2,1,0:T(1,128)S(1)}, u32[]{:S(2)}, u32[]{:S(2)}) async-start(f32[32,1,1024]{2,1,0:T(1,128)} %broadcast_in_dim.22), calls=%async_computation.1 | async-start | bytes 262144 | tf_op jit(solution)/shard_map/all_to_all | solution.py:217
  42.2 3.4 %copy-start = (f32[1024,2048]{1,0:T(8,128)S(1)}, f32[1024,2048]{1,0:T(8,128)}, u32[]{:S(2)}) copy-start(f32[1024,2048]{1,0:T(8,128)} %precision_ref.1) | copy-start | bytes 25165828
  45.6 2.9 %copy-start.4 = (bf16[1024,1024]{1,0:T(8,128)(2,1)S(1)}, bf16[1024,1024]{1,0:T(8,128)(2,1)}, u32[]{:S(2)}) copy-start(bf16[1024,1024]{1,0:T(8,128)(2,1)} %copy-done.3) | copy-start | bytes 6291460
  45.6 2.9 %copy-start.6 = (bf16[1024,1024]{1,0:T(8,128)(2,1)S(1)}, bf16[1024,1024]{1,0:T(8,128)(2,1)}, u32[]{:S(2)}) copy-start(bf16[1024,1024]{1,0:T(8,128)(2,1)} %copy-done.5) | copy-start | bytes 6291460
  48.5 1.0 %copy-start.8 = (s32[8]{0:T(128)S(1)}, s32[8]{0:T(128)}, u32[]{:S(2)}) copy-start(s32[8]{0:T(128)} %counts_ref.7) | copy-start | bytes 100
  49.3 7.3 %copy-start.2 = (bf16[1024,1024]{1,0:T(8,128)(2,1)S(1)}, bf16[1024,1024]{1,0:T(8,128)(2,1)}, u32[]{:S(2)}) copy-start(bf16[1024,1024]{1,0:T(8,128)(2,1)} %copy-done.1) | copy-start | bytes 6291460
  49.3 8.0 %collective-permute-start.3 = (f32[16,1024]{1,0:T(8,128)S(1)}, f32[16,1024]{1,0:T(8,128)S(1)}, u32[]{:S(2)}, u32[]{:S(2)}) collective-permute-start(f32[16,1024]{1,0:T(8,128)S(1)} %spread.2), channel_id=1, source_target_pairs={{1,0},{0,1},{3,2},{2,3},{5,4},{4,5},{7,6},{6,7},{9,8},{8,9},{11,10... | collective-permute-start | bytes 196616 | tf_op jit(solution)/shard_map/ppermute | solution.py:226

commit v4 on v2

v4 whole, which is shorter than its diff:
```python
import functools
import math

import jax
import jax.numpy as jnp
from jax import lax
from jax.experimental import pallas as pl
from jax.experimental.pallas import tpu as pltpu
from jax.sharding import PartitionSpec as P

COV_RANGE = 0.05
TAPER_LEN = 0.15
KNOT_REACH = 0.15
TAPER_SCALE = 0.1
PROJ_GAIN = 0.5
EXPAND_GAIN = 0.5
LOW_SCALE = 0.5
NUGGET = 0.25
LOG2E = math.log2(math.e)
STACK_ROWS = 24
TINY = 1e-30
TILE = 256
LANES = 128
LIMIT = 16 * 1024 * 1024
VMEM = pl.BlockSpec(memory_space=pltpu.VMEM)
SMEM = pl.BlockSpec(memory_space=pltpu.SMEM)


def halves(x):
    high = x.astype(jnp.bfloat16)
    return high, (x - high.astype(jnp.float32)).astype(jnp.bfloat16)


def stacked_halves(x):
    return jnp.concatenate(halves(x), axis=0)


def folded(x):
    rows = x.shape[0] // 2
    return x[:rows] + x[rows:]


def dot_nt(left, right):
    return lax.dot_general(
        left, right, (((1,), (1,)), ((), ())), preferred_element_type=jnp.float32
    )


def dot_nn(left, right):
    return jnp.dot(left, right, preferred_element_type=jnp.float32)


def distance(ax, ay, bx, by):
    dx = ax - bx
    dy = ay - by
    square = dx * dx + dy * dy
    return square * lax.rsqrt(jnp.maximum(square, TINY))


def as_columns(rows):
    fill = jnp.zeros((8 - rows.shape[0], rows.shape[1]), rows.dtype)
    return jnp.transpose(jnp.concatenate([rows, fill], axis=0))


def padded_halves(x, rows):
    fill = jnp.zeros((rows - 2 * x.shape[0], x.shape[1]), jnp.bfloat16)
    return jnp.concatenate([*halves(x), fill], axis=0)


def folded_columns(x, rows):
    x = jnp.transpose(x)
    return x[:rows] + x[rows : 2 * rows]


def cost(work, pairs, transcendentals=0):
    return pl.CostEstimate(flops=work * pairs, bytes_accessed=4 * pairs, transcendentals=transcendentals * pairs)


def prepare_kernel(probes_ref, locations_ref, knots_ref, stack_ref, knots_out_ref):
    probes, points = probes_ref.shape
    stack_ref[:probes, :] = probes_ref[...]
    fill = jnp.zeros((STACK_ROWS - probes - 2, points), jnp.float32)
    stack_ref[probes:, :] = jnp.concatenate([locations_ref[...], fill], axis=0)
    knots_out_ref[...] = knots_ref[...]


def prepare(probes, locations, knot_locs):
    return pl.pallas_call(
        prepare_kernel,
        out_shape=(
            jax.ShapeDtypeStruct((STACK_ROWS, probes.shape[1]), jnp.float32),
            jax.ShapeDtypeStruct(knot_locs.shape, jnp.float32),
        ),
        in_specs=[VMEM, VMEM, VMEM],
        out_specs=(VMEM, VMEM),
        compiler_params=pltpu.CompilerParams(vmem_limit_bytes=LIMIT),
        name="prepare",
    )(probes, locations, knot_locs)


def project_kernel(probes, scale, stack_ref, knots_ref, out_ref, high_ref, low_ref, columns, weights):
    points, knots = high_ref.shape
    tile = min(TILE, knots)
    wide = min(TILE, points)
    columns[...] = as_columns(stack_ref[probes : probes + 2, :] * scale)
    weights[...] = stacked_halves(stack_ref[:probes, :])

    @pl.loop(0, knots // tile)
    def _(step):
        lanes = pl.ds(pl.multiple_of(step * tile, tile), tile)
        kx = knots_ref[0:1, lanes] * scale
        ky = knots_ref[1:2, lanes] * scale
        total = jnp.zeros((2 * probes, tile), jnp.float32)
        for start in range(0, points, wide):
            rows = slice(start, start + wide)
            px = columns[rows, 0:1]
            py = columns[rows, 1:2]
            high, low = halves(jnp.exp2(-distance(px, py, kx, ky)))
            high_ref[rows, lanes] = high
            low_ref[rows, lanes] = low
            part = weights[:, rows]
            total = total + (dot_nn(part, high) + dot_nn(part, low))
        out_ref[:, lanes] = folded(total)


def project(stack, knot_locs, probes, scale):
    points, knots = stack.shape[1], knot_locs.shape[1]
    return pl.pallas_call(
        functools.partial(project_kernel, probes, scale),
        out_shape=(
            jax.ShapeDtypeStruct((probes, knots), jnp.float32),
            pltpu.VMEM((points, knots), jnp.bfloat16),
            pltpu.VMEM((points, knots), jnp.bfloat16),
        ),
        in_specs=[VMEM, VMEM],
        out_specs=(VMEM, VMEM, VMEM),
        scratch_shapes=[
            pltpu.VMEM((points, 8), jnp.float32),
            pltpu.VMEM((2 * probes, points), jnp.bfloat16),
        ],
        compiler_params=pltpu.CompilerParams(vmem_limit_bytes=LIMIT),
        cost_estimate=cost(3000, points * knots, 2),
        name="project",
    )(stack, knot_locs)


def factor_kernel(scale, step, before_ref, proj_ref, precision_ref, *rest):
    out_ref, weights = rest[-2:]
    probes, depth = proj_ref.shape
    all_rows = precision_ref.shape[0]
    tile = min(TILE, all_rows)
    wide = min(TILE, depth)
    weights[...] = padded_halves(proj_ref[...] * scale, weights.shape[0])
    owner = lax.rem(lax.axis_index("knot") + step, lax.axis_size("knot"))
    offset = owner * depth

    @pl.loop(0, all_rows // tile)
    def _(turn):
        rows = pl.ds(pl.multiple_of(turn * tile, tile), tile)
        total = jnp.zeros((tile, weights.shape[0]), jnp.float32)
        for start in range(0, depth, wide):
            lanes = pl.ds(pl.multiple_of(offset + start, wide), wide)
            high, low = halves(precision_ref[rows, lanes])
            part = weights[:, start : start + wide]
            total = total + (dot_nt(high, part) + dot_nt(low, part))
        found = folded_columns(total, probes)
        if before_ref is not None:
            found = found + before_ref[:, rows]
        out_ref[:, rows] = found


def factored(before, projection, precision, scale, step, after=()):
    probes, depth = projection.shape
    rows = precision.shape[0]
    kernel = functools.partial(factor_kernel, scale, step)
    operands = (projection, precision, *after)
    if before is None:
        kernel = functools.partial(kernel, None)
    else:
        operands = (before, *operands)
    return pl.pallas_call(
        kernel,
        out_shape=jax.ShapeDtypeStruct((probes, rows), jnp.float32),
        in_specs=[VMEM] * (len(operands) - len(after)) + [pl.BlockSpec(memory_space=pl.ANY)] * len(after),
        out_specs=VMEM,
        scratch_shapes=[pltpu.VMEM((LANES, depth), jnp.bfloat16)],
        compiler_params=pltpu.CompilerParams(vmem_limit_bytes=LIMIT),
        cost_estimate=cost(1200, rows * depth),
        name="factor",
    )(*operands)


def spread_kernel(scale, factor_ref, high_ref, low_ref, out_ref, weights):
    probes = factor_ref.shape[0]
    points = high_ref.shape[0]
    tile = min(TILE, points)
    weights[...] = padded_halves(factor_ref[...] * scale, weights.shape[0])
    for start in range(0, points, tile):
        rows = slice(start, start + tile)
        total = dot_nt(high_ref[rows, :], weights[...]) + dot_nt(low_ref[rows, :], weights[...])
        out_ref[:, rows] = folded_columns(total, probes)


def spread(factor, high, low, scale):
    (probes, knots), points = factor.shape, high.shape[0]
    high = pltpu.with_memory_space_constraint(high, pltpu.VMEM)
    low = pltpu.with_memory_space_constraint(low, pltpu.VMEM)
    return pl.pallas_call(
        functools.partial(spread_kernel, scale),
        out_shape=jax.ShapeDtypeStruct((probes, points), jnp.float32),
        in_specs=[VMEM, VMEM, VMEM],
        out_specs=VMEM,
        scratch_shapes=[pltpu.VMEM((LANES, knots), jnp.bfloat16)],
        compiler_params=pltpu.CompilerParams(vmem_limit_bytes=LIMIT),
        cost_estimate=cost(850, knots * points),
        name="spread",
    )(factor, high, low)


def taper_kernel(probes, first, ids_ref, counts_ref, own_ref, near_ref, out_ref, values):
    own_blocks, slots = ids_ref.shape
    block = own_ref.shape[1] // own_blocks
    near_blocks = near_ref.shape[1] // block
    column = lax.axis_index("space")
    north_base = lax.axis_index("knot") * own_blocks - 1
    north_cells = lax.axis_size("knot") * own_blocks
    inverse = 1.0 / TAPER_LEN
    decay = -LOG2E * TAPER_LEN / COV_RANGE
    values[:, near_blocks * block :] = jnp.zeros((values.shape[0], block), jnp.bfloat16)
    values[:, : near_blocks * block] = padded_halves(near_ref[:probes, :], values.shape[0])

    def place(group, slot):
        ahead = ids_ref[group, slot] - (column - 1) * north_cells
        east = jnp.where(ahead >= north_cells, 1, 0) + jnp.where(ahead >= 2 * north_cells, 1, 0)
        strip = jnp.where(east == 1, 0, 1 + lax.rem(column + lax.div(east, 2) + 1, 2))
        index = strip * (own_blocks + 2) + (ahead - east * north_cells - north_base)
        return index, jnp.where(slot < counts_ref[group], index, near_blocks)

    def lanes_of(index):
        return pl.ds(pl.multiple_of(index * block, block), block)

    for index in range(out_ref.shape[1] // block):
        group = first + index
        here = slice(group * block, (group + 1) * block)
        own = as_columns(own_ref[probes : probes + 2, here] * inverse)
        px = own[:, 0:1]
        py = own[:, 1:2]
        total = jnp.zeros((block, values.shape[0]), jnp.float32)
        for pair in range(0, slots, 2):
            highs, lows, parts = [], [], []
            for slot in range(pair, min(pair + 2, slots)):
                spot, value_spot = place(group, slot)
                lanes = lanes_of(spot)
                qx = near_ref[probes : probes + 1, lanes] * inverse
                qy = near_ref[probes + 1 : probes + 2, lanes] * inverse
                scaled = jnp.minimum(distance(px, py, qx, qy), 1.0)
                remain = (1.0 - scaled) * (1.0 - scaled)
                covariance = jnp.exp2(scaled * decay) * (remain * remain) * (1.0 + 4.0 * scaled)
                high, low = halves(covariance)
                highs.append(high)
                lows.append(low)
                parts.append(values[:, lanes_of(value_spot)])
            part = jnp.concatenate(parts, axis=1)
            total = total + (
                dot_nt(jnp.concatenate(highs, axis=1), part) + dot_nt(jnp.concatenate(lows, axis=1), part)
            )
        out_ref[:, index * block : (index + 1) * block] = (
            TAPER_SCALE * folded_columns(total, probes) + NUGGET * own_ref[:probes, here]
        )


def taper(ids, counts, own, near, probes, first, blocks):
    block = own.shape[1] // ids.shape[0]
    return pl.pallas_call(
        functools.partial(taper_kernel, probes, first),
        out_shape=jax.ShapeDtypeStruct((probes, blocks * block), jnp.float32),
        in_specs=[SMEM, SMEM, VMEM, VMEM],
        out_specs=VMEM,
        scratch_shapes=[pltpu.VMEM((LANES, near.shape[1] + block), jnp.bfloat16)],
        compiler_params=pltpu.CompilerParams(vmem_limit_bytes=LIMIT),
        cost_estimate=cost(6000, blocks * ids.shape[1] * block * block, 2),
        name="taper",
    )(ids, counts, own, near)


def doubling_sum(value, axis, other):
    count, groups = lax.axis_size(axis), lax.axis_size(other)
    if count & (count - 1):
        return lax.psum(value, axis)
    steps = [1 << i for i in range(count.bit_length() - 1)]
    half = len(steps) // 2
    for turn in range(len(steps)):
        pairs = []
        for j in range(groups):
            step = steps[(turn + half * (j % 2)) % len(steps)]
            pairs += [(i * groups + j, (i ^ step) * groups + j) for i in range(count)]
        value = value + lax.ppermute(value, (axis, other), pairs)
    return value


def shifted(value, axis, step):
    count = lax.axis_size(axis)
    if step % count == 0:
        return value
    return lax.ppermute(value, axis, [((i + step) % count, i) for i in range(count)])


def paired(value, axis, first):
    count = lax.axis_size(axis)
    pairs = [(i, i + 1) for i in range(first, count - 1, 2)]
    return lax.ppermute(value, axis, pairs + [(b, a) for a, b in pairs])


def shards(probes, locations, knot_locs, knot_precision, neighbours, counts):
    own_blocks = neighbours.shape[0]
    probe_count, row_count = probes.shape
    block_len = row_count // own_blocks
    knot_total = knot_precision.shape[1]
    device_count = lax.axis_size(("space", "knot"))
    groups = lax.axis_size("knot")
    knot_range = KNOT_REACH * math.sqrt(own_blocks * device_count / knot_total)
    proj_scale = PROJ_GAIN * math.sqrt(knot_total / (row_count * device_count))

    stack, knots = prepare(probes, locations, knot_locs)
    chunks = [shifted(stack, "knot", step) for step in range(groups)]
    strips = [paired(stack, "space", 0), paired(stack, "space", 1)]

    first_blocks = jnp.concatenate([strip[:, :block_len] for strip in strips], axis=1)
    last_blocks = jnp.concatenate([strip[:, row_count - block_len :] for strip in strips], axis=1)
    if groups == 2:
        edge = jnp.where(lax.axis_index("knot") == 0, last_blocks, first_blocks)
        above = below = shifted(edge, "knot", 1)
    else:
        above, below = shifted(first_blocks, "knot", 1), shifted(last_blocks, "knot", -1)
    near = jnp.concatenate(
        [
            chunks[-1][:, row_count - block_len :],
            stack,
            chunks[1 % groups][:, :block_len],
            below[:, :block_len],
            strips[0],
            above[:, :block_len],
            below[:, block_len:],
            strips[1],
            above[:, block_len:],
        ],
        axis=1,
    )
    pieces = math.gcd(own_blocks, 4)
    per_piece = own_blocks // pieces
    base = [
        taper(neighbours, counts, stack, near, probe_count, i * per_piece, per_piece) for i in range(pieces)
    ]

    rate = LOG2E / knot_range
    parts = [project(chunk, knots, probe_count, rate) for chunk in chunks]
    projection = doubling_sum(sum(part[0] for part in parts), "space", "knot")
    factor = factored(None, projection, knot_precision, proj_scale, 0, base[:-1])
    for step in range(1, groups):
        factor = factored(factor, shifted(projection, "knot", step), knot_precision, proj_scale, step)
    total = jnp.concatenate(base, axis=1)
    for step in reversed(range(groups)):
        share = spread(factor, parts[step][1], parts[step][2], LOW_SCALE * EXPAND_GAIN)
        total = total + shifted(share, "knot", -step)
    return total


def solution(mesh):
    return jax.shard_map(
        shards,
        mesh=mesh,
        in_specs=(
            P(None, ("space", "knot")),
            P(None, ("space", "knot")),
            P(None, "knot"),
            P("knot", None),
            P(("space", "knot"), None),
            P(("space", "knot")),
        ),
        out_specs=P(None, ("space", "knot")),
        check_vma=False,
    )
```

time: 47 us -> 43.3 us (0.921)
  waiting for transfers between devices: 7.24 us -> 3.45 us
  local copies, waits for them, and re-layouts: 0.73 us -> 3.67 us
  blocking collectives: 1.9 us -> 0 us
  other arithmetic: 2.38 us -> 0.75 us
  Pallas kernels: 18.6 us -> 20 us
  starting transfers between devices: 15.8 us -> 14.9 us
    ppermute x4, waiting for transfers between devices: 7.23 us -> 3.36 us  [doubling_sum(): value = value + lax.ppermute(value, (axis, other), pairs)]
    unnamed x12 -> x25, local copies, waits for them, and re-layouts: 0.72 us -> 3.66 us
    ppermute x4, starting transfers between devices: 10.1 us -> 7.36 us  [doubling_sum(): value = value + lax.ppermute(value, (axis, other), pairs)]
    all_gather x1 -> x0, blocking collectives: 1.9 us -> none  [shards(): projection = lax.all_gather(projection, 'knot', axis=1, tiled=True)]
    ppermute x2, starting transfers between devices: 4.96 us -> 6.4 us  [paired(): return lax.ppermute(value, axis, pairs + [(b, a) for a, b in pairs])]
    pallas_call x1 -> x3, Pallas kernels: 2.88 us -> 3.94 us  [the longest x2 3.93 us: factored(): pl.pallas_call(kernel, out_shape=jax.ShapeDtypeStruct((probes, rows), jnp...]
    pallas_call x2, Pallas kernels: 7.18 us -> 6.17 us  [project(): pl.pallas_call(functools.partial(project_kernel, probes, scale), out_shap...]
    pallas_call x2, Pallas kernels: 1.55 us -> 2.56 us  [spread(): pl.pallas_call(functools.partial(spread_kernel, scale), out_shape=jax.Sha...]
  transfers between devices with their start and end apart: 8 -> 10, of which waited for: 3 -> 5; matrix products, arithmetic and copies ran while one was open for 2% -> 0% of each run, Pallas kernels for 32% -> 39%
where the time goes in v4:
time: 43.3 us; the launch traced here: 43 us
  Pallas kernels  20 us (46%)
  starting transfers between devices  14.9 us (34%)
  local copies, waits for them, and re-layouts  3.67 us (8%)
  waiting for transfers between devices  3.45 us (8%)
  other arithmetic  0.75 us (2%)
    pallas_call x4, Pallas kernels, taper(): pl.pallas_call(functools.partial(taper_kernel, probes, first), out_shape=...  7.37 us
    ppermute x4, starting transfers between devices, doubling_sum(): value = value + lax.ppermute(value, (axis, other), pairs)  7.36 us
    ppermute x2, starting transfers between devices, paired(): return lax.ppermute(value, axis, pairs + [(b, a) for a, b in pairs])  6.4 us
    pallas_call x2, Pallas kernels, project(): pl.pallas_call(functools.partial(project_kernel, probes, scale), out_shap...  6.17 us
    pallas_call x2, Pallas kernels, factored(): pl.pallas_call(kernel, out_shape=jax.ShapeDtypeStruct((probes, rows), jnp...  3.93 us
    unnamed x25, local copies, waits for them, and re-layouts  3.66 us
    ppermute x4, waiting for transfers between devices, doubling_sum(): value = value + lax.ppermute(value, (axis, other), pairs)  3.36 us
    pallas_call x2, Pallas kernels, spread(): pl.pallas_call(functools.partial(spread_kernel, scale), out_shape=jax.Sha...  2.56 us
  transfers between devices with their start and end apart: 10, of which 5 were waited for; matrix products, arithmetic and copies ran while one was open for 0% of the time, Pallas kernels for 39%

profile of v4, /device:TPU:0, one launch (start us, length us, event | category | flops | bytes accessed | tf_op | source)
XLA Modules:
  0.0 43.0 jit_solution(17122693374617623237)
XLA Ops:
  0.0 0.0 copy-start.2
  0.0 0.8 %copy-done.2 = f32[16,1024]{1,0:T(8,128)S(1)} copy-done((f32[16,1024]{1,0:T(8,128)S(1)}, f32[16,1024]{1,0:T(8,128)}, u32[]{:S(2)}) %copy-start.2) | copy-done | bytes 65560
  0.8 0.0 copy-start.3
  0.8 0.7 %copy-done.3 = f32[2,1024]{1,0:T(2,128)S(1)} copy-done((f32[2,1024]{1,0:T(2,128)S(1)}, f32[2,1024]{1,0:T(2,128)}, u32[]{:S(2)}) %copy-start.3) | copy-done | bytes 8216
  1.5 0.0 copy-start.4
  1.5 0.7 %copy-done.4 = f32[2,1024]{1,0:T(2,128)S(1)} copy-done((f32[2,1024]{1,0:T(2,128)S(1)}, f32[2,1024]{1,0:T(2,128)}, u32[]{:S(2)}) %copy-start.4) | copy-done | bytes 8216
  2.2 0.7 %collective-permute-start.2 = (f32[24,1024]{1,0:T(8,128)S(1)}, f32[24,1024]{1,0:T(8,128)S(1)}, u32[]{:S(2)}, u32[]{:S(2)}) collective-permute-start(f32[24,1024]{1,0:T(8,128)S(1)} %get-tuple-element.13.own_ref.stack_ref), channel_id=1, source_target_pairs={{2,4},{6,8},{10,12},{14,16},{18,20},{22,24},{26,28},{4,2},{8,6},{1... | collective-permute-start | bytes 294920 | tf_op jit(solution)/shard_map/ppermute | solution.py:311
  2.9 5.7 %collective-permute-start.1 = (f32[24,1024]{1,0:T(8,128)S(1)}, f32[24,1024]{1,0:T(8,128)S(1)}, u32[]{:S(2)}, u32[]{:S(2)}) collective-permute-start(f32[24,1024]{1,0:T(8,128)S(1)} %get-tuple-element.13.own_ref.stack_ref), channel_id=1, source_target_pairs={{0,2},{4,6},{8,10},{12,14},{16,18},{20,22},{24,26},{28,30},{2,0},{... | collective-permute-start | bytes 294920 | tf_op jit(solution)/shard_map/ppermute | solution.py:311
  8.7 0.0 collective-permute-start
  8.7 3.1 %project.2 = (f32[16,1024]{1,0:T(8,128)S(1)}, bf16[1024,1024]{1,0:T(8,128)(2,1)S(1)}, bf16[1024,1024]{1,0:T(8,128)(2,1)S(1)}) custom-call(f32[24,1024]{1,0:T(8,128)S(1)} %get-tuple-element.13.own_ref.stack_ref, f32[2,1024]{1,0:T(2,128)S(1)} %get-tuple-element.14.knots_ref), custom_call_target="tpu_custom_call" | custom-call | flops 3145728000 | bytes 4194304 | tf_op jit(solution)/shard_map/project/pallas_call | solution.py:128
  11.7 0.0 copy-start
  11.8 1.4 %copy-done = bf16[1024,1024]{1,0:T(8,128)(2,1)} copy-done((bf16[1024,1024]{1,0:T(8,128)(2,1)}, bf16[1024,1024]{1,0:T(8,128)(2,1)S(1)}, u32[]{:S(2)}) %copy-start) | copy-done | bytes 2097176
  13.1 0.0 collective-permute-done.2
  13.1 0.1 collective-permute-done.1
  13.2 0.5 %collective-permute-start.3 = (f32[24,256]{1,0:T(8,128)S(1)}, f32[24,256]{1,0:T(8,128)S(1)}, u32[]{:S(2)}, u32[]{:S(2)}) collective-permute-start(f32[24,256]{1,0:T(8,128)S(1)} %maximum_select_fusion), channel_id=1, source_target_pairs={{1,0},{0,1},{3,2},{2,3},{5,4},{4,5},{7,6},{6,7},{9,8},{8,9},{11,10... | collective-permute-start | bytes 73736 | tf_op jit(solution)/shard_map/ppermute | solution.py:305
  13.7 0.0 collective-permute-done.stack_ref
  13.7 0.0 copy-start.5
  13.7 0.0 copy-start.6
  13.8 3.1 %project.3 = (f32[16,1024]{1,0:T(8,128)S(1)}, bf16[1024,1024]{1,0:T(8,128)(2,1)S(1)}, bf16[1024,1024]{1,0:T(8,128)(2,1)S(1)}) custom-call(f32[24,1024]{1,0:T(8,128)S(1)} %collective-permute-done.stack_ref, f32[2,1024]{1,0:T(2,128)S(1)} %get-tuple-element.14.knots_ref), custom_call_target="tpu_custom_call" | custom-call | flops 3145728000 | bytes 4194304 | tf_op jit(solution)/shard_map/project/pallas_call | solution.py:128
  16.9 1.5 %collective-permute-start.4 = (f32[16,1024]{1,0:T(8,128)S(1)}, f32[16,1024]{1,0:T(8,128)S(1)}, u32[]{:S(2)}, u32[]{:S(2)}) collective-permute-start(f32[16,1024]{1,0:T(8,128)S(1)} %add.21), channel_id=1, source_target_pairs={{0,2},{2,0},{4,6},{6,4},{8,10},{10,8},{12,14},{14,12},{16,18},{18,... | collective-permute-start | bytes 196616 | tf_op jit(solution)/shard_map/ppermute | solution.py:297
  18.4 0.0 collective-permute-done.3
  18.4 0.0 copy-done.5
  18.4 0.0 copy-done.6
  18.5 1.8 %taper.6.rest_2_ = f32[16,256]{1,0:T(8,128)S(1)} custom-call(s32[8,8]{1,0:T(8,128)S(1)} %copy-done.5, s32[8]{0:T(128)S(1)} %copy-done.6, f32[24,1024]{1,0:T(8,128)S(1)} %get-tuple-element.13.own_ref.stack_ref, f32[24,3840]{1,0:T(8,128)S(1)} %constant_dynamic-update-slice_fusion.near_ref), custom_call_target="tpu_custom_call" | custom-call | flops 1572864000 | bytes 1048576 | tf_op jit(solution)/shard_map/taper/pallas_call | solution.py:274
  20.3 0.9 %collective-permute-done.4 = f32[16,1024]{1,0:T(8,128)S(1)} collective-permute-done((f32[16,1024]{1,0:T(8,128)S(1)}, f32[16,1024]{1,0:T(8,128)S(1)}, u32[]{:S(2)}, u32[]{:S(2)}) %collective-permute-start.4) | collective-permute-done | bytes 65568 | tf_op jit(solution)/shard_map/ppermute | solution.py:297
  21.2 1.6 %collective-permute-start.5 = (f32[16,1024]{1,0:T(8,128)S(1)}, f32[16,1024]{1,0:T(8,128)S(1)}, u32[]{:S(2)}, u32[]{:S(2)}) collective-permute-start(f32[16,1024]{1,0:T(8,128)S(1)} %add.22), channel_id=1, source_target_pairs={{0,4},{2,6},{4,0},{6,2},{8,12},{10,14},{12,8},{14,10},{16,20},{18,... | collective-permute-start | bytes 196616 | tf_op jit(solution)/shard_map/ppermute | solution.py:297
  22.8 0.0 slice-start
  22.8 1.8 %taper.5.rest_1_ = f32[16,256]{1,0:T(8,128)S(1)} custom-call(s32[8,8]{1,0:T(8,128)S(1)} %copy-done.5, s32[8]{0:T(128)S(1)} %copy-done.6, f32[24,1024]{1,0:T(8,128)S(1)} %get-tuple-element.13.own_ref.stack_ref, f32[24,3840]{1,0:T(8,128)S(1)} %constant_dynamic-update-slice_fusion.near_ref), custom_call_target="tpu_custom_call" | custom-call | flops 1572864000 | bytes 1048576 | tf_op jit(solution)/shard_map/taper/pallas_call | solution.py:274
  24.7 0.9 %collective-permute-done.5 = f32[16,1024]{1,0:T(8,128)S(1)} collective-permute-done((f32[16,1024]{1,0:T(8,128)S(1)}, f32[16,1024]{1,0:T(8,128)S(1)}, u32[]{:S(2)}, u32[]{:S(2)}) %collective-permute-start.5) | collective-permute-done | bytes 65568 | tf_op jit(solution)/shard_map/ppermute | solution.py:297
  25.6 0.0 slice-start.1
  25.6 1.6 %collective-permute-start.6 = (f32[16,1024]{1,0:T(8,128)S(1)}, f32[16,1024]{1,0:T(8,128)S(1)}, u32[]{:S(2)}, u32[]{:S(2)}) collective-permute-start(f32[16,1024]{1,0:T(8,128)S(1)} %add.23), channel_id=1, source_target_pairs={{0,8},{2,10},{4,12},{6,14},{8,0},{10,2},{12,4},{14,6},{16,24},{18,... | collective-permute-start | bytes 196616 | tf_op jit(solution)/shard_map/ppermute | solution.py:297
  27.2 1.8 %taper.4.rest_0_ = f32[16,256]{1,0:T(8,128)S(1)} custom-call(s32[8,8]{1,0:T(8,128)S(1)} %copy-done.5, s32[8]{0:T(128)S(1)} %copy-done.6, f32[24,1024]{1,0:T(8,128)S(1)} %get-tuple-element.13.own_ref.stack_ref, f32[24,3840]{1,0:T(8,128)S(1)} %constant_dynamic-update-slice_fusion.near_ref), custom_call_target="tpu_custom_call" | custom-call | flops 1572864000 | bytes 1048576 | tf_op jit(solution)/shard_map/taper/pallas_call | solution.py:274
  29.1 0.8 %collective-permute-done.6 = f32[16,1024]{1,0:T(8,128)S(1)} collective-permute-done((f32[16,1024]{1,0:T(8,128)S(1)}, f32[16,1024]{1,0:T(8,128)S(1)}, u32[]{:S(2)}, u32[]{:S(2)}) %collective-permute-start.6) | collective-permute-done | bytes 65568 | tf_op jit(solution)/shard_map/ppermute | solution.py:297
  29.9 2.7 %collective-permute-start.7 = (f32[16,1024]{1,0:T(8,128)S(1)}, f32[16,1024]{1,0:T(8,128)S(1)}, u32[]{:S(2)}, u32[]{:S(2)}) collective-permute-start(f32[16,1024]{1,0:T(8,128)S(1)} %add.24), channel_id=1, source_target_pairs={{0,16},{2,18},{4,20},{6,22},{8,24},{10,26},{12,28},{14,30},{16,0},... | collective-permute-start | bytes 196616 | tf_op jit(solution)/shard_map/ppermute | solution.py:297
  32.6 1.8 %taper.7 = f32[16,256]{1,0:T(8,128)S(1)} custom-call(s32[8,8]{1,0:T(8,128)S(1)} %copy-done.5, s32[8]{0:T(128)S(1)} %copy-done.6, f32[24,1024]{1,0:T(8,128)S(1)} %get-tuple-element.13.own_ref.stack_ref, f32[24,3840]{1,0:T(8,128)S(1)} %constant_dynamic-update-slice_fusion.near_ref), custom_call_target="tpu_custom_call" | custom-call | flops 1572864000 | bytes 1048576 | tf_op jit(solution)/shard_map/taper/pallas_call | solution.py:274
  34.4 0.7 %collective-permute-done.7 = f32[16,1024]{1,0:T(8,128)S(1)} collective-permute-done((f32[16,1024]{1,0:T(8,128)S(1)}, f32[16,1024]{1,0:T(8,128)S(1)}, u32[]{:S(2)}, u32[]{:S(2)}) %collective-permute-start.7) | collective-permute-done | bytes 65568 | tf_op jit(solution)/shard_map/ppermute | solution.py:297
  35.2 0.1 collective-permute-start.8
  35.3 0.0 slice-done
  35.3 0.0 slice-done.1
  35.3 2.0 %factor.2.before_ref = f32[16,1024]{1,0:T(8,128)S(1)} custom-call(f32[16,1024]{1,0:T(8,128)S(1)} %add.25.proj_ref, f32[1024,2048]{1,0:T(8,128)S(1)} %bitcast.1, f32[16,256]{1,0:T(8,128)S(1)} %taper.4.rest_0_, f32[16,256]{1,0:T(8,128)S(1)} %taper.5.rest_1_, f32[16,256]{1,0:T(8,128)S(1)} %taper.6.rest_2_), custom_call_target="tpu_custom_call" | custom-call | flops 1258291200 | bytes 4194304 | tf_op jit(solution)/shard_map/factor/pallas_call | solution.py:181
  37.2 0.0 collective-permute-done.8.proj_ref
  37.2 2.0 %factor.3.factor_ref = f32[16,1024]{1,0:T(8,128)S(1)} custom-call(f32[16,1024]{1,0:T(8,128)S(1)} %factor.2.before_ref, f32[16,1024]{1,0:T(8,128)S(1)} %collective-permute-done.8.proj_ref, f32[1024,2048]{1,0:T(8,128)S(1)} %bitcast.1), custom_call_target="tpu_custom_call" | custom-call | flops 1258291200 | bytes 4194304 | tf_op jit(solution)/shard_map/factor/pallas_call | solution.py:181
  39.2 1.3 %spread.2 = f32[16,1024]{1,0:T(8,128)S(1)} custom-call(f32[16,1024]{1,0:T(8,128)S(1)} %factor.3.factor_ref, bf16[1024,1024]{1,0:T(8,128)(2,1)S(1)} %get-tuple-element.17.high_ref, bf16[1024,1024]{1,0:T(8,128)(2,1)S(1)} %get-tuple-element.18.low_ref), custom_call_target="tpu_custom_call" | custom-call | flops 891289600 | bytes 4194304 | tf_op jit(solution)/shard_map/spread/pallas_call | solution.py:208
  40.5 0.5 %collective-permute-start.9 = (f32[16,1024]{1,0:T(8,128)S(1)}, f32[16,1024]{1,0:T(8,128)S(1)}, u32[]{:S(2)}, u32[]{:S(2)}) collective-permute-start(f32[16,1024]{1,0:T(8,128)S(1)} %spread.2), channel_id=1, source_target_pairs={{1,0},{0,1},{3,2},{2,3},{5,4},{4,5},{7,6},{6,7},{9,8},{8,9},{11,10... | collective-permute-start | bytes 196616 | tf_op jit(solution)/shard_map/ppermute | solution.py:305
  41.0 0.0 copy-done.1
  41.1 1.3 %spread.3 = f32[16,1024]{1,0:T(8,128)S(1)} custom-call(f32[16,1024]{1,0:T(8,128)S(1)} %factor.3.factor_ref, bf16[1024,1024]{1,0:T(8,128)(2,1)S(1)} %get-tuple-element.19.high_ref, bf16[1024,1024]{1,0:T(8,128)(2,1)S(1)} %copy-done.1), custom_call_target="tpu_custom_call" | custom-call | flops 891289600 | bytes 4194304 | tf_op jit(solution)/shard_map/spread/pallas_call | solution.py:208
  42.3 0.0 collective-permute-done.9
  42.3 0.7 %fusion = f32[16,1024]{1,0:T(8,128)} fusion(f32[16,1024]{1,0:T(8,128)S(1)} %spread.3, f32[16,1024]{1,0:T(8,128)S(1)} %collective-permute-done.9, f32[16,256]{1,0:T(8,128)S(1)} %taper.7, f32[16,256]{1,0:T(8,128)S(1)} %taper.6.rest_2_, f32[16,256]{1,0:T(8,128)S(1)} %taper.5.rest_1_, f32[16,256]{1,0:T(8,128)S(1)} %taper.4.rest_0_), kind=kLoop, calls=%fused_computation.1 | loop fusion | flops 81920 | bytes 262144 | tf_op jit(solution)/shard_map/add | solution.py:364
  (19 shorter events, 0.1 us)
Async XLA Ops:
  0.0 0.8 %copy-start.2 = (f32[16,1024]{1,0:T(8,128)S(1)}, f32[16,1024]{1,0:T(8,128)}, u32[]{:S(2)}) copy-start(f32[16,1024]{1,0:T(8,128)} %probes_ref.1) | copy-start | bytes 196612
  0.8 0.7 %copy-start.3 = (f32[2,1024]{1,0:T(2,128)S(1)}, f32[2,1024]{1,0:T(2,128)}, u32[]{:S(2)}) copy-start(f32[2,1024]{1,0:T(2,128)} %locations_ref.1) | copy-start | bytes 24580
  1.5 0.7 %copy-start.4 = (f32[2,1024]{1,0:T(2,128)S(1)}, f32[2,1024]{1,0:T(2,128)}, u32[]{:S(2)}) copy-start(f32[2,1024]{1,0:T(2,128)} %knots_ref.1) | copy-start | bytes 24580
  2.2 10.9 %collective-permute-start.2 = (f32[24,1024]{1,0:T(8,128)S(1)}, f32[24,1024]{1,0:T(8,128)S(1)}, u32[]{:S(2)}, u32[]{:S(2)}) collective-permute-start(f32[24,1024]{1,0:T(8,128)S(1)} %get-tuple-element.13.own_ref.stack_ref), channel_id=1, source_target_pairs={{2,4},{6,8},{10,12},{14,16},{18,20},{22,24},{26,28},{4,2},{8,6},{1... | collective-permute-start | bytes 294920 | tf_op jit(solution)/shard_map/ppermute | solution.py:311
  2.9 10.3 %collective-permute-start.1 = (f32[24,1024]{1,0:T(8,128)S(1)}, f32[24,1024]{1,0:T(8,128)S(1)}, u32[]{:S(2)}, u32[]{:S(2)}) collective-permute-start(f32[24,1024]{1,0:T(8,128)S(1)} %get-tuple-element.13.own_ref.stack_ref), channel_id=1, source_target_pairs={{0,2},{4,6},{8,10},{12,14},{16,18},{20,22},{24,26},{28,30},{2,0},{... | collective-permute-start | bytes 294920 | tf_op jit(solution)/shard_map/ppermute | solution.py:311
  8.7 5.1 %collective-permute-start = (f32[24,1024]{1,0:T(8,128)S(1)}, f32[24,1024]{1,0:T(8,128)S(1)}, u32[]{:S(2)}, u32[]{:S(2)}) collective-permute-start(f32[24,1024]{1,0:T(8,128)S(1)} %get-tuple-element.13.own_ref.stack_ref), channel_id=1, source_target_pairs={{1,0},{0,1},{3,2},{2,3},{5,4},{4,5},{7,6},{6,7},{9,8},{8,9},{11,10... | collective-permute-start | bytes 294920 | tf_op jit(solution)/shard_map/ppermute | solution.py:305
  11.7 1.4 %copy-start = (bf16[1024,1024]{1,0:T(8,128)(2,1)}, bf16[1024,1024]{1,0:T(8,128)(2,1)S(1)}, u32[]{:S(2)}) copy-start(bf16[1024,1024]{1,0:T(8,128)(2,1)S(1)} %get-tuple-element.20.low_ref) | copy-start | bytes 6291460
  13.2 5.2 %collective-permute-start.3 = (f32[24,256]{1,0:T(8,128)S(1)}, f32[24,256]{1,0:T(8,128)S(1)}, u32[]{:S(2)}, u32[]{:S(2)}) collective-permute-start(f32[24,256]{1,0:T(8,128)S(1)} %maximum_select_fusion), channel_id=1, source_target_pairs={{1,0},{0,1},{3,2},{2,3},{5,4},{4,5},{7,6},{6,7},{9,8},{8,9},{11,10... | collective-permute-start | bytes 73736 | tf_op jit(solution)/shard_map/ppermute | solution.py:305
  13.7 4.7 %copy-start.5 = (s32[8,8]{1,0:T(8,128)S(1)}, s32[8,8]{1,0:T(8,128)}, u32[]{:S(2)}) copy-start(s32[8,8]{1,0:T(8,128)} %ids_ref.7) | copy-start | bytes 772
  13.7 4.7 %copy-start.6 = (s32[8]{0:T(128)S(1)}, s32[8]{0:T(128)}, u32[]{:S(2)}) copy-start(s32[8]{0:T(128)} %counts_ref.7) | copy-start | bytes 100
  16.9 4.3 %collective-permute-start.4 = (f32[16,1024]{1,0:T(8,128)S(1)}, f32[16,1024]{1,0:T(8,128)S(1)}, u32[]{:S(2)}, u32[]{:S(2)}) collective-permute-start(f32[16,1024]{1,0:T(8,128)S(1)} %add.21), channel_id=1, source_target_pairs={{0,2},{2,0},{4,6},{6,4},{8,10},{10,8},{12,14},{14,12},{16,18},{18,... | collective-permute-start | bytes 196616 | tf_op jit(solution)/shard_map/ppermute | solution.py:297
  21.2 4.3 %collective-permute-start.5 = (f32[16,1024]{1,0:T(8,128)S(1)}, f32[16,1024]{1,0:T(8,128)S(1)}, u32[]{:S(2)}, u32[]{:S(2)}) collective-permute-start(f32[16,1024]{1,0:T(8,128)S(1)} %add.22), channel_id=1, source_target_pairs={{0,4},{2,6},{4,0},{6,2},{8,12},{10,14},{12,8},{14,10},{16,20},{18,... | collective-permute-start | bytes 196616 | tf_op jit(solution)/shard_map/ppermute | solution.py:297
  22.8 12.4 %slice-start = ((s8[8388608]{0:T(1024)(128)(4,1)}), s8[4194304]{0:T(1024)(128)(4,1)S(1)}, s32[]{:S(2)}) async-start(s8[8388608]{0:T(1024)(128)(4,1)} %bitcast), calls=%async_computation | async-start | bytes 8388608
  25.6 9.7 %slice-start.1 = ((s8[8388608]{0:T(1024)(128)(4,1)}), s8[4194304]{0:T(1024)(128)(4,1)S(1)}, s32[]{:S(2)}) async-start(s8[8388608]{0:T(1024)(128)(4,1)} %bitcast), calls=%async_computation.1 | async-start | bytes 8388608
  25.6 4.3 %collective-permute-start.6 = (f32[16,1024]{1,0:T(8,128)S(1)}, f32[16,1024]{1,0:T(8,128)S(1)}, u32[]{:S(2)}, u32[]{:S(2)}) collective-permute-start(f32[16,1024]{1,0:T(8,128)S(1)} %add.23), channel_id=1, source_target_pairs={{0,8},{2,10},{4,12},{6,14},{8,0},{10,2},{12,4},{14,6},{16,24},{18,... | collective-permute-start | bytes 196616 | tf_op jit(solution)/shard_map/ppermute | solution.py:297
  29.9 5.2 %collective-permute-start.7 = (f32[16,1024]{1,0:T(8,128)S(1)}, f32[16,1024]{1,0:T(8,128)S(1)}, u32[]{:S(2)}, u32[]{:S(2)}) collective-permute-start(f32[16,1024]{1,0:T(8,128)S(1)} %add.24), channel_id=1, source_target_pairs={{0,16},{2,18},{4,20},{6,22},{8,24},{10,26},{12,28},{14,30},{16,0},... | collective-permute-start | bytes 196616 | tf_op jit(solution)/shard_map/ppermute | solution.py:297
  35.2 2.1 %collective-permute-start.8 = (f32[16,1024]{1,0:T(8,128)S(1)}, f32[16,1024]{1,0:T(8,128)S(1)}, u32[]{:S(2)}, u32[]{:S(2)}) collective-permute-start(f32[16,1024]{1,0:T(8,128)S(1)} %add.25.proj_ref), channel_id=1, source_target_pairs={{1,0},{0,1},{3,2},{2,3},{5,4},{4,5},{7,6},{6,7},{9,8},{8,9},{11,10... | collective-permute-start | bytes 196616 | tf_op jit(solution)/shard_map/ppermute | solution.py:305
  39.2 1.8 %copy-start.1 = (bf16[1024,1024]{1,0:T(8,128)(2,1)S(1)}, bf16[1024,1024]{1,0:T(8,128)(2,1)}, u32[]{:S(2)}) copy-start(bf16[1024,1024]{1,0:T(8,128)(2,1)} %copy-done) | copy-start | bytes 6291460
  40.5 1.8 %collective-permute-start.9 = (f32[16,1024]{1,0:T(8,128)S(1)}, f32[16,1024]{1,0:T(8,128)S(1)}, u32[]{:S(2)}, u32[]{:S(2)}) collective-permute-start(f32[16,1024]{1,0:T(8,128)S(1)} %spread.2), channel_id=1, source_target_pairs={{1,0},{0,1},{3,2},{2,3},{5,4},{4,5},{7,6},{6,7},{9,8},{8,9},{11,10... | collective-permute-start | bytes 196616 | tf_op jit(solution)/shard_map/ppermute | solution.py:305

commit v5 on v4

--- a/solution.py
+++ b/solution.py
@@ -21,8 +21,10 @@
 TINY = 1e-30
 TILE = 256
 LANES = 128
-LIMIT = 16 * 1024 * 1024
+SLAB = 32
+LIMIT = 6 * 1024 * 1024
 VMEM = pl.BlockSpec(memory_space=pltpu.VMEM)
+HBM = pl.BlockSpec(memory_space=pltpu.HBM)
 SMEM = pl.BlockSpec(memory_space=pltpu.SMEM)
 
 
@@ -76,33 +78,53 @@
     return pl.CostEstimate(flops=work * pairs, bytes_accessed=4 * pairs, transcendentals=transcendentals * pairs)
 
 
-def prepare_kernel(probes_ref, locations_ref, knots_ref, stack_ref, knots_out_ref):
+def prepare_kernel(probes_ref, locations_ref, knots_ref, stack_ref, knots_out_ref, coords, sems):
     probes, points = probes_ref.shape
-    stack_ref[:probes, :] = probes_ref[...]
+    copies = [
+        pltpu.make_async_copy(probes_ref, stack_ref.at[pl.ds(0, probes), :], sems.at[0]),
+        pltpu.make_async_copy(locations_ref, coords, sems.at[1]),
+        pltpu.make_async_copy(knots_ref, knots_out_ref, sems.at[2]),
+    ]
+    for copy in copies:
+        copy.start()
+    for copy in copies:
+        copy.wait()
     fill = jnp.zeros((STACK_ROWS - probes - 2, points), jnp.float32)
-    stack_ref[probes:, :] = jnp.concatenate([locations_ref[...], fill], axis=0)
-    knots_out_ref[...] = knots_ref[...]
+    stack_ref[probes:, :] = jnp.concatenate([coords[...], fill], axis=0)
 
 
 def prepare(probes, locations, knot_locs):
+    probes, locations, knot_locs = [
+        pltpu.with_memory_space_constraint(x, pltpu.HBM) for x in (probes, locations, knot_locs)
+    ]
     return pl.pallas_call(
         prepare_kernel,
         out_shape=(
             jax.ShapeDtypeStruct((STACK_ROWS, probes.shape[1]), jnp.float32),
             jax.ShapeDtypeStruct(knot_locs.shape, jnp.float32),
         ),
-        in_specs=[VMEM, VMEM, VMEM],
+        in_specs=[HBM, HBM, HBM],
         out_specs=(VMEM, VMEM),
+        scratch_shapes=[pltpu.VMEM(locations.shape, jnp.float32), pltpu.SemaphoreType.DMA((3,))],
         compiler_params=pltpu.CompilerParams(vmem_limit_bytes=LIMIT),
         name="prepare",
     )(probes, locations, knot_locs)
 
 
-def project_kernel(probes, scale, stack_ref, knots_ref, out_ref, high_ref, low_ref, columns, weights):
+def broadcast_columns(rows):
+    columns = as_columns(rows)
+    wide = (rows.shape[1], LANES)
+    return jnp.broadcast_to(columns[:, 0:1], wide), jnp.broadcast_to(columns[:, 1:2], wide)
+
+
+def project_kernel(probes, scale, stack_ref, knots_ref, out_ref, high_ref, low_ref, copy_ref, east, north, weights):
     points, knots = high_ref.shape
     tile = min(TILE, knots)
     wide = min(TILE, points)
-    columns[...] = as_columns(stack_ref[probes : probes + 2, :] * scale)
+    copy_ref[...] = stack_ref[...]
+    for start in range(0, points, LANES):
+        rows = slice(start, start + LANES)
+        east[rows, :], north[rows, :] = broadcast_columns(stack_ref[probes : probes + 2, rows] * scale)
     weights[...] = stacked_halves(stack_ref[:probes, :])
 
     @pl.loop(0, knots // tile)
@@ -112,14 +134,24 @@
         ky = knots_ref[1:2, lanes] * scale
         total = jnp.zeros((2 * probes, tile), jnp.float32)
         for start in range(0, points, wide):
-            rows = slice(start, start + wide)
-            px = columns[rows, 0:1]
-            py = columns[rows, 1:2]
-            high, low = halves(jnp.exp2(-distance(px, py, kx, ky)))
-            high_ref[rows, lanes] = high
-            low_ref[rows, lanes] = low
-            part = weights[:, rows]
-            total = total + (dot_nn(part, high) + dot_nn(part, low))
+            highs, lows = [], []
+            for slab in range(start, start + wide, SLAB):
+                rows = slice(slab, slab + SLAB)
+                px, py = east[rows, :], north[rows, :]
+                parts = [
+                    halves(jnp.exp2(-distance(px, py, kx[:, at : at + LANES], ky[:, at : at + LANES])))
+                    for at in range(0, tile, LANES)
+                ]
+                high = jnp.concatenate([part[0] for part in parts], axis=1)
+                low = jnp.concatenate([part[1] for part in parts], axis=1)
+                high_ref[rows, lanes] = high
+                low_ref[rows, lanes] = low
+                highs.append(high)
+                lows.append(low)
+            part = weights[:, start : start + wide]
+            total = total + (
+                dot_nn(part, jnp.concatenate(highs, axis=0)) + dot_nn(part, jnp.concatenate(lows, axis=0))
+            )
         out_ref[:, lanes] = folded(total)
 
 
@@ -131,15 +163,17 @@
             jax.ShapeDtypeStruct((probes, knots), jnp.float32),
             pltpu.VMEM((points, knots), jnp.bfloat16),
             pltpu.VMEM((points, knots), jnp.bfloat16),
+            jax.ShapeDtypeStruct(stack.shape, jnp.float32),
         ),
         in_specs=[VMEM, VMEM],
-        out_specs=(VMEM, VMEM, VMEM),
+        out_specs=(VMEM, VMEM, VMEM, VMEM),
         scratch_shapes=[
-            pltpu.VMEM((points, 8), jnp.float32),
+            pltpu.VMEM((points, LANES), jnp.float32),
+            pltpu.VMEM((points, LANES), jnp.float32),
             pltpu.VMEM((2 * probes, points), jnp.bfloat16),
         ],
         compiler_params=pltpu.CompilerParams(vmem_limit_bytes=LIMIT),
-        cost_estimate=cost(3000, points * knots, 2),
+        cost_estimate=cost(2300, points * knots, 2),
         name="project",
     )(stack, knot_locs)
 
@@ -150,20 +184,20 @@
     all_rows = precision_ref.shape[0]
     tile = min(TILE, all_rows)
     wide = min(TILE, depth)
-    weights[...] = padded_halves(proj_ref[...] * scale, weights.shape[0])
+    weights[...] = stacked_halves(proj_ref[...] * scale)
     owner = lax.rem(lax.axis_index("knot") + step, lax.axis_size("knot"))
     offset = owner * depth
 
     @pl.loop(0, all_rows // tile)
     def _(turn):
         rows = pl.ds(pl.multiple_of(turn * tile, tile), tile)
-        total = jnp.zeros((tile, weights.shape[0]), jnp.float32)
+        total = jnp.zeros((weights.shape[0], tile), jnp.float32)
         for start in range(0, depth, wide):
             lanes = pl.ds(pl.multiple_of(offset + start, wide), wide)
             high, low = halves(precision_ref[rows, lanes])
             part = weights[:, start : start + wide]
-            total = total + (dot_nt(high, part) + dot_nt(low, part))
-        found = folded_columns(total, probes)
+            total = total + (dot_nt(part, high) + dot_nt(part, low))
+        found = folded(total)
         if before_ref is not None:
             found = found + before_ref[:, rows]
         out_ref[:, rows] = found
@@ -183,7 +217,7 @@
         out_shape=jax.ShapeDtypeStruct((probes, rows), jnp.float32),
         in_specs=[VMEM] * (len(operands) - len(after)) + [pl.BlockSpec(memory_space=pl.ANY)] * len(after),
         out_specs=VMEM,
-        scratch_shapes=[pltpu.VMEM((LANES, depth), jnp.bfloat16)],
+        scratch_shapes=[pltpu.VMEM((2 * probes, depth), jnp.bfloat16)],
         compiler_params=pltpu.CompilerParams(vmem_limit_bytes=LIMIT),
         cost_estimate=cost(1200, rows * depth),
         name="factor",
@@ -217,6 +251,12 @@
     )(factor, high, low)
 
 
+def covariance(apart):
+    scaled = jnp.minimum(apart, 1.0)
+    remain = (1.0 - scaled) * (1.0 - scaled)
+    return jnp.exp2(scaled * (-LOG2E * TAPER_LEN / COV_RANGE)) * (remain * remain) * (1.0 + 4.0 * scaled)
+
+
 def taper_kernel(probes, first, ids_ref, counts_ref, own_ref, near_ref, out_ref, values):
     own_blocks, slots = ids_ref.shape
     block = own_ref.shape[1] // own_blocks
@@ -225,7 +265,6 @@
     north_base = lax.axis_index("knot") * own_blocks - 1
     north_cells = lax.axis_size("knot") * own_blocks
     inverse = 1.0 / TAPER_LEN
-    decay = -LOG2E * TAPER_LEN / COV_RANGE
     values[:, near_blocks * block :] = jnp.zeros((values.shape[0], block), jnp.bfloat16)
     values[:, : near_blocks * block] = padded_halves(near_ref[:probes, :], values.shape[0])
 
@@ -242,27 +281,24 @@
     for index in range(out_ref.shape[1] // block):
         group = first + index
         here = slice(group * block, (group + 1) * block)
-        own = as_columns(own_ref[probes : probes + 2, here] * inverse)
-        px = own[:, 0:1]
-        py = own[:, 1:2]
+        px, py = broadcast_columns(own_ref[probes : probes + 2, here] * inverse)
         total = jnp.zeros((block, values.shape[0]), jnp.float32)
         for pair in range(0, slots, 2):
-            highs, lows, parts = [], [], []
+            corners, parts = [], []
             for slot in range(pair, min(pair + 2, slots)):
                 spot, value_spot = place(group, slot)
                 lanes = lanes_of(spot)
-                qx = near_ref[probes : probes + 1, lanes] * inverse
-                qy = near_ref[probes + 1 : probes + 2, lanes] * inverse
-                scaled = jnp.minimum(distance(px, py, qx, qy), 1.0)
-                remain = (1.0 - scaled) * (1.0 - scaled)
-                covariance = jnp.exp2(scaled * decay) * (remain * remain) * (1.0 + 4.0 * scaled)
-                high, low = halves(covariance)
-                highs.append(high)
-                lows.append(low)
+                corners.append((near_ref[probes : probes + 1, lanes] * inverse, near_ref[probes + 1 : probes + 2, lanes] * inverse))
                 parts.append(values[:, lanes_of(value_spot)])
+            highs, lows = [], []
+            for slab in range(0, block, SLAB):
+                rows = slice(slab, slab + SLAB)
+                pieces = [halves(covariance(distance(px[rows], py[rows], *corner))) for corner in corners]
+                highs.append(jnp.concatenate([piece[0] for piece in pieces], axis=1))
+                lows.append(jnp.concatenate([piece[1] for piece in pieces], axis=1))
             part = jnp.concatenate(parts, axis=1)
             total = total + (
-                dot_nt(jnp.concatenate(highs, axis=1), part) + dot_nt(jnp.concatenate(lows, axis=1), part)
+                dot_nt(jnp.concatenate(highs, axis=0), part) + dot_nt(jnp.concatenate(lows, axis=0), part)
             )
         out_ref[:, index * block : (index + 1) * block] = (
             TAPER_SCALE * folded_columns(total, probes) + NUGGET * own_ref[:probes, here]
@@ -278,7 +314,7 @@
         out_specs=VMEM,
         scratch_shapes=[pltpu.VMEM((LANES, near.shape[1] + block), jnp.bfloat16)],
         compiler_params=pltpu.CompilerParams(vmem_limit_bytes=LIMIT),
-        cost_estimate=cost(6000, blocks * ids.shape[1] * block * block, 2),
+        cost_estimate=cost(4500, blocks * ids.shape[1] * block * block, 2),
         name="taper",
     )(ids, counts, own, near)
 
@@ -323,6 +359,9 @@
 
     stack, knots = prepare(probes, locations, knot_locs)
     chunks = [shifted(stack, "knot", step) for step in range(groups)]
+    rate = LOG2E / knot_range
+    parts = [project(chunk, knots, probe_count, rate) for chunk in chunks]
+    stack = parts[0][3]
     strips = [paired(stack, "space", 0), paired(stack, "space", 1)]
 
     first_blocks = jnp.concatenate([strip[:, :block_len] for strip in strips], axis=1)
@@ -352,8 +391,6 @@
         taper(neighbours, counts, stack, near, probe_count, i * per_piece, per_piece) for i in range(pieces)
     ]
 
-    rate = LOG2E / knot_range
-    parts = [project(chunk, knots, probe_count, rate) for chunk in chunks]
     projection = doubling_sum(sum(part[0] for part in parts), "space", "knot")
     factor = factored(None, projection, knot_precision, proj_scale, 0, base[:-1])
     for step in range(1, groups):

time: 43.3 us -> 46.3 us (1.069)
  waiting for transfers between devices: 3.45 us -> 9.6 us
  local copies, waits for them, and re-layouts: 3.67 us -> 1.43 us
  starting transfers between devices: 14.9 us -> 13.4 us
  Pallas kernels: 20 us -> 20.7 us
    ppermute x2, waiting for transfers between devices: 0.08 us -> 5.15 us  [paired(): return lax.ppermute(value, axis, pairs + [(b, a) for a, b in pairs])]
    unnamed x25 -> x19, local copies, waits for them, and re-layouts: 3.66 us -> 1.42 us
    ppermute x4, starting transfers between devices: 7.36 us -> 6.27 us  [doubling_sum(): value = value + lax.ppermute(value, (axis, other), pairs)]
    ppermute x4, waiting for transfers between devices: 3.36 us -> 4.44 us  [doubling_sum(): value = value + lax.ppermute(value, (axis, other), pairs)]
    pallas_call x1, Pallas kernels: 0.01 us -> 0.87 us  [prepare(): pl.pallas_call(prepare_kernel, out_shape=(jax.ShapeDtypeStruct((STACK_ROW...]
    pallas_call x2, Pallas kernels: 3.93 us -> 3.38 us  [factored(): pl.pallas_call(kernel, out_shape=jax.ShapeDtypeStruct((probes, rows), jnp...]
  transfers between devices with their start and end apart: 10 -> 10, of which waited for: 5 -> 5; matrix products, arithmetic and copies ran while one was open for 0% -> 0% of each run, Pallas kernels for 39% -> 37%
where the time goes in v5:
time: 46.3 us; the launch traced here: 46.1 us
  Pallas kernels  20.7 us (45%)
  starting transfers between devices  13.4 us (29%)
  waiting for transfers between devices  9.6 us (21%)
  local copies, waits for them, and re-layouts  1.43 us (3%)
  other arithmetic  0.74 us (2%)
    pallas_call x4, Pallas kernels, taper(): pl.pallas_call(functools.partial(taper_kernel, probes, first), out_shape=...  7.37 us
    pallas_call x2, Pallas kernels, project(): pl.pallas_call(functools.partial(project_kernel, probes, scale), out_shap...  6.55 us
    ppermute x4, starting transfers between devices, doubling_sum(): value = value + lax.ppermute(value, (axis, other), pairs)  6.27 us
    ppermute x2, starting transfers between devices, paired(): return lax.ppermute(value, axis, pairs + [(b, a) for a, b in pairs])  5.95 us
    ppermute x2, waiting for transfers between devices, paired(): return lax.ppermute(value, axis, pairs + [(b, a) for a, b in pairs])  5.15 us
    ppermute x4, waiting for transfers between devices, doubling_sum(): value = value + lax.ppermute(value, (axis, other), pairs)  4.44 us
    pallas_call x2, Pallas kernels, factored(): pl.pallas_call(kernel, out_shape=jax.ShapeDtypeStruct((probes, rows), jnp...  3.38 us
    pallas_call x2, Pallas kernels, spread(): pl.pallas_call(functools.partial(spread_kernel, scale), out_shape=jax.Sha...  2.56 us
  transfers between devices with their start and end apart: 10, of which 5 were waited for; matrix products, arithmetic and copies ran while one was open for 0% of the time, Pallas kernels for 37%

profile of v5, /device:TPU:0, one launch (start us, length us, event | category | flops | bytes accessed | tf_op | source)
XLA Modules:
  0.0 46.1 jit_solution(9461269358338879592)
XLA Ops:
  0.0 0.9 %prepare.1 = (f32[24,1024]{1,0:T(8,128)S(1)}, f32[2,1024]{1,0:T(2,128)S(1)}) custom-call(f32[16,1024]{1,0:T(8,128)} %probes_ref.1, f32[2,1024]{1,0:T(2,128)} %locations_ref.1, f32[2,1024]{1,0:T(2,128)} %knots_ref.1), custom_call_target="tpu_custom_call" | custom-call | tf_op jit(solution)/shard_map/prepare/pallas_call | solution.py:100
  0.9 0.5 %collective-permute-start = (f32[24,1024]{1,0:T(8,128)S(1)}, f32[24,1024]{1,0:T(8,128)S(1)}, u32[]{:S(2)}, u32[]{:S(2)}) collective-permute-start(f32[24,1024]{1,0:T(8,128)S(1)} %get-tuple-element.14.stack_ref), channel_id=1, source_target_pairs={{1,0},{0,1},{3,2},{2,3},{5,4},{4,5},{7,6},{6,7},{9,8},{8,9},{11,10... | collective-permute-start | bytes 294920 | tf_op jit(solution)/shard_map/ppermute | solution.py:341
  1.4 3.3 %project.2 = (f32[16,1024]{1,0:T(8,128)S(1)}, bf16[1024,1024]{1,0:T(8,128)(2,1)S(1)}, bf16[1024,1024]{1,0:T(8,128)(2,1)S(1)}, f32[24,1024]{1,0:T(8,128)S(1)}) custom-call(f32[24,1024]{1,0:T(8,128)S(1)} %get-tuple-element.14.stack_ref, f32[2,1024]{1,0:T(2,128)S(1)} %get-tuple-element.15.knots_ref), custom_call_target="tpu_custom_call" | custom-call | flops 2411724800 | bytes 4194304 | tf_op jit(solution)/shard_map/project/pallas_call | solution.py:160
  4.7 0.0 copy-start
  4.7 1.3 %copy-done = bf16[1024,1024]{1,0:T(8,128)(2,1)} copy-done((bf16[1024,1024]{1,0:T(8,128)(2,1)}, bf16[1024,1024]{1,0:T(8,128)(2,1)S(1)}, u32[]{:S(2)}) %copy-start) | copy-done | bytes 2097176
  6.0 0.7 %collective-permute-start.2 = (f32[24,1024]{1,0:T(8,128)S(1)}, f32[24,1024]{1,0:T(8,128)S(1)}, u32[]{:S(2)}, u32[]{:S(2)}) collective-permute-start(f32[24,1024]{1,0:T(8,128)S(1)} %get-tuple-element.16.own_ref), channel_id=1, source_target_pairs={{2,4},{6,8},{10,12},{14,16},{18,20},{22,24},{26,28},{4,2},{8,6},{1... | collective-permute-start | bytes 294920 | tf_op jit(solution)/shard_map/ppermute | solution.py:347
  6.7 5.3 %collective-permute-start.1 = (f32[24,1024]{1,0:T(8,128)S(1)}, f32[24,1024]{1,0:T(8,128)S(1)}, u32[]{:S(2)}, u32[]{:S(2)}) collective-permute-start(f32[24,1024]{1,0:T(8,128)S(1)} %get-tuple-element.16.own_ref), channel_id=1, source_target_pairs={{0,2},{4,6},{8,10},{12,14},{16,18},{20,22},{24,26},{28,30},{2,0},{... | collective-permute-start | bytes 294920 | tf_op jit(solution)/shard_map/ppermute | solution.py:347
  12.0 0.0 collective-permute-done.stack_ref
  12.0 0.0 collective-permute-done.2
  12.0 5.1 %collective-permute-done.1 = f32[24,1024]{1,0:T(8,128)S(1)} collective-permute-done((f32[24,1024]{1,0:T(8,128)S(1)}, f32[24,1024]{1,0:T(8,128)S(1)}, u32[]{:S(2)}, u32[]{:S(2)}) %collective-permute-start.1) | collective-permute-done | bytes 98336 | tf_op jit(solution)/shard_map/ppermute | solution.py:347
  17.2 0.0 copy-start.2
  17.2 0.0 copy-start.3
  17.2 0.1 collective-permute-start.3
  17.3 3.3 %project.3 = (f32[16,1024]{1,0:T(8,128)S(1)}, bf16[1024,1024]{1,0:T(8,128)(2,1)S(1)}, bf16[1024,1024]{1,0:T(8,128)(2,1)S(1)}, f32[24,1024]{1,0:T(8,128)}) custom-call(f32[24,1024]{1,0:T(8,128)S(1)} %collective-permute-done.stack_ref, f32[2,1024]{1,0:T(2,128)S(1)} %get-tuple-element.15.knots_ref), custom_call_target="tpu_custom_call" | custom-call | flops 2411724800 | bytes 4194304 | tf_op jit(solution)/shard_map/project/pallas_call | solution.py:160
  20.6 1.9 %collective-permute-start.4 = (f32[16,1024]{1,0:T(8,128)S(1)}, f32[16,1024]{1,0:T(8,128)S(1)}, u32[]{:S(2)}, u32[]{:S(2)}) collective-permute-start(f32[16,1024]{1,0:T(8,128)S(1)} %add.21), channel_id=1, source_target_pairs={{0,2},{2,0},{4,6},{6,4},{8,10},{10,8},{12,14},{14,12},{16,18},{18,... | collective-permute-start | bytes 196616 | tf_op jit(solution)/shard_map/ppermute | solution.py:333
  22.5 0.0 collective-permute-done.3
  22.6 0.0 copy-done.2
  22.6 0.0 copy-done.3
  22.6 0.0 slice-start
  22.6 1.8 %taper.6.rest_2_ = f32[16,256]{1,0:T(8,128)S(1)} custom-call(s32[8,8]{1,0:T(8,128)S(1)} %copy-done.2, s32[8]{0:T(128)S(1)} %copy-done.3, f32[24,1024]{1,0:T(8,128)S(1)} %get-tuple-element.16.own_ref, f32[24,3840]{1,0:T(8,128)S(1)} %constant_dynamic-update-slice_fusion.near_ref), custom_call_target="tpu_custom_call" | custom-call | flops 1179648000 | bytes 1048576 | tf_op jit(solution)/shard_map/taper/pallas_call | solution.py:310
  24.4 0.5 %collective-permute-done.4 = f32[16,1024]{1,0:T(8,128)S(1)} collective-permute-done((f32[16,1024]{1,0:T(8,128)S(1)}, f32[16,1024]{1,0:T(8,128)S(1)}, u32[]{:S(2)}, u32[]{:S(2)}) %collective-permute-start.4) | collective-permute-done | bytes 65568 | tf_op jit(solution)/shard_map/ppermute | solution.py:333
  24.9 0.1 collective-permute-start.5
  25.0 1.8 %taper.5.rest_1_ = f32[16,256]{1,0:T(8,128)S(1)} custom-call(s32[8,8]{1,0:T(8,128)S(1)} %copy-done.2, s32[8]{0:T(128)S(1)} %copy-done.3, f32[24,1024]{1,0:T(8,128)S(1)} %get-tuple-element.16.own_ref, f32[24,3840]{1,0:T(8,128)S(1)} %constant_dynamic-update-slice_fusion.near_ref), custom_call_target="tpu_custom_call" | custom-call | flops 1179648000 | bytes 1048576 | tf_op jit(solution)/shard_map/taper/pallas_call | solution.py:310
  26.9 2.4 %collective-permute-done.5 = f32[16,1024]{1,0:T(8,128)S(1)} collective-permute-done((f32[16,1024]{1,0:T(8,128)S(1)}, f32[16,1024]{1,0:T(8,128)S(1)}, u32[]{:S(2)}, u32[]{:S(2)}) %collective-permute-start.5) | collective-permute-done | bytes 65568 | tf_op jit(solution)/shard_map/ppermute | solution.py:333
  29.3 0.0 slice-start.1
  29.3 1.6 %collective-permute-start.6 = (f32[16,1024]{1,0:T(8,128)S(1)}, f32[16,1024]{1,0:T(8,128)S(1)}, u32[]{:S(2)}, u32[]{:S(2)}) collective-permute-start(f32[16,1024]{1,0:T(8,128)S(1)} %add.23), channel_id=1, source_target_pairs={{0,8},{2,10},{4,12},{6,14},{8,0},{10,2},{12,4},{14,6},{16,24},{18,... | collective-permute-start | bytes 196616 | tf_op jit(solution)/shard_map/ppermute | solution.py:333
  30.9 1.8 %taper.4.rest_0_ = f32[16,256]{1,0:T(8,128)S(1)} custom-call(s32[8,8]{1,0:T(8,128)S(1)} %copy-done.2, s32[8]{0:T(128)S(1)} %copy-done.3, f32[24,1024]{1,0:T(8,128)S(1)} %get-tuple-element.16.own_ref, f32[24,3840]{1,0:T(8,128)S(1)} %constant_dynamic-update-slice_fusion.near_ref), custom_call_target="tpu_custom_call" | custom-call | flops 1179648000 | bytes 1048576 | tf_op jit(solution)/shard_map/taper/pallas_call | solution.py:310
  32.8 0.8 %collective-permute-done.6 = f32[16,1024]{1,0:T(8,128)S(1)} collective-permute-done((f32[16,1024]{1,0:T(8,128)S(1)}, f32[16,1024]{1,0:T(8,128)S(1)}, u32[]{:S(2)}, u32[]{:S(2)}) %collective-permute-start.6) | collective-permute-done | bytes 65568 | tf_op jit(solution)/shard_map/ppermute | solution.py:333
  33.6 2.7 %collective-permute-start.7 = (f32[16,1024]{1,0:T(8,128)S(1)}, f32[16,1024]{1,0:T(8,128)S(1)}, u32[]{:S(2)}, u32[]{:S(2)}) collective-permute-start(f32[16,1024]{1,0:T(8,128)S(1)} %add.24), channel_id=1, source_target_pairs={{0,16},{2,18},{4,20},{6,22},{8,24},{10,26},{12,28},{14,30},{16,0},... | collective-permute-start | bytes 196616 | tf_op jit(solution)/shard_map/ppermute | solution.py:333
  36.3 1.8 %taper.7 = f32[16,256]{1,0:T(8,128)S(1)} custom-call(s32[8,8]{1,0:T(8,128)S(1)} %copy-done.2, s32[8]{0:T(128)S(1)} %copy-done.3, f32[24,1024]{1,0:T(8,128)S(1)} %get-tuple-element.16.own_ref, f32[24,3840]{1,0:T(8,128)S(1)} %constant_dynamic-update-slice_fusion.near_ref), custom_call_target="tpu_custom_call" | custom-call | flops 1179648000 | bytes 1048576 | tf_op jit(solution)/shard_map/taper/pallas_call | solution.py:310
  38.1 0.7 %collective-permute-done.7 = f32[16,1024]{1,0:T(8,128)S(1)} collective-permute-done((f32[16,1024]{1,0:T(8,128)S(1)}, f32[16,1024]{1,0:T(8,128)S(1)}, u32[]{:S(2)}, u32[]{:S(2)}) %collective-permute-start.7) | collective-permute-done | bytes 65568 | tf_op jit(solution)/shard_map/ppermute | solution.py:333
  38.9 0.1 collective-permute-start.8
  39.0 0.0 slice-done
  39.0 0.0 slice-done.1
  39.0 1.7 %factor.2.before_ref = f32[16,1024]{1,0:T(8,128)S(1)} custom-call(f32[16,1024]{1,0:T(8,128)S(1)} %add.25.proj_ref, f32[1024,2048]{1,0:T(8,128)S(1)} %bitcast.1, f32[16,256]{1,0:T(8,128)S(1)} %taper.4.rest_0_, f32[16,256]{1,0:T(8,128)S(1)} %taper.5.rest_1_, f32[16,256]{1,0:T(8,128)S(1)} %taper.6.rest_2_), custom_call_target="tpu_custom_call" | custom-call | flops 1258291200 | bytes 4194304 | tf_op jit(solution)/shard_map/factor/pallas_call | solution.py:215
  40.7 0.0 collective-permute-done.8.proj_ref
  40.7 1.7 %factor.3.factor_ref = f32[16,1024]{1,0:T(8,128)S(1)} custom-call(f32[16,1024]{1,0:T(8,128)S(1)} %factor.2.before_ref, f32[16,1024]{1,0:T(8,128)S(1)} %collective-permute-done.8.proj_ref, f32[1024,2048]{1,0:T(8,128)S(1)} %bitcast.1), custom_call_target="tpu_custom_call" | custom-call | flops 1258291200 | bytes 4194304 | tf_op jit(solution)/shard_map/factor/pallas_call | solution.py:215
  42.4 0.0 copy-start.1
  42.4 1.3 %spread.2 = f32[16,1024]{1,0:T(8,128)S(1)} custom-call(f32[16,1024]{1,0:T(8,128)S(1)} %factor.3.factor_ref, bf16[1024,1024]{1,0:T(8,128)(2,1)S(1)} %get-tuple-element.19.high_ref, bf16[1024,1024]{1,0:T(8,128)(2,1)S(1)} %get-tuple-element.20.low_ref), custom_call_target="tpu_custom_call" | custom-call | flops 891289600 | bytes 4194304 | tf_op jit(solution)/shard_map/spread/pallas_call | solution.py:242
  43.7 0.5 %collective-permute-start.9 = (f32[16,1024]{1,0:T(8,128)S(1)}, f32[16,1024]{1,0:T(8,128)S(1)}, u32[]{:S(2)}, u32[]{:S(2)}) collective-permute-start(f32[16,1024]{1,0:T(8,128)S(1)} %spread.2), channel_id=1, source_target_pairs={{1,0},{0,1},{3,2},{2,3},{5,4},{4,5},{7,6},{6,7},{9,8},{8,9},{11,10... | collective-permute-start | bytes 196616 | tf_op jit(solution)/shard_map/ppermute | solution.py:341
  44.2 0.0 copy-done.1
  44.2 1.3 %spread.3 = f32[16,1024]{1,0:T(8,128)S(1)} custom-call(f32[16,1024]{1,0:T(8,128)S(1)} %factor.3.factor_ref, bf16[1024,1024]{1,0:T(8,128)(2,1)S(1)} %get-tuple-element.21.high_ref, bf16[1024,1024]{1,0:T(8,128)(2,1)S(1)} %copy-done.1), custom_call_target="tpu_custom_call" | custom-call | flops 891289600 | bytes 4194304 | tf_op jit(solution)/shard_map/spread/pallas_call | solution.py:242
  45.5 0.0 collective-permute-done.9
  45.5 0.7 %fusion = f32[16,1024]{1,0:T(8,128)} fusion(f32[16,1024]{1,0:T(8,128)S(1)} %spread.3, f32[16,1024]{1,0:T(8,128)S(1)} %collective-permute-done.9, f32[16,256]{1,0:T(8,128)S(1)} %taper.7, f32[16,256]{1,0:T(8,128)S(1)} %taper.6.rest_2_, f32[16,256]{1,0:T(8,128)S(1)} %taper.5.rest_1_, f32[16,256]{1,0:T(8,128)S(1)} %taper.4.rest_0_), kind=kLoop, calls=%fused_computation.1 | loop fusion | flops 81920 | bytes 262144 | tf_op jit(solution)/shard_map/add | solution.py:401
  (17 shorter events, 0.1 us)
Async XLA Ops:
  0.9 11.1 %collective-permute-start = (f32[24,1024]{1,0:T(8,128)S(1)}, f32[24,1024]{1,0:T(8,128)S(1)}, u32[]{:S(2)}, u32[]{:S(2)}) collective-permute-start(f32[24,1024]{1,0:T(8,128)S(1)} %get-tuple-element.14.stack_ref), channel_id=1, source_target_pairs={{1,0},{0,1},{3,2},{2,3},{5,4},{4,5},{7,6},{6,7},{9,8},{8,9},{11,10... | collective-permute-start | bytes 294920 | tf_op jit(solution)/shard_map/ppermute | solution.py:341
  4.7 1.3 %copy-start = (bf16[1024,1024]{1,0:T(8,128)(2,1)}, bf16[1024,1024]{1,0:T(8,128)(2,1)S(1)}, u32[]{:S(2)}) copy-start(bf16[1024,1024]{1,0:T(8,128)(2,1)S(1)} %get-tuple-element.22.low_ref) | copy-start | bytes 6291460
  6.0 6.0 %collective-permute-start.2 = (f32[24,1024]{1,0:T(8,128)S(1)}, f32[24,1024]{1,0:T(8,128)S(1)}, u32[]{:S(2)}, u32[]{:S(2)}) collective-permute-start(f32[24,1024]{1,0:T(8,128)S(1)} %get-tuple-element.16.own_ref), channel_id=1, source_target_pairs={{2,4},{6,8},{10,12},{14,16},{18,20},{22,24},{26,28},{4,2},{8,6},{1... | collective-permute-start | bytes 294920 | tf_op jit(solution)/shard_map/ppermute | solution.py:347
  6.7 10.5 %collective-permute-start.1 = (f32[24,1024]{1,0:T(8,128)S(1)}, f32[24,1024]{1,0:T(8,128)S(1)}, u32[]{:S(2)}, u32[]{:S(2)}) collective-permute-start(f32[24,1024]{1,0:T(8,128)S(1)} %get-tuple-element.16.own_ref), channel_id=1, source_target_pairs={{0,2},{4,6},{8,10},{12,14},{16,18},{20,22},{24,26},{28,30},{2,0},{... | collective-permute-start | bytes 294920 | tf_op jit(solution)/shard_map/ppermute | solution.py:347
  17.2 5.4 %copy-start.2 = (s32[8,8]{1,0:T(8,128)S(1)}, s32[8,8]{1,0:T(8,128)}, u32[]{:S(2)}) copy-start(s32[8,8]{1,0:T(8,128)} %ids_ref.7) | copy-start | bytes 772
  17.2 5.4 %copy-start.3 = (s32[8]{0:T(128)S(1)}, s32[8]{0:T(128)}, u32[]{:S(2)}) copy-start(s32[8]{0:T(128)} %counts_ref.7) | copy-start | bytes 100
  17.2 5.3 %collective-permute-start.3 = (f32[24,256]{1,0:T(8,128)S(1)}, f32[24,256]{1,0:T(8,128)S(1)}, u32[]{:S(2)}, u32[]{:S(2)}) collective-permute-start(f32[24,256]{1,0:T(8,128)S(1)} %maximum_select_fusion), channel_id=1, source_target_pairs={{1,0},{0,1},{3,2},{2,3},{5,4},{4,5},{7,6},{6,7},{9,8},{8,9},{11,10... | collective-permute-start | bytes 73736 | tf_op jit(solution)/shard_map/ppermute | solution.py:341
  20.6 4.3 %collective-permute-start.4 = (f32[16,1024]{1,0:T(8,128)S(1)}, f32[16,1024]{1,0:T(8,128)S(1)}, u32[]{:S(2)}, u32[]{:S(2)}) collective-permute-start(f32[16,1024]{1,0:T(8,128)S(1)} %add.21), channel_id=1, source_target_pairs={{0,2},{2,0},{4,6},{6,4},{8,10},{10,8},{12,14},{14,12},{16,18},{18,... | collective-permute-start | bytes 196616 | tf_op jit(solution)/shard_map/ppermute | solution.py:333
  22.6 16.4 %slice-start = ((s8[8388608]{0:T(1024)(128)(4,1)}), s8[4194304]{0:T(1024)(128)(4,1)S(1)}, s32[]{:S(2)}) async-start(s8[8388608]{0:T(1024)(128)(4,1)} %bitcast), calls=%async_computation | async-start | bytes 8388608
  24.9 4.3 %collective-permute-start.5 = (f32[16,1024]{1,0:T(8,128)S(1)}, f32[16,1024]{1,0:T(8,128)S(1)}, u32[]{:S(2)}, u32[]{:S(2)}) collective-permute-start(f32[16,1024]{1,0:T(8,128)S(1)} %add.22), channel_id=1, source_target_pairs={{0,4},{2,6},{4,0},{6,2},{8,12},{10,14},{12,8},{14,10},{16,20},{18,... | collective-permute-start | bytes 196616 | tf_op jit(solution)/shard_map/ppermute | solution.py:333
  29.3 9.7 %slice-start.1 = ((s8[8388608]{0:T(1024)(128)(4,1)}), s8[4194304]{0:T(1024)(128)(4,1)S(1)}, s32[]{:S(2)}) async-start(s8[8388608]{0:T(1024)(128)(4,1)} %bitcast), calls=%async_computation.1 | async-start | bytes 8388608
  29.3 4.3 %collective-permute-start.6 = (f32[16,1024]{1,0:T(8,128)S(1)}, f32[16,1024]{1,0:T(8,128)S(1)}, u32[]{:S(2)}, u32[]{:S(2)}) collective-permute-start(f32[16,1024]{1,0:T(8,128)S(1)} %add.23), channel_id=1, source_target_pairs={{0,8},{2,10},{4,12},{6,14},{8,0},{10,2},{12,4},{14,6},{16,24},{18,... | collective-permute-start | bytes 196616 | tf_op jit(solution)/shard_map/ppermute | solution.py:333
  33.6 5.2 %collective-permute-start.7 = (f32[16,1024]{1,0:T(8,128)S(1)}, f32[16,1024]{1,0:T(8,128)S(1)}, u32[]{:S(2)}, u32[]{:S(2)}) collective-permute-start(f32[16,1024]{1,0:T(8,128)S(1)} %add.24), channel_id=1, source_target_pairs={{0,16},{2,18},{4,20},{6,22},{8,24},{10,26},{12,28},{14,30},{16,0},... | collective-permute-start | bytes 196616 | tf_op jit(solution)/shard_map/ppermute | solution.py:333
  38.9 1.8 %collective-permute-start.8 = (f32[16,1024]{1,0:T(8,128)S(1)}, f32[16,1024]{1,0:T(8,128)S(1)}, u32[]{:S(2)}, u32[]{:S(2)}) collective-permute-start(f32[16,1024]{1,0:T(8,128)S(1)} %add.25.proj_ref), channel_id=1, source_target_pairs={{1,0},{0,1},{3,2},{2,3},{5,4},{4,5},{7,6},{6,7},{9,8},{8,9},{11,10... | collective-permute-start | bytes 196616 | tf_op jit(solution)/shard_map/ppermute | solution.py:341
  42.4 1.8 %copy-start.1 = (bf16[1024,1024]{1,0:T(8,128)(2,1)S(1)}, bf16[1024,1024]{1,0:T(8,128)(2,1)}, u32[]{:S(2)}) copy-start(bf16[1024,1024]{1,0:T(8,128)(2,1)} %copy-done) | copy-start | bytes 6291460
  43.7 1.8 %collective-permute-start.9 = (f32[16,1024]{1,0:T(8,128)S(1)}, f32[16,1024]{1,0:T(8,128)S(1)}, u32[]{:S(2)}, u32[]{:S(2)}) collective-permute-start(f32[16,1024]{1,0:T(8,128)S(1)} %spread.2), channel_id=1, source_target_pairs={{1,0},{0,1},{3,2},{2,3},{5,4},{4,5},{7,6},{6,7},{9,8},{8,9},{11,10... | collective-permute-start | bytes 196616 | tf_op jit(solution)/shard_map/ppermute | solution.py:341

commit v6 on v5

v6 whole, which is shorter than its diff:
```python
import functools
import math

import jax
import jax.numpy as jnp
from jax import lax
from jax.experimental import pallas as pl
from jax.experimental.pallas import tpu as pltpu
from jax.sharding import PartitionSpec as P

COV_RANGE = 0.05
TAPER_LEN = 0.15
KNOT_REACH = 0.15
TAPER_SCALE = 0.1
PROJ_GAIN = 0.5
EXPAND_GAIN = 0.5
LOW_SCALE = 0.5
NUGGET = 0.25
LOG2E = math.log2(math.e)
CELL = 0.1
TINY = 1e-30
TILE = 256
LANES = 128
HALF_GRAIN = 2.0**-24
LIMIT = 6 * 1024 * 1024
VMEM = pl.BlockSpec(memory_space=pltpu.VMEM)
HBM = pl.BlockSpec(memory_space=pltpu.HBM)
SMEM = pl.BlockSpec(memory_space=pltpu.SMEM)


def halves(x):
    high = x.astype(jnp.bfloat16)
    return high, (x - high.astype(jnp.float32)).astype(jnp.bfloat16)


def stacked_halves(x):
    return jnp.concatenate(halves(x), axis=0)


def folded(x):
    rows = x.shape[0] // 2
    return x[:rows] + x[rows:]


def dot_nt(left, right):
    return lax.dot_general(
        left, right, (((1,), (1,)), ((), ())), preferred_element_type=jnp.float32
    )


def dot_nn(left, right):
    return jnp.dot(left, right, preferred_element_type=jnp.float32)


def distance(ax, ay, bx, by):
    dx = ax - bx
    dy = ay - by
    square = dx * dx + dy * dy
    return square * lax.rsqrt(jnp.maximum(square, TINY))


def padded_halves(x, rows):
    fill = jnp.zeros((rows - 2 * x.shape[0], x.shape[1]), jnp.bfloat16)
    return jnp.concatenate([*halves(x), fill], axis=0)


def folded_columns(x, rows):
    x = jnp.transpose(x)
    return x[:rows] + x[rows : 2 * rows]


def cost(work, pairs, transcendentals=0):
    return pl.CostEstimate(flops=work * pairs, bytes_accessed=4 * pairs, transcendentals=transcendentals * pairs)


def coordinate_rows(ref, points, axis):
    start = points + axis * LANES
    return ref[:, start : start + LANES]


def prepare_kernel(blocks, probes_ref, locations_ref, knots_ref, stack_ref, knots_out_ref, coords, sems):
    points = probes_ref.shape[1]
    block = points // blocks
    copies = [
        pltpu.make_async_copy(probes_ref, stack_ref.at[:, pl.ds(0, points)], sems.at[0]),
        pltpu.make_async_copy(locations_ref, coords, sems.at[1]),
        pltpu.make_async_copy(knots_ref, knots_out_ref, sems.at[2]),
    ]
    for copy in copies:
        copy.start()
    for copy in copies:
        copy.wait()
    stack_ref[:, points:] = jnp.zeros((stack_ref.shape[0], 2 * LANES), jnp.float32)
    for axis in range(2):
        lanes = slice(points + axis * LANES, points + (axis + 1) * LANES)
        for index in range(blocks):
            stack_ref[index : index + 1, lanes] = coords[axis : axis + 1, index * block : (index + 1) * block]


def prepare(probes, locations, knot_locs, blocks):
    rows, points = probes.shape
    assert points == blocks * LANES and blocks + 2 <= rows
    probes, locations, knot_locs = [
        pltpu.with_memory_space_constraint(x, pltpu.HBM) for x in (probes, locations, knot_locs)
    ]
    return pl.pallas_call(
        functools.partial(prepare_kernel, blocks),
        out_shape=(
            jax.ShapeDtypeStruct((rows, points + 2 * LANES), jnp.float32),
            jax.ShapeDtypeStruct(knot_locs.shape, jnp.float32),
        ),
        in_specs=[HBM, HBM, HBM],
        out_specs=(VMEM, VMEM),
        scratch_shapes=[pltpu.VMEM(locations.shape, jnp.float32), pltpu.SemaphoreType.DMA((3,))],
        compiler_params=pltpu.CompilerParams(vmem_limit_bytes=LIMIT),
        name="prepare",
    )(probes, locations, knot_locs)


def strip_kernel(below_ref, own_ref, above_ref, out_ref):
    rows, width = own_ref.shape
    points = width - 2 * LANES
    blocks = points // LANES
    out_ref[:, :LANES] = below_ref[:, points - LANES : points]
    out_ref[:, LANES : points + LANES] = own_ref[:, :points]
    out_ref[:, points + LANES : points + 2 * LANES] = above_ref[:, :LANES]
    for axis in range(2):
        lanes = slice(points + axis * LANES, points + (axis + 1) * LANES)
        target = slice(lanes.start + 2 * LANES, lanes.stop + 2 * LANES)
        out_ref[:, target] = jnp.zeros((rows, LANES), jnp.float32)
        out_ref[0:1, target] = below_ref[blocks - 1 : blocks, lanes]
        out_ref[1 : blocks + 1, target] = own_ref[:blocks, lanes]
        out_ref[blocks + 1 : blocks + 2, target] = above_ref[0:1, lanes]


def make_strip(below, own, above):
    return pl.pallas_call(
        strip_kernel,
        out_shape=jax.ShapeDtypeStruct((own.shape[0], own.shape[1] + 2 * LANES), jnp.float32),
        in_specs=[VMEM, VMEM, VMEM],
        out_specs=VMEM,
        compiler_params=pltpu.CompilerParams(vmem_limit_bytes=LIMIT),
        name="strip",
    )(below, own, above)


def project_kernel(scale, grain, stack_ref, knots_ref, out_ref, high_ref, low_ref, copy_ref, columns, weights):
    points, knots = high_ref.shape
    probes = stack_ref.shape[0]
    tile = min(TILE, knots)
    wide = min(TILE, points)
    copy_ref[...] = stack_ref[...]
    for axis in range(2):
        turned = jnp.transpose(coordinate_rows(stack_ref, points, axis) * scale)
        turned = (turned + grain) - grain
        for index in range(points // LANES):
            columns[index * LANES : (index + 1) * LANES, axis : axis + 1] = turned[:, index : index + 1]
    weights[...] = stacked_halves(stack_ref[:, :points])

    @pl.loop(0, knots // tile)
    def _(step):
        lanes = pl.ds(pl.multiple_of(step * tile, tile), tile)
        kx, ky = [
            (knots_ref[axis : axis + 1, lanes] * scale + grain) - (grain - grain * HALF_GRAIN) for axis in range(2)
        ]
        total = jnp.zeros((2 * probes, tile), jnp.float32)
        for start in range(0, points, wide):
            rows = slice(start, start + wide)
            dx = columns[rows, 0:1] - kx
            dy = columns[rows, 1:2] - ky
            square = dx * dx + dy * dy
            high, low = halves(jnp.exp2(-(square * lax.rsqrt(square))))
            high_ref[rows, lanes] = high
            low_ref[rows, lanes] = low
            part = weights[:, rows]
            total = total + (dot_nn(part, high) + dot_nn(part, low))
        out_ref[:, lanes] = folded(total)


def project(stack, knot_locs, scale, extent):
    probes, points, knots = stack.shape[0], stack.shape[1] - 2 * LANES, knot_locs.shape[1]
    grain = 2.0 ** math.ceil(math.log2(1.01 * scale * extent))
    return pl.pallas_call(
        functools.partial(project_kernel, scale, grain),
        out_shape=(
            jax.ShapeDtypeStruct((probes, knots), jnp.float32),
            pltpu.VMEM((points, knots), jnp.bfloat16),
            pltpu.VMEM((points, knots), jnp.bfloat16),
            jax.ShapeDtypeStruct(stack.shape, jnp.float32),
        ),
        in_specs=[VMEM, VMEM],
        out_specs=(VMEM, VMEM, VMEM, VMEM),
        scratch_shapes=[
            pltpu.VMEM((points, 8), jnp.float32),
            pltpu.VMEM((2 * probes, points), jnp.bfloat16),
        ],
        compiler_params=pltpu.CompilerParams(vmem_limit_bytes=LIMIT),
        cost_estimate=cost(2800, points * knots, 2),
        name="project",
    )(stack, knot_locs)


def factor_kernel(scale, step, before_ref, proj_ref, precision_ref, *rest):
    out_ref, weights = rest[-2:]
    probes, depth = proj_ref.shape
    all_rows = precision_ref.shape[0]
    tile = min(TILE, all_rows)
    wide = min(TILE, depth)
    weights[...] = stacked_halves(proj_ref[...] * scale)
    owner = lax.rem(lax.axis_index("knot") + step, lax.axis_size("knot"))
    offset = owner * depth

    @pl.loop(0, all_rows // tile)
    def _(turn):
        rows = pl.ds(pl.multiple_of(turn * tile, tile), tile)
        total = jnp.zeros((weights.shape[0], tile), jnp.float32)
        for start in range(0, depth, wide):
            lanes = pl.ds(pl.multiple_of(offset + start, wide), wide)
            high, low = halves(precision_ref[rows, lanes])
            part = weights[:, start : start + wide]
            total = total + (dot_nt(part, high) + dot_nt(part, low))
        found = folded(total)
        if before_ref is not None:
            found = found + before_ref[:, rows]
        out_ref[:, rows] = found


def factored(before, projection, precision, scale, step, after=()):
    probes, depth = projection.shape
    rows = precision.shape[0]
    kernel = functools.partial(factor_kernel, scale, step)
    operands = (projection, precision, *after)
    if before is None:
        kernel = functools.partial(kernel, None)
    else:
        operands = (before, *operands)
    return pl.pallas_call(
        kernel,
        out_shape=jax.ShapeDtypeStruct((probes, rows), jnp.float32),
        in_specs=[VMEM] * (len(operands) - len(after)) + [pl.BlockSpec(memory_space=pl.ANY)] * len(after),
        out_specs=VMEM,
        scratch_shapes=[pltpu.VMEM((2 * probes, depth), jnp.bfloat16)],
        compiler_params=pltpu.CompilerParams(vmem_limit_bytes=LIMIT),
        cost_estimate=cost(1200, rows * depth),
        name="factor",
    )(*operands)


def spread_kernel(scale, factor_ref, high_ref, low_ref, out_ref, weights):
    probes = factor_ref.shape[0]
    points = high_ref.shape[0]
    tile = min(TILE, points)
    weights[...] = padded_halves(factor_ref[...] * scale, weights.shape[0])
    for start in range(0, points, tile):
        rows = slice(start, start + tile)
        total = dot_nt(high_ref[rows, :], weights[...]) + dot_nt(low_ref[rows, :], weights[...])
        out_ref[:, rows] = folded_columns(total, probes)


def spread(factor, high, low, scale):
    (probes, knots), points = factor.shape, high.shape[0]
    high = pltpu.with_memory_space_constraint(high, pltpu.VMEM)
    low = pltpu.with_memory_space_constraint(low, pltpu.VMEM)
    return pl.pallas_call(
        functools.partial(spread_kernel, scale),
        out_shape=jax.ShapeDtypeStruct((probes, points), jnp.float32),
        in_specs=[VMEM, VMEM, VMEM],
        out_specs=VMEM,
        scratch_shapes=[pltpu.VMEM((LANES, knots), jnp.bfloat16)],
        compiler_params=pltpu.CompilerParams(vmem_limit_bytes=LIMIT),
        cost_estimate=cost(850, knots * points),
        name="spread",
    )(factor, high, low)


def covariance(apart):
    scaled = jnp.minimum(apart, 1.0)
    remain = (1.0 - scaled) * (1.0 - scaled)
    return jnp.exp2(scaled * (-LOG2E * TAPER_LEN / COV_RANGE)) * (remain * remain) * (1.0 + 4.0 * scaled)


def taper_kernel(first, ids_ref, counts_ref, own_ref, near_ref, out_ref, values, coords):
    own_blocks, slots = ids_ref.shape
    block = LANES
    strips, probes, width = near_ref.shape
    span = own_blocks + 2
    column = lax.axis_index("space")
    north_base = lax.axis_index("knot") * own_blocks - 1
    north_cells = lax.axis_size("knot") * own_blocks
    inverse = 1.0 / TAPER_LEN
    values[:, strips * span * block :] = jnp.zeros((values.shape[0], block), jnp.bfloat16)
    for strip in range(strips):
        values[:, strip * span * block : (strip + 1) * span * block] = padded_halves(
            near_ref[strip, :, : span * block], values.shape[0]
        )
        for axis in range(2):
            rows = near_ref[strip, :, (span + axis) * block : (span + axis + 1) * block] * inverse
            for index in range(span):
                start = (strip * span + index) * block
                coords[axis : axis + 1, start : start + block] = rows[index : index + 1]
    own_columns = [
        jnp.transpose(coordinate_rows(own_ref, own_blocks * block, axis) * inverse) for axis in range(2)
    ]

    def place(group, slot):
        ahead = ids_ref[group, slot] - (column - 1) * north_cells
        east = jnp.where(ahead >= north_cells, 1, 0) + jnp.where(ahead >= 2 * north_cells, 1, 0)
        strip = jnp.where(east == 1, 0, 1 + lax.rem(column + lax.div(east, 2) + 1, 2))
        index = strip * span + (ahead - east * north_cells - north_base)
        return lanes_of(index), lanes_of(jnp.where(slot < counts_ref[group], index, strips * span))

    def lanes_of(index):
        return pl.ds(pl.multiple_of(index * block, block), block)

    for index in range(out_ref.shape[1] // block):
        group = first + index
        px, py = [turned[:, group : group + 1] for turned in own_columns]
        total = jnp.zeros((block, values.shape[0]), jnp.float32)
        for pair in range(0, slots, 2):
            highs, lows, parts = [], [], []
            for slot in range(pair, min(pair + 2, slots)):
                lanes, value_lanes = place(group, slot)
                high, low = halves(covariance(distance(px, py, coords[0:1, lanes], coords[1:2, lanes])))
                highs.append(high)
                lows.append(low)
                parts.append(values[:, value_lanes])
            part = jnp.concatenate(parts, axis=1)
            total = total + (
                dot_nt(jnp.concatenate(highs, axis=1), part) + dot_nt(jnp.concatenate(lows, axis=1), part)
            )
        out_ref[:, index * block : (index + 1) * block] = (
            TAPER_SCALE * folded_columns(total, probes)
            + NUGGET * own_ref[:, group * block : (group + 1) * block]
        )


def taper(ids, counts, own, near, first, blocks):
    own_blocks, slots = ids.shape
    strips, probes, width = near.shape
    return pl.pallas_call(
        functools.partial(taper_kernel, first),
        out_shape=jax.ShapeDtypeStruct((probes, blocks * LANES), jnp.float32),
        in_specs=[SMEM, SMEM, VMEM, VMEM],
        out_specs=VMEM,
        scratch_shapes=[
            pltpu.VMEM((LANES, (strips * (own_blocks + 2) + 1) * LANES), jnp.bfloat16),
            pltpu.VMEM((2, strips * (own_blocks + 2) * LANES), jnp.float32),
        ],
        compiler_params=pltpu.CompilerParams(vmem_limit_bytes=LIMIT),
        cost_estimate=cost(6000, blocks * slots * LANES * LANES, 2),
        name="taper",
    )(ids, counts, own, near)


def doubling_sum(value, axis, other):
    count, groups = lax.axis_size(axis), lax.axis_size(other)
    if count & (count - 1):
        return lax.psum(value, axis)
    steps = [1 << i for i in range(count.bit_length() - 1)]
    half = len(steps) // 2
    for turn in range(len(steps)):
        pairs = []
        for j in range(groups):
            step = steps[(turn + half * (j % 2)) % len(steps)]
            pairs += [(i * groups + j, (i ^ step) * groups + j) for i in range(count)]
        value = value + lax.ppermute(value, (axis, other), pairs)
    return value


def shifted(value, axis, step):
    count = lax.axis_size(axis)
    if step % count == 0:
        return value
    return lax.ppermute(value, axis, [((i + step) % count, i) for i in range(count)])


def paired(value, axis, first):
    count = lax.axis_size(axis)
    pairs = [(i, i + 1) for i in range(first, count - 1, 2)]
    return lax.ppermute(value, axis, pairs + [(b, a) for a, b in pairs])


def shards(probes, locations, knot_locs, knot_precision, neighbours, counts):
    own_blocks = neighbours.shape[0]
    row_count = probes.shape[1]
    knot_total = knot_precision.shape[1]
    device_count = lax.axis_size(("space", "knot"))
    groups = lax.axis_size("knot")
    knot_range = KNOT_REACH * math.sqrt(own_blocks * device_count / knot_total)
    proj_scale = PROJ_GAIN * math.sqrt(knot_total / (row_count * device_count))

    stack, knots = prepare(probes, locations, knot_locs, own_blocks)
    chunks = [shifted(stack, "knot", step) for step in range(groups)]
    rate = LOG2E / knot_range
    extent = CELL * max(lax.axis_size("space"), groups * own_blocks)
    parts = [project(chunk, knots, rate, extent) for chunk in chunks]
    stack = parts[0][3]

    strip = make_strip(chunks[-1], stack, chunks[1 % groups])
    near = jnp.stack([strip, paired(strip, "space", 0), paired(strip, "space", 1)])
    pieces = math.gcd(own_blocks, 4)
    per_piece = own_blocks // pieces
    base = [taper(neighbours, counts, stack, near, i * per_piece, per_piece) for i in range(pieces)]

    projection = doubling_sum(sum(part[0] for part in parts), "space", "knot")
    factor = factored(None, projection, knot_precision, proj_scale, 0, base[:-1])
    for step in range(1, groups):
        factor = factored(factor, shifted(projection, "knot", step), knot_precision, proj_scale, step)
    total = jnp.concatenate(base, axis=1)
    for step in reversed(range(groups)):
        share = spread(factor, parts[step][1], parts[step][2], LOW_SCALE * EXPAND_GAIN)
        total = total + shifted(share, "knot", -step)
    return total


def solution(mesh):
    return jax.shard_map(
        shards,
        mesh=mesh,
        in_specs=(
            P(None, ("space", "knot")),
            P(None, ("space", "knot")),
            P(None, "knot"),
            P("knot", None),
            P(("space", "knot"), None),
            P(("space", "knot")),
        ),
        out_specs=P(None, ("space", "knot")),
        check_vma=False,
    )
```

time: 46.3 us -> 40.7 us (0.88)
  waiting for transfers between devices: 9.6 us -> 5.92 us
  local copies, waits for them, and re-layouts: 1.43 us -> 0.03 us
    ppermute x2, waiting for transfers between devices: 5.15 us -> 0.01 us  [paired(): return lax.ppermute(value, axis, pairs + [(b, a) for a, b in pairs])]
    ppermute x4, waiting for transfers between devices: 4.44 us -> 5.9 us  [doubling_sum(): value = value + lax.ppermute(value, (axis, other), pairs)]
    unnamed x19 -> x8, local copies, waits for them, and re-layouts: 1.42 us -> 0.03 us
    pallas_call x7 -> x8, Pallas kernels: 14.8 us -> 14.6 us  [the longest x4 7.24 us: taper(): pl.pallas_call(functools.partial(taper_kernel, first), out_shape=jax.Shap...]
    ppermute x4 -> x3, starting transfers between devices: 1.19 us -> 1.12 us  [shifted(): lax.ppermute(value, axis, [((i + step) % count, i) for i in range(count)])]
  transfers between devices with their start and end apart: 10 -> 9, of which waited for: 5 -> 3; matrix products, arithmetic and copies ran while one was open for 0% -> 0% of each run, Pallas kernels for 37% -> 41%
where the time goes in v6:
time: 40.7 us; the launch traced here: 40.5 us
  Pallas kernels  20.6 us (51%)
  starting transfers between devices  13.1 us (32%)
  waiting for transfers between devices  5.92 us (15%)
  other arithmetic  0.76 us (2%)
    pallas_call x4, Pallas kernels, taper(): pl.pallas_call(functools.partial(taper_kernel, first), out_shape=jax.Shap...  7.24 us
    pallas_call x2, Pallas kernels, project(): pl.pallas_call(functools.partial(project_kernel, scale, grain), out_shape...  6.48 us
    ppermute x2, starting transfers between devices, paired(): return lax.ppermute(value, axis, pairs + [(b, a) for a, b in pairs])  5.97 us
    ppermute x4, starting transfers between devices, doubling_sum(): value = value + lax.ppermute(value, (axis, other), pairs)  5.96 us
    ppermute x4, waiting for transfers between devices, doubling_sum(): value = value + lax.ppermute(value, (axis, other), pairs)  5.9 us
    pallas_call x2, Pallas kernels, factored(): pl.pallas_call(kernel, out_shape=jax.ShapeDtypeStruct((probes, rows), jnp...  3.38 us
    pallas_call x2, Pallas kernels, spread(): pl.pallas_call(functools.partial(spread_kernel, scale), out_shape=jax.Sha...  2.56 us
    ppermute x3, starting transfers between devices, shifted(): lax.ppermute(value, axis, [((i + step) % count, i) for i in range(count)])  1.12 us
  transfers between devices with their start and end apart: 9, of which 3 were waited for; matrix products, arithmetic and copies ran while one was open for 0% of the time, Pallas kernels for 41%

profile of v6, /device:TPU:0, one launch (start us, length us, event | category | flops | bytes accessed | tf_op | source)
XLA Modules:
  0.0 40.5 jit_solution(7941291044032944115)
XLA Ops:
  0.0 0.9 %prepare.1 = (f32[16,1280]{1,0:T(8,128)S(1)}, f32[2,1024]{1,0:T(2,128)S(1)}) custom-call(f32[16,1024]{1,0:T(8,128)} %probes_ref.1, f32[2,1024]{1,0:T(2,128)} %locations_ref.1, f32[2,1024]{1,0:T(2,128)} %knots_ref.1), custom_call_target="tpu_custom_call" | custom-call | tf_op jit(solution)/shard_map/prepare/pallas_call | solution.py:106
  0.9 0.5 %collective-permute-start = (f32[16,1280]{1,0:T(8,128)S(1)}, f32[16,1280]{1,0:T(8,128)S(1)}, u32[]{:S(2)}, u32[]{:S(2)}) collective-permute-start(f32[16,1280]{1,0:T(8,128)S(1)} %get-tuple-element.14.stack_ref), channel_id=1, source_target_pairs={{1,0},{0,1},{3,2},{2,3},{5,4},{4,5},{7,6},{6,7},{9,8},{8,9},{11,10... | collective-permute-start | bytes 245768 | tf_op jit(solution)/shard_map/ppermute | solution.py:374
  1.4 3.2 %project.2 = (f32[16,1024]{1,0:T(8,128)S(1)}, bf16[1024,1024]{1,0:T(8,128)(2,1)S(1)}, bf16[1024,1024]{1,0:T(8,128)(2,1)S(1)}, f32[16,1280]{1,0:T(8,128)S(1)}) custom-call(f32[16,1280]{1,0:T(8,128)S(1)} %get-tuple-element.14.stack_ref, f32[2,1024]{1,0:T(2,128)S(1)} %get-tuple-element.15.knots_ref), custom_call_target="tpu_custom_call" | custom-call | flops 2936012800 | bytes 4194304 | tf_op jit(solution)/shard_map/project/pallas_call | solution.py:183
  4.6 0.0 collective-permute-done.below_ref.above_ref.stack_ref
  4.7 0.0 copy-start
  4.7 0.0 copy-start.1
  4.7 0.7 %collective-permute-start.2 = (f32[16,1536]{1,0:T(8,128)S(1)}, f32[16,1536]{1,0:T(8,128)S(1)}, u32[]{:S(2)}, u32[]{:S(2)}) collective-permute-start(f32[16,1536]{1,0:T(8,128)S(1)} %strip.1), channel_id=1, source_target_pairs={{2,4},{6,8},{10,12},{14,16},{18,20},{22,24},{26,28},{4,2},{8,6},{1... | collective-permute-start | bytes 294920 | tf_op jit(solution)/shard_map/ppermute | solution.py:380
  5.4 5.3 %collective-permute-start.1 = (f32[16,1536]{1,0:T(8,128)S(1)}, f32[16,1536]{1,0:T(8,128)S(1)}, u32[]{:S(2)}, u32[]{:S(2)}) collective-permute-start(f32[16,1536]{1,0:T(8,128)S(1)} %strip.1), channel_id=1, source_target_pairs={{0,2},{4,6},{8,10},{12,14},{16,18},{20,22},{24,26},{28,30},{2,0},{... | collective-permute-start | bytes 294920 | tf_op jit(solution)/shard_map/ppermute | solution.py:380
  10.7 3.2 %project.3 = (f32[16,1024]{1,0:T(8,128)S(1)}, bf16[1024,1024]{1,0:T(8,128)(2,1)S(1)}, bf16[1024,1024]{1,0:T(8,128)(2,1)S(1)}, f32[16,1280]{1,0:T(8,128)}) custom-call(f32[16,1280]{1,0:T(8,128)S(1)} %collective-permute-done.below_ref.above_ref.stack_ref, f32[2,1024]{1,0:T(2,128)S(1)} %get-tuple-element.15.knots_ref), custom_call_target="tpu_custom_call" | custom-call | flops 2936012800 | bytes 4194304 | tf_op jit(solution)/shard_map/project/pallas_call | solution.py:183
  14.0 0.1 collective-permute-start.3
  14.0 4.2 %collective-permute-done.3 = f32[16,1024]{1,0:T(8,128)S(1)} collective-permute-done((f32[16,1024]{1,0:T(8,128)S(1)}, f32[16,1024]{1,0:T(8,128)S(1)}, u32[]{:S(2)}, u32[]{:S(2)}) %collective-permute-start.3) | collective-permute-done | bytes 65568 | tf_op jit(solution)/shard_map/ppermute | solution.py:366
  18.3 1.6 %collective-permute-start.4 = (f32[16,1024]{1,0:T(8,128)S(1)}, f32[16,1024]{1,0:T(8,128)S(1)}, u32[]{:S(2)}, u32[]{:S(2)}) collective-permute-start(f32[16,1024]{1,0:T(8,128)S(1)} %add.22), channel_id=1, source_target_pairs={{0,4},{2,6},{4,0},{6,2},{8,12},{10,14},{12,8},{14,10},{16,20},{18,... | collective-permute-start | bytes 196616 | tf_op jit(solution)/shard_map/ppermute | solution.py:366
  19.9 0.0 collective-permute-done.2
  19.9 0.0 collective-permute-done.1
  19.9 0.0 copy-done
  19.9 0.0 copy-done.1
  19.9 1.8 %taper.6.rest_2_ = f32[16,256]{1,0:T(8,128)S(1)} custom-call(s32[8,8]{1,0:T(8,128)S(1)} %copy-done, s32[8]{0:T(128)S(1)} %copy-done.1, f32[16,1280]{1,0:T(8,128)S(1)} %get-tuple-element.16.own_ref, f32[3,16,1536]{2,1,0:T(8,128)S(1)} %pad_maximum_fusion.near_ref), custom_call_target="tpu_custom_call" | custom-call | flops 1572864000 | bytes 1048576 | tf_op jit(solution)/shard_map/taper/pallas_call | solution.py:340
  21.8 0.0 slice-start
  21.8 1.8 %taper.5.rest_1_ = f32[16,256]{1,0:T(8,128)S(1)} custom-call(s32[8,8]{1,0:T(8,128)S(1)} %copy-done, s32[8]{0:T(128)S(1)} %copy-done.1, f32[16,1280]{1,0:T(8,128)S(1)} %get-tuple-element.16.own_ref, f32[3,16,1536]{2,1,0:T(8,128)S(1)} %pad_maximum_fusion.near_ref), custom_call_target="tpu_custom_call" | custom-call | flops 1572864000 | bytes 1048576 | tf_op jit(solution)/shard_map/taper/pallas_call | solution.py:340
  23.6 0.0 collective-permute-done.4
  23.6 0.0 slice-start.1
  23.7 1.6 %collective-permute-start.5 = (f32[16,1024]{1,0:T(8,128)S(1)}, f32[16,1024]{1,0:T(8,128)S(1)}, u32[]{:S(2)}, u32[]{:S(2)}) collective-permute-start(f32[16,1024]{1,0:T(8,128)S(1)} %add.23), channel_id=1, source_target_pairs={{0,8},{2,10},{4,12},{6,14},{8,0},{10,2},{12,4},{14,6},{16,24},{18,... | collective-permute-start | bytes 196616 | tf_op jit(solution)/shard_map/ppermute | solution.py:366
  25.3 1.8 %taper.4.rest_0_ = f32[16,256]{1,0:T(8,128)S(1)} custom-call(s32[8,8]{1,0:T(8,128)S(1)} %copy-done, s32[8]{0:T(128)S(1)} %copy-done.1, f32[16,1280]{1,0:T(8,128)S(1)} %get-tuple-element.16.own_ref, f32[3,16,1536]{2,1,0:T(8,128)S(1)} %pad_maximum_fusion.near_ref), custom_call_target="tpu_custom_call" | custom-call | flops 1572864000 | bytes 1048576 | tf_op jit(solution)/shard_map/taper/pallas_call | solution.py:340
  27.1 0.9 %collective-permute-done.5 = f32[16,1024]{1,0:T(8,128)S(1)} collective-permute-done((f32[16,1024]{1,0:T(8,128)S(1)}, f32[16,1024]{1,0:T(8,128)S(1)}, u32[]{:S(2)}, u32[]{:S(2)}) %collective-permute-start.5) | collective-permute-done | bytes 65568 | tf_op jit(solution)/shard_map/ppermute | solution.py:366
  28.0 2.7 %collective-permute-start.6 = (f32[16,1024]{1,0:T(8,128)S(1)}, f32[16,1024]{1,0:T(8,128)S(1)}, u32[]{:S(2)}, u32[]{:S(2)}) collective-permute-start(f32[16,1024]{1,0:T(8,128)S(1)} %add.24), channel_id=1, source_target_pairs={{0,16},{2,18},{4,20},{6,22},{8,24},{10,26},{12,28},{14,30},{16,0},... | collective-permute-start | bytes 196616 | tf_op jit(solution)/shard_map/ppermute | solution.py:366
  30.7 1.8 %taper.7 = f32[16,256]{1,0:T(8,128)S(1)} custom-call(s32[8,8]{1,0:T(8,128)S(1)} %copy-done, s32[8]{0:T(128)S(1)} %copy-done.1, f32[16,1280]{1,0:T(8,128)S(1)} %get-tuple-element.16.own_ref, f32[3,16,1536]{2,1,0:T(8,128)S(1)} %pad_maximum_fusion.near_ref), custom_call_target="tpu_custom_call" | custom-call | flops 1572864000 | bytes 1048576 | tf_op jit(solution)/shard_map/taper/pallas_call | solution.py:340
  32.5 0.7 %collective-permute-done.6 = f32[16,1024]{1,0:T(8,128)S(1)} collective-permute-done((f32[16,1024]{1,0:T(8,128)S(1)}, f32[16,1024]{1,0:T(8,128)S(1)}, u32[]{:S(2)}, u32[]{:S(2)}) %collective-permute-start.6) | collective-permute-done | bytes 65568 | tf_op jit(solution)/shard_map/ppermute | solution.py:366
  33.2 0.1 collective-permute-start.7
  33.3 0.0 slice-done
  33.3 0.0 slice-done.1
  33.4 1.7 %factor.2.before_ref = f32[16,1024]{1,0:T(8,128)S(1)} custom-call(f32[16,1024]{1,0:T(8,128)S(1)} %add.25.proj_ref, f32[1024,2048]{1,0:T(8,128)S(1)} %bitcast.4, f32[16,256]{1,0:T(8,128)S(1)} %taper.4.rest_0_, f32[16,256]{1,0:T(8,128)S(1)} %taper.5.rest_1_, f32[16,256]{1,0:T(8,128)S(1)} %taper.6.rest_2_), custom_call_target="tpu_custom_call" | custom-call | flops 1258291200 | bytes 4194304 | tf_op jit(solution)/shard_map/factor/pallas_call | solution.py:237
  35.0 0.0 collective-permute-done.7.proj_ref
  35.0 1.7 %factor.3.factor_ref = f32[16,1024]{1,0:T(8,128)S(1)} custom-call(f32[16,1024]{1,0:T(8,128)S(1)} %factor.2.before_ref, f32[16,1024]{1,0:T(8,128)S(1)} %collective-permute-done.7.proj_ref, f32[1024,2048]{1,0:T(8,128)S(1)} %bitcast.4), custom_call_target="tpu_custom_call" | custom-call | flops 1258291200 | bytes 4194304 | tf_op jit(solution)/shard_map/factor/pallas_call | solution.py:237
  36.7 1.3 %spread.2 = f32[16,1024]{1,0:T(8,128)S(1)} custom-call(f32[16,1024]{1,0:T(8,128)S(1)} %factor.3.factor_ref, bf16[1024,1024]{1,0:T(8,128)(2,1)S(1)} %get-tuple-element.19.high_ref, bf16[1024,1024]{1,0:T(8,128)(2,1)S(1)} %get-tuple-element.20.low_ref), custom_call_target="tpu_custom_call" | custom-call | flops 891289600 | bytes 4194304 | tf_op jit(solution)/shard_map/spread/pallas_call | solution.py:264
  38.0 0.5 %collective-permute-start.8 = (f32[16,1024]{1,0:T(8,128)S(1)}, f32[16,1024]{1,0:T(8,128)S(1)}, u32[]{:S(2)}, u32[]{:S(2)}) collective-permute-start(f32[16,1024]{1,0:T(8,128)S(1)} %spread.2), channel_id=1, source_target_pairs={{1,0},{0,1},{3,2},{2,3},{5,4},{4,5},{7,6},{6,7},{9,8},{8,9},{11,10... | collective-permute-start | bytes 196616 | tf_op jit(solution)/shard_map/ppermute | solution.py:374
  38.6 1.3 %spread.3 = f32[16,1024]{1,0:T(8,128)S(1)} custom-call(f32[16,1024]{1,0:T(8,128)S(1)} %factor.3.factor_ref, bf16[1024,1024]{1,0:T(8,128)(2,1)S(1)} %get-tuple-element.21.high_ref, bf16[1024,1024]{1,0:T(8,128)(2,1)S(1)} %get-tuple-element.22.low_ref), custom_call_target="tpu_custom_call" | custom-call | flops 891289600 | bytes 4194304 | tf_op jit(solution)/shard_map/spread/pallas_call | solution.py:264
  39.8 0.0 collective-permute-done.8
  39.8 0.7 %fusion = f32[16,1024]{1,0:T(8,128)} fusion(f32[16,1024]{1,0:T(8,128)S(1)} %spread.3, f32[16,1024]{1,0:T(8,128)S(1)} %collective-permute-done.8, f32[16,256]{1,0:T(8,128)S(1)} %taper.7, f32[16,256]{1,0:T(8,128)S(1)} %taper.6.rest_2_, f32[16,256]{1,0:T(8,128)S(1)} %taper.5.rest_1_, f32[16,256]{1,0:T(8,128)S(1)} %taper.4.rest_0_), kind=kLoop, calls=%fused_computation.2 | loop fusion | flops 81920 | bytes 262144 | tf_op jit(solution)/shard_map/add | solution.py:412
  (8 shorter events, 0.1 us)
Async XLA Ops:
  0.9 3.8 %collective-permute-start = (f32[16,1280]{1,0:T(8,128)S(1)}, f32[16,1280]{1,0:T(8,128)S(1)}, u32[]{:S(2)}, u32[]{:S(2)}) collective-permute-start(f32[16,1280]{1,0:T(8,128)S(1)} %get-tuple-element.14.stack_ref), channel_id=1, source_target_pairs={{1,0},{0,1},{3,2},{2,3},{5,4},{4,5},{7,6},{6,7},{9,8},{8,9},{11,10... | collective-permute-start | bytes 245768 | tf_op jit(solution)/shard_map/ppermute | solution.py:374
  4.7 15.2 %copy-start = (s32[8,8]{1,0:T(8,128)S(1)}, s32[8,8]{1,0:T(8,128)}, u32[]{:S(2)}) copy-start(s32[8,8]{1,0:T(8,128)} %ids_ref.7) | copy-start | bytes 772
  4.7 15.2 %copy-start.1 = (s32[8]{0:T(128)S(1)}, s32[8]{0:T(128)}, u32[]{:S(2)}) copy-start(s32[8]{0:T(128)} %counts_ref.7) | copy-start | bytes 100
  4.7 15.2 %collective-permute-start.2 = (f32[16,1536]{1,0:T(8,128)S(1)}, f32[16,1536]{1,0:T(8,128)S(1)}, u32[]{:S(2)}, u32[]{:S(2)}) collective-permute-start(f32[16,1536]{1,0:T(8,128)S(1)} %strip.1), channel_id=1, source_target_pairs={{2,4},{6,8},{10,12},{14,16},{18,20},{22,24},{26,28},{4,2},{8,6},{1... | collective-permute-start | bytes 294920 | tf_op jit(solution)/shard_map/ppermute | solution.py:380
  5.4 14.5 %collective-permute-start.1 = (f32[16,1536]{1,0:T(8,128)S(1)}, f32[16,1536]{1,0:T(8,128)S(1)}, u32[]{:S(2)}, u32[]{:S(2)}) collective-permute-start(f32[16,1536]{1,0:T(8,128)S(1)} %strip.1), channel_id=1, source_target_pairs={{0,2},{4,6},{8,10},{12,14},{16,18},{20,22},{24,26},{28,30},{2,0},{... | collective-permute-start | bytes 294920 | tf_op jit(solution)/shard_map/ppermute | solution.py:380
  14.0 4.3 %collective-permute-start.3 = (f32[16,1024]{1,0:T(8,128)S(1)}, f32[16,1024]{1,0:T(8,128)S(1)}, u32[]{:S(2)}, u32[]{:S(2)}) collective-permute-start(f32[16,1024]{1,0:T(8,128)S(1)} %add.21), channel_id=1, source_target_pairs={{0,2},{2,0},{4,6},{6,4},{8,10},{10,8},{12,14},{14,12},{16,18},{18,... | collective-permute-start | bytes 196616 | tf_op jit(solution)/shard_map/ppermute | solution.py:366
  18.3 5.3 %collective-permute-start.4 = (f32[16,1024]{1,0:T(8,128)S(1)}, f32[16,1024]{1,0:T(8,128)S(1)}, u32[]{:S(2)}, u32[]{:S(2)}) collective-permute-start(f32[16,1024]{1,0:T(8,128)S(1)} %add.22), channel_id=1, source_target_pairs={{0,4},{2,6},{4,0},{6,2},{8,12},{10,14},{12,8},{14,10},{16,20},{18,... | collective-permute-start | bytes 196616 | tf_op jit(solution)/shard_map/ppermute | solution.py:366
  21.8 11.6 %slice-start = ((s8[8388608]{0:T(1024)(128)(4,1)}), s8[4194304]{0:T(1024)(128)(4,1)S(1)}, s32[]{:S(2)}) async-start(s8[8388608]{0:T(1024)(128)(4,1)} %bitcast.3), calls=%async_computation | async-start | bytes 8388608
  23.6 9.7 %slice-start.1 = ((s8[8388608]{0:T(1024)(128)(4,1)}), s8[4194304]{0:T(1024)(128)(4,1)S(1)}, s32[]{:S(2)}) async-start(s8[8388608]{0:T(1024)(128)(4,1)} %bitcast.3), calls=%async_computation.1 | async-start | bytes 8388608
  23.7 4.3 %collective-permute-start.5 = (f32[16,1024]{1,0:T(8,128)S(1)}, f32[16,1024]{1,0:T(8,128)S(1)}, u32[]{:S(2)}, u32[]{:S(2)}) collective-permute-start(f32[16,1024]{1,0:T(8,128)S(1)} %add.23), channel_id=1, source_target_pairs={{0,8},{2,10},{4,12},{6,14},{8,0},{10,2},{12,4},{14,6},{16,24},{18,... | collective-permute-start | bytes 196616 | tf_op jit(solution)/shard_map/ppermute | solution.py:366
  28.0 5.2 %collective-permute-start.6 = (f32[16,1024]{1,0:T(8,128)S(1)}, f32[16,1024]{1,0:T(8,128)S(1)}, u32[]{:S(2)}, u32[]{:S(2)}) collective-permute-start(f32[16,1024]{1,0:T(8,128)S(1)} %add.24), channel_id=1, source_target_pairs={{0,16},{2,18},{4,20},{6,22},{8,24},{10,26},{12,28},{14,30},{16,0},... | collective-permute-start | bytes 196616 | tf_op jit(solution)/shard_map/ppermute | solution.py:366
  33.2 1.8 %collective-permute-start.7 = (f32[16,1024]{1,0:T(8,128)S(1)}, f32[16,1024]{1,0:T(8,128)S(1)}, u32[]{:S(2)}, u32[]{:S(2)}) collective-permute-start(f32[16,1024]{1,0:T(8,128)S(1)} %add.25.proj_ref), channel_id=1, source_target_pairs={{1,0},{0,1},{3,2},{2,3},{5,4},{4,5},{7,6},{6,7},{9,8},{8,9},{11,10... | collective-permute-start | bytes 196616 | tf_op jit(solution)/shard_map/ppermute | solution.py:374
  38.0 1.8 %collective-permute-start.8 = (f32[16,1024]{1,0:T(8,128)S(1)}, f32[16,1024]{1,0:T(8,128)S(1)}, u32[]{:S(2)}, u32[]{:S(2)}) collective-permute-start(f32[16,1024]{1,0:T(8,128)S(1)} %spread.2), channel_id=1, source_target_pairs={{1,0},{0,1},{3,2},{2,3},{5,4},{4,5},{7,6},{6,7},{9,8},{8,9},{11,10... | collective-permute-start | bytes 196616 | tf_op jit(solution)/shard_map/ppermute | solution.py:374

commit v7 on v6

--- a/solution.py
+++ b/solution.py
@@ -117,45 +117,101 @@
     )(probes, locations, knot_locs)
 
 
-def strip_kernel(below_ref, own_ref, above_ref, out_ref):
-    rows, width = own_ref.shape
+def corner_kernel(end, east_ref, west_ref, out_ref):
+    rows, width = east_ref.shape
     points = width - 2 * LANES
     blocks = points // LANES
-    out_ref[:, :LANES] = below_ref[:, points - LANES : points]
-    out_ref[:, LANES : points + LANES] = own_ref[:, :points]
-    out_ref[:, points + LANES : points + 2 * LANES] = above_ref[:, :LANES]
-    for axis in range(2):
-        lanes = slice(points + axis * LANES, points + (axis + 1) * LANES)
-        target = slice(lanes.start + 2 * LANES, lanes.stop + 2 * LANES)
-        out_ref[:, target] = jnp.zeros((rows, LANES), jnp.float32)
-        out_ref[0:1, target] = below_ref[blocks - 1 : blocks, lanes]
-        out_ref[1 : blocks + 1, target] = own_ref[:blocks, lanes]
-        out_ref[blocks + 1 : blocks + 2, target] = above_ref[0:1, lanes]
-
-
-def make_strip(below, own, above):
-    return pl.pallas_call(
-        strip_kernel,
-        out_shape=jax.ShapeDtypeStruct((own.shape[0], own.shape[1] + 2 * LANES), jnp.float32),
-        in_specs=[VMEM, VMEM, VMEM],
+
+    out_ref[...] = jnp.zeros(out_ref.shape, jnp.float32)
+    upper = lax.axis_index("knot") > 0
+    for turn, ref in enumerate((east_ref, west_ref)):
+        start = 2 * turn * LANES
+        first = [ref[:, :LANES], *[ref[0:1, points + axis * LANES : points + (axis + 1) * LANES] for axis in range(2)]]
+        last = [
+            ref[:, points - LANES : points],
+            *[ref[blocks - 1 : blocks, points + axis * LANES : points + (axis + 1) * LANES] for axis in range(2)],
+        ]
+        taken = {"first": first, "last": last, "inner": [jnp.where(upper, a, b) for a, b in zip(first, last)]}[end]
+        out_ref[:, start : start + LANES] = taken[0]
+        out_ref[0:1, start + LANES : start + 2 * LANES] = taken[1]
+        out_ref[1:2, start + LANES : start + 2 * LANES] = taken[2]
+
+
+def corner_blocks(end, strips):
+    return pl.pallas_call(
+        functools.partial(corner_kernel, end),
+        out_shape=jax.ShapeDtypeStruct((strips[0].shape[0], 4 * LANES), jnp.float32),
+        in_specs=[VMEM, VMEM],
         out_specs=VMEM,
         compiler_params=pltpu.CompilerParams(vmem_limit_bytes=LIMIT),
-        name="strip",
-    )(below, own, above)
-
-
-def project_kernel(scale, grain, stack_ref, knots_ref, out_ref, high_ref, low_ref, copy_ref, columns, weights):
+        name="corner",
+    )(*strips)
+
+
+def assemble_kernel(own_ref, below_ref, above_ref, east_ref, west_ref, low_ref, high_ref, values_ref, coords_ref):
+    probes, width = own_ref.shape
+    points = width - 2 * LANES
+    blocks = points // LANES
+    span = blocks + 2
+    inverse = 1.0 / TAPER_LEN
+
+    def put(place, vals, coords):
+        count = vals.shape[1] // LANES
+        values_ref[:, place * LANES : (place + count) * LANES] = stacked_halves(vals)
+        for index in range(count):
+            for axis in range(2):
+                lanes = slice((place + index) * LANES, (place + index + 1) * LANES)
+                coords_ref[axis : axis + 1, lanes] = coords[axis][index : index + 1] * inverse
+
+    def put_stack(place, ref, first, count):
+        lanes = [slice(points + axis * LANES, points + (axis + 1) * LANES) for axis in range(2)]
+        put(
+            place,
+            ref[:, first * LANES : (first + count) * LANES],
+            [ref[first : first + count, lanes[axis]] for axis in range(2)],
+        )
+
+    def put_corner(place, ref, turn):
+        start = 2 * turn * LANES
+        both = slice(start + LANES, start + 2 * LANES)
+        put(place, ref[:, start : start + LANES], [ref[axis : axis + 1, both] for axis in range(2)])
+
+    put_stack(0, below_ref, blocks - 1, 1)
+    put_stack(1, own_ref, 0, blocks)
+    put_stack(1 + blocks, above_ref, 0, 1)
+    for turn, ref in enumerate((east_ref, west_ref)):
+        place = (turn + 1) * span
+        put_corner(place, low_ref, turn)
+        put_stack(place + 1, ref, 0, blocks)
+        put_corner(place + 1 + blocks, high_ref, turn)
+    values_ref[:, 3 * points + 6 * LANES :] = jnp.zeros((2 * probes, LANES), jnp.bfloat16)
+
+
+def assemble(own, below, above, strips, low, high):
+    probes, width = own.shape
+    near = 3 * (width - 2 * LANES + 2 * LANES)
+    return pl.pallas_call(
+        assemble_kernel,
+        out_shape=(
+            jax.ShapeDtypeStruct((2 * probes, near + LANES), jnp.bfloat16),
+            jax.ShapeDtypeStruct((2, near), jnp.float32),
+        ),
+        in_specs=[VMEM] * 7,
+        out_specs=(VMEM, VMEM),
+        compiler_params=pltpu.CompilerParams(vmem_limit_bytes=LIMIT),
+        name="assemble",
+    )(own, below, above, *strips, low, high)
+
+
+def project_kernel(scale, grain, stack_ref, knots_ref, out_ref, high_ref, low_ref, weights):
     points, knots = high_ref.shape
     probes = stack_ref.shape[0]
     tile = min(TILE, knots)
     wide = min(TILE, points)
-    copy_ref[...] = stack_ref[...]
-    for axis in range(2):
-        turned = jnp.transpose(coordinate_rows(stack_ref, points, axis) * scale)
-        turned = (turned + grain) - grain
-        for index in range(points // LANES):
-            columns[index * LANES : (index + 1) * LANES, axis : axis + 1] = turned[:, index : index + 1]
     weights[...] = stacked_halves(stack_ref[:, :points])
+    east, north = [
+        (jnp.transpose(coordinate_rows(stack_ref, points, axis) * scale) + grain) - grain for axis in range(2)
+    ]
 
     @pl.loop(0, knots // tile)
     def _(step):
@@ -165,15 +221,21 @@
         ]
         total = jnp.zeros((2 * probes, tile), jnp.float32)
         for start in range(0, points, wide):
-            rows = slice(start, start + wide)
-            dx = columns[rows, 0:1] - kx
-            dy = columns[rows, 1:2] - ky
-            square = dx * dx + dy * dy
-            high, low = halves(jnp.exp2(-(square * lax.rsqrt(square))))
-            high_ref[rows, lanes] = high
-            low_ref[rows, lanes] = low
-            part = weights[:, rows]
-            total = total + (dot_nn(part, high) + dot_nn(part, low))
+            highs, lows = [], []
+            for row in range(start, start + wide, LANES):
+                block = row // LANES
+                dx = east[:, block : block + 1] - kx
+                dy = north[:, block : block + 1] - ky
+                square = dx * dx + dy * dy
+                high, low = halves(jnp.exp2(-(square * lax.rsqrt(square))))
+                high_ref[row : row + LANES, lanes] = high
+                low_ref[row : row + LANES, lanes] = low
+                highs.append(high)
+                lows.append(low)
+            part = weights[:, start : start + wide]
+            total = total + (
+                dot_nn(part, jnp.concatenate(highs, axis=0)) + dot_nn(part, jnp.concatenate(lows, axis=0))
+            )
         out_ref[:, lanes] = folded(total)
 
 
@@ -186,14 +248,10 @@
             jax.ShapeDtypeStruct((probes, knots), jnp.float32),
             pltpu.VMEM((points, knots), jnp.bfloat16),
             pltpu.VMEM((points, knots), jnp.bfloat16),
-            jax.ShapeDtypeStruct(stack.shape, jnp.float32),
         ),
         in_specs=[VMEM, VMEM],
-        out_specs=(VMEM, VMEM, VMEM, VMEM),
-        scratch_shapes=[
-            pltpu.VMEM((points, 8), jnp.float32),
-            pltpu.VMEM((2 * probes, points), jnp.bfloat16),
-        ],
+        out_specs=(VMEM, VMEM, VMEM),
+        scratch_shapes=[pltpu.VMEM((2 * probes, points), jnp.bfloat16)],
         compiler_params=pltpu.CompilerParams(vmem_limit_bytes=LIMIT),
         cost_estimate=cost(2800, points * knots, 2),
         name="project",
@@ -279,27 +337,17 @@
     return jnp.exp2(scaled * (-LOG2E * TAPER_LEN / COV_RANGE)) * (remain * remain) * (1.0 + 4.0 * scaled)
 
 
-def taper_kernel(first, ids_ref, counts_ref, own_ref, near_ref, out_ref, values, coords):
+def taper_kernel(first, ids_ref, counts_ref, own_ref, values_ref, coords_ref, out_ref):
     own_blocks, slots = ids_ref.shape
     block = LANES
-    strips, probes, width = near_ref.shape
+    probes = own_ref.shape[0]
     span = own_blocks + 2
+    zeros_place = coords_ref.shape[1] // block
     column = lax.axis_index("space")
     north_base = lax.axis_index("knot") * own_blocks - 1
     north_cells = lax.axis_size("knot") * own_blocks
-    inverse = 1.0 / TAPER_LEN
-    values[:, strips * span * block :] = jnp.zeros((values.shape[0], block), jnp.bfloat16)
-    for strip in range(strips):
-        values[:, strip * span * block : (strip + 1) * span * block] = padded_halves(
-            near_ref[strip, :, : span * block], values.shape[0]
-        )
-        for axis in range(2):
-            rows = near_ref[strip, :, (span + axis) * block : (span + axis + 1) * block] * inverse
-            for index in range(span):
-                start = (strip * span + index) * block
-                coords[axis : axis + 1, start : start + block] = rows[index : index + 1]
     own_columns = [
-        jnp.transpose(coordinate_rows(own_ref, own_blocks * block, axis) * inverse) for axis in range(2)
+        jnp.transpose(coordinate_rows(own_ref, own_blocks * block, axis) * (1.0 / TAPER_LEN)) for axis in range(2)
     ]
 
     def place(group, slot):
@@ -307,7 +355,7 @@
         east = jnp.where(ahead >= north_cells, 1, 0) + jnp.where(ahead >= 2 * north_cells, 1, 0)
         strip = jnp.where(east == 1, 0, 1 + lax.rem(column + lax.div(east, 2) + 1, 2))
         index = strip * span + (ahead - east * north_cells - north_base)
-        return lanes_of(index), lanes_of(jnp.where(slot < counts_ref[group], index, strips * span))
+        return lanes_of(index), lanes_of(jnp.where(slot < counts_ref[group], index, zeros_place))
 
     def lanes_of(index):
         return pl.ds(pl.multiple_of(index * block, block), block)
@@ -315,15 +363,15 @@
     for index in range(out_ref.shape[1] // block):
         group = first + index
         px, py = [turned[:, group : group + 1] for turned in own_columns]
-        total = jnp.zeros((block, values.shape[0]), jnp.float32)
+        total = jnp.zeros((block, 2 * probes), jnp.float32)
         for pair in range(0, slots, 2):
             highs, lows, parts = [], [], []
             for slot in range(pair, min(pair + 2, slots)):
                 lanes, value_lanes = place(group, slot)
-                high, low = halves(covariance(distance(px, py, coords[0:1, lanes], coords[1:2, lanes])))
+                high, low = halves(covariance(distance(px, py, coords_ref[0:1, lanes], coords_ref[1:2, lanes])))
                 highs.append(high)
                 lows.append(low)
-                parts.append(values[:, value_lanes])
+                parts.append(values_ref[:, value_lanes])
             part = jnp.concatenate(parts, axis=1)
             total = total + (
                 dot_nt(jnp.concatenate(highs, axis=1), part) + dot_nt(jnp.concatenate(lows, axis=1), part)
@@ -334,36 +382,37 @@
         )
 
 
-def taper(ids, counts, own, near, first, blocks):
-    own_blocks, slots = ids.shape
-    strips, probes, width = near.shape
+def taper(ids, counts, own, values, coords, first, blocks):
+    slots = ids.shape[1]
     return pl.pallas_call(
         functools.partial(taper_kernel, first),
-        out_shape=jax.ShapeDtypeStruct((probes, blocks * LANES), jnp.float32),
-        in_specs=[SMEM, SMEM, VMEM, VMEM],
+        out_shape=jax.ShapeDtypeStruct((own.shape[0], blocks * LANES), jnp.float32),
+        in_specs=[SMEM, SMEM, VMEM, VMEM, VMEM],
         out_specs=VMEM,
-        scratch_shapes=[
-            pltpu.VMEM((LANES, (strips * (own_blocks + 2) + 1) * LANES), jnp.bfloat16),
-            pltpu.VMEM((2, strips * (own_blocks + 2) * LANES), jnp.float32),
-        ],
         compiler_params=pltpu.CompilerParams(vmem_limit_bytes=LIMIT),
         cost_estimate=cost(6000, blocks * slots * LANES * LANES, 2),
         name="taper",
-    )(ids, counts, own, near)
-
-
-def doubling_sum(value, axis, other):
+    )(ids, counts, own, values, coords)
+
+
+def butterfly_sum(value, axis, other):
     count, groups = lax.axis_size(axis), lax.axis_size(other)
     if count & (count - 1):
         return lax.psum(value, axis)
-    steps = [1 << i for i in range(count.bit_length() - 1)]
-    half = len(steps) // 2
-    for turn in range(len(steps)):
-        pairs = []
-        for j in range(groups):
-            step = steps[(turn + half * (j % 2)) % len(steps)]
-            pairs += [(i * groups + j, (i ^ step) * groups + j) for i in range(count)]
-        value = value + lax.ppermute(value, (axis, other), pairs)
+    bits = [1 << i for i in range(count.bit_length() - 1)]
+    rounds = [(low | high, high, low) for low, high in zip(bits[0::2], bits[1::2])]
+    half = len(rounds) // 2
+    for turn in range(len(rounds)):
+        got = []
+        for kind in range(3):
+            pairs = []
+            for j in range(groups):
+                step = rounds[(turn + half * (j % 2)) % len(rounds)][kind]
+                pairs += [(i * groups + j, (i ^ step) * groups + j) for i in range(count)]
+            got.append(lax.ppermute(value, (axis, other), pairs))
+        value = (value + got[2]) + (got[1] + got[0])
+    if len(bits) % 2:
+        value = value + lax.ppermute(value, axis, [(i, i ^ bits[-1]) for i in range(count)])
     return value
 
 
@@ -394,15 +443,20 @@
     rate = LOG2E / knot_range
     extent = CELL * max(lax.axis_size("space"), groups * own_blocks)
     parts = [project(chunk, knots, rate, extent) for chunk in chunks]
-    stack = parts[0][3]
-
-    strip = make_strip(chunks[-1], stack, chunks[1 % groups])
-    near = jnp.stack([strip, paired(strip, "space", 0), paired(strip, "space", 1)])
+    strips = [paired(stack, "space", 0), paired(stack, "space", 1)]
+    if groups == 2:
+        low = high = shifted(corner_blocks("inner", strips), "knot", 1)
+    else:
+        low = shifted(corner_blocks("last", strips), "knot", -1)
+        high = shifted(corner_blocks("first", strips), "knot", 1)
+    values, coords = assemble(stack, chunks[-1], chunks[1 % groups], strips, low, high)
     pieces = math.gcd(own_blocks, 4)
     per_piece = own_blocks // pieces
-    base = [taper(neighbours, counts, stack, near, i * per_piece, per_piece) for i in range(pieces)]
-
-    projection = doubling_sum(sum(part[0] for part in parts), "space", "knot")
+    base = [
+        taper(neighbours, counts, stack, values, coords, i * per_piece, per_piece) for i in range(pieces)
+    ]
+
+    projection = butterfly_sum(sum(part[0] for part in parts), "space", "knot")
     factor = factored(None, projection, knot_precision, proj_scale, 0, base[:-1])
     for step in range(1, groups):
         factor = factored(factor, shifted(projection, "knot", step), knot_precision, proj_scale, step)

time: 40.7 us -> 39.5 us (0.971)
  waiting for transfers between devices: 5.92 us -> 3.76 us
  starting transfers between devices: 13.1 us -> 15.2 us
  Pallas kernels: 20.6 us -> 19.5 us
    ppermute x4 -> x6, waiting for transfers between devices: 5.9 us -> 2.81 us  [butterfly_sum(): got.append(lax.ppermute(value, (axis, other), pairs))]
    ppermute x4 -> x6, starting transfers between devices: 5.96 us -> 8.11 us  [butterfly_sum(): got.append(lax.ppermute(value, (axis, other), pairs))]
    ppermute x2, waiting for transfers between devices: 0.01 us -> 0.94 us  [paired(): return lax.ppermute(value, axis, pairs + [(b, a) for a, b in pairs])]
    pallas_call x2, Pallas kernels: 6.48 us -> 5.77 us  [project(): pl.pallas_call(functools.partial(project_kernel, scale, grain), out_shape...]
    ppermute x3 -> x4, starting transfers between devices: 1.12 us -> 0.67 us  [shifted(): lax.ppermute(value, axis, [((i + step) % count, i) for i in range(count)])]
    ppermute x2, starting transfers between devices: 5.97 us -> 6.4 us  [paired(): return lax.ppermute(value, axis, pairs + [(b, a) for a, b in pairs])]
    pallas_call x4, Pallas kernels: 7.24 us -> 6.81 us  [taper(): pl.pallas_call(functools.partial(taper_kernel, first), out_shape=jax.Shap...]
  transfers between devices with their start and end apart: 9 -> 12, of which waited for: 3 -> 2; matrix products, arithmetic and copies ran while one was open for 0% -> 0% of each run, Pallas kernels for 41% -> 40%
where the time goes in v7:
time: 39.5 us; the launch traced here: 39.4 us
  Pallas kernels  19.5 us (49%)
  starting transfers between devices  15.2 us (38%)
  waiting for transfers between devices  3.76 us (10%)
  other arithmetic  0.73 us (2%)
    ppermute x6, starting transfers between devices, butterfly_sum(): got.append(lax.ppermute(value, (axis, other), pairs))  8.11 us
    pallas_call x4, Pallas kernels, taper(): pl.pallas_call(functools.partial(taper_kernel, first), out_shape=jax.Shap...  6.81 us
    ppermute x2, starting transfers between devices, paired(): return lax.ppermute(value, axis, pairs + [(b, a) for a, b in pairs])  6.4 us
    pallas_call x2, Pallas kernels, project(): pl.pallas_call(functools.partial(project_kernel, scale, grain), out_shape...  5.77 us
    pallas_call x2, Pallas kernels, factored(): pl.pallas_call(kernel, out_shape=jax.ShapeDtypeStruct((probes, rows), jnp...  3.38 us
    ppermute x6, waiting for transfers between devices, butterfly_sum(): got.append(lax.ppermute(value, (axis, other), pairs))  2.81 us
    pallas_call x2, Pallas kernels, spread(): pl.pallas_call(functools.partial(spread_kernel, scale), out_shape=jax.Sha...  2.56 us
    ppermute x2, waiting for transfers between devices, paired(): return lax.ppermute(value, axis, pairs + [(b, a) for a, b in pairs])  0.94 us
  transfers between devices with their start and end apart: 12, of which 2 were waited for; matrix products, arithmetic and copies ran while one was open for 0% of the time, Pallas kernels for 40%

profile of v7, /device:TPU:0, one launch (start us, length us, event | category | flops | bytes accessed | tf_op | source)
XLA Modules:
  0.0 39.4 jit_solution(364613616574922665)
XLA Ops:
  0.0 0.9 %prepare.1 = (f32[16,1280]{1,0:T(8,128)S(1)}, f32[2,1024]{1,0:T(2,128)S(1)}) custom-call(f32[16,1024]{1,0:T(8,128)} %probes_ref.1, f32[2,1024]{1,0:T(2,128)} %locations_ref.1, f32[2,1024]{1,0:T(2,128)} %knots_ref.1), custom_call_target="tpu_custom_call" | custom-call | tf_op jit(solution)/shard_map/prepare/pallas_call | solution.py:106
  0.9 0.7 %collective-permute-start.2 = (f32[16,1280]{1,0:T(8,128)S(1)}, f32[16,1280]{1,0:T(8,128)S(1)}, u32[]{:S(2)}, u32[]{:S(2)}) collective-permute-start(f32[16,1280]{1,0:T(8,128)S(1)} %get-tuple-element.15.own_ref.stack_ref), channel_id=1, source_target_pairs={{2,4},{6,8},{10,12},{14,16},{18,20},{22,24},{26,28},{4,2},{8,6},{1... | collective-permute-start | bytes 245768 | tf_op jit(solution)/shard_map/ppermute | solution.py:429
  1.6 5.7 %collective-permute-start.1 = (f32[16,1280]{1,0:T(8,128)S(1)}, f32[16,1280]{1,0:T(8,128)S(1)}, u32[]{:S(2)}, u32[]{:S(2)}) collective-permute-start(f32[16,1280]{1,0:T(8,128)S(1)} %get-tuple-element.15.own_ref.stack_ref), channel_id=1, source_target_pairs={{0,2},{4,6},{8,10},{12,14},{16,18},{20,22},{24,26},{28,30},{2,0},{... | collective-permute-start | bytes 245768 | tf_op jit(solution)/shard_map/ppermute | solution.py:429
  7.3 0.0 collective-permute-start
  7.3 2.9 %project.2 = (f32[16,1024]{1,0:T(8,128)S(1)}, bf16[1024,1024]{1,0:T(8,128)(2,1)S(1)}, bf16[1024,1024]{1,0:T(8,128)(2,1)S(1)}) custom-call(f32[16,1280]{1,0:T(8,128)S(1)} %get-tuple-element.15.own_ref.stack_ref, f32[2,1024]{1,0:T(2,128)S(1)} %get-tuple-element.18.knots_ref), custom_call_target="tpu_custom_call" | custom-call | flops 2936012800 | bytes 4194304 | tf_op jit(solution)/shard_map/project/pallas_call | solution.py:245
  10.2 0.0 collective-permute-done.2.west_ref
  10.2 0.9 %collective-permute-done.1.east_ref = f32[16,1280]{1,0:T(8,128)S(1)} collective-permute-done((f32[16,1280]{1,0:T(8,128)S(1)}, f32[16,1280]{1,0:T(8,128)S(1)}, u32[]{:S(2)}, u32[]{:S(2)}) %collective-permute-start.1) | collective-permute-done | bytes 81952 | tf_op jit(solution)/shard_map/ppermute | solution.py:429
  11.1 0.0 copy-start
  11.1 0.0 copy-start.1
  11.2 0.1 collective-permute-start.3
  11.2 0.0 collective-permute-done.below_ref.above_ref.stack_ref
  11.2 2.9 %project.3 = (f32[16,1024]{1,0:T(8,128)S(1)}, bf16[1024,1024]{1,0:T(8,128)(2,1)S(1)}, bf16[1024,1024]{1,0:T(8,128)(2,1)S(1)}) custom-call(f32[16,1280]{1,0:T(8,128)S(1)} %collective-permute-done.below_ref.above_ref.stack_ref, f32[2,1024]{1,0:T(2,128)S(1)} %get-tuple-element.18.knots_ref), custom_call_target="tpu_custom_call" | custom-call | flops 2936012800 | bytes 4194304 | tf_op jit(solution)/shard_map/project/pallas_call | solution.py:245
  14.2 1.9 %collective-permute-start.6 = (f32[16,1024]{1,0:T(8,128)S(1)}, f32[16,1024]{1,0:T(8,128)S(1)}, u32[]{:S(2)}, u32[]{:S(2)}) collective-permute-start(f32[16,1024]{1,0:T(8,128)S(1)} %add.27), channel_id=1, source_target_pairs={{0,6},{2,4},{4,2},{6,0},{8,14},{10,12},{12,10},{14,8},{16,22},{18,... | collective-permute-start | bytes 196616 | tf_op jit(solution)/shard_map/ppermute | solution.py:412
  16.1 1.4 %collective-permute-start.5 = (f32[16,1024]{1,0:T(8,128)S(1)}, f32[16,1024]{1,0:T(8,128)S(1)}, u32[]{:S(2)}, u32[]{:S(2)}) collective-permute-start(f32[16,1024]{1,0:T(8,128)S(1)} %add.27), channel_id=1, source_target_pairs={{0,4},{2,6},{4,0},{6,2},{8,12},{10,14},{12,8},{14,10},{16,20},{18,... | collective-permute-start | bytes 196616 | tf_op jit(solution)/shard_map/ppermute | solution.py:412
  17.5 0.2 collective-permute-start.4
  17.7 0.0 collective-permute-done.3.low_ref.high_ref
  17.8 0.0 copy-done
  17.8 0.0 copy-done.1
  17.8 1.7 %taper.6.rest_2_ = f32[16,256]{1,0:T(8,128)S(1)} custom-call(s32[8,8]{1,0:T(8,128)S(1)} %copy-done, s32[8]{0:T(128)S(1)} %copy-done.1, f32[16,1280]{1,0:T(8,128)S(1)} %get-tuple-element.15.own_ref.stack_ref, bf16[32,3968]{1,0:T(8,128)(2,1)S(1)} %get-tuple-element.16.values_ref, f32[2,3840]{1,0:T(2,128)S(1)} %get-tuple-element.17.coords_ref), custom_call_target="tpu_custom_call" | custom-call | flops 1572864000 | bytes 1048576 | tf_op jit(solution)/shard_map/taper/pallas_call | solution.py:387
  19.5 0.0 slice-start
  19.5 1.7 %taper.5.rest_1_ = f32[16,256]{1,0:T(8,128)S(1)} custom-call(s32[8,8]{1,0:T(8,128)S(1)} %copy-done, s32[8]{0:T(128)S(1)} %copy-done.1, f32[16,1280]{1,0:T(8,128)S(1)} %get-tuple-element.15.own_ref.stack_ref, bf16[32,3968]{1,0:T(8,128)(2,1)S(1)} %get-tuple-element.16.values_ref, f32[2,3840]{1,0:T(2,128)S(1)} %get-tuple-element.17.coords_ref), custom_call_target="tpu_custom_call" | custom-call | flops 1572864000 | bytes 1048576 | tf_op jit(solution)/shard_map/taper/pallas_call | solution.py:387
  21.2 0.0 slice-start.1
  21.2 1.7 %taper.4.rest_0_ = f32[16,256]{1,0:T(8,128)S(1)} custom-call(s32[8,8]{1,0:T(8,128)S(1)} %copy-done, s32[8]{0:T(128)S(1)} %copy-done.1, f32[16,1280]{1,0:T(8,128)S(1)} %get-tuple-element.15.own_ref.stack_ref, bf16[32,3968]{1,0:T(8,128)(2,1)S(1)} %get-tuple-element.16.values_ref, f32[2,3840]{1,0:T(2,128)S(1)} %get-tuple-element.17.coords_ref), custom_call_target="tpu_custom_call" | custom-call | flops 1572864000 | bytes 1048576 | tf_op jit(solution)/shard_map/taper/pallas_call | solution.py:387
  23.0 0.0 collective-permute-done.6
  23.0 0.0 collective-permute-done.5
  23.0 0.0 collective-permute-done.4
  23.0 3.9 %collective-permute-start.9 = (f32[16,1024]{1,0:T(8,128)S(1)}, f32[16,1024]{1,0:T(8,128)S(1)}, u32[]{:S(2)}, u32[]{:S(2)}) collective-permute-start(f32[16,1024]{1,0:T(8,128)S(1)} %add_add_fusion.1), channel_id=1, source_target_pairs={{0,24},{2,26},{4,28},{6,30},{8,16},{10,18},{12,20},{14,22},{16,8},... | collective-permute-start | bytes 196616 | tf_op jit(solution)/shard_map/ppermute | solution.py:412
  26.9 0.0 collective-permute-start.8
  26.9 0.6 %collective-permute-start.7 = (f32[16,1024]{1,0:T(8,128)S(1)}, f32[16,1024]{1,0:T(8,128)S(1)}, u32[]{:S(2)}, u32[]{:S(2)}) collective-permute-start(f32[16,1024]{1,0:T(8,128)S(1)} %add_add_fusion.1), channel_id=1, source_target_pairs={{0,8},{2,10},{4,12},{6,14},{8,0},{10,2},{12,4},{14,6},{16,24},{18,... | collective-permute-start | bytes 196616 | tf_op jit(solution)/shard_map/ppermute | solution.py:412
  27.6 1.7 %taper.7 = f32[16,256]{1,0:T(8,128)S(1)} custom-call(s32[8,8]{1,0:T(8,128)S(1)} %copy-done, s32[8]{0:T(128)S(1)} %copy-done.1, f32[16,1280]{1,0:T(8,128)S(1)} %get-tuple-element.15.own_ref.stack_ref, bf16[32,3968]{1,0:T(8,128)(2,1)S(1)} %get-tuple-element.16.values_ref, f32[2,3840]{1,0:T(2,128)S(1)} %get-tuple-element.17.coords_ref), custom_call_target="tpu_custom_call" | custom-call | flops 1572864000 | bytes 1048576 | tf_op jit(solution)/shard_map/taper/pallas_call | solution.py:387
  29.3 0.0 collective-permute-done.9
  29.3 2.8 %collective-permute-done.8 = f32[16,1024]{1,0:T(8,128)S(1)} collective-permute-done((f32[16,1024]{1,0:T(8,128)S(1)}, f32[16,1024]{1,0:T(8,128)S(1)}, u32[]{:S(2)}, u32[]{:S(2)}) %collective-permute-start.8) | collective-permute-done | bytes 65568 | tf_op jit(solution)/shard_map/ppermute | solution.py:412
  32.1 0.0 collective-permute-done.7
  32.1 0.1 collective-permute-start.10
  32.2 0.0 slice-done
  32.2 0.0 slice-done.1
  32.2 1.7 %factor.2.before_ref = f32[16,1024]{1,0:T(8,128)S(1)} custom-call(f32[16,1024]{1,0:T(8,128)S(1)} %add_add_fusion.proj_ref, f32[1024,2048]{1,0:T(8,128)S(1)} %bitcast.1, f32[16,256]{1,0:T(8,128)S(1)} %taper.4.rest_0_, f32[16,256]{1,0:T(8,128)S(1)} %taper.5.rest_1_, f32[16,256]{1,0:T(8,128)S(1)} %taper.6.rest_2_), custom_call_target="tpu_custom_call" | custom-call | flops 1258291200 | bytes 4194304 | tf_op jit(solution)/shard_map/factor/pallas_call | solution.py:295
  33.9 0.0 collective-permute-done.10.proj_ref
  33.9 1.7 %factor.3.factor_ref = f32[16,1024]{1,0:T(8,128)S(1)} custom-call(f32[16,1024]{1,0:T(8,128)S(1)} %factor.2.before_ref, f32[16,1024]{1,0:T(8,128)S(1)} %collective-permute-done.10.proj_ref, f32[1024,2048]{1,0:T(8,128)S(1)} %bitcast.1), custom_call_target="tpu_custom_call" | custom-call | flops 1258291200 | bytes 4194304 | tf_op jit(solution)/shard_map/factor/pallas_call | solution.py:295
  35.6 1.3 %spread.2 = f32[16,1024]{1,0:T(8,128)S(1)} custom-call(f32[16,1024]{1,0:T(8,128)S(1)} %factor.3.factor_ref, bf16[1024,1024]{1,0:T(8,128)(2,1)S(1)} %get-tuple-element.21.high_ref, bf16[1024,1024]{1,0:T(8,128)(2,1)S(1)} %get-tuple-element.22.low_ref), custom_call_target="tpu_custom_call" | custom-call | flops 891289600 | bytes 4194304 | tf_op jit(solution)/shard_map/spread/pallas_call | solution.py:322
  36.9 0.5 %collective-permute-start.11 = (f32[16,1024]{1,0:T(8,128)S(1)}, f32[16,1024]{1,0:T(8,128)S(1)}, u32[]{:S(2)}, u32[]{:S(2)}) collective-permute-start(f32[16,1024]{1,0:T(8,128)S(1)} %spread.2), channel_id=1, source_target_pairs={{1,0},{0,1},{3,2},{2,3},{5,4},{4,5},{7,6},{6,7},{9,8},{8,9},{11,10... | collective-permute-start | bytes 196616 | tf_op jit(solution)/shard_map/ppermute | solution.py:423
  37.4 1.3 %spread.3 = f32[16,1024]{1,0:T(8,128)S(1)} custom-call(f32[16,1024]{1,0:T(8,128)S(1)} %factor.3.factor_ref, bf16[1024,1024]{1,0:T(8,128)(2,1)S(1)} %get-tuple-element.23.high_ref, bf16[1024,1024]{1,0:T(8,128)(2,1)S(1)} %get-tuple-element.24.low_ref), custom_call_target="tpu_custom_call" | custom-call | flops 891289600 | bytes 4194304 | tf_op jit(solution)/shard_map/spread/pallas_call | solution.py:322
  38.7 0.0 collective-permute-done.11
  38.7 0.7 %fusion = f32[16,1024]{1,0:T(8,128)} fusion(f32[16,1024]{1,0:T(8,128)S(1)} %spread.3, f32[16,1024]{1,0:T(8,128)S(1)} %collective-permute-done.11, f32[16,256]{1,0:T(8,128)S(1)} %taper.7, f32[16,256]{1,0:T(8,128)S(1)} %taper.6.rest_2_, f32[16,256]{1,0:T(8,128)S(1)} %taper.5.rest_1_, f32[16,256]{1,0:T(8,128)S(1)} %taper.4.rest_0_), kind=kLoop, calls=%fused_computation.1 | loop fusion | flops 81920 | bytes 262144 | tf_op jit(solution)/shard_map/add | solution.py:466
  (6 shorter events, 0.1 us)
Async XLA Ops:
  0.9 9.3 %collective-permute-start.2 = (f32[16,1280]{1,0:T(8,128)S(1)}, f32[16,1280]{1,0:T(8,128)S(1)}, u32[]{:S(2)}, u32[]{:S(2)}) collective-permute-start(f32[16,1280]{1,0:T(8,128)S(1)} %get-tuple-element.15.own_ref.stack_ref), channel_id=1, source_target_pairs={{2,4},{6,8},{10,12},{14,16},{18,20},{22,24},{26,28},{4,2},{8,6},{1... | collective-permute-start | bytes 245768 | tf_op jit(solution)/shard_map/ppermute | solution.py:429
  1.6 9.6 %collective-permute-start.1 = (f32[16,1280]{1,0:T(8,128)S(1)}, f32[16,1280]{1,0:T(8,128)S(1)}, u32[]{:S(2)}, u32[]{:S(2)}) collective-permute-start(f32[16,1280]{1,0:T(8,128)S(1)} %get-tuple-element.15.own_ref.stack_ref), channel_id=1, source_target_pairs={{0,2},{4,6},{8,10},{12,14},{16,18},{20,22},{24,26},{28,30},{2,0},{... | collective-permute-start | bytes 245768 | tf_op jit(solution)/shard_map/ppermute | solution.py:429
  7.3 3.9 %collective-permute-start = (f32[16,1280]{1,0:T(8,128)S(1)}, f32[16,1280]{1,0:T(8,128)S(1)}, u32[]{:S(2)}, u32[]{:S(2)}) collective-permute-start(f32[16,1280]{1,0:T(8,128)S(1)} %get-tuple-element.15.own_ref.stack_ref), channel_id=1, source_target_pairs={{1,0},{0,1},{3,2},{2,3},{5,4},{4,5},{7,6},{6,7},{9,8},{8,9},{11,10... | collective-permute-start | bytes 245768 | tf_op jit(solution)/shard_map/ppermute | solution.py:423
  11.1 6.6 %copy-start = (s32[8,8]{1,0:T(8,128)S(1)}, s32[8,8]{1,0:T(8,128)}, u32[]{:S(2)}) copy-start(s32[8,8]{1,0:T(8,128)} %ids_ref.7) | copy-start | bytes 772
  11.1 6.6 %copy-start.1 = (s32[8]{0:T(128)S(1)}, s32[8]{0:T(128)}, u32[]{:S(2)}) copy-start(s32[8]{0:T(128)} %counts_ref.7) | copy-start | bytes 100
  11.2 6.6 %collective-permute-start.3 = (f32[16,512]{1,0:T(8,128)S(1)}, f32[16,512]{1,0:T(8,128)S(1)}, u32[]{:S(2)}, u32[]{:S(2)}) collective-permute-start(f32[16,512]{1,0:T(8,128)S(1)} %corner.1), channel_id=1, source_target_pairs={{1,0},{0,1},{3,2},{2,3},{5,4},{4,5},{7,6},{6,7},{9,8},{8,9},{11,10... | collective-permute-start | bytes 98312 | tf_op jit(solution)/shard_map/ppermute | solution.py:423
  14.2 8.8 %collective-permute-start.6 = (f32[16,1024]{1,0:T(8,128)S(1)}, f32[16,1024]{1,0:T(8,128)S(1)}, u32[]{:S(2)}, u32[]{:S(2)}) collective-permute-start(f32[16,1024]{1,0:T(8,128)S(1)} %add.27), channel_id=1, source_target_pairs={{0,6},{2,4},{4,2},{6,0},{8,14},{10,12},{12,10},{14,8},{16,22},{18,... | collective-permute-start | bytes 196616 | tf_op jit(solution)/shard_map/ppermute | solution.py:412
  16.1 6.9 %collective-permute-start.5 = (f32[16,1024]{1,0:T(8,128)S(1)}, f32[16,1024]{1,0:T(8,128)S(1)}, u32[]{:S(2)}, u32[]{:S(2)}) collective-permute-start(f32[16,1024]{1,0:T(8,128)S(1)} %add.27), channel_id=1, source_target_pairs={{0,4},{2,6},{4,0},{6,2},{8,12},{10,14},{12,8},{14,10},{16,20},{18,... | collective-permute-start | bytes 196616 | tf_op jit(solution)/shard_map/ppermute | solution.py:412
  17.5 5.5 %collective-permute-start.4 = (f32[16,1024]{1,0:T(8,128)S(1)}, f32[16,1024]{1,0:T(8,128)S(1)}, u32[]{:S(2)}, u32[]{:S(2)}) collective-permute-start(f32[16,1024]{1,0:T(8,128)S(1)} %add.27), channel_id=1, source_target_pairs={{0,2},{2,0},{4,6},{6,4},{8,10},{10,8},{12,14},{14,12},{16,18},{18,... | collective-permute-start | bytes 196616 | tf_op jit(solution)/shard_map/ppermute | solution.py:412
  19.5 12.7 %slice-start = ((s8[8388608]{0:T(1024)(128)(4,1)}), s8[4194304]{0:T(1024)(128)(4,1)S(1)}, s32[]{:S(2)}) async-start(s8[8388608]{0:T(1024)(128)(4,1)} %bitcast), calls=%async_computation | async-start | bytes 8388608
  21.2 11.0 %slice-start.1 = ((s8[8388608]{0:T(1024)(128)(4,1)}), s8[4194304]{0:T(1024)(128)(4,1)S(1)}, s32[]{:S(2)}) async-start(s8[8388608]{0:T(1024)(128)(4,1)} %bitcast), calls=%async_computation.1 | async-start | bytes 8388608
  23.0 6.3 %collective-permute-start.9 = (f32[16,1024]{1,0:T(8,128)S(1)}, f32[16,1024]{1,0:T(8,128)S(1)}, u32[]{:S(2)}, u32[]{:S(2)}) collective-permute-start(f32[16,1024]{1,0:T(8,128)S(1)} %add_add_fusion.1), channel_id=1, source_target_pairs={{0,24},{2,26},{4,28},{6,30},{8,16},{10,18},{12,20},{14,22},{16,8},... | collective-permute-start | bytes 196616 | tf_op jit(solution)/shard_map/ppermute | solution.py:412
  26.9 5.2 %collective-permute-start.8 = (f32[16,1024]{1,0:T(8,128)S(1)}, f32[16,1024]{1,0:T(8,128)S(1)}, u32[]{:S(2)}, u32[]{:S(2)}) collective-permute-start(f32[16,1024]{1,0:T(8,128)S(1)} %add_add_fusion.1), channel_id=1, source_target_pairs={{0,16},{2,18},{4,20},{6,22},{8,24},{10,26},{12,28},{14,30},{16,0},... | collective-permute-start | bytes 196616 | tf_op jit(solution)/shard_map/ppermute | solution.py:412
  26.9 5.2 %collective-permute-start.7 = (f32[16,1024]{1,0:T(8,128)S(1)}, f32[16,1024]{1,0:T(8,128)S(1)}, u32[]{:S(2)}, u32[]{:S(2)}) collective-permute-start(f32[16,1024]{1,0:T(8,128)S(1)} %add_add_fusion.1), channel_id=1, source_target_pairs={{0,8},{2,10},{4,12},{6,14},{8,0},{10,2},{12,4},{14,6},{16,24},{18,... | collective-permute-start | bytes 196616 | tf_op jit(solution)/shard_map/ppermute | solution.py:412
  32.1 1.8 %collective-permute-start.10 = (f32[16,1024]{1,0:T(8,128)S(1)}, f32[16,1024]{1,0:T(8,128)S(1)}, u32[]{:S(2)}, u32[]{:S(2)}) collective-permute-start(f32[16,1024]{1,0:T(8,128)S(1)} %add_add_fusion.proj_ref), channel_id=1, source_target_pairs={{1,0},{0,1},{3,2},{2,3},{5,4},{4,5},{7,6},{6,7},{9,8},{8,9},{11,10... | collective-permute-start | bytes 196616 | tf_op jit(solution)/shard_map/ppermute | solution.py:423
  36.9 1.8 %collective-permute-start.11 = (f32[16,1024]{1,0:T(8,128)S(1)}, f32[16,1024]{1,0:T(8,128)S(1)}, u32[]{:S(2)}, u32[]{:S(2)}) collective-permute-start(f32[16,1024]{1,0:T(8,128)S(1)} %spread.2), channel_id=1, source_target_pairs={{1,0},{0,1},{3,2},{2,3},{5,4},{4,5},{7,6},{6,7},{9,8},{8,9},{11,10... | collective-permute-start | bytes 196616 | tf_op jit(solution)/shard_map/ppermute | solution.py:423

commit v8 on v6

--- a/solution.py
+++ b/solution.py
@@ -25,6 +25,7 @@
 LIMIT = 6 * 1024 * 1024
 VMEM = pl.BlockSpec(memory_space=pltpu.VMEM)
 HBM = pl.BlockSpec(memory_space=pltpu.HBM)
+ANY = pl.BlockSpec(memory_space=pl.ANY)
 SMEM = pl.BlockSpec(memory_space=pltpu.SMEM)
 
 
@@ -144,18 +145,47 @@
     )(below, own, above)
 
 
-def project_kernel(scale, grain, stack_ref, knots_ref, out_ref, high_ref, low_ref, copy_ref, columns, weights):
+def assemble_kernel(own_ref, east_ref, west_ref, values_ref, coords_ref):
+    probes, width = own_ref.shape
+    points = width - 2 * LANES
+    inverse = 1.0 / TAPER_LEN
+    for turn, ref in enumerate((own_ref, east_ref, west_ref)):
+        start = turn * points
+        values_ref[:, start : start + points] = stacked_halves(ref[:, :points])
+        for axis in range(2):
+            rows = coordinate_rows(ref, points, axis) * inverse
+            for index in range(points // LANES):
+                lanes = slice(start + index * LANES, start + (index + 1) * LANES)
+                coords_ref[axis : axis + 1, lanes] = rows[index : index + 1]
+    values_ref[:, 3 * points :] = jnp.zeros((2 * probes, LANES), jnp.bfloat16)
+
+
+def assemble(strips):
+    probes, width = strips[0].shape
+    near = 3 * (width - 2 * LANES)
+    return pl.pallas_call(
+        assemble_kernel,
+        out_shape=(
+            jax.ShapeDtypeStruct((2 * probes, near + LANES), jnp.bfloat16),
+            jax.ShapeDtypeStruct((2, near), jnp.float32),
+        ),
+        in_specs=[VMEM] * 3,
+        out_specs=(VMEM, VMEM),
+        compiler_params=pltpu.CompilerParams(vmem_limit_bytes=LIMIT),
+        name="assemble",
+    )(*strips)
+
+
+def project_kernel(scale, grain, stack_ref, knots_ref, out_ref, high_ref, low_ref, copy_ref, weights):
     points, knots = high_ref.shape
     probes = stack_ref.shape[0]
     tile = min(TILE, knots)
     wide = min(TILE, points)
     copy_ref[...] = stack_ref[...]
-    for axis in range(2):
-        turned = jnp.transpose(coordinate_rows(stack_ref, points, axis) * scale)
-        turned = (turned + grain) - grain
-        for index in range(points // LANES):
-            columns[index * LANES : (index + 1) * LANES, axis : axis + 1] = turned[:, index : index + 1]
     weights[...] = stacked_halves(stack_ref[:, :points])
+    east, north = [
+        (jnp.transpose(coordinate_rows(stack_ref, points, axis) * scale) + grain) - grain for axis in range(2)
+    ]
 
     @pl.loop(0, knots // tile)
     def _(step):
@@ -165,15 +195,21 @@
         ]
         total = jnp.zeros((2 * probes, tile), jnp.float32)
         for start in range(0, points, wide):
-            rows = slice(start, start + wide)
-            dx = columns[rows, 0:1] - kx
-            dy = columns[rows, 1:2] - ky
-            square = dx * dx + dy * dy
-            high, low = halves(jnp.exp2(-(square * lax.rsqrt(square))))
-            high_ref[rows, lanes] = high
-            low_ref[rows, lanes] = low
-            part = weights[:, rows]
-            total = total + (dot_nn(part, high) + dot_nn(part, low))
+            highs, lows = [], []
+            for row in range(start, start + wide, LANES):
+                block = row // LANES
+                dx = east[:, block : block + 1] - kx
+                dy = north[:, block : block + 1] - ky
+                square = dx * dx + dy * dy
+                high, low = halves(jnp.exp2(-(square * lax.rsqrt(square))))
+                high_ref[row : row + LANES, lanes] = high
+                low_ref[row : row + LANES, lanes] = low
+                highs.append(high)
+                lows.append(low)
+            part = weights[:, start : start + wide]
+            total = total + (
+                dot_nn(part, jnp.concatenate(highs, axis=0)) + dot_nn(part, jnp.concatenate(lows, axis=0))
+            )
         out_ref[:, lanes] = folded(total)
 
 
@@ -190,46 +226,61 @@
         ),
         in_specs=[VMEM, VMEM],
         out_specs=(VMEM, VMEM, VMEM, VMEM),
-        scratch_shapes=[
-            pltpu.VMEM((points, 8), jnp.float32),
-            pltpu.VMEM((2 * probes, points), jnp.bfloat16),
-        ],
+        scratch_shapes=[pltpu.VMEM((2 * probes, points), jnp.bfloat16)],
         compiler_params=pltpu.CompilerParams(vmem_limit_bytes=LIMIT),
         cost_estimate=cost(2800, points * knots, 2),
         name="project",
     )(stack, knot_locs)
 
 
-def factor_kernel(scale, step, before_ref, proj_ref, precision_ref, *rest):
-    out_ref, weights = rest[-2:]
+def split_kernel(first, precision_ref, *rest):
+    high_ref, low_ref = rest[-2:]
+    rows = high_ref.shape[0]
+    tile = min(TILE, rows)
+    for start in range(0, rows, tile):
+        here = slice(start, start + tile)
+        high_ref[here, :], low_ref[here, :] = halves(precision_ref[first + start : first + start + tile, :])
+
+
+def split_rows(precision, first, rows, after):
+    depth = precision.shape[1]
+    return pl.pallas_call(
+        functools.partial(split_kernel, first),
+        out_shape=(pltpu.VMEM((rows, depth), jnp.bfloat16), pltpu.VMEM((rows, depth), jnp.bfloat16)),
+        in_specs=[VMEM] + [ANY] * len(after),
+        out_specs=(VMEM, VMEM),
+        compiler_params=pltpu.CompilerParams(vmem_limit_bytes=LIMIT),
+        cost_estimate=cost(60, rows * depth),
+        name="split",
+    )(precision, *after)
+
+
+def factor_kernel(scale, step, parts, before_ref, proj_ref, *rest):
+    highs, lows, (out_ref, weights) = rest[:parts], rest[parts : 2 * parts], rest[-2:]
     probes, depth = proj_ref.shape
-    all_rows = precision_ref.shape[0]
-    tile = min(TILE, all_rows)
-    wide = min(TILE, depth)
     weights[...] = stacked_halves(proj_ref[...] * scale)
     owner = lax.rem(lax.axis_index("knot") + step, lax.axis_size("knot"))
-    offset = owner * depth
-
-    @pl.loop(0, all_rows // tile)
-    def _(turn):
-        rows = pl.ds(pl.multiple_of(turn * tile, tile), tile)
-        total = jnp.zeros((weights.shape[0], tile), jnp.float32)
-        for start in range(0, depth, wide):
-            lanes = pl.ds(pl.multiple_of(offset + start, wide), wide)
-            high, low = halves(precision_ref[rows, lanes])
-            part = weights[:, start : start + wide]
-            total = total + (dot_nt(part, high) + dot_nt(part, low))
-        found = folded(total)
-        if before_ref is not None:
-            found = found + before_ref[:, rows]
-        out_ref[:, rows] = found
-
-
-def factored(before, projection, precision, scale, step, after=()):
+    lanes = pl.ds(pl.multiple_of(owner * depth, depth), depth)
+    rows = highs[0].shape[0]
+    tile = min(TILE, rows)
+    for part, (high_ref, low_ref) in enumerate(zip(highs, lows)):
+        for start in range(0, rows, tile):
+            here = slice(start, start + tile)
+            found = folded(dot_nt(weights[...], high_ref[here, lanes]) + dot_nt(weights[...], low_ref[here, lanes]))
+            target = slice(part * rows + start, part * rows + start + tile)
+            if before_ref is not None:
+                found = found + before_ref[:, target]
+            out_ref[:, target] = found
+
+
+def factored(before, projection, splits, scale, step):
     probes, depth = projection.shape
-    rows = precision.shape[0]
-    kernel = functools.partial(factor_kernel, scale, step)
-    operands = (projection, precision, *after)
+    highs, lows = [
+        [pltpu.with_memory_space_constraint(split[half], pltpu.VMEM) for split in splits] for half in range(2)
+    ]
+    rows = sum(high.shape[0] for high in highs)
+    kernel = functools.partial(factor_kernel, scale, step, len(splits))
+    operands = (projection, *highs, *lows)
     if before is None:
         kernel = functools.partial(kernel, None)
     else:
@@ -237,11 +288,11 @@
     return pl.pallas_call(
         kernel,
         out_shape=jax.ShapeDtypeStruct((probes, rows), jnp.float32),
-        in_specs=[VMEM] * (len(operands) - len(after)) + [pl.BlockSpec(memory_space=pl.ANY)] * len(after),
+        in_specs=[VMEM] * len(operands),
         out_specs=VMEM,
         scratch_shapes=[pltpu.VMEM((2 * probes, depth), jnp.bfloat16)],
         compiler_params=pltpu.CompilerParams(vmem_limit_bytes=LIMIT),
-        cost_estimate=cost(1200, rows * depth),
+        cost_estimate=cost(1000, rows * depth),
         name="factor",
     )(*operands)
 
@@ -279,27 +330,18 @@
     return jnp.exp2(scaled * (-LOG2E * TAPER_LEN / COV_RANGE)) * (remain * remain) * (1.0 + 4.0 * scaled)
 
 
-def taper_kernel(first, ids_ref, counts_ref, own_ref, near_ref, out_ref, values, coords):
+def taper_kernel(first, ids_ref, counts_ref, own_ref, values_ref, coords_ref, *rest):
+    out_ref = rest[-1]
     own_blocks, slots = ids_ref.shape
     block = LANES
-    strips, probes, width = near_ref.shape
+    probes = own_ref.shape[0]
     span = own_blocks + 2
+    zeros_place = coords_ref.shape[1] // block
     column = lax.axis_index("space")
     north_base = lax.axis_index("knot") * own_blocks - 1
     north_cells = lax.axis_size("knot") * own_blocks
-    inverse = 1.0 / TAPER_LEN
-    values[:, strips * span * block :] = jnp.zeros((values.shape[0], block), jnp.bfloat16)
-    for strip in range(strips):
-        values[:, strip * span * block : (strip + 1) * span * block] = padded_halves(
-            near_ref[strip, :, : span * block], values.shape[0]
-        )
-        for axis in range(2):
-            rows = near_ref[strip, :, (span + axis) * block : (span + axis + 1) * block] * inverse
-            for index in range(span):
-                start = (strip * span + index) * block
-                coords[axis : axis + 1, start : start + block] = rows[index : index + 1]
     own_columns = [
-        jnp.transpose(coordinate_rows(own_ref, own_blocks * block, axis) * inverse) for axis in range(2)
+        jnp.transpose(coordinate_rows(own_ref, own_blocks * block, axis) * (1.0 / TAPER_LEN)) for axis in range(2)
     ]
 
     def place(group, slot):
@@ -307,7 +349,7 @@
         east = jnp.where(ahead >= north_cells, 1, 0) + jnp.where(ahead >= 2 * north_cells, 1, 0)
         strip = jnp.where(east == 1, 0, 1 + lax.rem(column + lax.div(east, 2) + 1, 2))
         index = strip * span + (ahead - east * north_cells - north_base)
-        return lanes_of(index), lanes_of(jnp.where(slot < counts_ref[group], index, strips * span))
+        return lanes_of(index), lanes_of(jnp.where(slot < counts_ref[group], index, zeros_place))
 
     def lanes_of(index):
         return pl.ds(pl.multiple_of(index * block, block), block)
@@ -315,15 +357,15 @@
     for index in range(out_ref.shape[1] // block):
         group = first + index
         px, py = [turned[:, group : group + 1] for turned in own_columns]
-        total = jnp.zeros((block, values.shape[0]), jnp.float32)
+        total = jnp.zeros((block, 2 * probes), jnp.float32)
         for pair in range(0, slots, 2):
             highs, lows, parts = [], [], []
             for slot in range(pair, min(pair + 2, slots)):
                 lanes, value_lanes = place(group, slot)
-                high, low = halves(covariance(distance(px, py, coords[0:1, lanes], coords[1:2, lanes])))
+                high, low = halves(covariance(distance(px, py, coords_ref[0:1, lanes], coords_ref[1:2, lanes])))
                 highs.append(high)
                 lows.append(low)
-                parts.append(values[:, value_lanes])
+                parts.append(values_ref[:, value_lanes])
             part = jnp.concatenate(parts, axis=1)
             total = total + (
                 dot_nt(jnp.concatenate(highs, axis=1), part) + dot_nt(jnp.concatenate(lows, axis=1), part)
@@ -334,37 +376,56 @@
         )
 
 
-def taper(ids, counts, own, near, first, blocks):
-    own_blocks, slots = ids.shape
-    strips, probes, width = near.shape
+def taper(ids, counts, own, values, coords, first, blocks, after):
+    slots = ids.shape[1]
     return pl.pallas_call(
         functools.partial(taper_kernel, first),
-        out_shape=jax.ShapeDtypeStruct((probes, blocks * LANES), jnp.float32),
-        in_specs=[SMEM, SMEM, VMEM, VMEM],
+        out_shape=jax.ShapeDtypeStruct((own.shape[0], blocks * LANES), jnp.float32),
+        in_specs=[SMEM, SMEM, VMEM, VMEM, VMEM] + [ANY] * len(after),
         out_specs=VMEM,
-        scratch_shapes=[
-            pltpu.VMEM((LANES, (strips * (own_blocks + 2) + 1) * LANES), jnp.bfloat16),
-            pltpu.VMEM((2, strips * (own_blocks + 2) * LANES), jnp.float32),
-        ],
-        compiler_params=pltpu.CompilerParams(vmem_limit_bytes=LIMIT),
-        cost_estimate=cost(6000, blocks * slots * LANES * LANES, 2),
+        compiler_params=pltpu.CompilerParams(vmem_limit_bytes=LIMIT),
+        cost_estimate=cost(500, blocks * slots * LANES * LANES, 2),
         name="taper",
-    )(ids, counts, own, near)
-
-
-def doubling_sum(value, axis, other):
+    )(ids, counts, own, values, coords, *after)
+
+
+def add_kernel(count, *refs):
+    total = refs[0][...]
+    for ref in refs[1:count]:
+        total = total + ref[...]
+    refs[-1][...] = total
+
+
+def add_all(values, after):
+    return pl.pallas_call(
+        functools.partial(add_kernel, len(values)),
+        out_shape=jax.ShapeDtypeStruct(values[0].shape, jnp.float32),
+        in_specs=[VMEM] * len(values) + [ANY] * len(after),
+        out_specs=VMEM,
+        compiler_params=pltpu.CompilerParams(vmem_limit_bytes=LIMIT),
+        name="add",
+    )(*values, *after)
+
+
+def butterfly_rounds(count):
+    assert count & (count - 1) == 0
+    bits = [1 << i for i in range(count.bit_length() - 1)]
+    rounds = [(low | high, high, low) for low, high in zip(bits[0::2], bits[1::2])]
+    return rounds + [(bit,) for bit in bits[len(rounds) * 2 :]]
+
+
+def butterfly_round(value, axis, other, turn):
     count, groups = lax.axis_size(axis), lax.axis_size(other)
-    if count & (count - 1):
-        return lax.psum(value, axis)
-    steps = [1 << i for i in range(count.bit_length() - 1)]
-    half = len(steps) // 2
-    for turn in range(len(steps)):
+    rounds = butterfly_rounds(count)
+    half = len(rounds) // 2 if len({len(steps) for steps in rounds}) == 1 else 0
+    got = []
+    for kind in range(len(rounds[turn])):
         pairs = []
         for j in range(groups):
-            step = steps[(turn + half * (j % 2)) % len(steps)]
+            step = rounds[(turn + half * (j % 2)) % len(rounds)][kind]
             pairs += [(i * groups + j, (i ^ step) * groups + j) for i in range(count)]
-        value = value + lax.ppermute(value, (axis, other), pairs)
-    return value
+        got.append(lax.ppermute(value, (axis, other), pairs))
+    return got
 
 
 def shifted(value, axis, step):
@@ -397,15 +458,31 @@
     stack = parts[0][3]
 
     strip = make_strip(chunks[-1], stack, chunks[1 % groups])
-    near = jnp.stack([strip, paired(strip, "space", 0), paired(strip, "space", 1)])
-    pieces = math.gcd(own_blocks, 4)
+    values, coords = assemble([strip, paired(strip, "space", 0), paired(strip, "space", 1)])
+    projection = sum(part[0] for part in parts)
+    rounds = len(butterfly_rounds(lax.axis_size("space")))
+    pieces = math.gcd(own_blocks, 2 * rounds)
     per_piece = own_blocks // pieces
-    base = [taper(neighbours, counts, stack, near, i * per_piece, per_piece) for i in range(pieces)]
-
-    projection = doubling_sum(sum(part[0] for part in parts), "space", "knot")
-    factor = factored(None, projection, knot_precision, proj_scale, 0, base[:-1])
+    row_pieces = math.gcd(knot_precision.shape[0] // LANES, rounds)
+    per_split = knot_precision.shape[0] // row_pieces
+    base, splits = [], []
+    for turn in range(rounds):
+        got = butterfly_round(projection, "space", "knot", turn)
+        beside = []
+        for i in range(pieces):
+            if i * rounds // pieces == turn:
+                base.append(
+                    taper(neighbours, counts, stack, values, coords, i * per_piece, per_piece, [projection])
+                )
+                beside.append(base[-1])
+        for i in range(row_pieces):
+            if i * rounds // row_pieces == turn:
+                splits.append(split_rows(knot_precision, i * per_split, per_split, [projection]))
+                beside.extend(splits[-1])
+        projection = add_all([projection, *got], beside)
+    factor = factored(None, projection, splits, proj_scale, 0)
     for step in range(1, groups):
-        factor = factored(factor, shifted(projection, "knot", step), knot_precision, proj_scale, step)
+        factor = factored(factor, shifted(projection, "knot", step), splits, proj_scale, step)
     total = jnp.concatenate(base, axis=1)
     for step in reversed(range(groups)):
         share = spread(factor, parts[step][1], parts[step][2], LOW_SCALE * EXPAND_GAIN)

time: 40.7 us -> 38.2 us (0.939)
  waiting for transfers between devices: 5.92 us -> 1.83 us
  starting transfers between devices: 13.1 us -> 15.4 us
  Pallas kernels: 20.6 us -> 19.9 us
    ppermute x4 -> x6, waiting for transfers between devices: 5.9 us -> 1.82 us  [butterfly_round(): got.append(lax.ppermute(value, (axis, other), pairs))]
    ppermute x4 -> x6, starting transfers between devices: 5.96 us -> 8.01 us  [butterfly_round(): got.append(lax.ppermute(value, (axis, other), pairs))]
    pallas_call x0 -> x5, Pallas kernels: none -> 1.26 us  [the longest x2 1.18 us: split_rows(): pl.pallas_call(functools.partial(split_kernel, first), out_shape=(pltpu.V...]
    pallas_call x2, Pallas kernels: 3.38 us -> 2.6 us  [factored(): pl.pallas_call(kernel, out_shape=jax.ShapeDtypeStruct((probes, rows), jnp...]
    pallas_call x2, Pallas kernels: 6.48 us -> 5.76 us  [project(): pl.pallas_call(functools.partial(project_kernel, scale, grain), out_shape...]
    pallas_call x4, Pallas kernels: 7.24 us -> 6.82 us  [taper(): pl.pallas_call(functools.partial(taper_kernel, first), out_shape=jax.Shap...]
  transfers between devices with their start and end apart: 9 -> 11, of which waited for: 3 -> 1; matrix products, arithmetic and copies ran while one was open for 0% -> 0% of each run, Pallas kernels for 41% -> 43%
where the time goes in v8:
time: 38.2 us; the launch traced here: 38 us
  Pallas kernels  19.9 us (52%)
  starting transfers between devices  15.4 us (40%)
  waiting for transfers between devices  1.83 us (5%)
  other arithmetic  0.7 us (2%)
    ppermute x6, starting transfers between devices, butterfly_round(): got.append(lax.ppermute(value, (axis, other), pairs))  8.01 us
    pallas_call x4, Pallas kernels, taper(): pl.pallas_call(functools.partial(taper_kernel, first), out_shape=jax.Shap...  6.82 us
    ppermute x2, starting transfers between devices, paired(): return lax.ppermute(value, axis, pairs + [(b, a) for a, b in pairs])  6.24 us
    pallas_call x2, Pallas kernels, project(): pl.pallas_call(functools.partial(project_kernel, scale, grain), out_shape...  5.76 us
    pallas_call x2, Pallas kernels, factored(): pl.pallas_call(kernel, out_shape=jax.ShapeDtypeStruct((probes, rows), jnp...  2.6 us
    pallas_call x2, Pallas kernels, spread(): pl.pallas_call(functools.partial(spread_kernel, scale), out_shape=jax.Sha...  2.56 us
    ppermute x6, waiting for transfers between devices, butterfly_round(): got.append(lax.ppermute(value, (axis, other), pairs))  1.82 us
    pallas_call x2, Pallas kernels, split_rows(): pl.pallas_call(functools.partial(split_kernel, first), out_shape=(pltpu.V...  1.18 us
  transfers between devices with their start and end apart: 11, of which 1 were waited for; matrix products, arithmetic and copies ran while one was open for 0% of the time, Pallas kernels for 43%

profile of v8, /device:TPU:0, one launch (start us, length us, event | category | flops | bytes accessed | tf_op | source)
XLA Modules:
  0.0 38.0 jit_solution(808755514061442715)
XLA Ops:
  0.0 0.9 %prepare.1 = (f32[16,1280]{1,0:T(8,128)S(1)}, f32[2,1024]{1,0:T(2,128)S(1)}) custom-call(f32[16,1024]{1,0:T(8,128)} %probes_ref.1, f32[2,1024]{1,0:T(2,128)} %locations_ref.1, f32[2,1024]{1,0:T(2,128)} %knots_ref.1), custom_call_target="tpu_custom_call" | custom-call | tf_op jit(solution)/shard_map/prepare/pallas_call | solution.py:107
  0.9 0.5 %collective-permute-start = (f32[16,1280]{1,0:T(8,128)S(1)}, f32[16,1280]{1,0:T(8,128)S(1)}, u32[]{:S(2)}, u32[]{:S(2)}) collective-permute-start(f32[16,1280]{1,0:T(8,128)S(1)} %get-tuple-element.20.stack_ref), channel_id=1, source_target_pairs={{1,0},{0,1},{3,2},{2,3},{5,4},{4,5},{7,6},{6,7},{9,8},{8,9},{11,10... | collective-permute-start | bytes 245768 | tf_op jit(solution)/shard_map/ppermute | solution.py:435
  1.4 0.0 slice-start
  1.4 2.9 %project.2 = (f32[16,1024]{1,0:T(8,128)S(1)}, bf16[1024,1024]{1,0:T(8,128)(2,1)S(1)}, bf16[1024,1024]{1,0:T(8,128)(2,1)S(1)}, f32[16,1280]{1,0:T(8,128)S(1)}) custom-call(f32[16,1280]{1,0:T(8,128)S(1)} %get-tuple-element.20.stack_ref, f32[2,1024]{1,0:T(2,128)S(1)} %get-tuple-element.21.knots_ref), custom_call_target="tpu_custom_call" | custom-call | flops 2936012800 | bytes 4194304 | tf_op jit(solution)/shard_map/project/pallas_call | solution.py:219
  4.3 0.0 collective-permute-done.below_ref.above_ref.stack_ref
  4.3 0.0 slice-start.1
  4.3 0.8 %collective-permute-start.2 = (f32[16,1536]{1,0:T(8,128)S(1)}, f32[16,1536]{1,0:T(8,128)S(1)}, u32[]{:S(2)}, u32[]{:S(2)}) collective-permute-start(f32[16,1536]{1,0:T(8,128)S(1)} %strip.1.own_ref), channel_id=1, source_target_pairs={{2,4},{6,8},{10,12},{14,16},{18,20},{22,24},{26,28},{4,2},{8,6},{1... | collective-permute-start | bytes 294920 | tf_op jit(solution)/shard_map/ppermute | solution.py:441
  5.1 5.4 %collective-permute-start.1 = (f32[16,1536]{1,0:T(8,128)S(1)}, f32[16,1536]{1,0:T(8,128)S(1)}, u32[]{:S(2)}, u32[]{:S(2)}) collective-permute-start(f32[16,1536]{1,0:T(8,128)S(1)} %strip.1.own_ref), channel_id=1, source_target_pairs={{0,2},{4,6},{8,10},{12,14},{16,18},{20,22},{24,26},{28,30},{2,0},{... | collective-permute-start | bytes 294920 | tf_op jit(solution)/shard_map/ppermute | solution.py:441
  10.6 2.9 %project.3 = (f32[16,1024]{1,0:T(8,128)S(1)}, bf16[1024,1024]{1,0:T(8,128)(2,1)S(1)}, bf16[1024,1024]{1,0:T(8,128)(2,1)S(1)}, f32[16,1280]{1,0:T(8,128)}) custom-call(f32[16,1280]{1,0:T(8,128)S(1)} %collective-permute-done.below_ref.above_ref.stack_ref, f32[2,1024]{1,0:T(2,128)S(1)} %get-tuple-element.21.knots_ref), custom_call_target="tpu_custom_call" | custom-call | flops 2936012800 | bytes 4194304 | tf_op jit(solution)/shard_map/project/pallas_call | solution.py:219
  13.5 0.0 copy-start
  13.5 0.0 copy-start.1
  13.5 0.1 collective-permute-start.5
  13.6 2.0 %collective-permute-start.4 = (f32[16,1024]{1,0:T(8,128)S(1)}, f32[16,1024]{1,0:T(8,128)S(1)}, u32[]{:S(2)}, u32[]{:S(2)}) collective-permute-start(f32[16,1024]{1,0:T(8,128)S(1)} %add.11.rest_0_.refs_0_), channel_id=1, source_target_pairs={{0,4},{2,6},{4,0},{6,2},{8,12},{10,14},{12,8},{14,10},{16,20},{18,... | collective-permute-start | bytes 196616 | tf_op jit(solution)/shard_map/ppermute | solution.py:427
  15.6 1.5 %collective-permute-start.3 = (f32[16,1024]{1,0:T(8,128)S(1)}, f32[16,1024]{1,0:T(8,128)S(1)}, u32[]{:S(2)}, u32[]{:S(2)}) collective-permute-start(f32[16,1024]{1,0:T(8,128)S(1)} %add.11.rest_0_.refs_0_), channel_id=1, source_target_pairs={{0,6},{2,4},{4,2},{6,0},{8,14},{10,12},{12,10},{14,8},{16,22},{18,... | collective-permute-start | bytes 196616 | tf_op jit(solution)/shard_map/ppermute | solution.py:427
  17.1 0.0 slice-done
  17.1 0.0 slice-done.1
  17.1 0.6 %split.2 = (bf16[512,2048]{1,0:T(8,128)(2,1)S(1)}, bf16[512,2048]{1,0:T(8,128)(2,1)S(1)}) custom-call(f32[1024,2048]{1,0:T(8,128)S(1)} %bitcast.1, f32[16,1024]{1,0:T(8,128)S(1)} %add.11.rest_0_.refs_0_), custom_call_target="tpu_custom_call" | custom-call | flops 62914560 | bytes 4194304 | tf_op jit(solution)/shard_map/split/pallas_call | solution.py:247
  17.7 0.0 collective-permute-done.2.west_ref
  17.7 0.0 collective-permute-done.1.east_ref
  17.8 0.0 copy-done
  17.8 0.0 copy-done.1
  17.8 1.7 %taper.5.refs_5_ = f32[16,256]{1,0:T(8,128)S(1)} custom-call(s32[8,8]{1,0:T(8,128)S(1)} %copy-done, s32[8]{0:T(128)S(1)} %copy-done.1, f32[16,1280]{1,0:T(8,128)S(1)} %get-tuple-element.22.own_ref, bf16[32,3968]{1,0:T(8,128)(2,1)S(1)} %get-tuple-element.23.values_ref, f32[2,3840]{1,0:T(2,128)S(1)} %get-tuple-element.24.coords_ref, ...), custom_call_target="tpu_custom_call" | custom-call | flops 131072000 | bytes 1048576 | tf_op jit(solution)/shard_map/taper/pallas_call | solution.py:381
  19.5 1.7 %taper.4.refs_4_ = f32[16,256]{1,0:T(8,128)S(1)} custom-call(s32[8,8]{1,0:T(8,128)S(1)} %copy-done, s32[8]{0:T(128)S(1)} %copy-done.1, f32[16,1280]{1,0:T(8,128)S(1)} %get-tuple-element.22.own_ref, bf16[32,3968]{1,0:T(8,128)(2,1)S(1)} %get-tuple-element.23.values_ref, f32[2,3840]{1,0:T(2,128)S(1)} %get-tuple-element.24.coords_ref, ...), custom_call_target="tpu_custom_call" | custom-call | flops 131072000 | bytes 1048576 | tf_op jit(solution)/shard_map/taper/pallas_call | solution.py:381
  21.2 0.0 collective-permute-done.5.refs_3_
  21.2 0.0 collective-permute-done.4.refs_2_
  21.2 0.0 collective-permute-done.3.refs_1_
  21.3 1.7 %collective-permute-start.8 = (f32[16,1024]{1,0:T(8,128)S(1)}, f32[16,1024]{1,0:T(8,128)S(1)}, u32[]{:S(2)}, u32[]{:S(2)}) collective-permute-start(f32[16,1024]{1,0:T(8,128)S(1)} %add.18.rest_0_.refs_0_), channel_id=1, source_target_pairs={{0,8},{2,10},{4,12},{6,14},{8,0},{10,2},{12,4},{14,6},{16,24},{18,... | collective-permute-start | bytes 196616 | tf_op jit(solution)/shard_map/ppermute | solution.py:427
  22.9 2.6 %collective-permute-start.7 = (f32[16,1024]{1,0:T(8,128)S(1)}, f32[16,1024]{1,0:T(8,128)S(1)}, u32[]{:S(2)}, u32[]{:S(2)}) collective-permute-start(f32[16,1024]{1,0:T(8,128)S(1)} %add.18.rest_0_.refs_0_), channel_id=1, source_target_pairs={{0,16},{2,18},{4,20},{6,22},{8,24},{10,26},{12,28},{14,30},{16,0},... | collective-permute-start | bytes 196616 | tf_op jit(solution)/shard_map/ppermute | solution.py:427
  25.5 0.2 collective-permute-start.6
  25.7 0.6 %split.3 = (bf16[512,2048]{1,0:T(8,128)(2,1)S(1)}, bf16[512,2048]{1,0:T(8,128)(2,1)S(1)}) custom-call(f32[1024,2048]{1,0:T(8,128)S(1)} %bitcast.1, f32[16,1024]{1,0:T(8,128)S(1)} %add.18.rest_0_.refs_0_), custom_call_target="tpu_custom_call" | custom-call | flops 62914560 | bytes 4194304 | tf_op jit(solution)/shard_map/split/pallas_call | solution.py:247
  26.3 1.7 %taper.7.refs_5_ = f32[16,256]{1,0:T(8,128)S(1)} custom-call(s32[8,8]{1,0:T(8,128)S(1)} %copy-done, s32[8]{0:T(128)S(1)} %copy-done.1, f32[16,1280]{1,0:T(8,128)S(1)} %get-tuple-element.22.own_ref, bf16[32,3968]{1,0:T(8,128)(2,1)S(1)} %get-tuple-element.23.values_ref, f32[2,3840]{1,0:T(2,128)S(1)} %get-tuple-element.24.coords_ref, ...), custom_call_target="tpu_custom_call" | custom-call | flops 131072000 | bytes 1048576 | tf_op jit(solution)/shard_map/taper/pallas_call | solution.py:381
  28.0 1.7 %taper.6.refs_4_ = f32[16,256]{1,0:T(8,128)S(1)} custom-call(s32[8,8]{1,0:T(8,128)S(1)} %copy-done, s32[8]{0:T(128)S(1)} %copy-done.1, f32[16,1280]{1,0:T(8,128)S(1)} %get-tuple-element.22.own_ref, bf16[32,3968]{1,0:T(8,128)(2,1)S(1)} %get-tuple-element.23.values_ref, f32[2,3840]{1,0:T(2,128)S(1)} %get-tuple-element.24.coords_ref, ...), custom_call_target="tpu_custom_call" | custom-call | flops 131072000 | bytes 1048576 | tf_op jit(solution)/shard_map/taper/pallas_call | solution.py:381
  29.7 0.0 collective-permute-done.8.refs_3_
  29.7 0.0 collective-permute-done.7.refs_2_
  29.8 1.8 %collective-permute-done.6.refs_1_ = f32[16,1024]{1,0:T(8,128)S(1)} collective-permute-done((f32[16,1024]{1,0:T(8,128)S(1)}, f32[16,1024]{1,0:T(8,128)S(1)}, u32[]{:S(2)}, u32[]{:S(2)}) %collective-permute-start.6) | collective-permute-done | bytes 65568 | tf_op jit(solution)/shard_map/ppermute | solution.py:427
  31.6 0.1 collective-permute-start.9
  31.7 1.3 %factor.2.before_ref = f32[16,1024]{1,0:T(8,128)S(1)} custom-call(f32[16,1024]{1,0:T(8,128)S(1)} %add.19.proj_ref, bf16[512,2048]{1,0:T(8,128)(2,1)S(1)} %get-tuple-element.27.refs_6_.rest_0_, bf16[512,2048]{1,0:T(8,128)(2,1)S(1)} %get-tuple-element.29.refs_6_.rest_1_, bf16[512,2048]{1,0:T(8,128)(2,1)S(1)} %get-tuple-element.28.refs_7_.rest_2_, ...), custom_call_target="tpu_custom_call" | custom-call | flops 1048576000 | bytes 4194304 | tf_op jit(solution)/shard_map/factor/pallas_call | solution.py:288
  33.0 0.0 collective-permute-done.9.proj_ref
  33.0 1.3 %factor.3.factor_ref = f32[16,1024]{1,0:T(8,128)S(1)} custom-call(f32[16,1024]{1,0:T(8,128)S(1)} %factor.2.before_ref, f32[16,1024]{1,0:T(8,128)S(1)} %collective-permute-done.9.proj_ref, bf16[512,2048]{1,0:T(8,128)(2,1)S(1)} %get-tuple-element.27.refs_6_.rest_0_, bf16[512,2048]{1,0:T(8,128)(2,1)S(1)} %get-tuple-element.29.refs_6_.rest_1_, ...), custom_call_target="tpu_custom_call" | custom-call | flops 1048576000 | bytes 4194304 | tf_op jit(solution)/shard_map/factor/pallas_call | solution.py:288
  34.3 1.3 %spread.2 = f32[16,1024]{1,0:T(8,128)S(1)} custom-call(f32[16,1024]{1,0:T(8,128)S(1)} %factor.3.factor_ref, bf16[1024,1024]{1,0:T(8,128)(2,1)S(1)} %get-tuple-element.31.high_ref, bf16[1024,1024]{1,0:T(8,128)(2,1)S(1)} %get-tuple-element.32.low_ref), custom_call_target="tpu_custom_call" | custom-call | flops 891289600 | bytes 4194304 | tf_op jit(solution)/shard_map/spread/pallas_call | solution.py:315
  35.5 0.5 %collective-permute-start.10 = (f32[16,1024]{1,0:T(8,128)S(1)}, f32[16,1024]{1,0:T(8,128)S(1)}, u32[]{:S(2)}, u32[]{:S(2)}) collective-permute-start(f32[16,1024]{1,0:T(8,128)S(1)} %spread.2), channel_id=1, source_target_pairs={{1,0},{0,1},{3,2},{2,3},{5,4},{4,5},{7,6},{6,7},{9,8},{8,9},{11,10... | collective-permute-start | bytes 196616 | tf_op jit(solution)/shard_map/ppermute | solution.py:435
  36.1 1.3 %spread.3 = f32[16,1024]{1,0:T(8,128)S(1)} custom-call(f32[16,1024]{1,0:T(8,128)S(1)} %factor.3.factor_ref, bf16[1024,1024]{1,0:T(8,128)(2,1)S(1)} %get-tuple-element.33.high_ref, bf16[1024,1024]{1,0:T(8,128)(2,1)S(1)} %get-tuple-element.34.low_ref), custom_call_target="tpu_custom_call" | custom-call | flops 891289600 | bytes 4194304 | tf_op jit(solution)/shard_map/spread/pallas_call | solution.py:315
  37.4 0.0 collective-permute-done.10
  37.4 0.7 %fusion = f32[16,1024]{1,0:T(8,128)} fusion(f32[16,1024]{1,0:T(8,128)S(1)} %spread.3, f32[16,1024]{1,0:T(8,128)S(1)} %collective-permute-done.10, f32[16,256]{1,0:T(8,128)S(1)} %taper.7.refs_5_, f32[16,256]{1,0:T(8,128)S(1)} %taper.6.refs_4_, f32[16,256]{1,0:T(8,128)S(1)} %taper.5.refs_5_, f32[16,256]{1,0:T(8,128)S(1)} %taper.4.refs_4_), kind=kLoop, calls=%fused_computation.1 | loop fusion | flops 81920 | bytes 262144 | tf_op jit(solution)/shard_map/add | solution.py:489
  (6 shorter events, 0.1 us)
Async XLA Ops:
  0.9 3.4 %collective-permute-start = (f32[16,1280]{1,0:T(8,128)S(1)}, f32[16,1280]{1,0:T(8,128)S(1)}, u32[]{:S(2)}, u32[]{:S(2)}) collective-permute-start(f32[16,1280]{1,0:T(8,128)S(1)} %get-tuple-element.20.stack_ref), channel_id=1, source_target_pairs={{1,0},{0,1},{3,2},{2,3},{5,4},{4,5},{7,6},{6,7},{9,8},{8,9},{11,10... | collective-permute-start | bytes 245768 | tf_op jit(solution)/shard_map/ppermute | solution.py:435
  1.4 15.7 %slice-start = ((s8[8388608]{0:T(1024)(128)(4,1)}), s8[4194304]{0:T(1024)(128)(4,1)S(1)}, s32[]{:S(2)}) async-start(s8[8388608]{0:T(1024)(128)(4,1)} %bitcast), calls=%async_computation | async-start | bytes 8388608
  4.3 12.8 %slice-start.1 = ((s8[8388608]{0:T(1024)(128)(4,1)}), s8[4194304]{0:T(1024)(128)(4,1)S(1)}, s32[]{:S(2)}) async-start(s8[8388608]{0:T(1024)(128)(4,1)} %bitcast), calls=%async_computation.1 | async-start | bytes 8388608
  4.3 13.3 %collective-permute-start.2 = (f32[16,1536]{1,0:T(8,128)S(1)}, f32[16,1536]{1,0:T(8,128)S(1)}, u32[]{:S(2)}, u32[]{:S(2)}) collective-permute-start(f32[16,1536]{1,0:T(8,128)S(1)} %strip.1.own_ref), channel_id=1, source_target_pairs={{2,4},{6,8},{10,12},{14,16},{18,20},{22,24},{26,28},{4,2},{8,6},{1... | collective-permute-start | bytes 294920 | tf_op jit(solution)/shard_map/ppermute | solution.py:441
  5.1 12.5 %collective-permute-start.1 = (f32[16,1536]{1,0:T(8,128)S(1)}, f32[16,1536]{1,0:T(8,128)S(1)}, u32[]{:S(2)}, u32[]{:S(2)}) collective-permute-start(f32[16,1536]{1,0:T(8,128)S(1)} %strip.1.own_ref), channel_id=1, source_target_pairs={{0,2},{4,6},{8,10},{12,14},{16,18},{20,22},{24,26},{28,30},{2,0},{... | collective-permute-start | bytes 294920 | tf_op jit(solution)/shard_map/ppermute | solution.py:441
  13.5 4.3 %copy-start = (s32[8,8]{1,0:T(8,128)S(1)}, s32[8,8]{1,0:T(8,128)}, u32[]{:S(2)}) copy-start(s32[8,8]{1,0:T(8,128)} %ids_ref.7) | copy-start | bytes 772
  13.5 4.3 %copy-start.1 = (s32[8]{0:T(128)S(1)}, s32[8]{0:T(128)}, u32[]{:S(2)}) copy-start(s32[8]{0:T(128)} %counts_ref.7) | copy-start | bytes 100
  13.5 7.7 %collective-permute-start.5 = (f32[16,1024]{1,0:T(8,128)S(1)}, f32[16,1024]{1,0:T(8,128)S(1)}, u32[]{:S(2)}, u32[]{:S(2)}) collective-permute-start(f32[16,1024]{1,0:T(8,128)S(1)} %add.11.rest_0_.refs_0_), channel_id=1, source_target_pairs={{0,2},{2,0},{4,6},{6,4},{8,10},{10,8},{12,14},{14,12},{16,18},{18,... | collective-permute-start | bytes 196616 | tf_op jit(solution)/shard_map/ppermute | solution.py:427
  13.6 7.6 %collective-permute-start.4 = (f32[16,1024]{1,0:T(8,128)S(1)}, f32[16,1024]{1,0:T(8,128)S(1)}, u32[]{:S(2)}, u32[]{:S(2)}) collective-permute-start(f32[16,1024]{1,0:T(8,128)S(1)} %add.11.rest_0_.refs_0_), channel_id=1, source_target_pairs={{0,4},{2,6},{4,0},{6,2},{8,12},{10,14},{12,8},{14,10},{16,20},{18,... | collective-permute-start | bytes 196616 | tf_op jit(solution)/shard_map/ppermute | solution.py:427
  15.6 5.6 %collective-permute-start.3 = (f32[16,1024]{1,0:T(8,128)S(1)}, f32[16,1024]{1,0:T(8,128)S(1)}, u32[]{:S(2)}, u32[]{:S(2)}) collective-permute-start(f32[16,1024]{1,0:T(8,128)S(1)} %add.11.rest_0_.refs_0_), channel_id=1, source_target_pairs={{0,6},{2,4},{4,2},{6,0},{8,14},{10,12},{12,10},{14,8},{16,22},{18,... | collective-permute-start | bytes 196616 | tf_op jit(solution)/shard_map/ppermute | solution.py:427
  21.3 8.5 %collective-permute-start.8 = (f32[16,1024]{1,0:T(8,128)S(1)}, f32[16,1024]{1,0:T(8,128)S(1)}, u32[]{:S(2)}, u32[]{:S(2)}) collective-permute-start(f32[16,1024]{1,0:T(8,128)S(1)} %add.18.rest_0_.refs_0_), channel_id=1, source_target_pairs={{0,8},{2,10},{4,12},{6,14},{8,0},{10,2},{12,4},{14,6},{16,24},{18,... | collective-permute-start | bytes 196616 | tf_op jit(solution)/shard_map/ppermute | solution.py:427
  22.9 6.8 %collective-permute-start.7 = (f32[16,1024]{1,0:T(8,128)S(1)}, f32[16,1024]{1,0:T(8,128)S(1)}, u32[]{:S(2)}, u32[]{:S(2)}) collective-permute-start(f32[16,1024]{1,0:T(8,128)S(1)} %add.18.rest_0_.refs_0_), channel_id=1, source_target_pairs={{0,16},{2,18},{4,20},{6,22},{8,24},{10,26},{12,28},{14,30},{16,0},... | collective-permute-start | bytes 196616 | tf_op jit(solution)/shard_map/ppermute | solution.py:427
  25.5 6.1 %collective-permute-start.6 = (f32[16,1024]{1,0:T(8,128)S(1)}, f32[16,1024]{1,0:T(8,128)S(1)}, u32[]{:S(2)}, u32[]{:S(2)}) collective-permute-start(f32[16,1024]{1,0:T(8,128)S(1)} %add.18.rest_0_.refs_0_), channel_id=1, source_target_pairs={{0,24},{2,26},{4,28},{6,30},{8,16},{10,18},{12,20},{14,22},{16,8},... | collective-permute-start | bytes 196616 | tf_op jit(solution)/shard_map/ppermute | solution.py:427
  31.6 1.4 %collective-permute-start.9 = (f32[16,1024]{1,0:T(8,128)S(1)}, f32[16,1024]{1,0:T(8,128)S(1)}, u32[]{:S(2)}, u32[]{:S(2)}) collective-permute-start(f32[16,1024]{1,0:T(8,128)S(1)} %add.19.proj_ref), channel_id=1, source_target_pairs={{1,0},{0,1},{3,2},{2,3},{5,4},{4,5},{7,6},{6,7},{9,8},{8,9},{11,10... | collective-permute-start | bytes 196616 | tf_op jit(solution)/shard_map/ppermute | solution.py:435
  35.5 1.8 %collective-permute-start.10 = (f32[16,1024]{1,0:T(8,128)S(1)}, f32[16,1024]{1,0:T(8,128)S(1)}, u32[]{:S(2)}, u32[]{:S(2)}) collective-permute-start(f32[16,1024]{1,0:T(8,128)S(1)} %spread.2), channel_id=1, source_target_pairs={{1,0},{0,1},{3,2},{2,3},{5,4},{4,5},{7,6},{6,7},{9,8},{8,9},{11,10... | collective-permute-start | bytes 196616 | tf_op jit(solution)/shard_map/ppermute | solution.py:435

commit v9 on v8

--- a/solution.py
+++ b/solution.py
@@ -17,8 +17,8 @@
 LOW_SCALE = 0.5
 NUGGET = 0.25
 LOG2E = math.log2(math.e)
+TAPER_RATE = LOG2E / COV_RANGE
 CELL = 0.1
-TINY = 1e-30
 TILE = 256
 LANES = 128
 HALF_GRAIN = 2.0**-24
@@ -51,13 +51,6 @@
 
 def dot_nn(left, right):
     return jnp.dot(left, right, preferred_element_type=jnp.float32)
-
-
-def distance(ax, ay, bx, by):
-    dx = ax - bx
-    dy = ay - by
-    square = dx * dx + dy * dy
-    return square * lax.rsqrt(jnp.maximum(square, TINY))
 
 
 def padded_halves(x, rows):
@@ -145,26 +138,25 @@
     )(below, own, above)
 
 
-def assemble_kernel(own_ref, east_ref, west_ref, values_ref, coords_ref):
+def assemble_kernel(grain, own_ref, east_ref, west_ref, values_ref, coords_ref):
     probes, width = own_ref.shape
     points = width - 2 * LANES
-    inverse = 1.0 / TAPER_LEN
     for turn, ref in enumerate((own_ref, east_ref, west_ref)):
         start = turn * points
-        values_ref[:, start : start + points] = stacked_halves(ref[:, :points])
+        values_ref[:, start : start + points] = stacked_halves(ref[:, :points] * (1.0 / 256.0))
         for axis in range(2):
-            rows = coordinate_rows(ref, points, axis) * inverse
+            rows = off_grid(coordinate_rows(ref, points, axis) * TAPER_RATE, grain)
             for index in range(points // LANES):
                 lanes = slice(start + index * LANES, start + (index + 1) * LANES)
                 coords_ref[axis : axis + 1, lanes] = rows[index : index + 1]
     values_ref[:, 3 * points :] = jnp.zeros((2 * probes, LANES), jnp.bfloat16)
 
 
-def assemble(strips):
+def assemble(strips, extent):
     probes, width = strips[0].shape
     near = 3 * (width - 2 * LANES)
     return pl.pallas_call(
-        assemble_kernel,
+        functools.partial(assemble_kernel, grain_of(TAPER_RATE * extent)),
         out_shape=(
             jax.ShapeDtypeStruct((2 * probes, near + LANES), jnp.bfloat16),
             jax.ShapeDtypeStruct((2, near), jnp.float32),
@@ -174,6 +166,18 @@
         compiler_params=pltpu.CompilerParams(vmem_limit_bytes=LIMIT),
         name="assemble",
     )(*strips)
+
+
+def grain_of(bound):
+    return 2.0 ** math.ceil(math.log2(1.01 * bound))
+
+
+def on_grid(x, grain):
+    return (x + grain) - grain
+
+
+def off_grid(x, grain):
+    return (x + grain) - (grain - grain * HALF_GRAIN)
 
 
 def project_kernel(scale, grain, stack_ref, knots_ref, out_ref, high_ref, low_ref, copy_ref, weights):
@@ -184,15 +188,13 @@
     copy_ref[...] = stack_ref[...]
     weights[...] = stacked_halves(stack_ref[:, :points])
     east, north = [
-        (jnp.transpose(coordinate_rows(stack_ref, points, axis) * scale) + grain) - grain for axis in range(2)
+        on_grid(jnp.transpose(coordinate_rows(stack_ref, points, axis) * scale), grain) for axis in range(2)
     ]
 
     @pl.loop(0, knots // tile)
     def _(step):
         lanes = pl.ds(pl.multiple_of(step * tile, tile), tile)
-        kx, ky = [
-            (knots_ref[axis : axis + 1, lanes] * scale + grain) - (grain - grain * HALF_GRAIN) for axis in range(2)
-        ]
+        kx, ky = [off_grid(knots_ref[axis : axis + 1, lanes] * scale, grain) for axis in range(2)]
         total = jnp.zeros((2 * probes, tile), jnp.float32)
         for start in range(0, points, wide):
             highs, lows = [], []
@@ -215,9 +217,8 @@
 
 def project(stack, knot_locs, scale, extent):
     probes, points, knots = stack.shape[0], stack.shape[1] - 2 * LANES, knot_locs.shape[1]
-    grain = 2.0 ** math.ceil(math.log2(1.01 * scale * extent))
-    return pl.pallas_call(
-        functools.partial(project_kernel, scale, grain),
+    return pl.pallas_call(
+        functools.partial(project_kernel, scale, grain_of(scale * extent)),
         out_shape=(
             jax.ShapeDtypeStruct((probes, knots), jnp.float32),
             pltpu.VMEM((points, knots), jnp.bfloat16),
@@ -324,13 +325,14 @@
     )(factor, high, low)
 
 
-def covariance(apart):
-    scaled = jnp.minimum(apart, 1.0)
-    remain = (1.0 - scaled) * (1.0 - scaled)
-    return jnp.exp2(scaled * (-LOG2E * TAPER_LEN / COV_RANGE)) * (remain * remain) * (1.0 + 4.0 * scaled)
-
-
-def taper_kernel(first, ids_ref, counts_ref, own_ref, values_ref, coords_ref, *rest):
+def covariance(square):
+    apart = square * lax.rsqrt(square)
+    remain = jnp.maximum(4.0 - apart * (4.0 / (TAPER_LEN * TAPER_RATE)), 0.0)
+    twice = remain * remain
+    return (jnp.exp2(-apart) * (twice * twice)) * (5.0 - remain)
+
+
+def taper_kernel(first, grain, ids_ref, counts_ref, own_ref, values_ref, coords_ref, *rest):
     out_ref = rest[-1]
     own_blocks, slots = ids_ref.shape
     block = LANES
@@ -341,7 +343,8 @@
     north_base = lax.axis_index("knot") * own_blocks - 1
     north_cells = lax.axis_size("knot") * own_blocks
     own_columns = [
-        jnp.transpose(coordinate_rows(own_ref, own_blocks * block, axis) * (1.0 / TAPER_LEN)) for axis in range(2)
+        on_grid(jnp.transpose(coordinate_rows(own_ref, own_blocks * block, axis) * TAPER_RATE), grain)
+        for axis in range(2)
     ]
 
     def place(group, slot):
@@ -362,7 +365,9 @@
             highs, lows, parts = [], [], []
             for slot in range(pair, min(pair + 2, slots)):
                 lanes, value_lanes = place(group, slot)
-                high, low = halves(covariance(distance(px, py, coords_ref[0:1, lanes], coords_ref[1:2, lanes])))
+                dx = px - coords_ref[0:1, lanes]
+                dy = py - coords_ref[1:2, lanes]
+                high, low = halves(covariance(dx * dx + dy * dy))
                 highs.append(high)
                 lows.append(low)
                 parts.append(values_ref[:, value_lanes])
@@ -376,10 +381,10 @@
         )
 
 
-def taper(ids, counts, own, values, coords, first, blocks, after):
+def taper(ids, counts, own, values, coords, extent, first, blocks, after):
     slots = ids.shape[1]
     return pl.pallas_call(
-        functools.partial(taper_kernel, first),
+        functools.partial(taper_kernel, first, grain_of(TAPER_RATE * extent)),
         out_shape=jax.ShapeDtypeStruct((own.shape[0], blocks * LANES), jnp.float32),
         in_specs=[SMEM, SMEM, VMEM, VMEM, VMEM] + [ANY] * len(after),
         out_specs=VMEM,
@@ -438,7 +443,9 @@
 def paired(value, axis, first):
     count = lax.axis_size(axis)
     pairs = [(i, i + 1) for i in range(first, count - 1, 2)]
-    return lax.ppermute(value, axis, pairs + [(b, a) for a, b in pairs])
+    pairs += [(b, a) for a, b in pairs]
+    taken = {a for a, b in pairs}
+    return lax.ppermute(value, axis, pairs + [(i, i) for i in range(count) if i not in taken])
 
 
 def shards(probes, locations, knot_locs, knot_precision, neighbours, counts):
@@ -458,10 +465,10 @@
     stack = parts[0][3]
 
     strip = make_strip(chunks[-1], stack, chunks[1 % groups])
-    values, coords = assemble([strip, paired(strip, "space", 0), paired(strip, "space", 1)])
+    values, coords = assemble([strip, paired(strip, "space", 0), paired(strip, "space", 1)], extent)
     projection = sum(part[0] for part in parts)
     rounds = len(butterfly_rounds(lax.axis_size("space")))
-    pieces = math.gcd(own_blocks, 2 * rounds)
+    pieces = math.gcd(own_blocks, rounds)
     per_piece = own_blocks // pieces
     row_pieces = math.gcd(knot_precision.shape[0] // LANES, rounds)
     per_split = knot_precision.shape[0] // row_pieces
@@ -472,7 +479,9 @@
         for i in range(pieces):
             if i * rounds // pieces == turn:
                 base.append(
-                    taper(neighbours, counts, stack, values, coords, i * per_piece, per_piece, [projection])
+                    taper(
+                        neighbours, counts, stack, values, coords, extent, i * per_piece, per_piece, [projection]
+                    )
                 )
                 beside.append(base[-1])
         for i in range(row_pieces):

time: 38.2 us -> 37.7 us (0.987)
  Pallas kernels: 19.9 us -> 17.9 us
  waiting for transfers between devices: 1.83 us -> 3.39 us
    pallas_call x7 -> x5, Pallas kernels: 12.6 us -> 10.6 us  [the longest x2 5.76 us: project(): pl.pallas_call(functools.partial(project_kernel, scale, grain_of(scale *...]
    ppermute x6, waiting for transfers between devices: 1.82 us -> 3.37 us  [butterfly_round(): got.append(lax.ppermute(value, (axis, other), pairs))]
  transfers between devices with their start and end apart: 11 -> 11, of which waited for: 1 -> 2; matrix products, arithmetic and copies ran while one was open for 0% -> 0% of each run, Pallas kernels for 43% -> 38%
where the time goes in v9:
time: 37.7 us; the launch traced here: 37.6 us
  Pallas kernels  17.9 us (47%)
  starting transfers between devices  15.4 us (41%)
  waiting for transfers between devices  3.39 us (9%)
  other arithmetic  0.7 us (2%)
    ppermute x6, starting transfers between devices, butterfly_round(): got.append(lax.ppermute(value, (axis, other), pairs))  8.01 us
    ppermute x2, starting transfers between devices, paired(): lax.ppermute(value, axis, pairs + [(i, i) for i in range(count) if i not...  6.24 us
    pallas_call x2, Pallas kernels, project(): pl.pallas_call(functools.partial(project_kernel, scale, grain_of(scale *...  5.76 us
    pallas_call x2, Pallas kernels, taper(): pl.pallas_call(functools.partial(taper_kernel, first, grain_of(TAPER_RATE...  4.81 us
    ppermute x6, waiting for transfers between devices, butterfly_round(): got.append(lax.ppermute(value, (axis, other), pairs))  3.37 us
    pallas_call x2, Pallas kernels, factored(): pl.pallas_call(kernel, out_shape=jax.ShapeDtypeStruct((probes, rows), jnp...  2.6 us
    pallas_call x2, Pallas kernels, spread(): pl.pallas_call(functools.partial(spread_kernel, scale), out_shape=jax.Sha...  2.56 us
    pallas_call x2, Pallas kernels, split_rows(): pl.pallas_call(functools.partial(split_kernel, first), out_shape=(pltpu.V...  1.18 us
  transfers between devices with their start and end apart: 11, of which 2 were waited for; matrix products, arithmetic and copies ran while one was open for 0% of the time, Pallas kernels for 38%

profile of v9, /device:TPU:0, one launch (start us, length us, event | category | flops | bytes accessed | tf_op | source)
XLA Modules:
  0.0 37.6 jit_solution(14192856329889301806)
XLA Ops:
  0.0 0.9 %prepare.1 = (f32[16,1280]{1,0:T(8,128)S(1)}, f32[2,1024]{1,0:T(2,128)S(1)}) custom-call(f32[16,1024]{1,0:T(8,128)} %probes_ref.1, f32[2,1024]{1,0:T(2,128)} %locations_ref.1, f32[2,1024]{1,0:T(2,128)} %knots_ref.1), custom_call_target="tpu_custom_call" | custom-call | tf_op jit(solution)/shard_map/prepare/pallas_call | solution.py:100
  0.9 0.5 %collective-permute-start = (f32[16,1280]{1,0:T(8,128)S(1)}, f32[16,1280]{1,0:T(8,128)S(1)}, u32[]{:S(2)}, u32[]{:S(2)}) collective-permute-start(f32[16,1280]{1,0:T(8,128)S(1)} %get-tuple-element.20.stack_ref), channel_id=1, source_target_pairs={{1,0},{0,1},{3,2},{2,3},{5,4},{4,5},{7,6},{6,7},{9,8},{8,9},{11,10... | collective-permute-start | bytes 245768 | tf_op jit(solution)/shard_map/ppermute | solution.py:440
  1.4 0.0 slice-start
  1.4 2.9 %project.2 = (f32[16,1024]{1,0:T(8,128)S(1)}, bf16[1024,1024]{1,0:T(8,128)(2,1)S(1)}, bf16[1024,1024]{1,0:T(8,128)(2,1)S(1)}, f32[16,1280]{1,0:T(8,128)S(1)}) custom-call(f32[16,1280]{1,0:T(8,128)S(1)} %get-tuple-element.20.stack_ref, f32[2,1024]{1,0:T(2,128)S(1)} %get-tuple-element.21.knots_ref), custom_call_target="tpu_custom_call" | custom-call | flops 2936012800 | bytes 4194304 | tf_op jit(solution)/shard_map/project/pallas_call | solution.py:220
  4.3 0.0 collective-permute-done.below_ref.above_ref.stack_ref
  4.3 0.0 slice-start.1
  4.3 0.8 %collective-permute-start.2 = (f32[16,1536]{1,0:T(8,128)S(1)}, f32[16,1536]{1,0:T(8,128)S(1)}, u32[]{:S(2)}, u32[]{:S(2)}) collective-permute-start(f32[16,1536]{1,0:T(8,128)S(1)} %strip.1.own_ref), channel_id=1, source_target_pairs={{2,4},{6,8},{10,12},{14,16},{18,20},{22,24},{26,28},{4,2},{8,6},{1... | collective-permute-start | bytes 294920 | tf_op jit(solution)/shard_map/ppermute | solution.py:448
  5.1 5.4 %collective-permute-start.1 = (f32[16,1536]{1,0:T(8,128)S(1)}, f32[16,1536]{1,0:T(8,128)S(1)}, u32[]{:S(2)}, u32[]{:S(2)}) collective-permute-start(f32[16,1536]{1,0:T(8,128)S(1)} %strip.1.own_ref), channel_id=1, source_target_pairs={{0,2},{4,6},{8,10},{12,14},{16,18},{20,22},{24,26},{28,30},{2,0},{... | collective-permute-start | bytes 294920 | tf_op jit(solution)/shard_map/ppermute | solution.py:448
  10.6 2.9 %project.3 = (f32[16,1024]{1,0:T(8,128)S(1)}, bf16[1024,1024]{1,0:T(8,128)(2,1)S(1)}, bf16[1024,1024]{1,0:T(8,128)(2,1)S(1)}, f32[16,1280]{1,0:T(8,128)}) custom-call(f32[16,1280]{1,0:T(8,128)S(1)} %collective-permute-done.below_ref.above_ref.stack_ref, f32[2,1024]{1,0:T(2,128)S(1)} %get-tuple-element.21.knots_ref), custom_call_target="tpu_custom_call" | custom-call | flops 2936012800 | bytes 4194304 | tf_op jit(solution)/shard_map/project/pallas_call | solution.py:220
  13.5 0.0 copy-start
  13.5 0.0 copy-start.1
  13.5 0.1 collective-permute-start.5
  13.6 2.0 %collective-permute-start.4 = (f32[16,1024]{1,0:T(8,128)S(1)}, f32[16,1024]{1,0:T(8,128)S(1)}, u32[]{:S(2)}, u32[]{:S(2)}) collective-permute-start(f32[16,1024]{1,0:T(8,128)S(1)} %add.11.rest_0_.refs_0_), channel_id=1, source_target_pairs={{0,4},{2,6},{4,0},{6,2},{8,12},{10,14},{12,8},{14,10},{16,20},{18,... | collective-permute-start | bytes 196616 | tf_op jit(solution)/shard_map/ppermute | solution.py:432
  15.6 1.5 %collective-permute-start.3 = (f32[16,1024]{1,0:T(8,128)S(1)}, f32[16,1024]{1,0:T(8,128)S(1)}, u32[]{:S(2)}, u32[]{:S(2)}) collective-permute-start(f32[16,1024]{1,0:T(8,128)S(1)} %add.11.rest_0_.refs_0_), channel_id=1, source_target_pairs={{0,6},{2,4},{4,2},{6,0},{8,14},{10,12},{12,10},{14,8},{16,22},{18,... | collective-permute-start | bytes 196616 | tf_op jit(solution)/shard_map/ppermute | solution.py:432
  17.1 0.0 slice-done
  17.1 0.0 slice-done.1
  17.1 0.6 %split.2 = (bf16[512,2048]{1,0:T(8,128)(2,1)S(1)}, bf16[512,2048]{1,0:T(8,128)(2,1)S(1)}) custom-call(f32[1024,2048]{1,0:T(8,128)S(1)} %bitcast.1, f32[16,1024]{1,0:T(8,128)S(1)} %add.11.rest_0_.refs_0_), custom_call_target="tpu_custom_call" | custom-call | flops 62914560 | bytes 4194304 | tf_op jit(solution)/shard_map/split/pallas_call | solution.py:248
  17.7 0.0 collective-permute-done.2.west_ref
  17.7 0.0 collective-permute-done.1.east_ref
  17.7 0.1 assemble.1
  17.8 0.0 copy-done
  17.8 0.0 copy-done.1
  17.8 2.4 %taper.2.refs_4_ = f32[16,512]{1,0:T(8,128)S(1)} custom-call(s32[8,8]{1,0:T(8,128)S(1)} %copy-done, s32[8]{0:T(128)S(1)} %copy-done.1, f32[16,1280]{1,0:T(8,128)S(1)} %get-tuple-element.22.own_ref, bf16[32,3968]{1,0:T(8,128)(2,1)S(1)} %get-tuple-element.23.values_ref, f32[2,3840]{1,0:T(2,128)S(1)} %get-tuple-element.24.coords_ref, ...), custom_call_target="tpu_custom_call" | custom-call | flops 262144000 | bytes 2097152 | tf_op jit(solution)/shard_map/taper/pallas_call | solution.py:386
  20.2 0.0 collective-permute-done.5.refs_3_
  20.2 0.0 collective-permute-done.4.refs_2_
  20.2 0.5 %collective-permute-done.3.refs_1_ = f32[16,1024]{1,0:T(8,128)S(1)} collective-permute-done((f32[16,1024]{1,0:T(8,128)S(1)}, f32[16,1024]{1,0:T(8,128)S(1)}, u32[]{:S(2)}, u32[]{:S(2)}) %collective-permute-start.3) | collective-permute-done | bytes 65568 | tf_op jit(solution)/shard_map/ppermute | solution.py:432
  20.8 1.6 %collective-permute-start.8 = (f32[16,1024]{1,0:T(8,128)S(1)}, f32[16,1024]{1,0:T(8,128)S(1)}, u32[]{:S(2)}, u32[]{:S(2)}) collective-permute-start(f32[16,1024]{1,0:T(8,128)S(1)} %add.18.rest_0_.refs_0_), channel_id=1, source_target_pairs={{0,8},{2,10},{4,12},{6,14},{8,0},{10,2},{12,4},{14,6},{16,24},{18,... | collective-permute-start | bytes 196616 | tf_op jit(solution)/shard_map/ppermute | solution.py:432
  22.4 2.6 %collective-permute-start.7 = (f32[16,1024]{1,0:T(8,128)S(1)}, f32[16,1024]{1,0:T(8,128)S(1)}, u32[]{:S(2)}, u32[]{:S(2)}) collective-permute-start(f32[16,1024]{1,0:T(8,128)S(1)} %add.18.rest_0_.refs_0_), channel_id=1, source_target_pairs={{0,16},{2,18},{4,20},{6,22},{8,24},{10,26},{12,28},{14,30},{16,0},... | collective-permute-start | bytes 196616 | tf_op jit(solution)/shard_map/ppermute | solution.py:432
  25.0 0.2 collective-permute-start.6
  25.2 0.6 %split.3 = (bf16[512,2048]{1,0:T(8,128)(2,1)S(1)}, bf16[512,2048]{1,0:T(8,128)(2,1)S(1)}) custom-call(f32[1024,2048]{1,0:T(8,128)S(1)} %bitcast.1, f32[16,1024]{1,0:T(8,128)S(1)} %add.18.rest_0_.refs_0_), custom_call_target="tpu_custom_call" | custom-call | flops 62914560 | bytes 4194304 | tf_op jit(solution)/shard_map/split/pallas_call | solution.py:248
  25.8 2.4 %taper.3.refs_4_ = f32[16,512]{1,0:T(8,128)S(1)} custom-call(s32[8,8]{1,0:T(8,128)S(1)} %copy-done, s32[8]{0:T(128)S(1)} %copy-done.1, f32[16,1280]{1,0:T(8,128)S(1)} %get-tuple-element.22.own_ref, bf16[32,3968]{1,0:T(8,128)(2,1)S(1)} %get-tuple-element.23.values_ref, f32[2,3840]{1,0:T(2,128)S(1)} %get-tuple-element.24.coords_ref, ...), custom_call_target="tpu_custom_call" | custom-call | flops 262144000 | bytes 2097152 | tf_op jit(solution)/shard_map/taper/pallas_call | solution.py:386
  28.2 0.0 collective-permute-done.8.refs_3_
  28.2 0.0 collective-permute-done.7.refs_2_
  28.3 2.8 %collective-permute-done.6.refs_1_ = f32[16,1024]{1,0:T(8,128)S(1)} collective-permute-done((f32[16,1024]{1,0:T(8,128)S(1)}, f32[16,1024]{1,0:T(8,128)S(1)}, u32[]{:S(2)}, u32[]{:S(2)}) %collective-permute-start.6) | collective-permute-done | bytes 65568 | tf_op jit(solution)/shard_map/ppermute | solution.py:432
  31.1 0.1 collective-permute-start.9
  31.2 1.3 %factor.2.before_ref = f32[16,1024]{1,0:T(8,128)S(1)} custom-call(f32[16,1024]{1,0:T(8,128)S(1)} %add.19.proj_ref, bf16[512,2048]{1,0:T(8,128)(2,1)S(1)} %get-tuple-element.27.refs_5_.rest_0_, bf16[512,2048]{1,0:T(8,128)(2,1)S(1)} %get-tuple-element.29.refs_5_.rest_1_, bf16[512,2048]{1,0:T(8,128)(2,1)S(1)} %get-tuple-element.28.refs_6_.rest_2_, ...), custom_call_target="tpu_custom_call" | custom-call | flops 1048576000 | bytes 4194304 | tf_op jit(solution)/shard_map/factor/pallas_call | solution.py:289
  32.5 0.0 collective-permute-done.9.proj_ref
  32.5 1.3 %factor.3.factor_ref = f32[16,1024]{1,0:T(8,128)S(1)} custom-call(f32[16,1024]{1,0:T(8,128)S(1)} %factor.2.before_ref, f32[16,1024]{1,0:T(8,128)S(1)} %collective-permute-done.9.proj_ref, bf16[512,2048]{1,0:T(8,128)(2,1)S(1)} %get-tuple-element.27.refs_5_.rest_0_, bf16[512,2048]{1,0:T(8,128)(2,1)S(1)} %get-tuple-element.29.refs_5_.rest_1_, ...), custom_call_target="tpu_custom_call" | custom-call | flops 1048576000 | bytes 4194304 | tf_op jit(solution)/shard_map/factor/pallas_call | solution.py:289
  33.8 1.3 %spread.2 = f32[16,1024]{1,0:T(8,128)S(1)} custom-call(f32[16,1024]{1,0:T(8,128)S(1)} %factor.3.factor_ref, bf16[1024,1024]{1,0:T(8,128)(2,1)S(1)} %get-tuple-element.31.high_ref, bf16[1024,1024]{1,0:T(8,128)(2,1)S(1)} %get-tuple-element.32.low_ref), custom_call_target="tpu_custom_call" | custom-call | flops 891289600 | bytes 4194304 | tf_op jit(solution)/shard_map/spread/pallas_call | solution.py:316
  35.1 0.5 %collective-permute-start.10 = (f32[16,1024]{1,0:T(8,128)S(1)}, f32[16,1024]{1,0:T(8,128)S(1)}, u32[]{:S(2)}, u32[]{:S(2)}) collective-permute-start(f32[16,1024]{1,0:T(8,128)S(1)} %spread.2), channel_id=1, source_target_pairs={{1,0},{0,1},{3,2},{2,3},{5,4},{4,5},{7,6},{6,7},{9,8},{8,9},{11,10... | collective-permute-start | bytes 196616 | tf_op jit(solution)/shard_map/ppermute | solution.py:440
  35.6 1.3 %spread.3 = f32[16,1024]{1,0:T(8,128)S(1)} custom-call(f32[16,1024]{1,0:T(8,128)S(1)} %factor.3.factor_ref, bf16[1024,1024]{1,0:T(8,128)(2,1)S(1)} %get-tuple-element.33.high_ref, bf16[1024,1024]{1,0:T(8,128)(2,1)S(1)} %get-tuple-element.34.low_ref), custom_call_target="tpu_custom_call" | custom-call | flops 891289600 | bytes 4194304 | tf_op jit(solution)/shard_map/spread/pallas_call | solution.py:316
  36.9 0.0 collective-permute-done.10
  36.9 0.7 %fusion = f32[16,1024]{1,0:T(8,128)} fusion(f32[16,1024]{1,0:T(8,128)S(1)} %spread.3, f32[16,1024]{1,0:T(8,128)S(1)} %collective-permute-done.10, f32[16,512]{1,0:T(8,128)S(1)} %taper.3.refs_4_, f32[16,512]{1,0:T(8,128)S(1)} %taper.2.refs_4_), kind=kLoop, calls=%fused_computation.1 | loop fusion | flops 49152 | bytes 262144 | tf_op jit(solution)/shard_map/add | solution.py:498
  (5 shorter events, 0.1 us)
Async XLA Ops:
  0.9 3.4 %collective-permute-start = (f32[16,1280]{1,0:T(8,128)S(1)}, f32[16,1280]{1,0:T(8,128)S(1)}, u32[]{:S(2)}, u32[]{:S(2)}) collective-permute-start(f32[16,1280]{1,0:T(8,128)S(1)} %get-tuple-element.20.stack_ref), channel_id=1, source_target_pairs={{1,0},{0,1},{3,2},{2,3},{5,4},{4,5},{7,6},{6,7},{9,8},{8,9},{11,10... | collective-permute-start | bytes 245768 | tf_op jit(solution)/shard_map/ppermute | solution.py:440
  1.4 15.7 %slice-start = ((s8[8388608]{0:T(1024)(128)(4,1)}), s8[4194304]{0:T(1024)(128)(4,1)S(1)}, s32[]{:S(2)}) async-start(s8[8388608]{0:T(1024)(128)(4,1)} %bitcast), calls=%async_computation | async-start | bytes 8388608
  4.3 12.8 %slice-start.1 = ((s8[8388608]{0:T(1024)(128)(4,1)}), s8[4194304]{0:T(1024)(128)(4,1)S(1)}, s32[]{:S(2)}) async-start(s8[8388608]{0:T(1024)(128)(4,1)} %bitcast), calls=%async_computation.1 | async-start | bytes 8388608
  4.3 13.3 %collective-permute-start.2 = (f32[16,1536]{1,0:T(8,128)S(1)}, f32[16,1536]{1,0:T(8,128)S(1)}, u32[]{:S(2)}, u32[]{:S(2)}) collective-permute-start(f32[16,1536]{1,0:T(8,128)S(1)} %strip.1.own_ref), channel_id=1, source_target_pairs={{2,4},{6,8},{10,12},{14,16},{18,20},{22,24},{26,28},{4,2},{8,6},{1... | collective-permute-start | bytes 294920 | tf_op jit(solution)/shard_map/ppermute | solution.py:448
  5.1 12.5 %collective-permute-start.1 = (f32[16,1536]{1,0:T(8,128)S(1)}, f32[16,1536]{1,0:T(8,128)S(1)}, u32[]{:S(2)}, u32[]{:S(2)}) collective-permute-start(f32[16,1536]{1,0:T(8,128)S(1)} %strip.1.own_ref), channel_id=1, source_target_pairs={{0,2},{4,6},{8,10},{12,14},{16,18},{20,22},{24,26},{28,30},{2,0},{... | collective-permute-start | bytes 294920 | tf_op jit(solution)/shard_map/ppermute | solution.py:448
  13.5 4.3 %copy-start = (s32[8,8]{1,0:T(8,128)S(1)}, s32[8,8]{1,0:T(8,128)}, u32[]{:S(2)}) copy-start(s32[8,8]{1,0:T(8,128)} %ids_ref.3) | copy-start | bytes 772
  13.5 4.3 %copy-start.1 = (s32[8]{0:T(128)S(1)}, s32[8]{0:T(128)}, u32[]{:S(2)}) copy-start(s32[8]{0:T(128)} %counts_ref.3) | copy-start | bytes 100
  13.5 6.7 %collective-permute-start.5 = (f32[16,1024]{1,0:T(8,128)S(1)}, f32[16,1024]{1,0:T(8,128)S(1)}, u32[]{:S(2)}, u32[]{:S(2)}) collective-permute-start(f32[16,1024]{1,0:T(8,128)S(1)} %add.11.rest_0_.refs_0_), channel_id=1, source_target_pairs={{0,2},{2,0},{4,6},{6,4},{8,10},{10,8},{12,14},{14,12},{16,18},{18,... | collective-permute-start | bytes 196616 | tf_op jit(solution)/shard_map/ppermute | solution.py:432
  13.6 6.6 %collective-permute-start.4 = (f32[16,1024]{1,0:T(8,128)S(1)}, f32[16,1024]{1,0:T(8,128)S(1)}, u32[]{:S(2)}, u32[]{:S(2)}) collective-permute-start(f32[16,1024]{1,0:T(8,128)S(1)} %add.11.rest_0_.refs_0_), channel_id=1, source_target_pairs={{0,4},{2,6},{4,0},{6,2},{8,12},{10,14},{12,8},{14,10},{16,20},{18,... | collective-permute-start | bytes 196616 | tf_op jit(solution)/shard_map/ppermute | solution.py:432
  15.6 5.2 %collective-permute-start.3 = (f32[16,1024]{1,0:T(8,128)S(1)}, f32[16,1024]{1,0:T(8,128)S(1)}, u32[]{:S(2)}, u32[]{:S(2)}) collective-permute-start(f32[16,1024]{1,0:T(8,128)S(1)} %add.11.rest_0_.refs_0_), channel_id=1, source_target_pairs={{0,6},{2,4},{4,2},{6,0},{8,14},{10,12},{12,10},{14,8},{16,22},{18,... | collective-permute-start | bytes 196616 | tf_op jit(solution)/shard_map/ppermute | solution.py:432
  20.8 7.5 %collective-permute-start.8 = (f32[16,1024]{1,0:T(8,128)S(1)}, f32[16,1024]{1,0:T(8,128)S(1)}, u32[]{:S(2)}, u32[]{:S(2)}) collective-permute-start(f32[16,1024]{1,0:T(8,128)S(1)} %add.18.rest_0_.refs_0_), channel_id=1, source_target_pairs={{0,8},{2,10},{4,12},{6,14},{8,0},{10,2},{12,4},{14,6},{16,24},{18,... | collective-permute-start | bytes 196616 | tf_op jit(solution)/shard_map/ppermute | solution.py:432
  22.4 5.9 %collective-permute-start.7 = (f32[16,1024]{1,0:T(8,128)S(1)}, f32[16,1024]{1,0:T(8,128)S(1)}, u32[]{:S(2)}, u32[]{:S(2)}) collective-permute-start(f32[16,1024]{1,0:T(8,128)S(1)} %add.18.rest_0_.refs_0_), channel_id=1, source_target_pairs={{0,16},{2,18},{4,20},{6,22},{8,24},{10,26},{12,28},{14,30},{16,0},... | collective-permute-start | bytes 196616 | tf_op jit(solution)/shard_map/ppermute | solution.py:432
  25.0 6.1 %collective-permute-start.6 = (f32[16,1024]{1,0:T(8,128)S(1)}, f32[16,1024]{1,0:T(8,128)S(1)}, u32[]{:S(2)}, u32[]{:S(2)}) collective-permute-start(f32[16,1024]{1,0:T(8,128)S(1)} %add.18.rest_0_.refs_0_), channel_id=1, source_target_pairs={{0,24},{2,26},{4,28},{6,30},{8,16},{10,18},{12,20},{14,22},{16,8},... | collective-permute-start | bytes 196616 | tf_op jit(solution)/shard_map/ppermute | solution.py:432
  31.1 1.4 %collective-permute-start.9 = (f32[16,1024]{1,0:T(8,128)S(1)}, f32[16,1024]{1,0:T(8,128)S(1)}, u32[]{:S(2)}, u32[]{:S(2)}) collective-permute-start(f32[16,1024]{1,0:T(8,128)S(1)} %add.19.proj_ref), channel_id=1, source_target_pairs={{1,0},{0,1},{3,2},{2,3},{5,4},{4,5},{7,6},{6,7},{9,8},{8,9},{11,10... | collective-permute-start | bytes 196616 | tf_op jit(solution)/shard_map/ppermute | solution.py:440
  35.1 1.8 %collective-permute-start.10 = (f32[16,1024]{1,0:T(8,128)S(1)}, f32[16,1024]{1,0:T(8,128)S(1)}, u32[]{:S(2)}, u32[]{:S(2)}) collective-permute-start(f32[16,1024]{1,0:T(8,128)S(1)} %spread.2), channel_id=1, source_target_pairs={{1,0},{0,1},{3,2},{2,3},{5,4},{4,5},{7,6},{6,7},{9,8},{8,9},{11,10... | collective-permute-start | bytes 196616 | tf_op jit(solution)/shard_map/ppermute | solution.py:440

commit v10 on v9

--- a/solution.py
+++ b/solution.py
@@ -442,10 +442,8 @@
 
 def paired(value, axis, first):
     count = lax.axis_size(axis)
-    pairs = [(i, i + 1) for i in range(first, count - 1, 2)]
-    pairs += [(b, a) for a, b in pairs]
-    taken = {a for a, b in pairs}
-    return lax.ppermute(value, axis, pairs + [(i, i) for i in range(count) if i not in taken])
+    pairs = [((first + i) % count, (first + i + 1) % count) for i in range(0, count - 1, 2)]
+    return lax.ppermute(value, axis, pairs + [(b, a) for a, b in pairs])
 
 
 def shards(probes, locations, knot_locs, knot_precision, neighbours, counts):

time: 37.7 us -> 35.5 us (0.942)
  waiting for transfers between devices: 3.39 us -> 0.8 us
  starting transfers between devices: 15.4 us -> 15.8 us
    ppermute x6, waiting for transfers between devices: 3.37 us -> 0.79 us  [butterfly_round(): got.append(lax.ppermute(value, (axis, other), pairs))]
  transfers between devices with their start and end apart: 11 -> 11, of which waited for: 2 -> 2; matrix products, arithmetic and copies ran while one was open for 0% -> 0% of each run, Pallas kernels for 38% -> 41%
where the time goes in v10:
time: 35.5 us; the launch traced here: 35.4 us
  Pallas kernels  17.9 us (50%)
  starting transfers between devices  15.8 us (45%)
  waiting for transfers between devices  0.8 us (2%)
  other arithmetic  0.7 us (2%)
    ppermute x6, starting transfers between devices, butterfly_round(): got.append(lax.ppermute(value, (axis, other), pairs))  8.07 us
    ppermute x2, starting transfers between devices, paired(): return lax.ppermute(value, axis, pairs + [(b, a) for a, b in pairs])  6.57 us
    pallas_call x2, Pallas kernels, project(): pl.pallas_call(functools.partial(project_kernel, scale, grain_of(scale *...  5.76 us
    pallas_call x2, Pallas kernels, taper(): pl.pallas_call(functools.partial(taper_kernel, first, grain_of(TAPER_RATE...  4.8 us
    pallas_call x2, Pallas kernels, factored(): pl.pallas_call(kernel, out_shape=jax.ShapeDtypeStruct((probes, rows), jnp...  2.6 us
    pallas_call x2, Pallas kernels, spread(): pl.pallas_call(functools.partial(spread_kernel, scale), out_shape=jax.Sha...  2.56 us
    pallas_call x2, Pallas kernels, split_rows(): pl.pallas_call(functools.partial(split_kernel, first), out_shape=(pltpu.V...  1.18 us
    ppermute x3, starting transfers between devices, shifted(): lax.ppermute(value, axis, [((i + step) % count, i) for i in range(count)])  1.13 us
  transfers between devices with their start and end apart: 11, of which 2 were waited for; matrix products, arithmetic and copies ran while one was open for 0% of the time, Pallas kernels for 41%

profile of v10, /device:TPU:0, one launch (start us, length us, event | category | flops | bytes accessed | tf_op | source)
XLA Modules:
  0.0 35.4 jit_solution(8526370571443802713)
XLA Ops:
  0.0 0.9 %prepare.1 = (f32[16,1280]{1,0:T(8,128)S(1)}, f32[2,1024]{1,0:T(2,128)S(1)}) custom-call(f32[16,1024]{1,0:T(8,128)} %probes_ref.1, f32[2,1024]{1,0:T(2,128)} %locations_ref.1, f32[2,1024]{1,0:T(2,128)} %knots_ref.1), custom_call_target="tpu_custom_call" | custom-call | tf_op jit(solution)/shard_map/prepare/pallas_call | solution.py:100
  0.9 0.5 %collective-permute-start = (f32[16,1280]{1,0:T(8,128)S(1)}, f32[16,1280]{1,0:T(8,128)S(1)}, u32[]{:S(2)}, u32[]{:S(2)}) collective-permute-start(f32[16,1280]{1,0:T(8,128)S(1)} %get-tuple-element.20.stack_ref), channel_id=1, source_target_pairs={{1,0},{0,1},{3,2},{2,3},{5,4},{4,5},{7,6},{6,7},{9,8},{8,9},{11,10... | collective-permute-start | bytes 245768 | tf_op jit(solution)/shard_map/ppermute | solution.py:440
  1.4 0.0 slice-start
  1.4 2.9 %project.2 = (f32[16,1024]{1,0:T(8,128)S(1)}, bf16[1024,1024]{1,0:T(8,128)(2,1)S(1)}, bf16[1024,1024]{1,0:T(8,128)(2,1)S(1)}, f32[16,1280]{1,0:T(8,128)S(1)}) custom-call(f32[16,1280]{1,0:T(8,128)S(1)} %get-tuple-element.20.stack_ref, f32[2,1024]{1,0:T(2,128)S(1)} %get-tuple-element.21.knots_ref), custom_call_target="tpu_custom_call" | custom-call | flops 2936012800 | bytes 4194304 | tf_op jit(solution)/shard_map/project/pallas_call | solution.py:220
  4.3 0.0 collective-permute-done.below_ref.above_ref.stack_ref
  4.3 0.0 slice-start.1
  4.3 6.6 %collective-permute-start.2 = (f32[16,1536]{1,0:T(8,128)S(1)}, f32[16,1536]{1,0:T(8,128)S(1)}, u32[]{:S(2)}, u32[]{:S(2)}) collective-permute-start(f32[16,1536]{1,0:T(8,128)S(1)} %strip.1.own_ref), channel_id=1, source_target_pairs={{2,4},{6,8},{10,12},{14,16},{18,20},{22,24},{26,28},{30,0},{4,2},{... | collective-permute-start | bytes 294920 | tf_op jit(solution)/shard_map/ppermute | solution.py:446
  10.9 0.0 collective-permute-start.1
  10.9 2.9 %project.3 = (f32[16,1024]{1,0:T(8,128)S(1)}, bf16[1024,1024]{1,0:T(8,128)(2,1)S(1)}, bf16[1024,1024]{1,0:T(8,128)(2,1)S(1)}, f32[16,1280]{1,0:T(8,128)}) custom-call(f32[16,1280]{1,0:T(8,128)S(1)} %collective-permute-done.below_ref.above_ref.stack_ref, f32[2,1024]{1,0:T(2,128)S(1)} %get-tuple-element.21.knots_ref), custom_call_target="tpu_custom_call" | custom-call | flops 2936012800 | bytes 4194304 | tf_op jit(solution)/shard_map/project/pallas_call | solution.py:220
  13.8 0.0 copy-start
  13.8 0.0 copy-start.1
  13.8 2.1 %collective-permute-start.5 = (f32[16,1024]{1,0:T(8,128)S(1)}, f32[16,1024]{1,0:T(8,128)S(1)}, u32[]{:S(2)}, u32[]{:S(2)}) collective-permute-start(f32[16,1024]{1,0:T(8,128)S(1)} %add.11.rest_0_.refs_0_), channel_id=1, source_target_pairs={{0,2},{2,0},{4,6},{6,4},{8,10},{10,8},{12,14},{14,12},{16,18},{18,... | collective-permute-start | bytes 196616 | tf_op jit(solution)/shard_map/ppermute | solution.py:432
  15.9 0.0 collective-permute-start.4
  15.9 1.5 %collective-permute-start.3 = (f32[16,1024]{1,0:T(8,128)S(1)}, f32[16,1024]{1,0:T(8,128)S(1)}, u32[]{:S(2)}, u32[]{:S(2)}) collective-permute-start(f32[16,1024]{1,0:T(8,128)S(1)} %add.11.rest_0_.refs_0_), channel_id=1, source_target_pairs={{0,6},{2,4},{4,2},{6,0},{8,14},{10,12},{12,10},{14,8},{16,22},{18,... | collective-permute-start | bytes 196616 | tf_op jit(solution)/shard_map/ppermute | solution.py:432
  17.5 0.0 slice-done
  17.5 0.0 slice-done.1
  17.5 0.6 %split.2 = (bf16[512,2048]{1,0:T(8,128)(2,1)S(1)}, bf16[512,2048]{1,0:T(8,128)(2,1)S(1)}) custom-call(f32[1024,2048]{1,0:T(8,128)S(1)} %bitcast.1, f32[16,1024]{1,0:T(8,128)S(1)} %add.11.rest_0_.refs_0_), custom_call_target="tpu_custom_call" | custom-call | flops 62914560 | bytes 4194304 | tf_op jit(solution)/shard_map/split/pallas_call | solution.py:248
  18.1 0.0 collective-permute-done.2.west_ref
  18.1 0.0 collective-permute-done.1.east_ref
  18.1 0.1 assemble.1
  18.2 0.0 copy-done
  18.2 0.0 copy-done.1
  18.2 2.4 %taper.2.refs_4_ = f32[16,512]{1,0:T(8,128)S(1)} custom-call(s32[8,8]{1,0:T(8,128)S(1)} %copy-done, s32[8]{0:T(128)S(1)} %copy-done.1, f32[16,1280]{1,0:T(8,128)S(1)} %get-tuple-element.22.own_ref, bf16[32,3968]{1,0:T(8,128)(2,1)S(1)} %get-tuple-element.23.values_ref, f32[2,3840]{1,0:T(2,128)S(1)} %get-tuple-element.24.coords_ref, ...), custom_call_target="tpu_custom_call" | custom-call | flops 262144000 | bytes 2097152 | tf_op jit(solution)/shard_map/taper/pallas_call | solution.py:386
  20.6 0.0 collective-permute-done.5.refs_3_
  20.6 0.0 collective-permute-done.4.refs_2_
  20.6 0.5 %collective-permute-done.3.refs_1_ = f32[16,1024]{1,0:T(8,128)S(1)} collective-permute-done((f32[16,1024]{1,0:T(8,128)S(1)}, f32[16,1024]{1,0:T(8,128)S(1)}, u32[]{:S(2)}, u32[]{:S(2)}) %collective-permute-start.3) | collective-permute-done | bytes 65568 | tf_op jit(solution)/shard_map/ppermute | solution.py:432
  21.1 0.1 collective-permute-start.8
  21.2 1.6 %collective-permute-start.7 = (f32[16,1024]{1,0:T(8,128)S(1)}, f32[16,1024]{1,0:T(8,128)S(1)}, u32[]{:S(2)}, u32[]{:S(2)}) collective-permute-start(f32[16,1024]{1,0:T(8,128)S(1)} %add.18.rest_0_.refs_0_), channel_id=1, source_target_pairs={{0,16},{2,18},{4,20},{6,22},{8,24},{10,26},{12,28},{14,30},{16,0},... | collective-permute-start | bytes 196616 | tf_op jit(solution)/shard_map/ppermute | solution.py:432
  22.8 2.8 %collective-permute-start.6 = (f32[16,1024]{1,0:T(8,128)S(1)}, f32[16,1024]{1,0:T(8,128)S(1)}, u32[]{:S(2)}, u32[]{:S(2)}) collective-permute-start(f32[16,1024]{1,0:T(8,128)S(1)} %add.18.rest_0_.refs_0_), channel_id=1, source_target_pairs={{0,24},{2,26},{4,28},{6,30},{8,16},{10,18},{12,20},{14,22},{16,8},... | collective-permute-start | bytes 196616 | tf_op jit(solution)/shard_map/ppermute | solution.py:432
  25.6 0.6 %split.3 = (bf16[512,2048]{1,0:T(8,128)(2,1)S(1)}, bf16[512,2048]{1,0:T(8,128)(2,1)S(1)}) custom-call(f32[1024,2048]{1,0:T(8,128)S(1)} %bitcast.1, f32[16,1024]{1,0:T(8,128)S(1)} %add.18.rest_0_.refs_0_), custom_call_target="tpu_custom_call" | custom-call | flops 62914560 | bytes 4194304 | tf_op jit(solution)/shard_map/split/pallas_call | solution.py:248
  26.2 2.4 %taper.3.refs_4_ = f32[16,512]{1,0:T(8,128)S(1)} custom-call(s32[8,8]{1,0:T(8,128)S(1)} %copy-done, s32[8]{0:T(128)S(1)} %copy-done.1, f32[16,1280]{1,0:T(8,128)S(1)} %get-tuple-element.22.own_ref, bf16[32,3968]{1,0:T(8,128)(2,1)S(1)} %get-tuple-element.23.values_ref, f32[2,3840]{1,0:T(2,128)S(1)} %get-tuple-element.24.coords_ref, ...), custom_call_target="tpu_custom_call" | custom-call | flops 262144000 | bytes 2097152 | tf_op jit(solution)/shard_map/taper/pallas_call | solution.py:386
  28.6 0.0 collective-permute-done.8.refs_3_
  28.6 0.0 collective-permute-done.7.refs_2_
  28.6 0.3 collective-permute-done.6.refs_1_
  28.9 0.1 collective-permute-start.9
  29.0 1.3 %factor.2.before_ref = f32[16,1024]{1,0:T(8,128)S(1)} custom-call(f32[16,1024]{1,0:T(8,128)S(1)} %add.19.proj_ref, bf16[512,2048]{1,0:T(8,128)(2,1)S(1)} %get-tuple-element.27.refs_5_.rest_0_, bf16[512,2048]{1,0:T(8,128)(2,1)S(1)} %get-tuple-element.29.refs_5_.rest_1_, bf16[512,2048]{1,0:T(8,128)(2,1)S(1)} %get-tuple-element.28.refs_6_.rest_2_, ...), custom_call_target="tpu_custom_call" | custom-call | flops 1048576000 | bytes 4194304 | tf_op jit(solution)/shard_map/factor/pallas_call | solution.py:289
  30.3 0.0 collective-permute-done.9.proj_ref
  30.3 1.3 %factor.3.factor_ref = f32[16,1024]{1,0:T(8,128)S(1)} custom-call(f32[16,1024]{1,0:T(8,128)S(1)} %factor.2.before_ref, f32[16,1024]{1,0:T(8,128)S(1)} %collective-permute-done.9.proj_ref, bf16[512,2048]{1,0:T(8,128)(2,1)S(1)} %get-tuple-element.27.refs_5_.rest_0_, bf16[512,2048]{1,0:T(8,128)(2,1)S(1)} %get-tuple-element.29.refs_5_.rest_1_, ...), custom_call_target="tpu_custom_call" | custom-call | flops 1048576000 | bytes 4194304 | tf_op jit(solution)/shard_map/factor/pallas_call | solution.py:289
  31.6 1.3 %spread.2 = f32[16,1024]{1,0:T(8,128)S(1)} custom-call(f32[16,1024]{1,0:T(8,128)S(1)} %factor.3.factor_ref, bf16[1024,1024]{1,0:T(8,128)(2,1)S(1)} %get-tuple-element.31.high_ref, bf16[1024,1024]{1,0:T(8,128)(2,1)S(1)} %get-tuple-element.32.low_ref), custom_call_target="tpu_custom_call" | custom-call | flops 891289600 | bytes 4194304 | tf_op jit(solution)/shard_map/spread/pallas_call | solution.py:316
  32.9 0.5 %collective-permute-start.10 = (f32[16,1024]{1,0:T(8,128)S(1)}, f32[16,1024]{1,0:T(8,128)S(1)}, u32[]{:S(2)}, u32[]{:S(2)}) collective-permute-start(f32[16,1024]{1,0:T(8,128)S(1)} %spread.2), channel_id=1, source_target_pairs={{1,0},{0,1},{3,2},{2,3},{5,4},{4,5},{7,6},{6,7},{9,8},{8,9},{11,10... | collective-permute-start | bytes 196616 | tf_op jit(solution)/shard_map/ppermute | solution.py:440
  33.4 1.3 %spread.3 = f32[16,1024]{1,0:T(8,128)S(1)} custom-call(f32[16,1024]{1,0:T(8,128)S(1)} %factor.3.factor_ref, bf16[1024,1024]{1,0:T(8,128)(2,1)S(1)} %get-tuple-element.33.high_ref, bf16[1024,1024]{1,0:T(8,128)(2,1)S(1)} %get-tuple-element.34.low_ref), custom_call_target="tpu_custom_call" | custom-call | flops 891289600 | bytes 4194304 | tf_op jit(solution)/shard_map/spread/pallas_call | solution.py:316
  34.7 0.0 collective-permute-done.10
  34.7 0.7 %fusion = f32[16,1024]{1,0:T(8,128)} fusion(f32[16,1024]{1,0:T(8,128)S(1)} %spread.3, f32[16,1024]{1,0:T(8,128)S(1)} %collective-permute-done.10, f32[16,512]{1,0:T(8,128)S(1)} %taper.3.refs_4_, f32[16,512]{1,0:T(8,128)S(1)} %taper.2.refs_4_), kind=kLoop, calls=%fused_computation.1 | loop fusion | flops 49152 | bytes 262144 | tf_op jit(solution)/shard_map/add | solution.py:496
  (5 shorter events, 0.1 us)
Async XLA Ops:
  0.9 3.4 %collective-permute-start = (f32[16,1280]{1,0:T(8,128)S(1)}, f32[16,1280]{1,0:T(8,128)S(1)}, u32[]{:S(2)}, u32[]{:S(2)}) collective-permute-start(f32[16,1280]{1,0:T(8,128)S(1)} %get-tuple-element.20.stack_ref), channel_id=1, source_target_pairs={{1,0},{0,1},{3,2},{2,3},{5,4},{4,5},{7,6},{6,7},{9,8},{8,9},{11,10... | collective-permute-start | bytes 245768 | tf_op jit(solution)/shard_map/ppermute | solution.py:440
  1.4 16.1 %slice-start = ((s8[8388608]{0:T(1024)(128)(4,1)}), s8[4194304]{0:T(1024)(128)(4,1)S(1)}, s32[]{:S(2)}) async-start(s8[8388608]{0:T(1024)(128)(4,1)} %bitcast), calls=%async_computation | async-start | bytes 8388608
  4.3 13.2 %slice-start.1 = ((s8[8388608]{0:T(1024)(128)(4,1)}), s8[4194304]{0:T(1024)(128)(4,1)S(1)}, s32[]{:S(2)}) async-start(s8[8388608]{0:T(1024)(128)(4,1)} %bitcast), calls=%async_computation.1 | async-start | bytes 8388608
  4.3 13.7 %collective-permute-start.2 = (f32[16,1536]{1,0:T(8,128)S(1)}, f32[16,1536]{1,0:T(8,128)S(1)}, u32[]{:S(2)}, u32[]{:S(2)}) collective-permute-start(f32[16,1536]{1,0:T(8,128)S(1)} %strip.1.own_ref), channel_id=1, source_target_pairs={{2,4},{6,8},{10,12},{14,16},{18,20},{22,24},{26,28},{30,0},{4,2},{... | collective-permute-start | bytes 294920 | tf_op jit(solution)/shard_map/ppermute | solution.py:446
  10.9 7.2 %collective-permute-start.1 = (f32[16,1536]{1,0:T(8,128)S(1)}, f32[16,1536]{1,0:T(8,128)S(1)}, u32[]{:S(2)}, u32[]{:S(2)}) collective-permute-start(f32[16,1536]{1,0:T(8,128)S(1)} %strip.1.own_ref), channel_id=1, source_target_pairs={{0,2},{4,6},{8,10},{12,14},{16,18},{20,22},{24,26},{28,30},{2,0},{... | collective-permute-start | bytes 294920 | tf_op jit(solution)/shard_map/ppermute | solution.py:446
  13.8 4.3 %copy-start = (s32[8,8]{1,0:T(8,128)S(1)}, s32[8,8]{1,0:T(8,128)}, u32[]{:S(2)}) copy-start(s32[8,8]{1,0:T(8,128)} %ids_ref.3) | copy-start | bytes 772
  13.8 4.3 %copy-start.1 = (s32[8]{0:T(128)S(1)}, s32[8]{0:T(128)}, u32[]{:S(2)}) copy-start(s32[8]{0:T(128)} %counts_ref.3) | copy-start | bytes 100
  13.8 6.7 %collective-permute-start.5 = (f32[16,1024]{1,0:T(8,128)S(1)}, f32[16,1024]{1,0:T(8,128)S(1)}, u32[]{:S(2)}, u32[]{:S(2)}) collective-permute-start(f32[16,1024]{1,0:T(8,128)S(1)} %add.11.rest_0_.refs_0_), channel_id=1, source_target_pairs={{0,2},{2,0},{4,6},{6,4},{8,10},{10,8},{12,14},{14,12},{16,18},{18,... | collective-permute-start | bytes 196616 | tf_op jit(solution)/shard_map/ppermute | solution.py:432
  15.9 4.7 %collective-permute-start.4 = (f32[16,1024]{1,0:T(8,128)S(1)}, f32[16,1024]{1,0:T(8,128)S(1)}, u32[]{:S(2)}, u32[]{:S(2)}) collective-permute-start(f32[16,1024]{1,0:T(8,128)S(1)} %add.11.rest_0_.refs_0_), channel_id=1, source_target_pairs={{0,4},{2,6},{4,0},{6,2},{8,12},{10,14},{12,8},{14,10},{16,20},{18,... | collective-permute-start | bytes 196616 | tf_op jit(solution)/shard_map/ppermute | solution.py:432
  15.9 5.2 %collective-permute-start.3 = (f32[16,1024]{1,0:T(8,128)S(1)}, f32[16,1024]{1,0:T(8,128)S(1)}, u32[]{:S(2)}, u32[]{:S(2)}) collective-permute-start(f32[16,1024]{1,0:T(8,128)S(1)} %add.11.rest_0_.refs_0_), channel_id=1, source_target_pairs={{0,6},{2,4},{4,2},{6,0},{8,14},{10,12},{12,10},{14,8},{16,22},{18,... | collective-permute-start | bytes 196616 | tf_op jit(solution)/shard_map/ppermute | solution.py:432
  21.1 7.5 %collective-permute-start.8 = (f32[16,1024]{1,0:T(8,128)S(1)}, f32[16,1024]{1,0:T(8,128)S(1)}, u32[]{:S(2)}, u32[]{:S(2)}) collective-permute-start(f32[16,1024]{1,0:T(8,128)S(1)} %add.18.rest_0_.refs_0_), channel_id=1, source_target_pairs={{0,8},{2,10},{4,12},{6,14},{8,0},{10,2},{12,4},{14,6},{16,24},{18,... | collective-permute-start | bytes 196616 | tf_op jit(solution)/shard_map/ppermute | solution.py:432
  21.2 7.4 %collective-permute-start.7 = (f32[16,1024]{1,0:T(8,128)S(1)}, f32[16,1024]{1,0:T(8,128)S(1)}, u32[]{:S(2)}, u32[]{:S(2)}) collective-permute-start(f32[16,1024]{1,0:T(8,128)S(1)} %add.18.rest_0_.refs_0_), channel_id=1, source_target_pairs={{0,16},{2,18},{4,20},{6,22},{8,24},{10,26},{12,28},{14,30},{16,0},... | collective-permute-start | bytes 196616 | tf_op jit(solution)/shard_map/ppermute | solution.py:432
  22.8 6.1 %collective-permute-start.6 = (f32[16,1024]{1,0:T(8,128)S(1)}, f32[16,1024]{1,0:T(8,128)S(1)}, u32[]{:S(2)}, u32[]{:S(2)}) collective-permute-start(f32[16,1024]{1,0:T(8,128)S(1)} %add.18.rest_0_.refs_0_), channel_id=1, source_target_pairs={{0,24},{2,26},{4,28},{6,30},{8,16},{10,18},{12,20},{14,22},{16,8},... | collective-permute-start | bytes 196616 | tf_op jit(solution)/shard_map/ppermute | solution.py:432
  28.9 1.4 %collective-permute-start.9 = (f32[16,1024]{1,0:T(8,128)S(1)}, f32[16,1024]{1,0:T(8,128)S(1)}, u32[]{:S(2)}, u32[]{:S(2)}) collective-permute-start(f32[16,1024]{1,0:T(8,128)S(1)} %add.19.proj_ref), channel_id=1, source_target_pairs={{1,0},{0,1},{3,2},{2,3},{5,4},{4,5},{7,6},{6,7},{9,8},{8,9},{11,10... | collective-permute-start | bytes 196616 | tf_op jit(solution)/shard_map/ppermute | solution.py:440
  32.9 1.8 %collective-permute-start.10 = (f32[16,1024]{1,0:T(8,128)S(1)}, f32[16,1024]{1,0:T(8,128)S(1)}, u32[]{:S(2)}, u32[]{:S(2)}) collective-permute-start(f32[16,1024]{1,0:T(8,128)S(1)} %spread.2), channel_id=1, source_target_pairs={{1,0},{0,1},{3,2},{2,3},{5,4},{4,5},{7,6},{6,7},{9,8},{8,9},{11,10... | collective-permute-start | bytes 196616 | tf_op jit(solution)/shard_map/ppermute | solution.py:440

commit v11 on v10

--- a/solution.py
+++ b/solution.py
@@ -440,10 +440,19 @@
     return lax.ppermute(value, axis, [((i + step) % count, i) for i in range(count)])
 
 
-def paired(value, axis, first):
-    count = lax.axis_size(axis)
-    pairs = [((first + i) % count, (first + i + 1) % count) for i in range(0, count - 1, 2)]
-    return lax.ppermute(value, axis, pairs + [(b, a) for a, b in pairs])
+def paired(value, axis, other, first):
+    count, groups = lax.axis_size(axis), lax.axis_size(other)
+    partner = {}
+    for i in range(first, count - 1, 2):
+        partner[i], partner[i + 1] = i + 1, i
+    pairs = []
+    for i in range(count):
+        for j in range(groups):
+            if i in partner:
+                pairs.append((i * groups + j, partner[i] * groups + j))
+            elif j ^ 1 < groups:
+                pairs.append((i * groups + j, i * groups + (j ^ 1)))
+    return lax.ppermute(value, (axis, other), pairs)
 
 
 def shards(probes, locations, knot_locs, knot_precision, neighbours, counts):
@@ -463,7 +472,7 @@
     stack = parts[0][3]
 
     strip = make_strip(chunks[-1], stack, chunks[1 % groups])
-    values, coords = assemble([strip, paired(strip, "space", 0), paired(strip, "space", 1)], extent)
+    values, coords = assemble([strip, paired(strip, "space", "knot", 0), paired(strip, "space", "knot", 1)], extent)
     projection = sum(part[0] for part in parts)
     rounds = len(butterfly_rounds(lax.axis_size("space")))
     pieces = math.gcd(own_blocks, rounds)

time: 35.5 us -> 35.5 us (level)
  starting transfers between devices: 15.8 us -> 13.2 us
  waiting for transfers between devices: 0.8 us -> 3.39 us
    ppermute x6, waiting for transfers between devices: 0.79 us -> 3.38 us  [butterfly_round(): got.append(lax.ppermute(value, (axis, other), pairs))]
    ppermute x2, starting transfers between devices: 6.57 us -> 4.07 us  [paired(): return lax.ppermute(value, (axis, other), pairs)]
where the time goes in v11:
time: 35.5 us; the launch traced here: 35.4 us
  Pallas kernels  17.9 us (50%)
  starting transfers between devices  13.2 us (37%)
  waiting for transfers between devices  3.39 us (10%)
  other arithmetic  0.7 us (2%)
    ppermute x6, starting transfers between devices, butterfly_round(): got.append(lax.ppermute(value, (axis, other), pairs))  8 us
    pallas_call x2, Pallas kernels, project(): pl.pallas_call(functools.partial(project_kernel, scale, grain_of(scale *...  5.76 us
    pallas_call x2, Pallas kernels, taper(): pl.pallas_call(functools.partial(taper_kernel, first, grain_of(TAPER_RATE...  4.8 us
    ppermute x2, starting transfers between devices, paired(): return lax.ppermute(value, (axis, other), pairs)  4.07 us
    ppermute x6, waiting for transfers between devices, butterfly_round(): got.append(lax.ppermute(value, (axis, other), pairs))  3.38 us
    pallas_call x2, Pallas kernels, factored(): pl.pallas_call(kernel, out_shape=jax.ShapeDtypeStruct((probes, rows), jnp...  2.6 us
    pallas_call x2, Pallas kernels, spread(): pl.pallas_call(functools.partial(spread_kernel, scale), out_shape=jax.Sha...  2.56 us
    pallas_call x2, Pallas kernels, split_rows(): pl.pallas_call(functools.partial(split_kernel, first), out_shape=(pltpu.V...  1.18 us
  transfers between devices with their start and end apart: 11, of which 2 were waited for; matrix products, arithmetic and copies ran while one was open for 0% of the time, Pallas kernels for 41%

profile of v11, /device:TPU:0, one launch (start us, length us, event | category | flops | bytes accessed | tf_op | source)
XLA Modules:
  0.0 35.4 jit_solution(8218883328265412509)
XLA Ops:
  0.0 0.9 %prepare.1 = (f32[16,1280]{1,0:T(8,128)S(1)}, f32[2,1024]{1,0:T(2,128)S(1)}) custom-call(f32[16,1024]{1,0:T(8,128)} %probes_ref.1, f32[2,1024]{1,0:T(2,128)} %locations_ref.1, f32[2,1024]{1,0:T(2,128)} %knots_ref.1), custom_call_target="tpu_custom_call" | custom-call | tf_op jit(solution)/shard_map/prepare/pallas_call | solution.py:100
  0.9 0.5 %collective-permute-start = (f32[16,1280]{1,0:T(8,128)S(1)}, f32[16,1280]{1,0:T(8,128)S(1)}, u32[]{:S(2)}, u32[]{:S(2)}) collective-permute-start(f32[16,1280]{1,0:T(8,128)S(1)} %get-tuple-element.20.stack_ref), channel_id=1, source_target_pairs={{1,0},{0,1},{3,2},{2,3},{5,4},{4,5},{7,6},{6,7},{9,8},{8,9},{11,10... | collective-permute-start | bytes 245768 | tf_op jit(solution)/shard_map/ppermute | solution.py:440
  1.4 0.0 slice-start
  1.4 2.9 %project.2 = (f32[16,1024]{1,0:T(8,128)S(1)}, bf16[1024,1024]{1,0:T(8,128)(2,1)S(1)}, bf16[1024,1024]{1,0:T(8,128)(2,1)S(1)}, f32[16,1280]{1,0:T(8,128)S(1)}) custom-call(f32[16,1280]{1,0:T(8,128)S(1)} %get-tuple-element.20.stack_ref, f32[2,1024]{1,0:T(2,128)S(1)} %get-tuple-element.21.knots_ref), custom_call_target="tpu_custom_call" | custom-call | flops 2936012800 | bytes 4194304 | tf_op jit(solution)/shard_map/project/pallas_call | solution.py:220
  4.3 0.0 collective-permute-done.below_ref.above_ref.stack_ref
  4.3 0.0 slice-start.1
  4.3 0.1 collective-permute-start.2
  4.5 3.9 %collective-permute-start.1 = (f32[16,1536]{1,0:T(8,128)S(1)}, f32[16,1536]{1,0:T(8,128)S(1)}, u32[]{:S(2)}, u32[]{:S(2)}) collective-permute-start(f32[16,1536]{1,0:T(8,128)S(1)} %strip.1.own_ref), channel_id=1, source_target_pairs={{0,2},{1,3},{2,0},{3,1},{4,6},{5,7},{6,4},{7,5},{8,10},{9,11},{10,... | collective-permute-start | bytes 294920 | tf_op jit(solution)/shard_map/ppermute | solution.py:455
  8.4 2.9 %project.3 = (f32[16,1024]{1,0:T(8,128)S(1)}, bf16[1024,1024]{1,0:T(8,128)(2,1)S(1)}, bf16[1024,1024]{1,0:T(8,128)(2,1)S(1)}, f32[16,1280]{1,0:T(8,128)}) custom-call(f32[16,1280]{1,0:T(8,128)S(1)} %collective-permute-done.below_ref.above_ref.stack_ref, f32[2,1024]{1,0:T(2,128)S(1)} %get-tuple-element.21.knots_ref), custom_call_target="tpu_custom_call" | custom-call | flops 2936012800 | bytes 4194304 | tf_op jit(solution)/shard_map/project/pallas_call | solution.py:220
  11.3 0.0 copy-start
  11.3 0.0 copy-start.1
  11.3 0.1 collective-permute-start.5
  11.4 2.0 %collective-permute-start.4 = (f32[16,1024]{1,0:T(8,128)S(1)}, f32[16,1024]{1,0:T(8,128)S(1)}, u32[]{:S(2)}, u32[]{:S(2)}) collective-permute-start(f32[16,1024]{1,0:T(8,128)S(1)} %add.11.rest_0_.refs_0_), channel_id=1, source_target_pairs={{0,4},{2,6},{4,0},{6,2},{8,12},{10,14},{12,8},{14,10},{16,20},{18,... | collective-permute-start | bytes 196616 | tf_op jit(solution)/shard_map/ppermute | solution.py:432
  13.4 1.5 %collective-permute-start.3 = (f32[16,1024]{1,0:T(8,128)S(1)}, f32[16,1024]{1,0:T(8,128)S(1)}, u32[]{:S(2)}, u32[]{:S(2)}) collective-permute-start(f32[16,1024]{1,0:T(8,128)S(1)} %add.11.rest_0_.refs_0_), channel_id=1, source_target_pairs={{0,6},{2,4},{4,2},{6,0},{8,14},{10,12},{12,10},{14,8},{16,22},{18,... | collective-permute-start | bytes 196616 | tf_op jit(solution)/shard_map/ppermute | solution.py:432
  14.9 0.0 slice-done
  14.9 0.0 slice-done.1
  14.9 0.6 %split.2 = (bf16[512,2048]{1,0:T(8,128)(2,1)S(1)}, bf16[512,2048]{1,0:T(8,128)(2,1)S(1)}) custom-call(f32[1024,2048]{1,0:T(8,128)S(1)} %bitcast.1, f32[16,1024]{1,0:T(8,128)S(1)} %add.11.rest_0_.refs_0_), custom_call_target="tpu_custom_call" | custom-call | flops 62914560 | bytes 4194304 | tf_op jit(solution)/shard_map/split/pallas_call | solution.py:248
  15.5 0.0 collective-permute-done.2.west_ref
  15.5 0.0 collective-permute-done.1.east_ref
  15.5 0.1 assemble.1
  15.6 0.0 copy-done
  15.6 0.0 copy-done.1
  15.6 2.4 %taper.2.refs_4_ = f32[16,512]{1,0:T(8,128)S(1)} custom-call(s32[8,8]{1,0:T(8,128)S(1)} %copy-done, s32[8]{0:T(128)S(1)} %copy-done.1, f32[16,1280]{1,0:T(8,128)S(1)} %get-tuple-element.22.own_ref, bf16[32,3968]{1,0:T(8,128)(2,1)S(1)} %get-tuple-element.23.values_ref, f32[2,3840]{1,0:T(2,128)S(1)} %get-tuple-element.24.coords_ref, ...), custom_call_target="tpu_custom_call" | custom-call | flops 262144000 | bytes 2097152 | tf_op jit(solution)/shard_map/taper/pallas_call | solution.py:386
  18.0 0.0 collective-permute-done.5.refs_3_
  18.0 0.0 collective-permute-done.4.refs_2_
  18.0 0.5 %collective-permute-done.3.refs_1_ = f32[16,1024]{1,0:T(8,128)S(1)} collective-permute-done((f32[16,1024]{1,0:T(8,128)S(1)}, f32[16,1024]{1,0:T(8,128)S(1)}, u32[]{:S(2)}, u32[]{:S(2)}) %collective-permute-start.3) | collective-permute-done | bytes 65568 | tf_op jit(solution)/shard_map/ppermute | solution.py:432
  18.6 1.6 %collective-permute-start.8 = (f32[16,1024]{1,0:T(8,128)S(1)}, f32[16,1024]{1,0:T(8,128)S(1)}, u32[]{:S(2)}, u32[]{:S(2)}) collective-permute-start(f32[16,1024]{1,0:T(8,128)S(1)} %add.18.rest_0_.refs_0_), channel_id=1, source_target_pairs={{0,8},{2,10},{4,12},{6,14},{8,0},{10,2},{12,4},{14,6},{16,24},{18,... | collective-permute-start | bytes 196616 | tf_op jit(solution)/shard_map/ppermute | solution.py:432
  20.2 2.6 %collective-permute-start.7 = (f32[16,1024]{1,0:T(8,128)S(1)}, f32[16,1024]{1,0:T(8,128)S(1)}, u32[]{:S(2)}, u32[]{:S(2)}) collective-permute-start(f32[16,1024]{1,0:T(8,128)S(1)} %add.18.rest_0_.refs_0_), channel_id=1, source_target_pairs={{0,16},{2,18},{4,20},{6,22},{8,24},{10,26},{12,28},{14,30},{16,0},... | collective-permute-start | bytes 196616 | tf_op jit(solution)/shard_map/ppermute | solution.py:432
  22.8 0.2 collective-permute-start.6
  23.0 0.6 %split.3 = (bf16[512,2048]{1,0:T(8,128)(2,1)S(1)}, bf16[512,2048]{1,0:T(8,128)(2,1)S(1)}) custom-call(f32[1024,2048]{1,0:T(8,128)S(1)} %bitcast.1, f32[16,1024]{1,0:T(8,128)S(1)} %add.18.rest_0_.refs_0_), custom_call_target="tpu_custom_call" | custom-call | flops 62914560 | bytes 4194304 | tf_op jit(solution)/shard_map/split/pallas_call | solution.py:248
  23.6 2.4 %taper.3.refs_4_ = f32[16,512]{1,0:T(8,128)S(1)} custom-call(s32[8,8]{1,0:T(8,128)S(1)} %copy-done, s32[8]{0:T(128)S(1)} %copy-done.1, f32[16,1280]{1,0:T(8,128)S(1)} %get-tuple-element.22.own_ref, bf16[32,3968]{1,0:T(8,128)(2,1)S(1)} %get-tuple-element.23.values_ref, f32[2,3840]{1,0:T(2,128)S(1)} %get-tuple-element.24.coords_ref, ...), custom_call_target="tpu_custom_call" | custom-call | flops 262144000 | bytes 2097152 | tf_op jit(solution)/shard_map/taper/pallas_call | solution.py:386
  26.0 0.0 collective-permute-done.8.refs_3_
  26.1 0.0 collective-permute-done.7.refs_2_
  26.1 2.8 %collective-permute-done.6.refs_1_ = f32[16,1024]{1,0:T(8,128)S(1)} collective-permute-done((f32[16,1024]{1,0:T(8,128)S(1)}, f32[16,1024]{1,0:T(8,128)S(1)}, u32[]{:S(2)}, u32[]{:S(2)}) %collective-permute-start.6) | collective-permute-done | bytes 65568 | tf_op jit(solution)/shard_map/ppermute | solution.py:432
  28.9 0.1 collective-permute-start.9
  29.0 1.3 %factor.2.before_ref = f32[16,1024]{1,0:T(8,128)S(1)} custom-call(f32[16,1024]{1,0:T(8,128)S(1)} %add.19.proj_ref, bf16[512,2048]{1,0:T(8,128)(2,1)S(1)} %get-tuple-element.27.refs_5_.rest_0_, bf16[512,2048]{1,0:T(8,128)(2,1)S(1)} %get-tuple-element.29.refs_5_.rest_1_, bf16[512,2048]{1,0:T(8,128)(2,1)S(1)} %get-tuple-element.28.refs_6_.rest_2_, ...), custom_call_target="tpu_custom_call" | custom-call | flops 1048576000 | bytes 4194304 | tf_op jit(solution)/shard_map/factor/pallas_call | solution.py:289
  30.3 0.0 collective-permute-done.9.proj_ref
  30.3 1.3 %factor.3.factor_ref = f32[16,1024]{1,0:T(8,128)S(1)} custom-call(f32[16,1024]{1,0:T(8,128)S(1)} %factor.2.before_ref, f32[16,1024]{1,0:T(8,128)S(1)} %collective-permute-done.9.proj_ref, bf16[512,2048]{1,0:T(8,128)(2,1)S(1)} %get-tuple-element.27.refs_5_.rest_0_, bf16[512,2048]{1,0:T(8,128)(2,1)S(1)} %get-tuple-element.29.refs_5_.rest_1_, ...), custom_call_target="tpu_custom_call" | custom-call | flops 1048576000 | bytes 4194304 | tf_op jit(solution)/shard_map/factor/pallas_call | solution.py:289
  31.6 1.3 %spread.2 = f32[16,1024]{1,0:T(8,128)S(1)} custom-call(f32[16,1024]{1,0:T(8,128)S(1)} %factor.3.factor_ref, bf16[1024,1024]{1,0:T(8,128)(2,1)S(1)} %get-tuple-element.31.high_ref, bf16[1024,1024]{1,0:T(8,128)(2,1)S(1)} %get-tuple-element.32.low_ref), custom_call_target="tpu_custom_call" | custom-call | flops 891289600 | bytes 4194304 | tf_op jit(solution)/shard_map/spread/pallas_call | solution.py:316
  32.9 0.5 %collective-permute-start.10 = (f32[16,1024]{1,0:T(8,128)S(1)}, f32[16,1024]{1,0:T(8,128)S(1)}, u32[]{:S(2)}, u32[]{:S(2)}) collective-permute-start(f32[16,1024]{1,0:T(8,128)S(1)} %spread.2), channel_id=1, source_target_pairs={{1,0},{0,1},{3,2},{2,3},{5,4},{4,5},{7,6},{6,7},{9,8},{8,9},{11,10... | collective-permute-start | bytes 196616 | tf_op jit(solution)/shard_map/ppermute | solution.py:440
  33.4 1.3 %spread.3 = f32[16,1024]{1,0:T(8,128)S(1)} custom-call(f32[16,1024]{1,0:T(8,128)S(1)} %factor.3.factor_ref, bf16[1024,1024]{1,0:T(8,128)(2,1)S(1)} %get-tuple-element.33.high_ref, bf16[1024,1024]{1,0:T(8,128)(2,1)S(1)} %get-tuple-element.34.low_ref), custom_call_target="tpu_custom_call" | custom-call | flops 891289600 | bytes 4194304 | tf_op jit(solution)/shard_map/spread/pallas_call | solution.py:316
  34.7 0.0 collective-permute-done.10
  34.7 0.7 %fusion = f32[16,1024]{1,0:T(8,128)} fusion(f32[16,1024]{1,0:T(8,128)S(1)} %spread.3, f32[16,1024]{1,0:T(8,128)S(1)} %collective-permute-done.10, f32[16,512]{1,0:T(8,128)S(1)} %taper.3.refs_4_, f32[16,512]{1,0:T(8,128)S(1)} %taper.2.refs_4_), kind=kLoop, calls=%fused_computation.1 | loop fusion | flops 49152 | bytes 262144 | tf_op jit(solution)/shard_map/add | solution.py:505
  (5 shorter events, 0.1 us)
Async XLA Ops:
  0.9 3.4 %collective-permute-start = (f32[16,1280]{1,0:T(8,128)S(1)}, f32[16,1280]{1,0:T(8,128)S(1)}, u32[]{:S(2)}, u32[]{:S(2)}) collective-permute-start(f32[16,1280]{1,0:T(8,128)S(1)} %get-tuple-element.20.stack_ref), channel_id=1, source_target_pairs={{1,0},{0,1},{3,2},{2,3},{5,4},{4,5},{7,6},{6,7},{9,8},{8,9},{11,10... | collective-permute-start | bytes 245768 | tf_op jit(solution)/shard_map/ppermute | solution.py:440
  1.4 13.5 %slice-start = ((s8[8388608]{0:T(1024)(128)(4,1)}), s8[4194304]{0:T(1024)(128)(4,1)S(1)}, s32[]{:S(2)}) async-start(s8[8388608]{0:T(1024)(128)(4,1)} %bitcast), calls=%async_computation | async-start | bytes 8388608
  4.3 10.6 %slice-start.1 = ((s8[8388608]{0:T(1024)(128)(4,1)}), s8[4194304]{0:T(1024)(128)(4,1)S(1)}, s32[]{:S(2)}) async-start(s8[8388608]{0:T(1024)(128)(4,1)} %bitcast), calls=%async_computation.1 | async-start | bytes 8388608
  4.3 11.2 %collective-permute-start.2 = (f32[16,1536]{1,0:T(8,128)S(1)}, f32[16,1536]{1,0:T(8,128)S(1)}, u32[]{:S(2)}, u32[]{:S(2)}) collective-permute-start(f32[16,1536]{1,0:T(8,128)S(1)} %strip.1.own_ref), channel_id=1, source_target_pairs={{0,1},{1,0},{2,4},{3,5},{4,2},{5,3},{6,8},{7,9},{8,6},{9,7},{10,12... | collective-permute-start | bytes 294920 | tf_op jit(solution)/shard_map/ppermute | solution.py:455
  4.5 11.0 %collective-permute-start.1 = (f32[16,1536]{1,0:T(8,128)S(1)}, f32[16,1536]{1,0:T(8,128)S(1)}, u32[]{:S(2)}, u32[]{:S(2)}) collective-permute-start(f32[16,1536]{1,0:T(8,128)S(1)} %strip.1.own_ref), channel_id=1, source_target_pairs={{0,2},{1,3},{2,0},{3,1},{4,6},{5,7},{6,4},{7,5},{8,10},{9,11},{10,... | collective-permute-start | bytes 294920 | tf_op jit(solution)/shard_map/ppermute | solution.py:455
  11.3 4.3 %copy-start = (s32[8,8]{1,0:T(8,128)S(1)}, s32[8,8]{1,0:T(8,128)}, u32[]{:S(2)}) copy-start(s32[8,8]{1,0:T(8,128)} %ids_ref.3) | copy-start | bytes 772
  11.3 4.3 %copy-start.1 = (s32[8]{0:T(128)S(1)}, s32[8]{0:T(128)}, u32[]{:S(2)}) copy-start(s32[8]{0:T(128)} %counts_ref.3) | copy-start | bytes 100
  11.3 6.7 %collective-permute-start.5 = (f32[16,1024]{1,0:T(8,128)S(1)}, f32[16,1024]{1,0:T(8,128)S(1)}, u32[]{:S(2)}, u32[]{:S(2)}) collective-permute-start(f32[16,1024]{1,0:T(8,128)S(1)} %add.11.rest_0_.refs_0_), channel_id=1, source_target_pairs={{0,2},{2,0},{4,6},{6,4},{8,10},{10,8},{12,14},{14,12},{16,18},{18,... | collective-permute-start | bytes 196616 | tf_op jit(solution)/shard_map/ppermute | solution.py:432
  11.4 6.6 %collective-permute-start.4 = (f32[16,1024]{1,0:T(8,128)S(1)}, f32[16,1024]{1,0:T(8,128)S(1)}, u32[]{:S(2)}, u32[]{:S(2)}) collective-permute-start(f32[16,1024]{1,0:T(8,128)S(1)} %add.11.rest_0_.refs_0_), channel_id=1, source_target_pairs={{0,4},{2,6},{4,0},{6,2},{8,12},{10,14},{12,8},{14,10},{16,20},{18,... | collective-permute-start | bytes 196616 | tf_op jit(solution)/shard_map/ppermute | solution.py:432
  13.4 5.2 %collective-permute-start.3 = (f32[16,1024]{1,0:T(8,128)S(1)}, f32[16,1024]{1,0:T(8,128)S(1)}, u32[]{:S(2)}, u32[]{:S(2)}) collective-permute-start(f32[16,1024]{1,0:T(8,128)S(1)} %add.11.rest_0_.refs_0_), channel_id=1, source_target_pairs={{0,6},{2,4},{4,2},{6,0},{8,14},{10,12},{12,10},{14,8},{16,22},{18,... | collective-permute-start | bytes 196616 | tf_op jit(solution)/shard_map/ppermute | solution.py:432
  18.6 7.5 %collective-permute-start.8 = (f32[16,1024]{1,0:T(8,128)S(1)}, f32[16,1024]{1,0:T(8,128)S(1)}, u32[]{:S(2)}, u32[]{:S(2)}) collective-permute-start(f32[16,1024]{1,0:T(8,128)S(1)} %add.18.rest_0_.refs_0_), channel_id=1, source_target_pairs={{0,8},{2,10},{4,12},{6,14},{8,0},{10,2},{12,4},{14,6},{16,24},{18,... | collective-permute-start | bytes 196616 | tf_op jit(solution)/shard_map/ppermute | solution.py:432
  20.2 5.9 %collective-permute-start.7 = (f32[16,1024]{1,0:T(8,128)S(1)}, f32[16,1024]{1,0:T(8,128)S(1)}, u32[]{:S(2)}, u32[]{:S(2)}) collective-permute-start(f32[16,1024]{1,0:T(8,128)S(1)} %add.18.rest_0_.refs_0_), channel_id=1, source_target_pairs={{0,16},{2,18},{4,20},{6,22},{8,24},{10,26},{12,28},{14,30},{16,0},... | collective-permute-start | bytes 196616 | tf_op jit(solution)/shard_map/ppermute | solution.py:432
  22.8 6.1 %collective-permute-start.6 = (f32[16,1024]{1,0:T(8,128)S(1)}, f32[16,1024]{1,0:T(8,128)S(1)}, u32[]{:S(2)}, u32[]{:S(2)}) collective-permute-start(f32[16,1024]{1,0:T(8,128)S(1)} %add.18.rest_0_.refs_0_), channel_id=1, source_target_pairs={{0,24},{2,26},{4,28},{6,30},{8,16},{10,18},{12,20},{14,22},{16,8},... | collective-permute-start | bytes 196616 | tf_op jit(solution)/shard_map/ppermute | solution.py:432
  28.9 1.4 %collective-permute-start.9 = (f32[16,1024]{1,0:T(8,128)S(1)}, f32[16,1024]{1,0:T(8,128)S(1)}, u32[]{:S(2)}, u32[]{:S(2)}) collective-permute-start(f32[16,1024]{1,0:T(8,128)S(1)} %add.19.proj_ref), channel_id=1, source_target_pairs={{1,0},{0,1},{3,2},{2,3},{5,4},{4,5},{7,6},{6,7},{9,8},{8,9},{11,10... | collective-permute-start | bytes 196616 | tf_op jit(solution)/shard_map/ppermute | solution.py:440
  32.9 1.8 %collective-permute-start.10 = (f32[16,1024]{1,0:T(8,128)S(1)}, f32[16,1024]{1,0:T(8,128)S(1)}, u32[]{:S(2)}, u32[]{:S(2)}) collective-permute-start(f32[16,1024]{1,0:T(8,128)S(1)} %spread.2), channel_id=1, source_target_pairs={{1,0},{0,1},{3,2},{2,3},{5,4},{4,5},{7,6},{6,7},{9,8},{8,9},{11,10... | collective-permute-start | bytes 196616 | tf_op jit(solution)/shard_map/ppermute | solution.py:440

commit v12 on v11

--- a/solution.py
+++ b/solution.py
@@ -180,39 +180,39 @@
     return (x + grain) - (grain - grain * HALF_GRAIN)
 
 
-def project_kernel(scale, grain, stack_ref, knots_ref, out_ref, high_ref, low_ref, copy_ref, weights):
-    points, knots = high_ref.shape
+def project_kernel(scale, grain, stack_ref, knots_ref, out_ref, high_ref, low_ref, copy_ref, weights, columns):
+    knots, points = high_ref.shape
     probes = stack_ref.shape[0]
     tile = min(TILE, knots)
     wide = min(TILE, points)
     copy_ref[...] = stack_ref[...]
     weights[...] = stacked_halves(stack_ref[:, :points])
-    east, north = [
-        on_grid(jnp.transpose(coordinate_rows(stack_ref, points, axis) * scale), grain) for axis in range(2)
-    ]
+    fill = jnp.zeros((6, knots), jnp.float32)
+    columns[...] = jnp.transpose(jnp.concatenate([off_grid(knots_ref[...] * scale, grain), fill], axis=0))
+    east, north = [on_grid(coordinate_rows(stack_ref, points, axis) * scale, grain) for axis in range(2)]
 
     @pl.loop(0, knots // tile)
     def _(step):
-        lanes = pl.ds(pl.multiple_of(step * tile, tile), tile)
-        kx, ky = [off_grid(knots_ref[axis : axis + 1, lanes] * scale, grain) for axis in range(2)]
+        rows = pl.ds(pl.multiple_of(step * tile, tile), tile)
+        kx, ky = [columns[rows, axis : axis + 1] for axis in range(2)]
         total = jnp.zeros((2 * probes, tile), jnp.float32)
         for start in range(0, points, wide):
             highs, lows = [], []
-            for row in range(start, start + wide, LANES):
-                block = row // LANES
-                dx = east[:, block : block + 1] - kx
-                dy = north[:, block : block + 1] - ky
+            for lane in range(start, start + wide, LANES):
+                block = lane // LANES
+                dx = east[block : block + 1, :] - kx
+                dy = north[block : block + 1, :] - ky
                 square = dx * dx + dy * dy
                 high, low = halves(jnp.exp2(-(square * lax.rsqrt(square))))
-                high_ref[row : row + LANES, lanes] = high
-                low_ref[row : row + LANES, lanes] = low
+                high_ref[rows, lane : lane + LANES] = high
+                low_ref[rows, lane : lane + LANES] = low
                 highs.append(high)
                 lows.append(low)
             part = weights[:, start : start + wide]
             total = total + (
-                dot_nn(part, jnp.concatenate(highs, axis=0)) + dot_nn(part, jnp.concatenate(lows, axis=0))
+                dot_nt(part, jnp.concatenate(highs, axis=1)) + dot_nt(part, jnp.concatenate(lows, axis=1))
             )
-        out_ref[:, lanes] = folded(total)
+        out_ref[:, rows] = folded(total)
 
 
 def project(stack, knot_locs, scale, extent):
@@ -221,13 +221,16 @@
         functools.partial(project_kernel, scale, grain_of(scale * extent)),
         out_shape=(
             jax.ShapeDtypeStruct((probes, knots), jnp.float32),
-            pltpu.VMEM((points, knots), jnp.bfloat16),
-            pltpu.VMEM((points, knots), jnp.bfloat16),
+            pltpu.VMEM((knots, points), jnp.bfloat16),
+            pltpu.VMEM((knots, points), jnp.bfloat16),
             jax.ShapeDtypeStruct(stack.shape, jnp.float32),
         ),
         in_specs=[VMEM, VMEM],
         out_specs=(VMEM, VMEM, VMEM, VMEM),
-        scratch_shapes=[pltpu.VMEM((2 * probes, points), jnp.bfloat16)],
+        scratch_shapes=[
+            pltpu.VMEM((2 * probes, points), jnp.bfloat16),
+            pltpu.VMEM((knots, 8), jnp.float32),
+        ],
         compiler_params=pltpu.CompilerParams(vmem_limit_bytes=LIMIT),
         cost_estimate=cost(2800, points * knots, 2),
         name="project",
@@ -298,19 +301,17 @@
     )(*operands)
 
 
-def spread_kernel(scale, factor_ref, high_ref, low_ref, out_ref, weights):
-    probes = factor_ref.shape[0]
-    points = high_ref.shape[0]
+def spread_kernel(scale, factor_ref, high_ref, low_ref, out_ref):
+    points = high_ref.shape[1]
     tile = min(TILE, points)
-    weights[...] = padded_halves(factor_ref[...] * scale, weights.shape[0])
+    weights = stacked_halves(factor_ref[...] * scale)
     for start in range(0, points, tile):
-        rows = slice(start, start + tile)
-        total = dot_nt(high_ref[rows, :], weights[...]) + dot_nt(low_ref[rows, :], weights[...])
-        out_ref[:, rows] = folded_columns(total, probes)
+        lanes = slice(start, start + tile)
+        out_ref[:, lanes] = folded(dot_nn(weights, high_ref[:, lanes]) + dot_nn(weights, low_ref[:, lanes]))
 
 
 def spread(factor, high, low, scale):
-    (probes, knots), points = factor.shape, high.shape[0]
+    (probes, knots), points = factor.shape, high.shape[1]
     high = pltpu.with_memory_space_constraint(high, pltpu.VMEM)
     low = pltpu.with_memory_space_constraint(low, pltpu.VMEM)
     return pl.pallas_call(
@@ -318,7 +319,6 @@
         out_shape=jax.ShapeDtypeStruct((probes, points), jnp.float32),
         in_specs=[VMEM, VMEM, VMEM],
         out_specs=VMEM,
-        scratch_shapes=[pltpu.VMEM((LANES, knots), jnp.bfloat16)],
         compiler_params=pltpu.CompilerParams(vmem_limit_bytes=LIMIT),
         cost_estimate=cost(850, knots * points),
         name="spread",

time: 35.5 us -> 36 us (1.014)
  Pallas kernels: 17.9 us -> 18.3 us
    pallas_call x2, Pallas kernels: 5.76 us -> 7.19 us  [project(): pl.pallas_call(functools.partial(project_kernel, scale, grain_of(scale *...]
    pallas_call x2, Pallas kernels: 2.56 us -> 1.54 us  [spread(): pl.pallas_call(functools.partial(spread_kernel, scale), out_shape=jax.Sha...]
  transfers between devices with their start and end apart: 11 -> 11, of which waited for: 2 -> 3; matrix products, arithmetic and copies ran while one was open for 0% -> 0% of each run, Pallas kernels for 41% -> 43%
where the time goes in v12:
time: 36 us; the launch traced here: 35.9 us
  Pallas kernels  18.3 us (51%)
  starting transfers between devices  13.2 us (37%)
  waiting for transfers between devices  3.53 us (10%)
  other arithmetic  0.67 us (2%)
    ppermute x6, starting transfers between devices, butterfly_round(): got.append(lax.ppermute(value, (axis, other), pairs))  8 us
    pallas_call x2, Pallas kernels, project(): pl.pallas_call(functools.partial(project_kernel, scale, grain_of(scale *...  7.19 us
    pallas_call x2, Pallas kernels, taper(): pl.pallas_call(functools.partial(taper_kernel, first, grain_of(TAPER_RATE...  4.8 us
    ppermute x2, starting transfers between devices, paired(): return lax.ppermute(value, (axis, other), pairs)  4.07 us
    ppermute x6, waiting for transfers between devices, butterfly_round(): got.append(lax.ppermute(value, (axis, other), pairs))  3.38 us
    pallas_call x2, Pallas kernels, factored(): pl.pallas_call(kernel, out_shape=jax.ShapeDtypeStruct((probes, rows), jnp...  2.6 us
    pallas_call x2, Pallas kernels, spread(): pl.pallas_call(functools.partial(spread_kernel, scale), out_shape=jax.Sha...  1.54 us
    pallas_call x2, Pallas kernels, split_rows(): pl.pallas_call(functools.partial(split_kernel, first), out_shape=(pltpu.V...  1.18 us
  transfers between devices with their start and end apart: 11, of which 3 were waited for; matrix products, arithmetic and copies ran while one was open for 0% of the time, Pallas kernels for 43%

profile of v12, /device:TPU:0, one launch (start us, length us, event | category | flops | bytes accessed | tf_op | source)
XLA Modules:
  0.0 35.9 jit_solution(1273797943319908067)
XLA Ops:
  0.0 0.9 %prepare.1 = (f32[16,1280]{1,0:T(8,128)S(1)}, f32[2,1024]{1,0:T(2,128)S(1)}) custom-call(f32[16,1024]{1,0:T(8,128)} %probes_ref.1, f32[2,1024]{1,0:T(2,128)} %locations_ref.1, f32[2,1024]{1,0:T(2,128)} %knots_ref.1), custom_call_target="tpu_custom_call" | custom-call | tf_op jit(solution)/shard_map/prepare/pallas_call | solution.py:100
  0.9 0.5 %collective-permute-start = (f32[16,1280]{1,0:T(8,128)S(1)}, f32[16,1280]{1,0:T(8,128)S(1)}, u32[]{:S(2)}, u32[]{:S(2)}) collective-permute-start(f32[16,1280]{1,0:T(8,128)S(1)} %get-tuple-element.20.stack_ref), channel_id=1, source_target_pairs={{1,0},{0,1},{3,2},{2,3},{5,4},{4,5},{7,6},{6,7},{9,8},{8,9},{11,10... | collective-permute-start | bytes 245768 | tf_op jit(solution)/shard_map/ppermute | solution.py:440
  1.4 0.0 slice-start
  1.4 3.6 %project.2 = (f32[16,1024]{1,0:T(8,128)S(1)}, bf16[1024,1024]{1,0:T(8,128)(2,1)S(1)}, bf16[1024,1024]{1,0:T(8,128)(2,1)S(1)}, f32[16,1280]{1,0:T(8,128)S(1)}) custom-call(f32[16,1280]{1,0:T(8,128)S(1)} %get-tuple-element.20.stack_ref, f32[2,1024]{1,0:T(2,128)S(1)} %get-tuple-element.21.knots_ref), custom_call_target="tpu_custom_call" | custom-call | flops 2936012800 | bytes 4194304 | tf_op jit(solution)/shard_map/project/pallas_call | solution.py:220
  5.0 0.0 collective-permute-done.below_ref.above_ref.stack_ref
  5.0 0.0 slice-start.1
  5.1 0.1 collective-permute-start.2
  5.2 3.9 %collective-permute-start.1 = (f32[16,1536]{1,0:T(8,128)S(1)}, f32[16,1536]{1,0:T(8,128)S(1)}, u32[]{:S(2)}, u32[]{:S(2)}) collective-permute-start(f32[16,1536]{1,0:T(8,128)S(1)} %strip.1.own_ref), channel_id=1, source_target_pairs={{0,2},{1,3},{2,0},{3,1},{4,6},{5,7},{6,4},{7,5},{8,10},{9,11},{10,... | collective-permute-start | bytes 294920 | tf_op jit(solution)/shard_map/ppermute | solution.py:455
  9.1 3.6 %project.3 = (f32[16,1024]{1,0:T(8,128)S(1)}, bf16[1024,1024]{1,0:T(8,128)(2,1)S(1)}, bf16[1024,1024]{1,0:T(8,128)(2,1)S(1)}, f32[16,1280]{1,0:T(8,128)}) custom-call(f32[16,1280]{1,0:T(8,128)S(1)} %collective-permute-done.below_ref.above_ref.stack_ref, f32[2,1024]{1,0:T(2,128)S(1)} %get-tuple-element.21.knots_ref), custom_call_target="tpu_custom_call" | custom-call | flops 2936012800 | bytes 4194304 | tf_op jit(solution)/shard_map/project/pallas_call | solution.py:220
  12.8 0.0 copy-start
  12.8 0.0 copy-start.1
  12.8 0.1 collective-permute-start.5
  12.9 2.0 %collective-permute-start.4 = (f32[16,1024]{1,0:T(8,128)S(1)}, f32[16,1024]{1,0:T(8,128)S(1)}, u32[]{:S(2)}, u32[]{:S(2)}) collective-permute-start(f32[16,1024]{1,0:T(8,128)S(1)} %add.11.rest_0_.refs_0_), channel_id=1, source_target_pairs={{0,4},{2,6},{4,0},{6,2},{8,12},{10,14},{12,8},{14,10},{16,20},{18,... | collective-permute-start | bytes 196616 | tf_op jit(solution)/shard_map/ppermute | solution.py:432
  14.8 1.5 %collective-permute-start.3 = (f32[16,1024]{1,0:T(8,128)S(1)}, f32[16,1024]{1,0:T(8,128)S(1)}, u32[]{:S(2)}, u32[]{:S(2)}) collective-permute-start(f32[16,1024]{1,0:T(8,128)S(1)} %add.11.rest_0_.refs_0_), channel_id=1, source_target_pairs={{0,6},{2,4},{4,2},{6,0},{8,14},{10,12},{12,10},{14,8},{16,22},{18,... | collective-permute-start | bytes 196616 | tf_op jit(solution)/shard_map/ppermute | solution.py:432
  16.3 0.0 slice-done
  16.3 0.0 slice-done.1
  16.3 0.6 %split.2 = (bf16[512,2048]{1,0:T(8,128)(2,1)S(1)}, bf16[512,2048]{1,0:T(8,128)(2,1)S(1)}) custom-call(f32[1024,2048]{1,0:T(8,128)S(1)} %bitcast.1, f32[16,1024]{1,0:T(8,128)S(1)} %add.11.rest_0_.refs_0_), custom_call_target="tpu_custom_call" | custom-call | flops 62914560 | bytes 4194304 | tf_op jit(solution)/shard_map/split/pallas_call | solution.py:251
  16.9 0.0 collective-permute-done.2.west_ref
  16.9 0.0 collective-permute-done.1.east_ref
  17.0 0.1 assemble.1
  17.0 0.0 copy-done
  17.0 0.0 copy-done.1
  17.0 2.4 %taper.2.refs_4_ = f32[16,512]{1,0:T(8,128)S(1)} custom-call(s32[8,8]{1,0:T(8,128)S(1)} %copy-done, s32[8]{0:T(128)S(1)} %copy-done.1, f32[16,1280]{1,0:T(8,128)S(1)} %get-tuple-element.22.own_ref, bf16[32,3968]{1,0:T(8,128)(2,1)S(1)} %get-tuple-element.23.values_ref, f32[2,3840]{1,0:T(2,128)S(1)} %get-tuple-element.24.coords_ref, ...), custom_call_target="tpu_custom_call" | custom-call | flops 262144000 | bytes 2097152 | tf_op jit(solution)/shard_map/taper/pallas_call | solution.py:386
  19.4 0.0 collective-permute-done.5.refs_3_
  19.5 0.0 collective-permute-done.4.refs_2_
  19.5 0.5 %collective-permute-done.3.refs_1_ = f32[16,1024]{1,0:T(8,128)S(1)} collective-permute-done((f32[16,1024]{1,0:T(8,128)S(1)}, f32[16,1024]{1,0:T(8,128)S(1)}, u32[]{:S(2)}, u32[]{:S(2)}) %collective-permute-start.3) | collective-permute-done | bytes 65568 | tf_op jit(solution)/shard_map/ppermute | solution.py:432
  20.0 1.6 %collective-permute-start.8 = (f32[16,1024]{1,0:T(8,128)S(1)}, f32[16,1024]{1,0:T(8,128)S(1)}, u32[]{:S(2)}, u32[]{:S(2)}) collective-permute-start(f32[16,1024]{1,0:T(8,128)S(1)} %add.18.rest_0_.refs_0_), channel_id=1, source_target_pairs={{0,8},{2,10},{4,12},{6,14},{8,0},{10,2},{12,4},{14,6},{16,24},{18,... | collective-permute-start | bytes 196616 | tf_op jit(solution)/shard_map/ppermute | solution.py:432
  21.7 2.6 %collective-permute-start.7 = (f32[16,1024]{1,0:T(8,128)S(1)}, f32[16,1024]{1,0:T(8,128)S(1)}, u32[]{:S(2)}, u32[]{:S(2)}) collective-permute-start(f32[16,1024]{1,0:T(8,128)S(1)} %add.18.rest_0_.refs_0_), channel_id=1, source_target_pairs={{0,16},{2,18},{4,20},{6,22},{8,24},{10,26},{12,28},{14,30},{16,0},... | collective-permute-start | bytes 196616 | tf_op jit(solution)/shard_map/ppermute | solution.py:432
  24.3 0.2 collective-permute-start.6
  24.5 0.6 %split.3 = (bf16[512,2048]{1,0:T(8,128)(2,1)S(1)}, bf16[512,2048]{1,0:T(8,128)(2,1)S(1)}) custom-call(f32[1024,2048]{1,0:T(8,128)S(1)} %bitcast.1, f32[16,1024]{1,0:T(8,128)S(1)} %add.18.rest_0_.refs_0_), custom_call_target="tpu_custom_call" | custom-call | flops 62914560 | bytes 4194304 | tf_op jit(solution)/shard_map/split/pallas_call | solution.py:251
  25.1 2.4 %taper.3.refs_4_ = f32[16,512]{1,0:T(8,128)S(1)} custom-call(s32[8,8]{1,0:T(8,128)S(1)} %copy-done, s32[8]{0:T(128)S(1)} %copy-done.1, f32[16,1280]{1,0:T(8,128)S(1)} %get-tuple-element.22.own_ref, bf16[32,3968]{1,0:T(8,128)(2,1)S(1)} %get-tuple-element.23.values_ref, f32[2,3840]{1,0:T(2,128)S(1)} %get-tuple-element.24.coords_ref, ...), custom_call_target="tpu_custom_call" | custom-call | flops 262144000 | bytes 2097152 | tf_op jit(solution)/shard_map/taper/pallas_call | solution.py:386
  27.5 0.0 collective-permute-done.8.refs_3_
  27.5 0.0 collective-permute-done.7.refs_2_
  27.5 2.8 %collective-permute-done.6.refs_1_ = f32[16,1024]{1,0:T(8,128)S(1)} collective-permute-done((f32[16,1024]{1,0:T(8,128)S(1)}, f32[16,1024]{1,0:T(8,128)S(1)}, u32[]{:S(2)}, u32[]{:S(2)}) %collective-permute-start.6) | collective-permute-done | bytes 65568 | tf_op jit(solution)/shard_map/ppermute | solution.py:432
  30.3 0.1 collective-permute-start.9
  30.4 1.3 %factor.2.before_ref = f32[16,1024]{1,0:T(8,128)S(1)} custom-call(f32[16,1024]{1,0:T(8,128)S(1)} %add.19.proj_ref, bf16[512,2048]{1,0:T(8,128)(2,1)S(1)} %get-tuple-element.27.refs_5_.rest_0_, bf16[512,2048]{1,0:T(8,128)(2,1)S(1)} %get-tuple-element.29.refs_5_.rest_1_, bf16[512,2048]{1,0:T(8,128)(2,1)S(1)} %get-tuple-element.28.refs_6_.rest_2_, ...), custom_call_target="tpu_custom_call" | custom-call | flops 1048576000 | bytes 4194304 | tf_op jit(solution)/shard_map/factor/pallas_call | solution.py:292
  31.7 0.0 collective-permute-done.9.proj_ref
  31.7 1.3 %factor.3.factor_ref = f32[16,1024]{1,0:T(8,128)S(1)} custom-call(f32[16,1024]{1,0:T(8,128)S(1)} %factor.2.before_ref, f32[16,1024]{1,0:T(8,128)S(1)} %collective-permute-done.9.proj_ref, bf16[512,2048]{1,0:T(8,128)(2,1)S(1)} %get-tuple-element.27.refs_5_.rest_0_, bf16[512,2048]{1,0:T(8,128)(2,1)S(1)} %get-tuple-element.29.refs_5_.rest_1_, ...), custom_call_target="tpu_custom_call" | custom-call | flops 1048576000 | bytes 4194304 | tf_op jit(solution)/shard_map/factor/pallas_call | solution.py:292
  33.0 0.8 %spread.2 = f32[16,1024]{1,0:T(8,128)S(1)} custom-call(f32[16,1024]{1,0:T(8,128)S(1)} %factor.3.factor_ref, bf16[1024,1024]{1,0:T(8,128)(2,1)S(1)} %get-tuple-element.31.high_ref, bf16[1024,1024]{1,0:T(8,128)(2,1)S(1)} %get-tuple-element.32.low_ref), custom_call_target="tpu_custom_call" | custom-call | flops 891289600 | bytes 4194304 | tf_op jit(solution)/shard_map/spread/pallas_call | solution.py:317
  33.8 0.5 %collective-permute-start.10 = (f32[16,1024]{1,0:T(8,128)S(1)}, f32[16,1024]{1,0:T(8,128)S(1)}, u32[]{:S(2)}, u32[]{:S(2)}) collective-permute-start(f32[16,1024]{1,0:T(8,128)S(1)} %spread.2), channel_id=1, source_target_pairs={{1,0},{0,1},{3,2},{2,3},{5,4},{4,5},{7,6},{6,7},{9,8},{8,9},{11,10... | collective-permute-start | bytes 196616 | tf_op jit(solution)/shard_map/ppermute | solution.py:440
  34.3 0.8 %spread.3 = f32[16,1024]{1,0:T(8,128)S(1)} custom-call(f32[16,1024]{1,0:T(8,128)S(1)} %factor.3.factor_ref, bf16[1024,1024]{1,0:T(8,128)(2,1)S(1)} %get-tuple-element.33.high_ref, bf16[1024,1024]{1,0:T(8,128)(2,1)S(1)} %get-tuple-element.34.low_ref), custom_call_target="tpu_custom_call" | custom-call | flops 891289600 | bytes 4194304 | tf_op jit(solution)/shard_map/spread/pallas_call | solution.py:317
  35.1 0.1 collective-permute-done.10
  35.2 0.6 %fusion = f32[16,1024]{1,0:T(8,128)} fusion(f32[16,1024]{1,0:T(8,128)S(1)} %spread.3, f32[16,1024]{1,0:T(8,128)S(1)} %collective-permute-done.10, f32[16,512]{1,0:T(8,128)S(1)} %taper.3.refs_4_, f32[16,512]{1,0:T(8,128)S(1)} %taper.2.refs_4_), kind=kLoop, calls=%fused_computation.1 | loop fusion | flops 49152 | bytes 262144 | tf_op jit(solution)/shard_map/add | solution.py:505
  (5 shorter events, 0.1 us)
Async XLA Ops:
  0.9 4.1 %collective-permute-start = (f32[16,1280]{1,0:T(8,128)S(1)}, f32[16,1280]{1,0:T(8,128)S(1)}, u32[]{:S(2)}, u32[]{:S(2)}) collective-permute-start(f32[16,1280]{1,0:T(8,128)S(1)} %get-tuple-element.20.stack_ref), channel_id=1, source_target_pairs={{1,0},{0,1},{3,2},{2,3},{5,4},{4,5},{7,6},{6,7},{9,8},{8,9},{11,10... | collective-permute-start | bytes 245768 | tf_op jit(solution)/shard_map/ppermute | solution.py:440
  1.4 14.9 %slice-start = ((s8[8388608]{0:T(1024)(128)(4,1)}), s8[4194304]{0:T(1024)(128)(4,1)S(1)}, s32[]{:S(2)}) async-start(s8[8388608]{0:T(1024)(128)(4,1)} %bitcast), calls=%async_computation | async-start | bytes 8388608
  5.0 11.3 %slice-start.1 = ((s8[8388608]{0:T(1024)(128)(4,1)}), s8[4194304]{0:T(1024)(128)(4,1)S(1)}, s32[]{:S(2)}) async-start(s8[8388608]{0:T(1024)(128)(4,1)} %bitcast), calls=%async_computation.1 | async-start | bytes 8388608
  5.1 11.9 %collective-permute-start.2 = (f32[16,1536]{1,0:T(8,128)S(1)}, f32[16,1536]{1,0:T(8,128)S(1)}, u32[]{:S(2)}, u32[]{:S(2)}) collective-permute-start(f32[16,1536]{1,0:T(8,128)S(1)} %strip.1.own_ref), channel_id=1, source_target_pairs={{0,1},{1,0},{2,4},{3,5},{4,2},{5,3},{6,8},{7,9},{8,6},{9,7},{10,12... | collective-permute-start | bytes 294920 | tf_op jit(solution)/shard_map/ppermute | solution.py:455
  5.2 11.8 %collective-permute-start.1 = (f32[16,1536]{1,0:T(8,128)S(1)}, f32[16,1536]{1,0:T(8,128)S(1)}, u32[]{:S(2)}, u32[]{:S(2)}) collective-permute-start(f32[16,1536]{1,0:T(8,128)S(1)} %strip.1.own_ref), channel_id=1, source_target_pairs={{0,2},{1,3},{2,0},{3,1},{4,6},{5,7},{6,4},{7,5},{8,10},{9,11},{10,... | collective-permute-start | bytes 294920 | tf_op jit(solution)/shard_map/ppermute | solution.py:455
  12.8 4.3 %copy-start = (s32[8,8]{1,0:T(8,128)S(1)}, s32[8,8]{1,0:T(8,128)}, u32[]{:S(2)}) copy-start(s32[8,8]{1,0:T(8,128)} %ids_ref.3) | copy-start | bytes 772
  12.8 4.3 %copy-start.1 = (s32[8]{0:T(128)S(1)}, s32[8]{0:T(128)}, u32[]{:S(2)}) copy-start(s32[8]{0:T(128)} %counts_ref.3) | copy-start | bytes 100
  12.8 6.7 %collective-permute-start.5 = (f32[16,1024]{1,0:T(8,128)S(1)}, f32[16,1024]{1,0:T(8,128)S(1)}, u32[]{:S(2)}, u32[]{:S(2)}) collective-permute-start(f32[16,1024]{1,0:T(8,128)S(1)} %add.11.rest_0_.refs_0_), channel_id=1, source_target_pairs={{0,2},{2,0},{4,6},{6,4},{8,10},{10,8},{12,14},{14,12},{16,18},{18,... | collective-permute-start | bytes 196616 | tf_op jit(solution)/shard_map/ppermute | solution.py:432
  12.9 6.6 %collective-permute-start.4 = (f32[16,1024]{1,0:T(8,128)S(1)}, f32[16,1024]{1,0:T(8,128)S(1)}, u32[]{:S(2)}, u32[]{:S(2)}) collective-permute-start(f32[16,1024]{1,0:T(8,128)S(1)} %add.11.rest_0_.refs_0_), channel_id=1, source_target_pairs={{0,4},{2,6},{4,0},{6,2},{8,12},{10,14},{12,8},{14,10},{16,20},{18,... | collective-permute-start | bytes 196616 | tf_op jit(solution)/shard_map/ppermute | solution.py:432
  14.8 5.2 %collective-permute-start.3 = (f32[16,1024]{1,0:T(8,128)S(1)}, f32[16,1024]{1,0:T(8,128)S(1)}, u32[]{:S(2)}, u32[]{:S(2)}) collective-permute-start(f32[16,1024]{1,0:T(8,128)S(1)} %add.11.rest_0_.refs_0_), channel_id=1, source_target_pairs={{0,6},{2,4},{4,2},{6,0},{8,14},{10,12},{12,10},{14,8},{16,22},{18,... | collective-permute-start | bytes 196616 | tf_op jit(solution)/shard_map/ppermute | solution.py:432
  20.0 7.5 %collective-permute-start.8 = (f32[16,1024]{1,0:T(8,128)S(1)}, f32[16,1024]{1,0:T(8,128)S(1)}, u32[]{:S(2)}, u32[]{:S(2)}) collective-permute-start(f32[16,1024]{1,0:T(8,128)S(1)} %add.18.rest_0_.refs_0_), channel_id=1, source_target_pairs={{0,8},{2,10},{4,12},{6,14},{8,0},{10,2},{12,4},{14,6},{16,24},{18,... | collective-permute-start | bytes 196616 | tf_op jit(solution)/shard_map/ppermute | solution.py:432
  21.7 5.9 %collective-permute-start.7 = (f32[16,1024]{1,0:T(8,128)S(1)}, f32[16,1024]{1,0:T(8,128)S(1)}, u32[]{:S(2)}, u32[]{:S(2)}) collective-permute-start(f32[16,1024]{1,0:T(8,128)S(1)} %add.18.rest_0_.refs_0_), channel_id=1, source_target_pairs={{0,16},{2,18},{4,20},{6,22},{8,24},{10,26},{12,28},{14,30},{16,0},... | collective-permute-start | bytes 196616 | tf_op jit(solution)/shard_map/ppermute | solution.py:432
  24.3 6.1 %collective-permute-start.6 = (f32[16,1024]{1,0:T(8,128)S(1)}, f32[16,1024]{1,0:T(8,128)S(1)}, u32[]{:S(2)}, u32[]{:S(2)}) collective-permute-start(f32[16,1024]{1,0:T(8,128)S(1)} %add.18.rest_0_.refs_0_), channel_id=1, source_target_pairs={{0,24},{2,26},{4,28},{6,30},{8,16},{10,18},{12,20},{14,22},{16,8},... | collective-permute-start | bytes 196616 | tf_op jit(solution)/shard_map/ppermute | solution.py:432
  30.3 1.4 %collective-permute-start.9 = (f32[16,1024]{1,0:T(8,128)S(1)}, f32[16,1024]{1,0:T(8,128)S(1)}, u32[]{:S(2)}, u32[]{:S(2)}) collective-permute-start(f32[16,1024]{1,0:T(8,128)S(1)} %add.19.proj_ref), channel_id=1, source_target_pairs={{1,0},{0,1},{3,2},{2,3},{5,4},{4,5},{7,6},{6,7},{9,8},{8,9},{11,10... | collective-permute-start | bytes 196616 | tf_op jit(solution)/shard_map/ppermute | solution.py:440
  33.8 1.4 %collective-permute-start.10 = (f32[16,1024]{1,0:T(8,128)S(1)}, f32[16,1024]{1,0:T(8,128)S(1)}, u32[]{:S(2)}, u32[]{:S(2)}) collective-permute-start(f32[16,1024]{1,0:T(8,128)S(1)} %spread.2), channel_id=1, source_target_pairs={{1,0},{0,1},{3,2},{2,3},{5,4},{4,5},{7,6},{6,7},{9,8},{8,9},{11,10... | collective-permute-start | bytes 196616 | tf_op jit(solution)/shard_map/ppermute | solution.py:440

commit v13 on v11

--- a/solution.py
+++ b/solution.py
@@ -394,17 +394,25 @@
     )(ids, counts, own, values, coords, *after)
 
 
-def add_kernel(count, *refs):
-    total = refs[0][...]
-    for ref in refs[1:count]:
-        total = total + ref[...]
-    refs[-1][...] = total
-
-
-def add_all(values, after):
-    return pl.pallas_call(
-        functools.partial(add_kernel, len(values)),
-        out_shape=jax.ShapeDtypeStruct(values[0].shape, jnp.float32),
+def add_kernel(count, copies, *refs):
+    if count:
+        total = refs[0][...]
+        for ref in refs[1:count]:
+            total = total + ref[...]
+    else:
+        total = jnp.sum(refs[0][...], axis=0)
+    if copies:
+        for index in range(copies):
+            refs[-1][index] = total
+    else:
+        refs[-1][...] = total
+
+
+def add_all(values, after, copies):
+    shape = values[0].shape[-2:]
+    return pl.pallas_call(
+        functools.partial(add_kernel, len(values) if values[0].ndim == 2 else 0, copies),
+        out_shape=jax.ShapeDtypeStruct((copies, *shape) if copies else shape, jnp.float32),
         in_specs=[VMEM] * len(values) + [ANY] * len(after),
         out_specs=VMEM,
         compiler_params=pltpu.CompilerParams(vmem_limit_bytes=LIMIT),
@@ -415,22 +423,19 @@
 def butterfly_rounds(count):
     assert count & (count - 1) == 0
     bits = [1 << i for i in range(count.bit_length() - 1)]
-    rounds = [(low | high, high, low) for low, high in zip(bits[0::2], bits[1::2])]
-    return rounds + [(bit,) for bit in bits[len(rounds) * 2 :]]
-
-
-def butterfly_round(value, axis, other, turn):
-    count, groups = lax.axis_size(axis), lax.axis_size(other)
+    return [tuple(bits[i : i + 2]) for i in range(0, len(bits), 2)]
+
+
+def round_groups(count, groups, turn):
     rounds = butterfly_rounds(count)
     half = len(rounds) // 2 if len({len(steps) for steps in rounds}) == 1 else 0
-    got = []
-    for kind in range(len(rounds[turn])):
-        pairs = []
-        for j in range(groups):
-            step = rounds[(turn + half * (j % 2)) % len(rounds)][kind]
-            pairs += [(i * groups + j, (i ^ step) * groups + j) for i in range(count)]
-        got.append(lax.ppermute(value, (axis, other), pairs))
-    return got
+    found = []
+    for j in range(groups):
+        members = [0]
+        for step in rounds[(turn + half * (j % 2)) % len(rounds)]:
+            members += [member | step for member in members]
+        found += [[(i | m) * groups + j for m in members] for i in range(count) if not i & members[-1]]
+    return found
 
 
 def shifted(value, axis, step):
@@ -473,15 +478,18 @@
 
     strip = make_strip(chunks[-1], stack, chunks[1 % groups])
     values, coords = assemble([strip, paired(strip, "space", "knot", 0), paired(strip, "space", "knot", 1)], extent)
-    projection = sum(part[0] for part in parts)
-    rounds = len(butterfly_rounds(lax.axis_size("space")))
+    space, rounds = lax.axis_size("space"), len(butterfly_rounds(lax.axis_size("space")))
+    sizes = [1 << len(steps) for steps in butterfly_rounds(space)]
+    projection = add_all([part[0] for part in parts], [], sizes[0])
     pieces = math.gcd(own_blocks, rounds)
     per_piece = own_blocks // pieces
     row_pieces = math.gcd(knot_precision.shape[0] // LANES, rounds)
     per_split = knot_precision.shape[0] // row_pieces
     base, splits = [], []
     for turn in range(rounds):
-        got = butterfly_round(projection, "space", "knot", turn)
+        got = lax.all_to_all(
+            projection, ("space", "knot"), 0, 0, axis_index_groups=round_groups(space, groups, turn), tiled=True
+        )
         beside = []
         for i in range(pieces):
             if i * rounds // pieces == turn:
@@ -495,7 +503,7 @@
             if i * rounds // row_pieces == turn:
                 splits.append(split_rows(knot_precision, i * per_split, per_split, [projection]))
                 beside.extend(splits[-1])
-        projection = add_all([projection, *got], beside)
+        projection = add_all([got], beside, sizes[turn + 1] if turn + 1 < rounds else 0)
     factor = factored(None, projection, splits, proj_scale, 0)
     for step in range(1, groups):
         factor = factored(factor, shifted(projection, "knot", step), splits, proj_scale, step)

time: 35.5 us -> 59.3 us (1.67)
  local copies, waits for them, and re-layouts: 0.04 us -> 24.3 us
  waiting for transfers between devices: 3.39 us -> 0.51 us
  Pallas kernels: 17.9 us -> 19.3 us
  starting transfers between devices: 13.2 us -> 13.8 us
    unnamed x8 -> x38, local copies, waits for them, and re-layouts: 0.04 us -> 24.3 us
    all_to_all x0 -> x2, starting transfers between devices: none -> 9.61 us  [shards(): lax.all_to_all(projection, ('space', 'knot'), 0, 0, axis_index_groups=rou...]
    ppermute x6 -> x0, starting transfers between devices: 8 us -> none  [butterfly_round(): got.append(lax.ppermute(value, (axis, other), pairs))]
    ppermute x6 -> x0, waiting for transfers between devices: 3.38 us -> none  [butterfly_round(): got.append(lax.ppermute(value, (axis, other), pairs))]
    pallas_call x2 -> x3, Pallas kernels: 0.04 us -> 1.5 us  [add_all(): pl.pallas_call(functools.partial(add_kernel, len(values) if values[0].ndi...]
  transfers between devices with their start and end apart: 11 -> 7, of which waited for: 2 -> 1; matrix products, arithmetic and copies ran while one was open for 0% -> 0% of each run, Pallas kernels for 41% -> 20%
where the time goes in v13:
time: 59.3 us; the launch traced here: 58.8 us
  local copies, waits for them, and re-layouts  24.3 us (41%)
  Pallas kernels  19.3 us (33%)
  starting transfers between devices  13.8 us (23%)
  other arithmetic  0.67 us (1%)
    unnamed x38, local copies, waits for them, and re-layouts  24.3 us
    all_to_all x2, starting transfers between devices, shards(): lax.all_to_all(projection, ('space', 'knot'), 0, 0, axis_index_groups=rou...  9.61 us
    pallas_call x2, Pallas kernels, project(): pl.pallas_call(functools.partial(project_kernel, scale, grain_of(scale *...  5.76 us
    pallas_call x2, Pallas kernels, taper(): pl.pallas_call(functools.partial(taper_kernel, first, grain_of(TAPER_RATE...  4.8 us
    ppermute x2, starting transfers between devices, paired(): return lax.ppermute(value, (axis, other), pairs)  3.55 us
    pallas_call x2, Pallas kernels, factored(): pl.pallas_call(kernel, out_shape=jax.ShapeDtypeStruct((probes, rows), jnp...  2.58 us
    pallas_call x2, Pallas kernels, spread(): pl.pallas_call(functools.partial(spread_kernel, scale), out_shape=jax.Sha...  2.54 us
    pallas_call x3, Pallas kernels, add_all(): pl.pallas_call(functools.partial(add_kernel, len(values) if values[0].ndi...  1.5 us
  transfers between devices with their start and end apart: 7, of which 1 were waited for; matrix products, arithmetic and copies ran while one was open for 0% of the time, Pallas kernels for 20%

profile of v13, /device:TPU:0, one launch (start us, length us, event | category | flops | bytes accessed | tf_op | source)
XLA Modules:
  0.0 58.8 jit_solution(1618121170864124944)
XLA Ops:
  0.0 0.9 %prepare.1 = (f32[16,1280]{1,0:T(8,128)S(1)}, f32[2,1024]{1,0:T(2,128)S(1)}) custom-call(f32[16,1024]{1,0:T(8,128)} %probes_ref.1, f32[2,1024]{1,0:T(2,128)} %locations_ref.1, f32[2,1024]{1,0:T(2,128)} %knots_ref.1), custom_call_target="tpu_custom_call" | custom-call | tf_op jit(solution)/shard_map/prepare/pallas_call | solution.py:100
  0.9 0.5 collective-permute-start
  1.4 2.9 %project.2 = (f32[16,1024]{1,0:T(8,128)S(1)}, bf16[1024,1024]{1,0:T(8,128)(2,1)S(1)}, bf16[1024,1024]{1,0:T(8,128)(2,1)S(1)}, f32[16,1280]{1,0:T(8,128)S(1)}) custom-call(f32[16,1280]{1,0:T(8,128)S(1)} %get-tuple-element.20.stack_ref, f32[2,1024]{1,0:T(2,128)S(1)} %get-tuple-element.21.knots_ref), custom_call_target="tpu_custom_call" | custom-call | flops 2936012800 | bytes 4194304 | tf_op jit(solution)/shard_map/project/pallas_call | solution.py:220
  4.3 1.4 %copy-done.9 = bf16[1024,1024]{1,0:T(8,128)(2,1)} copy-done((bf16[1024,1024]{1,0:T(8,128)(2,1)}, bf16[1024,1024]{1,0:T(8,128)(2,1)S(1)}, u32[]{:S(2)}) %copy-start.9) | copy-done | bytes 2097176
  5.7 1.3 %copy-done.11 = bf16[1024,1024]{1,0:T(8,128)(2,1)} copy-done((bf16[1024,1024]{1,0:T(8,128)(2,1)}, bf16[1024,1024]{1,0:T(8,128)(2,1)S(1)}, u32[]{:S(2)}) %copy-start.11) | copy-done | bytes 2097176
  7.0 0.0 collective-permute-done.below_ref.above_ref.stack_ref
  7.0 2.9 %project.3 = (f32[16,1024]{1,0:T(8,128)S(1)}, bf16[1024,1024]{1,0:T(8,128)(2,1)S(1)}, bf16[1024,1024]{1,0:T(8,128)(2,1)S(1)}, f32[16,1280]{1,0:T(8,128)}) custom-call(f32[16,1280]{1,0:T(8,128)S(1)} %collective-permute-done.below_ref.above_ref.stack_ref, f32[2,1024]{1,0:T(2,128)S(1)} %get-tuple-element.21.knots_ref), custom_call_target="tpu_custom_call" | custom-call | flops 2936012800 | bytes 4194304 | tf_op jit(solution)/shard_map/project/pallas_call | solution.py:220
  9.9 1.4 %copy-done.13 = bf16[1024,1024]{1,0:T(8,128)(2,1)} copy-done((bf16[1024,1024]{1,0:T(8,128)(2,1)}, bf16[1024,1024]{1,0:T(8,128)(2,1)S(1)}, u32[]{:S(2)}) %copy-start.13) | copy-done | bytes 2097176
  11.3 1.4 %copy-done.15 = bf16[1024,1024]{1,0:T(8,128)(2,1)} copy-done((bf16[1024,1024]{1,0:T(8,128)(2,1)}, bf16[1024,1024]{1,0:T(8,128)(2,1)S(1)}, u32[]{:S(2)}) %copy-start.15) | copy-done | bytes 2097176
  12.7 0.7 %add.15.rest_0_ = f32[4,16,1024]{2,1,0:T(8,128)} custom-call(f32[16,1024]{1,0:T(8,128)S(1)} %get-tuple-element.25.refs_0_, f32[16,1024]{1,0:T(8,128)S(1)} %get-tuple-element.26.refs_1_), custom_call_target="tpu_custom_call" | custom-call | tf_op jit(solution)/shard_map/add/pallas_call | solution.py:413
  13.4 4.7 %all-to-all-start = ((f32[4,16,1024]{2,1,0:T(8,128)}), f32[4,16,1024]{2,1,0:T(8,128)S(1)}, u32[]{:S(2)}, u32[]{:S(2)}) async-start(f32[4,16,1024]{2,1,0:T(8,128)} %add.15.rest_0_), calls=%async_computation | async-start | bytes 524288 | tf_op jit(solution)/shard_map/all_to_all | solution.py:490
  18.2 1.4 %collective-permute-start.2 = (f32[16,1536]{1,0:T(8,128)S(1)}, f32[16,1536]{1,0:T(8,128)S(1)}, u32[]{:S(2)}, u32[]{:S(2)}) collective-permute-start(f32[16,1536]{1,0:T(8,128)S(1)} %strip.1.own_ref), channel_id=1, source_target_pairs={{0,1},{1,0},{2,4},{3,5},{4,2},{5,3},{6,8},{7,9},{8,6},{9,7},{10,12... | collective-permute-start | bytes 294920 | tf_op jit(solution)/shard_map/ppermute | solution.py:460
  19.6 2.1 %collective-permute-start.1 = (f32[16,1536]{1,0:T(8,128)S(1)}, f32[16,1536]{1,0:T(8,128)S(1)}, u32[]{:S(2)}, u32[]{:S(2)}) collective-permute-start(f32[16,1536]{1,0:T(8,128)S(1)} %strip.1.own_ref), channel_id=1, source_target_pairs={{0,2},{1,3},{2,0},{3,1},{4,6},{5,7},{6,4},{7,5},{8,10},{9,11},{10,... | collective-permute-start | bytes 294920 | tf_op jit(solution)/shard_map/ppermute | solution.py:460
  21.7 3.4 %copy-done = f32[1024,2048]{1,0:T(8,128)S(1)} copy-done((f32[1024,2048]{1,0:T(8,128)S(1)}, f32[1024,2048]{1,0:T(8,128)}, u32[]{:S(2)}) %copy-start) | copy-done | bytes 8388632
  25.1 0.6 %split.2 = (bf16[512,2048]{1,0:T(8,128)(2,1)S(1)}, bf16[512,2048]{1,0:T(8,128)(2,1)S(1)}) custom-call(f32[1024,2048]{1,0:T(8,128)S(1)} %copy-done, f32[4,16,1024]{2,1,0:T(8,128)} %add.15.rest_0_), custom_call_target="tpu_custom_call" | custom-call | flops 62914560 | bytes 4194304 | tf_op jit(solution)/shard_map/split/pallas_call | solution.py:248
  25.7 0.0 copy-start.2
  25.7 1.3 %copy-done.2 = bf16[512,2048]{1,0:T(8,128)(2,1)} copy-done((bf16[512,2048]{1,0:T(8,128)(2,1)}, bf16[512,2048]{1,0:T(8,128)(2,1)S(1)}, u32[]{:S(2)}) %copy-start.2) | copy-done | bytes 2097176
  27.0 0.0 collective-permute-done.2.west_ref
  27.0 0.5 collective-permute-done.1.east_ref
  27.5 0.1 assemble.1
  27.6 2.4 %taper.2.refs_1_ = f32[16,512]{1,0:T(8,128)S(1)} custom-call(s32[8,8]{1,0:T(8,128)S(1)} %copy-done.17, s32[8]{0:T(128)S(1)} %copy-done.18, f32[16,1280]{1,0:T(8,128)S(1)} %get-tuple-element.22.own_ref, bf16[32,3968]{1,0:T(8,128)(2,1)S(1)} %get-tuple-element.23.values_ref, f32[2,3840]{1,0:T(2,128)S(1)} %get-tuple-element.24.coords_ref, ...), custom_call_target="tpu_custom_call" | custom-call | flops 262144000 | bytes 2097152 | tf_op jit(solution)/shard_map/taper/pallas_call | solution.py:386
  30.0 0.0 all-to-all-done.refs_0_
  30.0 1.6 %copy-done.3 = bf16[512,2048]{1,0:T(8,128)(2,1)S(1)} copy-done((bf16[512,2048]{1,0:T(8,128)(2,1)S(1)}, bf16[512,2048]{1,0:T(8,128)(2,1)}, u32[]{:S(2)}) %copy-start.3) | copy-done | bytes 2097176
  31.6 0.7 %add.16.rest_0_ = f32[4,16,1024]{2,1,0:T(8,128)} custom-call(f32[4,16,1024]{2,1,0:T(8,128)S(1)} %all-to-all-done.refs_0_, f32[16,512]{1,0:T(8,128)S(1)} %taper.2.refs_1_, bf16[512,2048]{1,0:T(8,128)(2,1)S(1)} %get-tuple-element.27.refs_2_.rest_0_, bf16[512,2048]{1,0:T(8,128)(2,1)S(1)} %copy-done.3), custom_call_target="tpu_custom_call" | custom-call | tf_op jit(solution)/shard_map/add/pallas_call | solution.py:413
  32.4 4.9 %all-to-all-start.1 = ((f32[4,16,1024]{2,1,0:T(8,128)}), f32[4,16,1024]{2,1,0:T(8,128)S(1)}, u32[]{:S(2)}, u32[]{:S(2)}) async-start(f32[4,16,1024]{2,1,0:T(8,128)} %add.16.rest_0_), calls=%async_computation.1 | async-start | bytes 524288 | tf_op jit(solution)/shard_map/all_to_all | solution.py:490
  37.2 3.4 %copy-done.1 = f32[1024,2048]{1,0:T(8,128)S(1)} copy-done((f32[1024,2048]{1,0:T(8,128)S(1)}, f32[1024,2048]{1,0:T(8,128)}, u32[]{:S(2)}) %copy-start.1) | copy-done | bytes 8388632
  40.6 0.6 %split.3 = (bf16[512,2048]{1,0:T(8,128)(2,1)S(1)}, bf16[512,2048]{1,0:T(8,128)(2,1)S(1)}) custom-call(f32[1024,2048]{1,0:T(8,128)S(1)} %copy-done.1, f32[4,16,1024]{2,1,0:T(8,128)} %add.16.rest_0_), custom_call_target="tpu_custom_call" | custom-call | flops 62914560 | bytes 4194304 | tf_op jit(solution)/shard_map/split/pallas_call | solution.py:248
  41.2 1.4 %copy-done.5 = bf16[512,2048]{1,0:T(8,128)(2,1)} copy-done((bf16[512,2048]{1,0:T(8,128)(2,1)}, bf16[512,2048]{1,0:T(8,128)(2,1)S(1)}, u32[]{:S(2)}) %copy-start.5) | copy-done | bytes 2097176
  42.6 1.3 %copy-done.7 = bf16[512,2048]{1,0:T(8,128)(2,1)} copy-done((bf16[512,2048]{1,0:T(8,128)(2,1)}, bf16[512,2048]{1,0:T(8,128)(2,1)S(1)}, u32[]{:S(2)}) %copy-start.7) | copy-done | bytes 2097176
  43.9 2.4 %taper.3.refs_1_ = f32[16,512]{1,0:T(8,128)S(1)} custom-call(s32[8,8]{1,0:T(8,128)S(1)} %copy-done.17, s32[8]{0:T(128)S(1)} %copy-done.18, f32[16,1280]{1,0:T(8,128)S(1)} %get-tuple-element.22.own_ref, bf16[32,3968]{1,0:T(8,128)(2,1)S(1)} %get-tuple-element.23.values_ref, f32[2,3840]{1,0:T(2,128)S(1)} %get-tuple-element.24.coords_ref, ...), custom_call_target="tpu_custom_call" | custom-call | flops 262144000 | bytes 2097152 | tf_op jit(solution)/shard_map/taper/pallas_call | solution.py:386
  46.3 0.0 all-to-all-done.1.refs_0_
  46.3 0.0 copy-start.6
  46.3 1.6 %copy-done.6 = bf16[512,2048]{1,0:T(8,128)(2,1)S(1)} copy-done((bf16[512,2048]{1,0:T(8,128)(2,1)S(1)}, bf16[512,2048]{1,0:T(8,128)(2,1)}, u32[]{:S(2)}) %copy-start.6) | copy-done | bytes 2097176
  47.9 1.6 %copy-done.8 = bf16[512,2048]{1,0:T(8,128)(2,1)S(1)} copy-done((bf16[512,2048]{1,0:T(8,128)(2,1)S(1)}, bf16[512,2048]{1,0:T(8,128)(2,1)}, u32[]{:S(2)}) %copy-start.8) | copy-done | bytes 2097176
  49.5 0.1 collective-permute-start.3
  49.6 1.5 %copy-done.4 = bf16[512,2048]{1,0:T(8,128)(2,1)S(1)} copy-done((bf16[512,2048]{1,0:T(8,128)(2,1)S(1)}, bf16[512,2048]{1,0:T(8,128)(2,1)}, u32[]{:S(2)}) %copy-start.4) | copy-done | bytes 2097176
  51.1 1.3 %factor.2.before_ref = f32[16,1024]{1,0:T(8,128)S(1)} custom-call(f32[16,1024]{1,0:T(8,128)S(1)} %add.17.proj_ref, bf16[512,2048]{1,0:T(8,128)(2,1)S(1)} %get-tuple-element.27.refs_2_.rest_0_, bf16[512,2048]{1,0:T(8,128)(2,1)S(1)} %copy-done.6, bf16[512,2048]{1,0:T(8,128)(2,1)S(1)} %copy-done.4, bf16[512,2048]{1,0:T(8,128)(2,1)S(1)} %copy-done.8), custom_call_target="tpu_custom_call" | custom-call | flops 1048576000 | bytes 4194304 | tf_op jit(solution)/shard_map/factor/pallas_call | solution.py:289
  52.4 0.0 collective-permute-done.3.proj_ref
  52.4 1.3 %factor.3.factor_ref = f32[16,1024]{1,0:T(8,128)S(1)} custom-call(f32[16,1024]{1,0:T(8,128)S(1)} %factor.2.before_ref, f32[16,1024]{1,0:T(8,128)S(1)} %collective-permute-done.3.proj_ref, bf16[512,2048]{1,0:T(8,128)(2,1)S(1)} %get-tuple-element.27.refs_2_.rest_0_, bf16[512,2048]{1,0:T(8,128)(2,1)S(1)} %copy-done.6, bf16[512,2048]{1,0:T(8,128)(2,1)S(1)} %copy-done.4, ...), custom_call_target="tpu_custom_call" | custom-call | flops 1048576000 | bytes 4194304 | tf_op jit(solution)/shard_map/factor/pallas_call | solution.py:289
  53.7 0.3 copy-done.14
  54.0 0.6 %copy-done.16 = bf16[1024,1024]{1,0:T(8,128)(2,1)S(1)} copy-done((bf16[1024,1024]{1,0:T(8,128)(2,1)S(1)}, bf16[1024,1024]{1,0:T(8,128)(2,1)}, u32[]{:S(2)}) %copy-start.16) | copy-done | bytes 2097176
  54.6 1.3 %spread.2 = f32[16,1024]{1,0:T(8,128)S(1)} custom-call(f32[16,1024]{1,0:T(8,128)S(1)} %factor.3.factor_ref, bf16[1024,1024]{1,0:T(8,128)(2,1)S(1)} %copy-done.14, bf16[1024,1024]{1,0:T(8,128)(2,1)S(1)} %copy-done.16), custom_call_target="tpu_custom_call" | custom-call | flops 891289600 | bytes 4194304 | tf_op jit(solution)/shard_map/spread/pallas_call | solution.py:316
  55.9 0.1 collective-permute-start.4
  56.0 0.2 copy-done.10
  56.2 0.6 %copy-done.12 = bf16[1024,1024]{1,0:T(8,128)(2,1)S(1)} copy-done((bf16[1024,1024]{1,0:T(8,128)(2,1)S(1)}, bf16[1024,1024]{1,0:T(8,128)(2,1)}, u32[]{:S(2)}) %copy-start.12) | copy-done | bytes 2097176
  56.8 1.3 %spread.3 = f32[16,1024]{1,0:T(8,128)S(1)} custom-call(f32[16,1024]{1,0:T(8,128)S(1)} %factor.3.factor_ref, bf16[1024,1024]{1,0:T(8,128)(2,1)S(1)} %copy-done.10, bf16[1024,1024]{1,0:T(8,128)(2,1)S(1)} %copy-done.12), custom_call_target="tpu_custom_call" | custom-call | flops 891289600 | bytes 4194304 | tf_op jit(solution)/shard_map/spread/pallas_call | solution.py:316
  58.1 0.0 collective-permute-done.4
  58.1 0.7 %fusion = f32[16,1024]{1,0:T(8,128)} fusion(f32[16,1024]{1,0:T(8,128)S(1)} %spread.3, f32[16,1024]{1,0:T(8,128)S(1)} %collective-permute-done.4, f32[16,512]{1,0:T(8,128)S(1)} %taper.3.refs_1_, f32[16,512]{1,0:T(8,128)S(1)} %taper.2.refs_1_), kind=kLoop, calls=%fused_computation.1 | loop fusion | flops 49152 | bytes 262144 | tf_op jit(solution)/shard_map/add | solution.py:513
  (21 shorter events, 0.1 us)
Async XLA Ops:
  0.9 6.1 %collective-permute-start = (f32[16,1280]{1,0:T(8,128)S(1)}, f32[16,1280]{1,0:T(8,128)S(1)}, u32[]{:S(2)}, u32[]{:S(2)}) collective-permute-start(f32[16,1280]{1,0:T(8,128)S(1)} %get-tuple-element.20.stack_ref), channel_id=1, source_target_pairs={{1,0},{0,1},{3,2},{2,3},{5,4},{4,5},{7,6},{6,7},{9,8},{8,9},{11,10... | collective-permute-start | bytes 245768 | tf_op jit(solution)/shard_map/ppermute | solution.py:445
  4.3 1.4 %copy-start.9 = (bf16[1024,1024]{1,0:T(8,128)(2,1)}, bf16[1024,1024]{1,0:T(8,128)(2,1)S(1)}, u32[]{:S(2)}) copy-start(bf16[1024,1024]{1,0:T(8,128)(2,1)S(1)} %get-tuple-element.33.high_ref) | copy-start | bytes 6291460
  5.7 1.3 %copy-start.11 = (bf16[1024,1024]{1,0:T(8,128)(2,1)}, bf16[1024,1024]{1,0:T(8,128)(2,1)S(1)}, u32[]{:S(2)}) copy-start(bf16[1024,1024]{1,0:T(8,128)(2,1)S(1)} %get-tuple-element.34.low_ref) | copy-start | bytes 6291460
  9.9 1.4 %copy-start.13 = (bf16[1024,1024]{1,0:T(8,128)(2,1)}, bf16[1024,1024]{1,0:T(8,128)(2,1)S(1)}, u32[]{:S(2)}) copy-start(bf16[1024,1024]{1,0:T(8,128)(2,1)S(1)} %get-tuple-element.31.high_ref) | copy-start | bytes 6291460
  11.3 1.4 %copy-start.15 = (bf16[1024,1024]{1,0:T(8,128)(2,1)}, bf16[1024,1024]{1,0:T(8,128)(2,1)S(1)}, u32[]{:S(2)}) copy-start(bf16[1024,1024]{1,0:T(8,128)(2,1)S(1)} %get-tuple-element.32.low_ref) | copy-start | bytes 6291460
  13.4 16.6 %all-to-all-start = ((f32[4,16,1024]{2,1,0:T(8,128)}), f32[4,16,1024]{2,1,0:T(8,128)S(1)}, u32[]{:S(2)}, u32[]{:S(2)}) async-start(f32[4,16,1024]{2,1,0:T(8,128)} %add.15.rest_0_), calls=%async_computation | async-start | bytes 524288 | tf_op jit(solution)/shard_map/all_to_all | solution.py:490
  18.1 9.5 %copy-start.17 = (s32[8,8]{1,0:T(8,128)S(1)}, s32[8,8]{1,0:T(8,128)}, u32[]{:S(2)}) copy-start(s32[8,8]{1,0:T(8,128)} %ids_ref.3) | copy-start | bytes 772
  18.1 9.5 %copy-start.18 = (s32[8]{0:T(128)S(1)}, s32[8]{0:T(128)}, u32[]{:S(2)}) copy-start(s32[8]{0:T(128)} %counts_ref.3) | copy-start | bytes 100
  18.2 8.9 %collective-permute-start.2 = (f32[16,1536]{1,0:T(8,128)S(1)}, f32[16,1536]{1,0:T(8,128)S(1)}, u32[]{:S(2)}, u32[]{:S(2)}) collective-permute-start(f32[16,1536]{1,0:T(8,128)S(1)} %strip.1.own_ref), channel_id=1, source_target_pairs={{0,1},{1,0},{2,4},{3,5},{4,2},{5,3},{6,8},{7,9},{8,6},{9,7},{10,12... | collective-permute-start | bytes 294920 | tf_op jit(solution)/shard_map/ppermute | solution.py:460
  19.6 7.9 %collective-permute-start.1 = (f32[16,1536]{1,0:T(8,128)S(1)}, f32[16,1536]{1,0:T(8,128)S(1)}, u32[]{:S(2)}, u32[]{:S(2)}) collective-permute-start(f32[16,1536]{1,0:T(8,128)S(1)} %strip.1.own_ref), channel_id=1, source_target_pairs={{0,2},{1,3},{2,0},{3,1},{4,6},{5,7},{6,4},{7,5},{8,10},{9,11},{10,... | collective-permute-start | bytes 294920 | tf_op jit(solution)/shard_map/ppermute | solution.py:460
  21.7 3.4 %copy-start = (f32[1024,2048]{1,0:T(8,128)S(1)}, f32[1024,2048]{1,0:T(8,128)}, u32[]{:S(2)}) copy-start(f32[1024,2048]{1,0:T(8,128)} %precision_ref.3) | copy-start | bytes 25165828
  25.7 1.4 %copy-start.2 = (bf16[512,2048]{1,0:T(8,128)(2,1)}, bf16[512,2048]{1,0:T(8,128)(2,1)S(1)}, u32[]{:S(2)}) copy-start(bf16[512,2048]{1,0:T(8,128)(2,1)S(1)} %get-tuple-element.28.refs_3_.rest_2_) | copy-start | bytes 6291460
  30.0 1.6 %copy-start.3 = (bf16[512,2048]{1,0:T(8,128)(2,1)S(1)}, bf16[512,2048]{1,0:T(8,128)(2,1)}, u32[]{:S(2)}) copy-start(bf16[512,2048]{1,0:T(8,128)(2,1)} %copy-done.2) | copy-start | bytes 6291460
  32.4 13.9 %all-to-all-start.1 = ((f32[4,16,1024]{2,1,0:T(8,128)}), f32[4,16,1024]{2,1,0:T(8,128)S(1)}, u32[]{:S(2)}, u32[]{:S(2)}) async-start(f32[4,16,1024]{2,1,0:T(8,128)} %add.16.rest_0_), calls=%async_computation.1 | async-start | bytes 524288 | tf_op jit(solution)/shard_map/all_to_all | solution.py:490
  37.2 3.4 %copy-start.1 = (f32[1024,2048]{1,0:T(8,128)S(1)}, f32[1024,2048]{1,0:T(8,128)}, u32[]{:S(2)}) copy-start(f32[1024,2048]{1,0:T(8,128)} %precision_ref.3) | copy-start | bytes 25165828
  41.2 1.4 %copy-start.5 = (bf16[512,2048]{1,0:T(8,128)(2,1)}, bf16[512,2048]{1,0:T(8,128)(2,1)S(1)}, u32[]{:S(2)}) copy-start(bf16[512,2048]{1,0:T(8,128)(2,1)S(1)} %get-tuple-element.29.refs_2_.rest_1_) | copy-start | bytes 6291460
  42.6 1.3 %copy-start.7 = (bf16[512,2048]{1,0:T(8,128)(2,1)}, bf16[512,2048]{1,0:T(8,128)(2,1)S(1)}, u32[]{:S(2)}) copy-start(bf16[512,2048]{1,0:T(8,128)(2,1)S(1)} %get-tuple-element.30.refs_3_.rest_3_) | copy-start | bytes 6291460
  46.3 1.6 %copy-start.6 = (bf16[512,2048]{1,0:T(8,128)(2,1)S(1)}, bf16[512,2048]{1,0:T(8,128)(2,1)}, u32[]{:S(2)}) copy-start(bf16[512,2048]{1,0:T(8,128)(2,1)} %copy-done.5) | copy-start | bytes 6291460
  47.9 1.6 %copy-start.8 = (bf16[512,2048]{1,0:T(8,128)(2,1)S(1)}, bf16[512,2048]{1,0:T(8,128)(2,1)}, u32[]{:S(2)}) copy-start(bf16[512,2048]{1,0:T(8,128)(2,1)} %copy-done.7) | copy-start | bytes 6291460
  49.5 1.6 %copy-start.4 = (bf16[512,2048]{1,0:T(8,128)(2,1)S(1)}, bf16[512,2048]{1,0:T(8,128)(2,1)}, u32[]{:S(2)}) copy-start(bf16[512,2048]{1,0:T(8,128)(2,1)} %copy-done.2) | copy-start | bytes 6291460
  49.5 2.9 %collective-permute-start.3 = (f32[16,1024]{1,0:T(8,128)S(1)}, f32[16,1024]{1,0:T(8,128)S(1)}, u32[]{:S(2)}, u32[]{:S(2)}) collective-permute-start(f32[16,1024]{1,0:T(8,128)S(1)} %add.17.proj_ref), channel_id=1, source_target_pairs={{1,0},{0,1},{3,2},{2,3},{5,4},{4,5},{7,6},{6,7},{9,8},{8,9},{11,10... | collective-permute-start | bytes 196616 | tf_op jit(solution)/shard_map/ppermute | solution.py:445
  52.4 1.6 %copy-start.14 = (bf16[1024,1024]{1,0:T(8,128)(2,1)S(1)}, bf16[1024,1024]{1,0:T(8,128)(2,1)}, u32[]{:S(2)}) copy-start(bf16[1024,1024]{1,0:T(8,128)(2,1)} %copy-done.13) | copy-start | bytes 6291460
  52.4 2.2 %copy-start.16 = (bf16[1024,1024]{1,0:T(8,128)(2,1)S(1)}, bf16[1024,1024]{1,0:T(8,128)(2,1)}, u32[]{:S(2)}) copy-start(bf16[1024,1024]{1,0:T(8,128)(2,1)} %copy-done.15) | copy-start | bytes 6291460
  54.6 1.6 %copy-start.10 = (bf16[1024,1024]{1,0:T(8,128)(2,1)S(1)}, bf16[1024,1024]{1,0:T(8,128)(2,1)}, u32[]{:S(2)}) copy-start(bf16[1024,1024]{1,0:T(8,128)(2,1)} %copy-done.9) | copy-start | bytes 6291460
  54.6 2.2 %copy-start.12 = (bf16[1024,1024]{1,0:T(8,128)(2,1)S(1)}, bf16[1024,1024]{1,0:T(8,128)(2,1)}, u32[]{:S(2)}) copy-start(bf16[1024,1024]{1,0:T(8,128)(2,1)} %copy-done.11) | copy-start | bytes 6291460
  55.9 2.2 %collective-permute-start.4 = (f32[16,1024]{1,0:T(8,128)S(1)}, f32[16,1024]{1,0:T(8,128)S(1)}, u32[]{:S(2)}, u32[]{:S(2)}) collective-permute-start(f32[16,1024]{1,0:T(8,128)S(1)} %spread.2), channel_id=1, source_target_pairs={{1,0},{0,1},{3,2},{2,3},{5,4},{4,5},{7,6},{6,7},{9,8},{8,9},{11,10... | collective-permute-start | bytes 196616 | tf_op jit(solution)/shard_map/ppermute | solution.py:445

commit v14 on v12

--- a/solution.py
+++ b/solution.py
@@ -184,35 +184,23 @@
     knots, points = high_ref.shape
     probes = stack_ref.shape[0]
     tile = min(TILE, knots)
-    wide = min(TILE, points)
     copy_ref[...] = stack_ref[...]
-    weights[...] = stacked_halves(stack_ref[:, :points])
+    weights[...] = padded_halves(stack_ref[:, :points], weights.shape[0])
     fill = jnp.zeros((6, knots), jnp.float32)
     columns[...] = jnp.transpose(jnp.concatenate([off_grid(knots_ref[...] * scale, grain), fill], axis=0))
     east, north = [on_grid(coordinate_rows(stack_ref, points, axis) * scale, grain) for axis in range(2)]
 
-    @pl.loop(0, knots // tile)
-    def _(step):
-        rows = pl.ds(pl.multiple_of(step * tile, tile), tile)
+    for start in range(0, knots, tile):
+        rows = slice(start, start + tile)
         kx, ky = [columns[rows, axis : axis + 1] for axis in range(2)]
-        total = jnp.zeros((2 * probes, tile), jnp.float32)
-        for start in range(0, points, wide):
-            highs, lows = [], []
-            for lane in range(start, start + wide, LANES):
-                block = lane // LANES
-                dx = east[block : block + 1, :] - kx
-                dy = north[block : block + 1, :] - ky
-                square = dx * dx + dy * dy
-                high, low = halves(jnp.exp2(-(square * lax.rsqrt(square))))
-                high_ref[rows, lane : lane + LANES] = high
-                low_ref[rows, lane : lane + LANES] = low
-                highs.append(high)
-                lows.append(low)
-            part = weights[:, start : start + wide]
-            total = total + (
-                dot_nt(part, jnp.concatenate(highs, axis=1)) + dot_nt(part, jnp.concatenate(lows, axis=1))
-            )
-        out_ref[:, rows] = folded(total)
+        for block in range(points // LANES):
+            lanes = slice(block * LANES, (block + 1) * LANES)
+            dx = east[block : block + 1, :] - kx
+            dy = north[block : block + 1, :] - ky
+            square = dx * dx + dy * dy
+            high_ref[rows, lanes], low_ref[rows, lanes] = halves(jnp.exp2(-(square * lax.rsqrt(square))))
+        total = dot_nt(high_ref[rows, :], weights[...]) + dot_nt(low_ref[rows, :], weights[...])
+        out_ref[:, rows] = folded_columns(total, probes)
 
 
 def project(stack, knot_locs, scale, extent):
@@ -228,7 +216,7 @@
         in_specs=[VMEM, VMEM],
         out_specs=(VMEM, VMEM, VMEM, VMEM),
         scratch_shapes=[
-            pltpu.VMEM((2 * probes, points), jnp.bfloat16),
+            pltpu.VMEM((LANES, points), jnp.bfloat16),
             pltpu.VMEM((knots, 8), jnp.float32),
         ],
         compiler_params=pltpu.CompilerParams(vmem_limit_bytes=LIMIT),

time: 36 us -> 35.3 us (0.981)
  Pallas kernels: 18.3 us -> 17.6 us
    pallas_call x2, Pallas kernels: 7.19 us -> 6.47 us  [project(): pl.pallas_call(functools.partial(project_kernel, scale, grain_of(scale *...]
  transfers between devices with their start and end apart: 11 -> 11, of which waited for: 3 -> 3; matrix products, arithmetic and copies ran while one was open for 0% -> 0% of each run, Pallas kernels for 43% -> 41%
where the time goes in v14:
time: 35.3 us; the launch traced here: 35.1 us
  Pallas kernels  17.6 us (50%)
  starting transfers between devices  13.2 us (37%)
  waiting for transfers between devices  3.53 us (10%)
  other arithmetic  0.65 us (2%)
    ppermute x6, starting transfers between devices, butterfly_round(): got.append(lax.ppermute(value, (axis, other), pairs))  8 us
    pallas_call x2, Pallas kernels, project(): pl.pallas_call(functools.partial(project_kernel, scale, grain_of(scale *...  6.47 us
    pallas_call x2, Pallas kernels, taper(): pl.pallas_call(functools.partial(taper_kernel, first, grain_of(TAPER_RATE...  4.8 us
    ppermute x2, starting transfers between devices, paired(): return lax.ppermute(value, (axis, other), pairs)  4.07 us
    ppermute x6, waiting for transfers between devices, butterfly_round(): got.append(lax.ppermute(value, (axis, other), pairs))  3.38 us
    pallas_call x2, Pallas kernels, factored(): pl.pallas_call(kernel, out_shape=jax.ShapeDtypeStruct((probes, rows), jnp...  2.6 us
    pallas_call x2, Pallas kernels, spread(): pl.pallas_call(functools.partial(spread_kernel, scale), out_shape=jax.Sha...  1.53 us
    pallas_call x2, Pallas kernels, split_rows(): pl.pallas_call(functools.partial(split_kernel, first), out_shape=(pltpu.V...  1.18 us
  transfers between devices with their start and end apart: 11, of which 3 were waited for; matrix products, arithmetic and copies ran while one was open for 0% of the time, Pallas kernels for 41%

profile of v14, /device:TPU:0, one launch (start us, length us, event | category | flops | bytes accessed | tf_op | source)
XLA Modules:
  0.0 35.1 jit_solution(12416531365211297001)
XLA Ops:
  0.0 0.9 %prepare.1 = (f32[16,1280]{1,0:T(8,128)S(1)}, f32[2,1024]{1,0:T(2,128)S(1)}) custom-call(f32[16,1024]{1,0:T(8,128)} %probes_ref.1, f32[2,1024]{1,0:T(2,128)} %locations_ref.1, f32[2,1024]{1,0:T(2,128)} %knots_ref.1), custom_call_target="tpu_custom_call" | custom-call | tf_op jit(solution)/shard_map/prepare/pallas_call | solution.py:100
  0.9 0.5 %collective-permute-start = (f32[16,1280]{1,0:T(8,128)S(1)}, f32[16,1280]{1,0:T(8,128)S(1)}, u32[]{:S(2)}, u32[]{:S(2)}) collective-permute-start(f32[16,1280]{1,0:T(8,128)S(1)} %get-tuple-element.20.stack_ref), channel_id=1, source_target_pairs={{1,0},{0,1},{3,2},{2,3},{5,4},{4,5},{7,6},{6,7},{9,8},{8,9},{11,10... | collective-permute-start | bytes 245768 | tf_op jit(solution)/shard_map/ppermute | solution.py:428
  1.4 0.0 slice-start
  1.4 3.0 %project.2 = (f32[16,1024]{1,0:T(8,128)S(1)}, bf16[1024,1024]{1,0:T(8,128)(2,1)S(1)}, bf16[1024,1024]{1,0:T(8,128)(2,1)S(1)}, f32[16,1280]{1,0:T(8,128)S(1)}) custom-call(f32[16,1280]{1,0:T(8,128)S(1)} %get-tuple-element.20.stack_ref, f32[2,1024]{1,0:T(2,128)S(1)} %get-tuple-element.21.knots_ref), custom_call_target="tpu_custom_call" | custom-call | flops 2936012800 | bytes 4194304 | tf_op jit(solution)/shard_map/project/pallas_call | solution.py:208
  4.4 0.0 collective-permute-done.below_ref.above_ref.stack_ref
  4.4 0.0 slice-start.1
  4.4 0.1 collective-permute-start.2
  4.5 3.9 %collective-permute-start.1 = (f32[16,1536]{1,0:T(8,128)S(1)}, f32[16,1536]{1,0:T(8,128)S(1)}, u32[]{:S(2)}, u32[]{:S(2)}) collective-permute-start(f32[16,1536]{1,0:T(8,128)S(1)} %strip.1.own_ref), channel_id=1, source_target_pairs={{0,2},{1,3},{2,0},{3,1},{4,6},{5,7},{6,4},{7,5},{8,10},{9,11},{10,... | collective-permute-start | bytes 294920 | tf_op jit(solution)/shard_map/ppermute | solution.py:443
  8.5 3.5 %project.3 = (f32[16,1024]{1,0:T(8,128)S(1)}, bf16[1024,1024]{1,0:T(8,128)(2,1)S(1)}, bf16[1024,1024]{1,0:T(8,128)(2,1)S(1)}, f32[16,1280]{1,0:T(8,128)}) custom-call(f32[16,1280]{1,0:T(8,128)S(1)} %collective-permute-done.below_ref.above_ref.stack_ref, f32[2,1024]{1,0:T(2,128)S(1)} %get-tuple-element.21.knots_ref), custom_call_target="tpu_custom_call" | custom-call | flops 2936012800 | bytes 4194304 | tf_op jit(solution)/shard_map/project/pallas_call | solution.py:208
  12.0 0.0 copy-start
  12.0 0.0 copy-start.1
  12.0 0.1 collective-permute-start.5
  12.1 2.0 %collective-permute-start.4 = (f32[16,1024]{1,0:T(8,128)S(1)}, f32[16,1024]{1,0:T(8,128)S(1)}, u32[]{:S(2)}, u32[]{:S(2)}) collective-permute-start(f32[16,1024]{1,0:T(8,128)S(1)} %add.11.rest_0_.refs_0_), channel_id=1, source_target_pairs={{0,4},{2,6},{4,0},{6,2},{8,12},{10,14},{12,8},{14,10},{16,20},{18,... | collective-permute-start | bytes 196616 | tf_op jit(solution)/shard_map/ppermute | solution.py:420
  14.1 1.5 %collective-permute-start.3 = (f32[16,1024]{1,0:T(8,128)S(1)}, f32[16,1024]{1,0:T(8,128)S(1)}, u32[]{:S(2)}, u32[]{:S(2)}) collective-permute-start(f32[16,1024]{1,0:T(8,128)S(1)} %add.11.rest_0_.refs_0_), channel_id=1, source_target_pairs={{0,6},{2,4},{4,2},{6,0},{8,14},{10,12},{12,10},{14,8},{16,22},{18,... | collective-permute-start | bytes 196616 | tf_op jit(solution)/shard_map/ppermute | solution.py:420
  15.6 0.0 slice-done
  15.6 0.0 slice-done.1
  15.6 0.6 %split.2 = (bf16[512,2048]{1,0:T(8,128)(2,1)S(1)}, bf16[512,2048]{1,0:T(8,128)(2,1)S(1)}) custom-call(f32[1024,2048]{1,0:T(8,128)S(1)} %bitcast.1, f32[16,1024]{1,0:T(8,128)S(1)} %add.11.rest_0_.refs_0_), custom_call_target="tpu_custom_call" | custom-call | flops 62914560 | bytes 4194304 | tf_op jit(solution)/shard_map/split/pallas_call | solution.py:239
  16.2 0.0 collective-permute-done.2.west_ref
  16.2 0.0 collective-permute-done.1.east_ref
  16.2 0.1 assemble.1
  16.3 0.0 copy-done
  16.3 0.0 copy-done.1
  16.3 2.4 %taper.2.refs_4_ = f32[16,512]{1,0:T(8,128)S(1)} custom-call(s32[8,8]{1,0:T(8,128)S(1)} %copy-done, s32[8]{0:T(128)S(1)} %copy-done.1, f32[16,1280]{1,0:T(8,128)S(1)} %get-tuple-element.22.own_ref, bf16[32,3968]{1,0:T(8,128)(2,1)S(1)} %get-tuple-element.23.values_ref, f32[2,3840]{1,0:T(2,128)S(1)} %get-tuple-element.24.coords_ref, ...), custom_call_target="tpu_custom_call" | custom-call | flops 262144000 | bytes 2097152 | tf_op jit(solution)/shard_map/taper/pallas_call | solution.py:374
  18.7 0.0 collective-permute-done.5.refs_3_
  18.7 0.0 collective-permute-done.4.refs_2_
  18.7 0.5 %collective-permute-done.3.refs_1_ = f32[16,1024]{1,0:T(8,128)S(1)} collective-permute-done((f32[16,1024]{1,0:T(8,128)S(1)}, f32[16,1024]{1,0:T(8,128)S(1)}, u32[]{:S(2)}, u32[]{:S(2)}) %collective-permute-start.3) | collective-permute-done | bytes 65568 | tf_op jit(solution)/shard_map/ppermute | solution.py:420
  19.3 1.6 %collective-permute-start.8 = (f32[16,1024]{1,0:T(8,128)S(1)}, f32[16,1024]{1,0:T(8,128)S(1)}, u32[]{:S(2)}, u32[]{:S(2)}) collective-permute-start(f32[16,1024]{1,0:T(8,128)S(1)} %add.18.rest_0_.refs_0_), channel_id=1, source_target_pairs={{0,8},{2,10},{4,12},{6,14},{8,0},{10,2},{12,4},{14,6},{16,24},{18,... | collective-permute-start | bytes 196616 | tf_op jit(solution)/shard_map/ppermute | solution.py:420
  20.9 2.6 %collective-permute-start.7 = (f32[16,1024]{1,0:T(8,128)S(1)}, f32[16,1024]{1,0:T(8,128)S(1)}, u32[]{:S(2)}, u32[]{:S(2)}) collective-permute-start(f32[16,1024]{1,0:T(8,128)S(1)} %add.18.rest_0_.refs_0_), channel_id=1, source_target_pairs={{0,16},{2,18},{4,20},{6,22},{8,24},{10,26},{12,28},{14,30},{16,0},... | collective-permute-start | bytes 196616 | tf_op jit(solution)/shard_map/ppermute | solution.py:420
  23.5 0.2 collective-permute-start.6
  23.7 0.6 %split.3 = (bf16[512,2048]{1,0:T(8,128)(2,1)S(1)}, bf16[512,2048]{1,0:T(8,128)(2,1)S(1)}) custom-call(f32[1024,2048]{1,0:T(8,128)S(1)} %bitcast.1, f32[16,1024]{1,0:T(8,128)S(1)} %add.18.rest_0_.refs_0_), custom_call_target="tpu_custom_call" | custom-call | flops 62914560 | bytes 4194304 | tf_op jit(solution)/shard_map/split/pallas_call | solution.py:239
  24.3 2.4 %taper.3.refs_4_ = f32[16,512]{1,0:T(8,128)S(1)} custom-call(s32[8,8]{1,0:T(8,128)S(1)} %copy-done, s32[8]{0:T(128)S(1)} %copy-done.1, f32[16,1280]{1,0:T(8,128)S(1)} %get-tuple-element.22.own_ref, bf16[32,3968]{1,0:T(8,128)(2,1)S(1)} %get-tuple-element.23.values_ref, f32[2,3840]{1,0:T(2,128)S(1)} %get-tuple-element.24.coords_ref, ...), custom_call_target="tpu_custom_call" | custom-call | flops 262144000 | bytes 2097152 | tf_op jit(solution)/shard_map/taper/pallas_call | solution.py:374
  26.7 0.0 collective-permute-done.8.refs_3_
  26.7 0.0 collective-permute-done.7.refs_2_
  26.8 2.8 %collective-permute-done.6.refs_1_ = f32[16,1024]{1,0:T(8,128)S(1)} collective-permute-done((f32[16,1024]{1,0:T(8,128)S(1)}, f32[16,1024]{1,0:T(8,128)S(1)}, u32[]{:S(2)}, u32[]{:S(2)}) %collective-permute-start.6) | collective-permute-done | bytes 65568 | tf_op jit(solution)/shard_map/ppermute | solution.py:420
  29.6 0.1 collective-permute-start.9
  29.7 1.3 %factor.2.before_ref = f32[16,1024]{1,0:T(8,128)S(1)} custom-call(f32[16,1024]{1,0:T(8,128)S(1)} %add.19.proj_ref, bf16[512,2048]{1,0:T(8,128)(2,1)S(1)} %get-tuple-element.27.refs_5_.rest_0_, bf16[512,2048]{1,0:T(8,128)(2,1)S(1)} %get-tuple-element.29.refs_5_.rest_1_, bf16[512,2048]{1,0:T(8,128)(2,1)S(1)} %get-tuple-element.28.refs_6_.rest_2_, ...), custom_call_target="tpu_custom_call" | custom-call | flops 1048576000 | bytes 4194304 | tf_op jit(solution)/shard_map/factor/pallas_call | solution.py:280
  31.0 0.0 collective-permute-done.9.proj_ref
  31.0 1.3 %factor.3.factor_ref = f32[16,1024]{1,0:T(8,128)S(1)} custom-call(f32[16,1024]{1,0:T(8,128)S(1)} %factor.2.before_ref, f32[16,1024]{1,0:T(8,128)S(1)} %collective-permute-done.9.proj_ref, bf16[512,2048]{1,0:T(8,128)(2,1)S(1)} %get-tuple-element.27.refs_5_.rest_0_, bf16[512,2048]{1,0:T(8,128)(2,1)S(1)} %get-tuple-element.29.refs_5_.rest_1_, ...), custom_call_target="tpu_custom_call" | custom-call | flops 1048576000 | bytes 4194304 | tf_op jit(solution)/shard_map/factor/pallas_call | solution.py:280
  32.3 0.8 %spread.2 = f32[16,1024]{1,0:T(8,128)S(1)} custom-call(f32[16,1024]{1,0:T(8,128)S(1)} %factor.3.factor_ref, bf16[1024,1024]{1,0:T(8,128)(2,1)S(1)} %get-tuple-element.31.high_ref, bf16[1024,1024]{1,0:T(8,128)(2,1)S(1)} %get-tuple-element.32.low_ref), custom_call_target="tpu_custom_call" | custom-call | flops 891289600 | bytes 4194304 | tf_op jit(solution)/shard_map/spread/pallas_call | solution.py:305
  33.0 0.5 %collective-permute-start.10 = (f32[16,1024]{1,0:T(8,128)S(1)}, f32[16,1024]{1,0:T(8,128)S(1)}, u32[]{:S(2)}, u32[]{:S(2)}) collective-permute-start(f32[16,1024]{1,0:T(8,128)S(1)} %spread.2), channel_id=1, source_target_pairs={{1,0},{0,1},{3,2},{2,3},{5,4},{4,5},{7,6},{6,7},{9,8},{8,9},{11,10... | collective-permute-start | bytes 196616 | tf_op jit(solution)/shard_map/ppermute | solution.py:428
  33.6 0.8 %spread.3 = f32[16,1024]{1,0:T(8,128)S(1)} custom-call(f32[16,1024]{1,0:T(8,128)S(1)} %factor.3.factor_ref, bf16[1024,1024]{1,0:T(8,128)(2,1)S(1)} %get-tuple-element.33.high_ref, bf16[1024,1024]{1,0:T(8,128)(2,1)S(1)} %get-tuple-element.34.low_ref), custom_call_target="tpu_custom_call" | custom-call | flops 891289600 | bytes 4194304 | tf_op jit(solution)/shard_map/spread/pallas_call | solution.py:305
  34.3 0.1 collective-permute-done.10
  34.5 0.6 %fusion = f32[16,1024]{1,0:T(8,128)} fusion(f32[16,1024]{1,0:T(8,128)S(1)} %spread.3, f32[16,1024]{1,0:T(8,128)S(1)} %collective-permute-done.10, f32[16,512]{1,0:T(8,128)S(1)} %taper.3.refs_4_, f32[16,512]{1,0:T(8,128)S(1)} %taper.2.refs_4_), kind=kLoop, calls=%fused_computation.1 | loop fusion | flops 49152 | bytes 262144 | tf_op jit(solution)/shard_map/add | solution.py:493
  (5 shorter events, 0.1 us)
Async XLA Ops:
  0.9 3.5 %collective-permute-start = (f32[16,1280]{1,0:T(8,128)S(1)}, f32[16,1280]{1,0:T(8,128)S(1)}, u32[]{:S(2)}, u32[]{:S(2)}) collective-permute-start(f32[16,1280]{1,0:T(8,128)S(1)} %get-tuple-element.20.stack_ref), channel_id=1, source_target_pairs={{1,0},{0,1},{3,2},{2,3},{5,4},{4,5},{7,6},{6,7},{9,8},{8,9},{11,10... | collective-permute-start | bytes 245768 | tf_op jit(solution)/shard_map/ppermute | solution.py:428
  1.4 14.2 %slice-start = ((s8[8388608]{0:T(1024)(128)(4,1)}), s8[4194304]{0:T(1024)(128)(4,1)S(1)}, s32[]{:S(2)}) async-start(s8[8388608]{0:T(1024)(128)(4,1)} %bitcast), calls=%async_computation | async-start | bytes 8388608
  4.4 11.2 %slice-start.1 = ((s8[8388608]{0:T(1024)(128)(4,1)}), s8[4194304]{0:T(1024)(128)(4,1)S(1)}, s32[]{:S(2)}) async-start(s8[8388608]{0:T(1024)(128)(4,1)} %bitcast), calls=%async_computation.1 | async-start | bytes 8388608
  4.4 11.8 %collective-permute-start.2 = (f32[16,1536]{1,0:T(8,128)S(1)}, f32[16,1536]{1,0:T(8,128)S(1)}, u32[]{:S(2)}, u32[]{:S(2)}) collective-permute-start(f32[16,1536]{1,0:T(8,128)S(1)} %strip.1.own_ref), channel_id=1, source_target_pairs={{0,1},{1,0},{2,4},{3,5},{4,2},{5,3},{6,8},{7,9},{8,6},{9,7},{10,12... | collective-permute-start | bytes 294920 | tf_op jit(solution)/shard_map/ppermute | solution.py:443
  4.5 11.7 %collective-permute-start.1 = (f32[16,1536]{1,0:T(8,128)S(1)}, f32[16,1536]{1,0:T(8,128)S(1)}, u32[]{:S(2)}, u32[]{:S(2)}) collective-permute-start(f32[16,1536]{1,0:T(8,128)S(1)} %strip.1.own_ref), channel_id=1, source_target_pairs={{0,2},{1,3},{2,0},{3,1},{4,6},{5,7},{6,4},{7,5},{8,10},{9,11},{10,... | collective-permute-start | bytes 294920 | tf_op jit(solution)/shard_map/ppermute | solution.py:443
  12.0 4.3 %copy-start = (s32[8,8]{1,0:T(8,128)S(1)}, s32[8,8]{1,0:T(8,128)}, u32[]{:S(2)}) copy-start(s32[8,8]{1,0:T(8,128)} %ids_ref.3) | copy-start | bytes 772
  12.0 4.3 %copy-start.1 = (s32[8]{0:T(128)S(1)}, s32[8]{0:T(128)}, u32[]{:S(2)}) copy-start(s32[8]{0:T(128)} %counts_ref.3) | copy-start | bytes 100
  12.0 6.7 %collective-permute-start.5 = (f32[16,1024]{1,0:T(8,128)S(1)}, f32[16,1024]{1,0:T(8,128)S(1)}, u32[]{:S(2)}, u32[]{:S(2)}) collective-permute-start(f32[16,1024]{1,0:T(8,128)S(1)} %add.11.rest_0_.refs_0_), channel_id=1, source_target_pairs={{0,2},{2,0},{4,6},{6,4},{8,10},{10,8},{12,14},{14,12},{16,18},{18,... | collective-permute-start | bytes 196616 | tf_op jit(solution)/shard_map/ppermute | solution.py:420
  12.1 6.6 %collective-permute-start.4 = (f32[16,1024]{1,0:T(8,128)S(1)}, f32[16,1024]{1,0:T(8,128)S(1)}, u32[]{:S(2)}, u32[]{:S(2)}) collective-permute-start(f32[16,1024]{1,0:T(8,128)S(1)} %add.11.rest_0_.refs_0_), channel_id=1, source_target_pairs={{0,4},{2,6},{4,0},{6,2},{8,12},{10,14},{12,8},{14,10},{16,20},{18,... | collective-permute-start | bytes 196616 | tf_op jit(solution)/shard_map/ppermute | solution.py:420
  14.1 5.2 %collective-permute-start.3 = (f32[16,1024]{1,0:T(8,128)S(1)}, f32[16,1024]{1,0:T(8,128)S(1)}, u32[]{:S(2)}, u32[]{:S(2)}) collective-permute-start(f32[16,1024]{1,0:T(8,128)S(1)} %add.11.rest_0_.refs_0_), channel_id=1, source_target_pairs={{0,6},{2,4},{4,2},{6,0},{8,14},{10,12},{12,10},{14,8},{16,22},{18,... | collective-permute-start | bytes 196616 | tf_op jit(solution)/shard_map/ppermute | solution.py:420
  19.3 7.5 %collective-permute-start.8 = (f32[16,1024]{1,0:T(8,128)S(1)}, f32[16,1024]{1,0:T(8,128)S(1)}, u32[]{:S(2)}, u32[]{:S(2)}) collective-permute-start(f32[16,1024]{1,0:T(8,128)S(1)} %add.18.rest_0_.refs_0_), channel_id=1, source_target_pairs={{0,8},{2,10},{4,12},{6,14},{8,0},{10,2},{12,4},{14,6},{16,24},{18,... | collective-permute-start | bytes 196616 | tf_op jit(solution)/shard_map/ppermute | solution.py:420
  20.9 5.9 %collective-permute-start.7 = (f32[16,1024]{1,0:T(8,128)S(1)}, f32[16,1024]{1,0:T(8,128)S(1)}, u32[]{:S(2)}, u32[]{:S(2)}) collective-permute-start(f32[16,1024]{1,0:T(8,128)S(1)} %add.18.rest_0_.refs_0_), channel_id=1, source_target_pairs={{0,16},{2,18},{4,20},{6,22},{8,24},{10,26},{12,28},{14,30},{16,0},... | collective-permute-start | bytes 196616 | tf_op jit(solution)/shard_map/ppermute | solution.py:420
  23.5 6.1 %collective-permute-start.6 = (f32[16,1024]{1,0:T(8,128)S(1)}, f32[16,1024]{1,0:T(8,128)S(1)}, u32[]{:S(2)}, u32[]{:S(2)}) collective-permute-start(f32[16,1024]{1,0:T(8,128)S(1)} %add.18.rest_0_.refs_0_), channel_id=1, source_target_pairs={{0,24},{2,26},{4,28},{6,30},{8,16},{10,18},{12,20},{14,22},{16,8},... | collective-permute-start | bytes 196616 | tf_op jit(solution)/shard_map/ppermute | solution.py:420
  29.6 1.4 %collective-permute-start.9 = (f32[16,1024]{1,0:T(8,128)S(1)}, f32[16,1024]{1,0:T(8,128)S(1)}, u32[]{:S(2)}, u32[]{:S(2)}) collective-permute-start(f32[16,1024]{1,0:T(8,128)S(1)} %add.19.proj_ref), channel_id=1, source_target_pairs={{1,0},{0,1},{3,2},{2,3},{5,4},{4,5},{7,6},{6,7},{9,8},{8,9},{11,10... | collective-permute-start | bytes 196616 | tf_op jit(solution)/shard_map/ppermute | solution.py:428
  33.0 1.4 %collective-permute-start.10 = (f32[16,1024]{1,0:T(8,128)S(1)}, f32[16,1024]{1,0:T(8,128)S(1)}, u32[]{:S(2)}, u32[]{:S(2)}) collective-permute-start(f32[16,1024]{1,0:T(8,128)S(1)} %spread.2), channel_id=1, source_target_pairs={{1,0},{0,1},{3,2},{2,3},{5,4},{4,5},{7,6},{6,7},{9,8},{8,9},{11,10... | collective-permute-start | bytes 196616 | tf_op jit(solution)/shard_map/ppermute | solution.py:428

commit v15 on v14

--- a/solution.py
+++ b/solution.py
@@ -180,11 +180,13 @@
     return (x + grain) - (grain - grain * HALF_GRAIN)
 
 
-def project_kernel(scale, grain, stack_ref, knots_ref, out_ref, high_ref, low_ref, copy_ref, weights, columns):
+def project_kernel(scale, grain, stack_ref, knots_ref, out_ref, high_ref, low_ref, *rest):
+    *copies, weights, columns = rest
     knots, points = high_ref.shape
     probes = stack_ref.shape[0]
     tile = min(TILE, knots)
-    copy_ref[...] = stack_ref[...]
+    for copy_ref in copies:
+        copy_ref[...] = stack_ref[...]
     weights[...] = padded_halves(stack_ref[:, :points], weights.shape[0])
     fill = jnp.zeros((6, knots), jnp.float32)
     columns[...] = jnp.transpose(jnp.concatenate([off_grid(knots_ref[...] * scale, grain), fill], axis=0))
@@ -203,7 +205,7 @@
         out_ref[:, rows] = folded_columns(total, probes)
 
 
-def project(stack, knot_locs, scale, extent):
+def project(stack, knot_locs, scale, extent, copies):
     probes, points, knots = stack.shape[0], stack.shape[1] - 2 * LANES, knot_locs.shape[1]
     return pl.pallas_call(
         functools.partial(project_kernel, scale, grain_of(scale * extent)),
@@ -211,10 +213,10 @@
             jax.ShapeDtypeStruct((probes, knots), jnp.float32),
             pltpu.VMEM((knots, points), jnp.bfloat16),
             pltpu.VMEM((knots, points), jnp.bfloat16),
-            jax.ShapeDtypeStruct(stack.shape, jnp.float32),
+            *[jax.ShapeDtypeStruct(stack.shape, jnp.float32)] * copies,
         ),
         in_specs=[VMEM, VMEM],
-        out_specs=(VMEM, VMEM, VMEM, VMEM),
+        out_specs=(VMEM,) * (3 + copies),
         scratch_shapes=[
             pltpu.VMEM((LANES, points), jnp.bfloat16),
             pltpu.VMEM((knots, 8), jnp.float32),
@@ -227,18 +229,21 @@
 
 def split_kernel(first, precision_ref, *rest):
     high_ref, low_ref = rest[-2:]
-    rows = high_ref.shape[0]
+    depth, rows = high_ref.shape
     tile = min(TILE, rows)
+    wide = min(TILE, depth)
     for start in range(0, rows, tile):
-        here = slice(start, start + tile)
-        high_ref[here, :], low_ref[here, :] = halves(precision_ref[first + start : first + start + tile, :])
+        for deep in range(0, depth, wide):
+            turned = jnp.transpose(precision_ref[first + start : first + start + tile, deep : deep + wide])
+            here = slice(deep, deep + wide), slice(start, start + tile)
+            high_ref[here], low_ref[here] = halves(turned)
 
 
 def split_rows(precision, first, rows, after):
     depth = precision.shape[1]
     return pl.pallas_call(
         functools.partial(split_kernel, first),
-        out_shape=(pltpu.VMEM((rows, depth), jnp.bfloat16), pltpu.VMEM((rows, depth), jnp.bfloat16)),
+        out_shape=(pltpu.VMEM((depth, rows), jnp.bfloat16), pltpu.VMEM((depth, rows), jnp.bfloat16)),
         in_specs=[VMEM] + [ANY] * len(after),
         out_specs=(VMEM, VMEM),
         compiler_params=pltpu.CompilerParams(vmem_limit_bytes=LIMIT),
@@ -252,13 +257,13 @@
     probes, depth = proj_ref.shape
     weights[...] = stacked_halves(proj_ref[...] * scale)
     owner = lax.rem(lax.axis_index("knot") + step, lax.axis_size("knot"))
-    lanes = pl.ds(pl.multiple_of(owner * depth, depth), depth)
-    rows = highs[0].shape[0]
+    deep = pl.ds(pl.multiple_of(owner * depth, depth), depth)
+    rows = highs[0].shape[1]
     tile = min(TILE, rows)
     for part, (high_ref, low_ref) in enumerate(zip(highs, lows)):
         for start in range(0, rows, tile):
             here = slice(start, start + tile)
-            found = folded(dot_nt(weights[...], high_ref[here, lanes]) + dot_nt(weights[...], low_ref[here, lanes]))
+            found = folded(dot_nn(weights[...], high_ref[deep, here]) + dot_nn(weights[...], low_ref[deep, here]))
             target = slice(part * rows + start, part * rows + start + tile)
             if before_ref is not None:
                 found = found + before_ref[:, target]
@@ -270,7 +275,7 @@
     highs, lows = [
         [pltpu.with_memory_space_constraint(split[half], pltpu.VMEM) for split in splits] for half in range(2)
     ]
-    rows = sum(high.shape[0] for high in highs)
+    rows = sum(high.shape[1] for high in highs)
     kernel = functools.partial(factor_kernel, scale, step, len(splits))
     operands = (projection, *highs, *lows)
     if before is None:
@@ -456,7 +461,7 @@
     chunks = [shifted(stack, "knot", step) for step in range(groups)]
     rate = LOG2E / knot_range
     extent = CELL * max(lax.axis_size("space"), groups * own_blocks)
-    parts = [project(chunk, knots, rate, extent) for chunk in chunks]
+    parts = [project(chunk, knots, rate, extent, int(step == 0)) for step, chunk in enumerate(chunks)]
     stack = parts[0][3]
 
     strip = make_strip(chunks[-1], stack, chunks[1 % groups])

time: 35.3 us -> 34 us (0.963)
  Pallas kernels: 17.6 us -> 17 us
  waiting for transfers between devices: 3.53 us -> 3.1 us
  starting transfers between devices: 13.2 us -> 12.8 us
    pallas_call x2, Pallas kernels: 1.18 us -> 2.29 us  [split_rows(): pl.pallas_call(functools.partial(split_kernel, first), out_shape=(pltpu.V...]
    ppermute x6, waiting for transfers between devices: 3.38 us -> 2.29 us  [butterfly_round(): got.append(lax.ppermute(value, (axis, other), pairs))]
    pallas_call x2, Pallas kernels: 2.6 us -> 1.53 us  [factored(): pl.pallas_call(kernel, out_shape=jax.ShapeDtypeStruct((probes, rows), jnp...]
    ppermute x3, waiting for transfers between devices: 0.15 us -> 0.81 us  [shifted(): lax.ppermute(value, axis, [((i + step) % count, i) for i in range(count)])]
    pallas_call x2, Pallas kernels: 6.47 us -> 5.86 us  [project(): pl.pallas_call(functools.partial(project_kernel, scale, grain_of(scale *...]
  transfers between devices with their start and end apart: 11 -> 11, of which waited for: 3 -> 3; matrix products, arithmetic and copies ran while one was open for 0% -> 0% of each run, Pallas kernels for 41% -> 43%
where the time goes in v15:
time: 34 us; the launch traced here: 33.8 us
  Pallas kernels  17 us (50%)
  starting transfers between devices  12.8 us (38%)
  waiting for transfers between devices  3.1 us (9%)
  other arithmetic  0.67 us (2%)
    ppermute x6, starting transfers between devices, butterfly_round(): got.append(lax.ppermute(value, (axis, other), pairs))  8 us
    pallas_call x2, Pallas kernels, project(): pl.pallas_call(functools.partial(project_kernel, scale, grain_of(scale *...  5.86 us
    pallas_call x2, Pallas kernels, taper(): pl.pallas_call(functools.partial(taper_kernel, first, grain_of(TAPER_RATE...  4.79 us
    ppermute x2, starting transfers between devices, paired(): return lax.ppermute(value, (axis, other), pairs)  4.07 us
    pallas_call x2, Pallas kernels, split_rows(): pl.pallas_call(functools.partial(split_kernel, first), out_shape=(pltpu.V...  2.29 us
    ppermute x6, waiting for transfers between devices, butterfly_round(): got.append(lax.ppermute(value, (axis, other), pairs))  2.29 us
    pallas_call x2, Pallas kernels, spread(): pl.pallas_call(functools.partial(spread_kernel, scale), out_shape=jax.Sha...  1.54 us
    pallas_call x2, Pallas kernels, factored(): pl.pallas_call(kernel, out_shape=jax.ShapeDtypeStruct((probes, rows), jnp...  1.53 us
  transfers between devices with their start and end apart: 11, of which 3 were waited for; matrix products, arithmetic and copies ran while one was open for 0% of the time, Pallas kernels for 43%

profile of v15, /device:TPU:0, one launch (start us, length us, event | category | flops | bytes accessed | tf_op | source)
XLA Modules:
  0.0 33.8 jit_solution(12123002721230120952)
XLA Ops:
  0.0 0.9 %prepare.1 = (f32[16,1280]{1,0:T(8,128)S(1)}, f32[2,1024]{1,0:T(2,128)S(1)}) custom-call(f32[16,1024]{1,0:T(8,128)} %probes_ref.1, f32[2,1024]{1,0:T(2,128)} %locations_ref.1, f32[2,1024]{1,0:T(2,128)} %knots_ref.1), custom_call_target="tpu_custom_call" | custom-call | tf_op jit(solution)/shard_map/prepare/pallas_call | solution.py:100
  0.9 0.5 %collective-permute-start = (f32[16,1280]{1,0:T(8,128)S(1)}, f32[16,1280]{1,0:T(8,128)S(1)}, u32[]{:S(2)}, u32[]{:S(2)}) collective-permute-start(f32[16,1280]{1,0:T(8,128)S(1)} %get-tuple-element.20.stack_ref), channel_id=1, source_target_pairs={{1,0},{0,1},{3,2},{2,3},{5,4},{4,5},{7,6},{6,7},{9,8},{8,9},{11,10... | collective-permute-start | bytes 245768 | tf_op jit(solution)/shard_map/ppermute | solution.py:433
  1.4 0.0 slice-start
  1.4 3.0 %project.2 = (f32[16,1024]{1,0:T(8,128)S(1)}, bf16[1024,1024]{1,0:T(8,128)(2,1)S(1)}, bf16[1024,1024]{1,0:T(8,128)(2,1)S(1)}, f32[16,1280]{1,0:T(8,128)S(1)}) custom-call(f32[16,1280]{1,0:T(8,128)S(1)} %get-tuple-element.20.stack_ref, f32[2,1024]{1,0:T(2,128)S(1)} %get-tuple-element.21.knots_ref), custom_call_target="tpu_custom_call" | custom-call | flops 2936012800 | bytes 4194304 | tf_op jit(solution)/shard_map/project/pallas_call | solution.py:210
  4.4 0.0 collective-permute-done.below_ref.above_ref.stack_ref
  4.4 0.0 slice-start.1
  4.4 0.1 collective-permute-start.2
  4.5 3.9 %collective-permute-start.1 = (f32[16,1536]{1,0:T(8,128)S(1)}, f32[16,1536]{1,0:T(8,128)S(1)}, u32[]{:S(2)}, u32[]{:S(2)}) collective-permute-start(f32[16,1536]{1,0:T(8,128)S(1)} %strip.1.own_ref), channel_id=1, source_target_pairs={{0,2},{1,3},{2,0},{3,1},{4,6},{5,7},{6,4},{7,5},{8,10},{9,11},{10,... | collective-permute-start | bytes 294920 | tf_op jit(solution)/shard_map/ppermute | solution.py:448
  8.5 2.9 %project.3 = (f32[16,1024]{1,0:T(8,128)S(1)}, bf16[1024,1024]{1,0:T(8,128)(2,1)S(1)}, bf16[1024,1024]{1,0:T(8,128)(2,1)S(1)}) custom-call(f32[16,1280]{1,0:T(8,128)S(1)} %collective-permute-done.below_ref.above_ref.stack_ref, f32[2,1024]{1,0:T(2,128)S(1)} %get-tuple-element.21.knots_ref), custom_call_target="tpu_custom_call" | custom-call | flops 2936012800 | bytes 4194304 | tf_op jit(solution)/shard_map/project/pallas_call | solution.py:210
  11.4 0.0 copy-start
  11.4 0.0 copy-start.1
  11.4 0.1 collective-permute-start.5
  11.5 2.0 %collective-permute-start.4 = (f32[16,1024]{1,0:T(8,128)S(1)}, f32[16,1024]{1,0:T(8,128)S(1)}, u32[]{:S(2)}, u32[]{:S(2)}) collective-permute-start(f32[16,1024]{1,0:T(8,128)S(1)} %add.11.rest_0_.refs_0_), channel_id=1, source_target_pairs={{0,4},{2,6},{4,0},{6,2},{8,12},{10,14},{12,8},{14,10},{16,20},{18,... | collective-permute-start | bytes 196616 | tf_op jit(solution)/shard_map/ppermute | solution.py:425
  13.5 1.5 %collective-permute-start.3 = (f32[16,1024]{1,0:T(8,128)S(1)}, f32[16,1024]{1,0:T(8,128)S(1)}, u32[]{:S(2)}, u32[]{:S(2)}) collective-permute-start(f32[16,1024]{1,0:T(8,128)S(1)} %add.11.rest_0_.refs_0_), channel_id=1, source_target_pairs={{0,6},{2,4},{4,2},{6,0},{8,14},{10,12},{12,10},{14,8},{16,22},{18,... | collective-permute-start | bytes 196616 | tf_op jit(solution)/shard_map/ppermute | solution.py:425
  15.0 0.0 slice-done
  15.0 0.0 slice-done.1
  15.0 1.1 %split.2 = (bf16[2048,512]{1,0:T(8,128)(2,1)S(1)}, bf16[2048,512]{1,0:T(8,128)(2,1)S(1)}) custom-call(f32[1024,2048]{1,0:T(8,128)S(1)} %bitcast.1, f32[16,1024]{1,0:T(8,128)S(1)} %add.11.rest_0_.refs_0_), custom_call_target="tpu_custom_call" | custom-call | flops 62914560 | bytes 4194304 | tf_op jit(solution)/shard_map/split/pallas_call | solution.py:244
  16.2 0.0 collective-permute-done.2.west_ref
  16.2 0.0 collective-permute-done.1.east_ref
  16.2 0.1 assemble.1
  16.2 0.0 copy-done
  16.3 0.0 copy-done.1
  16.3 2.4 %taper.2.refs_4_ = f32[16,512]{1,0:T(8,128)S(1)} custom-call(s32[8,8]{1,0:T(8,128)S(1)} %copy-done, s32[8]{0:T(128)S(1)} %copy-done.1, f32[16,1280]{1,0:T(8,128)S(1)} %get-tuple-element.22.own_ref, bf16[32,3968]{1,0:T(8,128)(2,1)S(1)} %get-tuple-element.23.values_ref, f32[2,3840]{1,0:T(2,128)S(1)} %get-tuple-element.24.coords_ref, ...), custom_call_target="tpu_custom_call" | custom-call | flops 262144000 | bytes 2097152 | tf_op jit(solution)/shard_map/taper/pallas_call | solution.py:379
  18.7 0.0 collective-permute-done.5.refs_3_
  18.7 0.0 collective-permute-done.4.refs_2_
  18.7 0.0 collective-permute-done.3.refs_1_
  18.7 1.6 %collective-permute-start.8 = (f32[16,1024]{1,0:T(8,128)S(1)}, f32[16,1024]{1,0:T(8,128)S(1)}, u32[]{:S(2)}, u32[]{:S(2)}) collective-permute-start(f32[16,1024]{1,0:T(8,128)S(1)} %add.18.rest_0_.refs_0_), channel_id=1, source_target_pairs={{0,8},{2,10},{4,12},{6,14},{8,0},{10,2},{12,4},{14,6},{16,24},{18,... | collective-permute-start | bytes 196616 | tf_op jit(solution)/shard_map/ppermute | solution.py:425
  20.4 2.6 %collective-permute-start.7 = (f32[16,1024]{1,0:T(8,128)S(1)}, f32[16,1024]{1,0:T(8,128)S(1)}, u32[]{:S(2)}, u32[]{:S(2)}) collective-permute-start(f32[16,1024]{1,0:T(8,128)S(1)} %add.18.rest_0_.refs_0_), channel_id=1, source_target_pairs={{0,16},{2,18},{4,20},{6,22},{8,24},{10,26},{12,28},{14,30},{16,0},... | collective-permute-start | bytes 196616 | tf_op jit(solution)/shard_map/ppermute | solution.py:425
  23.0 0.2 collective-permute-start.6
  23.2 1.1 %split.3 = (bf16[2048,512]{1,0:T(8,128)(2,1)S(1)}, bf16[2048,512]{1,0:T(8,128)(2,1)S(1)}) custom-call(f32[1024,2048]{1,0:T(8,128)S(1)} %bitcast.1, f32[16,1024]{1,0:T(8,128)S(1)} %add.18.rest_0_.refs_0_), custom_call_target="tpu_custom_call" | custom-call | flops 62914560 | bytes 4194304 | tf_op jit(solution)/shard_map/split/pallas_call | solution.py:244
  24.3 2.4 %taper.3.refs_4_ = f32[16,512]{1,0:T(8,128)S(1)} custom-call(s32[8,8]{1,0:T(8,128)S(1)} %copy-done, s32[8]{0:T(128)S(1)} %copy-done.1, f32[16,1280]{1,0:T(8,128)S(1)} %get-tuple-element.22.own_ref, bf16[32,3968]{1,0:T(8,128)(2,1)S(1)} %get-tuple-element.23.values_ref, f32[2,3840]{1,0:T(2,128)S(1)} %get-tuple-element.24.coords_ref, ...), custom_call_target="tpu_custom_call" | custom-call | flops 262144000 | bytes 2097152 | tf_op jit(solution)/shard_map/taper/pallas_call | solution.py:379
  26.7 0.0 collective-permute-done.8.refs_3_
  26.8 0.0 collective-permute-done.7.refs_2_
  26.8 2.3 %collective-permute-done.6.refs_1_ = f32[16,1024]{1,0:T(8,128)S(1)} collective-permute-done((f32[16,1024]{1,0:T(8,128)S(1)}, f32[16,1024]{1,0:T(8,128)S(1)}, u32[]{:S(2)}, u32[]{:S(2)}) %collective-permute-start.6) | collective-permute-done | bytes 65568 | tf_op jit(solution)/shard_map/ppermute | solution.py:425
  29.1 0.1 collective-permute-start.9
  29.1 0.8 %factor.2.before_ref = f32[16,1024]{1,0:T(8,128)S(1)} custom-call(f32[16,1024]{1,0:T(8,128)S(1)} %add.19.proj_ref, bf16[2048,512]{1,0:T(8,128)(2,1)S(1)} %get-tuple-element.27.refs_5_.rest_0_, bf16[2048,512]{1,0:T(8,128)(2,1)S(1)} %get-tuple-element.29.refs_5_.rest_1_, bf16[2048,512]{1,0:T(8,128)(2,1)S(1)} %get-tuple-element.28.refs_6_.rest_2_, ...), custom_call_target="tpu_custom_call" | custom-call | flops 1048576000 | bytes 4194304 | tf_op jit(solution)/shard_map/factor/pallas_call | solution.py:285
  29.9 0.5 %collective-permute-done.9.proj_ref = f32[16,1024]{1,0:T(8,128)S(1)} collective-permute-done((f32[16,1024]{1,0:T(8,128)S(1)}, f32[16,1024]{1,0:T(8,128)S(1)}, u32[]{:S(2)}, u32[]{:S(2)}) %collective-permute-start.9) | collective-permute-done | bytes 65568 | tf_op jit(solution)/shard_map/ppermute | solution.py:433
  30.4 0.8 %factor.3.factor_ref = f32[16,1024]{1,0:T(8,128)S(1)} custom-call(f32[16,1024]{1,0:T(8,128)S(1)} %factor.2.before_ref, f32[16,1024]{1,0:T(8,128)S(1)} %collective-permute-done.9.proj_ref, bf16[2048,512]{1,0:T(8,128)(2,1)S(1)} %get-tuple-element.27.refs_5_.rest_0_, bf16[2048,512]{1,0:T(8,128)(2,1)S(1)} %get-tuple-element.29.refs_5_.rest_1_, ...), custom_call_target="tpu_custom_call" | custom-call | flops 1048576000 | bytes 4194304 | tf_op jit(solution)/shard_map/factor/pallas_call | solution.py:285
  31.1 0.8 %spread.2 = f32[16,1024]{1,0:T(8,128)S(1)} custom-call(f32[16,1024]{1,0:T(8,128)S(1)} %factor.3.factor_ref, bf16[1024,1024]{1,0:T(8,128)(2,1)S(1)} %get-tuple-element.31.high_ref, bf16[1024,1024]{1,0:T(8,128)(2,1)S(1)} %get-tuple-element.32.low_ref), custom_call_target="tpu_custom_call" | custom-call | flops 891289600 | bytes 4194304 | tf_op jit(solution)/shard_map/spread/pallas_call | solution.py:310
  31.9 0.2 collective-permute-start.10
  32.1 0.8 %spread.3 = f32[16,1024]{1,0:T(8,128)S(1)} custom-call(f32[16,1024]{1,0:T(8,128)S(1)} %factor.3.factor_ref, bf16[1024,1024]{1,0:T(8,128)(2,1)S(1)} %get-tuple-element.33.high_ref, bf16[1024,1024]{1,0:T(8,128)(2,1)S(1)} %get-tuple-element.34.low_ref), custom_call_target="tpu_custom_call" | custom-call | flops 891289600 | bytes 4194304 | tf_op jit(solution)/shard_map/spread/pallas_call | solution.py:310
  32.9 0.3 collective-permute-done.10
  33.2 0.6 %fusion = f32[16,1024]{1,0:T(8,128)} fusion(f32[16,1024]{1,0:T(8,128)S(1)} %spread.3, f32[16,1024]{1,0:T(8,128)S(1)} %collective-permute-done.10, f32[16,512]{1,0:T(8,128)S(1)} %taper.3.refs_4_, f32[16,512]{1,0:T(8,128)S(1)} %taper.2.refs_4_), kind=kLoop, calls=%fused_computation.1 | loop fusion | flops 49152 | bytes 262144 | tf_op jit(solution)/shard_map/add | solution.py:498
  (5 shorter events, 0.1 us)
Async XLA Ops:
  0.9 3.5 %collective-permute-start = (f32[16,1280]{1,0:T(8,128)S(1)}, f32[16,1280]{1,0:T(8,128)S(1)}, u32[]{:S(2)}, u32[]{:S(2)}) collective-permute-start(f32[16,1280]{1,0:T(8,128)S(1)} %get-tuple-element.20.stack_ref), channel_id=1, source_target_pairs={{1,0},{0,1},{3,2},{2,3},{5,4},{4,5},{7,6},{6,7},{9,8},{8,9},{11,10... | collective-permute-start | bytes 245768 | tf_op jit(solution)/shard_map/ppermute | solution.py:433
  1.4 13.6 %slice-start = ((s8[8388608]{0:T(1024)(128)(4,1)}), s8[4194304]{0:T(1024)(128)(4,1)S(1)}, s32[]{:S(2)}) async-start(s8[8388608]{0:T(1024)(128)(4,1)} %bitcast), calls=%async_computation | async-start | bytes 8388608
  4.4 10.6 %slice-start.1 = ((s8[8388608]{0:T(1024)(128)(4,1)}), s8[4194304]{0:T(1024)(128)(4,1)S(1)}, s32[]{:S(2)}) async-start(s8[8388608]{0:T(1024)(128)(4,1)} %bitcast), calls=%async_computation.1 | async-start | bytes 8388608
  4.4 11.8 %collective-permute-start.2 = (f32[16,1536]{1,0:T(8,128)S(1)}, f32[16,1536]{1,0:T(8,128)S(1)}, u32[]{:S(2)}, u32[]{:S(2)}) collective-permute-start(f32[16,1536]{1,0:T(8,128)S(1)} %strip.1.own_ref), channel_id=1, source_target_pairs={{0,1},{1,0},{2,4},{3,5},{4,2},{5,3},{6,8},{7,9},{8,6},{9,7},{10,12... | collective-permute-start | bytes 294920 | tf_op jit(solution)/shard_map/ppermute | solution.py:448
  4.5 11.7 %collective-permute-start.1 = (f32[16,1536]{1,0:T(8,128)S(1)}, f32[16,1536]{1,0:T(8,128)S(1)}, u32[]{:S(2)}, u32[]{:S(2)}) collective-permute-start(f32[16,1536]{1,0:T(8,128)S(1)} %strip.1.own_ref), channel_id=1, source_target_pairs={{0,2},{1,3},{2,0},{3,1},{4,6},{5,7},{6,4},{7,5},{8,10},{9,11},{10,... | collective-permute-start | bytes 294920 | tf_op jit(solution)/shard_map/ppermute | solution.py:448
  11.4 4.8 %copy-start = (s32[8,8]{1,0:T(8,128)S(1)}, s32[8,8]{1,0:T(8,128)}, u32[]{:S(2)}) copy-start(s32[8,8]{1,0:T(8,128)} %ids_ref.3) | copy-start | bytes 772
  11.4 4.8 %copy-start.1 = (s32[8]{0:T(128)S(1)}, s32[8]{0:T(128)}, u32[]{:S(2)}) copy-start(s32[8]{0:T(128)} %counts_ref.3) | copy-start | bytes 100
  11.4 7.2 %collective-permute-start.5 = (f32[16,1024]{1,0:T(8,128)S(1)}, f32[16,1024]{1,0:T(8,128)S(1)}, u32[]{:S(2)}, u32[]{:S(2)}) collective-permute-start(f32[16,1024]{1,0:T(8,128)S(1)} %add.11.rest_0_.refs_0_), channel_id=1, source_target_pairs={{0,2},{2,0},{4,6},{6,4},{8,10},{10,8},{12,14},{14,12},{16,18},{18,... | collective-permute-start | bytes 196616 | tf_op jit(solution)/shard_map/ppermute | solution.py:425
  11.5 7.2 %collective-permute-start.4 = (f32[16,1024]{1,0:T(8,128)S(1)}, f32[16,1024]{1,0:T(8,128)S(1)}, u32[]{:S(2)}, u32[]{:S(2)}) collective-permute-start(f32[16,1024]{1,0:T(8,128)S(1)} %add.11.rest_0_.refs_0_), channel_id=1, source_target_pairs={{0,4},{2,6},{4,0},{6,2},{8,12},{10,14},{12,8},{14,10},{16,20},{18,... | collective-permute-start | bytes 196616 | tf_op jit(solution)/shard_map/ppermute | solution.py:425
  13.5 5.2 %collective-permute-start.3 = (f32[16,1024]{1,0:T(8,128)S(1)}, f32[16,1024]{1,0:T(8,128)S(1)}, u32[]{:S(2)}, u32[]{:S(2)}) collective-permute-start(f32[16,1024]{1,0:T(8,128)S(1)} %add.11.rest_0_.refs_0_), channel_id=1, source_target_pairs={{0,6},{2,4},{4,2},{6,0},{8,14},{10,12},{12,10},{14,8},{16,22},{18,... | collective-permute-start | bytes 196616 | tf_op jit(solution)/shard_map/ppermute | solution.py:425
  18.7 8.0 %collective-permute-start.8 = (f32[16,1024]{1,0:T(8,128)S(1)}, f32[16,1024]{1,0:T(8,128)S(1)}, u32[]{:S(2)}, u32[]{:S(2)}) collective-permute-start(f32[16,1024]{1,0:T(8,128)S(1)} %add.18.rest_0_.refs_0_), channel_id=1, source_target_pairs={{0,8},{2,10},{4,12},{6,14},{8,0},{10,2},{12,4},{14,6},{16,24},{18,... | collective-permute-start | bytes 196616 | tf_op jit(solution)/shard_map/ppermute | solution.py:425
  20.4 6.4 %collective-permute-start.7 = (f32[16,1024]{1,0:T(8,128)S(1)}, f32[16,1024]{1,0:T(8,128)S(1)}, u32[]{:S(2)}, u32[]{:S(2)}) collective-permute-start(f32[16,1024]{1,0:T(8,128)S(1)} %add.18.rest_0_.refs_0_), channel_id=1, source_target_pairs={{0,16},{2,18},{4,20},{6,22},{8,24},{10,26},{12,28},{14,30},{16,0},... | collective-permute-start | bytes 196616 | tf_op jit(solution)/shard_map/ppermute | solution.py:425
  23.0 6.1 %collective-permute-start.6 = (f32[16,1024]{1,0:T(8,128)S(1)}, f32[16,1024]{1,0:T(8,128)S(1)}, u32[]{:S(2)}, u32[]{:S(2)}) collective-permute-start(f32[16,1024]{1,0:T(8,128)S(1)} %add.18.rest_0_.refs_0_), channel_id=1, source_target_pairs={{0,24},{2,26},{4,28},{6,30},{8,16},{10,18},{12,20},{14,22},{16,8},... | collective-permute-start | bytes 196616 | tf_op jit(solution)/shard_map/ppermute | solution.py:425
  29.1 1.3 %collective-permute-start.9 = (f32[16,1024]{1,0:T(8,128)S(1)}, f32[16,1024]{1,0:T(8,128)S(1)}, u32[]{:S(2)}, u32[]{:S(2)}) collective-permute-start(f32[16,1024]{1,0:T(8,128)S(1)} %add.19.proj_ref), channel_id=1, source_target_pairs={{1,0},{0,1},{3,2},{2,3},{5,4},{4,5},{7,6},{6,7},{9,8},{8,9},{11,10... | collective-permute-start | bytes 196616 | tf_op jit(solution)/shard_map/ppermute | solution.py:433
  31.9 1.3 %collective-permute-start.10 = (f32[16,1024]{1,0:T(8,128)S(1)}, f32[16,1024]{1,0:T(8,128)S(1)}, u32[]{:S(2)}, u32[]{:S(2)}) collective-permute-start(f32[16,1024]{1,0:T(8,128)S(1)} %spread.2), channel_id=1, source_target_pairs={{1,0},{0,1},{3,2},{2,3},{5,4},{4,5},{7,6},{6,7},{9,8},{8,9},{11,10... | collective-permute-start | bytes 196616 | tf_op jit(solution)/shard_map/ppermute | solution.py:433

commit v16 on v15

--- a/solution.py
+++ b/solution.py
@@ -408,7 +408,7 @@
 def butterfly_rounds(count):
     assert count & (count - 1) == 0
     bits = [1 << i for i in range(count.bit_length() - 1)]
-    rounds = [(low | high, high, low) for low, high in zip(bits[0::2], bits[1::2])]
+    rounds = [(low, high, low | high) for low, high in zip(bits[0::2], bits[1::2])]
     return rounds + [(bit,) for bit in bits[len(rounds) * 2 :]]
 
 

time: 34 us -> 32.5 us (0.956)
  waiting for transfers between devices: 3.1 us -> 1.65 us
    ppermute x6, waiting for transfers between devices: 2.29 us -> 0.83 us  [butterfly_round(): got.append(lax.ppermute(value, (axis, other), pairs))]
  transfers between devices with their start and end apart: 11 -> 11, of which waited for: 3 -> 3; matrix products, arithmetic and copies ran while one was open for 0% -> 0% of each run, Pallas kernels for 43% -> 45%
where the time goes in v16:
time: 32.5 us; the launch traced here: 32.4 us
  Pallas kernels  17 us (52%)
  starting transfers between devices  12.8 us (39%)
  waiting for transfers between devices  1.65 us (5%)
  other arithmetic  0.67 us (2%)
    ppermute x6, starting transfers between devices, butterfly_round(): got.append(lax.ppermute(value, (axis, other), pairs))  8.01 us
    pallas_call x2, Pallas kernels, project(): pl.pallas_call(functools.partial(project_kernel, scale, grain_of(scale *...  5.86 us
    pallas_call x2, Pallas kernels, taper(): pl.pallas_call(functools.partial(taper_kernel, first, grain_of(TAPER_RATE...  4.8 us
    ppermute x2, starting transfers between devices, paired(): return lax.ppermute(value, (axis, other), pairs)  4.07 us
    pallas_call x2, Pallas kernels, split_rows(): pl.pallas_call(functools.partial(split_kernel, first), out_shape=(pltpu.V...  2.29 us
    pallas_call x2, Pallas kernels, spread(): pl.pallas_call(functools.partial(spread_kernel, scale), out_shape=jax.Sha...  1.54 us
    pallas_call x2, Pallas kernels, factored(): pl.pallas_call(kernel, out_shape=jax.ShapeDtypeStruct((probes, rows), jnp...  1.53 us
    pallas_call x1, Pallas kernels, prepare(): pl.pallas_call(functools.partial(prepare_kernel, blocks), out_shape=(jax....  0.87 us
  transfers between devices with their start and end apart: 11, of which 3 were waited for; matrix products, arithmetic and copies ran while one was open for 0% of the time, Pallas kernels for 45%

profile of v16, /device:TPU:0, one launch (start us, length us, event | category | flops | bytes accessed | tf_op | source)
XLA Modules:
  0.0 32.4 jit_solution(11111728601880995528)
XLA Ops:
  0.0 0.9 %prepare.1 = (f32[16,1280]{1,0:T(8,128)S(1)}, f32[2,1024]{1,0:T(2,128)S(1)}) custom-call(f32[16,1024]{1,0:T(8,128)} %probes_ref.1, f32[2,1024]{1,0:T(2,128)} %locations_ref.1, f32[2,1024]{1,0:T(2,128)} %knots_ref.1), custom_call_target="tpu_custom_call" | custom-call | tf_op jit(solution)/shard_map/prepare/pallas_call | solution.py:100
  0.9 0.5 %collective-permute-start = (f32[16,1280]{1,0:T(8,128)S(1)}, f32[16,1280]{1,0:T(8,128)S(1)}, u32[]{:S(2)}, u32[]{:S(2)}) collective-permute-start(f32[16,1280]{1,0:T(8,128)S(1)} %get-tuple-element.20.stack_ref), channel_id=1, source_target_pairs={{1,0},{0,1},{3,2},{2,3},{5,4},{4,5},{7,6},{6,7},{9,8},{8,9},{11,10... | collective-permute-start | bytes 245768 | tf_op jit(solution)/shard_map/ppermute | solution.py:433
  1.4 0.0 slice-start
  1.4 3.0 %project.2 = (f32[16,1024]{1,0:T(8,128)S(1)}, bf16[1024,1024]{1,0:T(8,128)(2,1)S(1)}, bf16[1024,1024]{1,0:T(8,128)(2,1)S(1)}, f32[16,1280]{1,0:T(8,128)S(1)}) custom-call(f32[16,1280]{1,0:T(8,128)S(1)} %get-tuple-element.20.stack_ref, f32[2,1024]{1,0:T(2,128)S(1)} %get-tuple-element.21.knots_ref), custom_call_target="tpu_custom_call" | custom-call | flops 2936012800 | bytes 4194304 | tf_op jit(solution)/shard_map/project/pallas_call | solution.py:210
  4.4 0.0 collective-permute-done.below_ref.above_ref.stack_ref
  4.4 0.0 slice-start.1
  4.4 0.1 collective-permute-start.2
  4.5 3.9 %collective-permute-start.1 = (f32[16,1536]{1,0:T(8,128)S(1)}, f32[16,1536]{1,0:T(8,128)S(1)}, u32[]{:S(2)}, u32[]{:S(2)}) collective-permute-start(f32[16,1536]{1,0:T(8,128)S(1)} %strip.1.own_ref), channel_id=1, source_target_pairs={{0,2},{1,3},{2,0},{3,1},{4,6},{5,7},{6,4},{7,5},{8,10},{9,11},{10,... | collective-permute-start | bytes 294920 | tf_op jit(solution)/shard_map/ppermute | solution.py:448
  8.5 2.9 %project.3 = (f32[16,1024]{1,0:T(8,128)S(1)}, bf16[1024,1024]{1,0:T(8,128)(2,1)S(1)}, bf16[1024,1024]{1,0:T(8,128)(2,1)S(1)}) custom-call(f32[16,1280]{1,0:T(8,128)S(1)} %collective-permute-done.below_ref.above_ref.stack_ref, f32[2,1024]{1,0:T(2,128)S(1)} %get-tuple-element.21.knots_ref), custom_call_target="tpu_custom_call" | custom-call | flops 2936012800 | bytes 4194304 | tf_op jit(solution)/shard_map/project/pallas_call | solution.py:210
  11.4 0.0 copy-start
  11.4 0.0 copy-start.1
  11.4 1.5 %collective-permute-start.5 = (f32[16,1024]{1,0:T(8,128)S(1)}, f32[16,1024]{1,0:T(8,128)S(1)}, u32[]{:S(2)}, u32[]{:S(2)}) collective-permute-start(f32[16,1024]{1,0:T(8,128)S(1)} %add.11.rest_0_.refs_0_), channel_id=1, source_target_pairs={{0,6},{2,4},{4,2},{6,0},{8,14},{10,12},{12,10},{14,8},{16,22},{18,... | collective-permute-start | bytes 196616 | tf_op jit(solution)/shard_map/ppermute | solution.py:425
  12.9 0.2 collective-permute-start.4
  13.1 1.9 %collective-permute-start.3 = (f32[16,1024]{1,0:T(8,128)S(1)}, f32[16,1024]{1,0:T(8,128)S(1)}, u32[]{:S(2)}, u32[]{:S(2)}) collective-permute-start(f32[16,1024]{1,0:T(8,128)S(1)} %add.11.rest_0_.refs_0_), channel_id=1, source_target_pairs={{0,2},{2,0},{4,6},{6,4},{8,10},{10,8},{12,14},{14,12},{16,18},{18,... | collective-permute-start | bytes 196616 | tf_op jit(solution)/shard_map/ppermute | solution.py:425
  15.0 0.0 slice-done
  15.0 0.0 slice-done.1
  15.0 1.1 %split.2 = (bf16[2048,512]{1,0:T(8,128)(2,1)S(1)}, bf16[2048,512]{1,0:T(8,128)(2,1)S(1)}) custom-call(f32[1024,2048]{1,0:T(8,128)S(1)} %bitcast.1, f32[16,1024]{1,0:T(8,128)S(1)} %add.11.rest_0_.refs_0_), custom_call_target="tpu_custom_call" | custom-call | flops 62914560 | bytes 4194304 | tf_op jit(solution)/shard_map/split/pallas_call | solution.py:244
  16.2 0.0 collective-permute-done.2.west_ref
  16.2 0.0 collective-permute-done.1.east_ref
  16.2 0.1 assemble.1
  16.2 0.0 copy-done
  16.3 0.0 copy-done.1
  16.3 2.4 %taper.2.refs_4_ = f32[16,512]{1,0:T(8,128)S(1)} custom-call(s32[8,8]{1,0:T(8,128)S(1)} %copy-done, s32[8]{0:T(128)S(1)} %copy-done.1, f32[16,1280]{1,0:T(8,128)S(1)} %get-tuple-element.22.own_ref, bf16[32,3968]{1,0:T(8,128)(2,1)S(1)} %get-tuple-element.23.values_ref, f32[2,3840]{1,0:T(2,128)S(1)} %get-tuple-element.24.coords_ref, ...), custom_call_target="tpu_custom_call" | custom-call | flops 262144000 | bytes 2097152 | tf_op jit(solution)/shard_map/taper/pallas_call | solution.py:379
  18.7 0.0 collective-permute-done.5.refs_3_
  18.7 0.0 collective-permute-done.4.refs_2_
  18.7 0.0 collective-permute-done.3.refs_1_
  18.7 3.7 %collective-permute-start.8 = (f32[16,1024]{1,0:T(8,128)S(1)}, f32[16,1024]{1,0:T(8,128)S(1)}, u32[]{:S(2)}, u32[]{:S(2)}) collective-permute-start(f32[16,1024]{1,0:T(8,128)S(1)} %add.18.rest_0_.refs_0_), channel_id=1, source_target_pairs={{0,24},{2,26},{4,28},{6,30},{8,16},{10,18},{12,20},{14,22},{16,8},... | collective-permute-start | bytes 196616 | tf_op jit(solution)/shard_map/ppermute | solution.py:425
  22.4 0.0 collective-permute-start.7
  22.4 0.8 %collective-permute-start.6 = (f32[16,1024]{1,0:T(8,128)S(1)}, f32[16,1024]{1,0:T(8,128)S(1)}, u32[]{:S(2)}, u32[]{:S(2)}) collective-permute-start(f32[16,1024]{1,0:T(8,128)S(1)} %add.18.rest_0_.refs_0_), channel_id=1, source_target_pairs={{0,8},{2,10},{4,12},{6,14},{8,0},{10,2},{12,4},{14,6},{16,24},{18,... | collective-permute-start | bytes 196616 | tf_op jit(solution)/shard_map/ppermute | solution.py:425
  23.2 1.1 %split.3 = (bf16[2048,512]{1,0:T(8,128)(2,1)S(1)}, bf16[2048,512]{1,0:T(8,128)(2,1)S(1)}) custom-call(f32[1024,2048]{1,0:T(8,128)S(1)} %bitcast.1, f32[16,1024]{1,0:T(8,128)S(1)} %add.18.rest_0_.refs_0_), custom_call_target="tpu_custom_call" | custom-call | flops 62914560 | bytes 4194304 | tf_op jit(solution)/shard_map/split/pallas_call | solution.py:244
  24.3 2.4 %taper.3.refs_4_ = f32[16,512]{1,0:T(8,128)S(1)} custom-call(s32[8,8]{1,0:T(8,128)S(1)} %copy-done, s32[8]{0:T(128)S(1)} %copy-done.1, f32[16,1280]{1,0:T(8,128)S(1)} %get-tuple-element.22.own_ref, bf16[32,3968]{1,0:T(8,128)(2,1)S(1)} %get-tuple-element.23.values_ref, f32[2,3840]{1,0:T(2,128)S(1)} %get-tuple-element.24.coords_ref, ...), custom_call_target="tpu_custom_call" | custom-call | flops 262144000 | bytes 2097152 | tf_op jit(solution)/shard_map/taper/pallas_call | solution.py:379
  26.8 0.0 collective-permute-done.8.refs_3_
  26.8 0.8 %collective-permute-done.7.refs_2_ = f32[16,1024]{1,0:T(8,128)S(1)} collective-permute-done((f32[16,1024]{1,0:T(8,128)S(1)}, f32[16,1024]{1,0:T(8,128)S(1)}, u32[]{:S(2)}, u32[]{:S(2)}) %collective-permute-start.7) | collective-permute-done | bytes 65568 | tf_op jit(solution)/shard_map/ppermute | solution.py:425
  27.6 0.0 collective-permute-done.6.refs_1_
  27.6 0.1 collective-permute-start.9
  27.7 0.8 %factor.2.before_ref = f32[16,1024]{1,0:T(8,128)S(1)} custom-call(f32[16,1024]{1,0:T(8,128)S(1)} %add.19.proj_ref, bf16[2048,512]{1,0:T(8,128)(2,1)S(1)} %get-tuple-element.27.refs_5_.rest_0_, bf16[2048,512]{1,0:T(8,128)(2,1)S(1)} %get-tuple-element.29.refs_5_.rest_1_, bf16[2048,512]{1,0:T(8,128)(2,1)S(1)} %get-tuple-element.28.refs_6_.rest_2_, ...), custom_call_target="tpu_custom_call" | custom-call | flops 1048576000 | bytes 4194304 | tf_op jit(solution)/shard_map/factor/pallas_call | solution.py:285
  28.4 0.5 %collective-permute-done.9.proj_ref = f32[16,1024]{1,0:T(8,128)S(1)} collective-permute-done((f32[16,1024]{1,0:T(8,128)S(1)}, f32[16,1024]{1,0:T(8,128)S(1)}, u32[]{:S(2)}, u32[]{:S(2)}) %collective-permute-start.9) | collective-permute-done | bytes 65568 | tf_op jit(solution)/shard_map/ppermute | solution.py:433
  28.9 0.8 %factor.3.factor_ref = f32[16,1024]{1,0:T(8,128)S(1)} custom-call(f32[16,1024]{1,0:T(8,128)S(1)} %factor.2.before_ref, f32[16,1024]{1,0:T(8,128)S(1)} %collective-permute-done.9.proj_ref, bf16[2048,512]{1,0:T(8,128)(2,1)S(1)} %get-tuple-element.27.refs_5_.rest_0_, bf16[2048,512]{1,0:T(8,128)(2,1)S(1)} %get-tuple-element.29.refs_5_.rest_1_, ...), custom_call_target="tpu_custom_call" | custom-call | flops 1048576000 | bytes 4194304 | tf_op jit(solution)/shard_map/factor/pallas_call | solution.py:285
  29.7 0.8 %spread.2 = f32[16,1024]{1,0:T(8,128)S(1)} custom-call(f32[16,1024]{1,0:T(8,128)S(1)} %factor.3.factor_ref, bf16[1024,1024]{1,0:T(8,128)(2,1)S(1)} %get-tuple-element.31.high_ref, bf16[1024,1024]{1,0:T(8,128)(2,1)S(1)} %get-tuple-element.32.low_ref), custom_call_target="tpu_custom_call" | custom-call | flops 891289600 | bytes 4194304 | tf_op jit(solution)/shard_map/spread/pallas_call | solution.py:310
  30.5 0.2 collective-permute-start.10
  30.6 0.8 %spread.3 = f32[16,1024]{1,0:T(8,128)S(1)} custom-call(f32[16,1024]{1,0:T(8,128)S(1)} %factor.3.factor_ref, bf16[1024,1024]{1,0:T(8,128)(2,1)S(1)} %get-tuple-element.33.high_ref, bf16[1024,1024]{1,0:T(8,128)(2,1)S(1)} %get-tuple-element.34.low_ref), custom_call_target="tpu_custom_call" | custom-call | flops 891289600 | bytes 4194304 | tf_op jit(solution)/shard_map/spread/pallas_call | solution.py:310
  31.4 0.3 %collective-permute-done.10 = f32[16,1024]{1,0:T(8,128)S(1)} collective-permute-done((f32[16,1024]{1,0:T(8,128)S(1)}, f32[16,1024]{1,0:T(8,128)S(1)}, u32[]{:S(2)}, u32[]{:S(2)}) %collective-permute-start.10) | collective-permute-done | bytes 65568 | tf_op jit(solution)/shard_map/ppermute | solution.py:433
  31.7 0.6 %fusion = f32[16,1024]{1,0:T(8,128)} fusion(f32[16,1024]{1,0:T(8,128)S(1)} %spread.3, f32[16,1024]{1,0:T(8,128)S(1)} %collective-permute-done.10, f32[16,512]{1,0:T(8,128)S(1)} %taper.3.refs_4_, f32[16,512]{1,0:T(8,128)S(1)} %taper.2.refs_4_), kind=kLoop, calls=%fused_computation.1 | loop fusion | flops 49152 | bytes 262144 | tf_op jit(solution)/shard_map/add | solution.py:498
  (5 shorter events, 0.1 us)
Async XLA Ops:
  0.9 3.5 %collective-permute-start = (f32[16,1280]{1,0:T(8,128)S(1)}, f32[16,1280]{1,0:T(8,128)S(1)}, u32[]{:S(2)}, u32[]{:S(2)}) collective-permute-start(f32[16,1280]{1,0:T(8,128)S(1)} %get-tuple-element.20.stack_ref), channel_id=1, source_target_pairs={{1,0},{0,1},{3,2},{2,3},{5,4},{4,5},{7,6},{6,7},{9,8},{8,9},{11,10... | collective-permute-start | bytes 245768 | tf_op jit(solution)/shard_map/ppermute | solution.py:433
  1.4 13.6 %slice-start = ((s8[8388608]{0:T(1024)(128)(4,1)}), s8[4194304]{0:T(1024)(128)(4,1)S(1)}, s32[]{:S(2)}) async-start(s8[8388608]{0:T(1024)(128)(4,1)} %bitcast), calls=%async_computation | async-start | bytes 8388608
  4.4 10.6 %slice-start.1 = ((s8[8388608]{0:T(1024)(128)(4,1)}), s8[4194304]{0:T(1024)(128)(4,1)S(1)}, s32[]{:S(2)}) async-start(s8[8388608]{0:T(1024)(128)(4,1)} %bitcast), calls=%async_computation.1 | async-start | bytes 8388608
  4.4 11.8 %collective-permute-start.2 = (f32[16,1536]{1,0:T(8,128)S(1)}, f32[16,1536]{1,0:T(8,128)S(1)}, u32[]{:S(2)}, u32[]{:S(2)}) collective-permute-start(f32[16,1536]{1,0:T(8,128)S(1)} %strip.1.own_ref), channel_id=1, source_target_pairs={{0,1},{1,0},{2,4},{3,5},{4,2},{5,3},{6,8},{7,9},{8,6},{9,7},{10,12... | collective-permute-start | bytes 294920 | tf_op jit(solution)/shard_map/ppermute | solution.py:448
  4.5 11.7 %collective-permute-start.1 = (f32[16,1536]{1,0:T(8,128)S(1)}, f32[16,1536]{1,0:T(8,128)S(1)}, u32[]{:S(2)}, u32[]{:S(2)}) collective-permute-start(f32[16,1536]{1,0:T(8,128)S(1)} %strip.1.own_ref), channel_id=1, source_target_pairs={{0,2},{1,3},{2,0},{3,1},{4,6},{5,7},{6,4},{7,5},{8,10},{9,11},{10,... | collective-permute-start | bytes 294920 | tf_op jit(solution)/shard_map/ppermute | solution.py:448
  11.4 4.8 %copy-start = (s32[8,8]{1,0:T(8,128)S(1)}, s32[8,8]{1,0:T(8,128)}, u32[]{:S(2)}) copy-start(s32[8,8]{1,0:T(8,128)} %ids_ref.3) | copy-start | bytes 772
  11.4 4.8 %copy-start.1 = (s32[8]{0:T(128)S(1)}, s32[8]{0:T(128)}, u32[]{:S(2)}) copy-start(s32[8]{0:T(128)} %counts_ref.3) | copy-start | bytes 100
  11.4 7.2 %collective-permute-start.5 = (f32[16,1024]{1,0:T(8,128)S(1)}, f32[16,1024]{1,0:T(8,128)S(1)}, u32[]{:S(2)}, u32[]{:S(2)}) collective-permute-start(f32[16,1024]{1,0:T(8,128)S(1)} %add.11.rest_0_.refs_0_), channel_id=1, source_target_pairs={{0,6},{2,4},{4,2},{6,0},{8,14},{10,12},{12,10},{14,8},{16,22},{18,... | collective-permute-start | bytes 196616 | tf_op jit(solution)/shard_map/ppermute | solution.py:425
  12.9 5.7 %collective-permute-start.4 = (f32[16,1024]{1,0:T(8,128)S(1)}, f32[16,1024]{1,0:T(8,128)S(1)}, u32[]{:S(2)}, u32[]{:S(2)}) collective-permute-start(f32[16,1024]{1,0:T(8,128)S(1)} %add.11.rest_0_.refs_0_), channel_id=1, source_target_pairs={{0,4},{2,6},{4,0},{6,2},{8,12},{10,14},{12,8},{14,10},{16,20},{18,... | collective-permute-start | bytes 196616 | tf_op jit(solution)/shard_map/ppermute | solution.py:425
  13.1 5.6 %collective-permute-start.3 = (f32[16,1024]{1,0:T(8,128)S(1)}, f32[16,1024]{1,0:T(8,128)S(1)}, u32[]{:S(2)}, u32[]{:S(2)}) collective-permute-start(f32[16,1024]{1,0:T(8,128)S(1)} %add.11.rest_0_.refs_0_), channel_id=1, source_target_pairs={{0,2},{2,0},{4,6},{6,4},{8,10},{10,8},{12,14},{14,12},{16,18},{18,... | collective-permute-start | bytes 196616 | tf_op jit(solution)/shard_map/ppermute | solution.py:425
  18.7 8.0 %collective-permute-start.8 = (f32[16,1024]{1,0:T(8,128)S(1)}, f32[16,1024]{1,0:T(8,128)S(1)}, u32[]{:S(2)}, u32[]{:S(2)}) collective-permute-start(f32[16,1024]{1,0:T(8,128)S(1)} %add.18.rest_0_.refs_0_), channel_id=1, source_target_pairs={{0,24},{2,26},{4,28},{6,30},{8,16},{10,18},{12,20},{14,22},{16,8},... | collective-permute-start | bytes 196616 | tf_op jit(solution)/shard_map/ppermute | solution.py:425
  22.4 5.2 %collective-permute-start.7 = (f32[16,1024]{1,0:T(8,128)S(1)}, f32[16,1024]{1,0:T(8,128)S(1)}, u32[]{:S(2)}, u32[]{:S(2)}) collective-permute-start(f32[16,1024]{1,0:T(8,128)S(1)} %add.18.rest_0_.refs_0_), channel_id=1, source_target_pairs={{0,16},{2,18},{4,20},{6,22},{8,24},{10,26},{12,28},{14,30},{16,0},... | collective-permute-start | bytes 196616 | tf_op jit(solution)/shard_map/ppermute | solution.py:425
  22.4 5.2 %collective-permute-start.6 = (f32[16,1024]{1,0:T(8,128)S(1)}, f32[16,1024]{1,0:T(8,128)S(1)}, u32[]{:S(2)}, u32[]{:S(2)}) collective-permute-start(f32[16,1024]{1,0:T(8,128)S(1)} %add.18.rest_0_.refs_0_), channel_id=1, source_target_pairs={{0,8},{2,10},{4,12},{6,14},{8,0},{10,2},{12,4},{14,6},{16,24},{18,... | collective-permute-start | bytes 196616 | tf_op jit(solution)/shard_map/ppermute | solution.py:425
  27.6 1.3 %collective-permute-start.9 = (f32[16,1024]{1,0:T(8,128)S(1)}, f32[16,1024]{1,0:T(8,128)S(1)}, u32[]{:S(2)}, u32[]{:S(2)}) collective-permute-start(f32[16,1024]{1,0:T(8,128)S(1)} %add.19.proj_ref), channel_id=1, source_target_pairs={{1,0},{0,1},{3,2},{2,3},{5,4},{4,5},{7,6},{6,7},{9,8},{8,9},{11,10... | collective-permute-start | bytes 196616 | tf_op jit(solution)/shard_map/ppermute | solution.py:433
  30.5 1.3 %collective-permute-start.10 = (f32[16,1024]{1,0:T(8,128)S(1)}, f32[16,1024]{1,0:T(8,128)S(1)}, u32[]{:S(2)}, u32[]{:S(2)}) collective-permute-start(f32[16,1024]{1,0:T(8,128)S(1)} %spread.2), channel_id=1, source_target_pairs={{1,0},{0,1},{3,2},{2,3},{5,4},{4,5},{7,6},{6,7},{9,8},{8,9},{11,10... | collective-permute-start | bytes 196616 | tf_op jit(solution)/shard_map/ppermute | solution.py:433

commit v17 on v16

--- a/solution.py
+++ b/solution.py
@@ -17,7 +17,7 @@
 LOW_SCALE = 0.5
 NUGGET = 0.25
 LOG2E = math.log2(math.e)
-TAPER_RATE = LOG2E / COV_RANGE
+TAPER_RATE = 4.0 / TAPER_LEN
 CELL = 0.1
 TILE = 256
 LANES = 128
@@ -320,9 +320,9 @@
 
 def covariance(square):
     apart = square * lax.rsqrt(square)
-    remain = jnp.maximum(4.0 - apart * (4.0 / (TAPER_LEN * TAPER_RATE)), 0.0)
+    remain = jnp.maximum(4.0 - apart, 0.0)
     twice = remain * remain
-    return (jnp.exp2(-apart) * (twice * twice)) * (5.0 - remain)
+    return (jnp.exp2(apart * (-LOG2E / (COV_RANGE * TAPER_RATE))) * (twice * twice)) * (5.0 - remain)
 
 
 def taper_kernel(first, grain, ids_ref, counts_ref, own_ref, values_ref, coords_ref, *rest):
@@ -420,7 +420,7 @@
     for kind in range(len(rounds[turn])):
         pairs = []
         for j in range(groups):
-            step = rounds[(turn + half * (j % 2)) % len(rounds)][kind]
+            step = rounds[(turn + half * ((j + 1) % 2)) % len(rounds)][kind]
             pairs += [(i * groups + j, (i ^ step) * groups + j) for i in range(count)]
         got.append(lax.ppermute(value, (axis, other), pairs))
     return got

time: 32.5 us -> 32.4 us (level)
  transfers between devices with their start and end apart: 11 -> 11, of which waited for: 3 -> 4; matrix products, arithmetic and copies ran while one was open for 0% -> 0% of each run, Pallas kernels for 45% -> 45%
where the time goes in v17:
time: 32.4 us; the launch traced here: 32.3 us
  Pallas kernels  16.9 us (52%)
  starting transfers between devices  12.8 us (40%)
  waiting for transfers between devices  1.69 us (5%)
  other arithmetic  0.67 us (2%)
    ppermute x6, starting transfers between devices, butterfly_round(): got.append(lax.ppermute(value, (axis, other), pairs))  8.01 us
    pallas_call x2, Pallas kernels, project(): pl.pallas_call(functools.partial(project_kernel, scale, grain_of(scale *...  5.86 us
    pallas_call x2, Pallas kernels, taper(): pl.pallas_call(functools.partial(taper_kernel, first, grain_of(TAPER_RATE...  4.66 us
    ppermute x2, starting transfers between devices, paired(): return lax.ppermute(value, (axis, other), pairs)  4.07 us
    pallas_call x2, Pallas kernels, split_rows(): pl.pallas_call(functools.partial(split_kernel, first), out_shape=(pltpu.V...  2.29 us
    pallas_call x2, Pallas kernels, spread(): pl.pallas_call(functools.partial(spread_kernel, scale), out_shape=jax.Sha...  1.53 us
    pallas_call x2, Pallas kernels, factored(): pl.pallas_call(kernel, out_shape=jax.ShapeDtypeStruct((probes, rows), jnp...  1.53 us
    pallas_call x1, Pallas kernels, prepare(): pl.pallas_call(functools.partial(prepare_kernel, blocks), out_shape=(jax....  0.87 us
  transfers between devices with their start and end apart: 11, of which 4 were waited for; matrix products, arithmetic and copies ran while one was open for 0% of the time, Pallas kernels for 45%

profile of v17, /device:TPU:0, one launch (start us, length us, event | category | flops | bytes accessed | tf_op | source)
XLA Modules:
  0.0 32.3 jit_solution(15718417885706780615)
XLA Ops:
  0.0 0.9 %prepare.1 = (f32[16,1280]{1,0:T(8,128)S(1)}, f32[2,1024]{1,0:T(2,128)S(1)}) custom-call(f32[16,1024]{1,0:T(8,128)} %probes_ref.1, f32[2,1024]{1,0:T(2,128)} %locations_ref.1, f32[2,1024]{1,0:T(2,128)} %knots_ref.1), custom_call_target="tpu_custom_call" | custom-call | tf_op jit(solution)/shard_map/prepare/pallas_call | solution.py:100
  0.9 0.5 %collective-permute-start = (f32[16,1280]{1,0:T(8,128)S(1)}, f32[16,1280]{1,0:T(8,128)S(1)}, u32[]{:S(2)}, u32[]{:S(2)}) collective-permute-start(f32[16,1280]{1,0:T(8,128)S(1)} %get-tuple-element.20.stack_ref), channel_id=1, source_target_pairs={{1,0},{0,1},{3,2},{2,3},{5,4},{4,5},{7,6},{6,7},{9,8},{8,9},{11,10... | collective-permute-start | bytes 245768 | tf_op jit(solution)/shard_map/ppermute | solution.py:433
  1.4 0.0 slice-start
  1.4 3.0 %project.2 = (f32[16,1024]{1,0:T(8,128)S(1)}, bf16[1024,1024]{1,0:T(8,128)(2,1)S(1)}, bf16[1024,1024]{1,0:T(8,128)(2,1)S(1)}, f32[16,1280]{1,0:T(8,128)S(1)}) custom-call(f32[16,1280]{1,0:T(8,128)S(1)} %get-tuple-element.20.stack_ref, f32[2,1024]{1,0:T(2,128)S(1)} %get-tuple-element.21.knots_ref), custom_call_target="tpu_custom_call" | custom-call | flops 2936012800 | bytes 4194304 | tf_op jit(solution)/shard_map/project/pallas_call | solution.py:210
  4.4 0.0 collective-permute-done.below_ref.above_ref.stack_ref
  4.4 0.0 slice-start.1
  4.4 0.1 collective-permute-start.2
  4.5 3.9 %collective-permute-start.1 = (f32[16,1536]{1,0:T(8,128)S(1)}, f32[16,1536]{1,0:T(8,128)S(1)}, u32[]{:S(2)}, u32[]{:S(2)}) collective-permute-start(f32[16,1536]{1,0:T(8,128)S(1)} %strip.1.own_ref), channel_id=1, source_target_pairs={{0,2},{1,3},{2,0},{3,1},{4,6},{5,7},{6,4},{7,5},{8,10},{9,11},{10,... | collective-permute-start | bytes 294920 | tf_op jit(solution)/shard_map/ppermute | solution.py:448
  8.5 2.9 %project.3 = (f32[16,1024]{1,0:T(8,128)S(1)}, bf16[1024,1024]{1,0:T(8,128)(2,1)S(1)}, bf16[1024,1024]{1,0:T(8,128)(2,1)S(1)}) custom-call(f32[16,1280]{1,0:T(8,128)S(1)} %collective-permute-done.below_ref.above_ref.stack_ref, f32[2,1024]{1,0:T(2,128)S(1)} %get-tuple-element.21.knots_ref), custom_call_target="tpu_custom_call" | custom-call | flops 2936012800 | bytes 4194304 | tf_op jit(solution)/shard_map/project/pallas_call | solution.py:210
  11.4 0.0 copy-start
  11.4 0.0 copy-start.1
  11.4 3.7 %collective-permute-start.5 = (f32[16,1024]{1,0:T(8,128)S(1)}, f32[16,1024]{1,0:T(8,128)S(1)}, u32[]{:S(2)}, u32[]{:S(2)}) collective-permute-start(f32[16,1024]{1,0:T(8,128)S(1)} %add.11.rest_0_.refs_0_), channel_id=1, source_target_pairs={{0,24},{2,26},{4,28},{6,30},{8,16},{10,18},{12,20},{14,22},{16,8},... | collective-permute-start | bytes 196616 | tf_op jit(solution)/shard_map/ppermute | solution.py:425
  15.1 0.0 collective-permute-start.4
  15.1 0.8 %collective-permute-start.3 = (f32[16,1024]{1,0:T(8,128)S(1)}, f32[16,1024]{1,0:T(8,128)S(1)}, u32[]{:S(2)}, u32[]{:S(2)}) collective-permute-start(f32[16,1024]{1,0:T(8,128)S(1)} %add.11.rest_0_.refs_0_), channel_id=1, source_target_pairs={{0,8},{2,10},{4,12},{6,14},{8,0},{10,2},{12,4},{14,6},{16,24},{18,... | collective-permute-start | bytes 196616 | tf_op jit(solution)/shard_map/ppermute | solution.py:425
  15.9 0.0 slice-done
  15.9 0.0 slice-done.1
  15.9 1.1 %split.2 = (bf16[2048,512]{1,0:T(8,128)(2,1)S(1)}, bf16[2048,512]{1,0:T(8,128)(2,1)S(1)}) custom-call(f32[1024,2048]{1,0:T(8,128)S(1)} %bitcast.1, f32[16,1024]{1,0:T(8,128)S(1)} %add.11.rest_0_.refs_0_), custom_call_target="tpu_custom_call" | custom-call | flops 62914560 | bytes 4194304 | tf_op jit(solution)/shard_map/split/pallas_call | solution.py:244
  17.1 0.0 collective-permute-done.2.west_ref
  17.1 0.0 collective-permute-done.1.east_ref
  17.1 0.1 assemble.1
  17.1 0.0 copy-done
  17.2 0.0 copy-done.1
  17.2 2.3 %taper.2.refs_4_ = f32[16,512]{1,0:T(8,128)S(1)} custom-call(s32[8,8]{1,0:T(8,128)S(1)} %copy-done, s32[8]{0:T(128)S(1)} %copy-done.1, f32[16,1280]{1,0:T(8,128)S(1)} %get-tuple-element.22.own_ref, bf16[32,3968]{1,0:T(8,128)(2,1)S(1)} %get-tuple-element.23.values_ref, f32[2,3840]{1,0:T(2,128)S(1)} %get-tuple-element.24.coords_ref, ...), custom_call_target="tpu_custom_call" | custom-call | flops 262144000 | bytes 2097152 | tf_op jit(solution)/shard_map/taper/pallas_call | solution.py:379
  19.5 0.0 collective-permute-done.5.refs_3_
  19.5 0.8 %collective-permute-done.4.refs_2_ = f32[16,1024]{1,0:T(8,128)S(1)} collective-permute-done((f32[16,1024]{1,0:T(8,128)S(1)}, f32[16,1024]{1,0:T(8,128)S(1)}, u32[]{:S(2)}, u32[]{:S(2)}) %collective-permute-start.4) | collective-permute-done | bytes 65568 | tf_op jit(solution)/shard_map/ppermute | solution.py:425
  20.3 0.0 collective-permute-done.3.refs_1_
  20.3 1.5 %collective-permute-start.8 = (f32[16,1024]{1,0:T(8,128)S(1)}, f32[16,1024]{1,0:T(8,128)S(1)}, u32[]{:S(2)}, u32[]{:S(2)}) collective-permute-start(f32[16,1024]{1,0:T(8,128)S(1)} %add.18.rest_0_.refs_0_), channel_id=1, source_target_pairs={{0,6},{2,4},{4,2},{6,0},{8,14},{10,12},{12,10},{14,8},{16,22},{18,... | collective-permute-start | bytes 196616 | tf_op jit(solution)/shard_map/ppermute | solution.py:425
  21.8 1.4 %collective-permute-start.7 = (f32[16,1024]{1,0:T(8,128)S(1)}, f32[16,1024]{1,0:T(8,128)S(1)}, u32[]{:S(2)}, u32[]{:S(2)}) collective-permute-start(f32[16,1024]{1,0:T(8,128)S(1)} %add.18.rest_0_.refs_0_), channel_id=1, source_target_pairs={{0,4},{2,6},{4,0},{6,2},{8,12},{10,14},{12,8},{14,10},{16,20},{18,... | collective-permute-start | bytes 196616 | tf_op jit(solution)/shard_map/ppermute | solution.py:425
  23.2 0.7 %collective-permute-start.6 = (f32[16,1024]{1,0:T(8,128)S(1)}, f32[16,1024]{1,0:T(8,128)S(1)}, u32[]{:S(2)}, u32[]{:S(2)}) collective-permute-start(f32[16,1024]{1,0:T(8,128)S(1)} %add.18.rest_0_.refs_0_), channel_id=1, source_target_pairs={{0,2},{2,0},{4,6},{6,4},{8,10},{10,8},{12,14},{14,12},{16,18},{18,... | collective-permute-start | bytes 196616 | tf_op jit(solution)/shard_map/ppermute | solution.py:425
  23.9 1.1 %split.3 = (bf16[2048,512]{1,0:T(8,128)(2,1)S(1)}, bf16[2048,512]{1,0:T(8,128)(2,1)S(1)}) custom-call(f32[1024,2048]{1,0:T(8,128)S(1)} %bitcast.1, f32[16,1024]{1,0:T(8,128)S(1)} %add.18.rest_0_.refs_0_), custom_call_target="tpu_custom_call" | custom-call | flops 62914560 | bytes 4194304 | tf_op jit(solution)/shard_map/split/pallas_call | solution.py:244
  25.0 2.3 %taper.3.refs_4_ = f32[16,512]{1,0:T(8,128)S(1)} custom-call(s32[8,8]{1,0:T(8,128)S(1)} %copy-done, s32[8]{0:T(128)S(1)} %copy-done.1, f32[16,1280]{1,0:T(8,128)S(1)} %get-tuple-element.22.own_ref, bf16[32,3968]{1,0:T(8,128)(2,1)S(1)} %get-tuple-element.23.values_ref, f32[2,3840]{1,0:T(2,128)S(1)} %get-tuple-element.24.coords_ref, ...), custom_call_target="tpu_custom_call" | custom-call | flops 262144000 | bytes 2097152 | tf_op jit(solution)/shard_map/taper/pallas_call | solution.py:379
  27.4 0.0 collective-permute-done.8.refs_3_
  27.4 0.0 collective-permute-done.7.refs_2_
  27.4 0.1 collective-permute-done.6.refs_1_
  27.5 0.1 collective-permute-start.9
  27.6 0.8 %factor.2.before_ref = f32[16,1024]{1,0:T(8,128)S(1)} custom-call(f32[16,1024]{1,0:T(8,128)S(1)} %add.19.proj_ref, bf16[2048,512]{1,0:T(8,128)(2,1)S(1)} %get-tuple-element.27.refs_5_.rest_0_, bf16[2048,512]{1,0:T(8,128)(2,1)S(1)} %get-tuple-element.29.refs_5_.rest_1_, bf16[2048,512]{1,0:T(8,128)(2,1)S(1)} %get-tuple-element.28.refs_6_.rest_2_, ...), custom_call_target="tpu_custom_call" | custom-call | flops 1048576000 | bytes 4194304 | tf_op jit(solution)/shard_map/factor/pallas_call | solution.py:285
  28.3 0.5 %collective-permute-done.9.proj_ref = f32[16,1024]{1,0:T(8,128)S(1)} collective-permute-done((f32[16,1024]{1,0:T(8,128)S(1)}, f32[16,1024]{1,0:T(8,128)S(1)}, u32[]{:S(2)}, u32[]{:S(2)}) %collective-permute-start.9) | collective-permute-done | bytes 65568 | tf_op jit(solution)/shard_map/ppermute | solution.py:433
  28.8 0.8 %factor.3.factor_ref = f32[16,1024]{1,0:T(8,128)S(1)} custom-call(f32[16,1024]{1,0:T(8,128)S(1)} %factor.2.before_ref, f32[16,1024]{1,0:T(8,128)S(1)} %collective-permute-done.9.proj_ref, bf16[2048,512]{1,0:T(8,128)(2,1)S(1)} %get-tuple-element.27.refs_5_.rest_0_, bf16[2048,512]{1,0:T(8,128)(2,1)S(1)} %get-tuple-element.29.refs_5_.rest_1_, ...), custom_call_target="tpu_custom_call" | custom-call | flops 1048576000 | bytes 4194304 | tf_op jit(solution)/shard_map/factor/pallas_call | solution.py:285
  29.6 0.8 %spread.2 = f32[16,1024]{1,0:T(8,128)S(1)} custom-call(f32[16,1024]{1,0:T(8,128)S(1)} %factor.3.factor_ref, bf16[1024,1024]{1,0:T(8,128)(2,1)S(1)} %get-tuple-element.31.high_ref, bf16[1024,1024]{1,0:T(8,128)(2,1)S(1)} %get-tuple-element.32.low_ref), custom_call_target="tpu_custom_call" | custom-call | flops 891289600 | bytes 4194304 | tf_op jit(solution)/shard_map/spread/pallas_call | solution.py:310
  30.4 0.2 collective-permute-start.10
  30.5 0.8 %spread.3 = f32[16,1024]{1,0:T(8,128)S(1)} custom-call(f32[16,1024]{1,0:T(8,128)S(1)} %factor.3.factor_ref, bf16[1024,1024]{1,0:T(8,128)(2,1)S(1)} %get-tuple-element.33.high_ref, bf16[1024,1024]{1,0:T(8,128)(2,1)S(1)} %get-tuple-element.34.low_ref), custom_call_target="tpu_custom_call" | custom-call | flops 891289600 | bytes 4194304 | tf_op jit(solution)/shard_map/spread/pallas_call | solution.py:310
  31.3 0.3 %collective-permute-done.10 = f32[16,1024]{1,0:T(8,128)S(1)} collective-permute-done((f32[16,1024]{1,0:T(8,128)S(1)}, f32[16,1024]{1,0:T(8,128)S(1)}, u32[]{:S(2)}, u32[]{:S(2)}) %collective-permute-start.10) | collective-permute-done | bytes 65568 | tf_op jit(solution)/shard_map/ppermute | solution.py:433
  31.6 0.6 %fusion = f32[16,1024]{1,0:T(8,128)} fusion(f32[16,1024]{1,0:T(8,128)S(1)} %spread.3, f32[16,1024]{1,0:T(8,128)S(1)} %collective-permute-done.10, f32[16,512]{1,0:T(8,128)S(1)} %taper.3.refs_4_, f32[16,512]{1,0:T(8,128)S(1)} %taper.2.refs_4_), kind=kLoop, calls=%fused_computation.1 | loop fusion | flops 49152 | bytes 262144 | tf_op jit(solution)/shard_map/add | solution.py:498
  (5 shorter events, 0.1 us)
Async XLA Ops:
  0.9 3.5 %collective-permute-start = (f32[16,1280]{1,0:T(8,128)S(1)}, f32[16,1280]{1,0:T(8,128)S(1)}, u32[]{:S(2)}, u32[]{:S(2)}) collective-permute-start(f32[16,1280]{1,0:T(8,128)S(1)} %get-tuple-element.20.stack_ref), channel_id=1, source_target_pairs={{1,0},{0,1},{3,2},{2,3},{5,4},{4,5},{7,6},{6,7},{9,8},{8,9},{11,10... | collective-permute-start | bytes 245768 | tf_op jit(solution)/shard_map/ppermute | solution.py:433
  1.4 14.5 %slice-start = ((s8[8388608]{0:T(1024)(128)(4,1)}), s8[4194304]{0:T(1024)(128)(4,1)S(1)}, s32[]{:S(2)}) async-start(s8[8388608]{0:T(1024)(128)(4,1)} %bitcast), calls=%async_computation | async-start | bytes 8388608
  4.4 11.5 %slice-start.1 = ((s8[8388608]{0:T(1024)(128)(4,1)}), s8[4194304]{0:T(1024)(128)(4,1)S(1)}, s32[]{:S(2)}) async-start(s8[8388608]{0:T(1024)(128)(4,1)} %bitcast), calls=%async_computation.1 | async-start | bytes 8388608
  4.4 12.7 %collective-permute-start.2 = (f32[16,1536]{1,0:T(8,128)S(1)}, f32[16,1536]{1,0:T(8,128)S(1)}, u32[]{:S(2)}, u32[]{:S(2)}) collective-permute-start(f32[16,1536]{1,0:T(8,128)S(1)} %strip.1.own_ref), channel_id=1, source_target_pairs={{0,1},{1,0},{2,4},{3,5},{4,2},{5,3},{6,8},{7,9},{8,6},{9,7},{10,12... | collective-permute-start | bytes 294920 | tf_op jit(solution)/shard_map/ppermute | solution.py:448
  4.5 12.5 %collective-permute-start.1 = (f32[16,1536]{1,0:T(8,128)S(1)}, f32[16,1536]{1,0:T(8,128)S(1)}, u32[]{:S(2)}, u32[]{:S(2)}) collective-permute-start(f32[16,1536]{1,0:T(8,128)S(1)} %strip.1.own_ref), channel_id=1, source_target_pairs={{0,2},{1,3},{2,0},{3,1},{4,6},{5,7},{6,4},{7,5},{8,10},{9,11},{10,... | collective-permute-start | bytes 294920 | tf_op jit(solution)/shard_map/ppermute | solution.py:448
  11.4 5.7 %copy-start = (s32[8,8]{1,0:T(8,128)S(1)}, s32[8,8]{1,0:T(8,128)}, u32[]{:S(2)}) copy-start(s32[8,8]{1,0:T(8,128)} %ids_ref.3) | copy-start | bytes 772
  11.4 5.7 %copy-start.1 = (s32[8]{0:T(128)S(1)}, s32[8]{0:T(128)}, u32[]{:S(2)}) copy-start(s32[8]{0:T(128)} %counts_ref.3) | copy-start | bytes 100
  11.4 8.1 %collective-permute-start.5 = (f32[16,1024]{1,0:T(8,128)S(1)}, f32[16,1024]{1,0:T(8,128)S(1)}, u32[]{:S(2)}, u32[]{:S(2)}) collective-permute-start(f32[16,1024]{1,0:T(8,128)S(1)} %add.11.rest_0_.refs_0_), channel_id=1, source_target_pairs={{0,24},{2,26},{4,28},{6,30},{8,16},{10,18},{12,20},{14,22},{16,8},... | collective-permute-start | bytes 196616 | tf_op jit(solution)/shard_map/ppermute | solution.py:425
  15.1 5.2 %collective-permute-start.4 = (f32[16,1024]{1,0:T(8,128)S(1)}, f32[16,1024]{1,0:T(8,128)S(1)}, u32[]{:S(2)}, u32[]{:S(2)}) collective-permute-start(f32[16,1024]{1,0:T(8,128)S(1)} %add.11.rest_0_.refs_0_), channel_id=1, source_target_pairs={{0,16},{2,18},{4,20},{6,22},{8,24},{10,26},{12,28},{14,30},{16,0},... | collective-permute-start | bytes 196616 | tf_op jit(solution)/shard_map/ppermute | solution.py:425
  15.1 5.2 %collective-permute-start.3 = (f32[16,1024]{1,0:T(8,128)S(1)}, f32[16,1024]{1,0:T(8,128)S(1)}, u32[]{:S(2)}, u32[]{:S(2)}) collective-permute-start(f32[16,1024]{1,0:T(8,128)S(1)} %add.11.rest_0_.refs_0_), channel_id=1, source_target_pairs={{0,8},{2,10},{4,12},{6,14},{8,0},{10,2},{12,4},{14,6},{16,24},{18,... | collective-permute-start | bytes 196616 | tf_op jit(solution)/shard_map/ppermute | solution.py:425
  20.3 7.1 %collective-permute-start.8 = (f32[16,1024]{1,0:T(8,128)S(1)}, f32[16,1024]{1,0:T(8,128)S(1)}, u32[]{:S(2)}, u32[]{:S(2)}) collective-permute-start(f32[16,1024]{1,0:T(8,128)S(1)} %add.18.rest_0_.refs_0_), channel_id=1, source_target_pairs={{0,6},{2,4},{4,2},{6,0},{8,14},{10,12},{12,10},{14,8},{16,22},{18,... | collective-permute-start | bytes 196616 | tf_op jit(solution)/shard_map/ppermute | solution.py:425
  21.8 5.6 %collective-permute-start.7 = (f32[16,1024]{1,0:T(8,128)S(1)}, f32[16,1024]{1,0:T(8,128)S(1)}, u32[]{:S(2)}, u32[]{:S(2)}) collective-permute-start(f32[16,1024]{1,0:T(8,128)S(1)} %add.18.rest_0_.refs_0_), channel_id=1, source_target_pairs={{0,4},{2,6},{4,0},{6,2},{8,12},{10,14},{12,8},{14,10},{16,20},{18,... | collective-permute-start | bytes 196616 | tf_op jit(solution)/shard_map/ppermute | solution.py:425
  23.2 4.3 %collective-permute-start.6 = (f32[16,1024]{1,0:T(8,128)S(1)}, f32[16,1024]{1,0:T(8,128)S(1)}, u32[]{:S(2)}, u32[]{:S(2)}) collective-permute-start(f32[16,1024]{1,0:T(8,128)S(1)} %add.18.rest_0_.refs_0_), channel_id=1, source_target_pairs={{0,2},{2,0},{4,6},{6,4},{8,10},{10,8},{12,14},{14,12},{16,18},{18,... | collective-permute-start | bytes 196616 | tf_op jit(solution)/shard_map/ppermute | solution.py:425
  27.5 1.3 %collective-permute-start.9 = (f32[16,1024]{1,0:T(8,128)S(1)}, f32[16,1024]{1,0:T(8,128)S(1)}, u32[]{:S(2)}, u32[]{:S(2)}) collective-permute-start(f32[16,1024]{1,0:T(8,128)S(1)} %add.19.proj_ref), channel_id=1, source_target_pairs={{1,0},{0,1},{3,2},{2,3},{5,4},{4,5},{7,6},{6,7},{9,8},{8,9},{11,10... | collective-permute-start | bytes 196616 | tf_op jit(solution)/shard_map/ppermute | solution.py:433
  30.4 1.3 %collective-permute-start.10 = (f32[16,1024]{1,0:T(8,128)S(1)}, f32[16,1024]{1,0:T(8,128)S(1)}, u32[]{:S(2)}, u32[]{:S(2)}) collective-permute-start(f32[16,1024]{1,0:T(8,128)S(1)} %spread.2), channel_id=1, source_target_pairs={{1,0},{0,1},{3,2},{2,3},{5,4},{4,5},{7,6},{6,7},{9,8},{8,9},{11,10... | collective-permute-start | bytes 196616 | tf_op jit(solution)/shard_map/ppermute | solution.py:433

commit v18 on v17

--- a/solution.py
+++ b/solution.py
@@ -138,10 +138,10 @@
     )(below, own, above)
 
 
-def assemble_kernel(grain, own_ref, east_ref, west_ref, values_ref, coords_ref):
+def assemble_kernel(grain, own_ref, odd_ref, even_ref, values_ref, coords_ref):
     probes, width = own_ref.shape
     points = width - 2 * LANES
-    for turn, ref in enumerate((own_ref, east_ref, west_ref)):
+    for turn, ref in enumerate((own_ref, odd_ref, even_ref)):
         start = turn * points
         values_ref[:, start : start + points] = stacked_halves(ref[:, :points] * (1.0 / 256.0))
         for axis in range(2):
@@ -225,31 +225,6 @@
         cost_estimate=cost(2800, points * knots, 2),
         name="project",
     )(stack, knot_locs)
-
-
-def split_kernel(first, precision_ref, *rest):
-    high_ref, low_ref = rest[-2:]
-    depth, rows = high_ref.shape
-    tile = min(TILE, rows)
-    wide = min(TILE, depth)
-    for start in range(0, rows, tile):
-        for deep in range(0, depth, wide):
-            turned = jnp.transpose(precision_ref[first + start : first + start + tile, deep : deep + wide])
-            here = slice(deep, deep + wide), slice(start, start + tile)
-            high_ref[here], low_ref[here] = halves(turned)
-
-
-def split_rows(precision, first, rows, after):
-    depth = precision.shape[1]
-    return pl.pallas_call(
-        functools.partial(split_kernel, first),
-        out_shape=(pltpu.VMEM((depth, rows), jnp.bfloat16), pltpu.VMEM((depth, rows), jnp.bfloat16)),
-        in_specs=[VMEM] + [ANY] * len(after),
-        out_specs=(VMEM, VMEM),
-        compiler_params=pltpu.CompilerParams(vmem_limit_bytes=LIMIT),
-        cost_estimate=cost(60, rows * depth),
-        name="split",
-    )(precision, *after)
 
 
 def factor_kernel(scale, step, parts, before_ref, proj_ref, *rest):
@@ -325,8 +300,8 @@
     return (jnp.exp2(apart * (-LOG2E / (COV_RANGE * TAPER_RATE))) * (twice * twice)) * (5.0 - remain)
 
 
-def taper_kernel(first, grain, ids_ref, counts_ref, own_ref, values_ref, coords_ref, *rest):
-    out_ref = rest[-1]
+def beside_kernel(first, first_row, grain, ids_ref, counts_ref, own_ref, values_ref, coords_ref, precision_ref, *rest):
+    out_ref, high_ref, low_ref = rest[-3:]
     own_blocks, slots = ids_ref.shape
     block = LANES
     probes = own_ref.shape[0]
@@ -343,14 +318,21 @@
     def place(group, slot):
         ahead = ids_ref[group, slot] - (column - 1) * north_cells
         east = jnp.where(ahead >= north_cells, 1, 0) + jnp.where(ahead >= 2 * north_cells, 1, 0)
-        strip = jnp.where(east == 1, 0, 1 + lax.rem(column + lax.div(east, 2) + 1, 2))
+        strip = jnp.where(east == 1, 0, 2 - lax.rem(column + lax.div(east, 2) + 1, 2))
         index = strip * span + (ahead - east * north_cells - north_base)
         return lanes_of(index), lanes_of(jnp.where(slot < counts_ref[group], index, zeros_place))
 
     def lanes_of(index):
         return pl.ds(pl.multiple_of(index * block, block), block)
 
-    for index in range(out_ref.shape[1] // block):
+    depth, rows = high_ref.shape
+    tile = min(TILE, rows)
+    wide = min(TILE, depth)
+    tiles = [(start, deep) for start in range(0, rows, tile) for deep in range(0, depth, wide)]
+    groups = out_ref.shape[1] // block
+    turns = groups * -(-slots // 2)
+
+    for index in range(groups):
         group = first + index
         px, py = [turned[:, group : group + 1] for turned in own_columns]
         total = jnp.zeros((block, 2 * probes), jnp.float32)
@@ -368,23 +350,33 @@
             total = total + (
                 dot_nt(jnp.concatenate(highs, axis=1), part) + dot_nt(jnp.concatenate(lows, axis=1), part)
             )
+            turn = index * -(-slots // 2) + pair // 2
+            for start, deep in tiles[turn * len(tiles) // turns : (turn + 1) * len(tiles) // turns]:
+                from_row = first_row + start
+                turned = jnp.transpose(precision_ref[from_row : from_row + tile, deep : deep + wide])
+                here = slice(deep, deep + wide), slice(start, start + tile)
+                high_ref[here], low_ref[here] = halves(turned)
         out_ref[:, index * block : (index + 1) * block] = (
             TAPER_SCALE * folded_columns(total, probes)
             + NUGGET * own_ref[:, group * block : (group + 1) * block]
         )
 
 
-def taper(ids, counts, own, values, coords, extent, first, blocks, after):
-    slots = ids.shape[1]
-    return pl.pallas_call(
-        functools.partial(taper_kernel, first, grain_of(TAPER_RATE * extent)),
-        out_shape=jax.ShapeDtypeStruct((own.shape[0], blocks * LANES), jnp.float32),
-        in_specs=[SMEM, SMEM, VMEM, VMEM, VMEM] + [ANY] * len(after),
-        out_specs=VMEM,
+def beside_round(ids, counts, own, values, coords, precision, extent, first, blocks, first_row, rows, after):
+    slots, depth = ids.shape[1], precision.shape[1]
+    return pl.pallas_call(
+        functools.partial(beside_kernel, first, first_row, grain_of(TAPER_RATE * extent)),
+        out_shape=(
+            jax.ShapeDtypeStruct((own.shape[0], blocks * LANES), jnp.float32),
+            pltpu.VMEM((depth, rows), jnp.bfloat16),
+            pltpu.VMEM((depth, rows), jnp.bfloat16),
+        ),
+        in_specs=[SMEM, SMEM, VMEM, VMEM, VMEM, VMEM] + [ANY] * len(after),
+        out_specs=(VMEM, VMEM, VMEM),
         compiler_params=pltpu.CompilerParams(vmem_limit_bytes=LIMIT),
         cost_estimate=cost(500, blocks * slots * LANES * LANES, 2),
-        name="taper",
-    )(ids, counts, own, values, coords, *after)
+        name="beside",
+    )(ids, counts, own, values, coords, precision, *after)
 
 
 def add_kernel(count, *refs):
@@ -408,7 +400,7 @@
 def butterfly_rounds(count):
     assert count & (count - 1) == 0
     bits = [1 << i for i in range(count.bit_length() - 1)]
-    rounds = [(low, high, low | high) for low, high in zip(bits[0::2], bits[1::2])]
+    rounds = [(low | high, high, low) for low, high in zip(bits[0::2], bits[1::2])]
     return rounds + [(bit,) for bit in bits[len(rounds) * 2 :]]
 
 
@@ -465,29 +457,25 @@
     stack = parts[0][3]
 
     strip = make_strip(chunks[-1], stack, chunks[1 % groups])
-    values, coords = assemble([strip, paired(strip, "space", "knot", 0), paired(strip, "space", "knot", 1)], extent)
+    odd = paired(strip, "space", "knot", 1)
+    values, coords = assemble([strip, odd, paired(strip, "space", "knot", 0)], extent)
     projection = sum(part[0] for part in parts)
     rounds = len(butterfly_rounds(lax.axis_size("space")))
-    pieces = math.gcd(own_blocks, rounds)
-    per_piece = own_blocks // pieces
-    row_pieces = math.gcd(knot_precision.shape[0] // LANES, rounds)
-    per_split = knot_precision.shape[0] // row_pieces
+    pieces = math.gcd(math.gcd(own_blocks, rounds), knot_precision.shape[0] // LANES)
+    per_piece, per_split = own_blocks // pieces, knot_precision.shape[0] // pieces
     base, splits = [], []
     for turn in range(rounds):
         got = butterfly_round(projection, "space", "knot", turn)
         beside = []
         for i in range(pieces):
             if i * rounds // pieces == turn:
-                base.append(
-                    taper(
-                        neighbours, counts, stack, values, coords, extent, i * per_piece, per_piece, [projection]
-                    )
+                done = beside_round(
+                    neighbours, counts, stack, values, coords, knot_precision, extent,
+                    i * per_piece, per_piece, i * per_split, per_split, [projection],
                 )
-                beside.append(base[-1])
-        for i in range(row_pieces):
-            if i * rounds // row_pieces == turn:
-                splits.append(split_rows(knot_precision, i * per_split, per_split, [projection]))
-                beside.extend(splits[-1])
+                base.append(done[0])
+                splits.append(done[1:])
+                beside.extend(done)
         projection = add_all([projection, *got], beside)
     factor = factored(None, projection, splits, proj_scale, 0)
     for step in range(1, groups):

time: 32.4 us -> 32.4 us (level)
  waiting for transfers between devices: 1.69 us -> 2.61 us
  Pallas kernels: 16.9 us -> 16 us
    ppermute x6, waiting for transfers between devices: 0.87 us -> 1.79 us  [butterfly_round(): got.append(lax.ppermute(value, (axis, other), pairs))]
    pallas_call x4 -> x2, Pallas kernels: 6.96 us -> 6.05 us  [beside_round(): pl.pallas_call(functools.partial(beside_kernel, first, first_row, grain_o...]
  transfers between devices with their start and end apart: 11 -> 11, of which waited for: 4 -> 4; matrix products, arithmetic and copies ran while one was open for 0% -> 0% of each run, Pallas kernels for 45% -> 42%
where the time goes in v18:
time: 32.4 us; the launch traced here: 32.3 us
  Pallas kernels  16 us (49%)
  starting transfers between devices  12.8 us (40%)
  waiting for transfers between devices  2.61 us (8%)
  other arithmetic  0.68 us (2%)
    ppermute x6, starting transfers between devices, butterfly_round(): got.append(lax.ppermute(value, (axis, other), pairs))  8.01 us
    pallas_call x2, Pallas kernels, beside_round(): pl.pallas_call(functools.partial(beside_kernel, first, first_row, grain_o...  6.05 us
    pallas_call x2, Pallas kernels, project(): pl.pallas_call(functools.partial(project_kernel, scale, grain_of(scale *...  5.85 us
    ppermute x2, starting transfers between devices, paired(): return lax.ppermute(value, (axis, other), pairs)  4.07 us
    ppermute x6, waiting for transfers between devices, butterfly_round(): got.append(lax.ppermute(value, (axis, other), pairs))  1.79 us
    pallas_call x2, Pallas kernels, spread(): pl.pallas_call(functools.partial(spread_kernel, scale), out_shape=jax.Sha...  1.54 us
    pallas_call x2, Pallas kernels, factored(): pl.pallas_call(kernel, out_shape=jax.ShapeDtypeStruct((probes, rows), jnp...  1.53 us
    pallas_call x1, Pallas kernels, prepare(): pl.pallas_call(functools.partial(prepare_kernel, blocks), out_shape=(jax....  0.87 us
  transfers between devices with their start and end apart: 11, of which 4 were waited for; matrix products, arithmetic and copies ran while one was open for 0% of the time, Pallas kernels for 42%

profile of v18, /device:TPU:0, one launch (start us, length us, event | category | flops | bytes accessed | tf_op | source)
XLA Modules:
  0.0 32.3 jit_solution(13418891295395889957)
XLA Ops:
  0.0 0.9 %prepare.1 = (f32[16,1280]{1,0:T(8,128)S(1)}, f32[2,1024]{1,0:T(2,128)S(1)}) custom-call(f32[16,1024]{1,0:T(8,128)} %probes_ref.1, f32[2,1024]{1,0:T(2,128)} %locations_ref.1, f32[2,1024]{1,0:T(2,128)} %knots_ref.1), custom_call_target="tpu_custom_call" | custom-call | tf_op jit(solution)/shard_map/prepare/pallas_call | solution.py:100
  0.9 0.5 %collective-permute-start = (f32[16,1280]{1,0:T(8,128)S(1)}, f32[16,1280]{1,0:T(8,128)S(1)}, u32[]{:S(2)}, u32[]{:S(2)}) collective-permute-start(f32[16,1280]{1,0:T(8,128)S(1)} %get-tuple-element.22.stack_ref), channel_id=1, source_target_pairs={{1,0},{0,1},{3,2},{2,3},{5,4},{4,5},{7,6},{6,7},{9,8},{8,9},{11,10... | collective-permute-start | bytes 245768 | tf_op jit(solution)/shard_map/ppermute | solution.py:425
  1.4 0.0 slice-start
  1.4 2.9 %project.2 = (f32[16,1024]{1,0:T(8,128)S(1)}, bf16[1024,1024]{1,0:T(8,128)(2,1)S(1)}, bf16[1024,1024]{1,0:T(8,128)(2,1)S(1)}, f32[16,1280]{1,0:T(8,128)S(1)}) custom-call(f32[16,1280]{1,0:T(8,128)S(1)} %get-tuple-element.22.stack_ref, f32[2,1024]{1,0:T(2,128)S(1)} %get-tuple-element.23.knots_ref), custom_call_target="tpu_custom_call" | custom-call | flops 2936012800 | bytes 4194304 | tf_op jit(solution)/shard_map/project/pallas_call | solution.py:210
  4.4 0.0 collective-permute-done.below_ref.above_ref.stack_ref
  4.4 0.0 slice-start.1
  4.4 0.0 copy-start
  4.4 0.0 copy-start.1
  4.4 0.1 collective-permute-start.1
  4.6 3.9 %collective-permute-start.2 = (f32[16,1536]{1,0:T(8,128)S(1)}, f32[16,1536]{1,0:T(8,128)S(1)}, u32[]{:S(2)}, u32[]{:S(2)}) collective-permute-start(f32[16,1536]{1,0:T(8,128)S(1)} %strip.1.own_ref), channel_id=1, source_target_pairs={{0,2},{1,3},{2,0},{3,1},{4,6},{5,7},{6,4},{7,5},{8,10},{9,11},{10,... | collective-permute-start | bytes 294920 | tf_op jit(solution)/shard_map/ppermute | solution.py:440
  8.5 2.9 %project.3 = (f32[16,1024]{1,0:T(8,128)S(1)}, bf16[1024,1024]{1,0:T(8,128)(2,1)S(1)}, bf16[1024,1024]{1,0:T(8,128)(2,1)S(1)}) custom-call(f32[16,1280]{1,0:T(8,128)S(1)} %collective-permute-done.below_ref.above_ref.stack_ref, f32[2,1024]{1,0:T(2,128)S(1)} %get-tuple-element.23.knots_ref), custom_call_target="tpu_custom_call" | custom-call | flops 2936012800 | bytes 4194304 | tf_op jit(solution)/shard_map/project/pallas_call | solution.py:210
  11.5 3.7 %collective-permute-start.3 = (f32[16,1024]{1,0:T(8,128)S(1)}, f32[16,1024]{1,0:T(8,128)S(1)}, u32[]{:S(2)}, u32[]{:S(2)}) collective-permute-start(f32[16,1024]{1,0:T(8,128)S(1)} %add.11.rest_0_.refs_0_), channel_id=1, source_target_pairs={{0,24},{2,26},{4,28},{6,30},{8,16},{10,18},{12,20},{14,22},{16,8},... | collective-permute-start | bytes 196616 | tf_op jit(solution)/shard_map/ppermute | solution.py:417
  15.1 0.0 collective-permute-start.4
  15.1 0.8 %collective-permute-start.5 = (f32[16,1024]{1,0:T(8,128)S(1)}, f32[16,1024]{1,0:T(8,128)S(1)}, u32[]{:S(2)}, u32[]{:S(2)}) collective-permute-start(f32[16,1024]{1,0:T(8,128)S(1)} %add.11.rest_0_.refs_0_), channel_id=1, source_target_pairs={{0,8},{2,10},{4,12},{6,14},{8,0},{10,2},{12,4},{14,6},{16,24},{18,... | collective-permute-start | bytes 196616 | tf_op jit(solution)/shard_map/ppermute | solution.py:417
  15.9 0.0 collective-permute-done.1.odd_ref
  15.9 0.0 collective-permute-done.2.even_ref
  15.9 0.1 assemble.1
  16.0 0.0 slice-done
  16.0 0.0 slice-done.1
  16.0 0.0 copy-done
  16.0 0.0 copy-done.1
  16.0 3.0 %beside.2 = (f32[16,512]{1,0:T(8,128)S(1)}, bf16[2048,512]{1,0:T(8,128)(2,1)S(1)}, bf16[2048,512]{1,0:T(8,128)(2,1)S(1)}) custom-call(s32[8,8]{1,0:T(8,128)S(1)} %copy-done, s32[8]{0:T(128)S(1)} %copy-done.1, f32[16,1280]{1,0:T(8,128)S(1)} %get-tuple-element.24.own_ref, bf16[32,3968]{1,0:T(8,128)(2,1)S(1)} %get-tuple-element.25.values_ref, ...), custom_call_target="tpu_custom_call" | custom-call | flops 262144000 | bytes 2097152 | tf_op jit(solution)/shard_map/beside/pallas_call | solution.py:367
  19.1 0.0 collective-permute-done.3.refs_1_
  19.1 1.2 %collective-permute-done.4.refs_2_ = f32[16,1024]{1,0:T(8,128)S(1)} collective-permute-done((f32[16,1024]{1,0:T(8,128)S(1)}, f32[16,1024]{1,0:T(8,128)S(1)}, u32[]{:S(2)}, u32[]{:S(2)}) %collective-permute-start.4) | collective-permute-done | bytes 65568 | tf_op jit(solution)/shard_map/ppermute | solution.py:417
  20.3 0.0 collective-permute-done.5.refs_3_
  20.3 1.5 %collective-permute-start.6 = (f32[16,1024]{1,0:T(8,128)S(1)}, f32[16,1024]{1,0:T(8,128)S(1)}, u32[]{:S(2)}, u32[]{:S(2)}) collective-permute-start(f32[16,1024]{1,0:T(8,128)S(1)} %add.18.rest_0_.refs_0_), channel_id=1, source_target_pairs={{0,6},{2,4},{4,2},{6,0},{8,14},{10,12},{12,10},{14,8},{16,22},{18,... | collective-permute-start | bytes 196616 | tf_op jit(solution)/shard_map/ppermute | solution.py:417
  21.8 1.4 %collective-permute-start.7 = (f32[16,1024]{1,0:T(8,128)S(1)}, f32[16,1024]{1,0:T(8,128)S(1)}, u32[]{:S(2)}, u32[]{:S(2)}) collective-permute-start(f32[16,1024]{1,0:T(8,128)S(1)} %add.18.rest_0_.refs_0_), channel_id=1, source_target_pairs={{0,4},{2,6},{4,0},{6,2},{8,12},{10,14},{12,8},{14,10},{16,20},{18,... | collective-permute-start | bytes 196616 | tf_op jit(solution)/shard_map/ppermute | solution.py:417
  23.2 0.6 %collective-permute-start.8 = (f32[16,1024]{1,0:T(8,128)S(1)}, f32[16,1024]{1,0:T(8,128)S(1)}, u32[]{:S(2)}, u32[]{:S(2)}) collective-permute-start(f32[16,1024]{1,0:T(8,128)S(1)} %add.18.rest_0_.refs_0_), channel_id=1, source_target_pairs={{0,2},{2,0},{4,6},{6,4},{8,10},{10,8},{12,14},{14,12},{16,18},{18,... | collective-permute-start | bytes 196616 | tf_op jit(solution)/shard_map/ppermute | solution.py:417
  23.9 3.0 %beside.3 = (f32[16,512]{1,0:T(8,128)S(1)}, bf16[2048,512]{1,0:T(8,128)(2,1)S(1)}, bf16[2048,512]{1,0:T(8,128)(2,1)S(1)}) custom-call(s32[8,8]{1,0:T(8,128)S(1)} %copy-done, s32[8]{0:T(128)S(1)} %copy-done.1, f32[16,1280]{1,0:T(8,128)S(1)} %get-tuple-element.24.own_ref, bf16[32,3968]{1,0:T(8,128)(2,1)S(1)} %get-tuple-element.25.values_ref, ...), custom_call_target="tpu_custom_call" | custom-call | flops 262144000 | bytes 2097152 | tf_op jit(solution)/shard_map/beside/pallas_call | solution.py:367
  26.9 0.0 collective-permute-done.6.refs_1_
  26.9 0.0 collective-permute-done.7.refs_2_
  26.9 0.6 %collective-permute-done.8.refs_3_ = f32[16,1024]{1,0:T(8,128)S(1)} collective-permute-done((f32[16,1024]{1,0:T(8,128)S(1)}, f32[16,1024]{1,0:T(8,128)S(1)}, u32[]{:S(2)}, u32[]{:S(2)}) %collective-permute-start.8) | collective-permute-done | bytes 65568 | tf_op jit(solution)/shard_map/ppermute | solution.py:417
  27.5 0.1 collective-permute-start.9
  27.6 0.8 %factor.2.before_ref = f32[16,1024]{1,0:T(8,128)S(1)} custom-call(f32[16,1024]{1,0:T(8,128)S(1)} %add.19.proj_ref, bf16[2048,512]{1,0:T(8,128)(2,1)S(1)} %get-tuple-element.30.refs_5_.rest_0_, bf16[2048,512]{1,0:T(8,128)(2,1)S(1)} %get-tuple-element.33.refs_5_.rest_1_, bf16[2048,512]{1,0:T(8,128)(2,1)S(1)} %get-tuple-element.31.refs_6_.rest_2_, ...), custom_call_target="tpu_custom_call" | custom-call | flops 1048576000 | bytes 4194304 | tf_op jit(solution)/shard_map/factor/pallas_call | solution.py:260
  28.3 0.5 %collective-permute-done.9.proj_ref = f32[16,1024]{1,0:T(8,128)S(1)} collective-permute-done((f32[16,1024]{1,0:T(8,128)S(1)}, f32[16,1024]{1,0:T(8,128)S(1)}, u32[]{:S(2)}, u32[]{:S(2)}) %collective-permute-start.9) | collective-permute-done | bytes 65568 | tf_op jit(solution)/shard_map/ppermute | solution.py:425
  28.8 0.8 %factor.3.factor_ref = f32[16,1024]{1,0:T(8,128)S(1)} custom-call(f32[16,1024]{1,0:T(8,128)S(1)} %factor.2.before_ref, f32[16,1024]{1,0:T(8,128)S(1)} %collective-permute-done.9.proj_ref, bf16[2048,512]{1,0:T(8,128)(2,1)S(1)} %get-tuple-element.30.refs_5_.rest_0_, bf16[2048,512]{1,0:T(8,128)(2,1)S(1)} %get-tuple-element.33.refs_5_.rest_1_, ...), custom_call_target="tpu_custom_call" | custom-call | flops 1048576000 | bytes 4194304 | tf_op jit(solution)/shard_map/factor/pallas_call | solution.py:260
  29.6 0.8 %spread.2 = f32[16,1024]{1,0:T(8,128)S(1)} custom-call(f32[16,1024]{1,0:T(8,128)S(1)} %factor.3.factor_ref, bf16[1024,1024]{1,0:T(8,128)(2,1)S(1)} %get-tuple-element.35.high_ref, bf16[1024,1024]{1,0:T(8,128)(2,1)S(1)} %get-tuple-element.36.low_ref), custom_call_target="tpu_custom_call" | custom-call | flops 891289600 | bytes 4194304 | tf_op jit(solution)/shard_map/spread/pallas_call | solution.py:285
  30.4 0.2 collective-permute-start.10
  30.5 0.8 %spread.3 = f32[16,1024]{1,0:T(8,128)S(1)} custom-call(f32[16,1024]{1,0:T(8,128)S(1)} %factor.3.factor_ref, bf16[1024,1024]{1,0:T(8,128)(2,1)S(1)} %get-tuple-element.37.high_ref, bf16[1024,1024]{1,0:T(8,128)(2,1)S(1)} %get-tuple-element.38.low_ref), custom_call_target="tpu_custom_call" | custom-call | flops 891289600 | bytes 4194304 | tf_op jit(solution)/shard_map/spread/pallas_call | solution.py:285
  31.3 0.3 %collective-permute-done.10 = f32[16,1024]{1,0:T(8,128)S(1)} collective-permute-done((f32[16,1024]{1,0:T(8,128)S(1)}, f32[16,1024]{1,0:T(8,128)S(1)}, u32[]{:S(2)}, u32[]{:S(2)}) %collective-permute-start.10) | collective-permute-done | bytes 65568 | tf_op jit(solution)/shard_map/ppermute | solution.py:425
  31.6 0.6 %fusion = f32[16,1024]{1,0:T(8,128)} fusion(f32[16,1024]{1,0:T(8,128)S(1)} %spread.3, f32[16,1024]{1,0:T(8,128)S(1)} %collective-permute-done.10, f32[16,512]{1,0:T(8,128)S(1)} %get-tuple-element.32.refs_4_, f32[16,512]{1,0:T(8,128)S(1)} %get-tuple-element.29.refs_4_), kind=kLoop, calls=%fused_computation.1 | loop fusion | flops 49152 | bytes 262144 | tf_op jit(solution)/shard_map/add | solution.py:486
  (5 shorter events, 0.1 us)
Async XLA Ops:
  0.9 3.5 %collective-permute-start = (f32[16,1280]{1,0:T(8,128)S(1)}, f32[16,1280]{1,0:T(8,128)S(1)}, u32[]{:S(2)}, u32[]{:S(2)}) collective-permute-start(f32[16,1280]{1,0:T(8,128)S(1)} %get-tuple-element.22.stack_ref), channel_id=1, source_target_pairs={{1,0},{0,1},{3,2},{2,3},{5,4},{4,5},{7,6},{6,7},{9,8},{8,9},{11,10... | collective-permute-start | bytes 245768 | tf_op jit(solution)/shard_map/ppermute | solution.py:425
  1.4 14.6 %slice-start = ((s8[8388608]{0:T(1024)(128)(4,1)}), s8[4194304]{0:T(1024)(128)(4,1)S(1)}, s32[]{:S(2)}) async-start(s8[8388608]{0:T(1024)(128)(4,1)} %bitcast), calls=%async_computation | async-start | bytes 8388608
  4.4 11.6 %slice-start.1 = ((s8[8388608]{0:T(1024)(128)(4,1)}), s8[4194304]{0:T(1024)(128)(4,1)S(1)}, s32[]{:S(2)}) async-start(s8[8388608]{0:T(1024)(128)(4,1)} %bitcast), calls=%async_computation.1 | async-start | bytes 8388608
  4.4 11.6 %copy-start = (s32[8,8]{1,0:T(8,128)S(1)}, s32[8,8]{1,0:T(8,128)}, u32[]{:S(2)}) copy-start(s32[8,8]{1,0:T(8,128)} %ids_ref.3) | copy-start | bytes 772
  4.4 11.6 %copy-start.1 = (s32[8]{0:T(128)S(1)}, s32[8]{0:T(128)}, u32[]{:S(2)}) copy-start(s32[8]{0:T(128)} %counts_ref.3) | copy-start | bytes 100
  4.4 11.5 %collective-permute-start.1 = (f32[16,1536]{1,0:T(8,128)S(1)}, f32[16,1536]{1,0:T(8,128)S(1)}, u32[]{:S(2)}, u32[]{:S(2)}) collective-permute-start(f32[16,1536]{1,0:T(8,128)S(1)} %strip.1.own_ref), channel_id=1, source_target_pairs={{0,1},{1,0},{2,4},{3,5},{4,2},{5,3},{6,8},{7,9},{8,6},{9,7},{10,12... | collective-permute-start | bytes 294920 | tf_op jit(solution)/shard_map/ppermute | solution.py:440
  4.6 11.4 %collective-permute-start.2 = (f32[16,1536]{1,0:T(8,128)S(1)}, f32[16,1536]{1,0:T(8,128)S(1)}, u32[]{:S(2)}, u32[]{:S(2)}) collective-permute-start(f32[16,1536]{1,0:T(8,128)S(1)} %strip.1.own_ref), channel_id=1, source_target_pairs={{0,2},{1,3},{2,0},{3,1},{4,6},{5,7},{6,4},{7,5},{8,10},{9,11},{10,... | collective-permute-start | bytes 294920 | tf_op jit(solution)/shard_map/ppermute | solution.py:440
  11.5 7.6 %collective-permute-start.3 = (f32[16,1024]{1,0:T(8,128)S(1)}, f32[16,1024]{1,0:T(8,128)S(1)}, u32[]{:S(2)}, u32[]{:S(2)}) collective-permute-start(f32[16,1024]{1,0:T(8,128)S(1)} %add.11.rest_0_.refs_0_), channel_id=1, source_target_pairs={{0,24},{2,26},{4,28},{6,30},{8,16},{10,18},{12,20},{14,22},{16,8},... | collective-permute-start | bytes 196616 | tf_op jit(solution)/shard_map/ppermute | solution.py:417
  15.1 5.2 %collective-permute-start.4 = (f32[16,1024]{1,0:T(8,128)S(1)}, f32[16,1024]{1,0:T(8,128)S(1)}, u32[]{:S(2)}, u32[]{:S(2)}) collective-permute-start(f32[16,1024]{1,0:T(8,128)S(1)} %add.11.rest_0_.refs_0_), channel_id=1, source_target_pairs={{0,16},{2,18},{4,20},{6,22},{8,24},{10,26},{12,28},{14,30},{16,0},... | collective-permute-start | bytes 196616 | tf_op jit(solution)/shard_map/ppermute | solution.py:417
  15.1 5.2 %collective-permute-start.5 = (f32[16,1024]{1,0:T(8,128)S(1)}, f32[16,1024]{1,0:T(8,128)S(1)}, u32[]{:S(2)}, u32[]{:S(2)}) collective-permute-start(f32[16,1024]{1,0:T(8,128)S(1)} %add.11.rest_0_.refs_0_), channel_id=1, source_target_pairs={{0,8},{2,10},{4,12},{6,14},{8,0},{10,2},{12,4},{14,6},{16,24},{18,... | collective-permute-start | bytes 196616 | tf_op jit(solution)/shard_map/ppermute | solution.py:417
  20.3 6.6 %collective-permute-start.6 = (f32[16,1024]{1,0:T(8,128)S(1)}, f32[16,1024]{1,0:T(8,128)S(1)}, u32[]{:S(2)}, u32[]{:S(2)}) collective-permute-start(f32[16,1024]{1,0:T(8,128)S(1)} %add.18.rest_0_.refs_0_), channel_id=1, source_target_pairs={{0,6},{2,4},{4,2},{6,0},{8,14},{10,12},{12,10},{14,8},{16,22},{18,... | collective-permute-start | bytes 196616 | tf_op jit(solution)/shard_map/ppermute | solution.py:417
  21.8 5.1 %collective-permute-start.7 = (f32[16,1024]{1,0:T(8,128)S(1)}, f32[16,1024]{1,0:T(8,128)S(1)}, u32[]{:S(2)}, u32[]{:S(2)}) collective-permute-start(f32[16,1024]{1,0:T(8,128)S(1)} %add.18.rest_0_.refs_0_), channel_id=1, source_target_pairs={{0,4},{2,6},{4,0},{6,2},{8,12},{10,14},{12,8},{14,10},{16,20},{18,... | collective-permute-start | bytes 196616 | tf_op jit(solution)/shard_map/ppermute | solution.py:417
  23.2 4.3 %collective-permute-start.8 = (f32[16,1024]{1,0:T(8,128)S(1)}, f32[16,1024]{1,0:T(8,128)S(1)}, u32[]{:S(2)}, u32[]{:S(2)}) collective-permute-start(f32[16,1024]{1,0:T(8,128)S(1)} %add.18.rest_0_.refs_0_), channel_id=1, source_target_pairs={{0,2},{2,0},{4,6},{6,4},{8,10},{10,8},{12,14},{14,12},{16,18},{18,... | collective-permute-start | bytes 196616 | tf_op jit(solution)/shard_map/ppermute | solution.py:417
  27.5 1.3 %collective-permute-start.9 = (f32[16,1024]{1,0:T(8,128)S(1)}, f32[16,1024]{1,0:T(8,128)S(1)}, u32[]{:S(2)}, u32[]{:S(2)}) collective-permute-start(f32[16,1024]{1,0:T(8,128)S(1)} %add.19.proj_ref), channel_id=1, source_target_pairs={{1,0},{0,1},{3,2},{2,3},{5,4},{4,5},{7,6},{6,7},{9,8},{8,9},{11,10... | collective-permute-start | bytes 196616 | tf_op jit(solution)/shard_map/ppermute | solution.py:425
  30.4 1.3 %collective-permute-start.10 = (f32[16,1024]{1,0:T(8,128)S(1)}, f32[16,1024]{1,0:T(8,128)S(1)}, u32[]{:S(2)}, u32[]{:S(2)}) collective-permute-start(f32[16,1024]{1,0:T(8,128)S(1)} %spread.2), channel_id=1, source_target_pairs={{1,0},{0,1},{3,2},{2,3},{5,4},{4,5},{7,6},{6,7},{9,8},{8,9},{11,10... | collective-permute-start | bytes 196616 | tf_op jit(solution)/shard_map/ppermute | solution.py:425

commit v19 on v18

--- a/solution.py
+++ b/solution.py
@@ -180,16 +180,18 @@
     return (x + grain) - (grain - grain * HALF_GRAIN)
 
 
-def project_kernel(scale, grain, stack_ref, knots_ref, out_ref, high_ref, low_ref, *rest):
-    *copies, weights, columns = rest
+def project_kernel(scale, grain, follows, stack_ref, *rest):
+    if follows:
+        before_ref, columns, out_ref, high_ref, low_ref, weights = rest
+    else:
+        knots_ref, out_ref, high_ref, low_ref, columns, copy_ref, weights = rest
+        copy_ref[...] = stack_ref[...]
+        fill = jnp.zeros((6, knots_ref.shape[1]), jnp.float32)
+        columns[...] = jnp.transpose(jnp.concatenate([off_grid(knots_ref[...] * scale, grain), fill], axis=0))
     knots, points = high_ref.shape
     probes = stack_ref.shape[0]
     tile = min(TILE, knots)
-    for copy_ref in copies:
-        copy_ref[...] = stack_ref[...]
     weights[...] = padded_halves(stack_ref[:, :points], weights.shape[0])
-    fill = jnp.zeros((6, knots), jnp.float32)
-    columns[...] = jnp.transpose(jnp.concatenate([off_grid(knots_ref[...] * scale, grain), fill], axis=0))
     east, north = [on_grid(coordinate_rows(stack_ref, points, axis) * scale, grain) for axis in range(2)]
 
     for start in range(0, knots, tile):
@@ -202,29 +204,36 @@
             square = dx * dx + dy * dy
             high_ref[rows, lanes], low_ref[rows, lanes] = halves(jnp.exp2(-(square * lax.rsqrt(square))))
         total = dot_nt(high_ref[rows, :], weights[...]) + dot_nt(low_ref[rows, :], weights[...])
-        out_ref[:, rows] = folded_columns(total, probes)
-
-
-def project(stack, knot_locs, scale, extent, copies):
+        found = folded_columns(total, probes)
+        out_ref[:, rows] = found + before_ref[:, rows] if follows else found
+
+
+def project(stack, knot_locs, scale, extent, before=None):
     probes, points, knots = stack.shape[0], stack.shape[1] - 2 * LANES, knot_locs.shape[1]
-    return pl.pallas_call(
-        functools.partial(project_kernel, scale, grain_of(scale * extent)),
-        out_shape=(
-            jax.ShapeDtypeStruct((probes, knots), jnp.float32),
-            pltpu.VMEM((knots, points), jnp.bfloat16),
-            pltpu.VMEM((knots, points), jnp.bfloat16),
-            *[jax.ShapeDtypeStruct(stack.shape, jnp.float32)] * copies,
-        ),
-        in_specs=[VMEM, VMEM],
-        out_specs=(VMEM,) * (3 + copies),
-        scratch_shapes=[
-            pltpu.VMEM((LANES, points), jnp.bfloat16),
-            pltpu.VMEM((knots, 8), jnp.float32),
-        ],
+    out_shape = [
+        jax.ShapeDtypeStruct((probes, knots), jnp.float32),
+        pltpu.VMEM((knots, points), jnp.bfloat16),
+        pltpu.VMEM((knots, points), jnp.bfloat16),
+    ]
+    if before is None:
+        operands = (stack, knot_locs)
+        out_shape += [
+            jax.ShapeDtypeStruct((knots, 8), jnp.float32),
+            jax.ShapeDtypeStruct(stack.shape, jnp.float32),
+        ]
+    else:
+        operands = (stack, before[0], before[3])
+    found = pl.pallas_call(
+        functools.partial(project_kernel, scale, grain_of(scale * extent), before is not None),
+        out_shape=out_shape,
+        in_specs=[VMEM] * len(operands),
+        out_specs=[VMEM] * len(out_shape),
+        scratch_shapes=[pltpu.VMEM((LANES, points), jnp.bfloat16)],
         compiler_params=pltpu.CompilerParams(vmem_limit_bytes=LIMIT),
         cost_estimate=cost(2800, points * knots, 2),
         name="project",
-    )(stack, knot_locs)
+    )(*operands)
+    return found if before is None else [*found, *before[3:]]
 
 
 def factor_kernel(scale, step, parts, before_ref, proj_ref, *rest):
@@ -401,6 +410,7 @@
     assert count & (count - 1) == 0
     bits = [1 << i for i in range(count.bit_length() - 1)]
     rounds = [(low | high, high, low) for low, high in zip(bits[0::2], bits[1::2])]
+    rounds[1:] = [(high, both, low) for both, high, low in rounds[1:]]
     return rounds + [(bit,) for bit in bits[len(rounds) * 2 :]]
 
 
@@ -453,13 +463,15 @@
     chunks = [shifted(stack, "knot", step) for step in range(groups)]
     rate = LOG2E / knot_range
     extent = CELL * max(lax.axis_size("space"), groups * own_blocks)
-    parts = [project(chunk, knots, rate, extent, int(step == 0)) for step, chunk in enumerate(chunks)]
-    stack = parts[0][3]
+    parts = []
+    for chunk in chunks:
+        parts.append(project(chunk, knots, rate, extent, parts[-1] if parts else None))
+    stack = parts[0][4]
 
     strip = make_strip(chunks[-1], stack, chunks[1 % groups])
     odd = paired(strip, "space", "knot", 1)
     values, coords = assemble([strip, odd, paired(strip, "space", "knot", 0)], extent)
-    projection = sum(part[0] for part in parts)
+    projection = parts[-1][0]
     rounds = len(butterfly_rounds(lax.axis_size("space")))
     pieces = math.gcd(math.gcd(own_blocks, rounds), knot_precision.shape[0] // LANES)
     per_piece, per_split = own_blocks // pieces, knot_precision.shape[0] // pieces

time: 32.4 us -> 32.3 us (level)
  waiting for transfers between devices: 2.61 us -> 2.97 us
    ppermute x6, waiting for transfers between devices: 1.79 us -> 2.15 us  [butterfly_round(): got.append(lax.ppermute(value, (axis, other), pairs))]
  transfers between devices with their start and end apart: 11 -> 11, of which waited for: 4 -> 5; matrix products, arithmetic and copies ran while one was open for 0% -> 0% of each run, Pallas kernels for 42% -> 41%
where the time goes in v19:
time: 32.3 us; the launch traced here: 32.2 us
  Pallas kernels  15.8 us (49%)
  starting transfers between devices  12.6 us (39%)
  waiting for transfers between devices  2.97 us (9%)
  other arithmetic  0.64 us (2%)
    ppermute x6, starting transfers between devices, butterfly_round(): got.append(lax.ppermute(value, (axis, other), pairs))  7.78 us
    pallas_call x2, Pallas kernels, beside_round(): pl.pallas_call(functools.partial(beside_kernel, first, first_row, grain_o...  6.05 us
    pallas_call x2, Pallas kernels, project(): pl.pallas_call(functools.partial(project_kernel, scale, grain_of(scale *...  5.71 us
    ppermute x2, starting transfers between devices, paired(): return lax.ppermute(value, (axis, other), pairs)  4.07 us
    ppermute x6, waiting for transfers between devices, butterfly_round(): got.append(lax.ppermute(value, (axis, other), pairs))  2.15 us
    pallas_call x2, Pallas kernels, spread(): pl.pallas_call(functools.partial(spread_kernel, scale), out_shape=jax.Sha...  1.53 us
    pallas_call x2, Pallas kernels, factored(): pl.pallas_call(kernel, out_shape=jax.ShapeDtypeStruct((probes, rows), jnp...  1.53 us
    pallas_call x1, Pallas kernels, prepare(): pl.pallas_call(functools.partial(prepare_kernel, blocks), out_shape=(jax....  0.87 us
  transfers between devices with their start and end apart: 11, of which 5 were waited for; matrix products, arithmetic and copies ran while one was open for 0% of the time, Pallas kernels for 41%

profile of v19, /device:TPU:0, one launch (start us, length us, event | category | flops | bytes accessed | tf_op | source)
XLA Modules:
  0.0 32.2 jit_solution(12950522435441510746)
XLA Ops:
  0.0 0.9 %prepare.1 = (f32[16,1280]{1,0:T(8,128)S(1)}, f32[2,1024]{1,0:T(2,128)S(1)}) custom-call(f32[16,1024]{1,0:T(8,128)} %probes_ref.1, f32[2,1024]{1,0:T(2,128)} %locations_ref.1, f32[2,1024]{1,0:T(2,128)} %knots_ref.1), custom_call_target="tpu_custom_call" | custom-call | tf_op jit(solution)/shard_map/prepare/pallas_call | solution.py:100
  0.9 0.5 %collective-permute-start = (f32[16,1280]{1,0:T(8,128)S(1)}, f32[16,1280]{1,0:T(8,128)S(1)}, u32[]{:S(2)}, u32[]{:S(2)}) collective-permute-start(f32[16,1280]{1,0:T(8,128)S(1)} %get-tuple-element.23.stack_ref), channel_id=1, source_target_pairs={{1,0},{0,1},{3,2},{2,3},{5,4},{4,5},{7,6},{6,7},{9,8},{8,9},{11,10... | collective-permute-start | bytes 245768 | tf_op jit(solution)/shard_map/ppermute | solution.py:435
  1.4 0.0 slice-start
  1.4 3.0 %project.2 = (f32[16,1024]{1,0:T(8,128)S(1)}, bf16[1024,1024]{1,0:T(8,128)(2,1)S(1)}, bf16[1024,1024]{1,0:T(8,128)(2,1)S(1)}, f32[1024,8]{1,0:T(8,128)S(1)}, f32[16,1280]{1,0:T(8,128)S(1)}) custom-call(f32[16,1280]{1,0:T(8,128)S(1)} %get-tuple-element.23.stack_ref, f32[2,1024]{1,0:T(2,128)S(1)} %get-tuple-element.24.rest_0_), custom_call_target="tpu_custom_call" | custom-call | flops 2936012800 | bytes 4194304 | tf_op jit(solution)/shard_map/project/pallas_call | solution.py:226
  4.4 0.0 collective-permute-done.below_ref.above_ref.stack_ref
  4.4 0.0 slice-start.1
  4.4 0.1 collective-permute-start.1
  4.5 3.9 %collective-permute-start.2 = (f32[16,1536]{1,0:T(8,128)S(1)}, f32[16,1536]{1,0:T(8,128)S(1)}, u32[]{:S(2)}, u32[]{:S(2)}) collective-permute-start(f32[16,1536]{1,0:T(8,128)S(1)} %strip.1.own_ref), channel_id=1, source_target_pairs={{0,2},{1,3},{2,0},{3,1},{4,6},{5,7},{6,4},{7,5},{8,10},{9,11},{10,... | collective-permute-start | bytes 294920 | tf_op jit(solution)/shard_map/ppermute | solution.py:450
  8.5 0.0 copy-start
  8.5 0.0 copy-start.1
  8.5 2.7 %project.3 = (f32[16,1024]{1,0:T(8,128)S(1)}, bf16[1024,1024]{1,0:T(8,128)(2,1)S(1)}, bf16[1024,1024]{1,0:T(8,128)(2,1)S(1)}) custom-call(f32[16,1280]{1,0:T(8,128)S(1)} %collective-permute-done.below_ref.above_ref.stack_ref, f32[16,1024]{1,0:T(8,128)S(1)} %get-tuple-element.28.rest_0_, f32[1024,8]{1,0:T(8,128)S(1)} %get-tuple-element.29.rest_1_), custom_call_target="tpu_custom_call" | custom-call | flops 2936012800 | bytes 4194304 | tf_op jit(solution)/shard_map/project/pallas_call | solution.py:226
  11.2 2.6 %collective-permute-start.3 = (f32[16,1024]{1,0:T(8,128)S(1)}, f32[16,1024]{1,0:T(8,128)S(1)}, u32[]{:S(2)}, u32[]{:S(2)}) collective-permute-start(f32[16,1024]{1,0:T(8,128)S(1)} %get-tuple-element.30.rest_0_.refs_0_), channel_id=1, source_target_pairs={{0,16},{2,18},{4,20},{6,22},{8,24},{10,26},{12,28},{14,30},{16,0},... | collective-permute-start | bytes 196616 | tf_op jit(solution)/shard_map/ppermute | solution.py:427
  13.9 1.3 %collective-permute-start.4 = (f32[16,1024]{1,0:T(8,128)S(1)}, f32[16,1024]{1,0:T(8,128)S(1)}, u32[]{:S(2)}, u32[]{:S(2)}) collective-permute-start(f32[16,1024]{1,0:T(8,128)S(1)} %get-tuple-element.30.rest_0_.refs_0_), channel_id=1, source_target_pairs={{0,24},{2,26},{4,28},{6,30},{8,16},{10,18},{12,20},{14,22},{16,8},... | collective-permute-start | bytes 196616 | tf_op jit(solution)/shard_map/ppermute | solution.py:427
  15.2 0.2 collective-permute-start.5
  15.5 0.0 collective-permute-done.1.odd_ref
  15.5 0.0 collective-permute-done.2.even_ref
  15.5 0.1 assemble.1
  15.5 0.0 slice-done
  15.5 0.0 slice-done.1
  15.6 0.0 copy-done
  15.6 0.0 copy-done.1
  15.6 3.0 %beside.2 = (f32[16,512]{1,0:T(8,128)S(1)}, bf16[2048,512]{1,0:T(8,128)(2,1)S(1)}, bf16[2048,512]{1,0:T(8,128)(2,1)S(1)}) custom-call(s32[8,8]{1,0:T(8,128)S(1)} %copy-done, s32[8]{0:T(128)S(1)} %copy-done.1, f32[16,1280]{1,0:T(8,128)S(1)} %get-tuple-element.25.own_ref, bf16[32,3968]{1,0:T(8,128)(2,1)S(1)} %get-tuple-element.26.values_ref, ...), custom_call_target="tpu_custom_call" | custom-call | flops 262144000 | bytes 2097152 | tf_op jit(solution)/shard_map/beside/pallas_call | solution.py:376
  18.6 0.0 collective-permute-done.3.refs_1_
  18.6 1.4 %collective-permute-done.4.refs_2_ = f32[16,1024]{1,0:T(8,128)S(1)} collective-permute-done((f32[16,1024]{1,0:T(8,128)S(1)}, f32[16,1024]{1,0:T(8,128)S(1)}, u32[]{:S(2)}, u32[]{:S(2)}) %collective-permute-start.4) | collective-permute-done | bytes 65568 | tf_op jit(solution)/shard_map/ppermute | solution.py:427
  20.1 0.1 collective-permute-done.5.refs_3_
  20.2 1.5 %collective-permute-start.6 = (f32[16,1024]{1,0:T(8,128)S(1)}, f32[16,1024]{1,0:T(8,128)S(1)}, u32[]{:S(2)}, u32[]{:S(2)}) collective-permute-start(f32[16,1024]{1,0:T(8,128)S(1)} %add.14.rest_0_.refs_0_), channel_id=1, source_target_pairs={{0,6},{2,4},{4,2},{6,0},{8,14},{10,12},{12,10},{14,8},{16,22},{18,... | collective-permute-start | bytes 196616 | tf_op jit(solution)/shard_map/ppermute | solution.py:427
  21.7 1.4 %collective-permute-start.7 = (f32[16,1024]{1,0:T(8,128)S(1)}, f32[16,1024]{1,0:T(8,128)S(1)}, u32[]{:S(2)}, u32[]{:S(2)}) collective-permute-start(f32[16,1024]{1,0:T(8,128)S(1)} %add.14.rest_0_.refs_0_), channel_id=1, source_target_pairs={{0,4},{2,6},{4,0},{6,2},{8,12},{10,14},{12,8},{14,10},{16,20},{18,... | collective-permute-start | bytes 196616 | tf_op jit(solution)/shard_map/ppermute | solution.py:427
  23.1 0.6 %collective-permute-start.8 = (f32[16,1024]{1,0:T(8,128)S(1)}, f32[16,1024]{1,0:T(8,128)S(1)}, u32[]{:S(2)}, u32[]{:S(2)}) collective-permute-start(f32[16,1024]{1,0:T(8,128)S(1)} %add.14.rest_0_.refs_0_), channel_id=1, source_target_pairs={{0,2},{2,0},{4,6},{6,4},{8,10},{10,8},{12,14},{14,12},{16,18},{18,... | collective-permute-start | bytes 196616 | tf_op jit(solution)/shard_map/ppermute | solution.py:427
  23.8 3.0 %beside.3 = (f32[16,512]{1,0:T(8,128)S(1)}, bf16[2048,512]{1,0:T(8,128)(2,1)S(1)}, bf16[2048,512]{1,0:T(8,128)(2,1)S(1)}) custom-call(s32[8,8]{1,0:T(8,128)S(1)} %copy-done, s32[8]{0:T(128)S(1)} %copy-done.1, f32[16,1280]{1,0:T(8,128)S(1)} %get-tuple-element.25.own_ref, bf16[32,3968]{1,0:T(8,128)(2,1)S(1)} %get-tuple-element.26.values_ref, ...), custom_call_target="tpu_custom_call" | custom-call | flops 262144000 | bytes 2097152 | tf_op jit(solution)/shard_map/beside/pallas_call | solution.py:376
  26.8 0.0 collective-permute-done.6.refs_1_
  26.8 0.0 collective-permute-done.7.refs_2_
  26.8 0.6 %collective-permute-done.8.refs_3_ = f32[16,1024]{1,0:T(8,128)S(1)} collective-permute-done((f32[16,1024]{1,0:T(8,128)S(1)}, f32[16,1024]{1,0:T(8,128)S(1)}, u32[]{:S(2)}, u32[]{:S(2)}) %collective-permute-start.8) | collective-permute-done | bytes 65568 | tf_op jit(solution)/shard_map/ppermute | solution.py:427
  27.4 0.1 collective-permute-start.9
  27.5 0.8 %factor.2.before_ref = f32[16,1024]{1,0:T(8,128)S(1)} custom-call(f32[16,1024]{1,0:T(8,128)S(1)} %add.15.proj_ref, bf16[2048,512]{1,0:T(8,128)(2,1)S(1)} %get-tuple-element.32.refs_5_.rest_0_, bf16[2048,512]{1,0:T(8,128)(2,1)S(1)} %get-tuple-element.35.refs_5_.rest_1_, bf16[2048,512]{1,0:T(8,128)(2,1)S(1)} %get-tuple-element.33.refs_6_.rest_2_, ...), custom_call_target="tpu_custom_call" | custom-call | flops 1048576000 | bytes 4194304 | tf_op jit(solution)/shard_map/factor/pallas_call | solution.py:269
  28.3 0.5 %collective-permute-done.9.proj_ref = f32[16,1024]{1,0:T(8,128)S(1)} collective-permute-done((f32[16,1024]{1,0:T(8,128)S(1)}, f32[16,1024]{1,0:T(8,128)S(1)}, u32[]{:S(2)}, u32[]{:S(2)}) %collective-permute-start.9) | collective-permute-done | bytes 65568 | tf_op jit(solution)/shard_map/ppermute | solution.py:435
  28.7 0.8 %factor.3.factor_ref = f32[16,1024]{1,0:T(8,128)S(1)} custom-call(f32[16,1024]{1,0:T(8,128)S(1)} %factor.2.before_ref, f32[16,1024]{1,0:T(8,128)S(1)} %collective-permute-done.9.proj_ref, bf16[2048,512]{1,0:T(8,128)(2,1)S(1)} %get-tuple-element.32.refs_5_.rest_0_, bf16[2048,512]{1,0:T(8,128)(2,1)S(1)} %get-tuple-element.35.refs_5_.rest_1_, ...), custom_call_target="tpu_custom_call" | custom-call | flops 1048576000 | bytes 4194304 | tf_op jit(solution)/shard_map/factor/pallas_call | solution.py:269
  29.5 0.8 %spread.2 = f32[16,1024]{1,0:T(8,128)S(1)} custom-call(f32[16,1024]{1,0:T(8,128)S(1)} %factor.3.factor_ref, bf16[1024,1024]{1,0:T(8,128)(2,1)S(1)} %get-tuple-element.37.high_ref, bf16[1024,1024]{1,0:T(8,128)(2,1)S(1)} %get-tuple-element.38.low_ref), custom_call_target="tpu_custom_call" | custom-call | flops 891289600 | bytes 4194304 | tf_op jit(solution)/shard_map/spread/pallas_call | solution.py:294
  30.3 0.2 collective-permute-start.10
  30.4 0.8 %spread.3 = f32[16,1024]{1,0:T(8,128)S(1)} custom-call(f32[16,1024]{1,0:T(8,128)S(1)} %factor.3.factor_ref, bf16[1024,1024]{1,0:T(8,128)(2,1)S(1)} %get-tuple-element.39.high_ref, bf16[1024,1024]{1,0:T(8,128)(2,1)S(1)} %get-tuple-element.40.low_ref), custom_call_target="tpu_custom_call" | custom-call | flops 891289600 | bytes 4194304 | tf_op jit(solution)/shard_map/spread/pallas_call | solution.py:294
  31.2 0.3 %collective-permute-done.10 = f32[16,1024]{1,0:T(8,128)S(1)} collective-permute-done((f32[16,1024]{1,0:T(8,128)S(1)}, f32[16,1024]{1,0:T(8,128)S(1)}, u32[]{:S(2)}, u32[]{:S(2)}) %collective-permute-start.10) | collective-permute-done | bytes 65568 | tf_op jit(solution)/shard_map/ppermute | solution.py:435
  31.5 0.6 %fusion = f32[16,1024]{1,0:T(8,128)} fusion(f32[16,1024]{1,0:T(8,128)S(1)} %spread.3, f32[16,1024]{1,0:T(8,128)S(1)} %collective-permute-done.10, f32[16,512]{1,0:T(8,128)S(1)} %get-tuple-element.34.refs_4_, f32[16,512]{1,0:T(8,128)S(1)} %get-tuple-element.31.refs_4_), kind=kLoop, calls=%fused_computation.1 | loop fusion | flops 49152 | bytes 262144 | tf_op jit(solution)/shard_map/add | solution.py:498
  (4 shorter events, 0.1 us)
Async XLA Ops:
  0.9 3.5 %collective-permute-start = (f32[16,1280]{1,0:T(8,128)S(1)}, f32[16,1280]{1,0:T(8,128)S(1)}, u32[]{:S(2)}, u32[]{:S(2)}) collective-permute-start(f32[16,1280]{1,0:T(8,128)S(1)} %get-tuple-element.23.stack_ref), channel_id=1, source_target_pairs={{1,0},{0,1},{3,2},{2,3},{5,4},{4,5},{7,6},{6,7},{9,8},{8,9},{11,10... | collective-permute-start | bytes 245768 | tf_op jit(solution)/shard_map/ppermute | solution.py:435
  1.4 14.1 %slice-start = ((s8[8388608]{0:T(1024)(128)(4,1)}), s8[4194304]{0:T(1024)(128)(4,1)S(1)}, s32[]{:S(2)}) async-start(s8[8388608]{0:T(1024)(128)(4,1)} %bitcast), calls=%async_computation | async-start | bytes 8388608
  4.4 11.2 %slice-start.1 = ((s8[8388608]{0:T(1024)(128)(4,1)}), s8[4194304]{0:T(1024)(128)(4,1)S(1)}, s32[]{:S(2)}) async-start(s8[8388608]{0:T(1024)(128)(4,1)} %bitcast), calls=%async_computation.1 | async-start | bytes 8388608
  4.4 11.1 %collective-permute-start.1 = (f32[16,1536]{1,0:T(8,128)S(1)}, f32[16,1536]{1,0:T(8,128)S(1)}, u32[]{:S(2)}, u32[]{:S(2)}) collective-permute-start(f32[16,1536]{1,0:T(8,128)S(1)} %strip.1.own_ref), channel_id=1, source_target_pairs={{0,1},{1,0},{2,4},{3,5},{4,2},{5,3},{6,8},{7,9},{8,6},{9,7},{10,12... | collective-permute-start | bytes 294920 | tf_op jit(solution)/shard_map/ppermute | solution.py:450
  4.5 10.9 %collective-permute-start.2 = (f32[16,1536]{1,0:T(8,128)S(1)}, f32[16,1536]{1,0:T(8,128)S(1)}, u32[]{:S(2)}, u32[]{:S(2)}) collective-permute-start(f32[16,1536]{1,0:T(8,128)S(1)} %strip.1.own_ref), channel_id=1, source_target_pairs={{0,2},{1,3},{2,0},{3,1},{4,6},{5,7},{6,4},{7,5},{8,10},{9,11},{10,... | collective-permute-start | bytes 294920 | tf_op jit(solution)/shard_map/ppermute | solution.py:450
  8.5 7.1 %copy-start = (s32[8,8]{1,0:T(8,128)S(1)}, s32[8,8]{1,0:T(8,128)}, u32[]{:S(2)}) copy-start(s32[8,8]{1,0:T(8,128)} %ids_ref.3) | copy-start | bytes 772
  8.5 7.1 %copy-start.1 = (s32[8]{0:T(128)S(1)}, s32[8]{0:T(128)}, u32[]{:S(2)}) copy-start(s32[8]{0:T(128)} %counts_ref.3) | copy-start | bytes 100
  11.2 7.4 %collective-permute-start.3 = (f32[16,1024]{1,0:T(8,128)S(1)}, f32[16,1024]{1,0:T(8,128)S(1)}, u32[]{:S(2)}, u32[]{:S(2)}) collective-permute-start(f32[16,1024]{1,0:T(8,128)S(1)} %get-tuple-element.30.rest_0_.refs_0_), channel_id=1, source_target_pairs={{0,16},{2,18},{4,20},{6,22},{8,24},{10,26},{12,28},{14,30},{16,0},... | collective-permute-start | bytes 196616 | tf_op jit(solution)/shard_map/ppermute | solution.py:427
  13.9 6.2 %collective-permute-start.4 = (f32[16,1024]{1,0:T(8,128)S(1)}, f32[16,1024]{1,0:T(8,128)S(1)}, u32[]{:S(2)}, u32[]{:S(2)}) collective-permute-start(f32[16,1024]{1,0:T(8,128)S(1)} %get-tuple-element.30.rest_0_.refs_0_), channel_id=1, source_target_pairs={{0,24},{2,26},{4,28},{6,30},{8,16},{10,18},{12,20},{14,22},{16,8},... | collective-permute-start | bytes 196616 | tf_op jit(solution)/shard_map/ppermute | solution.py:427
  15.2 5.0 %collective-permute-start.5 = (f32[16,1024]{1,0:T(8,128)S(1)}, f32[16,1024]{1,0:T(8,128)S(1)}, u32[]{:S(2)}, u32[]{:S(2)}) collective-permute-start(f32[16,1024]{1,0:T(8,128)S(1)} %get-tuple-element.30.rest_0_.refs_0_), channel_id=1, source_target_pairs={{0,8},{2,10},{4,12},{6,14},{8,0},{10,2},{12,4},{14,6},{16,24},{18,... | collective-permute-start | bytes 196616 | tf_op jit(solution)/shard_map/ppermute | solution.py:427
  20.2 6.6 %collective-permute-start.6 = (f32[16,1024]{1,0:T(8,128)S(1)}, f32[16,1024]{1,0:T(8,128)S(1)}, u32[]{:S(2)}, u32[]{:S(2)}) collective-permute-start(f32[16,1024]{1,0:T(8,128)S(1)} %add.14.rest_0_.refs_0_), channel_id=1, source_target_pairs={{0,6},{2,4},{4,2},{6,0},{8,14},{10,12},{12,10},{14,8},{16,22},{18,... | collective-permute-start | bytes 196616 | tf_op jit(solution)/shard_map/ppermute | solution.py:427
  21.7 5.1 %collective-permute-start.7 = (f32[16,1024]{1,0:T(8,128)S(1)}, f32[16,1024]{1,0:T(8,128)S(1)}, u32[]{:S(2)}, u32[]{:S(2)}) collective-permute-start(f32[16,1024]{1,0:T(8,128)S(1)} %add.14.rest_0_.refs_0_), channel_id=1, source_target_pairs={{0,4},{2,6},{4,0},{6,2},{8,12},{10,14},{12,8},{14,10},{16,20},{18,... | collective-permute-start | bytes 196616 | tf_op jit(solution)/shard_map/ppermute | solution.py:427
  23.1 4.3 %collective-permute-start.8 = (f32[16,1024]{1,0:T(8,128)S(1)}, f32[16,1024]{1,0:T(8,128)S(1)}, u32[]{:S(2)}, u32[]{:S(2)}) collective-permute-start(f32[16,1024]{1,0:T(8,128)S(1)} %add.14.rest_0_.refs_0_), channel_id=1, source_target_pairs={{0,2},{2,0},{4,6},{6,4},{8,10},{10,8},{12,14},{14,12},{16,18},{18,... | collective-permute-start | bytes 196616 | tf_op jit(solution)/shard_map/ppermute | solution.py:427
  27.4 1.3 %collective-permute-start.9 = (f32[16,1024]{1,0:T(8,128)S(1)}, f32[16,1024]{1,0:T(8,128)S(1)}, u32[]{:S(2)}, u32[]{:S(2)}) collective-permute-start(f32[16,1024]{1,0:T(8,128)S(1)} %add.15.proj_ref), channel_id=1, source_target_pairs={{1,0},{0,1},{3,2},{2,3},{5,4},{4,5},{7,6},{6,7},{9,8},{8,9},{11,10... | collective-permute-start | bytes 196616 | tf_op jit(solution)/shard_map/ppermute | solution.py:435
  30.3 1.3 %collective-permute-start.10 = (f32[16,1024]{1,0:T(8,128)S(1)}, f32[16,1024]{1,0:T(8,128)S(1)}, u32[]{:S(2)}, u32[]{:S(2)}) collective-permute-start(f32[16,1024]{1,0:T(8,128)S(1)} %spread.2), channel_id=1, source_target_pairs={{1,0},{0,1},{3,2},{2,3},{5,4},{4,5},{7,6},{6,7},{9,8},{8,9},{11,10... | collective-permute-start | bytes 196616 | tf_op jit(solution)/shard_map/ppermute | solution.py:435

commit v20 on v19

--- a/solution.py
+++ b/solution.py
@@ -202,7 +202,7 @@
             dx = east[block : block + 1, :] - kx
             dy = north[block : block + 1, :] - ky
             square = dx * dx + dy * dy
-            high_ref[rows, lanes], low_ref[rows, lanes] = halves(jnp.exp2(-(square * lax.rsqrt(square))))
+            high_ref[rows, lanes], low_ref[rows, lanes] = halves(jnp.exp2(-lax.sqrt(square)))
         total = dot_nt(high_ref[rows, :], weights[...]) + dot_nt(low_ref[rows, :], weights[...])
         found = folded_columns(total, probes)
         out_ref[:, rows] = found + before_ref[:, rows] if follows else found
@@ -278,32 +278,66 @@
     )(*operands)
 
 
-def spread_kernel(scale, factor_ref, high_ref, low_ref, out_ref):
+def spread_kernel(scale, factor_ref, high_ref, low_ref, *rest):
+    *base, out_ref = rest
     points = high_ref.shape[1]
     tile = min(TILE, points)
     weights = stacked_halves(factor_ref[...] * scale)
     for start in range(0, points, tile):
         lanes = slice(start, start + tile)
         out_ref[:, lanes] = folded(dot_nn(weights, high_ref[:, lanes]) + dot_nn(weights, low_ref[:, lanes]))
-
-
-def spread(factor, high, low, scale):
+    start = 0
+    for ref in base:
+        lanes = slice(start, start + ref.shape[1])
+        out_ref[:, lanes] = out_ref[:, lanes] + ref[...]
+        start = lanes.stop
+
+
+def spread(factor, high, low, scale, base=()):
     (probes, knots), points = factor.shape, high.shape[1]
     high = pltpu.with_memory_space_constraint(high, pltpu.VMEM)
     low = pltpu.with_memory_space_constraint(low, pltpu.VMEM)
     return pl.pallas_call(
         functools.partial(spread_kernel, scale),
         out_shape=jax.ShapeDtypeStruct((probes, points), jnp.float32),
-        in_specs=[VMEM, VMEM, VMEM],
+        in_specs=[VMEM] * (3 + len(base)),
         out_specs=VMEM,
         compiler_params=pltpu.CompilerParams(vmem_limit_bytes=LIMIT),
         cost_estimate=cost(850, knots * points),
         name="spread",
-    )(factor, high, low)
+    )(factor, high, low, *base)
+
+
+def finish_kernel(count, *refs):
+    out_ref, total, sems = refs[count:]
+    half = total.shape[0] // 2
+    copies = []
+    for part in range(2):
+        rows = pl.ds(part * half, half)
+        value = refs[0][rows, :]
+        for ref in refs[1:count]:
+            value = value + ref[rows, :]
+        total[rows, :] = value
+        copies.append(pltpu.make_async_copy(total.at[rows, :], out_ref.at[rows, :], sems.at[part]))
+        copies[-1].start()
+    for copy in copies:
+        copy.wait()
+
+
+def finish(values):
+    return pl.pallas_call(
+        functools.partial(finish_kernel, len(values)),
+        out_shape=jax.ShapeDtypeStruct(values[0].shape, jnp.float32),
+        in_specs=[VMEM] * len(values),
+        out_specs=HBM,
+        scratch_shapes=[pltpu.VMEM(values[0].shape, jnp.float32), pltpu.SemaphoreType.DMA((2,))],
+        compiler_params=pltpu.CompilerParams(vmem_limit_bytes=LIMIT),
+        name="finish",
+    )(*values)
 
 
 def covariance(square):
-    apart = square * lax.rsqrt(square)
+    apart = lax.sqrt(square)
     remain = jnp.maximum(4.0 - apart, 0.0)
     twice = remain * remain
     return (jnp.exp2(apart * (-LOG2E / (COV_RANGE * TAPER_RATE))) * (twice * twice)) * (5.0 - remain)
@@ -492,11 +526,11 @@
     factor = factored(None, projection, splits, proj_scale, 0)
     for step in range(1, groups):
         factor = factored(factor, shifted(projection, "knot", step), splits, proj_scale, step)
-    total = jnp.concatenate(base, axis=1)
-    for step in reversed(range(groups)):
-        share = spread(factor, parts[step][1], parts[step][2], LOW_SCALE * EXPAND_GAIN)
-        total = total + shifted(share, "knot", -step)
-    return total
+    gain = LOW_SCALE * EXPAND_GAIN
+    shares = []
+    for step in reversed(range(1, groups)):
+        shares.append(shifted(spread(factor, parts[step][1], parts[step][2], gain), "knot", -step))
+    return finish([spread(factor, parts[0][1], parts[0][2], gain, base), *shares])
 
 
 def solution(mesh):

time: 32.3 us -> 33.8 us (1.046)
  Pallas kernels: 15.8 us -> 18.6 us
  waiting for transfers between devices: 2.97 us -> 2.19 us
  other arithmetic: 0.64 us -> 0.01 us
    pallas_call x2, Pallas kernels: 5.71 us -> 7.03 us  [project(): pl.pallas_call(functools.partial(project_kernel, scale, grain_of(scale *...]
    ppermute x6, waiting for transfers between devices: 2.15 us -> 1.36 us  [butterfly_round(): got.append(lax.ppermute(value, (axis, other), pairs))]
    pallas_call x2, Pallas kernels: 6.05 us -> 6.84 us  [beside_round(): pl.pallas_call(functools.partial(beside_kernel, first, first_row, grain_o...]
    pallas_call x0 -> x1, Pallas kernels: none -> 0.65 us  [finish(): pl.pallas_call(functools.partial(finish_kernel, len(values)), out_shape=j...]
    add x1 -> x0, other arithmetic: 0.64 us -> none  [shards(): total = total + shifted(share, 'knot', -step)]
  transfers between devices with their start and end apart: 11 -> 11, of which waited for: 5 -> 5; matrix products, arithmetic and copies ran while one was open for 0% -> 0% of each run, Pallas kernels for 41% -> 46%
where the time goes in v20:
time: 33.8 us; the launch traced here: 33.7 us
  Pallas kernels  18.6 us (55%)
  starting transfers between devices  12.6 us (37%)
  waiting for transfers between devices  2.19 us (6%)
    ppermute x6, starting transfers between devices, butterfly_round(): got.append(lax.ppermute(value, (axis, other), pairs))  7.78 us
    pallas_call x2, Pallas kernels, project(): pl.pallas_call(functools.partial(project_kernel, scale, grain_of(scale *...  7.03 us
    pallas_call x2, Pallas kernels, beside_round(): pl.pallas_call(functools.partial(beside_kernel, first, first_row, grain_o...  6.84 us
    ppermute x2, starting transfers between devices, paired(): return lax.ppermute(value, (axis, other), pairs)  4.07 us
    pallas_call x2, Pallas kernels, spread(): pl.pallas_call(functools.partial(spread_kernel, scale), out_shape=jax.Sha...  1.53 us
    pallas_call x2, Pallas kernels, factored(): pl.pallas_call(kernel, out_shape=jax.ShapeDtypeStruct((probes, rows), jnp...  1.53 us
    ppermute x6, waiting for transfers between devices, butterfly_round(): got.append(lax.ppermute(value, (axis, other), pairs))  1.36 us
    pallas_call x1, Pallas kernels, prepare(): pl.pallas_call(functools.partial(prepare_kernel, blocks), out_shape=(jax....  0.87 us
  transfers between devices with their start and end apart: 11, of which 5 were waited for; matrix products, arithmetic and copies ran while one was open for 0% of the time, Pallas kernels for 46%

profile of v20, /device:TPU:0, one launch (start us, length us, event | category | flops | bytes accessed | tf_op | source)
XLA Modules:
  0.0 33.7 jit_solution(208249238222661060)
XLA Ops:
  0.0 0.9 %prepare.1 = (f32[16,1280]{1,0:T(8,128)S(1)}, f32[2,1024]{1,0:T(2,128)S(1)}) custom-call(f32[16,1024]{1,0:T(8,128)} %probes_ref.1, f32[2,1024]{1,0:T(2,128)} %locations_ref.1, f32[2,1024]{1,0:T(2,128)} %knots_ref.1), custom_call_target="tpu_custom_call" | custom-call | tf_op jit(solution)/shard_map/prepare/pallas_call | solution.py:100
  0.9 0.5 %collective-permute-start = (f32[16,1280]{1,0:T(8,128)S(1)}, f32[16,1280]{1,0:T(8,128)S(1)}, u32[]{:S(2)}, u32[]{:S(2)}) collective-permute-start(f32[16,1280]{1,0:T(8,128)S(1)} %get-tuple-element.23.stack_ref), channel_id=1, source_target_pairs={{1,0},{0,1},{3,2},{2,3},{5,4},{4,5},{7,6},{6,7},{9,8},{8,9},{11,10... | collective-permute-start | bytes 245768 | tf_op jit(solution)/shard_map/ppermute | solution.py:469
  1.4 0.0 slice-start
  1.4 3.6 %project.2 = (f32[16,1024]{1,0:T(8,128)S(1)}, bf16[1024,1024]{1,0:T(8,128)(2,1)S(1)}, bf16[1024,1024]{1,0:T(8,128)(2,1)S(1)}, f32[1024,8]{1,0:T(8,128)S(1)}, f32[16,1280]{1,0:T(8,128)S(1)}) custom-call(f32[16,1280]{1,0:T(8,128)S(1)} %get-tuple-element.23.stack_ref, f32[2,1024]{1,0:T(2,128)S(1)} %get-tuple-element.24.rest_0_), custom_call_target="tpu_custom_call" | custom-call | flops 2936012800 | bytes 4194304 | tf_op jit(solution)/shard_map/project/pallas_call | solution.py:226
  5.1 0.0 collective-permute-done.stack_ref.below_ref.above_ref
  5.1 0.0 slice-start.1
  5.1 0.1 collective-permute-start.4
  5.2 3.9 %collective-permute-start.5 = (f32[16,1536]{1,0:T(8,128)S(1)}, f32[16,1536]{1,0:T(8,128)S(1)}, u32[]{:S(2)}, u32[]{:S(2)}) collective-permute-start(f32[16,1536]{1,0:T(8,128)S(1)} %strip.1.own_ref), channel_id=1, source_target_pairs={{0,2},{1,3},{2,0},{3,1},{4,6},{5,7},{6,4},{7,5},{8,10},{9,11},{10,... | collective-permute-start | bytes 294920 | tf_op jit(solution)/shard_map/ppermute | solution.py:484
  9.2 0.0 copy-start
  9.2 0.0 copy-start.1
  9.2 3.4 %project.3 = (f32[16,1024]{1,0:T(8,128)S(1)}, bf16[1024,1024]{1,0:T(8,128)(2,1)S(1)}, bf16[1024,1024]{1,0:T(8,128)(2,1)S(1)}) custom-call(f32[16,1280]{1,0:T(8,128)S(1)} %collective-permute-done.stack_ref.below_ref.above_ref, f32[16,1024]{1,0:T(8,128)S(1)} %get-tuple-element.25.rest_0_, f32[1024,8]{1,0:T(8,128)S(1)} %get-tuple-element.26.rest_1_), custom_call_target="tpu_custom_call" | custom-call | flops 2936012800 | bytes 4194304 | tf_op jit(solution)/shard_map/project/pallas_call | solution.py:226
  12.6 2.7 %collective-permute-start.1 = (f32[16,1024]{1,0:T(8,128)S(1)}, f32[16,1024]{1,0:T(8,128)S(1)}, u32[]{:S(2)}, u32[]{:S(2)}) collective-permute-start(f32[16,1024]{1,0:T(8,128)S(1)} %get-tuple-element.27.rest_0_.refs_0_), channel_id=1, source_target_pairs={{0,16},{2,18},{4,20},{6,22},{8,24},{10,26},{12,28},{14,30},{16,0},... | collective-permute-start | bytes 196616 | tf_op jit(solution)/shard_map/ppermute | solution.py:461
  15.2 1.3 %collective-permute-start.2 = (f32[16,1024]{1,0:T(8,128)S(1)}, f32[16,1024]{1,0:T(8,128)S(1)}, u32[]{:S(2)}, u32[]{:S(2)}) collective-permute-start(f32[16,1024]{1,0:T(8,128)S(1)} %get-tuple-element.27.rest_0_.refs_0_), channel_id=1, source_target_pairs={{0,24},{2,26},{4,28},{6,30},{8,16},{10,18},{12,20},{14,22},{16,8},... | collective-permute-start | bytes 196616 | tf_op jit(solution)/shard_map/ppermute | solution.py:461
  16.6 0.2 collective-permute-start.3
  16.8 0.0 collective-permute-done.4.odd_ref
  16.8 0.0 collective-permute-done.5.even_ref
  16.8 0.1 assemble.1
  16.9 0.0 slice-done
  16.9 0.0 slice-done.1
  16.9 0.0 copy-done
  16.9 0.0 copy-done.1
  16.9 3.3 %beside.2 = (f32[16,512]{1,0:T(8,128)S(1)}, bf16[2048,512]{1,0:T(8,128)(2,1)S(1)}, bf16[2048,512]{1,0:T(8,128)(2,1)S(1)}) custom-call(s32[8,8]{1,0:T(8,128)S(1)} %copy-done, s32[8]{0:T(128)S(1)} %copy-done.1, f32[16,1280]{1,0:T(8,128)S(1)} %get-tuple-element.28.own_ref, bf16[32,3968]{1,0:T(8,128)(2,1)S(1)} %get-tuple-element.29.values_ref, ...), custom_call_target="tpu_custom_call" | custom-call | flops 262144000 | bytes 2097152 | tf_op jit(solution)/shard_map/beside/pallas_call | solution.py:410
  20.2 0.0 collective-permute-done.1.refs_1_
  20.3 1.1 %collective-permute-done.2.refs_2_ = f32[16,1024]{1,0:T(8,128)S(1)} collective-permute-done((f32[16,1024]{1,0:T(8,128)S(1)}, f32[16,1024]{1,0:T(8,128)S(1)}, u32[]{:S(2)}, u32[]{:S(2)}) %collective-permute-start.2) | collective-permute-done | bytes 65568 | tf_op jit(solution)/shard_map/ppermute | solution.py:461
  21.4 0.1 collective-permute-done.3.refs_3_
  21.5 1.5 %collective-permute-start.6 = (f32[16,1024]{1,0:T(8,128)S(1)}, f32[16,1024]{1,0:T(8,128)S(1)}, u32[]{:S(2)}, u32[]{:S(2)}) collective-permute-start(f32[16,1024]{1,0:T(8,128)S(1)} %add.2.rest_0_.refs_0_), channel_id=1, source_target_pairs={{0,6},{2,4},{4,2},{6,0},{8,14},{10,12},{12,10},{14,8},{16,22},{18,... | collective-permute-start | bytes 196616 | tf_op jit(solution)/shard_map/ppermute | solution.py:461
  23.0 1.4 %collective-permute-start.7 = (f32[16,1024]{1,0:T(8,128)S(1)}, f32[16,1024]{1,0:T(8,128)S(1)}, u32[]{:S(2)}, u32[]{:S(2)}) collective-permute-start(f32[16,1024]{1,0:T(8,128)S(1)} %add.2.rest_0_.refs_0_), channel_id=1, source_target_pairs={{0,4},{2,6},{4,0},{6,2},{8,12},{10,14},{12,8},{14,10},{16,20},{18,... | collective-permute-start | bytes 196616 | tf_op jit(solution)/shard_map/ppermute | solution.py:461
  24.5 0.6 %collective-permute-start.8 = (f32[16,1024]{1,0:T(8,128)S(1)}, f32[16,1024]{1,0:T(8,128)S(1)}, u32[]{:S(2)}, u32[]{:S(2)}) collective-permute-start(f32[16,1024]{1,0:T(8,128)S(1)} %add.2.rest_0_.refs_0_), channel_id=1, source_target_pairs={{0,2},{2,0},{4,6},{6,4},{8,10},{10,8},{12,14},{14,12},{16,18},{18,... | collective-permute-start | bytes 196616 | tf_op jit(solution)/shard_map/ppermute | solution.py:461
  25.1 3.5 %beside.3 = (f32[16,512]{1,0:T(8,128)S(1)}, bf16[2048,512]{1,0:T(8,128)(2,1)S(1)}, bf16[2048,512]{1,0:T(8,128)(2,1)S(1)}) custom-call(s32[8,8]{1,0:T(8,128)S(1)} %copy-done, s32[8]{0:T(128)S(1)} %copy-done.1, f32[16,1280]{1,0:T(8,128)S(1)} %get-tuple-element.28.own_ref, bf16[32,3968]{1,0:T(8,128)(2,1)S(1)} %get-tuple-element.29.values_ref, ...), custom_call_target="tpu_custom_call" | custom-call | flops 262144000 | bytes 2097152 | tf_op jit(solution)/shard_map/beside/pallas_call | solution.py:410
  28.6 0.0 collective-permute-done.6.refs_1_
  28.6 0.0 collective-permute-done.7.refs_2_
  28.6 0.1 collective-permute-done.8.refs_3_
  28.7 0.1 collective-permute-start.9
  28.8 0.8 %factor.2.before_ref = f32[16,1024]{1,0:T(8,128)S(1)} custom-call(f32[16,1024]{1,0:T(8,128)S(1)} %add.3.proj_ref, bf16[2048,512]{1,0:T(8,128)(2,1)S(1)} %get-tuple-element.32.refs_5_.rest_0_, bf16[2048,512]{1,0:T(8,128)(2,1)S(1)} %get-tuple-element.35.refs_5_.rest_1_, bf16[2048,512]{1,0:T(8,128)(2,1)S(1)} %get-tuple-element.33.refs_6_.rest_2_, ...), custom_call_target="tpu_custom_call" | custom-call | flops 1048576000 | bytes 4194304 | tf_op jit(solution)/shard_map/factor/pallas_call | solution.py:269
  29.6 0.5 %collective-permute-done.9.proj_ref = f32[16,1024]{1,0:T(8,128)S(1)} collective-permute-done((f32[16,1024]{1,0:T(8,128)S(1)}, f32[16,1024]{1,0:T(8,128)S(1)}, u32[]{:S(2)}, u32[]{:S(2)}) %collective-permute-start.9) | collective-permute-done | bytes 65568 | tf_op jit(solution)/shard_map/ppermute | solution.py:469
  30.1 0.8 %factor.3.factor_ref = f32[16,1024]{1,0:T(8,128)S(1)} custom-call(f32[16,1024]{1,0:T(8,128)S(1)} %factor.2.before_ref, f32[16,1024]{1,0:T(8,128)S(1)} %collective-permute-done.9.proj_ref, bf16[2048,512]{1,0:T(8,128)(2,1)S(1)} %get-tuple-element.32.refs_5_.rest_0_, bf16[2048,512]{1,0:T(8,128)(2,1)S(1)} %get-tuple-element.35.refs_5_.rest_1_, ...), custom_call_target="tpu_custom_call" | custom-call | flops 1048576000 | bytes 4194304 | tf_op jit(solution)/shard_map/factor/pallas_call | solution.py:269
  30.8 0.8 %spread.3 = f32[16,1024]{1,0:T(8,128)S(1)} custom-call(f32[16,1024]{1,0:T(8,128)S(1)} %factor.3.factor_ref, bf16[1024,1024]{1,0:T(8,128)(2,1)S(1)} %get-tuple-element.39.high_ref, bf16[1024,1024]{1,0:T(8,128)(2,1)S(1)} %get-tuple-element.40.low_ref), custom_call_target="tpu_custom_call" | custom-call | flops 891289600 | bytes 4194304 | tf_op jit(solution)/shard_map/spread/pallas_call | solution.py:300
  31.6 0.2 collective-permute-start.10
  31.8 0.8 %spread.2.refs_0_ = f32[16,1024]{1,0:T(8,128)S(1)} custom-call(f32[16,1024]{1,0:T(8,128)S(1)} %factor.3.factor_ref, bf16[1024,1024]{1,0:T(8,128)(2,1)S(1)} %get-tuple-element.37.high_ref, bf16[1024,1024]{1,0:T(8,128)(2,1)S(1)} %get-tuple-element.38.low_ref, f32[16,512]{1,0:T(8,128)S(1)} %get-tuple-element.31.refs_4_.rest_0_, ...), custom_call_target="tpu_custom_call" | custom-call | flops 891289600 | bytes 4194304 | tf_op jit(solution)/shard_map/spread/pallas_call | solution.py:300
  32.5 0.3 %collective-permute-done.10.refs_1_ = f32[16,1024]{1,0:T(8,128)S(1)} collective-permute-done((f32[16,1024]{1,0:T(8,128)S(1)}, f32[16,1024]{1,0:T(8,128)S(1)}, u32[]{:S(2)}, u32[]{:S(2)}) %collective-permute-start.10) | collective-permute-done | bytes 65568 | tf_op jit(solution)/shard_map/ppermute | solution.py:469
  32.9 0.6 %finish.1 = f32[16,1024]{1,0:T(8,128)} custom-call(f32[16,1024]{1,0:T(8,128)S(1)} %spread.2.refs_0_, f32[16,1024]{1,0:T(8,128)S(1)} %collective-permute-done.10.refs_1_), custom_call_target="tpu_custom_call" | custom-call | tf_op jit(solution)/shard_map/finish/pallas_call | solution.py:328
  (4 shorter events, 0.1 us)
Async XLA Ops:
  0.9 4.2 %collective-permute-start = (f32[16,1280]{1,0:T(8,128)S(1)}, f32[16,1280]{1,0:T(8,128)S(1)}, u32[]{:S(2)}, u32[]{:S(2)}) collective-permute-start(f32[16,1280]{1,0:T(8,128)S(1)} %get-tuple-element.23.stack_ref), channel_id=1, source_target_pairs={{1,0},{0,1},{3,2},{2,3},{5,4},{4,5},{7,6},{6,7},{9,8},{8,9},{11,10... | collective-permute-start | bytes 245768 | tf_op jit(solution)/shard_map/ppermute | solution.py:469
  1.4 15.5 %slice-start = ((s8[8388608]{0:T(1024)(128)(4,1)}), s8[4194304]{0:T(1024)(128)(4,1)S(1)}, s32[]{:S(2)}) async-start(s8[8388608]{0:T(1024)(128)(4,1)} %bitcast), calls=%async_computation | async-start | bytes 8388608
  5.1 11.8 %slice-start.1 = ((s8[8388608]{0:T(1024)(128)(4,1)}), s8[4194304]{0:T(1024)(128)(4,1)S(1)}, s32[]{:S(2)}) async-start(s8[8388608]{0:T(1024)(128)(4,1)} %bitcast), calls=%async_computation.1 | async-start | bytes 8388608
  5.1 11.7 %collective-permute-start.4 = (f32[16,1536]{1,0:T(8,128)S(1)}, f32[16,1536]{1,0:T(8,128)S(1)}, u32[]{:S(2)}, u32[]{:S(2)}) collective-permute-start(f32[16,1536]{1,0:T(8,128)S(1)} %strip.1.own_ref), channel_id=1, source_target_pairs={{0,1},{1,0},{2,4},{3,5},{4,2},{5,3},{6,8},{7,9},{8,6},{9,7},{10,12... | collective-permute-start | bytes 294920 | tf_op jit(solution)/shard_map/ppermute | solution.py:484
  5.2 11.6 %collective-permute-start.5 = (f32[16,1536]{1,0:T(8,128)S(1)}, f32[16,1536]{1,0:T(8,128)S(1)}, u32[]{:S(2)}, u32[]{:S(2)}) collective-permute-start(f32[16,1536]{1,0:T(8,128)S(1)} %strip.1.own_ref), channel_id=1, source_target_pairs={{0,2},{1,3},{2,0},{3,1},{4,6},{5,7},{6,4},{7,5},{8,10},{9,11},{10,... | collective-permute-start | bytes 294920 | tf_op jit(solution)/shard_map/ppermute | solution.py:484
  9.2 7.7 %copy-start = (s32[8,8]{1,0:T(8,128)S(1)}, s32[8,8]{1,0:T(8,128)}, u32[]{:S(2)}) copy-start(s32[8,8]{1,0:T(8,128)} %ids_ref.3) | copy-start | bytes 772
  9.2 7.7 %copy-start.1 = (s32[8]{0:T(128)S(1)}, s32[8]{0:T(128)}, u32[]{:S(2)}) copy-start(s32[8]{0:T(128)} %counts_ref.3) | copy-start | bytes 100
  12.6 7.7 %collective-permute-start.1 = (f32[16,1024]{1,0:T(8,128)S(1)}, f32[16,1024]{1,0:T(8,128)S(1)}, u32[]{:S(2)}, u32[]{:S(2)}) collective-permute-start(f32[16,1024]{1,0:T(8,128)S(1)} %get-tuple-element.27.rest_0_.refs_0_), channel_id=1, source_target_pairs={{0,16},{2,18},{4,20},{6,22},{8,24},{10,26},{12,28},{14,30},{16,0},... | collective-permute-start | bytes 196616 | tf_op jit(solution)/shard_map/ppermute | solution.py:461
  15.2 6.2 %collective-permute-start.2 = (f32[16,1024]{1,0:T(8,128)S(1)}, f32[16,1024]{1,0:T(8,128)S(1)}, u32[]{:S(2)}, u32[]{:S(2)}) collective-permute-start(f32[16,1024]{1,0:T(8,128)S(1)} %get-tuple-element.27.rest_0_.refs_0_), channel_id=1, source_target_pairs={{0,24},{2,26},{4,28},{6,30},{8,16},{10,18},{12,20},{14,22},{16,8},... | collective-permute-start | bytes 196616 | tf_op jit(solution)/shard_map/ppermute | solution.py:461
  16.6 5.0 %collective-permute-start.3 = (f32[16,1024]{1,0:T(8,128)S(1)}, f32[16,1024]{1,0:T(8,128)S(1)}, u32[]{:S(2)}, u32[]{:S(2)}) collective-permute-start(f32[16,1024]{1,0:T(8,128)S(1)} %get-tuple-element.27.rest_0_.refs_0_), channel_id=1, source_target_pairs={{0,8},{2,10},{4,12},{6,14},{8,0},{10,2},{12,4},{14,6},{16,24},{18,... | collective-permute-start | bytes 196616 | tf_op jit(solution)/shard_map/ppermute | solution.py:461
  21.5 7.1 %collective-permute-start.6 = (f32[16,1024]{1,0:T(8,128)S(1)}, f32[16,1024]{1,0:T(8,128)S(1)}, u32[]{:S(2)}, u32[]{:S(2)}) collective-permute-start(f32[16,1024]{1,0:T(8,128)S(1)} %add.2.rest_0_.refs_0_), channel_id=1, source_target_pairs={{0,6},{2,4},{4,2},{6,0},{8,14},{10,12},{12,10},{14,8},{16,22},{18,... | collective-permute-start | bytes 196616 | tf_op jit(solution)/shard_map/ppermute | solution.py:461
  23.0 5.6 %collective-permute-start.7 = (f32[16,1024]{1,0:T(8,128)S(1)}, f32[16,1024]{1,0:T(8,128)S(1)}, u32[]{:S(2)}, u32[]{:S(2)}) collective-permute-start(f32[16,1024]{1,0:T(8,128)S(1)} %add.2.rest_0_.refs_0_), channel_id=1, source_target_pairs={{0,4},{2,6},{4,0},{6,2},{8,12},{10,14},{12,8},{14,10},{16,20},{18,... | collective-permute-start | bytes 196616 | tf_op jit(solution)/shard_map/ppermute | solution.py:461
  24.5 4.3 %collective-permute-start.8 = (f32[16,1024]{1,0:T(8,128)S(1)}, f32[16,1024]{1,0:T(8,128)S(1)}, u32[]{:S(2)}, u32[]{:S(2)}) collective-permute-start(f32[16,1024]{1,0:T(8,128)S(1)} %add.2.rest_0_.refs_0_), channel_id=1, source_target_pairs={{0,2},{2,0},{4,6},{6,4},{8,10},{10,8},{12,14},{14,12},{16,18},{18,... | collective-permute-start | bytes 196616 | tf_op jit(solution)/shard_map/ppermute | solution.py:461
  28.7 1.3 %collective-permute-start.9 = (f32[16,1024]{1,0:T(8,128)S(1)}, f32[16,1024]{1,0:T(8,128)S(1)}, u32[]{:S(2)}, u32[]{:S(2)}) collective-permute-start(f32[16,1024]{1,0:T(8,128)S(1)} %add.3.proj_ref), channel_id=1, source_target_pairs={{1,0},{0,1},{3,2},{2,3},{5,4},{4,5},{7,6},{6,7},{9,8},{8,9},{11,10... | collective-permute-start | bytes 196616 | tf_op jit(solution)/shard_map/ppermute | solution.py:469
  31.6 1.3 %collective-permute-start.10 = (f32[16,1024]{1,0:T(8,128)S(1)}, f32[16,1024]{1,0:T(8,128)S(1)}, u32[]{:S(2)}, u32[]{:S(2)}) collective-permute-start(f32[16,1024]{1,0:T(8,128)S(1)} %spread.3), channel_id=1, source_target_pairs={{1,0},{0,1},{3,2},{2,3},{5,4},{4,5},{7,6},{6,7},{9,8},{8,9},{11,10... | collective-permute-start | bytes 196616 | tf_op jit(solution)/shard_map/ppermute | solution.py:469

commit v21 on v19

--- a/solution.py
+++ b/solution.py
@@ -68,13 +68,12 @@
 
 
 def coordinate_rows(ref, points, axis):
-    start = points + axis * LANES
-    return ref[:, start : start + LANES]
+    blocks = points // LANES
+    return ref[axis * blocks : (axis + 1) * blocks, points : points + LANES]
 
 
 def prepare_kernel(blocks, probes_ref, locations_ref, knots_ref, stack_ref, knots_out_ref, coords, sems):
     points = probes_ref.shape[1]
-    block = points // blocks
     copies = [
         pltpu.make_async_copy(probes_ref, stack_ref.at[:, pl.ds(0, points)], sems.at[0]),
         pltpu.make_async_copy(locations_ref, coords, sems.at[1]),
@@ -84,23 +83,24 @@
         copy.start()
     for copy in copies:
         copy.wait()
-    stack_ref[:, points:] = jnp.zeros((stack_ref.shape[0], 2 * LANES), jnp.float32)
+    if 2 * blocks < stack_ref.shape[0]:
+        stack_ref[:, points:] = jnp.zeros((stack_ref.shape[0], LANES), jnp.float32)
     for axis in range(2):
-        lanes = slice(points + axis * LANES, points + (axis + 1) * LANES)
         for index in range(blocks):
-            stack_ref[index : index + 1, lanes] = coords[axis : axis + 1, index * block : (index + 1) * block]
+            row = axis * blocks + index
+            stack_ref[row : row + 1, points:] = coords[axis : axis + 1, index * LANES : (index + 1) * LANES]
 
 
 def prepare(probes, locations, knot_locs, blocks):
     rows, points = probes.shape
-    assert points == blocks * LANES and blocks + 2 <= rows
+    assert points == blocks * LANES and 2 * blocks <= rows
     probes, locations, knot_locs = [
         pltpu.with_memory_space_constraint(x, pltpu.HBM) for x in (probes, locations, knot_locs)
     ]
     return pl.pallas_call(
         functools.partial(prepare_kernel, blocks),
         out_shape=(
-            jax.ShapeDtypeStruct((rows, points + 2 * LANES), jnp.float32),
+            jax.ShapeDtypeStruct((rows, points + LANES), jnp.float32),
             jax.ShapeDtypeStruct(knot_locs.shape, jnp.float32),
         ),
         in_specs=[HBM, HBM, HBM],
@@ -111,61 +111,85 @@
     )(probes, locations, knot_locs)
 
 
-def strip_kernel(below_ref, own_ref, above_ref, out_ref):
-    rows, width = own_ref.shape
-    points = width - 2 * LANES
+def corner_kernel(end, odd_ref, even_ref, *rest):
+    out_ref = rest[-1]
+    points = odd_ref.shape[1] - LANES
+    upper = lax.axis_index("knot") > 0
+    out_ref[...] = jnp.zeros(out_ref.shape, jnp.float32)
+    for turn, ref in enumerate((odd_ref, even_ref)):
+        start = 2 * turn * LANES
+        coords = [coordinate_rows(ref, points, axis) for axis in range(2)]
+        first = [ref[:, :LANES], *[rows[:1] for rows in coords]]
+        last = [ref[:, points - LANES : points], *[rows[-1:] for rows in coords]]
+        taken = {"first": first, "last": last, "inner": [jnp.where(upper, a, b) for a, b in zip(first, last)]}[end]
+        out_ref[:, start : start + LANES] = taken[0]
+        for axis in range(2):
+            out_ref[axis : axis + 1, start + LANES : start + 2 * LANES] = taken[1 + axis]
+
+
+def corner_blocks(end, strips, after):
+    return pl.pallas_call(
+        functools.partial(corner_kernel, end),
+        out_shape=jax.ShapeDtypeStruct((strips[0].shape[0], 4 * LANES), jnp.float32),
+        in_specs=[VMEM, VMEM] + [ANY] * len(after),
+        out_specs=VMEM,
+        compiler_params=pltpu.CompilerParams(vmem_limit_bytes=LIMIT),
+        name="corner",
+    )(*strips, *after)
+
+
+def assemble_kernel(grain, own_ref, below_ref, above_ref, odd_ref, even_ref, *rest):
+    *corners, values_ref, coords_ref = rest
+    probes, width = own_ref.shape
+    points = width - LANES
     blocks = points // LANES
-    out_ref[:, :LANES] = below_ref[:, points - LANES : points]
-    out_ref[:, LANES : points + LANES] = own_ref[:, :points]
-    out_ref[:, points + LANES : points + 2 * LANES] = above_ref[:, :LANES]
-    for axis in range(2):
-        lanes = slice(points + axis * LANES, points + (axis + 1) * LANES)
-        target = slice(lanes.start + 2 * LANES, lanes.stop + 2 * LANES)
-        out_ref[:, target] = jnp.zeros((rows, LANES), jnp.float32)
-        out_ref[0:1, target] = below_ref[blocks - 1 : blocks, lanes]
-        out_ref[1 : blocks + 1, target] = own_ref[:blocks, lanes]
-        out_ref[blocks + 1 : blocks + 2, target] = above_ref[0:1, lanes]
-
-
-def make_strip(below, own, above):
-    return pl.pallas_call(
-        strip_kernel,
-        out_shape=jax.ShapeDtypeStruct((own.shape[0], own.shape[1] + 2 * LANES), jnp.float32),
-        in_specs=[VMEM, VMEM, VMEM],
-        out_specs=VMEM,
-        compiler_params=pltpu.CompilerParams(vmem_limit_bytes=LIMIT),
-        name="strip",
-    )(below, own, above)
-
-
-def assemble_kernel(grain, own_ref, odd_ref, even_ref, values_ref, coords_ref):
-    probes, width = own_ref.shape
-    points = width - 2 * LANES
-    for turn, ref in enumerate((own_ref, odd_ref, even_ref)):
-        start = turn * points
-        values_ref[:, start : start + points] = stacked_halves(ref[:, :points] * (1.0 / 256.0))
+    span = blocks + 2
+
+    def put(place, vals, coords):
+        count = vals.shape[1] // LANES
+        values_ref[:, place * LANES : (place + count) * LANES] = stacked_halves(vals * (1.0 / 256.0))
         for axis in range(2):
-            rows = off_grid(coordinate_rows(ref, points, axis) * TAPER_RATE, grain)
-            for index in range(points // LANES):
-                lanes = slice(start + index * LANES, start + (index + 1) * LANES)
-                coords_ref[axis : axis + 1, lanes] = rows[index : index + 1]
-    values_ref[:, 3 * points :] = jnp.zeros((2 * probes, LANES), jnp.bfloat16)
-
-
-def assemble(strips, extent):
-    probes, width = strips[0].shape
-    near = 3 * (width - 2 * LANES)
+            rows = off_grid(coords[axis] * TAPER_RATE, grain)
+            for index in range(count):
+                coords_ref[axis : axis + 1, (place + index) * LANES : (place + index + 1) * LANES] = rows[index : index + 1]
+
+    def put_stack(place, ref, first, count):
+        put(
+            place,
+            ref[:, first * LANES : (first + count) * LANES],
+            [coordinate_rows(ref, points, axis)[first : first + count] for axis in range(2)],
+        )
+
+    def put_corner(place, ref, turn):
+        start = 2 * turn * LANES
+        both = slice(start + LANES, start + 2 * LANES)
+        put(place, ref[:, start : start + LANES], [ref[axis : axis + 1, both] for axis in range(2)])
+
+    put_stack(0, below_ref, blocks - 1, 1)
+    put_stack(1, own_ref, 0, blocks)
+    put_stack(1 + blocks, above_ref, 0, 1)
+    for turn, ref in enumerate((odd_ref, even_ref)):
+        place = (turn + 1) * span
+        put_stack(place + 1, ref, 0, blocks)
+        for corner, spot in zip(corners, (place, place + 1 + blocks)):
+            put_corner(spot, corner, turn)
+    values_ref[:, 3 * span * LANES :] = jnp.zeros((2 * probes, LANES), jnp.bfloat16)
+
+
+def assemble(own, below, above, strips, corners, extent):
+    probes, width = own.shape
+    near = 3 * (width + LANES)
     return pl.pallas_call(
         functools.partial(assemble_kernel, grain_of(TAPER_RATE * extent)),
         out_shape=(
             jax.ShapeDtypeStruct((2 * probes, near + LANES), jnp.bfloat16),
             jax.ShapeDtypeStruct((2, near), jnp.float32),
         ),
-        in_specs=[VMEM] * 3,
+        in_specs=[VMEM] * (5 + len(corners)),
         out_specs=(VMEM, VMEM),
         compiler_params=pltpu.CompilerParams(vmem_limit_bytes=LIMIT),
         name="assemble",
-    )(*strips)
+    )(own, below, above, *strips, *corners)
 
 
 def grain_of(bound):
@@ -184,8 +208,7 @@
     if follows:
         before_ref, columns, out_ref, high_ref, low_ref, weights = rest
     else:
-        knots_ref, out_ref, high_ref, low_ref, columns, copy_ref, weights = rest
-        copy_ref[...] = stack_ref[...]
+        knots_ref, out_ref, high_ref, low_ref, columns, weights = rest
         fill = jnp.zeros((6, knots_ref.shape[1]), jnp.float32)
         columns[...] = jnp.transpose(jnp.concatenate([off_grid(knots_ref[...] * scale, grain), fill], axis=0))
     knots, points = high_ref.shape
@@ -209,7 +232,7 @@
 
 
 def project(stack, knot_locs, scale, extent, before=None):
-    probes, points, knots = stack.shape[0], stack.shape[1] - 2 * LANES, knot_locs.shape[1]
+    probes, points, knots = stack.shape[0], stack.shape[1] - LANES, knot_locs.shape[1]
     out_shape = [
         jax.ShapeDtypeStruct((probes, knots), jnp.float32),
         pltpu.VMEM((knots, points), jnp.bfloat16),
@@ -217,10 +240,7 @@
     ]
     if before is None:
         operands = (stack, knot_locs)
-        out_shape += [
-            jax.ShapeDtypeStruct((knots, 8), jnp.float32),
-            jax.ShapeDtypeStruct(stack.shape, jnp.float32),
-        ]
+        out_shape.append(jax.ShapeDtypeStruct((knots, 8), jnp.float32))
     else:
         operands = (stack, before[0], before[3])
     found = pl.pallas_call(
@@ -309,7 +329,7 @@
     return (jnp.exp2(apart * (-LOG2E / (COV_RANGE * TAPER_RATE))) * (twice * twice)) * (5.0 - remain)
 
 
-def beside_kernel(first, first_row, grain, ids_ref, counts_ref, own_ref, values_ref, coords_ref, precision_ref, *rest):
+def beside_kernel(chosen, first_row, grain, ids_ref, counts_ref, own_ref, values_ref, coords_ref, precision_ref, *rest):
     out_ref, high_ref, low_ref = rest[-3:]
     own_blocks, slots = ids_ref.shape
     block = LANES
@@ -338,11 +358,9 @@
     tile = min(TILE, rows)
     wide = min(TILE, depth)
     tiles = [(start, deep) for start in range(0, rows, tile) for deep in range(0, depth, wide)]
-    groups = out_ref.shape[1] // block
-    turns = groups * -(-slots // 2)
-
-    for index in range(groups):
-        group = first + index
+    turns = len(chosen) * -(-slots // 2)
+
+    for index, group in enumerate(chosen):
         px, py = [turned[:, group : group + 1] for turned in own_columns]
         total = jnp.zeros((block, 2 * probes), jnp.float32)
         for pair in range(0, slots, 2):
@@ -371,19 +389,19 @@
         )
 
 
-def beside_round(ids, counts, own, values, coords, precision, extent, first, blocks, first_row, rows, after):
+def beside_round(ids, counts, own, values, coords, precision, extent, chosen, first_row, rows, after):
     slots, depth = ids.shape[1], precision.shape[1]
     return pl.pallas_call(
-        functools.partial(beside_kernel, first, first_row, grain_of(TAPER_RATE * extent)),
+        functools.partial(beside_kernel, chosen, first_row, grain_of(TAPER_RATE * extent)),
         out_shape=(
-            jax.ShapeDtypeStruct((own.shape[0], blocks * LANES), jnp.float32),
+            jax.ShapeDtypeStruct((own.shape[0], len(chosen) * LANES), jnp.float32),
             pltpu.VMEM((depth, rows), jnp.bfloat16),
             pltpu.VMEM((depth, rows), jnp.bfloat16),
         ),
         in_specs=[SMEM, SMEM, VMEM, VMEM, VMEM, VMEM] + [ANY] * len(after),
         out_specs=(VMEM, VMEM, VMEM),
         compiler_params=pltpu.CompilerParams(vmem_limit_bytes=LIMIT),
-        cost_estimate=cost(500, blocks * slots * LANES * LANES, 2),
+        cost_estimate=cost(500, len(chosen) * slots * LANES * LANES, 2),
         name="beside",
     )(ids, counts, own, values, coords, precision, *after)
 
@@ -460,30 +478,36 @@
     proj_scale = PROJ_GAIN * math.sqrt(knot_total / (row_count * device_count))
 
     stack, knots = prepare(probes, locations, knot_locs, own_blocks)
+    strips = [paired(stack, "space", "knot", 1), paired(stack, "space", "knot", 0)]
     chunks = [shifted(stack, "knot", step) for step in range(groups)]
     rate = LOG2E / knot_range
     extent = CELL * max(lax.axis_size("space"), groups * own_blocks)
     parts = []
     for chunk in chunks:
         parts.append(project(chunk, knots, rate, extent, parts[-1] if parts else None))
-    stack = parts[0][4]
-
-    strip = make_strip(chunks[-1], stack, chunks[1 % groups])
-    odd = paired(strip, "space", "knot", 1)
-    values, coords = assemble([strip, odd, paired(strip, "space", "knot", 0)], extent)
     projection = parts[-1][0]
+    if groups == 2:
+        low = high = shifted(corner_blocks("inner", strips, [projection]), "knot", 1)
+    else:
+        low = shifted(corner_blocks("last", strips, [projection]), "knot", -1)
+        high = shifted(corner_blocks("first", strips, [projection]), "knot", 1)
+    around = (stack, chunks[-1], chunks[1 % groups], strips)
+    near = [assemble(*around, corners, extent) for corners in ((), (low, high))]
     rounds = len(butterfly_rounds(lax.axis_size("space")))
     pieces = math.gcd(math.gcd(own_blocks, rounds), knot_precision.shape[0] // LANES)
     per_piece, per_split = own_blocks // pieces, knot_precision.shape[0] // pieces
+    order = [*range(1, own_blocks), 0]
     base, splits = [], []
     for turn in range(rounds):
         got = butterfly_round(projection, "space", "knot", turn)
-        beside = []
+        beside = [] if turn else [low, high]
         for i in range(pieces):
             if i * rounds // pieces == turn:
+                chosen = order[i * per_piece : (i + 1) * per_piece]
+                values, coords = near[0 in chosen or own_blocks - 1 in chosen]
                 done = beside_round(
                     neighbours, counts, stack, values, coords, knot_precision, extent,
-                    i * per_piece, per_piece, i * per_split, per_split, [projection],
+                    chosen, i * per_split, per_split, [projection],
                 )
                 base.append(done[0])
                 splits.append(done[1:])
@@ -492,7 +516,8 @@
     factor = factored(None, projection, splits, proj_scale, 0)
     for step in range(1, groups):
         factor = factored(factor, shifted(projection, "knot", step), splits, proj_scale, step)
-    total = jnp.concatenate(base, axis=1)
+    base = jnp.concatenate(base, axis=1)
+    total = jnp.concatenate([base[:, -LANES:], base[:, :-LANES]], axis=1)
     for step in reversed(range(groups)):
         share = spread(factor, parts[step][1], parts[step][2], LOW_SCALE * EXPAND_GAIN)
         total = total + shifted(share, "knot", -step)

time: 32.3 us -> 32.5 us (level)
    ppermute x3 -> x4, starting transfers between devices: 0.76 us -> 0.83 us  [shifted(): lax.ppermute(value, axis, [((i + step) % count, i) for i in range(count)])]
    ppermute x3 -> x4, waiting for transfers between devices: 0.82 us -> 0.82 us  [shifted(): lax.ppermute(value, axis, [((i + step) % count, i) for i in range(count)])]
  transfers between devices with their start and end apart: 11 -> 12, of which waited for: 5 -> 5; matrix products, arithmetic and copies ran while one was open for 0% -> 0% of each run, Pallas kernels for 41% -> 42%
where the time goes in v21:
time: 32.5 us; the launch traced here: 32.3 us
  Pallas kernels  16 us (49%)
  starting transfers between devices  12.7 us (39%)
  waiting for transfers between devices  2.73 us (8%)
  other arithmetic  0.65 us (2%)
    ppermute x6, starting transfers between devices, butterfly_round(): got.append(lax.ppermute(value, (axis, other), pairs))  7.79 us
    pallas_call x2, Pallas kernels, beside_round(): pl.pallas_call(functools.partial(beside_kernel, chosen, first_row, grain_...  6.11 us
    pallas_call x2, Pallas kernels, project(): pl.pallas_call(functools.partial(project_kernel, scale, grain_of(scale *...  5.83 us
    ppermute x2, starting transfers between devices, paired(): return lax.ppermute(value, (axis, other), pairs)  4.06 us
    ppermute x6, waiting for transfers between devices, butterfly_round(): got.append(lax.ppermute(value, (axis, other), pairs))  1.91 us
    pallas_call x2, Pallas kernels, spread(): pl.pallas_call(functools.partial(spread_kernel, scale), out_shape=jax.Sha...  1.54 us
    pallas_call x2, Pallas kernels, factored(): pl.pallas_call(kernel, out_shape=jax.ShapeDtypeStruct((probes, rows), jnp...  1.53 us
    pallas_call x1, Pallas kernels, prepare(): pl.pallas_call(functools.partial(prepare_kernel, blocks), out_shape=(jax....  0.87 us
  transfers between devices with their start and end apart: 12, of which 5 were waited for; matrix products, arithmetic and copies ran while one was open for 0% of the time, Pallas kernels for 42%

profile of v21, /device:TPU:0, one launch (start us, length us, event | category | flops | bytes accessed | tf_op | source)
XLA Modules:
  0.0 32.3 jit_solution(12792283032626220886)
XLA Ops:
  0.0 0.9 %prepare.1 = (f32[16,1152]{1,0:T(8,128)S(1)}, f32[2,1024]{1,0:T(2,128)S(1)}) custom-call(f32[16,1024]{1,0:T(8,128)} %probes_ref.1, f32[2,1024]{1,0:T(2,128)} %locations_ref.1, f32[2,1024]{1,0:T(2,128)} %knots_ref.1), custom_call_target="tpu_custom_call" | custom-call | tf_op jit(solution)/shard_map/prepare/pallas_call | solution.py:100
  0.9 0.5 %collective-permute-start = (f32[16,1152]{1,0:T(8,128)S(1)}, f32[16,1152]{1,0:T(8,128)S(1)}, u32[]{:S(2)}, u32[]{:S(2)}) collective-permute-start(f32[16,1152]{1,0:T(8,128)S(1)} %get-tuple-element.24.stack_ref.own_ref), channel_id=1, source_target_pairs={{1,0},{0,1},{3,2},{2,3},{5,4},{4,5},{7,6},{6,7},{9,8},{8,9},{11,10... | collective-permute-start | bytes 221192 | tf_op jit(solution)/shard_map/ppermute | solution.py:453
  1.4 0.1 collective-permute-start.1
  1.5 4.0 %collective-permute-start.2 = (f32[16,1152]{1,0:T(8,128)S(1)}, f32[16,1152]{1,0:T(8,128)S(1)}, u32[]{:S(2)}, u32[]{:S(2)}) collective-permute-start(f32[16,1152]{1,0:T(8,128)S(1)} %get-tuple-element.24.stack_ref.own_ref), channel_id=1, source_target_pairs={{0,2},{1,3},{2,0},{3,1},{4,6},{5,7},{6,4},{7,5},{8,10},{9,11},{10,... | collective-permute-start | bytes 221192 | tf_op jit(solution)/shard_map/ppermute | solution.py:468
  5.5 0.0 slice-start
  5.5 3.0 %project.2 = (f32[16,1024]{1,0:T(8,128)S(1)}, bf16[1024,1024]{1,0:T(8,128)(2,1)S(1)}, bf16[1024,1024]{1,0:T(8,128)(2,1)S(1)}, f32[1024,8]{1,0:T(8,128)S(1)}) custom-call(f32[16,1152]{1,0:T(8,128)S(1)} %get-tuple-element.24.stack_ref.own_ref, f32[2,1024]{1,0:T(2,128)S(1)} %get-tuple-element.25.rest_0_), custom_call_target="tpu_custom_call" | custom-call | flops 2936012800 | bytes 4194304 | tf_op jit(solution)/shard_map/project/pallas_call | solution.py:246
  8.5 0.0 collective-permute-done.stack_ref.below_ref.above_ref
  8.5 0.0 slice-start.1
  8.5 0.0 copy-start
  8.5 0.0 copy-start.1
  8.5 2.8 %project.3 = (f32[16,1024]{1,0:T(8,128)S(1)}, bf16[1024,1024]{1,0:T(8,128)(2,1)S(1)}, bf16[1024,1024]{1,0:T(8,128)(2,1)S(1)}) custom-call(f32[16,1152]{1,0:T(8,128)S(1)} %collective-permute-done.stack_ref.below_ref.above_ref, f32[16,1024]{1,0:T(8,128)S(1)} %get-tuple-element.26.rest_0_, f32[1024,8]{1,0:T(8,128)S(1)} %get-tuple-element.27.rest_1_), custom_call_target="tpu_custom_call" | custom-call | flops 2936012800 | bytes 4194304 | tf_op jit(solution)/shard_map/project/pallas_call | solution.py:246
  11.3 2.7 %collective-permute-start.4 = (f32[16,1024]{1,0:T(8,128)S(1)}, f32[16,1024]{1,0:T(8,128)S(1)}, u32[]{:S(2)}, u32[]{:S(2)}) collective-permute-start(f32[16,1024]{1,0:T(8,128)S(1)} %get-tuple-element.28.rest_0_.refs_0_), channel_id=1, source_target_pairs={{0,16},{2,18},{4,20},{6,22},{8,24},{10,26},{12,28},{14,30},{16,0},... | collective-permute-start | bytes 196616 | tf_op jit(solution)/shard_map/ppermute | solution.py:445
  14.0 1.3 %collective-permute-start.5 = (f32[16,1024]{1,0:T(8,128)S(1)}, f32[16,1024]{1,0:T(8,128)S(1)}, u32[]{:S(2)}, u32[]{:S(2)}) collective-permute-start(f32[16,1024]{1,0:T(8,128)S(1)} %get-tuple-element.28.rest_0_.refs_0_), channel_id=1, source_target_pairs={{0,24},{2,26},{4,28},{6,30},{8,16},{10,18},{12,20},{14,22},{16,8},... | collective-permute-start | bytes 196616 | tf_op jit(solution)/shard_map/ppermute | solution.py:445
  15.3 0.2 collective-permute-start.6
  15.6 0.0 collective-permute-done.1.odd_ref
  15.6 0.0 collective-permute-done.2.even_ref
  15.6 0.1 collective-permute-start.3
  15.7 0.1 assemble.3
  15.7 0.0 slice-done
  15.7 0.0 slice-done.1
  15.8 0.0 copy-done
  15.8 0.0 copy-done.1
  15.8 3.1 %beside.2 = (f32[16,512]{1,0:T(8,128)S(1)}, bf16[2048,512]{1,0:T(8,128)(2,1)S(1)}, bf16[2048,512]{1,0:T(8,128)(2,1)S(1)}) custom-call(s32[8,8]{1,0:T(8,128)S(1)} %copy-done, s32[8]{0:T(128)S(1)} %copy-done.1, f32[16,1152]{1,0:T(8,128)S(1)} %get-tuple-element.24.stack_ref.own_ref, bf16[32,3968]{1,0:T(8,128)(2,1)S(1)} %get-tuple-element.31.values_ref, ...), custom_call_target="tpu_custom_call" | custom-call | flops 262144000 | bytes 2097152 | tf_op jit(solution)/shard_map/beside/pallas_call | solution.py:394
  18.8 0.0 collective-permute-done.3.rest_0_.rest_1_.refs_4_.refs_5_
  18.9 0.0 collective-permute-done.4.refs_1_
  18.9 1.3 %collective-permute-done.5.refs_2_ = f32[16,1024]{1,0:T(8,128)S(1)} collective-permute-done((f32[16,1024]{1,0:T(8,128)S(1)}, f32[16,1024]{1,0:T(8,128)S(1)}, u32[]{:S(2)}, u32[]{:S(2)}) %collective-permute-start.5) | collective-permute-done | bytes 65568 | tf_op jit(solution)/shard_map/ppermute | solution.py:445
  20.2 0.1 collective-permute-done.6.refs_3_
  20.3 1.5 %collective-permute-start.7 = (f32[16,1024]{1,0:T(8,128)S(1)}, f32[16,1024]{1,0:T(8,128)S(1)}, u32[]{:S(2)}, u32[]{:S(2)}) collective-permute-start(f32[16,1024]{1,0:T(8,128)S(1)} %add.14.rest_0_.refs_0_), channel_id=1, source_target_pairs={{0,6},{2,4},{4,2},{6,0},{8,14},{10,12},{12,10},{14,8},{16,22},{18,... | collective-permute-start | bytes 196616 | tf_op jit(solution)/shard_map/ppermute | solution.py:445
  21.8 1.4 %collective-permute-start.8 = (f32[16,1024]{1,0:T(8,128)S(1)}, f32[16,1024]{1,0:T(8,128)S(1)}, u32[]{:S(2)}, u32[]{:S(2)}) collective-permute-start(f32[16,1024]{1,0:T(8,128)S(1)} %add.14.rest_0_.refs_0_), channel_id=1, source_target_pairs={{0,4},{2,6},{4,0},{6,2},{8,12},{10,14},{12,8},{14,10},{16,20},{18,... | collective-permute-start | bytes 196616 | tf_op jit(solution)/shard_map/ppermute | solution.py:445
  23.2 0.6 %collective-permute-start.9 = (f32[16,1024]{1,0:T(8,128)S(1)}, f32[16,1024]{1,0:T(8,128)S(1)}, u32[]{:S(2)}, u32[]{:S(2)}) collective-permute-start(f32[16,1024]{1,0:T(8,128)S(1)} %add.14.rest_0_.refs_0_), channel_id=1, source_target_pairs={{0,2},{2,0},{4,6},{6,4},{8,10},{10,8},{12,14},{14,12},{16,18},{18,... | collective-permute-start | bytes 196616 | tf_op jit(solution)/shard_map/ppermute | solution.py:445
  23.9 0.1 assemble.2
  23.9 3.1 %beside.3 = (f32[16,512]{1,0:T(8,128)S(1)}, bf16[2048,512]{1,0:T(8,128)(2,1)S(1)}, bf16[2048,512]{1,0:T(8,128)(2,1)S(1)}) custom-call(s32[8,8]{1,0:T(8,128)S(1)} %copy-done, s32[8]{0:T(128)S(1)} %copy-done.1, f32[16,1152]{1,0:T(8,128)S(1)} %get-tuple-element.24.stack_ref.own_ref, bf16[32,3968]{1,0:T(8,128)(2,1)S(1)} %get-tuple-element.29.values_ref, ...), custom_call_target="tpu_custom_call" | custom-call | flops 262144000 | bytes 2097152 | tf_op jit(solution)/shard_map/beside/pallas_call | solution.py:394
  27.0 0.0 collective-permute-done.7.refs_1_
  27.0 0.0 collective-permute-done.8.refs_2_
  27.0 0.5 %collective-permute-done.9.refs_3_ = f32[16,1024]{1,0:T(8,128)S(1)} collective-permute-done((f32[16,1024]{1,0:T(8,128)S(1)}, f32[16,1024]{1,0:T(8,128)S(1)}, u32[]{:S(2)}, u32[]{:S(2)}) %collective-permute-start.9) | collective-permute-done | bytes 65568 | tf_op jit(solution)/shard_map/ppermute | solution.py:445
  27.5 0.1 collective-permute-start.10
  27.6 0.8 %factor.2.before_ref = f32[16,1024]{1,0:T(8,128)S(1)} custom-call(f32[16,1024]{1,0:T(8,128)S(1)} %add.15.proj_ref, bf16[2048,512]{1,0:T(8,128)(2,1)S(1)} %get-tuple-element.34.refs_7_.rest_0_, bf16[2048,512]{1,0:T(8,128)(2,1)S(1)} %get-tuple-element.37.refs_5_.rest_1_, bf16[2048,512]{1,0:T(8,128)(2,1)S(1)} %get-tuple-element.35.refs_8_.rest_2_, ...), custom_call_target="tpu_custom_call" | custom-call | flops 1048576000 | bytes 4194304 | tf_op jit(solution)/shard_map/factor/pallas_call | solution.py:289
  28.4 0.5 %collective-permute-done.10.proj_ref = f32[16,1024]{1,0:T(8,128)S(1)} collective-permute-done((f32[16,1024]{1,0:T(8,128)S(1)}, f32[16,1024]{1,0:T(8,128)S(1)}, u32[]{:S(2)}, u32[]{:S(2)}) %collective-permute-start.10) | collective-permute-done | bytes 65568 | tf_op jit(solution)/shard_map/ppermute | solution.py:453
  28.8 0.8 %factor.3.factor_ref = f32[16,1024]{1,0:T(8,128)S(1)} custom-call(f32[16,1024]{1,0:T(8,128)S(1)} %factor.2.before_ref, f32[16,1024]{1,0:T(8,128)S(1)} %collective-permute-done.10.proj_ref, bf16[2048,512]{1,0:T(8,128)(2,1)S(1)} %get-tuple-element.34.refs_7_.rest_0_, bf16[2048,512]{1,0:T(8,128)(2,1)S(1)} %get-tuple-element.37.refs_5_.rest_1_, ...), custom_call_target="tpu_custom_call" | custom-call | flops 1048576000 | bytes 4194304 | tf_op jit(solution)/shard_map/factor/pallas_call | solution.py:289
  29.6 0.8 %spread.2 = f32[16,1024]{1,0:T(8,128)S(1)} custom-call(f32[16,1024]{1,0:T(8,128)S(1)} %factor.3.factor_ref, bf16[1024,1024]{1,0:T(8,128)(2,1)S(1)} %get-tuple-element.39.high_ref, bf16[1024,1024]{1,0:T(8,128)(2,1)S(1)} %get-tuple-element.40.low_ref), custom_call_target="tpu_custom_call" | custom-call | flops 891289600 | bytes 4194304 | tf_op jit(solution)/shard_map/spread/pallas_call | solution.py:314
  30.4 0.2 collective-permute-start.11
  30.6 0.8 %spread.3 = f32[16,1024]{1,0:T(8,128)S(1)} custom-call(f32[16,1024]{1,0:T(8,128)S(1)} %factor.3.factor_ref, bf16[1024,1024]{1,0:T(8,128)(2,1)S(1)} %get-tuple-element.41.high_ref, bf16[1024,1024]{1,0:T(8,128)(2,1)S(1)} %get-tuple-element.42.low_ref), custom_call_target="tpu_custom_call" | custom-call | flops 891289600 | bytes 4194304 | tf_op jit(solution)/shard_map/spread/pallas_call | solution.py:314
  31.3 0.3 %collective-permute-done.11 = f32[16,1024]{1,0:T(8,128)S(1)} collective-permute-done((f32[16,1024]{1,0:T(8,128)S(1)}, f32[16,1024]{1,0:T(8,128)S(1)}, u32[]{:S(2)}, u32[]{:S(2)}) %collective-permute-start.11) | collective-permute-done | bytes 65568 | tf_op jit(solution)/shard_map/ppermute | solution.py:453
  31.7 0.6 %fusion.2 = f32[16,1024]{1,0:T(8,128)} fusion(f32[16,1024]{1,0:T(8,128)S(1)} %spread.3, f32[16,1024]{1,0:T(8,128)S(1)} %collective-permute-done.11, f32[16,512]{1,0:T(8,128)S(1)} %get-tuple-element.36.refs_4_, f32[16,512]{1,0:T(8,128)S(1)} %get-tuple-element.33.refs_6_, f32[16,128]{1,0:T(8,128)S(1)} %slice.6), kind=kLoop, calls=%fused_computation.3 | loop fusion | flops 65536 | bytes 270336 | tf_op jit(solution)/shard_map/add | solution.py:523
  (5 shorter events, 0.1 us)
Async XLA Ops:
  0.9 7.6 %collective-permute-start = (f32[16,1152]{1,0:T(8,128)S(1)}, f32[16,1152]{1,0:T(8,128)S(1)}, u32[]{:S(2)}, u32[]{:S(2)}) collective-permute-start(f32[16,1152]{1,0:T(8,128)S(1)} %get-tuple-element.24.stack_ref.own_ref), channel_id=1, source_target_pairs={{1,0},{0,1},{3,2},{2,3},{5,4},{4,5},{7,6},{6,7},{9,8},{8,9},{11,10... | collective-permute-start | bytes 221192 | tf_op jit(solution)/shard_map/ppermute | solution.py:453
  1.4 14.2 %collective-permute-start.1 = (f32[16,1152]{1,0:T(8,128)S(1)}, f32[16,1152]{1,0:T(8,128)S(1)}, u32[]{:S(2)}, u32[]{:S(2)}) collective-permute-start(f32[16,1152]{1,0:T(8,128)S(1)} %get-tuple-element.24.stack_ref.own_ref), channel_id=1, source_target_pairs={{0,1},{1,0},{2,4},{3,5},{4,2},{5,3},{6,8},{7,9},{8,6},{9,7},{10,12... | collective-permute-start | bytes 221192 | tf_op jit(solution)/shard_map/ppermute | solution.py:468
  1.5 14.1 %collective-permute-start.2 = (f32[16,1152]{1,0:T(8,128)S(1)}, f32[16,1152]{1,0:T(8,128)S(1)}, u32[]{:S(2)}, u32[]{:S(2)}) collective-permute-start(f32[16,1152]{1,0:T(8,128)S(1)} %get-tuple-element.24.stack_ref.own_ref), channel_id=1, source_target_pairs={{0,2},{1,3},{2,0},{3,1},{4,6},{5,7},{6,4},{7,5},{8,10},{9,11},{10,... | collective-permute-start | bytes 221192 | tf_op jit(solution)/shard_map/ppermute | solution.py:468
  5.5 10.3 %slice-start = ((s8[8388608]{0:T(1024)(128)(4,1)}), s8[4194304]{0:T(1024)(128)(4,1)S(1)}, s32[]{:S(2)}) async-start(s8[8388608]{0:T(1024)(128)(4,1)} %bitcast), calls=%async_computation | async-start | bytes 8388608
  8.5 7.3 %slice-start.1 = ((s8[8388608]{0:T(1024)(128)(4,1)}), s8[4194304]{0:T(1024)(128)(4,1)S(1)}, s32[]{:S(2)}) async-start(s8[8388608]{0:T(1024)(128)(4,1)} %bitcast), calls=%async_computation.1 | async-start | bytes 8388608
  8.5 7.3 %copy-start = (s32[8,8]{1,0:T(8,128)S(1)}, s32[8,8]{1,0:T(8,128)}, u32[]{:S(2)}) copy-start(s32[8,8]{1,0:T(8,128)} %ids_ref.3) | copy-start | bytes 772
  8.5 7.3 %copy-start.1 = (s32[8]{0:T(128)S(1)}, s32[8]{0:T(128)}, u32[]{:S(2)}) copy-start(s32[8]{0:T(128)} %counts_ref.3) | copy-start | bytes 100
  11.3 7.5 %collective-permute-start.4 = (f32[16,1024]{1,0:T(8,128)S(1)}, f32[16,1024]{1,0:T(8,128)S(1)}, u32[]{:S(2)}, u32[]{:S(2)}) collective-permute-start(f32[16,1024]{1,0:T(8,128)S(1)} %get-tuple-element.28.rest_0_.refs_0_), channel_id=1, source_target_pairs={{0,16},{2,18},{4,20},{6,22},{8,24},{10,26},{12,28},{14,30},{16,0},... | collective-permute-start | bytes 196616 | tf_op jit(solution)/shard_map/ppermute | solution.py:445
  14.0 6.2 %collective-permute-start.5 = (f32[16,1024]{1,0:T(8,128)S(1)}, f32[16,1024]{1,0:T(8,128)S(1)}, u32[]{:S(2)}, u32[]{:S(2)}) collective-permute-start(f32[16,1024]{1,0:T(8,128)S(1)} %get-tuple-element.28.rest_0_.refs_0_), channel_id=1, source_target_pairs={{0,24},{2,26},{4,28},{6,30},{8,16},{10,18},{12,20},{14,22},{16,8},... | collective-permute-start | bytes 196616 | tf_op jit(solution)/shard_map/ppermute | solution.py:445
  15.3 5.0 %collective-permute-start.6 = (f32[16,1024]{1,0:T(8,128)S(1)}, f32[16,1024]{1,0:T(8,128)S(1)}, u32[]{:S(2)}, u32[]{:S(2)}) collective-permute-start(f32[16,1024]{1,0:T(8,128)S(1)} %get-tuple-element.28.rest_0_.refs_0_), channel_id=1, source_target_pairs={{0,8},{2,10},{4,12},{6,14},{8,0},{10,2},{12,4},{14,6},{16,24},{18,... | collective-permute-start | bytes 196616 | tf_op jit(solution)/shard_map/ppermute | solution.py:445
  15.6 3.3 %collective-permute-start.3 = (f32[16,512]{1,0:T(8,128)S(1)}, f32[16,512]{1,0:T(8,128)S(1)}, u32[]{:S(2)}, u32[]{:S(2)}) collective-permute-start(f32[16,512]{1,0:T(8,128)S(1)} %corner.1), channel_id=1, source_target_pairs={{1,0},{0,1},{3,2},{2,3},{5,4},{4,5},{7,6},{6,7},{9,8},{8,9},{11,10... | collective-permute-start | bytes 98312 | tf_op jit(solution)/shard_map/ppermute | solution.py:453
  20.3 6.7 %collective-permute-start.7 = (f32[16,1024]{1,0:T(8,128)S(1)}, f32[16,1024]{1,0:T(8,128)S(1)}, u32[]{:S(2)}, u32[]{:S(2)}) collective-permute-start(f32[16,1024]{1,0:T(8,128)S(1)} %add.14.rest_0_.refs_0_), channel_id=1, source_target_pairs={{0,6},{2,4},{4,2},{6,0},{8,14},{10,12},{12,10},{14,8},{16,22},{18,... | collective-permute-start | bytes 196616 | tf_op jit(solution)/shard_map/ppermute | solution.py:445
  21.8 5.2 %collective-permute-start.8 = (f32[16,1024]{1,0:T(8,128)S(1)}, f32[16,1024]{1,0:T(8,128)S(1)}, u32[]{:S(2)}, u32[]{:S(2)}) collective-permute-start(f32[16,1024]{1,0:T(8,128)S(1)} %add.14.rest_0_.refs_0_), channel_id=1, source_target_pairs={{0,4},{2,6},{4,0},{6,2},{8,12},{10,14},{12,8},{14,10},{16,20},{18,... | collective-permute-start | bytes 196616 | tf_op jit(solution)/shard_map/ppermute | solution.py:445
  23.2 4.3 %collective-permute-start.9 = (f32[16,1024]{1,0:T(8,128)S(1)}, f32[16,1024]{1,0:T(8,128)S(1)}, u32[]{:S(2)}, u32[]{:S(2)}) collective-permute-start(f32[16,1024]{1,0:T(8,128)S(1)} %add.14.rest_0_.refs_0_), channel_id=1, source_target_pairs={{0,2},{2,0},{4,6},{6,4},{8,10},{10,8},{12,14},{14,12},{16,18},{18,... | collective-permute-start | bytes 196616 | tf_op jit(solution)/shard_map/ppermute | solution.py:445
  27.5 1.3 %collective-permute-start.10 = (f32[16,1024]{1,0:T(8,128)S(1)}, f32[16,1024]{1,0:T(8,128)S(1)}, u32[]{:S(2)}, u32[]{:S(2)}) collective-permute-start(f32[16,1024]{1,0:T(8,128)S(1)} %add.15.proj_ref), channel_id=1, source_target_pairs={{1,0},{0,1},{3,2},{2,3},{5,4},{4,5},{7,6},{6,7},{9,8},{8,9},{11,10... | collective-permute-start | bytes 196616 | tf_op jit(solution)/shard_map/ppermute | solution.py:453
  30.4 1.3 %collective-permute-start.11 = (f32[16,1024]{1,0:T(8,128)S(1)}, f32[16,1024]{1,0:T(8,128)S(1)}, u32[]{:S(2)}, u32[]{:S(2)}) collective-permute-start(f32[16,1024]{1,0:T(8,128)S(1)} %spread.2), channel_id=1, source_target_pairs={{1,0},{0,1},{3,2},{2,3},{5,4},{4,5},{7,6},{6,7},{9,8},{8,9},{11,10... | collective-permute-start | bytes 196616 | tf_op jit(solution)/shard_map/ppermute | solution.py:453

commit v22 on v19

--- a/solution.py
+++ b/solution.py
@@ -414,18 +414,11 @@
     return rounds + [(bit,) for bit in bits[len(rounds) * 2 :]]
 
 
-def butterfly_round(value, axis, other, turn):
-    count, groups = lax.axis_size(axis), lax.axis_size(other)
-    rounds = butterfly_rounds(count)
-    half = len(rounds) // 2 if len({len(steps) for steps in rounds}) == 1 else 0
-    got = []
-    for kind in range(len(rounds[turn])):
-        pairs = []
-        for j in range(groups):
-            step = rounds[(turn + half * ((j + 1) % 2)) % len(rounds)][kind]
-            pairs += [(i * groups + j, (i ^ step) * groups + j) for i in range(count)]
-        got.append(lax.ppermute(value, (axis, other), pairs))
-    return got
+def butterfly_round(value, axis, turn):
+    count = lax.axis_size(axis)
+    return [
+        lax.ppermute(value, axis, [(i, i ^ step) for i in range(count)]) for step in butterfly_rounds(count)[turn]
+    ]
 
 
 def shifted(value, axis, step):
@@ -477,7 +470,7 @@
     per_piece, per_split = own_blocks // pieces, knot_precision.shape[0] // pieces
     base, splits = [], []
     for turn in range(rounds):
-        got = butterfly_round(projection, "space", "knot", turn)
+        got = butterfly_round(projection, "space", turn)
         beside = []
         for i in range(pieces):
             if i * rounds // pieces == turn:

time: 32.3 us -> 32.3 us (level)
  waiting for transfers between devices: 2.97 us -> 2.53 us
  starting transfers between devices: 12.6 us -> 13 us
    ppermute x6, waiting for transfers between devices: 2.15 us -> 1.71 us  [butterfly_round(): lax.ppermute(value, axis, [(i, i ^ step) for i in range(count)])]
    ppermute x6, starting transfers between devices: 7.78 us -> 8.21 us  [butterfly_round(): lax.ppermute(value, axis, [(i, i ^ step) for i in range(count)])]
  transfers between devices with their start and end apart: 11 -> 11, of which waited for: 5 -> 4; matrix products, arithmetic and copies ran while one was open for 0% -> 0% of each run, Pallas kernels for 41% -> 41%
where the time goes in v22:
time: 32.3 us; the launch traced here: 32.2 us
  Pallas kernels  15.8 us (49%)
  starting transfers between devices  13 us (40%)
  waiting for transfers between devices  2.53 us (8%)
  other arithmetic  0.64 us (2%)
    ppermute x6, starting transfers between devices, butterfly_round(): lax.ppermute(value, axis, [(i, i ^ step) for i in range(count)])  8.21 us
    pallas_call x2, Pallas kernels, beside_round(): pl.pallas_call(functools.partial(beside_kernel, first, first_row, grain_o...  6.05 us
    pallas_call x2, Pallas kernels, project(): pl.pallas_call(functools.partial(project_kernel, scale, grain_of(scale *...  5.71 us
    ppermute x2, starting transfers between devices, paired(): return lax.ppermute(value, (axis, other), pairs)  4.07 us
    ppermute x6, waiting for transfers between devices, butterfly_round(): lax.ppermute(value, axis, [(i, i ^ step) for i in range(count)])  1.71 us
    pallas_call x2, Pallas kernels, spread(): pl.pallas_call(functools.partial(spread_kernel, scale), out_shape=jax.Sha...  1.53 us
    pallas_call x2, Pallas kernels, factored(): pl.pallas_call(kernel, out_shape=jax.ShapeDtypeStruct((probes, rows), jnp...  1.53 us
    pallas_call x1, Pallas kernels, prepare(): pl.pallas_call(functools.partial(prepare_kernel, blocks), out_shape=(jax....  0.87 us
  transfers between devices with their start and end apart: 11, of which 4 were waited for; matrix products, arithmetic and copies ran while one was open for 0% of the time, Pallas kernels for 41%

profile of v22, /device:TPU:0, one launch (start us, length us, event | category | flops | bytes accessed | tf_op | source)
XLA Modules:
  0.0 32.2 jit_solution(6070421604844878291)
XLA Ops:
  0.0 0.9 %prepare.1 = (f32[16,1280]{1,0:T(8,128)S(1)}, f32[2,1024]{1,0:T(2,128)S(1)}) custom-call(f32[16,1024]{1,0:T(8,128)} %probes_ref.1, f32[2,1024]{1,0:T(2,128)} %locations_ref.1, f32[2,1024]{1,0:T(2,128)} %knots_ref.1), custom_call_target="tpu_custom_call" | custom-call | tf_op jit(solution)/shard_map/prepare/pallas_call | solution.py:100
  0.9 0.5 %collective-permute-start = (f32[16,1280]{1,0:T(8,128)S(1)}, f32[16,1280]{1,0:T(8,128)S(1)}, u32[]{:S(2)}, u32[]{:S(2)}) collective-permute-start(f32[16,1280]{1,0:T(8,128)S(1)} %get-tuple-element.23.stack_ref), channel_id=1, source_target_pairs={{1,0},{0,1},{3,2},{2,3},{5,4},{4,5},{7,6},{6,7},{9,8},{8,9},{11,10... | collective-permute-start | bytes 245768 | tf_op jit(solution)/shard_map/ppermute | solution.py:428
  1.4 0.0 slice-start
  1.4 3.0 %project.2 = (f32[16,1024]{1,0:T(8,128)S(1)}, bf16[1024,1024]{1,0:T(8,128)(2,1)S(1)}, bf16[1024,1024]{1,0:T(8,128)(2,1)S(1)}, f32[1024,8]{1,0:T(8,128)S(1)}, f32[16,1280]{1,0:T(8,128)S(1)}) custom-call(f32[16,1280]{1,0:T(8,128)S(1)} %get-tuple-element.23.stack_ref, f32[2,1024]{1,0:T(2,128)S(1)} %get-tuple-element.24.rest_0_), custom_call_target="tpu_custom_call" | custom-call | flops 2936012800 | bytes 4194304 | tf_op jit(solution)/shard_map/project/pallas_call | solution.py:226
  4.4 0.0 collective-permute-done.below_ref.above_ref.stack_ref
  4.4 0.0 slice-start.1
  4.4 0.1 collective-permute-start.1
  4.5 3.9 %collective-permute-start.2 = (f32[16,1536]{1,0:T(8,128)S(1)}, f32[16,1536]{1,0:T(8,128)S(1)}, u32[]{:S(2)}, u32[]{:S(2)}) collective-permute-start(f32[16,1536]{1,0:T(8,128)S(1)} %strip.1.own_ref), channel_id=1, source_target_pairs={{0,2},{1,3},{2,0},{3,1},{4,6},{5,7},{6,4},{7,5},{8,10},{9,11},{10,... | collective-permute-start | bytes 294920 | tf_op jit(solution)/shard_map/ppermute | solution.py:443
  8.5 0.0 copy-start
  8.5 0.0 copy-start.1
  8.5 2.7 %project.3 = (f32[16,1024]{1,0:T(8,128)S(1)}, bf16[1024,1024]{1,0:T(8,128)(2,1)S(1)}, bf16[1024,1024]{1,0:T(8,128)(2,1)S(1)}) custom-call(f32[16,1280]{1,0:T(8,128)S(1)} %collective-permute-done.below_ref.above_ref.stack_ref, f32[16,1024]{1,0:T(8,128)S(1)} %get-tuple-element.28.rest_0_, f32[1024,8]{1,0:T(8,128)S(1)} %get-tuple-element.29.rest_1_), custom_call_target="tpu_custom_call" | custom-call | flops 2936012800 | bytes 4194304 | tf_op jit(solution)/shard_map/project/pallas_call | solution.py:226
  11.2 1.5 %collective-permute-start.3 = (f32[16,1024]{1,0:T(8,128)S(1)}, f32[16,1024]{1,0:T(8,128)S(1)}, u32[]{:S(2)}, u32[]{:S(2)}) collective-permute-start(f32[16,1024]{1,0:T(8,128)S(1)} %get-tuple-element.30.rest_0_.refs_0_), channel_id=1, source_target_pairs={{0,6},{2,4},{4,2},{6,0},{8,14},{10,12},{12,10},{14,8},{16,22},{18,... | collective-permute-start | bytes 196616 | tf_op jit(solution)/shard_map/ppermute | solution.py:420
  12.7 0.2 collective-permute-start.4
  12.9 1.9 %collective-permute-start.5 = (f32[16,1024]{1,0:T(8,128)S(1)}, f32[16,1024]{1,0:T(8,128)S(1)}, u32[]{:S(2)}, u32[]{:S(2)}) collective-permute-start(f32[16,1024]{1,0:T(8,128)S(1)} %get-tuple-element.30.rest_0_.refs_0_), channel_id=1, source_target_pairs={{0,2},{2,0},{4,6},{6,4},{8,10},{10,8},{12,14},{14,12},{16,18},{18,... | collective-permute-start | bytes 196616 | tf_op jit(solution)/shard_map/ppermute | solution.py:420
  14.8 0.0 collective-permute-done.1.odd_ref
  14.8 0.0 collective-permute-done.2.even_ref
  14.8 0.1 assemble.1
  14.9 0.0 slice-done
  14.9 0.0 slice-done.1
  14.9 0.0 copy-done
  14.9 0.0 copy-done.1
  14.9 3.0 %beside.2 = (f32[16,512]{1,0:T(8,128)S(1)}, bf16[2048,512]{1,0:T(8,128)(2,1)S(1)}, bf16[2048,512]{1,0:T(8,128)(2,1)S(1)}) custom-call(s32[8,8]{1,0:T(8,128)S(1)} %copy-done, s32[8]{0:T(128)S(1)} %copy-done.1, f32[16,1280]{1,0:T(8,128)S(1)} %get-tuple-element.25.own_ref, bf16[32,3968]{1,0:T(8,128)(2,1)S(1)} %get-tuple-element.26.values_ref, ...), custom_call_target="tpu_custom_call" | custom-call | flops 262144000 | bytes 2097152 | tf_op jit(solution)/shard_map/beside/pallas_call | solution.py:376
  17.9 0.0 collective-permute-done.3.refs_1_
  17.9 0.0 collective-permute-done.4.refs_2_
  18.0 0.0 collective-permute-done.5.refs_3_
  18.0 3.1 %collective-permute-start.6 = (f32[16,1024]{1,0:T(8,128)S(1)}, f32[16,1024]{1,0:T(8,128)S(1)}, u32[]{:S(2)}, u32[]{:S(2)}) collective-permute-start(f32[16,1024]{1,0:T(8,128)S(1)} %add.14.rest_0_.refs_0_), channel_id=1, source_target_pairs={{0,16},{2,18},{4,20},{6,22},{8,24},{10,26},{12,28},{14,30},{16,0},... | collective-permute-start | bytes 196616 | tf_op jit(solution)/shard_map/ppermute | solution.py:420
  21.1 1.3 %collective-permute-start.7 = (f32[16,1024]{1,0:T(8,128)S(1)}, f32[16,1024]{1,0:T(8,128)S(1)}, u32[]{:S(2)}, u32[]{:S(2)}) collective-permute-start(f32[16,1024]{1,0:T(8,128)S(1)} %add.14.rest_0_.refs_0_), channel_id=1, source_target_pairs={{0,24},{2,26},{4,28},{6,30},{8,16},{10,18},{12,20},{14,22},{16,8},... | collective-permute-start | bytes 196616 | tf_op jit(solution)/shard_map/ppermute | solution.py:420
  22.4 0.2 collective-permute-start.8
  22.7 3.0 %beside.3 = (f32[16,512]{1,0:T(8,128)S(1)}, bf16[2048,512]{1,0:T(8,128)(2,1)S(1)}, bf16[2048,512]{1,0:T(8,128)(2,1)S(1)}) custom-call(s32[8,8]{1,0:T(8,128)S(1)} %copy-done, s32[8]{0:T(128)S(1)} %copy-done.1, f32[16,1280]{1,0:T(8,128)S(1)} %get-tuple-element.25.own_ref, bf16[32,3968]{1,0:T(8,128)(2,1)S(1)} %get-tuple-element.26.values_ref, ...), custom_call_target="tpu_custom_call" | custom-call | flops 262144000 | bytes 2097152 | tf_op jit(solution)/shard_map/beside/pallas_call | solution.py:376
  25.7 0.0 collective-permute-done.6.refs_1_
  25.7 1.5 %collective-permute-done.7.refs_2_ = f32[16,1024]{1,0:T(8,128)S(1)} collective-permute-done((f32[16,1024]{1,0:T(8,128)S(1)}, f32[16,1024]{1,0:T(8,128)S(1)}, u32[]{:S(2)}, u32[]{:S(2)}) %collective-permute-start.7) | collective-permute-done | bytes 65568 | tf_op jit(solution)/shard_map/ppermute | solution.py:420
  27.2 0.1 collective-permute-done.8.refs_3_
  27.4 0.1 collective-permute-start.9
  27.5 0.8 %factor.2.before_ref = f32[16,1024]{1,0:T(8,128)S(1)} custom-call(f32[16,1024]{1,0:T(8,128)S(1)} %add.15.proj_ref, bf16[2048,512]{1,0:T(8,128)(2,1)S(1)} %get-tuple-element.32.refs_5_.rest_0_, bf16[2048,512]{1,0:T(8,128)(2,1)S(1)} %get-tuple-element.35.refs_5_.rest_1_, bf16[2048,512]{1,0:T(8,128)(2,1)S(1)} %get-tuple-element.33.refs_6_.rest_2_, ...), custom_call_target="tpu_custom_call" | custom-call | flops 1048576000 | bytes 4194304 | tf_op jit(solution)/shard_map/factor/pallas_call | solution.py:269
  28.3 0.5 %collective-permute-done.9.proj_ref = f32[16,1024]{1,0:T(8,128)S(1)} collective-permute-done((f32[16,1024]{1,0:T(8,128)S(1)}, f32[16,1024]{1,0:T(8,128)S(1)}, u32[]{:S(2)}, u32[]{:S(2)}) %collective-permute-start.9) | collective-permute-done | bytes 65568 | tf_op jit(solution)/shard_map/ppermute | solution.py:428
  28.7 0.8 %factor.3.factor_ref = f32[16,1024]{1,0:T(8,128)S(1)} custom-call(f32[16,1024]{1,0:T(8,128)S(1)} %factor.2.before_ref, f32[16,1024]{1,0:T(8,128)S(1)} %collective-permute-done.9.proj_ref, bf16[2048,512]{1,0:T(8,128)(2,1)S(1)} %get-tuple-element.32.refs_5_.rest_0_, bf16[2048,512]{1,0:T(8,128)(2,1)S(1)} %get-tuple-element.35.refs_5_.rest_1_, ...), custom_call_target="tpu_custom_call" | custom-call | flops 1048576000 | bytes 4194304 | tf_op jit(solution)/shard_map/factor/pallas_call | solution.py:269
  29.5 0.8 %spread.2 = f32[16,1024]{1,0:T(8,128)S(1)} custom-call(f32[16,1024]{1,0:T(8,128)S(1)} %factor.3.factor_ref, bf16[1024,1024]{1,0:T(8,128)(2,1)S(1)} %get-tuple-element.37.high_ref, bf16[1024,1024]{1,0:T(8,128)(2,1)S(1)} %get-tuple-element.38.low_ref), custom_call_target="tpu_custom_call" | custom-call | flops 891289600 | bytes 4194304 | tf_op jit(solution)/shard_map/spread/pallas_call | solution.py:294
  30.3 0.2 collective-permute-start.10
  30.4 0.8 %spread.3 = f32[16,1024]{1,0:T(8,128)S(1)} custom-call(f32[16,1024]{1,0:T(8,128)S(1)} %factor.3.factor_ref, bf16[1024,1024]{1,0:T(8,128)(2,1)S(1)} %get-tuple-element.39.high_ref, bf16[1024,1024]{1,0:T(8,128)(2,1)S(1)} %get-tuple-element.40.low_ref), custom_call_target="tpu_custom_call" | custom-call | flops 891289600 | bytes 4194304 | tf_op jit(solution)/shard_map/spread/pallas_call | solution.py:294
  31.2 0.3 %collective-permute-done.10 = f32[16,1024]{1,0:T(8,128)S(1)} collective-permute-done((f32[16,1024]{1,0:T(8,128)S(1)}, f32[16,1024]{1,0:T(8,128)S(1)}, u32[]{:S(2)}, u32[]{:S(2)}) %collective-permute-start.10) | collective-permute-done | bytes 65568 | tf_op jit(solution)/shard_map/ppermute | solution.py:428
  31.5 0.6 %fusion = f32[16,1024]{1,0:T(8,128)} fusion(f32[16,1024]{1,0:T(8,128)S(1)} %spread.3, f32[16,1024]{1,0:T(8,128)S(1)} %collective-permute-done.10, f32[16,512]{1,0:T(8,128)S(1)} %get-tuple-element.34.refs_4_, f32[16,512]{1,0:T(8,128)S(1)} %get-tuple-element.31.refs_4_), kind=kLoop, calls=%fused_computation.1 | loop fusion | flops 49152 | bytes 262144 | tf_op jit(solution)/shard_map/add | solution.py:491
  (4 shorter events, 0.1 us)
Async XLA Ops:
  0.9 3.5 %collective-permute-start = (f32[16,1280]{1,0:T(8,128)S(1)}, f32[16,1280]{1,0:T(8,128)S(1)}, u32[]{:S(2)}, u32[]{:S(2)}) collective-permute-start(f32[16,1280]{1,0:T(8,128)S(1)} %get-tuple-element.23.stack_ref), channel_id=1, source_target_pairs={{1,0},{0,1},{3,2},{2,3},{5,4},{4,5},{7,6},{6,7},{9,8},{8,9},{11,10... | collective-permute-start | bytes 245768 | tf_op jit(solution)/shard_map/ppermute | solution.py:428
  1.4 13.5 %slice-start = ((s8[8388608]{0:T(1024)(128)(4,1)}), s8[4194304]{0:T(1024)(128)(4,1)S(1)}, s32[]{:S(2)}) async-start(s8[8388608]{0:T(1024)(128)(4,1)} %bitcast), calls=%async_computation | async-start | bytes 8388608
  4.4 10.5 %slice-start.1 = ((s8[8388608]{0:T(1024)(128)(4,1)}), s8[4194304]{0:T(1024)(128)(4,1)S(1)}, s32[]{:S(2)}) async-start(s8[8388608]{0:T(1024)(128)(4,1)} %bitcast), calls=%async_computation.1 | async-start | bytes 8388608
  4.4 10.4 %collective-permute-start.1 = (f32[16,1536]{1,0:T(8,128)S(1)}, f32[16,1536]{1,0:T(8,128)S(1)}, u32[]{:S(2)}, u32[]{:S(2)}) collective-permute-start(f32[16,1536]{1,0:T(8,128)S(1)} %strip.1.own_ref), channel_id=1, source_target_pairs={{0,1},{1,0},{2,4},{3,5},{4,2},{5,3},{6,8},{7,9},{8,6},{9,7},{10,12... | collective-permute-start | bytes 294920 | tf_op jit(solution)/shard_map/ppermute | solution.py:443
  4.5 10.3 %collective-permute-start.2 = (f32[16,1536]{1,0:T(8,128)S(1)}, f32[16,1536]{1,0:T(8,128)S(1)}, u32[]{:S(2)}, u32[]{:S(2)}) collective-permute-start(f32[16,1536]{1,0:T(8,128)S(1)} %strip.1.own_ref), channel_id=1, source_target_pairs={{0,2},{1,3},{2,0},{3,1},{4,6},{5,7},{6,4},{7,5},{8,10},{9,11},{10,... | collective-permute-start | bytes 294920 | tf_op jit(solution)/shard_map/ppermute | solution.py:443
  8.5 6.4 %copy-start = (s32[8,8]{1,0:T(8,128)S(1)}, s32[8,8]{1,0:T(8,128)}, u32[]{:S(2)}) copy-start(s32[8,8]{1,0:T(8,128)} %ids_ref.3) | copy-start | bytes 772
  8.5 6.4 %copy-start.1 = (s32[8]{0:T(128)S(1)}, s32[8]{0:T(128)}, u32[]{:S(2)}) copy-start(s32[8]{0:T(128)} %counts_ref.3) | copy-start | bytes 100
  11.2 6.7 %collective-permute-start.3 = (f32[16,1024]{1,0:T(8,128)S(1)}, f32[16,1024]{1,0:T(8,128)S(1)}, u32[]{:S(2)}, u32[]{:S(2)}) collective-permute-start(f32[16,1024]{1,0:T(8,128)S(1)} %get-tuple-element.30.rest_0_.refs_0_), channel_id=1, source_target_pairs={{0,6},{2,4},{4,2},{6,0},{8,14},{10,12},{12,10},{14,8},{16,22},{18,... | collective-permute-start | bytes 196616 | tf_op jit(solution)/shard_map/ppermute | solution.py:420
  12.7 5.2 %collective-permute-start.4 = (f32[16,1024]{1,0:T(8,128)S(1)}, f32[16,1024]{1,0:T(8,128)S(1)}, u32[]{:S(2)}, u32[]{:S(2)}) collective-permute-start(f32[16,1024]{1,0:T(8,128)S(1)} %get-tuple-element.30.rest_0_.refs_0_), channel_id=1, source_target_pairs={{0,4},{2,6},{4,0},{6,2},{8,12},{10,14},{12,8},{14,10},{16,20},{18,... | collective-permute-start | bytes 196616 | tf_op jit(solution)/shard_map/ppermute | solution.py:420
  12.9 5.1 %collective-permute-start.5 = (f32[16,1024]{1,0:T(8,128)S(1)}, f32[16,1024]{1,0:T(8,128)S(1)}, u32[]{:S(2)}, u32[]{:S(2)}) collective-permute-start(f32[16,1024]{1,0:T(8,128)S(1)} %get-tuple-element.30.rest_0_.refs_0_), channel_id=1, source_target_pairs={{0,2},{2,0},{4,6},{6,4},{8,10},{10,8},{12,14},{14,12},{16,18},{18,... | collective-permute-start | bytes 196616 | tf_op jit(solution)/shard_map/ppermute | solution.py:420
  18.0 7.7 %collective-permute-start.6 = (f32[16,1024]{1,0:T(8,128)S(1)}, f32[16,1024]{1,0:T(8,128)S(1)}, u32[]{:S(2)}, u32[]{:S(2)}) collective-permute-start(f32[16,1024]{1,0:T(8,128)S(1)} %add.14.rest_0_.refs_0_), channel_id=1, source_target_pairs={{0,16},{2,18},{4,20},{6,22},{8,24},{10,26},{12,28},{14,30},{16,0},... | collective-permute-start | bytes 196616 | tf_op jit(solution)/shard_map/ppermute | solution.py:420
  21.1 6.2 %collective-permute-start.7 = (f32[16,1024]{1,0:T(8,128)S(1)}, f32[16,1024]{1,0:T(8,128)S(1)}, u32[]{:S(2)}, u32[]{:S(2)}) collective-permute-start(f32[16,1024]{1,0:T(8,128)S(1)} %add.14.rest_0_.refs_0_), channel_id=1, source_target_pairs={{0,24},{2,26},{4,28},{6,30},{8,16},{10,18},{12,20},{14,22},{16,8},... | collective-permute-start | bytes 196616 | tf_op jit(solution)/shard_map/ppermute | solution.py:420
  22.4 5.0 %collective-permute-start.8 = (f32[16,1024]{1,0:T(8,128)S(1)}, f32[16,1024]{1,0:T(8,128)S(1)}, u32[]{:S(2)}, u32[]{:S(2)}) collective-permute-start(f32[16,1024]{1,0:T(8,128)S(1)} %add.14.rest_0_.refs_0_), channel_id=1, source_target_pairs={{0,8},{2,10},{4,12},{6,14},{8,0},{10,2},{12,4},{14,6},{16,24},{18,... | collective-permute-start | bytes 196616 | tf_op jit(solution)/shard_map/ppermute | solution.py:420
  27.4 1.3 %collective-permute-start.9 = (f32[16,1024]{1,0:T(8,128)S(1)}, f32[16,1024]{1,0:T(8,128)S(1)}, u32[]{:S(2)}, u32[]{:S(2)}) collective-permute-start(f32[16,1024]{1,0:T(8,128)S(1)} %add.15.proj_ref), channel_id=1, source_target_pairs={{1,0},{0,1},{3,2},{2,3},{5,4},{4,5},{7,6},{6,7},{9,8},{8,9},{11,10... | collective-permute-start | bytes 196616 | tf_op jit(solution)/shard_map/ppermute | solution.py:428
  30.3 1.3 %collective-permute-start.10 = (f32[16,1024]{1,0:T(8,128)S(1)}, f32[16,1024]{1,0:T(8,128)S(1)}, u32[]{:S(2)}, u32[]{:S(2)}) collective-permute-start(f32[16,1024]{1,0:T(8,128)S(1)} %spread.2), channel_id=1, source_target_pairs={{1,0},{0,1},{3,2},{2,3},{5,4},{4,5},{7,6},{6,7},{9,8},{8,9},{11,10... | collective-permute-start | bytes 196616 | tf_op jit(solution)/shard_map/ppermute | solution.py:428

commit v23 on v22

--- a/solution.py
+++ b/solution.py
@@ -410,7 +410,6 @@
     assert count & (count - 1) == 0
     bits = [1 << i for i in range(count.bit_length() - 1)]
     rounds = [(low | high, high, low) for low, high in zip(bits[0::2], bits[1::2])]
-    rounds[1:] = [(high, both, low) for both, high, low in rounds[1:]]
     return rounds + [(bit,) for bit in bits[len(rounds) * 2 :]]
 
 

time: 32.3 us -> 32.3 us (level)
  transfers between devices with their start and end apart: 11 -> 11, of which waited for: 4 -> 3; matrix products, arithmetic and copies ran while one was open for 0% -> 0% of each run, Pallas kernels for 41% -> 42%
where the time goes in v23:
time: 32.3 us; the launch traced here: 32.1 us
  Pallas kernels  15.8 us (49%)
  starting transfers between devices  13.1 us (41%)
  waiting for transfers between devices  2.39 us (7%)
  other arithmetic  0.64 us (2%)
    ppermute x6, starting transfers between devices, butterfly_round(): lax.ppermute(value, axis, [(i, i ^ step) for i in range(count)])  8.29 us
    pallas_call x2, Pallas kernels, beside_round(): pl.pallas_call(functools.partial(beside_kernel, first, first_row, grain_o...  6.05 us
    pallas_call x2, Pallas kernels, project(): pl.pallas_call(functools.partial(project_kernel, scale, grain_of(scale *...  5.71 us
    ppermute x2, starting transfers between devices, paired(): return lax.ppermute(value, (axis, other), pairs)  4.07 us
    ppermute x6, waiting for transfers between devices, butterfly_round(): lax.ppermute(value, axis, [(i, i ^ step) for i in range(count)])  1.57 us
    pallas_call x2, Pallas kernels, spread(): pl.pallas_call(functools.partial(spread_kernel, scale), out_shape=jax.Sha...  1.53 us
    pallas_call x2, Pallas kernels, factored(): pl.pallas_call(kernel, out_shape=jax.ShapeDtypeStruct((probes, rows), jnp...  1.53 us
    pallas_call x1, Pallas kernels, prepare(): pl.pallas_call(functools.partial(prepare_kernel, blocks), out_shape=(jax....  0.87 us
  transfers between devices with their start and end apart: 11, of which 3 were waited for; matrix products, arithmetic and copies ran while one was open for 0% of the time, Pallas kernels for 42%

profile of v23, /device:TPU:0, one launch (start us, length us, event | category | flops | bytes accessed | tf_op | source)
XLA Modules:
  0.0 32.1 jit_solution(12955634038915867065)
XLA Ops:
  0.0 0.9 %prepare.1 = (f32[16,1280]{1,0:T(8,128)S(1)}, f32[2,1024]{1,0:T(2,128)S(1)}) custom-call(f32[16,1024]{1,0:T(8,128)} %probes_ref.1, f32[2,1024]{1,0:T(2,128)} %locations_ref.1, f32[2,1024]{1,0:T(2,128)} %knots_ref.1), custom_call_target="tpu_custom_call" | custom-call | tf_op jit(solution)/shard_map/prepare/pallas_call | solution.py:100
  0.9 0.5 %collective-permute-start = (f32[16,1280]{1,0:T(8,128)S(1)}, f32[16,1280]{1,0:T(8,128)S(1)}, u32[]{:S(2)}, u32[]{:S(2)}) collective-permute-start(f32[16,1280]{1,0:T(8,128)S(1)} %get-tuple-element.23.stack_ref), channel_id=1, source_target_pairs={{1,0},{0,1},{3,2},{2,3},{5,4},{4,5},{7,6},{6,7},{9,8},{8,9},{11,10... | collective-permute-start | bytes 245768 | tf_op jit(solution)/shard_map/ppermute | solution.py:427
  1.4 0.0 slice-start
  1.4 3.0 %project.2 = (f32[16,1024]{1,0:T(8,128)S(1)}, bf16[1024,1024]{1,0:T(8,128)(2,1)S(1)}, bf16[1024,1024]{1,0:T(8,128)(2,1)S(1)}, f32[1024,8]{1,0:T(8,128)S(1)}, f32[16,1280]{1,0:T(8,128)S(1)}) custom-call(f32[16,1280]{1,0:T(8,128)S(1)} %get-tuple-element.23.stack_ref, f32[2,1024]{1,0:T(2,128)S(1)} %get-tuple-element.24.rest_0_), custom_call_target="tpu_custom_call" | custom-call | flops 2936012800 | bytes 4194304 | tf_op jit(solution)/shard_map/project/pallas_call | solution.py:226
  4.4 0.0 collective-permute-done.below_ref.above_ref.stack_ref
  4.4 0.0 slice-start.1
  4.4 0.1 collective-permute-start.1
  4.5 3.9 %collective-permute-start.2 = (f32[16,1536]{1,0:T(8,128)S(1)}, f32[16,1536]{1,0:T(8,128)S(1)}, u32[]{:S(2)}, u32[]{:S(2)}) collective-permute-start(f32[16,1536]{1,0:T(8,128)S(1)} %strip.1.own_ref), channel_id=1, source_target_pairs={{0,2},{1,3},{2,0},{3,1},{4,6},{5,7},{6,4},{7,5},{8,10},{9,11},{10,... | collective-permute-start | bytes 294920 | tf_op jit(solution)/shard_map/ppermute | solution.py:442
  8.5 0.0 copy-start
  8.5 0.0 copy-start.1
  8.5 2.7 %project.3 = (f32[16,1024]{1,0:T(8,128)S(1)}, bf16[1024,1024]{1,0:T(8,128)(2,1)S(1)}, bf16[1024,1024]{1,0:T(8,128)(2,1)S(1)}) custom-call(f32[16,1280]{1,0:T(8,128)S(1)} %collective-permute-done.below_ref.above_ref.stack_ref, f32[16,1024]{1,0:T(8,128)S(1)} %get-tuple-element.28.rest_0_, f32[1024,8]{1,0:T(8,128)S(1)} %get-tuple-element.29.rest_1_), custom_call_target="tpu_custom_call" | custom-call | flops 2936012800 | bytes 4194304 | tf_op jit(solution)/shard_map/project/pallas_call | solution.py:226
  11.2 1.5 %collective-permute-start.3 = (f32[16,1024]{1,0:T(8,128)S(1)}, f32[16,1024]{1,0:T(8,128)S(1)}, u32[]{:S(2)}, u32[]{:S(2)}) collective-permute-start(f32[16,1024]{1,0:T(8,128)S(1)} %get-tuple-element.30.rest_0_.refs_0_), channel_id=1, source_target_pairs={{0,6},{2,4},{4,2},{6,0},{8,14},{10,12},{12,10},{14,8},{16,22},{18,... | collective-permute-start | bytes 196616 | tf_op jit(solution)/shard_map/ppermute | solution.py:419
  12.7 0.2 collective-permute-start.4
  12.9 1.9 %collective-permute-start.5 = (f32[16,1024]{1,0:T(8,128)S(1)}, f32[16,1024]{1,0:T(8,128)S(1)}, u32[]{:S(2)}, u32[]{:S(2)}) collective-permute-start(f32[16,1024]{1,0:T(8,128)S(1)} %get-tuple-element.30.rest_0_.refs_0_), channel_id=1, source_target_pairs={{0,2},{2,0},{4,6},{6,4},{8,10},{10,8},{12,14},{14,12},{16,18},{18,... | collective-permute-start | bytes 196616 | tf_op jit(solution)/shard_map/ppermute | solution.py:419
  14.8 0.0 collective-permute-done.1.odd_ref
  14.8 0.0 collective-permute-done.2.even_ref
  14.8 0.1 assemble.1
  14.9 0.0 slice-done
  14.9 0.0 slice-done.1
  14.9 0.0 copy-done
  14.9 0.0 copy-done.1
  14.9 3.0 %beside.2 = (f32[16,512]{1,0:T(8,128)S(1)}, bf16[2048,512]{1,0:T(8,128)(2,1)S(1)}, bf16[2048,512]{1,0:T(8,128)(2,1)S(1)}) custom-call(s32[8,8]{1,0:T(8,128)S(1)} %copy-done, s32[8]{0:T(128)S(1)} %copy-done.1, f32[16,1280]{1,0:T(8,128)S(1)} %get-tuple-element.25.own_ref, bf16[32,3968]{1,0:T(8,128)(2,1)S(1)} %get-tuple-element.26.values_ref, ...), custom_call_target="tpu_custom_call" | custom-call | flops 262144000 | bytes 2097152 | tf_op jit(solution)/shard_map/beside/pallas_call | solution.py:376
  17.9 0.0 collective-permute-done.3.refs_1_
  17.9 0.0 collective-permute-done.4.refs_2_
  18.0 0.0 collective-permute-done.5.refs_3_
  18.0 4.1 %collective-permute-start.6 = (f32[16,1024]{1,0:T(8,128)S(1)}, f32[16,1024]{1,0:T(8,128)S(1)}, u32[]{:S(2)}, u32[]{:S(2)}) collective-permute-start(f32[16,1024]{1,0:T(8,128)S(1)} %add.14.rest_0_.refs_0_), channel_id=1, source_target_pairs={{0,24},{2,26},{4,28},{6,30},{8,16},{10,18},{12,20},{14,22},{16,8},... | collective-permute-start | bytes 196616 | tf_op jit(solution)/shard_map/ppermute | solution.py:419
  22.1 0.0 collective-permute-start.7
  22.1 0.6 %collective-permute-start.8 = (f32[16,1024]{1,0:T(8,128)S(1)}, f32[16,1024]{1,0:T(8,128)S(1)}, u32[]{:S(2)}, u32[]{:S(2)}) collective-permute-start(f32[16,1024]{1,0:T(8,128)S(1)} %add.14.rest_0_.refs_0_), channel_id=1, source_target_pairs={{0,8},{2,10},{4,12},{6,14},{8,0},{10,2},{12,4},{14,6},{16,24},{18,... | collective-permute-start | bytes 196616 | tf_op jit(solution)/shard_map/ppermute | solution.py:419
  22.7 3.0 %beside.3 = (f32[16,512]{1,0:T(8,128)S(1)}, bf16[2048,512]{1,0:T(8,128)(2,1)S(1)}, bf16[2048,512]{1,0:T(8,128)(2,1)S(1)}) custom-call(s32[8,8]{1,0:T(8,128)S(1)} %copy-done, s32[8]{0:T(128)S(1)} %copy-done.1, f32[16,1280]{1,0:T(8,128)S(1)} %get-tuple-element.25.own_ref, bf16[32,3968]{1,0:T(8,128)(2,1)S(1)} %get-tuple-element.26.values_ref, ...), custom_call_target="tpu_custom_call" | custom-call | flops 262144000 | bytes 2097152 | tf_op jit(solution)/shard_map/beside/pallas_call | solution.py:376
  25.8 0.0 collective-permute-done.6.refs_1_
  25.8 1.6 %collective-permute-done.7.refs_2_ = f32[16,1024]{1,0:T(8,128)S(1)} collective-permute-done((f32[16,1024]{1,0:T(8,128)S(1)}, f32[16,1024]{1,0:T(8,128)S(1)}, u32[]{:S(2)}, u32[]{:S(2)}) %collective-permute-start.7) | collective-permute-done | bytes 65568 | tf_op jit(solution)/shard_map/ppermute | solution.py:419
  27.3 0.0 collective-permute-done.8.refs_3_
  27.4 0.1 collective-permute-start.9
  27.4 0.8 %factor.2.before_ref = f32[16,1024]{1,0:T(8,128)S(1)} custom-call(f32[16,1024]{1,0:T(8,128)S(1)} %add.15.proj_ref, bf16[2048,512]{1,0:T(8,128)(2,1)S(1)} %get-tuple-element.32.refs_5_.rest_0_, bf16[2048,512]{1,0:T(8,128)(2,1)S(1)} %get-tuple-element.35.refs_5_.rest_1_, bf16[2048,512]{1,0:T(8,128)(2,1)S(1)} %get-tuple-element.33.refs_6_.rest_2_, ...), custom_call_target="tpu_custom_call" | custom-call | flops 1048576000 | bytes 4194304 | tf_op jit(solution)/shard_map/factor/pallas_call | solution.py:269
  28.2 0.5 %collective-permute-done.9.proj_ref = f32[16,1024]{1,0:T(8,128)S(1)} collective-permute-done((f32[16,1024]{1,0:T(8,128)S(1)}, f32[16,1024]{1,0:T(8,128)S(1)}, u32[]{:S(2)}, u32[]{:S(2)}) %collective-permute-start.9) | collective-permute-done | bytes 65568 | tf_op jit(solution)/shard_map/ppermute | solution.py:427
  28.7 0.8 %factor.3.factor_ref = f32[16,1024]{1,0:T(8,128)S(1)} custom-call(f32[16,1024]{1,0:T(8,128)S(1)} %factor.2.before_ref, f32[16,1024]{1,0:T(8,128)S(1)} %collective-permute-done.9.proj_ref, bf16[2048,512]{1,0:T(8,128)(2,1)S(1)} %get-tuple-element.32.refs_5_.rest_0_, bf16[2048,512]{1,0:T(8,128)(2,1)S(1)} %get-tuple-element.35.refs_5_.rest_1_, ...), custom_call_target="tpu_custom_call" | custom-call | flops 1048576000 | bytes 4194304 | tf_op jit(solution)/shard_map/factor/pallas_call | solution.py:269
  29.4 0.8 %spread.2 = f32[16,1024]{1,0:T(8,128)S(1)} custom-call(f32[16,1024]{1,0:T(8,128)S(1)} %factor.3.factor_ref, bf16[1024,1024]{1,0:T(8,128)(2,1)S(1)} %get-tuple-element.37.high_ref, bf16[1024,1024]{1,0:T(8,128)(2,1)S(1)} %get-tuple-element.38.low_ref), custom_call_target="tpu_custom_call" | custom-call | flops 891289600 | bytes 4194304 | tf_op jit(solution)/shard_map/spread/pallas_call | solution.py:294
  30.2 0.2 collective-permute-start.10
  30.4 0.8 %spread.3 = f32[16,1024]{1,0:T(8,128)S(1)} custom-call(f32[16,1024]{1,0:T(8,128)S(1)} %factor.3.factor_ref, bf16[1024,1024]{1,0:T(8,128)(2,1)S(1)} %get-tuple-element.39.high_ref, bf16[1024,1024]{1,0:T(8,128)(2,1)S(1)} %get-tuple-element.40.low_ref), custom_call_target="tpu_custom_call" | custom-call | flops 891289600 | bytes 4194304 | tf_op jit(solution)/shard_map/spread/pallas_call | solution.py:294
  31.1 0.3 %collective-permute-done.10 = f32[16,1024]{1,0:T(8,128)S(1)} collective-permute-done((f32[16,1024]{1,0:T(8,128)S(1)}, f32[16,1024]{1,0:T(8,128)S(1)}, u32[]{:S(2)}, u32[]{:S(2)}) %collective-permute-start.10) | collective-permute-done | bytes 65568 | tf_op jit(solution)/shard_map/ppermute | solution.py:427
  31.5 0.6 %fusion = f32[16,1024]{1,0:T(8,128)} fusion(f32[16,1024]{1,0:T(8,128)S(1)} %spread.3, f32[16,1024]{1,0:T(8,128)S(1)} %collective-permute-done.10, f32[16,512]{1,0:T(8,128)S(1)} %get-tuple-element.34.refs_4_, f32[16,512]{1,0:T(8,128)S(1)} %get-tuple-element.31.refs_4_), kind=kLoop, calls=%fused_computation.1 | loop fusion | flops 49152 | bytes 262144 | tf_op jit(solution)/shard_map/add | solution.py:490
  (4 shorter events, 0.1 us)
Async XLA Ops:
  0.9 3.5 %collective-permute-start = (f32[16,1280]{1,0:T(8,128)S(1)}, f32[16,1280]{1,0:T(8,128)S(1)}, u32[]{:S(2)}, u32[]{:S(2)}) collective-permute-start(f32[16,1280]{1,0:T(8,128)S(1)} %get-tuple-element.23.stack_ref), channel_id=1, source_target_pairs={{1,0},{0,1},{3,2},{2,3},{5,4},{4,5},{7,6},{6,7},{9,8},{8,9},{11,10... | collective-permute-start | bytes 245768 | tf_op jit(solution)/shard_map/ppermute | solution.py:427
  1.4 13.5 %slice-start = ((s8[8388608]{0:T(1024)(128)(4,1)}), s8[4194304]{0:T(1024)(128)(4,1)S(1)}, s32[]{:S(2)}) async-start(s8[8388608]{0:T(1024)(128)(4,1)} %bitcast), calls=%async_computation | async-start | bytes 8388608
  4.4 10.5 %slice-start.1 = ((s8[8388608]{0:T(1024)(128)(4,1)}), s8[4194304]{0:T(1024)(128)(4,1)S(1)}, s32[]{:S(2)}) async-start(s8[8388608]{0:T(1024)(128)(4,1)} %bitcast), calls=%async_computation.1 | async-start | bytes 8388608
  4.4 10.4 %collective-permute-start.1 = (f32[16,1536]{1,0:T(8,128)S(1)}, f32[16,1536]{1,0:T(8,128)S(1)}, u32[]{:S(2)}, u32[]{:S(2)}) collective-permute-start(f32[16,1536]{1,0:T(8,128)S(1)} %strip.1.own_ref), channel_id=1, source_target_pairs={{0,1},{1,0},{2,4},{3,5},{4,2},{5,3},{6,8},{7,9},{8,6},{9,7},{10,12... | collective-permute-start | bytes 294920 | tf_op jit(solution)/shard_map/ppermute | solution.py:442
  4.5 10.3 %collective-permute-start.2 = (f32[16,1536]{1,0:T(8,128)S(1)}, f32[16,1536]{1,0:T(8,128)S(1)}, u32[]{:S(2)}, u32[]{:S(2)}) collective-permute-start(f32[16,1536]{1,0:T(8,128)S(1)} %strip.1.own_ref), channel_id=1, source_target_pairs={{0,2},{1,3},{2,0},{3,1},{4,6},{5,7},{6,4},{7,5},{8,10},{9,11},{10,... | collective-permute-start | bytes 294920 | tf_op jit(solution)/shard_map/ppermute | solution.py:442
  8.5 6.4 %copy-start = (s32[8,8]{1,0:T(8,128)S(1)}, s32[8,8]{1,0:T(8,128)}, u32[]{:S(2)}) copy-start(s32[8,8]{1,0:T(8,128)} %ids_ref.3) | copy-start | bytes 772
  8.5 6.4 %copy-start.1 = (s32[8]{0:T(128)S(1)}, s32[8]{0:T(128)}, u32[]{:S(2)}) copy-start(s32[8]{0:T(128)} %counts_ref.3) | copy-start | bytes 100
  11.2 6.7 %collective-permute-start.3 = (f32[16,1024]{1,0:T(8,128)S(1)}, f32[16,1024]{1,0:T(8,128)S(1)}, u32[]{:S(2)}, u32[]{:S(2)}) collective-permute-start(f32[16,1024]{1,0:T(8,128)S(1)} %get-tuple-element.30.rest_0_.refs_0_), channel_id=1, source_target_pairs={{0,6},{2,4},{4,2},{6,0},{8,14},{10,12},{12,10},{14,8},{16,22},{18,... | collective-permute-start | bytes 196616 | tf_op jit(solution)/shard_map/ppermute | solution.py:419
  12.7 5.2 %collective-permute-start.4 = (f32[16,1024]{1,0:T(8,128)S(1)}, f32[16,1024]{1,0:T(8,128)S(1)}, u32[]{:S(2)}, u32[]{:S(2)}) collective-permute-start(f32[16,1024]{1,0:T(8,128)S(1)} %get-tuple-element.30.rest_0_.refs_0_), channel_id=1, source_target_pairs={{0,4},{2,6},{4,0},{6,2},{8,12},{10,14},{12,8},{14,10},{16,20},{18,... | collective-permute-start | bytes 196616 | tf_op jit(solution)/shard_map/ppermute | solution.py:419
  12.9 5.1 %collective-permute-start.5 = (f32[16,1024]{1,0:T(8,128)S(1)}, f32[16,1024]{1,0:T(8,128)S(1)}, u32[]{:S(2)}, u32[]{:S(2)}) collective-permute-start(f32[16,1024]{1,0:T(8,128)S(1)} %get-tuple-element.30.rest_0_.refs_0_), channel_id=1, source_target_pairs={{0,2},{2,0},{4,6},{6,4},{8,10},{10,8},{12,14},{14,12},{16,18},{18,... | collective-permute-start | bytes 196616 | tf_op jit(solution)/shard_map/ppermute | solution.py:419
  18.0 7.8 %collective-permute-start.6 = (f32[16,1024]{1,0:T(8,128)S(1)}, f32[16,1024]{1,0:T(8,128)S(1)}, u32[]{:S(2)}, u32[]{:S(2)}) collective-permute-start(f32[16,1024]{1,0:T(8,128)S(1)} %add.14.rest_0_.refs_0_), channel_id=1, source_target_pairs={{0,24},{2,26},{4,28},{6,30},{8,16},{10,18},{12,20},{14,22},{16,8},... | collective-permute-start | bytes 196616 | tf_op jit(solution)/shard_map/ppermute | solution.py:419
  22.1 5.2 %collective-permute-start.7 = (f32[16,1024]{1,0:T(8,128)S(1)}, f32[16,1024]{1,0:T(8,128)S(1)}, u32[]{:S(2)}, u32[]{:S(2)}) collective-permute-start(f32[16,1024]{1,0:T(8,128)S(1)} %add.14.rest_0_.refs_0_), channel_id=1, source_target_pairs={{0,16},{2,18},{4,20},{6,22},{8,24},{10,26},{12,28},{14,30},{16,0},... | collective-permute-start | bytes 196616 | tf_op jit(solution)/shard_map/ppermute | solution.py:419
  22.1 5.2 %collective-permute-start.8 = (f32[16,1024]{1,0:T(8,128)S(1)}, f32[16,1024]{1,0:T(8,128)S(1)}, u32[]{:S(2)}, u32[]{:S(2)}) collective-permute-start(f32[16,1024]{1,0:T(8,128)S(1)} %add.14.rest_0_.refs_0_), channel_id=1, source_target_pairs={{0,8},{2,10},{4,12},{6,14},{8,0},{10,2},{12,4},{14,6},{16,24},{18,... | collective-permute-start | bytes 196616 | tf_op jit(solution)/shard_map/ppermute | solution.py:419
  27.4 1.3 %collective-permute-start.9 = (f32[16,1024]{1,0:T(8,128)S(1)}, f32[16,1024]{1,0:T(8,128)S(1)}, u32[]{:S(2)}, u32[]{:S(2)}) collective-permute-start(f32[16,1024]{1,0:T(8,128)S(1)} %add.15.proj_ref), channel_id=1, source_target_pairs={{1,0},{0,1},{3,2},{2,3},{5,4},{4,5},{7,6},{6,7},{9,8},{8,9},{11,10... | collective-permute-start | bytes 196616 | tf_op jit(solution)/shard_map/ppermute | solution.py:427
  30.2 1.3 %collective-permute-start.10 = (f32[16,1024]{1,0:T(8,128)S(1)}, f32[16,1024]{1,0:T(8,128)S(1)}, u32[]{:S(2)}, u32[]{:S(2)}) collective-permute-start(f32[16,1024]{1,0:T(8,128)S(1)} %spread.2), channel_id=1, source_target_pairs={{1,0},{0,1},{3,2},{2,3},{5,4},{4,5},{7,6},{6,7},{9,8},{8,9},{11,10... | collective-permute-start | bytes 196616 | tf_op jit(solution)/shard_map/ppermute | solution.py:427

commit v24 on v23

--- a/solution.py
+++ b/solution.py
@@ -466,7 +466,8 @@
     projection = parts[-1][0]
     rounds = len(butterfly_rounds(lax.axis_size("space")))
     pieces = math.gcd(math.gcd(own_blocks, rounds), knot_precision.shape[0] // LANES)
-    per_piece, per_split = own_blocks // pieces, knot_precision.shape[0] // pieces
+    bounds = [own_blocks * i * (i + 2) // (pieces * (pieces + 2)) for i in range(pieces + 1)]
+    per_split = knot_precision.shape[0] // pieces
     base, splits = [], []
     for turn in range(rounds):
         got = butterfly_round(projection, "space", turn)
@@ -475,7 +476,7 @@
             if i * rounds // pieces == turn:
                 done = beside_round(
                     neighbours, counts, stack, values, coords, knot_precision, extent,
-                    i * per_piece, per_piece, i * per_split, per_split, [projection],
+                    bounds[i], bounds[i + 1] - bounds[i], i * per_split, per_split, [projection],
                 )
                 base.append(done[0])
                 splits.append(done[1:])

time: 32.3 us -> 32.4 us (level)
  waiting for transfers between devices: 2.39 us -> 1.98 us
    ppermute x6, waiting for transfers between devices: 1.57 us -> 1.17 us  [butterfly_round(): lax.ppermute(value, axis, [(i, i ^ step) for i in range(count)])]
where the time goes in v24:
time: 32.4 us; the launch traced here: 32.2 us
  Pallas kernels  16 us (49%)
  starting transfers between devices  13.4 us (41%)
  waiting for transfers between devices  1.98 us (6%)
  other arithmetic  0.65 us (2%)
    ppermute x6, starting transfers between devices, butterfly_round(): lax.ppermute(value, axis, [(i, i ^ step) for i in range(count)])  8.54 us
    pallas_call x2, Pallas kernels, beside_round(): pl.pallas_call(functools.partial(beside_kernel, first, first_row, grain_o...  6.2 us
    pallas_call x2, Pallas kernels, project(): pl.pallas_call(functools.partial(project_kernel, scale, grain_of(scale *...  5.79 us
    ppermute x2, starting transfers between devices, paired(): return lax.ppermute(value, (axis, other), pairs)  4.07 us
    pallas_call x2, Pallas kernels, spread(): pl.pallas_call(functools.partial(spread_kernel, scale), out_shape=jax.Sha...  1.53 us
    pallas_call x2, Pallas kernels, factored(): pl.pallas_call(kernel, out_shape=jax.ShapeDtypeStruct((probes, rows), jnp...  1.53 us
    ppermute x6, waiting for transfers between devices, butterfly_round(): lax.ppermute(value, axis, [(i, i ^ step) for i in range(count)])  1.17 us
    pallas_call x1, Pallas kernels, prepare(): pl.pallas_call(functools.partial(prepare_kernel, blocks), out_shape=(jax....  0.87 us
  transfers between devices with their start and end apart: 11, of which 3 were waited for; matrix products, arithmetic and copies ran while one was open for 0% of the time, Pallas kernels for 42%

profile of v24, /device:TPU:0, one launch (start us, length us, event | category | flops | bytes accessed | tf_op | source)
XLA Modules:
  0.0 32.2 jit_solution(4436418449745461825)
XLA Ops:
  0.0 0.9 %prepare.1 = (f32[16,1280]{1,0:T(8,128)S(1)}, f32[2,1024]{1,0:T(2,128)S(1)}) custom-call(f32[16,1024]{1,0:T(8,128)} %probes_ref.1, f32[2,1024]{1,0:T(2,128)} %locations_ref.1, f32[2,1024]{1,0:T(2,128)} %knots_ref.1), custom_call_target="tpu_custom_call" | custom-call | tf_op jit(solution)/shard_map/prepare/pallas_call | solution.py:100
  0.9 0.5 %collective-permute-start = (f32[16,1280]{1,0:T(8,128)S(1)}, f32[16,1280]{1,0:T(8,128)S(1)}, u32[]{:S(2)}, u32[]{:S(2)}) collective-permute-start(f32[16,1280]{1,0:T(8,128)S(1)} %get-tuple-element.23.stack_ref), channel_id=1, source_target_pairs={{1,0},{0,1},{3,2},{2,3},{5,4},{4,5},{7,6},{6,7},{9,8},{8,9},{11,10... | collective-permute-start | bytes 245768 | tf_op jit(solution)/shard_map/ppermute | solution.py:427
  1.4 0.0 slice-start
  1.4 3.0 %project.2 = (f32[16,1024]{1,0:T(8,128)S(1)}, bf16[1024,1024]{1,0:T(8,128)(2,1)S(1)}, bf16[1024,1024]{1,0:T(8,128)(2,1)S(1)}, f32[1024,8]{1,0:T(8,128)S(1)}, f32[16,1280]{1,0:T(8,128)S(1)}) custom-call(f32[16,1280]{1,0:T(8,128)S(1)} %get-tuple-element.23.stack_ref, f32[2,1024]{1,0:T(2,128)S(1)} %get-tuple-element.24.rest_0_), custom_call_target="tpu_custom_call" | custom-call | flops 2936012800 | bytes 4194304 | tf_op jit(solution)/shard_map/project/pallas_call | solution.py:226
  4.4 0.0 collective-permute-done.below_ref.above_ref.stack_ref
  4.4 0.0 slice-start.1
  4.5 0.1 collective-permute-start.1
  4.6 3.9 %collective-permute-start.2 = (f32[16,1536]{1,0:T(8,128)S(1)}, f32[16,1536]{1,0:T(8,128)S(1)}, u32[]{:S(2)}, u32[]{:S(2)}) collective-permute-start(f32[16,1536]{1,0:T(8,128)S(1)} %strip.1.own_ref), channel_id=1, source_target_pairs={{0,2},{1,3},{2,0},{3,1},{4,6},{5,7},{6,4},{7,5},{8,10},{9,11},{10,... | collective-permute-start | bytes 294920 | tf_op jit(solution)/shard_map/ppermute | solution.py:442
  8.5 0.0 copy-start
  8.5 0.0 copy-start.1
  8.5 2.8 %project.3 = (f32[16,1024]{1,0:T(8,128)S(1)}, bf16[1024,1024]{1,0:T(8,128)(2,1)S(1)}, bf16[1024,1024]{1,0:T(8,128)(2,1)S(1)}) custom-call(f32[16,1280]{1,0:T(8,128)S(1)} %collective-permute-done.below_ref.above_ref.stack_ref, f32[16,1024]{1,0:T(8,128)S(1)} %get-tuple-element.28.rest_0_, f32[1024,8]{1,0:T(8,128)S(1)} %get-tuple-element.29.rest_1_), custom_call_target="tpu_custom_call" | custom-call | flops 2936012800 | bytes 4194304 | tf_op jit(solution)/shard_map/project/pallas_call | solution.py:226
  11.3 1.5 %collective-permute-start.3 = (f32[16,1024]{1,0:T(8,128)S(1)}, f32[16,1024]{1,0:T(8,128)S(1)}, u32[]{:S(2)}, u32[]{:S(2)}) collective-permute-start(f32[16,1024]{1,0:T(8,128)S(1)} %get-tuple-element.30.rest_0_.refs_0_), channel_id=1, source_target_pairs={{0,6},{2,4},{4,2},{6,0},{8,14},{10,12},{12,10},{14,8},{16,22},{18,... | collective-permute-start | bytes 196616 | tf_op jit(solution)/shard_map/ppermute | solution.py:419
  12.8 0.2 collective-permute-start.4
  13.0 1.9 %collective-permute-start.5 = (f32[16,1024]{1,0:T(8,128)S(1)}, f32[16,1024]{1,0:T(8,128)S(1)}, u32[]{:S(2)}, u32[]{:S(2)}) collective-permute-start(f32[16,1024]{1,0:T(8,128)S(1)} %get-tuple-element.30.rest_0_.refs_0_), channel_id=1, source_target_pairs={{0,2},{2,0},{4,6},{6,4},{8,10},{10,8},{12,14},{14,12},{16,18},{18,... | collective-permute-start | bytes 196616 | tf_op jit(solution)/shard_map/ppermute | solution.py:419
  14.9 0.0 collective-permute-done.1.odd_ref
  14.9 0.0 collective-permute-done.2.even_ref
  14.9 0.1 assemble.1
  14.9 0.0 slice-done
  14.9 0.0 slice-done.1
  15.0 0.0 copy-done
  15.0 0.0 copy-done.1
  15.0 2.8 %beside.2 = (f32[16,384]{1,0:T(8,128)S(1)}, bf16[2048,512]{1,0:T(8,128)(2,1)S(1)}, bf16[2048,512]{1,0:T(8,128)(2,1)S(1)}) custom-call(s32[8,8]{1,0:T(8,128)S(1)} %copy-done, s32[8]{0:T(128)S(1)} %copy-done.1, f32[16,1280]{1,0:T(8,128)S(1)} %get-tuple-element.25.own_ref, bf16[32,3968]{1,0:T(8,128)(2,1)S(1)} %get-tuple-element.26.values_ref, ...), custom_call_target="tpu_custom_call" | custom-call | flops 196608000 | bytes 1572864 | tf_op jit(solution)/shard_map/beside/pallas_call | solution.py:376
  17.8 0.0 collective-permute-done.3.refs_1_
  17.8 0.0 collective-permute-done.4.refs_2_
  17.8 0.0 collective-permute-done.5.refs_3_
  17.8 4.3 %collective-permute-start.6 = (f32[16,1024]{1,0:T(8,128)S(1)}, f32[16,1024]{1,0:T(8,128)S(1)}, u32[]{:S(2)}, u32[]{:S(2)}) collective-permute-start(f32[16,1024]{1,0:T(8,128)S(1)} %add.14.rest_0_.refs_0_), channel_id=1, source_target_pairs={{0,24},{2,26},{4,28},{6,30},{8,16},{10,18},{12,20},{14,22},{16,8},... | collective-permute-start | bytes 196616 | tf_op jit(solution)/shard_map/ppermute | solution.py:419
  22.2 0.0 collective-permute-start.7
  22.2 0.6 %collective-permute-start.8 = (f32[16,1024]{1,0:T(8,128)S(1)}, f32[16,1024]{1,0:T(8,128)S(1)}, u32[]{:S(2)}, u32[]{:S(2)}) collective-permute-start(f32[16,1024]{1,0:T(8,128)S(1)} %add.14.rest_0_.refs_0_), channel_id=1, source_target_pairs={{0,8},{2,10},{4,12},{6,14},{8,0},{10,2},{12,4},{14,6},{16,24},{18,... | collective-permute-start | bytes 196616 | tf_op jit(solution)/shard_map/ppermute | solution.py:419
  22.8 3.4 %beside.3 = (f32[16,640]{1,0:T(8,128)S(1)}, bf16[2048,512]{1,0:T(8,128)(2,1)S(1)}, bf16[2048,512]{1,0:T(8,128)(2,1)S(1)}) custom-call(s32[8,8]{1,0:T(8,128)S(1)} %copy-done, s32[8]{0:T(128)S(1)} %copy-done.1, f32[16,1280]{1,0:T(8,128)S(1)} %get-tuple-element.25.own_ref, bf16[32,3968]{1,0:T(8,128)(2,1)S(1)} %get-tuple-element.26.values_ref, ...), custom_call_target="tpu_custom_call" | custom-call | flops 327680000 | bytes 2621440 | tf_op jit(solution)/shard_map/beside/pallas_call | solution.py:376
  26.2 0.0 collective-permute-done.6.refs_1_
  26.3 1.2 %collective-permute-done.7.refs_2_ = f32[16,1024]{1,0:T(8,128)S(1)} collective-permute-done((f32[16,1024]{1,0:T(8,128)S(1)}, f32[16,1024]{1,0:T(8,128)S(1)}, u32[]{:S(2)}, u32[]{:S(2)}) %collective-permute-start.7) | collective-permute-done | bytes 65568 | tf_op jit(solution)/shard_map/ppermute | solution.py:419
  27.4 0.0 collective-permute-done.8.refs_3_
  27.4 0.1 collective-permute-start.9
  27.5 0.8 %factor.2.before_ref = f32[16,1024]{1,0:T(8,128)S(1)} custom-call(f32[16,1024]{1,0:T(8,128)S(1)} %add.15.proj_ref, bf16[2048,512]{1,0:T(8,128)(2,1)S(1)} %get-tuple-element.32.refs_5_.rest_0_, bf16[2048,512]{1,0:T(8,128)(2,1)S(1)} %get-tuple-element.35.refs_5_.rest_1_, bf16[2048,512]{1,0:T(8,128)(2,1)S(1)} %get-tuple-element.33.refs_6_.rest_2_, ...), custom_call_target="tpu_custom_call" | custom-call | flops 1048576000 | bytes 4194304 | tf_op jit(solution)/shard_map/factor/pallas_call | solution.py:269
  28.3 0.5 %collective-permute-done.9.proj_ref = f32[16,1024]{1,0:T(8,128)S(1)} collective-permute-done((f32[16,1024]{1,0:T(8,128)S(1)}, f32[16,1024]{1,0:T(8,128)S(1)}, u32[]{:S(2)}, u32[]{:S(2)}) %collective-permute-start.9) | collective-permute-done | bytes 65568 | tf_op jit(solution)/shard_map/ppermute | solution.py:427
  28.8 0.8 %factor.3.factor_ref = f32[16,1024]{1,0:T(8,128)S(1)} custom-call(f32[16,1024]{1,0:T(8,128)S(1)} %factor.2.before_ref, f32[16,1024]{1,0:T(8,128)S(1)} %collective-permute-done.9.proj_ref, bf16[2048,512]{1,0:T(8,128)(2,1)S(1)} %get-tuple-element.32.refs_5_.rest_0_, bf16[2048,512]{1,0:T(8,128)(2,1)S(1)} %get-tuple-element.35.refs_5_.rest_1_, ...), custom_call_target="tpu_custom_call" | custom-call | flops 1048576000 | bytes 4194304 | tf_op jit(solution)/shard_map/factor/pallas_call | solution.py:269
  29.5 0.8 %spread.2 = f32[16,1024]{1,0:T(8,128)S(1)} custom-call(f32[16,1024]{1,0:T(8,128)S(1)} %factor.3.factor_ref, bf16[1024,1024]{1,0:T(8,128)(2,1)S(1)} %get-tuple-element.37.high_ref, bf16[1024,1024]{1,0:T(8,128)(2,1)S(1)} %get-tuple-element.38.low_ref), custom_call_target="tpu_custom_call" | custom-call | flops 891289600 | bytes 4194304 | tf_op jit(solution)/shard_map/spread/pallas_call | solution.py:294
  30.3 0.2 collective-permute-start.10
  30.5 0.8 %spread.3 = f32[16,1024]{1,0:T(8,128)S(1)} custom-call(f32[16,1024]{1,0:T(8,128)S(1)} %factor.3.factor_ref, bf16[1024,1024]{1,0:T(8,128)(2,1)S(1)} %get-tuple-element.39.high_ref, bf16[1024,1024]{1,0:T(8,128)(2,1)S(1)} %get-tuple-element.40.low_ref), custom_call_target="tpu_custom_call" | custom-call | flops 891289600 | bytes 4194304 | tf_op jit(solution)/shard_map/spread/pallas_call | solution.py:294
  31.2 0.3 %collective-permute-done.10 = f32[16,1024]{1,0:T(8,128)S(1)} collective-permute-done((f32[16,1024]{1,0:T(8,128)S(1)}, f32[16,1024]{1,0:T(8,128)S(1)}, u32[]{:S(2)}, u32[]{:S(2)}) %collective-permute-start.10) | collective-permute-done | bytes 65568 | tf_op jit(solution)/shard_map/ppermute | solution.py:427
  31.6 0.6 %fusion = f32[16,1024]{1,0:T(8,128)} fusion(f32[16,1024]{1,0:T(8,128)S(1)} %spread.3, f32[16,1024]{1,0:T(8,128)S(1)} %collective-permute-done.10, f32[16,640]{1,0:T(8,128)S(1)} %get-tuple-element.34.refs_4_, f32[16,384]{1,0:T(8,128)S(1)} %get-tuple-element.31.refs_4_), kind=kLoop, calls=%fused_computation.1 | loop fusion | flops 49152 | bytes 262144 | tf_op jit(solution)/shard_map/add | solution.py:491
  (4 shorter events, 0.1 us)
Async XLA Ops:
  0.9 3.5 %collective-permute-start = (f32[16,1280]{1,0:T(8,128)S(1)}, f32[16,1280]{1,0:T(8,128)S(1)}, u32[]{:S(2)}, u32[]{:S(2)}) collective-permute-start(f32[16,1280]{1,0:T(8,128)S(1)} %get-tuple-element.23.stack_ref), channel_id=1, source_target_pairs={{1,0},{0,1},{3,2},{2,3},{5,4},{4,5},{7,6},{6,7},{9,8},{8,9},{11,10... | collective-permute-start | bytes 245768 | tf_op jit(solution)/shard_map/ppermute | solution.py:427
  1.4 13.5 %slice-start = ((s8[8388608]{0:T(1024)(128)(4,1)}), s8[4194304]{0:T(1024)(128)(4,1)S(1)}, s32[]{:S(2)}) async-start(s8[8388608]{0:T(1024)(128)(4,1)} %bitcast), calls=%async_computation | async-start | bytes 8388608
  4.4 10.5 %slice-start.1 = ((s8[8388608]{0:T(1024)(128)(4,1)}), s8[4194304]{0:T(1024)(128)(4,1)S(1)}, s32[]{:S(2)}) async-start(s8[8388608]{0:T(1024)(128)(4,1)} %bitcast), calls=%async_computation.1 | async-start | bytes 8388608
  4.5 10.4 %collective-permute-start.1 = (f32[16,1536]{1,0:T(8,128)S(1)}, f32[16,1536]{1,0:T(8,128)S(1)}, u32[]{:S(2)}, u32[]{:S(2)}) collective-permute-start(f32[16,1536]{1,0:T(8,128)S(1)} %strip.1.own_ref), channel_id=1, source_target_pairs={{0,1},{1,0},{2,4},{3,5},{4,2},{5,3},{6,8},{7,9},{8,6},{9,7},{10,12... | collective-permute-start | bytes 294920 | tf_op jit(solution)/shard_map/ppermute | solution.py:442
  4.6 10.3 %collective-permute-start.2 = (f32[16,1536]{1,0:T(8,128)S(1)}, f32[16,1536]{1,0:T(8,128)S(1)}, u32[]{:S(2)}, u32[]{:S(2)}) collective-permute-start(f32[16,1536]{1,0:T(8,128)S(1)} %strip.1.own_ref), channel_id=1, source_target_pairs={{0,2},{1,3},{2,0},{3,1},{4,6},{5,7},{6,4},{7,5},{8,10},{9,11},{10,... | collective-permute-start | bytes 294920 | tf_op jit(solution)/shard_map/ppermute | solution.py:442
  8.5 6.4 %copy-start = (s32[8,8]{1,0:T(8,128)S(1)}, s32[8,8]{1,0:T(8,128)}, u32[]{:S(2)}) copy-start(s32[8,8]{1,0:T(8,128)} %ids_ref.3) | copy-start | bytes 772
  8.5 6.4 %copy-start.1 = (s32[8]{0:T(128)S(1)}, s32[8]{0:T(128)}, u32[]{:S(2)}) copy-start(s32[8]{0:T(128)} %counts_ref.3) | copy-start | bytes 100
  11.3 6.5 %collective-permute-start.3 = (f32[16,1024]{1,0:T(8,128)S(1)}, f32[16,1024]{1,0:T(8,128)S(1)}, u32[]{:S(2)}, u32[]{:S(2)}) collective-permute-start(f32[16,1024]{1,0:T(8,128)S(1)} %get-tuple-element.30.rest_0_.refs_0_), channel_id=1, source_target_pairs={{0,6},{2,4},{4,2},{6,0},{8,14},{10,12},{12,10},{14,8},{16,22},{18,... | collective-permute-start | bytes 196616 | tf_op jit(solution)/shard_map/ppermute | solution.py:419
  12.8 5.0 %collective-permute-start.4 = (f32[16,1024]{1,0:T(8,128)S(1)}, f32[16,1024]{1,0:T(8,128)S(1)}, u32[]{:S(2)}, u32[]{:S(2)}) collective-permute-start(f32[16,1024]{1,0:T(8,128)S(1)} %get-tuple-element.30.rest_0_.refs_0_), channel_id=1, source_target_pairs={{0,4},{2,6},{4,0},{6,2},{8,12},{10,14},{12,8},{14,10},{16,20},{18,... | collective-permute-start | bytes 196616 | tf_op jit(solution)/shard_map/ppermute | solution.py:419
  13.0 4.8 %collective-permute-start.5 = (f32[16,1024]{1,0:T(8,128)S(1)}, f32[16,1024]{1,0:T(8,128)S(1)}, u32[]{:S(2)}, u32[]{:S(2)}) collective-permute-start(f32[16,1024]{1,0:T(8,128)S(1)} %get-tuple-element.30.rest_0_.refs_0_), channel_id=1, source_target_pairs={{0,2},{2,0},{4,6},{6,4},{8,10},{10,8},{12,14},{14,12},{16,18},{18,... | collective-permute-start | bytes 196616 | tf_op jit(solution)/shard_map/ppermute | solution.py:419
  17.8 8.4 %collective-permute-start.6 = (f32[16,1024]{1,0:T(8,128)S(1)}, f32[16,1024]{1,0:T(8,128)S(1)}, u32[]{:S(2)}, u32[]{:S(2)}) collective-permute-start(f32[16,1024]{1,0:T(8,128)S(1)} %add.14.rest_0_.refs_0_), channel_id=1, source_target_pairs={{0,24},{2,26},{4,28},{6,30},{8,16},{10,18},{12,20},{14,22},{16,8},... | collective-permute-start | bytes 196616 | tf_op jit(solution)/shard_map/ppermute | solution.py:419
  22.2 5.2 %collective-permute-start.7 = (f32[16,1024]{1,0:T(8,128)S(1)}, f32[16,1024]{1,0:T(8,128)S(1)}, u32[]{:S(2)}, u32[]{:S(2)}) collective-permute-start(f32[16,1024]{1,0:T(8,128)S(1)} %add.14.rest_0_.refs_0_), channel_id=1, source_target_pairs={{0,16},{2,18},{4,20},{6,22},{8,24},{10,26},{12,28},{14,30},{16,0},... | collective-permute-start | bytes 196616 | tf_op jit(solution)/shard_map/ppermute | solution.py:419
  22.2 5.2 %collective-permute-start.8 = (f32[16,1024]{1,0:T(8,128)S(1)}, f32[16,1024]{1,0:T(8,128)S(1)}, u32[]{:S(2)}, u32[]{:S(2)}) collective-permute-start(f32[16,1024]{1,0:T(8,128)S(1)} %add.14.rest_0_.refs_0_), channel_id=1, source_target_pairs={{0,8},{2,10},{4,12},{6,14},{8,0},{10,2},{12,4},{14,6},{16,24},{18,... | collective-permute-start | bytes 196616 | tf_op jit(solution)/shard_map/ppermute | solution.py:419
  27.4 1.3 %collective-permute-start.9 = (f32[16,1024]{1,0:T(8,128)S(1)}, f32[16,1024]{1,0:T(8,128)S(1)}, u32[]{:S(2)}, u32[]{:S(2)}) collective-permute-start(f32[16,1024]{1,0:T(8,128)S(1)} %add.15.proj_ref), channel_id=1, source_target_pairs={{1,0},{0,1},{3,2},{2,3},{5,4},{4,5},{7,6},{6,7},{9,8},{8,9},{11,10... | collective-permute-start | bytes 196616 | tf_op jit(solution)/shard_map/ppermute | solution.py:427
  30.3 1.3 %collective-permute-start.10 = (f32[16,1024]{1,0:T(8,128)S(1)}, f32[16,1024]{1,0:T(8,128)S(1)}, u32[]{:S(2)}, u32[]{:S(2)}) collective-permute-start(f32[16,1024]{1,0:T(8,128)S(1)} %spread.2), channel_id=1, source_target_pairs={{1,0},{0,1},{3,2},{2,3},{5,4},{4,5},{7,6},{6,7},{9,8},{8,9},{11,10... | collective-permute-start | bytes 196616 | tf_op jit(solution)/shard_map/ppermute | solution.py:427

commit v25 on v24

--- a/solution.py
+++ b/solution.py
@@ -53,11 +53,6 @@
     return jnp.dot(left, right, preferred_element_type=jnp.float32)
 
 
-def padded_halves(x, rows):
-    fill = jnp.zeros((rows - 2 * x.shape[0], x.shape[1]), jnp.bfloat16)
-    return jnp.concatenate([*halves(x), fill], axis=0)
-
-
 def folded_columns(x, rows):
     x = jnp.transpose(x)
     return x[:rows] + x[rows : 2 * rows]
@@ -191,7 +186,7 @@
     knots, points = high_ref.shape
     probes = stack_ref.shape[0]
     tile = min(TILE, knots)
-    weights[...] = padded_halves(stack_ref[:, :points], weights.shape[0])
+    weights[...] = stacked_halves(stack_ref[:, :points])
     east, north = [on_grid(coordinate_rows(stack_ref, points, axis) * scale, grain) for axis in range(2)]
 
     for start in range(0, knots, tile):
@@ -228,7 +223,7 @@
         out_shape=out_shape,
         in_specs=[VMEM] * len(operands),
         out_specs=[VMEM] * len(out_shape),
-        scratch_shapes=[pltpu.VMEM((LANES, points), jnp.bfloat16)],
+        scratch_shapes=[pltpu.VMEM((2 * probes, points), jnp.bfloat16)],
         compiler_params=pltpu.CompilerParams(vmem_limit_bytes=LIMIT),
         cost_estimate=cost(2800, points * knots, 2),
         name="project",

time: 32.4 us -> 32.4 us (level)
  no operation moved by 1% of the time
where the time goes in v25:
time: 32.4 us; the launch traced here: 32.2 us
  Pallas kernels  16 us (49%)
  starting transfers between devices  13.4 us (41%)
  waiting for transfers between devices  1.99 us (6%)
  other arithmetic  0.65 us (2%)
    ppermute x6, starting transfers between devices, butterfly_round(): lax.ppermute(value, axis, [(i, i ^ step) for i in range(count)])  8.54 us
    pallas_call x2, Pallas kernels, beside_round(): pl.pallas_call(functools.partial(beside_kernel, first, first_row, grain_o...  6.2 us
    pallas_call x2, Pallas kernels, project(): pl.pallas_call(functools.partial(project_kernel, scale, grain_of(scale *...  5.79 us
    ppermute x2, starting transfers between devices, paired(): return lax.ppermute(value, (axis, other), pairs)  4.07 us
    pallas_call x2, Pallas kernels, spread(): pl.pallas_call(functools.partial(spread_kernel, scale), out_shape=jax.Sha...  1.53 us
    pallas_call x2, Pallas kernels, factored(): pl.pallas_call(kernel, out_shape=jax.ShapeDtypeStruct((probes, rows), jnp...  1.53 us
    ppermute x6, waiting for transfers between devices, butterfly_round(): lax.ppermute(value, axis, [(i, i ^ step) for i in range(count)])  1.17 us
    pallas_call x1, Pallas kernels, prepare(): pl.pallas_call(functools.partial(prepare_kernel, blocks), out_shape=(jax....  0.87 us
  transfers between devices with their start and end apart: 11, of which 3 were waited for; matrix products, arithmetic and copies ran while one was open for 0% of the time, Pallas kernels for 42%

profile of v25, /device:TPU:0, one launch (start us, length us, event | category | flops | bytes accessed | tf_op | source)
XLA Modules:
  0.0 32.2 jit_solution(4436418449745461825)
XLA Ops:
  0.0 0.9 %prepare.1 = (f32[16,1280]{1,0:T(8,128)S(1)}, f32[2,1024]{1,0:T(2,128)S(1)}) custom-call(f32[16,1024]{1,0:T(8,128)} %probes_ref.1, f32[2,1024]{1,0:T(2,128)} %locations_ref.1, f32[2,1024]{1,0:T(2,128)} %knots_ref.1), custom_call_target="tpu_custom_call" | custom-call | tf_op jit(solution)/shard_map/prepare/pallas_call | solution.py:95
  0.9 0.5 %collective-permute-start = (f32[16,1280]{1,0:T(8,128)S(1)}, f32[16,1280]{1,0:T(8,128)S(1)}, u32[]{:S(2)}, u32[]{:S(2)}) collective-permute-start(f32[16,1280]{1,0:T(8,128)S(1)} %get-tuple-element.23.stack_ref), channel_id=1, source_target_pairs={{1,0},{0,1},{3,2},{2,3},{5,4},{4,5},{7,6},{6,7},{9,8},{8,9},{11,10... | collective-permute-start | bytes 245768 | tf_op jit(solution)/shard_map/ppermute | solution.py:422
  1.4 0.0 slice-start
  1.4 3.0 %project.2 = (f32[16,1024]{1,0:T(8,128)S(1)}, bf16[1024,1024]{1,0:T(8,128)(2,1)S(1)}, bf16[1024,1024]{1,0:T(8,128)(2,1)S(1)}, f32[1024,8]{1,0:T(8,128)S(1)}, f32[16,1280]{1,0:T(8,128)S(1)}) custom-call(f32[16,1280]{1,0:T(8,128)S(1)} %get-tuple-element.23.stack_ref, f32[2,1024]{1,0:T(2,128)S(1)} %get-tuple-element.24.rest_0_), custom_call_target="tpu_custom_call" | custom-call | flops 2936012800 | bytes 4194304 | tf_op jit(solution)/shard_map/project/pallas_call | solution.py:221
  4.4 0.0 collective-permute-done.below_ref.above_ref.stack_ref
  4.4 0.0 slice-start.1
  4.5 0.1 collective-permute-start.1
  4.6 3.9 %collective-permute-start.2 = (f32[16,1536]{1,0:T(8,128)S(1)}, f32[16,1536]{1,0:T(8,128)S(1)}, u32[]{:S(2)}, u32[]{:S(2)}) collective-permute-start(f32[16,1536]{1,0:T(8,128)S(1)} %strip.1.own_ref), channel_id=1, source_target_pairs={{0,2},{1,3},{2,0},{3,1},{4,6},{5,7},{6,4},{7,5},{8,10},{9,11},{10,... | collective-permute-start | bytes 294920 | tf_op jit(solution)/shard_map/ppermute | solution.py:437
  8.5 0.0 copy-start
  8.5 0.0 copy-start.1
  8.5 2.8 %project.3 = (f32[16,1024]{1,0:T(8,128)S(1)}, bf16[1024,1024]{1,0:T(8,128)(2,1)S(1)}, bf16[1024,1024]{1,0:T(8,128)(2,1)S(1)}) custom-call(f32[16,1280]{1,0:T(8,128)S(1)} %collective-permute-done.below_ref.above_ref.stack_ref, f32[16,1024]{1,0:T(8,128)S(1)} %get-tuple-element.28.rest_0_, f32[1024,8]{1,0:T(8,128)S(1)} %get-tuple-element.29.rest_1_), custom_call_target="tpu_custom_call" | custom-call | flops 2936012800 | bytes 4194304 | tf_op jit(solution)/shard_map/project/pallas_call | solution.py:221
  11.3 1.5 %collective-permute-start.3 = (f32[16,1024]{1,0:T(8,128)S(1)}, f32[16,1024]{1,0:T(8,128)S(1)}, u32[]{:S(2)}, u32[]{:S(2)}) collective-permute-start(f32[16,1024]{1,0:T(8,128)S(1)} %get-tuple-element.30.rest_0_.refs_0_), channel_id=1, source_target_pairs={{0,6},{2,4},{4,2},{6,0},{8,14},{10,12},{12,10},{14,8},{16,22},{18,... | collective-permute-start | bytes 196616 | tf_op jit(solution)/shard_map/ppermute | solution.py:414
  12.8 0.2 collective-permute-start.4
  13.0 1.9 %collective-permute-start.5 = (f32[16,1024]{1,0:T(8,128)S(1)}, f32[16,1024]{1,0:T(8,128)S(1)}, u32[]{:S(2)}, u32[]{:S(2)}) collective-permute-start(f32[16,1024]{1,0:T(8,128)S(1)} %get-tuple-element.30.rest_0_.refs_0_), channel_id=1, source_target_pairs={{0,2},{2,0},{4,6},{6,4},{8,10},{10,8},{12,14},{14,12},{16,18},{18,... | collective-permute-start | bytes 196616 | tf_op jit(solution)/shard_map/ppermute | solution.py:414
  14.9 0.0 collective-permute-done.1.odd_ref
  14.9 0.0 collective-permute-done.2.even_ref
  14.9 0.1 assemble.1
  14.9 0.0 slice-done
  14.9 0.0 slice-done.1
  15.0 0.0 copy-done
  15.0 0.0 copy-done.1
  15.0 2.8 %beside.2 = (f32[16,384]{1,0:T(8,128)S(1)}, bf16[2048,512]{1,0:T(8,128)(2,1)S(1)}, bf16[2048,512]{1,0:T(8,128)(2,1)S(1)}) custom-call(s32[8,8]{1,0:T(8,128)S(1)} %copy-done, s32[8]{0:T(128)S(1)} %copy-done.1, f32[16,1280]{1,0:T(8,128)S(1)} %get-tuple-element.25.own_ref, bf16[32,3968]{1,0:T(8,128)(2,1)S(1)} %get-tuple-element.26.values_ref, ...), custom_call_target="tpu_custom_call" | custom-call | flops 196608000 | bytes 1572864 | tf_op jit(solution)/shard_map/beside/pallas_call | solution.py:371
  17.8 0.0 collective-permute-done.3.refs_1_
  17.8 0.0 collective-permute-done.4.refs_2_
  17.8 0.0 collective-permute-done.5.refs_3_
  17.8 4.3 %collective-permute-start.6 = (f32[16,1024]{1,0:T(8,128)S(1)}, f32[16,1024]{1,0:T(8,128)S(1)}, u32[]{:S(2)}, u32[]{:S(2)}) collective-permute-start(f32[16,1024]{1,0:T(8,128)S(1)} %add.14.rest_0_.refs_0_), channel_id=1, source_target_pairs={{0,24},{2,26},{4,28},{6,30},{8,16},{10,18},{12,20},{14,22},{16,8},... | collective-permute-start | bytes 196616 | tf_op jit(solution)/shard_map/ppermute | solution.py:414
  22.2 0.0 collective-permute-start.7
  22.2 0.6 %collective-permute-start.8 = (f32[16,1024]{1,0:T(8,128)S(1)}, f32[16,1024]{1,0:T(8,128)S(1)}, u32[]{:S(2)}, u32[]{:S(2)}) collective-permute-start(f32[16,1024]{1,0:T(8,128)S(1)} %add.14.rest_0_.refs_0_), channel_id=1, source_target_pairs={{0,8},{2,10},{4,12},{6,14},{8,0},{10,2},{12,4},{14,6},{16,24},{18,... | collective-permute-start | bytes 196616 | tf_op jit(solution)/shard_map/ppermute | solution.py:414
  22.8 3.4 %beside.3 = (f32[16,640]{1,0:T(8,128)S(1)}, bf16[2048,512]{1,0:T(8,128)(2,1)S(1)}, bf16[2048,512]{1,0:T(8,128)(2,1)S(1)}) custom-call(s32[8,8]{1,0:T(8,128)S(1)} %copy-done, s32[8]{0:T(128)S(1)} %copy-done.1, f32[16,1280]{1,0:T(8,128)S(1)} %get-tuple-element.25.own_ref, bf16[32,3968]{1,0:T(8,128)(2,1)S(1)} %get-tuple-element.26.values_ref, ...), custom_call_target="tpu_custom_call" | custom-call | flops 327680000 | bytes 2621440 | tf_op jit(solution)/shard_map/beside/pallas_call | solution.py:371
  26.2 0.0 collective-permute-done.6.refs_1_
  26.3 1.2 %collective-permute-done.7.refs_2_ = f32[16,1024]{1,0:T(8,128)S(1)} collective-permute-done((f32[16,1024]{1,0:T(8,128)S(1)}, f32[16,1024]{1,0:T(8,128)S(1)}, u32[]{:S(2)}, u32[]{:S(2)}) %collective-permute-start.7) | collective-permute-done | bytes 65568 | tf_op jit(solution)/shard_map/ppermute | solution.py:414
  27.4 0.0 collective-permute-done.8.refs_3_
  27.4 0.1 collective-permute-start.9
  27.5 0.8 %factor.2.before_ref = f32[16,1024]{1,0:T(8,128)S(1)} custom-call(f32[16,1024]{1,0:T(8,128)S(1)} %add.15.proj_ref, bf16[2048,512]{1,0:T(8,128)(2,1)S(1)} %get-tuple-element.32.refs_5_.rest_0_, bf16[2048,512]{1,0:T(8,128)(2,1)S(1)} %get-tuple-element.35.refs_5_.rest_1_, bf16[2048,512]{1,0:T(8,128)(2,1)S(1)} %get-tuple-element.33.refs_6_.rest_2_, ...), custom_call_target="tpu_custom_call" | custom-call | flops 1048576000 | bytes 4194304 | tf_op jit(solution)/shard_map/factor/pallas_call | solution.py:264
  28.3 0.5 %collective-permute-done.9.proj_ref = f32[16,1024]{1,0:T(8,128)S(1)} collective-permute-done((f32[16,1024]{1,0:T(8,128)S(1)}, f32[16,1024]{1,0:T(8,128)S(1)}, u32[]{:S(2)}, u32[]{:S(2)}) %collective-permute-start.9) | collective-permute-done | bytes 65568 | tf_op jit(solution)/shard_map/ppermute | solution.py:422
  28.8 0.8 %factor.3.factor_ref = f32[16,1024]{1,0:T(8,128)S(1)} custom-call(f32[16,1024]{1,0:T(8,128)S(1)} %factor.2.before_ref, f32[16,1024]{1,0:T(8,128)S(1)} %collective-permute-done.9.proj_ref, bf16[2048,512]{1,0:T(8,128)(2,1)S(1)} %get-tuple-element.32.refs_5_.rest_0_, bf16[2048,512]{1,0:T(8,128)(2,1)S(1)} %get-tuple-element.35.refs_5_.rest_1_, ...), custom_call_target="tpu_custom_call" | custom-call | flops 1048576000 | bytes 4194304 | tf_op jit(solution)/shard_map/factor/pallas_call | solution.py:264
  29.5 0.8 %spread.2 = f32[16,1024]{1,0:T(8,128)S(1)} custom-call(f32[16,1024]{1,0:T(8,128)S(1)} %factor.3.factor_ref, bf16[1024,1024]{1,0:T(8,128)(2,1)S(1)} %get-tuple-element.37.high_ref, bf16[1024,1024]{1,0:T(8,128)(2,1)S(1)} %get-tuple-element.38.low_ref), custom_call_target="tpu_custom_call" | custom-call | flops 891289600 | bytes 4194304 | tf_op jit(solution)/shard_map/spread/pallas_call | solution.py:289
  30.3 0.2 collective-permute-start.10
  30.5 0.8 %spread.3 = f32[16,1024]{1,0:T(8,128)S(1)} custom-call(f32[16,1024]{1,0:T(8,128)S(1)} %factor.3.factor_ref, bf16[1024,1024]{1,0:T(8,128)(2,1)S(1)} %get-tuple-element.39.high_ref, bf16[1024,1024]{1,0:T(8,128)(2,1)S(1)} %get-tuple-element.40.low_ref), custom_call_target="tpu_custom_call" | custom-call | flops 891289600 | bytes 4194304 | tf_op jit(solution)/shard_map/spread/pallas_call | solution.py:289
  31.2 0.3 %collective-permute-done.10 = f32[16,1024]{1,0:T(8,128)S(1)} collective-permute-done((f32[16,1024]{1,0:T(8,128)S(1)}, f32[16,1024]{1,0:T(8,128)S(1)}, u32[]{:S(2)}, u32[]{:S(2)}) %collective-permute-start.10) | collective-permute-done | bytes 65568 | tf_op jit(solution)/shard_map/ppermute | solution.py:422
  31.6 0.6 %fusion = f32[16,1024]{1,0:T(8,128)} fusion(f32[16,1024]{1,0:T(8,128)S(1)} %spread.3, f32[16,1024]{1,0:T(8,128)S(1)} %collective-permute-done.10, f32[16,640]{1,0:T(8,128)S(1)} %get-tuple-element.34.refs_4_, f32[16,384]{1,0:T(8,128)S(1)} %get-tuple-element.31.refs_4_), kind=kLoop, calls=%fused_computation.1 | loop fusion | flops 49152 | bytes 262144 | tf_op jit(solution)/shard_map/add | solution.py:486
  (4 shorter events, 0.1 us)
Async XLA Ops:
  0.9 3.5 %collective-permute-start = (f32[16,1280]{1,0:T(8,128)S(1)}, f32[16,1280]{1,0:T(8,128)S(1)}, u32[]{:S(2)}, u32[]{:S(2)}) collective-permute-start(f32[16,1280]{1,0:T(8,128)S(1)} %get-tuple-element.23.stack_ref), channel_id=1, source_target_pairs={{1,0},{0,1},{3,2},{2,3},{5,4},{4,5},{7,6},{6,7},{9,8},{8,9},{11,10... | collective-permute-start | bytes 245768 | tf_op jit(solution)/shard_map/ppermute | solution.py:422
  1.4 13.5 %slice-start = ((s8[8388608]{0:T(1024)(128)(4,1)}), s8[4194304]{0:T(1024)(128)(4,1)S(1)}, s32[]{:S(2)}) async-start(s8[8388608]{0:T(1024)(128)(4,1)} %bitcast), calls=%async_computation | async-start | bytes 8388608
  4.4 10.5 %slice-start.1 = ((s8[8388608]{0:T(1024)(128)(4,1)}), s8[4194304]{0:T(1024)(128)(4,1)S(1)}, s32[]{:S(2)}) async-start(s8[8388608]{0:T(1024)(128)(4,1)} %bitcast), calls=%async_computation.1 | async-start | bytes 8388608
  4.5 10.4 %collective-permute-start.1 = (f32[16,1536]{1,0:T(8,128)S(1)}, f32[16,1536]{1,0:T(8,128)S(1)}, u32[]{:S(2)}, u32[]{:S(2)}) collective-permute-start(f32[16,1536]{1,0:T(8,128)S(1)} %strip.1.own_ref), channel_id=1, source_target_pairs={{0,1},{1,0},{2,4},{3,5},{4,2},{5,3},{6,8},{7,9},{8,6},{9,7},{10,12... | collective-permute-start | bytes 294920 | tf_op jit(solution)/shard_map/ppermute | solution.py:437
  4.6 10.3 %collective-permute-start.2 = (f32[16,1536]{1,0:T(8,128)S(1)}, f32[16,1536]{1,0:T(8,128)S(1)}, u32[]{:S(2)}, u32[]{:S(2)}) collective-permute-start(f32[16,1536]{1,0:T(8,128)S(1)} %strip.1.own_ref), channel_id=1, source_target_pairs={{0,2},{1,3},{2,0},{3,1},{4,6},{5,7},{6,4},{7,5},{8,10},{9,11},{10,... | collective-permute-start | bytes 294920 | tf_op jit(solution)/shard_map/ppermute | solution.py:437
  8.5 6.4 %copy-start = (s32[8,8]{1,0:T(8,128)S(1)}, s32[8,8]{1,0:T(8,128)}, u32[]{:S(2)}) copy-start(s32[8,8]{1,0:T(8,128)} %ids_ref.3) | copy-start | bytes 772
  8.5 6.4 %copy-start.1 = (s32[8]{0:T(128)S(1)}, s32[8]{0:T(128)}, u32[]{:S(2)}) copy-start(s32[8]{0:T(128)} %counts_ref.3) | copy-start | bytes 100
  11.3 6.5 %collective-permute-start.3 = (f32[16,1024]{1,0:T(8,128)S(1)}, f32[16,1024]{1,0:T(8,128)S(1)}, u32[]{:S(2)}, u32[]{:S(2)}) collective-permute-start(f32[16,1024]{1,0:T(8,128)S(1)} %get-tuple-element.30.rest_0_.refs_0_), channel_id=1, source_target_pairs={{0,6},{2,4},{4,2},{6,0},{8,14},{10,12},{12,10},{14,8},{16,22},{18,... | collective-permute-start | bytes 196616 | tf_op jit(solution)/shard_map/ppermute | solution.py:414
  12.8 5.0 %collective-permute-start.4 = (f32[16,1024]{1,0:T(8,128)S(1)}, f32[16,1024]{1,0:T(8,128)S(1)}, u32[]{:S(2)}, u32[]{:S(2)}) collective-permute-start(f32[16,1024]{1,0:T(8,128)S(1)} %get-tuple-element.30.rest_0_.refs_0_), channel_id=1, source_target_pairs={{0,4},{2,6},{4,0},{6,2},{8,12},{10,14},{12,8},{14,10},{16,20},{18,... | collective-permute-start | bytes 196616 | tf_op jit(solution)/shard_map/ppermute | solution.py:414
  13.0 4.8 %collective-permute-start.5 = (f32[16,1024]{1,0:T(8,128)S(1)}, f32[16,1024]{1,0:T(8,128)S(1)}, u32[]{:S(2)}, u32[]{:S(2)}) collective-permute-start(f32[16,1024]{1,0:T(8,128)S(1)} %get-tuple-element.30.rest_0_.refs_0_), channel_id=1, source_target_pairs={{0,2},{2,0},{4,6},{6,4},{8,10},{10,8},{12,14},{14,12},{16,18},{18,... | collective-permute-start | bytes 196616 | tf_op jit(solution)/shard_map/ppermute | solution.py:414
  17.8 8.4 %collective-permute-start.6 = (f32[16,1024]{1,0:T(8,128)S(1)}, f32[16,1024]{1,0:T(8,128)S(1)}, u32[]{:S(2)}, u32[]{:S(2)}) collective-permute-start(f32[16,1024]{1,0:T(8,128)S(1)} %add.14.rest_0_.refs_0_), channel_id=1, source_target_pairs={{0,24},{2,26},{4,28},{6,30},{8,16},{10,18},{12,20},{14,22},{16,8},... | collective-permute-start | bytes 196616 | tf_op jit(solution)/shard_map/ppermute | solution.py:414
  22.2 5.2 %collective-permute-start.7 = (f32[16,1024]{1,0:T(8,128)S(1)}, f32[16,1024]{1,0:T(8,128)S(1)}, u32[]{:S(2)}, u32[]{:S(2)}) collective-permute-start(f32[16,1024]{1,0:T(8,128)S(1)} %add.14.rest_0_.refs_0_), channel_id=1, source_target_pairs={{0,16},{2,18},{4,20},{6,22},{8,24},{10,26},{12,28},{14,30},{16,0},... | collective-permute-start | bytes 196616 | tf_op jit(solution)/shard_map/ppermute | solution.py:414
  22.2 5.2 %collective-permute-start.8 = (f32[16,1024]{1,0:T(8,128)S(1)}, f32[16,1024]{1,0:T(8,128)S(1)}, u32[]{:S(2)}, u32[]{:S(2)}) collective-permute-start(f32[16,1024]{1,0:T(8,128)S(1)} %add.14.rest_0_.refs_0_), channel_id=1, source_target_pairs={{0,8},{2,10},{4,12},{6,14},{8,0},{10,2},{12,4},{14,6},{16,24},{18,... | collective-permute-start | bytes 196616 | tf_op jit(solution)/shard_map/ppermute | solution.py:414
  27.4 1.3 %collective-permute-start.9 = (f32[16,1024]{1,0:T(8,128)S(1)}, f32[16,1024]{1,0:T(8,128)S(1)}, u32[]{:S(2)}, u32[]{:S(2)}) collective-permute-start(f32[16,1024]{1,0:T(8,128)S(1)} %add.15.proj_ref), channel_id=1, source_target_pairs={{1,0},{0,1},{3,2},{2,3},{5,4},{4,5},{7,6},{6,7},{9,8},{8,9},{11,10... | collective-permute-start | bytes 196616 | tf_op jit(solution)/shard_map/ppermute | solution.py:422
  30.3 1.3 %collective-permute-start.10 = (f32[16,1024]{1,0:T(8,128)S(1)}, f32[16,1024]{1,0:T(8,128)S(1)}, u32[]{:S(2)}, u32[]{:S(2)}) collective-permute-start(f32[16,1024]{1,0:T(8,128)S(1)} %spread.2), channel_id=1, source_target_pairs={{1,0},{0,1},{3,2},{2,3},{5,4},{4,5},{7,6},{6,7},{9,8},{8,9},{11,10... | collective-permute-start | bytes 196616 | tf_op jit(solution)/shard_map/ppermute | solution.py:422

commit v26 on v25

--- a/solution.py
+++ b/solution.py
@@ -405,7 +405,7 @@
     assert count & (count - 1) == 0
     bits = [1 << i for i in range(count.bit_length() - 1)]
     rounds = [(low | high, high, low) for low, high in zip(bits[0::2], bits[1::2])]
-    return rounds + [(bit,) for bit in bits[len(rounds) * 2 :]]
+    return [(bit,) for bit in bits[len(rounds) * 2 :]] + rounds[::-1]
 
 
 def butterfly_round(value, axis, turn):
@@ -461,7 +461,7 @@
     projection = parts[-1][0]
     rounds = len(butterfly_rounds(lax.axis_size("space")))
     pieces = math.gcd(math.gcd(own_blocks, rounds), knot_precision.shape[0] // LANES)
-    bounds = [own_blocks * i * (i + 2) // (pieces * (pieces + 2)) for i in range(pieces + 1)]
+    bounds = [own_blocks - own_blocks * i * (i + 2) // (pieces * (pieces + 2)) for i in range(pieces, -1, -1)]
     per_split = knot_precision.shape[0] // pieces
     base, splits = [], []
     for turn in range(rounds):

time: 32.4 us -> 32.8 us (1.012)
  waiting for transfers between devices: 1.99 us -> 2.99 us
  starting transfers between devices: 13.4 us -> 12.8 us
    ppermute x6, waiting for transfers between devices: 1.17 us -> 2.17 us  [butterfly_round(): lax.ppermute(value, axis, [(i, i ^ step) for i in range(count)])]
    ppermute x6, starting transfers between devices: 8.54 us -> 8 us  [butterfly_round(): lax.ppermute(value, axis, [(i, i ^ step) for i in range(count)])]
  transfers between devices with their start and end apart: 11 -> 11, of which waited for: 3 -> 4; matrix products, arithmetic and copies ran while one was open for 0% -> 0% of each run, Pallas kernels for 42% -> 42%
where the time goes in v26:
time: 32.8 us; the launch traced here: 32.7 us
  Pallas kernels  16 us (49%)
  starting transfers between devices  12.8 us (39%)
  waiting for transfers between devices  2.99 us (9%)
  other arithmetic  0.65 us (2%)
    ppermute x6, starting transfers between devices, butterfly_round(): lax.ppermute(value, axis, [(i, i ^ step) for i in range(count)])  8 us
    pallas_call x2, Pallas kernels, beside_round(): pl.pallas_call(functools.partial(beside_kernel, first, first_row, grain_o...  6.2 us
    pallas_call x2, Pallas kernels, project(): pl.pallas_call(functools.partial(project_kernel, scale, grain_of(scale *...  5.79 us
    ppermute x2, starting transfers between devices, paired(): return lax.ppermute(value, (axis, other), pairs)  4.07 us
    ppermute x6, waiting for transfers between devices, butterfly_round(): lax.ppermute(value, axis, [(i, i ^ step) for i in range(count)])  2.17 us
    pallas_call x2, Pallas kernels, spread(): pl.pallas_call(functools.partial(spread_kernel, scale), out_shape=jax.Sha...  1.53 us
    pallas_call x2, Pallas kernels, factored(): pl.pallas_call(kernel, out_shape=jax.ShapeDtypeStruct((probes, rows), jnp...  1.53 us
    pallas_call x1, Pallas kernels, prepare(): pl.pallas_call(functools.partial(prepare_kernel, blocks), out_shape=(jax....  0.87 us
  transfers between devices with their start and end apart: 11, of which 4 were waited for; matrix products, arithmetic and copies ran while one was open for 0% of the time, Pallas kernels for 42%

profile of v26, /device:TPU:0, one launch (start us, length us, event | category | flops | bytes accessed | tf_op | source)
XLA Modules:
  0.0 32.7 jit_solution(3784452146748430567)
XLA Ops:
  0.0 0.9 %prepare.1 = (f32[16,1280]{1,0:T(8,128)S(1)}, f32[2,1024]{1,0:T(2,128)S(1)}) custom-call(f32[16,1024]{1,0:T(8,128)} %probes_ref.1, f32[2,1024]{1,0:T(2,128)} %locations_ref.1, f32[2,1024]{1,0:T(2,128)} %knots_ref.1), custom_call_target="tpu_custom_call" | custom-call | tf_op jit(solution)/shard_map/prepare/pallas_call | solution.py:95
  0.9 0.5 %collective-permute-start = (f32[16,1280]{1,0:T(8,128)S(1)}, f32[16,1280]{1,0:T(8,128)S(1)}, u32[]{:S(2)}, u32[]{:S(2)}) collective-permute-start(f32[16,1280]{1,0:T(8,128)S(1)} %get-tuple-element.23.stack_ref), channel_id=1, source_target_pairs={{1,0},{0,1},{3,2},{2,3},{5,4},{4,5},{7,6},{6,7},{9,8},{8,9},{11,10... | collective-permute-start | bytes 245768 | tf_op jit(solution)/shard_map/ppermute | solution.py:422
  1.4 0.0 slice-start
  1.4 3.0 %project.2 = (f32[16,1024]{1,0:T(8,128)S(1)}, bf16[1024,1024]{1,0:T(8,128)(2,1)S(1)}, bf16[1024,1024]{1,0:T(8,128)(2,1)S(1)}, f32[1024,8]{1,0:T(8,128)S(1)}, f32[16,1280]{1,0:T(8,128)S(1)}) custom-call(f32[16,1280]{1,0:T(8,128)S(1)} %get-tuple-element.23.stack_ref, f32[2,1024]{1,0:T(2,128)S(1)} %get-tuple-element.24.rest_0_), custom_call_target="tpu_custom_call" | custom-call | flops 2936012800 | bytes 4194304 | tf_op jit(solution)/shard_map/project/pallas_call | solution.py:221
  4.4 0.0 collective-permute-done.below_ref.above_ref.stack_ref
  4.4 0.0 slice-start.1
  4.5 0.1 collective-permute-start.1
  4.6 3.9 %collective-permute-start.2 = (f32[16,1536]{1,0:T(8,128)S(1)}, f32[16,1536]{1,0:T(8,128)S(1)}, u32[]{:S(2)}, u32[]{:S(2)}) collective-permute-start(f32[16,1536]{1,0:T(8,128)S(1)} %strip.1.own_ref), channel_id=1, source_target_pairs={{0,2},{1,3},{2,0},{3,1},{4,6},{5,7},{6,4},{7,5},{8,10},{9,11},{10,... | collective-permute-start | bytes 294920 | tf_op jit(solution)/shard_map/ppermute | solution.py:437
  8.5 0.0 copy-start
  8.5 0.0 copy-start.1
  8.5 2.8 %project.3 = (f32[16,1024]{1,0:T(8,128)S(1)}, bf16[1024,1024]{1,0:T(8,128)(2,1)S(1)}, bf16[1024,1024]{1,0:T(8,128)(2,1)S(1)}) custom-call(f32[16,1280]{1,0:T(8,128)S(1)} %collective-permute-done.below_ref.above_ref.stack_ref, f32[16,1024]{1,0:T(8,128)S(1)} %get-tuple-element.28.rest_0_, f32[1024,8]{1,0:T(8,128)S(1)} %get-tuple-element.29.rest_1_), custom_call_target="tpu_custom_call" | custom-call | flops 2936012800 | bytes 4194304 | tf_op jit(solution)/shard_map/project/pallas_call | solution.py:221
  11.3 3.7 %collective-permute-start.3 = (f32[16,1024]{1,0:T(8,128)S(1)}, f32[16,1024]{1,0:T(8,128)S(1)}, u32[]{:S(2)}, u32[]{:S(2)}) collective-permute-start(f32[16,1024]{1,0:T(8,128)S(1)} %get-tuple-element.30.rest_0_.refs_0_), channel_id=1, source_target_pairs={{0,24},{2,26},{4,28},{6,30},{8,16},{10,18},{12,20},{14,22},{16,8},... | collective-permute-start | bytes 196616 | tf_op jit(solution)/shard_map/ppermute | solution.py:414
  15.0 0.0 collective-permute-start.4
  15.0 0.8 %collective-permute-start.5 = (f32[16,1024]{1,0:T(8,128)S(1)}, f32[16,1024]{1,0:T(8,128)S(1)}, u32[]{:S(2)}, u32[]{:S(2)}) collective-permute-start(f32[16,1024]{1,0:T(8,128)S(1)} %get-tuple-element.30.rest_0_.refs_0_), channel_id=1, source_target_pairs={{0,8},{2,10},{4,12},{6,14},{8,0},{10,2},{12,4},{14,6},{16,24},{18,... | collective-permute-start | bytes 196616 | tf_op jit(solution)/shard_map/ppermute | solution.py:414
  15.8 0.0 collective-permute-done.1.odd_ref
  15.8 0.0 collective-permute-done.2.even_ref
  15.8 0.1 assemble.1
  15.8 0.0 slice-done
  15.8 0.0 slice-done.1
  15.9 0.0 copy-done
  15.9 0.0 copy-done.1
  15.9 3.4 %beside.2 = (f32[16,640]{1,0:T(8,128)S(1)}, bf16[2048,512]{1,0:T(8,128)(2,1)S(1)}, bf16[2048,512]{1,0:T(8,128)(2,1)S(1)}) custom-call(s32[8,8]{1,0:T(8,128)S(1)} %copy-done, s32[8]{0:T(128)S(1)} %copy-done.1, f32[16,1280]{1,0:T(8,128)S(1)} %get-tuple-element.25.own_ref, bf16[32,3968]{1,0:T(8,128)(2,1)S(1)} %get-tuple-element.26.values_ref, ...), custom_call_target="tpu_custom_call" | custom-call | flops 327680000 | bytes 2621440 | tf_op jit(solution)/shard_map/beside/pallas_call | solution.py:371
  19.3 0.0 collective-permute-done.3.refs_1_
  19.3 1.3 %collective-permute-done.4.refs_2_ = f32[16,1024]{1,0:T(8,128)S(1)} collective-permute-done((f32[16,1024]{1,0:T(8,128)S(1)}, f32[16,1024]{1,0:T(8,128)S(1)}, u32[]{:S(2)}, u32[]{:S(2)}) %collective-permute-start.4) | collective-permute-done | bytes 65568 | tf_op jit(solution)/shard_map/ppermute | solution.py:414
  20.7 0.0 collective-permute-done.5.refs_3_
  20.7 1.5 %collective-permute-start.6 = (f32[16,1024]{1,0:T(8,128)S(1)}, f32[16,1024]{1,0:T(8,128)S(1)}, u32[]{:S(2)}, u32[]{:S(2)}) collective-permute-start(f32[16,1024]{1,0:T(8,128)S(1)} %add.14.rest_0_.refs_0_), channel_id=1, source_target_pairs={{0,6},{2,4},{4,2},{6,0},{8,14},{10,12},{12,10},{14,8},{16,22},{18,... | collective-permute-start | bytes 196616 | tf_op jit(solution)/shard_map/ppermute | solution.py:414
  22.2 1.4 %collective-permute-start.7 = (f32[16,1024]{1,0:T(8,128)S(1)}, f32[16,1024]{1,0:T(8,128)S(1)}, u32[]{:S(2)}, u32[]{:S(2)}) collective-permute-start(f32[16,1024]{1,0:T(8,128)S(1)} %add.14.rest_0_.refs_0_), channel_id=1, source_target_pairs={{0,4},{2,6},{4,0},{6,2},{8,12},{10,14},{12,8},{14,10},{16,20},{18,... | collective-permute-start | bytes 196616 | tf_op jit(solution)/shard_map/ppermute | solution.py:414
  23.6 0.7 %collective-permute-start.8 = (f32[16,1024]{1,0:T(8,128)S(1)}, f32[16,1024]{1,0:T(8,128)S(1)}, u32[]{:S(2)}, u32[]{:S(2)}) collective-permute-start(f32[16,1024]{1,0:T(8,128)S(1)} %add.14.rest_0_.refs_0_), channel_id=1, source_target_pairs={{0,2},{2,0},{4,6},{6,4},{8,10},{10,8},{12,14},{14,12},{16,18},{18,... | collective-permute-start | bytes 196616 | tf_op jit(solution)/shard_map/ppermute | solution.py:414
  24.3 2.8 %beside.3 = (f32[16,384]{1,0:T(8,128)S(1)}, bf16[2048,512]{1,0:T(8,128)(2,1)S(1)}, bf16[2048,512]{1,0:T(8,128)(2,1)S(1)}) custom-call(s32[8,8]{1,0:T(8,128)S(1)} %copy-done, s32[8]{0:T(128)S(1)} %copy-done.1, f32[16,1280]{1,0:T(8,128)S(1)} %get-tuple-element.25.own_ref, bf16[32,3968]{1,0:T(8,128)(2,1)S(1)} %get-tuple-element.26.values_ref, ...), custom_call_target="tpu_custom_call" | custom-call | flops 196608000 | bytes 1572864 | tf_op jit(solution)/shard_map/beside/pallas_call | solution.py:371
  27.0 0.0 collective-permute-done.6.refs_1_
  27.0 0.0 collective-permute-done.7.refs_2_
  27.0 0.8 %collective-permute-done.8.refs_3_ = f32[16,1024]{1,0:T(8,128)S(1)} collective-permute-done((f32[16,1024]{1,0:T(8,128)S(1)}, f32[16,1024]{1,0:T(8,128)S(1)}, u32[]{:S(2)}, u32[]{:S(2)}) %collective-permute-start.8) | collective-permute-done | bytes 65568 | tf_op jit(solution)/shard_map/ppermute | solution.py:414
  27.9 0.1 collective-permute-start.9
  28.0 0.8 %factor.2.before_ref = f32[16,1024]{1,0:T(8,128)S(1)} custom-call(f32[16,1024]{1,0:T(8,128)S(1)} %add.15.proj_ref, bf16[2048,512]{1,0:T(8,128)(2,1)S(1)} %get-tuple-element.32.refs_5_.rest_0_, bf16[2048,512]{1,0:T(8,128)(2,1)S(1)} %get-tuple-element.35.refs_5_.rest_1_, bf16[2048,512]{1,0:T(8,128)(2,1)S(1)} %get-tuple-element.33.refs_6_.rest_2_, ...), custom_call_target="tpu_custom_call" | custom-call | flops 1048576000 | bytes 4194304 | tf_op jit(solution)/shard_map/factor/pallas_call | solution.py:264
  28.7 0.5 %collective-permute-done.9.proj_ref = f32[16,1024]{1,0:T(8,128)S(1)} collective-permute-done((f32[16,1024]{1,0:T(8,128)S(1)}, f32[16,1024]{1,0:T(8,128)S(1)}, u32[]{:S(2)}, u32[]{:S(2)}) %collective-permute-start.9) | collective-permute-done | bytes 65568 | tf_op jit(solution)/shard_map/ppermute | solution.py:422
  29.2 0.8 %factor.3.factor_ref = f32[16,1024]{1,0:T(8,128)S(1)} custom-call(f32[16,1024]{1,0:T(8,128)S(1)} %factor.2.before_ref, f32[16,1024]{1,0:T(8,128)S(1)} %collective-permute-done.9.proj_ref, bf16[2048,512]{1,0:T(8,128)(2,1)S(1)} %get-tuple-element.32.refs_5_.rest_0_, bf16[2048,512]{1,0:T(8,128)(2,1)S(1)} %get-tuple-element.35.refs_5_.rest_1_, ...), custom_call_target="tpu_custom_call" | custom-call | flops 1048576000 | bytes 4194304 | tf_op jit(solution)/shard_map/factor/pallas_call | solution.py:264
  30.0 0.8 %spread.2 = f32[16,1024]{1,0:T(8,128)S(1)} custom-call(f32[16,1024]{1,0:T(8,128)S(1)} %factor.3.factor_ref, bf16[1024,1024]{1,0:T(8,128)(2,1)S(1)} %get-tuple-element.37.high_ref, bf16[1024,1024]{1,0:T(8,128)(2,1)S(1)} %get-tuple-element.38.low_ref), custom_call_target="tpu_custom_call" | custom-call | flops 891289600 | bytes 4194304 | tf_op jit(solution)/shard_map/spread/pallas_call | solution.py:289
  30.7 0.2 collective-permute-start.10
  30.9 0.8 %spread.3 = f32[16,1024]{1,0:T(8,128)S(1)} custom-call(f32[16,1024]{1,0:T(8,128)S(1)} %factor.3.factor_ref, bf16[1024,1024]{1,0:T(8,128)(2,1)S(1)} %get-tuple-element.39.high_ref, bf16[1024,1024]{1,0:T(8,128)(2,1)S(1)} %get-tuple-element.40.low_ref), custom_call_target="tpu_custom_call" | custom-call | flops 891289600 | bytes 4194304 | tf_op jit(solution)/shard_map/spread/pallas_call | solution.py:289
  31.7 0.3 %collective-permute-done.10 = f32[16,1024]{1,0:T(8,128)S(1)} collective-permute-done((f32[16,1024]{1,0:T(8,128)S(1)}, f32[16,1024]{1,0:T(8,128)S(1)}, u32[]{:S(2)}, u32[]{:S(2)}) %collective-permute-start.10) | collective-permute-done | bytes 65568 | tf_op jit(solution)/shard_map/ppermute | solution.py:422
  32.0 0.6 %fusion = f32[16,1024]{1,0:T(8,128)} fusion(f32[16,1024]{1,0:T(8,128)S(1)} %spread.3, f32[16,1024]{1,0:T(8,128)S(1)} %collective-permute-done.10, f32[16,384]{1,0:T(8,128)S(1)} %get-tuple-element.34.refs_4_, f32[16,640]{1,0:T(8,128)S(1)} %get-tuple-element.31.refs_4_), kind=kLoop, calls=%fused_computation.1 | loop fusion | flops 49152 | bytes 262144 | tf_op jit(solution)/shard_map/add | solution.py:486
  (4 shorter events, 0.1 us)
Async XLA Ops:
  0.9 3.5 %collective-permute-start = (f32[16,1280]{1,0:T(8,128)S(1)}, f32[16,1280]{1,0:T(8,128)S(1)}, u32[]{:S(2)}, u32[]{:S(2)}) collective-permute-start(f32[16,1280]{1,0:T(8,128)S(1)} %get-tuple-element.23.stack_ref), channel_id=1, source_target_pairs={{1,0},{0,1},{3,2},{2,3},{5,4},{4,5},{7,6},{6,7},{9,8},{8,9},{11,10... | collective-permute-start | bytes 245768 | tf_op jit(solution)/shard_map/ppermute | solution.py:422
  1.4 14.4 %slice-start = ((s8[8388608]{0:T(1024)(128)(4,1)}), s8[4194304]{0:T(1024)(128)(4,1)S(1)}, s32[]{:S(2)}) async-start(s8[8388608]{0:T(1024)(128)(4,1)} %bitcast), calls=%async_computation | async-start | bytes 8388608
  4.4 11.4 %slice-start.1 = ((s8[8388608]{0:T(1024)(128)(4,1)}), s8[4194304]{0:T(1024)(128)(4,1)S(1)}, s32[]{:S(2)}) async-start(s8[8388608]{0:T(1024)(128)(4,1)} %bitcast), calls=%async_computation.1 | async-start | bytes 8388608
  4.5 11.3 %collective-permute-start.1 = (f32[16,1536]{1,0:T(8,128)S(1)}, f32[16,1536]{1,0:T(8,128)S(1)}, u32[]{:S(2)}, u32[]{:S(2)}) collective-permute-start(f32[16,1536]{1,0:T(8,128)S(1)} %strip.1.own_ref), channel_id=1, source_target_pairs={{0,1},{1,0},{2,4},{3,5},{4,2},{5,3},{6,8},{7,9},{8,6},{9,7},{10,12... | collective-permute-start | bytes 294920 | tf_op jit(solution)/shard_map/ppermute | solution.py:437
  4.6 11.2 %collective-permute-start.2 = (f32[16,1536]{1,0:T(8,128)S(1)}, f32[16,1536]{1,0:T(8,128)S(1)}, u32[]{:S(2)}, u32[]{:S(2)}) collective-permute-start(f32[16,1536]{1,0:T(8,128)S(1)} %strip.1.own_ref), channel_id=1, source_target_pairs={{0,2},{1,3},{2,0},{3,1},{4,6},{5,7},{6,4},{7,5},{8,10},{9,11},{10,... | collective-permute-start | bytes 294920 | tf_op jit(solution)/shard_map/ppermute | solution.py:437
  8.5 7.3 %copy-start = (s32[8,8]{1,0:T(8,128)S(1)}, s32[8,8]{1,0:T(8,128)}, u32[]{:S(2)}) copy-start(s32[8,8]{1,0:T(8,128)} %ids_ref.3) | copy-start | bytes 772
  8.5 7.3 %copy-start.1 = (s32[8]{0:T(128)S(1)}, s32[8]{0:T(128)}, u32[]{:S(2)}) copy-start(s32[8]{0:T(128)} %counts_ref.3) | copy-start | bytes 100
  11.3 8.0 %collective-permute-start.3 = (f32[16,1024]{1,0:T(8,128)S(1)}, f32[16,1024]{1,0:T(8,128)S(1)}, u32[]{:S(2)}, u32[]{:S(2)}) collective-permute-start(f32[16,1024]{1,0:T(8,128)S(1)} %get-tuple-element.30.rest_0_.refs_0_), channel_id=1, source_target_pairs={{0,24},{2,26},{4,28},{6,30},{8,16},{10,18},{12,20},{14,22},{16,8},... | collective-permute-start | bytes 196616 | tf_op jit(solution)/shard_map/ppermute | solution.py:414
  15.0 5.7 %collective-permute-start.4 = (f32[16,1024]{1,0:T(8,128)S(1)}, f32[16,1024]{1,0:T(8,128)S(1)}, u32[]{:S(2)}, u32[]{:S(2)}) collective-permute-start(f32[16,1024]{1,0:T(8,128)S(1)} %get-tuple-element.30.rest_0_.refs_0_), channel_id=1, source_target_pairs={{0,16},{2,18},{4,20},{6,22},{8,24},{10,26},{12,28},{14,30},{16,0},... | collective-permute-start | bytes 196616 | tf_op jit(solution)/shard_map/ppermute | solution.py:414
  15.0 5.7 %collective-permute-start.5 = (f32[16,1024]{1,0:T(8,128)S(1)}, f32[16,1024]{1,0:T(8,128)S(1)}, u32[]{:S(2)}, u32[]{:S(2)}) collective-permute-start(f32[16,1024]{1,0:T(8,128)S(1)} %get-tuple-element.30.rest_0_.refs_0_), channel_id=1, source_target_pairs={{0,8},{2,10},{4,12},{6,14},{8,0},{10,2},{12,4},{14,6},{16,24},{18,... | collective-permute-start | bytes 196616 | tf_op jit(solution)/shard_map/ppermute | solution.py:414
  20.7 6.3 %collective-permute-start.6 = (f32[16,1024]{1,0:T(8,128)S(1)}, f32[16,1024]{1,0:T(8,128)S(1)}, u32[]{:S(2)}, u32[]{:S(2)}) collective-permute-start(f32[16,1024]{1,0:T(8,128)S(1)} %add.14.rest_0_.refs_0_), channel_id=1, source_target_pairs={{0,6},{2,4},{4,2},{6,0},{8,14},{10,12},{12,10},{14,8},{16,22},{18,... | collective-permute-start | bytes 196616 | tf_op jit(solution)/shard_map/ppermute | solution.py:414
  22.2 4.8 %collective-permute-start.7 = (f32[16,1024]{1,0:T(8,128)S(1)}, f32[16,1024]{1,0:T(8,128)S(1)}, u32[]{:S(2)}, u32[]{:S(2)}) collective-permute-start(f32[16,1024]{1,0:T(8,128)S(1)} %add.14.rest_0_.refs_0_), channel_id=1, source_target_pairs={{0,4},{2,6},{4,0},{6,2},{8,12},{10,14},{12,8},{14,10},{16,20},{18,... | collective-permute-start | bytes 196616 | tf_op jit(solution)/shard_map/ppermute | solution.py:414
  23.6 4.3 %collective-permute-start.8 = (f32[16,1024]{1,0:T(8,128)S(1)}, f32[16,1024]{1,0:T(8,128)S(1)}, u32[]{:S(2)}, u32[]{:S(2)}) collective-permute-start(f32[16,1024]{1,0:T(8,128)S(1)} %add.14.rest_0_.refs_0_), channel_id=1, source_target_pairs={{0,2},{2,0},{4,6},{6,4},{8,10},{10,8},{12,14},{14,12},{16,18},{18,... | collective-permute-start | bytes 196616 | tf_op jit(solution)/shard_map/ppermute | solution.py:414
  27.9 1.3 %collective-permute-start.9 = (f32[16,1024]{1,0:T(8,128)S(1)}, f32[16,1024]{1,0:T(8,128)S(1)}, u32[]{:S(2)}, u32[]{:S(2)}) collective-permute-start(f32[16,1024]{1,0:T(8,128)S(1)} %add.15.proj_ref), channel_id=1, source_target_pairs={{1,0},{0,1},{3,2},{2,3},{5,4},{4,5},{7,6},{6,7},{9,8},{8,9},{11,10... | collective-permute-start | bytes 196616 | tf_op jit(solution)/shard_map/ppermute | solution.py:422
  30.7 1.3 %collective-permute-start.10 = (f32[16,1024]{1,0:T(8,128)S(1)}, f32[16,1024]{1,0:T(8,128)S(1)}, u32[]{:S(2)}, u32[]{:S(2)}) collective-permute-start(f32[16,1024]{1,0:T(8,128)S(1)} %spread.2), channel_id=1, source_target_pairs={{1,0},{0,1},{3,2},{2,3},{5,4},{4,5},{7,6},{6,7},{9,8},{8,9},{11,10... | collective-permute-start | bytes 196616 | tf_op jit(solution)/shard_map/ppermute | solution.py:422

commit v27 on v25

--- a/solution.py
+++ b/solution.py
@@ -181,8 +181,6 @@
     else:
         knots_ref, out_ref, high_ref, low_ref, columns, copy_ref, weights = rest
         copy_ref[...] = stack_ref[...]
-        fill = jnp.zeros((6, knots_ref.shape[1]), jnp.float32)
-        columns[...] = jnp.transpose(jnp.concatenate([off_grid(knots_ref[...] * scale, grain), fill], axis=0))
     knots, points = high_ref.shape
     probes = stack_ref.shape[0]
     tile = min(TILE, knots)
@@ -191,7 +189,13 @@
 
     for start in range(0, knots, tile):
         rows = slice(start, start + tile)
-        kx, ky = [columns[rows, axis : axis + 1] for axis in range(2)]
+        if follows:
+            turned = columns[rows, :]
+        else:
+            fill = jnp.zeros((6, tile), jnp.float32)
+            turned = jnp.transpose(jnp.concatenate([off_grid(knots_ref[:, rows] * scale, grain), fill], axis=0))
+            columns[rows, :] = turned
+        kx, ky = [turned[:, axis : axis + 1] for axis in range(2)]
         for block in range(points // LANES):
             lanes = slice(block * LANES, (block + 1) * LANES)
             dx = east[block : block + 1, :] - kx

time: 32.4 us -> 32.4 us (level)
  no operation moved by 1% of the time
where the time goes in v27:
time: 32.4 us; the launch traced here: 32.2 us
  Pallas kernels  16 us (49%)
  starting transfers between devices  13.4 us (41%)
  waiting for transfers between devices  1.99 us (6%)
  other arithmetic  0.65 us (2%)
    ppermute x6, starting transfers between devices, butterfly_round(): lax.ppermute(value, axis, [(i, i ^ step) for i in range(count)])  8.54 us
    pallas_call x2, Pallas kernels, beside_round(): pl.pallas_call(functools.partial(beside_kernel, first, first_row, grain_o...  6.2 us
    pallas_call x2, Pallas kernels, project(): pl.pallas_call(functools.partial(project_kernel, scale, grain_of(scale *...  5.79 us
    ppermute x2, starting transfers between devices, paired(): return lax.ppermute(value, (axis, other), pairs)  4.07 us
    pallas_call x2, Pallas kernels, spread(): pl.pallas_call(functools.partial(spread_kernel, scale), out_shape=jax.Sha...  1.54 us
    pallas_call x2, Pallas kernels, factored(): pl.pallas_call(kernel, out_shape=jax.ShapeDtypeStruct((probes, rows), jnp...  1.53 us
    ppermute x6, waiting for transfers between devices, butterfly_round(): lax.ppermute(value, axis, [(i, i ^ step) for i in range(count)])  1.17 us
    pallas_call x1, Pallas kernels, prepare(): pl.pallas_call(functools.partial(prepare_kernel, blocks), out_shape=(jax....  0.87 us
  transfers between devices with their start and end apart: 11, of which 3 were waited for; matrix products, arithmetic and copies ran while one was open for 0% of the time, Pallas kernels for 42%

profile of v27, /device:TPU:0, one launch (start us, length us, event | category | flops | bytes accessed | tf_op | source)
XLA Modules:
  0.0 32.2 jit_solution(3054200317036172636)
XLA Ops:
  0.0 0.9 %prepare.1 = (f32[16,1280]{1,0:T(8,128)S(1)}, f32[2,1024]{1,0:T(2,128)S(1)}) custom-call(f32[16,1024]{1,0:T(8,128)} %probes_ref.1, f32[2,1024]{1,0:T(2,128)} %locations_ref.1, f32[2,1024]{1,0:T(2,128)} %knots_ref.1), custom_call_target="tpu_custom_call" | custom-call | tf_op jit(solution)/shard_map/prepare/pallas_call | solution.py:95
  0.9 0.5 %collective-permute-start = (f32[16,1280]{1,0:T(8,128)S(1)}, f32[16,1280]{1,0:T(8,128)S(1)}, u32[]{:S(2)}, u32[]{:S(2)}) collective-permute-start(f32[16,1280]{1,0:T(8,128)S(1)} %get-tuple-element.23.stack_ref), channel_id=1, source_target_pairs={{1,0},{0,1},{3,2},{2,3},{5,4},{4,5},{7,6},{6,7},{9,8},{8,9},{11,10... | collective-permute-start | bytes 245768 | tf_op jit(solution)/shard_map/ppermute | solution.py:426
  1.4 0.0 slice-start
  1.4 3.0 %project.2 = (f32[16,1024]{1,0:T(8,128)S(1)}, bf16[1024,1024]{1,0:T(8,128)(2,1)S(1)}, bf16[1024,1024]{1,0:T(8,128)(2,1)S(1)}, f32[1024,8]{1,0:T(8,128)S(1)}, f32[16,1280]{1,0:T(8,128)S(1)}) custom-call(f32[16,1280]{1,0:T(8,128)S(1)} %get-tuple-element.23.stack_ref, f32[2,1024]{1,0:T(2,128)S(1)} %get-tuple-element.24.rest_0_), custom_call_target="tpu_custom_call" | custom-call | flops 2936012800 | bytes 4194304 | tf_op jit(solution)/shard_map/project/pallas_call | solution.py:225
  4.4 0.0 collective-permute-done.below_ref.above_ref.stack_ref
  4.4 0.0 slice-start.1
  4.5 0.1 collective-permute-start.1
  4.6 3.9 %collective-permute-start.2 = (f32[16,1536]{1,0:T(8,128)S(1)}, f32[16,1536]{1,0:T(8,128)S(1)}, u32[]{:S(2)}, u32[]{:S(2)}) collective-permute-start(f32[16,1536]{1,0:T(8,128)S(1)} %strip.1.own_ref), channel_id=1, source_target_pairs={{0,2},{1,3},{2,0},{3,1},{4,6},{5,7},{6,4},{7,5},{8,10},{9,11},{10,... | collective-permute-start | bytes 294920 | tf_op jit(solution)/shard_map/ppermute | solution.py:441
  8.5 0.0 copy-start
  8.5 0.0 copy-start.1
  8.5 2.8 %project.3 = (f32[16,1024]{1,0:T(8,128)S(1)}, bf16[1024,1024]{1,0:T(8,128)(2,1)S(1)}, bf16[1024,1024]{1,0:T(8,128)(2,1)S(1)}) custom-call(f32[16,1280]{1,0:T(8,128)S(1)} %collective-permute-done.below_ref.above_ref.stack_ref, f32[16,1024]{1,0:T(8,128)S(1)} %get-tuple-element.28.rest_0_, f32[1024,8]{1,0:T(8,128)S(1)} %get-tuple-element.29.rest_1_), custom_call_target="tpu_custom_call" | custom-call | flops 2936012800 | bytes 4194304 | tf_op jit(solution)/shard_map/project/pallas_call | solution.py:225
  11.3 1.5 %collective-permute-start.3 = (f32[16,1024]{1,0:T(8,128)S(1)}, f32[16,1024]{1,0:T(8,128)S(1)}, u32[]{:S(2)}, u32[]{:S(2)}) collective-permute-start(f32[16,1024]{1,0:T(8,128)S(1)} %get-tuple-element.30.rest_0_.refs_0_), channel_id=1, source_target_pairs={{0,6},{2,4},{4,2},{6,0},{8,14},{10,12},{12,10},{14,8},{16,22},{18,... | collective-permute-start | bytes 196616 | tf_op jit(solution)/shard_map/ppermute | solution.py:418
  12.8 0.2 collective-permute-start.4
  13.0 1.9 %collective-permute-start.5 = (f32[16,1024]{1,0:T(8,128)S(1)}, f32[16,1024]{1,0:T(8,128)S(1)}, u32[]{:S(2)}, u32[]{:S(2)}) collective-permute-start(f32[16,1024]{1,0:T(8,128)S(1)} %get-tuple-element.30.rest_0_.refs_0_), channel_id=1, source_target_pairs={{0,2},{2,0},{4,6},{6,4},{8,10},{10,8},{12,14},{14,12},{16,18},{18,... | collective-permute-start | bytes 196616 | tf_op jit(solution)/shard_map/ppermute | solution.py:418
  14.9 0.0 collective-permute-done.1.odd_ref
  14.9 0.0 collective-permute-done.2.even_ref
  14.9 0.1 assemble.1
  14.9 0.0 slice-done
  15.0 0.0 slice-done.1
  15.0 0.0 copy-done
  15.0 0.0 copy-done.1
  15.0 2.8 %beside.2 = (f32[16,384]{1,0:T(8,128)S(1)}, bf16[2048,512]{1,0:T(8,128)(2,1)S(1)}, bf16[2048,512]{1,0:T(8,128)(2,1)S(1)}) custom-call(s32[8,8]{1,0:T(8,128)S(1)} %copy-done, s32[8]{0:T(128)S(1)} %copy-done.1, f32[16,1280]{1,0:T(8,128)S(1)} %get-tuple-element.25.own_ref, bf16[32,3968]{1,0:T(8,128)(2,1)S(1)} %get-tuple-element.26.values_ref, ...), custom_call_target="tpu_custom_call" | custom-call | flops 196608000 | bytes 1572864 | tf_op jit(solution)/shard_map/beside/pallas_call | solution.py:375
  17.8 0.0 collective-permute-done.3.refs_1_
  17.8 0.0 collective-permute-done.4.refs_2_
  17.8 0.0 collective-permute-done.5.refs_3_
  17.8 4.3 %collective-permute-start.6 = (f32[16,1024]{1,0:T(8,128)S(1)}, f32[16,1024]{1,0:T(8,128)S(1)}, u32[]{:S(2)}, u32[]{:S(2)}) collective-permute-start(f32[16,1024]{1,0:T(8,128)S(1)} %add.14.rest_0_.refs_0_), channel_id=1, source_target_pairs={{0,24},{2,26},{4,28},{6,30},{8,16},{10,18},{12,20},{14,22},{16,8},... | collective-permute-start | bytes 196616 | tf_op jit(solution)/shard_map/ppermute | solution.py:418
  22.2 0.0 collective-permute-start.7
  22.2 0.6 %collective-permute-start.8 = (f32[16,1024]{1,0:T(8,128)S(1)}, f32[16,1024]{1,0:T(8,128)S(1)}, u32[]{:S(2)}, u32[]{:S(2)}) collective-permute-start(f32[16,1024]{1,0:T(8,128)S(1)} %add.14.rest_0_.refs_0_), channel_id=1, source_target_pairs={{0,8},{2,10},{4,12},{6,14},{8,0},{10,2},{12,4},{14,6},{16,24},{18,... | collective-permute-start | bytes 196616 | tf_op jit(solution)/shard_map/ppermute | solution.py:418
  22.8 3.4 %beside.3 = (f32[16,640]{1,0:T(8,128)S(1)}, bf16[2048,512]{1,0:T(8,128)(2,1)S(1)}, bf16[2048,512]{1,0:T(8,128)(2,1)S(1)}) custom-call(s32[8,8]{1,0:T(8,128)S(1)} %copy-done, s32[8]{0:T(128)S(1)} %copy-done.1, f32[16,1280]{1,0:T(8,128)S(1)} %get-tuple-element.25.own_ref, bf16[32,3968]{1,0:T(8,128)(2,1)S(1)} %get-tuple-element.26.values_ref, ...), custom_call_target="tpu_custom_call" | custom-call | flops 327680000 | bytes 2621440 | tf_op jit(solution)/shard_map/beside/pallas_call | solution.py:375
  26.3 0.0 collective-permute-done.6.refs_1_
  26.3 1.2 %collective-permute-done.7.refs_2_ = f32[16,1024]{1,0:T(8,128)S(1)} collective-permute-done((f32[16,1024]{1,0:T(8,128)S(1)}, f32[16,1024]{1,0:T(8,128)S(1)}, u32[]{:S(2)}, u32[]{:S(2)}) %collective-permute-start.7) | collective-permute-done | bytes 65568 | tf_op jit(solution)/shard_map/ppermute | solution.py:418
  27.4 0.0 collective-permute-done.8.refs_3_
  27.4 0.1 collective-permute-start.9
  27.5 0.8 %factor.2.before_ref = f32[16,1024]{1,0:T(8,128)S(1)} custom-call(f32[16,1024]{1,0:T(8,128)S(1)} %add.15.proj_ref, bf16[2048,512]{1,0:T(8,128)(2,1)S(1)} %get-tuple-element.32.refs_5_.rest_0_, bf16[2048,512]{1,0:T(8,128)(2,1)S(1)} %get-tuple-element.35.refs_5_.rest_1_, bf16[2048,512]{1,0:T(8,128)(2,1)S(1)} %get-tuple-element.33.refs_6_.rest_2_, ...), custom_call_target="tpu_custom_call" | custom-call | flops 1048576000 | bytes 4194304 | tf_op jit(solution)/shard_map/factor/pallas_call | solution.py:268
  28.3 0.5 %collective-permute-done.9.proj_ref = f32[16,1024]{1,0:T(8,128)S(1)} collective-permute-done((f32[16,1024]{1,0:T(8,128)S(1)}, f32[16,1024]{1,0:T(8,128)S(1)}, u32[]{:S(2)}, u32[]{:S(2)}) %collective-permute-start.9) | collective-permute-done | bytes 65568 | tf_op jit(solution)/shard_map/ppermute | solution.py:426
  28.8 0.8 %factor.3.factor_ref = f32[16,1024]{1,0:T(8,128)S(1)} custom-call(f32[16,1024]{1,0:T(8,128)S(1)} %factor.2.before_ref, f32[16,1024]{1,0:T(8,128)S(1)} %collective-permute-done.9.proj_ref, bf16[2048,512]{1,0:T(8,128)(2,1)S(1)} %get-tuple-element.32.refs_5_.rest_0_, bf16[2048,512]{1,0:T(8,128)(2,1)S(1)} %get-tuple-element.35.refs_5_.rest_1_, ...), custom_call_target="tpu_custom_call" | custom-call | flops 1048576000 | bytes 4194304 | tf_op jit(solution)/shard_map/factor/pallas_call | solution.py:268
  29.5 0.8 %spread.2 = f32[16,1024]{1,0:T(8,128)S(1)} custom-call(f32[16,1024]{1,0:T(8,128)S(1)} %factor.3.factor_ref, bf16[1024,1024]{1,0:T(8,128)(2,1)S(1)} %get-tuple-element.37.high_ref, bf16[1024,1024]{1,0:T(8,128)(2,1)S(1)} %get-tuple-element.38.low_ref), custom_call_target="tpu_custom_call" | custom-call | flops 891289600 | bytes 4194304 | tf_op jit(solution)/shard_map/spread/pallas_call | solution.py:293
  30.3 0.2 collective-permute-start.10
  30.5 0.8 %spread.3 = f32[16,1024]{1,0:T(8,128)S(1)} custom-call(f32[16,1024]{1,0:T(8,128)S(1)} %factor.3.factor_ref, bf16[1024,1024]{1,0:T(8,128)(2,1)S(1)} %get-tuple-element.39.high_ref, bf16[1024,1024]{1,0:T(8,128)(2,1)S(1)} %get-tuple-element.40.low_ref), custom_call_target="tpu_custom_call" | custom-call | flops 891289600 | bytes 4194304 | tf_op jit(solution)/shard_map/spread/pallas_call | solution.py:293
  31.2 0.3 %collective-permute-done.10 = f32[16,1024]{1,0:T(8,128)S(1)} collective-permute-done((f32[16,1024]{1,0:T(8,128)S(1)}, f32[16,1024]{1,0:T(8,128)S(1)}, u32[]{:S(2)}, u32[]{:S(2)}) %collective-permute-start.10) | collective-permute-done | bytes 65568 | tf_op jit(solution)/shard_map/ppermute | solution.py:426
  31.6 0.6 %fusion = f32[16,1024]{1,0:T(8,128)} fusion(f32[16,1024]{1,0:T(8,128)S(1)} %spread.3, f32[16,1024]{1,0:T(8,128)S(1)} %collective-permute-done.10, f32[16,640]{1,0:T(8,128)S(1)} %get-tuple-element.34.refs_4_, f32[16,384]{1,0:T(8,128)S(1)} %get-tuple-element.31.refs_4_), kind=kLoop, calls=%fused_computation.1 | loop fusion | flops 49152 | bytes 262144 | tf_op jit(solution)/shard_map/add | solution.py:490
  (4 shorter events, 0.1 us)
Async XLA Ops:
  0.9 3.5 %collective-permute-start = (f32[16,1280]{1,0:T(8,128)S(1)}, f32[16,1280]{1,0:T(8,128)S(1)}, u32[]{:S(2)}, u32[]{:S(2)}) collective-permute-start(f32[16,1280]{1,0:T(8,128)S(1)} %get-tuple-element.23.stack_ref), channel_id=1, source_target_pairs={{1,0},{0,1},{3,2},{2,3},{5,4},{4,5},{7,6},{6,7},{9,8},{8,9},{11,10... | collective-permute-start | bytes 245768 | tf_op jit(solution)/shard_map/ppermute | solution.py:426
  1.4 13.5 %slice-start = ((s8[8388608]{0:T(1024)(128)(4,1)}), s8[4194304]{0:T(1024)(128)(4,1)S(1)}, s32[]{:S(2)}) async-start(s8[8388608]{0:T(1024)(128)(4,1)} %bitcast), calls=%async_computation | async-start | bytes 8388608
  4.4 10.5 %slice-start.1 = ((s8[8388608]{0:T(1024)(128)(4,1)}), s8[4194304]{0:T(1024)(128)(4,1)S(1)}, s32[]{:S(2)}) async-start(s8[8388608]{0:T(1024)(128)(4,1)} %bitcast), calls=%async_computation.1 | async-start | bytes 8388608
  4.5 10.4 %collective-permute-start.1 = (f32[16,1536]{1,0:T(8,128)S(1)}, f32[16,1536]{1,0:T(8,128)S(1)}, u32[]{:S(2)}, u32[]{:S(2)}) collective-permute-start(f32[16,1536]{1,0:T(8,128)S(1)} %strip.1.own_ref), channel_id=1, source_target_pairs={{0,1},{1,0},{2,4},{3,5},{4,2},{5,3},{6,8},{7,9},{8,6},{9,7},{10,12... | collective-permute-start | bytes 294920 | tf_op jit(solution)/shard_map/ppermute | solution.py:441
  4.6 10.3 %collective-permute-start.2 = (f32[16,1536]{1,0:T(8,128)S(1)}, f32[16,1536]{1,0:T(8,128)S(1)}, u32[]{:S(2)}, u32[]{:S(2)}) collective-permute-start(f32[16,1536]{1,0:T(8,128)S(1)} %strip.1.own_ref), channel_id=1, source_target_pairs={{0,2},{1,3},{2,0},{3,1},{4,6},{5,7},{6,4},{7,5},{8,10},{9,11},{10,... | collective-permute-start | bytes 294920 | tf_op jit(solution)/shard_map/ppermute | solution.py:441
  8.5 6.4 %copy-start = (s32[8,8]{1,0:T(8,128)S(1)}, s32[8,8]{1,0:T(8,128)}, u32[]{:S(2)}) copy-start(s32[8,8]{1,0:T(8,128)} %ids_ref.3) | copy-start | bytes 772
  8.5 6.4 %copy-start.1 = (s32[8]{0:T(128)S(1)}, s32[8]{0:T(128)}, u32[]{:S(2)}) copy-start(s32[8]{0:T(128)} %counts_ref.3) | copy-start | bytes 100
  11.3 6.5 %collective-permute-start.3 = (f32[16,1024]{1,0:T(8,128)S(1)}, f32[16,1024]{1,0:T(8,128)S(1)}, u32[]{:S(2)}, u32[]{:S(2)}) collective-permute-start(f32[16,1024]{1,0:T(8,128)S(1)} %get-tuple-element.30.rest_0_.refs_0_), channel_id=1, source_target_pairs={{0,6},{2,4},{4,2},{6,0},{8,14},{10,12},{12,10},{14,8},{16,22},{18,... | collective-permute-start | bytes 196616 | tf_op jit(solution)/shard_map/ppermute | solution.py:418
  12.8 5.0 %collective-permute-start.4 = (f32[16,1024]{1,0:T(8,128)S(1)}, f32[16,1024]{1,0:T(8,128)S(1)}, u32[]{:S(2)}, u32[]{:S(2)}) collective-permute-start(f32[16,1024]{1,0:T(8,128)S(1)} %get-tuple-element.30.rest_0_.refs_0_), channel_id=1, source_target_pairs={{0,4},{2,6},{4,0},{6,2},{8,12},{10,14},{12,8},{14,10},{16,20},{18,... | collective-permute-start | bytes 196616 | tf_op jit(solution)/shard_map/ppermute | solution.py:418
  13.0 4.8 %collective-permute-start.5 = (f32[16,1024]{1,0:T(8,128)S(1)}, f32[16,1024]{1,0:T(8,128)S(1)}, u32[]{:S(2)}, u32[]{:S(2)}) collective-permute-start(f32[16,1024]{1,0:T(8,128)S(1)} %get-tuple-element.30.rest_0_.refs_0_), channel_id=1, source_target_pairs={{0,2},{2,0},{4,6},{6,4},{8,10},{10,8},{12,14},{14,12},{16,18},{18,... | collective-permute-start | bytes 196616 | tf_op jit(solution)/shard_map/ppermute | solution.py:418
  17.8 8.4 %collective-permute-start.6 = (f32[16,1024]{1,0:T(8,128)S(1)}, f32[16,1024]{1,0:T(8,128)S(1)}, u32[]{:S(2)}, u32[]{:S(2)}) collective-permute-start(f32[16,1024]{1,0:T(8,128)S(1)} %add.14.rest_0_.refs_0_), channel_id=1, source_target_pairs={{0,24},{2,26},{4,28},{6,30},{8,16},{10,18},{12,20},{14,22},{16,8},... | collective-permute-start | bytes 196616 | tf_op jit(solution)/shard_map/ppermute | solution.py:418
  22.2 5.2 %collective-permute-start.7 = (f32[16,1024]{1,0:T(8,128)S(1)}, f32[16,1024]{1,0:T(8,128)S(1)}, u32[]{:S(2)}, u32[]{:S(2)}) collective-permute-start(f32[16,1024]{1,0:T(8,128)S(1)} %add.14.rest_0_.refs_0_), channel_id=1, source_target_pairs={{0,16},{2,18},{4,20},{6,22},{8,24},{10,26},{12,28},{14,30},{16,0},... | collective-permute-start | bytes 196616 | tf_op jit(solution)/shard_map/ppermute | solution.py:418
  22.2 5.2 %collective-permute-start.8 = (f32[16,1024]{1,0:T(8,128)S(1)}, f32[16,1024]{1,0:T(8,128)S(1)}, u32[]{:S(2)}, u32[]{:S(2)}) collective-permute-start(f32[16,1024]{1,0:T(8,128)S(1)} %add.14.rest_0_.refs_0_), channel_id=1, source_target_pairs={{0,8},{2,10},{4,12},{6,14},{8,0},{10,2},{12,4},{14,6},{16,24},{18,... | collective-permute-start | bytes 196616 | tf_op jit(solution)/shard_map/ppermute | solution.py:418
  27.4 1.3 %collective-permute-start.9 = (f32[16,1024]{1,0:T(8,128)S(1)}, f32[16,1024]{1,0:T(8,128)S(1)}, u32[]{:S(2)}, u32[]{:S(2)}) collective-permute-start(f32[16,1024]{1,0:T(8,128)S(1)} %add.15.proj_ref), channel_id=1, source_target_pairs={{1,0},{0,1},{3,2},{2,3},{5,4},{4,5},{7,6},{6,7},{9,8},{8,9},{11,10... | collective-permute-start | bytes 196616 | tf_op jit(solution)/shard_map/ppermute | solution.py:426
  30.3 1.3 %collective-permute-start.10 = (f32[16,1024]{1,0:T(8,128)S(1)}, f32[16,1024]{1,0:T(8,128)S(1)}, u32[]{:S(2)}, u32[]{:S(2)}) collective-permute-start(f32[16,1024]{1,0:T(8,128)S(1)} %spread.2), channel_id=1, source_target_pairs={{1,0},{0,1},{3,2},{2,3},{5,4},{4,5},{7,6},{6,7},{9,8},{8,9},{11,10... | collective-permute-start | bytes 196616 | tf_op jit(solution)/shard_map/ppermute | solution.py:426

commit v28 on v27

--- a/solution.py
+++ b/solution.py
@@ -409,6 +409,7 @@
     assert count & (count - 1) == 0
     bits = [1 << i for i in range(count.bit_length() - 1)]
     rounds = [(low | high, high, low) for low, high in zip(bits[0::2], bits[1::2])]
+    rounds[:1] = [(high, both, low) for both, high, low in rounds[:1]]
     return rounds + [(bit,) for bit in bits[len(rounds) * 2 :]]
 
 

time: 32.4 us -> 32.5 us (level)
  waiting for transfers between devices: 1.99 us -> 2.48 us
  starting transfers between devices: 13.4 us -> 13 us
    ppermute x6, waiting for transfers between devices: 1.17 us -> 1.66 us  [butterfly_round(): lax.ppermute(value, axis, [(i, i ^ step) for i in range(count)])]
    ppermute x6, starting transfers between devices: 8.54 us -> 8.2 us  [butterfly_round(): lax.ppermute(value, axis, [(i, i ^ step) for i in range(count)])]
  transfers between devices with their start and end apart: 11 -> 11, of which waited for: 3 -> 4; matrix products, arithmetic and copies ran while one was open for 0% -> 0% of each run, Pallas kernels for 42% -> 42%
where the time goes in v28:
time: 32.5 us; the launch traced here: 32.3 us
  Pallas kernels  16 us (49%)
  starting transfers between devices  13 us (40%)
  waiting for transfers between devices  2.48 us (8%)
  other arithmetic  0.65 us (2%)
    ppermute x6, starting transfers between devices, butterfly_round(): lax.ppermute(value, axis, [(i, i ^ step) for i in range(count)])  8.2 us
    pallas_call x2, Pallas kernels, beside_round(): pl.pallas_call(functools.partial(beside_kernel, first, first_row, grain_o...  6.2 us
    pallas_call x2, Pallas kernels, project(): pl.pallas_call(functools.partial(project_kernel, scale, grain_of(scale *...  5.79 us
    ppermute x2, starting transfers between devices, paired(): return lax.ppermute(value, (axis, other), pairs)  4.07 us
    ppermute x6, waiting for transfers between devices, butterfly_round(): lax.ppermute(value, axis, [(i, i ^ step) for i in range(count)])  1.66 us
    pallas_call x2, Pallas kernels, spread(): pl.pallas_call(functools.partial(spread_kernel, scale), out_shape=jax.Sha...  1.53 us
    pallas_call x2, Pallas kernels, factored(): pl.pallas_call(kernel, out_shape=jax.ShapeDtypeStruct((probes, rows), jnp...  1.53 us
    pallas_call x1, Pallas kernels, prepare(): pl.pallas_call(functools.partial(prepare_kernel, blocks), out_shape=(jax....  0.87 us
  transfers between devices with their start and end apart: 11, of which 4 were waited for; matrix products, arithmetic and copies ran while one was open for 0% of the time, Pallas kernels for 42%

profile of v28, /device:TPU:0, one launch (start us, length us, event | category | flops | bytes accessed | tf_op | source)
XLA Modules:
  0.0 32.3 jit_solution(12664096203789444684)
XLA Ops:
  0.0 0.9 %prepare.1 = (f32[16,1280]{1,0:T(8,128)S(1)}, f32[2,1024]{1,0:T(2,128)S(1)}) custom-call(f32[16,1024]{1,0:T(8,128)} %probes_ref.1, f32[2,1024]{1,0:T(2,128)} %locations_ref.1, f32[2,1024]{1,0:T(2,128)} %knots_ref.1), custom_call_target="tpu_custom_call" | custom-call | tf_op jit(solution)/shard_map/prepare/pallas_call | solution.py:95
  0.9 0.5 %collective-permute-start = (f32[16,1280]{1,0:T(8,128)S(1)}, f32[16,1280]{1,0:T(8,128)S(1)}, u32[]{:S(2)}, u32[]{:S(2)}) collective-permute-start(f32[16,1280]{1,0:T(8,128)S(1)} %get-tuple-element.23.stack_ref), channel_id=1, source_target_pairs={{1,0},{0,1},{3,2},{2,3},{5,4},{4,5},{7,6},{6,7},{9,8},{8,9},{11,10... | collective-permute-start | bytes 245768 | tf_op jit(solution)/shard_map/ppermute | solution.py:427
  1.4 0.0 slice-start
  1.4 3.0 %project.2 = (f32[16,1024]{1,0:T(8,128)S(1)}, bf16[1024,1024]{1,0:T(8,128)(2,1)S(1)}, bf16[1024,1024]{1,0:T(8,128)(2,1)S(1)}, f32[1024,8]{1,0:T(8,128)S(1)}, f32[16,1280]{1,0:T(8,128)S(1)}) custom-call(f32[16,1280]{1,0:T(8,128)S(1)} %get-tuple-element.23.stack_ref, f32[2,1024]{1,0:T(2,128)S(1)} %get-tuple-element.24.rest_0_), custom_call_target="tpu_custom_call" | custom-call | flops 2936012800 | bytes 4194304 | tf_op jit(solution)/shard_map/project/pallas_call | solution.py:225
  4.4 0.0 collective-permute-done.below_ref.above_ref.stack_ref
  4.4 0.0 slice-start.1
  4.5 0.1 collective-permute-start.1
  4.6 3.9 %collective-permute-start.2 = (f32[16,1536]{1,0:T(8,128)S(1)}, f32[16,1536]{1,0:T(8,128)S(1)}, u32[]{:S(2)}, u32[]{:S(2)}) collective-permute-start(f32[16,1536]{1,0:T(8,128)S(1)} %strip.1.own_ref), channel_id=1, source_target_pairs={{0,2},{1,3},{2,0},{3,1},{4,6},{5,7},{6,4},{7,5},{8,10},{9,11},{10,... | collective-permute-start | bytes 294920 | tf_op jit(solution)/shard_map/ppermute | solution.py:442
  8.5 0.0 copy-start
  8.5 0.0 copy-start.1
  8.5 2.8 %project.3 = (f32[16,1024]{1,0:T(8,128)S(1)}, bf16[1024,1024]{1,0:T(8,128)(2,1)S(1)}, bf16[1024,1024]{1,0:T(8,128)(2,1)S(1)}) custom-call(f32[16,1280]{1,0:T(8,128)S(1)} %collective-permute-done.below_ref.above_ref.stack_ref, f32[16,1024]{1,0:T(8,128)S(1)} %get-tuple-element.28.rest_0_, f32[1024,8]{1,0:T(8,128)S(1)} %get-tuple-element.29.rest_1_), custom_call_target="tpu_custom_call" | custom-call | flops 2936012800 | bytes 4194304 | tf_op jit(solution)/shard_map/project/pallas_call | solution.py:225
  11.3 1.6 %collective-permute-start.3 = (f32[16,1024]{1,0:T(8,128)S(1)}, f32[16,1024]{1,0:T(8,128)S(1)}, u32[]{:S(2)}, u32[]{:S(2)}) collective-permute-start(f32[16,1024]{1,0:T(8,128)S(1)} %get-tuple-element.30.rest_0_.refs_0_), channel_id=1, source_target_pairs={{0,4},{2,6},{4,0},{6,2},{8,12},{10,14},{12,8},{14,10},{16,20},{18,... | collective-permute-start | bytes 196616 | tf_op jit(solution)/shard_map/ppermute | solution.py:419
  12.9 0.0 collective-permute-start.4
  12.9 2.0 %collective-permute-start.5 = (f32[16,1024]{1,0:T(8,128)S(1)}, f32[16,1024]{1,0:T(8,128)S(1)}, u32[]{:S(2)}, u32[]{:S(2)}) collective-permute-start(f32[16,1024]{1,0:T(8,128)S(1)} %get-tuple-element.30.rest_0_.refs_0_), channel_id=1, source_target_pairs={{0,2},{2,0},{4,6},{6,4},{8,10},{10,8},{12,14},{14,12},{16,18},{18,... | collective-permute-start | bytes 196616 | tf_op jit(solution)/shard_map/ppermute | solution.py:419
  14.9 0.0 collective-permute-done.1.odd_ref
  14.9 0.0 collective-permute-done.2.even_ref
  14.9 0.1 assemble.1
  14.9 0.0 slice-done
  15.0 0.0 slice-done.1
  15.0 0.0 copy-done
  15.0 0.0 copy-done.1
  15.0 2.8 %beside.2 = (f32[16,384]{1,0:T(8,128)S(1)}, bf16[2048,512]{1,0:T(8,128)(2,1)S(1)}, bf16[2048,512]{1,0:T(8,128)(2,1)S(1)}) custom-call(s32[8,8]{1,0:T(8,128)S(1)} %copy-done, s32[8]{0:T(128)S(1)} %copy-done.1, f32[16,1280]{1,0:T(8,128)S(1)} %get-tuple-element.25.own_ref, bf16[32,3968]{1,0:T(8,128)(2,1)S(1)} %get-tuple-element.26.values_ref, ...), custom_call_target="tpu_custom_call" | custom-call | flops 196608000 | bytes 1572864 | tf_op jit(solution)/shard_map/beside/pallas_call | solution.py:375
  17.8 0.0 collective-permute-done.3.refs_1_
  17.8 0.4 %collective-permute-done.4.refs_2_ = f32[16,1024]{1,0:T(8,128)S(1)} collective-permute-done((f32[16,1024]{1,0:T(8,128)S(1)}, f32[16,1024]{1,0:T(8,128)S(1)}, u32[]{:S(2)}, u32[]{:S(2)}) %collective-permute-start.4) | collective-permute-done | bytes 65568 | tf_op jit(solution)/shard_map/ppermute | solution.py:419
  18.1 0.0 collective-permute-done.5.refs_3_
  18.2 4.0 %collective-permute-start.6 = (f32[16,1024]{1,0:T(8,128)S(1)}, f32[16,1024]{1,0:T(8,128)S(1)}, u32[]{:S(2)}, u32[]{:S(2)}) collective-permute-start(f32[16,1024]{1,0:T(8,128)S(1)} %add.14.rest_0_.refs_0_), channel_id=1, source_target_pairs={{0,24},{2,26},{4,28},{6,30},{8,16},{10,18},{12,20},{14,22},{16,8},... | collective-permute-start | bytes 196616 | tf_op jit(solution)/shard_map/ppermute | solution.py:419
  22.2 0.0 collective-permute-start.7
  22.2 0.6 %collective-permute-start.8 = (f32[16,1024]{1,0:T(8,128)S(1)}, f32[16,1024]{1,0:T(8,128)S(1)}, u32[]{:S(2)}, u32[]{:S(2)}) collective-permute-start(f32[16,1024]{1,0:T(8,128)S(1)} %add.14.rest_0_.refs_0_), channel_id=1, source_target_pairs={{0,8},{2,10},{4,12},{6,14},{8,0},{10,2},{12,4},{14,6},{16,24},{18,... | collective-permute-start | bytes 196616 | tf_op jit(solution)/shard_map/ppermute | solution.py:419
  22.8 3.4 %beside.3 = (f32[16,640]{1,0:T(8,128)S(1)}, bf16[2048,512]{1,0:T(8,128)(2,1)S(1)}, bf16[2048,512]{1,0:T(8,128)(2,1)S(1)}) custom-call(s32[8,8]{1,0:T(8,128)S(1)} %copy-done, s32[8]{0:T(128)S(1)} %copy-done.1, f32[16,1280]{1,0:T(8,128)S(1)} %get-tuple-element.25.own_ref, bf16[32,3968]{1,0:T(8,128)(2,1)S(1)} %get-tuple-element.26.values_ref, ...), custom_call_target="tpu_custom_call" | custom-call | flops 327680000 | bytes 2621440 | tf_op jit(solution)/shard_map/beside/pallas_call | solution.py:375
  26.2 0.0 collective-permute-done.6.refs_1_
  26.3 1.3 %collective-permute-done.7.refs_2_ = f32[16,1024]{1,0:T(8,128)S(1)} collective-permute-done((f32[16,1024]{1,0:T(8,128)S(1)}, f32[16,1024]{1,0:T(8,128)S(1)}, u32[]{:S(2)}, u32[]{:S(2)}) %collective-permute-start.7) | collective-permute-done | bytes 65568 | tf_op jit(solution)/shard_map/ppermute | solution.py:419
  27.5 0.0 collective-permute-done.8.refs_3_
  27.6 0.1 collective-permute-start.9
  27.6 0.8 %factor.2.before_ref = f32[16,1024]{1,0:T(8,128)S(1)} custom-call(f32[16,1024]{1,0:T(8,128)S(1)} %add.15.proj_ref, bf16[2048,512]{1,0:T(8,128)(2,1)S(1)} %get-tuple-element.32.refs_5_.rest_0_, bf16[2048,512]{1,0:T(8,128)(2,1)S(1)} %get-tuple-element.35.refs_5_.rest_1_, bf16[2048,512]{1,0:T(8,128)(2,1)S(1)} %get-tuple-element.33.refs_6_.rest_2_, ...), custom_call_target="tpu_custom_call" | custom-call | flops 1048576000 | bytes 4194304 | tf_op jit(solution)/shard_map/factor/pallas_call | solution.py:268
  28.4 0.5 %collective-permute-done.9.proj_ref = f32[16,1024]{1,0:T(8,128)S(1)} collective-permute-done((f32[16,1024]{1,0:T(8,128)S(1)}, f32[16,1024]{1,0:T(8,128)S(1)}, u32[]{:S(2)}, u32[]{:S(2)}) %collective-permute-start.9) | collective-permute-done | bytes 65568 | tf_op jit(solution)/shard_map/ppermute | solution.py:427
  28.9 0.8 %factor.3.factor_ref = f32[16,1024]{1,0:T(8,128)S(1)} custom-call(f32[16,1024]{1,0:T(8,128)S(1)} %factor.2.before_ref, f32[16,1024]{1,0:T(8,128)S(1)} %collective-permute-done.9.proj_ref, bf16[2048,512]{1,0:T(8,128)(2,1)S(1)} %get-tuple-element.32.refs_5_.rest_0_, bf16[2048,512]{1,0:T(8,128)(2,1)S(1)} %get-tuple-element.35.refs_5_.rest_1_, ...), custom_call_target="tpu_custom_call" | custom-call | flops 1048576000 | bytes 4194304 | tf_op jit(solution)/shard_map/factor/pallas_call | solution.py:268
  29.6 0.8 %spread.2 = f32[16,1024]{1,0:T(8,128)S(1)} custom-call(f32[16,1024]{1,0:T(8,128)S(1)} %factor.3.factor_ref, bf16[1024,1024]{1,0:T(8,128)(2,1)S(1)} %get-tuple-element.37.high_ref, bf16[1024,1024]{1,0:T(8,128)(2,1)S(1)} %get-tuple-element.38.low_ref), custom_call_target="tpu_custom_call" | custom-call | flops 891289600 | bytes 4194304 | tf_op jit(solution)/shard_map/spread/pallas_call | solution.py:293
  30.4 0.2 collective-permute-start.10
  30.6 0.8 %spread.3 = f32[16,1024]{1,0:T(8,128)S(1)} custom-call(f32[16,1024]{1,0:T(8,128)S(1)} %factor.3.factor_ref, bf16[1024,1024]{1,0:T(8,128)(2,1)S(1)} %get-tuple-element.39.high_ref, bf16[1024,1024]{1,0:T(8,128)(2,1)S(1)} %get-tuple-element.40.low_ref), custom_call_target="tpu_custom_call" | custom-call | flops 891289600 | bytes 4194304 | tf_op jit(solution)/shard_map/spread/pallas_call | solution.py:293
  31.4 0.3 %collective-permute-done.10 = f32[16,1024]{1,0:T(8,128)S(1)} collective-permute-done((f32[16,1024]{1,0:T(8,128)S(1)}, f32[16,1024]{1,0:T(8,128)S(1)}, u32[]{:S(2)}, u32[]{:S(2)}) %collective-permute-start.10) | collective-permute-done | bytes 65568 | tf_op jit(solution)/shard_map/ppermute | solution.py:427
  31.7 0.6 %fusion = f32[16,1024]{1,0:T(8,128)} fusion(f32[16,1024]{1,0:T(8,128)S(1)} %spread.3, f32[16,1024]{1,0:T(8,128)S(1)} %collective-permute-done.10, f32[16,640]{1,0:T(8,128)S(1)} %get-tuple-element.34.refs_4_, f32[16,384]{1,0:T(8,128)S(1)} %get-tuple-element.31.refs_4_), kind=kLoop, calls=%fused_computation.1 | loop fusion | flops 49152 | bytes 262144 | tf_op jit(solution)/shard_map/add | solution.py:491
  (4 shorter events, 0.1 us)
Async XLA Ops:
  0.9 3.5 %collective-permute-start = (f32[16,1280]{1,0:T(8,128)S(1)}, f32[16,1280]{1,0:T(8,128)S(1)}, u32[]{:S(2)}, u32[]{:S(2)}) collective-permute-start(f32[16,1280]{1,0:T(8,128)S(1)} %get-tuple-element.23.stack_ref), channel_id=1, source_target_pairs={{1,0},{0,1},{3,2},{2,3},{5,4},{4,5},{7,6},{6,7},{9,8},{8,9},{11,10... | collective-permute-start | bytes 245768 | tf_op jit(solution)/shard_map/ppermute | solution.py:427
  1.4 13.5 %slice-start = ((s8[8388608]{0:T(1024)(128)(4,1)}), s8[4194304]{0:T(1024)(128)(4,1)S(1)}, s32[]{:S(2)}) async-start(s8[8388608]{0:T(1024)(128)(4,1)} %bitcast), calls=%async_computation | async-start | bytes 8388608
  4.4 10.5 %slice-start.1 = ((s8[8388608]{0:T(1024)(128)(4,1)}), s8[4194304]{0:T(1024)(128)(4,1)S(1)}, s32[]{:S(2)}) async-start(s8[8388608]{0:T(1024)(128)(4,1)} %bitcast), calls=%async_computation.1 | async-start | bytes 8388608
  4.5 10.4 %collective-permute-start.1 = (f32[16,1536]{1,0:T(8,128)S(1)}, f32[16,1536]{1,0:T(8,128)S(1)}, u32[]{:S(2)}, u32[]{:S(2)}) collective-permute-start(f32[16,1536]{1,0:T(8,128)S(1)} %strip.1.own_ref), channel_id=1, source_target_pairs={{0,1},{1,0},{2,4},{3,5},{4,2},{5,3},{6,8},{7,9},{8,6},{9,7},{10,12... | collective-permute-start | bytes 294920 | tf_op jit(solution)/shard_map/ppermute | solution.py:442
  4.6 10.3 %collective-permute-start.2 = (f32[16,1536]{1,0:T(8,128)S(1)}, f32[16,1536]{1,0:T(8,128)S(1)}, u32[]{:S(2)}, u32[]{:S(2)}) collective-permute-start(f32[16,1536]{1,0:T(8,128)S(1)} %strip.1.own_ref), channel_id=1, source_target_pairs={{0,2},{1,3},{2,0},{3,1},{4,6},{5,7},{6,4},{7,5},{8,10},{9,11},{10,... | collective-permute-start | bytes 294920 | tf_op jit(solution)/shard_map/ppermute | solution.py:442
  8.5 6.4 %copy-start = (s32[8,8]{1,0:T(8,128)S(1)}, s32[8,8]{1,0:T(8,128)}, u32[]{:S(2)}) copy-start(s32[8,8]{1,0:T(8,128)} %ids_ref.3) | copy-start | bytes 772
  8.5 6.4 %copy-start.1 = (s32[8]{0:T(128)S(1)}, s32[8]{0:T(128)}, u32[]{:S(2)}) copy-start(s32[8]{0:T(128)} %counts_ref.3) | copy-start | bytes 100
  11.3 6.5 %collective-permute-start.3 = (f32[16,1024]{1,0:T(8,128)S(1)}, f32[16,1024]{1,0:T(8,128)S(1)}, u32[]{:S(2)}, u32[]{:S(2)}) collective-permute-start(f32[16,1024]{1,0:T(8,128)S(1)} %get-tuple-element.30.rest_0_.refs_0_), channel_id=1, source_target_pairs={{0,4},{2,6},{4,0},{6,2},{8,12},{10,14},{12,8},{14,10},{16,20},{18,... | collective-permute-start | bytes 196616 | tf_op jit(solution)/shard_map/ppermute | solution.py:419
  12.9 5.2 %collective-permute-start.4 = (f32[16,1024]{1,0:T(8,128)S(1)}, f32[16,1024]{1,0:T(8,128)S(1)}, u32[]{:S(2)}, u32[]{:S(2)}) collective-permute-start(f32[16,1024]{1,0:T(8,128)S(1)} %get-tuple-element.30.rest_0_.refs_0_), channel_id=1, source_target_pairs={{0,6},{2,4},{4,2},{6,0},{8,14},{10,12},{12,10},{14,8},{16,22},{18,... | collective-permute-start | bytes 196616 | tf_op jit(solution)/shard_map/ppermute | solution.py:419
  12.9 5.2 %collective-permute-start.5 = (f32[16,1024]{1,0:T(8,128)S(1)}, f32[16,1024]{1,0:T(8,128)S(1)}, u32[]{:S(2)}, u32[]{:S(2)}) collective-permute-start(f32[16,1024]{1,0:T(8,128)S(1)} %get-tuple-element.30.rest_0_.refs_0_), channel_id=1, source_target_pairs={{0,2},{2,0},{4,6},{6,4},{8,10},{10,8},{12,14},{14,12},{16,18},{18,... | collective-permute-start | bytes 196616 | tf_op jit(solution)/shard_map/ppermute | solution.py:419
  18.2 8.1 %collective-permute-start.6 = (f32[16,1024]{1,0:T(8,128)S(1)}, f32[16,1024]{1,0:T(8,128)S(1)}, u32[]{:S(2)}, u32[]{:S(2)}) collective-permute-start(f32[16,1024]{1,0:T(8,128)S(1)} %add.14.rest_0_.refs_0_), channel_id=1, source_target_pairs={{0,24},{2,26},{4,28},{6,30},{8,16},{10,18},{12,20},{14,22},{16,8},... | collective-permute-start | bytes 196616 | tf_op jit(solution)/shard_map/ppermute | solution.py:419
  22.2 5.4 %collective-permute-start.7 = (f32[16,1024]{1,0:T(8,128)S(1)}, f32[16,1024]{1,0:T(8,128)S(1)}, u32[]{:S(2)}, u32[]{:S(2)}) collective-permute-start(f32[16,1024]{1,0:T(8,128)S(1)} %add.14.rest_0_.refs_0_), channel_id=1, source_target_pairs={{0,16},{2,18},{4,20},{6,22},{8,24},{10,26},{12,28},{14,30},{16,0},... | collective-permute-start | bytes 196616 | tf_op jit(solution)/shard_map/ppermute | solution.py:419
  22.2 5.4 %collective-permute-start.8 = (f32[16,1024]{1,0:T(8,128)S(1)}, f32[16,1024]{1,0:T(8,128)S(1)}, u32[]{:S(2)}, u32[]{:S(2)}) collective-permute-start(f32[16,1024]{1,0:T(8,128)S(1)} %add.14.rest_0_.refs_0_), channel_id=1, source_target_pairs={{0,8},{2,10},{4,12},{6,14},{8,0},{10,2},{12,4},{14,6},{16,24},{18,... | collective-permute-start | bytes 196616 | tf_op jit(solution)/shard_map/ppermute | solution.py:419
  27.6 1.3 %collective-permute-start.9 = (f32[16,1024]{1,0:T(8,128)S(1)}, f32[16,1024]{1,0:T(8,128)S(1)}, u32[]{:S(2)}, u32[]{:S(2)}) collective-permute-start(f32[16,1024]{1,0:T(8,128)S(1)} %add.15.proj_ref), channel_id=1, source_target_pairs={{1,0},{0,1},{3,2},{2,3},{5,4},{4,5},{7,6},{6,7},{9,8},{8,9},{11,10... | collective-permute-start | bytes 196616 | tf_op jit(solution)/shard_map/ppermute | solution.py:427
  30.4 1.3 %collective-permute-start.10 = (f32[16,1024]{1,0:T(8,128)S(1)}, f32[16,1024]{1,0:T(8,128)S(1)}, u32[]{:S(2)}, u32[]{:S(2)}) collective-permute-start(f32[16,1024]{1,0:T(8,128)S(1)} %spread.2), channel_id=1, source_target_pairs={{1,0},{0,1},{3,2},{2,3},{5,4},{4,5},{7,6},{6,7},{9,8},{8,9},{11,10... | collective-permute-start | bytes 196616 | tf_op jit(solution)/shard_map/ppermute | solution.py:427

commit v29 on v27

--- a/solution.py
+++ b/solution.py
@@ -277,28 +277,34 @@
     )(*operands)
 
 
-def spread_kernel(scale, factor_ref, high_ref, low_ref, out_ref):
+def spread_kernel(scale, factor_ref, high_ref, low_ref, *rest):
+    *base, out_ref = rest
     points = high_ref.shape[1]
     tile = min(TILE, points)
     weights = stacked_halves(factor_ref[...] * scale)
     for start in range(0, points, tile):
         lanes = slice(start, start + tile)
         out_ref[:, lanes] = folded(dot_nn(weights, high_ref[:, lanes]) + dot_nn(weights, low_ref[:, lanes]))
-
-
-def spread(factor, high, low, scale):
+    start = 0
+    for ref in base:
+        lanes = slice(start, start + ref.shape[1])
+        out_ref[:, lanes] = out_ref[:, lanes] + ref[...]
+        start = lanes.stop
+
+
+def spread(factor, high, low, scale, base=()):
     (probes, knots), points = factor.shape, high.shape[1]
     high = pltpu.with_memory_space_constraint(high, pltpu.VMEM)
     low = pltpu.with_memory_space_constraint(low, pltpu.VMEM)
     return pl.pallas_call(
         functools.partial(spread_kernel, scale),
         out_shape=jax.ShapeDtypeStruct((probes, points), jnp.float32),
-        in_specs=[VMEM, VMEM, VMEM],
+        in_specs=[VMEM] * (3 + len(base)),
         out_specs=VMEM,
         compiler_params=pltpu.CompilerParams(vmem_limit_bytes=LIMIT),
         cost_estimate=cost(850, knots * points),
         name="spread",
-    )(factor, high, low)
+    )(factor, high, low, *base)
 
 
 def covariance(square):
@@ -484,11 +490,11 @@
     factor = factored(None, projection, splits, proj_scale, 0)
     for step in range(1, groups):
         factor = factored(factor, shifted(projection, "knot", step), splits, proj_scale, step)
-    total = jnp.concatenate(base, axis=1)
-    for step in reversed(range(groups)):
-        share = spread(factor, parts[step][1], parts[step][2], LOW_SCALE * EXPAND_GAIN)
-        total = total + shifted(share, "knot", -step)
-    return total
+    gain = LOW_SCALE * EXPAND_GAIN
+    shares = []
+    for step in reversed(range(1, groups)):
+        shares.append(shifted(spread(factor, parts[step][1], parts[step][2], gain), "knot", -step))
+    return sum(shares, spread(factor, parts[0][1], parts[0][2], gain, base))
 
 
 def solution(mesh):

time: 32.4 us -> 32.4 us (level)
  no operation moved by 1% of the time
where the time goes in v29:
time: 32.4 us; the launch traced here: 32.2 us
  Pallas kernels  16.1 us (50%)
  starting transfers between devices  13.4 us (41%)
  waiting for transfers between devices  1.98 us (6%)
  other arithmetic  0.64 us (2%)
    ppermute x6, starting transfers between devices, butterfly_round(): lax.ppermute(value, axis, [(i, i ^ step) for i in range(count)])  8.54 us
    pallas_call x2, Pallas kernels, beside_round(): pl.pallas_call(functools.partial(beside_kernel, first, first_row, grain_o...  6.2 us
    pallas_call x2, Pallas kernels, project(): pl.pallas_call(functools.partial(project_kernel, scale, grain_of(scale *...  5.79 us
    ppermute x2, starting transfers between devices, paired(): return lax.ppermute(value, (axis, other), pairs)  4.07 us
    pallas_call x2, Pallas kernels, spread(): pl.pallas_call(functools.partial(spread_kernel, scale), out_shape=jax.Sha...  1.54 us
    pallas_call x2, Pallas kernels, factored(): pl.pallas_call(kernel, out_shape=jax.ShapeDtypeStruct((probes, rows), jnp...  1.53 us
    ppermute x6, waiting for transfers between devices, butterfly_round(): lax.ppermute(value, axis, [(i, i ^ step) for i in range(count)])  1.17 us
    pallas_call x1, Pallas kernels, prepare(): pl.pallas_call(functools.partial(prepare_kernel, blocks), out_shape=(jax....  0.87 us
  transfers between devices with their start and end apart: 11, of which 3 were waited for; matrix products, arithmetic and copies ran while one was open for 0% of the time, Pallas kernels for 42%

profile of v29, /device:TPU:0, one launch (start us, length us, event | category | flops | bytes accessed | tf_op | source)
XLA Modules:
  0.0 32.2 jit_solution(10909907145035800512)
XLA Ops:
  0.0 0.9 %prepare.1 = (f32[16,1280]{1,0:T(8,128)S(1)}, f32[2,1024]{1,0:T(2,128)S(1)}) custom-call(f32[16,1024]{1,0:T(8,128)} %probes_ref.1, f32[2,1024]{1,0:T(2,128)} %locations_ref.1, f32[2,1024]{1,0:T(2,128)} %knots_ref.1), custom_call_target="tpu_custom_call" | custom-call | tf_op jit(solution)/shard_map/prepare/pallas_call | solution.py:95
  0.9 0.5 %collective-permute-start = (f32[16,1280]{1,0:T(8,128)S(1)}, f32[16,1280]{1,0:T(8,128)S(1)}, u32[]{:S(2)}, u32[]{:S(2)}) collective-permute-start(f32[16,1280]{1,0:T(8,128)S(1)} %get-tuple-element.23.stack_ref), channel_id=1, source_target_pairs={{1,0},{0,1},{3,2},{2,3},{5,4},{4,5},{7,6},{6,7},{9,8},{8,9},{11,10... | collective-permute-start | bytes 245768 | tf_op jit(solution)/shard_map/ppermute | solution.py:432
  1.4 0.0 slice-start
  1.4 3.0 %project.2 = (f32[16,1024]{1,0:T(8,128)S(1)}, bf16[1024,1024]{1,0:T(8,128)(2,1)S(1)}, bf16[1024,1024]{1,0:T(8,128)(2,1)S(1)}, f32[1024,8]{1,0:T(8,128)S(1)}, f32[16,1280]{1,0:T(8,128)S(1)}) custom-call(f32[16,1280]{1,0:T(8,128)S(1)} %get-tuple-element.23.stack_ref, f32[2,1024]{1,0:T(2,128)S(1)} %get-tuple-element.24.rest_0_), custom_call_target="tpu_custom_call" | custom-call | flops 2936012800 | bytes 4194304 | tf_op jit(solution)/shard_map/project/pallas_call | solution.py:225
  4.4 0.0 collective-permute-done.stack_ref.below_ref.above_ref
  4.4 0.0 slice-start.1
  4.5 0.1 collective-permute-start.4
  4.6 3.9 %collective-permute-start.5 = (f32[16,1536]{1,0:T(8,128)S(1)}, f32[16,1536]{1,0:T(8,128)S(1)}, u32[]{:S(2)}, u32[]{:S(2)}) collective-permute-start(f32[16,1536]{1,0:T(8,128)S(1)} %strip.1.own_ref), channel_id=1, source_target_pairs={{0,2},{1,3},{2,0},{3,1},{4,6},{5,7},{6,4},{7,5},{8,10},{9,11},{10,... | collective-permute-start | bytes 294920 | tf_op jit(solution)/shard_map/ppermute | solution.py:447
  8.5 0.0 copy-start
  8.5 0.0 copy-start.1
  8.5 2.8 %project.3 = (f32[16,1024]{1,0:T(8,128)S(1)}, bf16[1024,1024]{1,0:T(8,128)(2,1)S(1)}, bf16[1024,1024]{1,0:T(8,128)(2,1)S(1)}) custom-call(f32[16,1280]{1,0:T(8,128)S(1)} %collective-permute-done.stack_ref.below_ref.above_ref, f32[16,1024]{1,0:T(8,128)S(1)} %get-tuple-element.25.rest_0_, f32[1024,8]{1,0:T(8,128)S(1)} %get-tuple-element.26.rest_1_), custom_call_target="tpu_custom_call" | custom-call | flops 2936012800 | bytes 4194304 | tf_op jit(solution)/shard_map/project/pallas_call | solution.py:225
  11.3 1.5 %collective-permute-start.1 = (f32[16,1024]{1,0:T(8,128)S(1)}, f32[16,1024]{1,0:T(8,128)S(1)}, u32[]{:S(2)}, u32[]{:S(2)}) collective-permute-start(f32[16,1024]{1,0:T(8,128)S(1)} %get-tuple-element.27.rest_0_.refs_0_), channel_id=1, source_target_pairs={{0,6},{2,4},{4,2},{6,0},{8,14},{10,12},{12,10},{14,8},{16,22},{18,... | collective-permute-start | bytes 196616 | tf_op jit(solution)/shard_map/ppermute | solution.py:424
  12.8 0.2 collective-permute-start.2
  13.0 1.9 %collective-permute-start.3 = (f32[16,1024]{1,0:T(8,128)S(1)}, f32[16,1024]{1,0:T(8,128)S(1)}, u32[]{:S(2)}, u32[]{:S(2)}) collective-permute-start(f32[16,1024]{1,0:T(8,128)S(1)} %get-tuple-element.27.rest_0_.refs_0_), channel_id=1, source_target_pairs={{0,2},{2,0},{4,6},{6,4},{8,10},{10,8},{12,14},{14,12},{16,18},{18,... | collective-permute-start | bytes 196616 | tf_op jit(solution)/shard_map/ppermute | solution.py:424
  14.9 0.0 collective-permute-done.4.odd_ref
  14.9 0.0 collective-permute-done.5.even_ref
  14.9 0.1 assemble.1
  14.9 0.0 slice-done
  15.0 0.0 slice-done.1
  15.0 0.0 copy-done
  15.0 0.0 copy-done.1
  15.0 2.8 %beside.2 = (f32[16,384]{1,0:T(8,128)S(1)}, bf16[2048,512]{1,0:T(8,128)(2,1)S(1)}, bf16[2048,512]{1,0:T(8,128)(2,1)S(1)}) custom-call(s32[8,8]{1,0:T(8,128)S(1)} %copy-done, s32[8]{0:T(128)S(1)} %copy-done.1, f32[16,1280]{1,0:T(8,128)S(1)} %get-tuple-element.28.own_ref, bf16[32,3968]{1,0:T(8,128)(2,1)S(1)} %get-tuple-element.29.values_ref, ...), custom_call_target="tpu_custom_call" | custom-call | flops 196608000 | bytes 1572864 | tf_op jit(solution)/shard_map/beside/pallas_call | solution.py:381
  17.8 0.0 collective-permute-done.1.refs_1_
  17.8 0.0 collective-permute-done.2.refs_2_
  17.8 0.0 collective-permute-done.3.refs_3_
  17.8 4.3 %collective-permute-start.6 = (f32[16,1024]{1,0:T(8,128)S(1)}, f32[16,1024]{1,0:T(8,128)S(1)}, u32[]{:S(2)}, u32[]{:S(2)}) collective-permute-start(f32[16,1024]{1,0:T(8,128)S(1)} %add.6.rest_0_.refs_0_), channel_id=1, source_target_pairs={{0,24},{2,26},{4,28},{6,30},{8,16},{10,18},{12,20},{14,22},{16,8},... | collective-permute-start | bytes 196616 | tf_op jit(solution)/shard_map/ppermute | solution.py:424
  22.2 0.0 collective-permute-start.7
  22.2 0.6 %collective-permute-start.8 = (f32[16,1024]{1,0:T(8,128)S(1)}, f32[16,1024]{1,0:T(8,128)S(1)}, u32[]{:S(2)}, u32[]{:S(2)}) collective-permute-start(f32[16,1024]{1,0:T(8,128)S(1)} %add.6.rest_0_.refs_0_), channel_id=1, source_target_pairs={{0,8},{2,10},{4,12},{6,14},{8,0},{10,2},{12,4},{14,6},{16,24},{18,... | collective-permute-start | bytes 196616 | tf_op jit(solution)/shard_map/ppermute | solution.py:424
  22.8 3.4 %beside.3 = (f32[16,640]{1,0:T(8,128)S(1)}, bf16[2048,512]{1,0:T(8,128)(2,1)S(1)}, bf16[2048,512]{1,0:T(8,128)(2,1)S(1)}) custom-call(s32[8,8]{1,0:T(8,128)S(1)} %copy-done, s32[8]{0:T(128)S(1)} %copy-done.1, f32[16,1280]{1,0:T(8,128)S(1)} %get-tuple-element.28.own_ref, bf16[32,3968]{1,0:T(8,128)(2,1)S(1)} %get-tuple-element.29.values_ref, ...), custom_call_target="tpu_custom_call" | custom-call | flops 327680000 | bytes 2621440 | tf_op jit(solution)/shard_map/beside/pallas_call | solution.py:381
  26.3 0.0 collective-permute-done.6.refs_1_
  26.3 1.2 %collective-permute-done.7.refs_2_ = f32[16,1024]{1,0:T(8,128)S(1)} collective-permute-done((f32[16,1024]{1,0:T(8,128)S(1)}, f32[16,1024]{1,0:T(8,128)S(1)}, u32[]{:S(2)}, u32[]{:S(2)}) %collective-permute-start.7) | collective-permute-done | bytes 65568 | tf_op jit(solution)/shard_map/ppermute | solution.py:424
  27.4 0.0 collective-permute-done.8.refs_3_
  27.4 0.1 collective-permute-start.9
  27.5 0.8 %factor.2.before_ref = f32[16,1024]{1,0:T(8,128)S(1)} custom-call(f32[16,1024]{1,0:T(8,128)S(1)} %add.7.proj_ref, bf16[2048,512]{1,0:T(8,128)(2,1)S(1)} %get-tuple-element.32.refs_5_.rest_0_, bf16[2048,512]{1,0:T(8,128)(2,1)S(1)} %get-tuple-element.35.refs_5_.rest_1_, bf16[2048,512]{1,0:T(8,128)(2,1)S(1)} %get-tuple-element.33.refs_6_.rest_2_, ...), custom_call_target="tpu_custom_call" | custom-call | flops 1048576000 | bytes 4194304 | tf_op jit(solution)/shard_map/factor/pallas_call | solution.py:268
  28.3 0.5 %collective-permute-done.9.proj_ref = f32[16,1024]{1,0:T(8,128)S(1)} collective-permute-done((f32[16,1024]{1,0:T(8,128)S(1)}, f32[16,1024]{1,0:T(8,128)S(1)}, u32[]{:S(2)}, u32[]{:S(2)}) %collective-permute-start.9) | collective-permute-done | bytes 65568 | tf_op jit(solution)/shard_map/ppermute | solution.py:432
  28.8 0.8 %factor.3.factor_ref = f32[16,1024]{1,0:T(8,128)S(1)} custom-call(f32[16,1024]{1,0:T(8,128)S(1)} %factor.2.before_ref, f32[16,1024]{1,0:T(8,128)S(1)} %collective-permute-done.9.proj_ref, bf16[2048,512]{1,0:T(8,128)(2,1)S(1)} %get-tuple-element.32.refs_5_.rest_0_, bf16[2048,512]{1,0:T(8,128)(2,1)S(1)} %get-tuple-element.35.refs_5_.rest_1_, ...), custom_call_target="tpu_custom_call" | custom-call | flops 1048576000 | bytes 4194304 | tf_op jit(solution)/shard_map/factor/pallas_call | solution.py:268
  29.5 0.8 %spread.3 = f32[16,1024]{1,0:T(8,128)S(1)} custom-call(f32[16,1024]{1,0:T(8,128)S(1)} %factor.3.factor_ref, bf16[1024,1024]{1,0:T(8,128)(2,1)S(1)} %get-tuple-element.39.high_ref, bf16[1024,1024]{1,0:T(8,128)(2,1)S(1)} %get-tuple-element.40.low_ref), custom_call_target="tpu_custom_call" | custom-call | flops 891289600 | bytes 4194304 | tf_op jit(solution)/shard_map/spread/pallas_call | solution.py:299
  30.3 0.2 collective-permute-start.10
  30.5 0.8 %spread.2 = f32[16,1024]{1,0:T(8,128)S(1)} custom-call(f32[16,1024]{1,0:T(8,128)S(1)} %factor.3.factor_ref, bf16[1024,1024]{1,0:T(8,128)(2,1)S(1)} %get-tuple-element.37.high_ref, bf16[1024,1024]{1,0:T(8,128)(2,1)S(1)} %get-tuple-element.38.low_ref, f32[16,384]{1,0:T(8,128)S(1)} %get-tuple-element.31.refs_4_.rest_0_, ...), custom_call_target="tpu_custom_call" | custom-call | flops 891289600 | bytes 4194304 | tf_op jit(solution)/shard_map/spread/pallas_call | solution.py:299
  31.2 0.3 %collective-permute-done.10 = f32[16,1024]{1,0:T(8,128)S(1)} collective-permute-done((f32[16,1024]{1,0:T(8,128)S(1)}, f32[16,1024]{1,0:T(8,128)S(1)}, u32[]{:S(2)}, u32[]{:S(2)}) %collective-permute-start.10) | collective-permute-done | bytes 65568 | tf_op jit(solution)/shard_map/ppermute | solution.py:432
  31.6 0.6 %add.5 = f32[16,1024]{1,0:T(8,128)} add(f32[16,1024]{1,0:T(8,128)S(1)} %spread.2, f32[16,1024]{1,0:T(8,128)S(1)} %collective-permute-done.10) | non-fusion elementwise | flops 16384 | bytes 196608 | tf_op jit(solution)/shard_map/add | solution.py:497
  (4 shorter events, 0.1 us)
Async XLA Ops:
  0.9 3.5 %collective-permute-start = (f32[16,1280]{1,0:T(8,128)S(1)}, f32[16,1280]{1,0:T(8,128)S(1)}, u32[]{:S(2)}, u32[]{:S(2)}) collective-permute-start(f32[16,1280]{1,0:T(8,128)S(1)} %get-tuple-element.23.stack_ref), channel_id=1, source_target_pairs={{1,0},{0,1},{3,2},{2,3},{5,4},{4,5},{7,6},{6,7},{9,8},{8,9},{11,10... | collective-permute-start | bytes 245768 | tf_op jit(solution)/shard_map/ppermute | solution.py:432
  1.4 13.5 %slice-start = ((s8[8388608]{0:T(1024)(128)(4,1)}), s8[4194304]{0:T(1024)(128)(4,1)S(1)}, s32[]{:S(2)}) async-start(s8[8388608]{0:T(1024)(128)(4,1)} %bitcast), calls=%async_computation | async-start | bytes 8388608
  4.4 10.5 %slice-start.1 = ((s8[8388608]{0:T(1024)(128)(4,1)}), s8[4194304]{0:T(1024)(128)(4,1)S(1)}, s32[]{:S(2)}) async-start(s8[8388608]{0:T(1024)(128)(4,1)} %bitcast), calls=%async_computation.1 | async-start | bytes 8388608
  4.5 10.4 %collective-permute-start.4 = (f32[16,1536]{1,0:T(8,128)S(1)}, f32[16,1536]{1,0:T(8,128)S(1)}, u32[]{:S(2)}, u32[]{:S(2)}) collective-permute-start(f32[16,1536]{1,0:T(8,128)S(1)} %strip.1.own_ref), channel_id=1, source_target_pairs={{0,1},{1,0},{2,4},{3,5},{4,2},{5,3},{6,8},{7,9},{8,6},{9,7},{10,12... | collective-permute-start | bytes 294920 | tf_op jit(solution)/shard_map/ppermute | solution.py:447
  4.6 10.3 %collective-permute-start.5 = (f32[16,1536]{1,0:T(8,128)S(1)}, f32[16,1536]{1,0:T(8,128)S(1)}, u32[]{:S(2)}, u32[]{:S(2)}) collective-permute-start(f32[16,1536]{1,0:T(8,128)S(1)} %strip.1.own_ref), channel_id=1, source_target_pairs={{0,2},{1,3},{2,0},{3,1},{4,6},{5,7},{6,4},{7,5},{8,10},{9,11},{10,... | collective-permute-start | bytes 294920 | tf_op jit(solution)/shard_map/ppermute | solution.py:447
  8.5 6.4 %copy-start = (s32[8,8]{1,0:T(8,128)S(1)}, s32[8,8]{1,0:T(8,128)}, u32[]{:S(2)}) copy-start(s32[8,8]{1,0:T(8,128)} %ids_ref.3) | copy-start | bytes 772
  8.5 6.4 %copy-start.1 = (s32[8]{0:T(128)S(1)}, s32[8]{0:T(128)}, u32[]{:S(2)}) copy-start(s32[8]{0:T(128)} %counts_ref.3) | copy-start | bytes 100
  11.3 6.5 %collective-permute-start.1 = (f32[16,1024]{1,0:T(8,128)S(1)}, f32[16,1024]{1,0:T(8,128)S(1)}, u32[]{:S(2)}, u32[]{:S(2)}) collective-permute-start(f32[16,1024]{1,0:T(8,128)S(1)} %get-tuple-element.27.rest_0_.refs_0_), channel_id=1, source_target_pairs={{0,6},{2,4},{4,2},{6,0},{8,14},{10,12},{12,10},{14,8},{16,22},{18,... | collective-permute-start | bytes 196616 | tf_op jit(solution)/shard_map/ppermute | solution.py:424
  12.8 5.0 %collective-permute-start.2 = (f32[16,1024]{1,0:T(8,128)S(1)}, f32[16,1024]{1,0:T(8,128)S(1)}, u32[]{:S(2)}, u32[]{:S(2)}) collective-permute-start(f32[16,1024]{1,0:T(8,128)S(1)} %get-tuple-element.27.rest_0_.refs_0_), channel_id=1, source_target_pairs={{0,4},{2,6},{4,0},{6,2},{8,12},{10,14},{12,8},{14,10},{16,20},{18,... | collective-permute-start | bytes 196616 | tf_op jit(solution)/shard_map/ppermute | solution.py:424
  13.0 4.8 %collective-permute-start.3 = (f32[16,1024]{1,0:T(8,128)S(1)}, f32[16,1024]{1,0:T(8,128)S(1)}, u32[]{:S(2)}, u32[]{:S(2)}) collective-permute-start(f32[16,1024]{1,0:T(8,128)S(1)} %get-tuple-element.27.rest_0_.refs_0_), channel_id=1, source_target_pairs={{0,2},{2,0},{4,6},{6,4},{8,10},{10,8},{12,14},{14,12},{16,18},{18,... | collective-permute-start | bytes 196616 | tf_op jit(solution)/shard_map/ppermute | solution.py:424
  17.8 8.4 %collective-permute-start.6 = (f32[16,1024]{1,0:T(8,128)S(1)}, f32[16,1024]{1,0:T(8,128)S(1)}, u32[]{:S(2)}, u32[]{:S(2)}) collective-permute-start(f32[16,1024]{1,0:T(8,128)S(1)} %add.6.rest_0_.refs_0_), channel_id=1, source_target_pairs={{0,24},{2,26},{4,28},{6,30},{8,16},{10,18},{12,20},{14,22},{16,8},... | collective-permute-start | bytes 196616 | tf_op jit(solution)/shard_map/ppermute | solution.py:424
  22.2 5.2 %collective-permute-start.7 = (f32[16,1024]{1,0:T(8,128)S(1)}, f32[16,1024]{1,0:T(8,128)S(1)}, u32[]{:S(2)}, u32[]{:S(2)}) collective-permute-start(f32[16,1024]{1,0:T(8,128)S(1)} %add.6.rest_0_.refs_0_), channel_id=1, source_target_pairs={{0,16},{2,18},{4,20},{6,22},{8,24},{10,26},{12,28},{14,30},{16,0},... | collective-permute-start | bytes 196616 | tf_op jit(solution)/shard_map/ppermute | solution.py:424
  22.2 5.2 %collective-permute-start.8 = (f32[16,1024]{1,0:T(8,128)S(1)}, f32[16,1024]{1,0:T(8,128)S(1)}, u32[]{:S(2)}, u32[]{:S(2)}) collective-permute-start(f32[16,1024]{1,0:T(8,128)S(1)} %add.6.rest_0_.refs_0_), channel_id=1, source_target_pairs={{0,8},{2,10},{4,12},{6,14},{8,0},{10,2},{12,4},{14,6},{16,24},{18,... | collective-permute-start | bytes 196616 | tf_op jit(solution)/shard_map/ppermute | solution.py:424
  27.4 1.3 %collective-permute-start.9 = (f32[16,1024]{1,0:T(8,128)S(1)}, f32[16,1024]{1,0:T(8,128)S(1)}, u32[]{:S(2)}, u32[]{:S(2)}) collective-permute-start(f32[16,1024]{1,0:T(8,128)S(1)} %add.7.proj_ref), channel_id=1, source_target_pairs={{1,0},{0,1},{3,2},{2,3},{5,4},{4,5},{7,6},{6,7},{9,8},{8,9},{11,10... | collective-permute-start | bytes 196616 | tf_op jit(solution)/shard_map/ppermute | solution.py:432
  30.3 1.3 %collective-permute-start.10 = (f32[16,1024]{1,0:T(8,128)S(1)}, f32[16,1024]{1,0:T(8,128)S(1)}, u32[]{:S(2)}, u32[]{:S(2)}) collective-permute-start(f32[16,1024]{1,0:T(8,128)S(1)} %spread.3), channel_id=1, source_target_pairs={{1,0},{0,1},{3,2},{2,3},{5,4},{4,5},{7,6},{6,7},{9,8},{8,9},{11,10... | collective-permute-start | bytes 196616 | tf_op jit(solution)/shard_map/ppermute | solution.py:432
